TPU v7x, 32 devices: a whole 2x2x4 slice. The times are simulated.
32 devices in a mesh: gx: 4 (over x, core), gy: 4 (over z), gz: 2 (over y).
Axes of the slice: x: 2, y: 2, z: 4, core: 2. Of those that a mesh axis runs over, the one named last changes fastest.
Arguments:
- layer_input: bfloat16 [1024, 6144], P(('gx', 'gy'), 'gz'), may hold values from -70 to 70
- out_cotangent: bfloat16 [1024, 6144], P(('gx', 'gy'), 'gz'), may hold values from -6 to 6
- w_query: bfloat16 [6144, 6144], P(('gz', 'gx'), 'gy'), may hold values from -0.078125 to 0.078125
- w_key: bfloat16 [6144, 6144], P(('gz', 'gx'), 'gy'), may hold values from -0.078125 to 0.078125
- w_value: bfloat16 [6144, 6144], P(('gz', 'gx'), 'gy'), may hold values from -0.078125 to 0.078125
- w_mlp_in: bfloat16 [6144, 24576], P(('gz', 'gx'), 'gy'), may hold values from -0.078125 to 0.078125
- w_attn_out: bfloat16 [6144, 6144], P(('gy', 'gx'), 'gz'), may hold values from -0.078125 to 0.078125
- w_mlp_out: bfloat16 [24576, 6144], P(('gy', 'gx'), 'gz'), may hold values from -0.0390625 to 0.0390625
Outputs:
- layer_out: bfloat16 [1024, 6144], P(('gx', 'gy'), 'gz')
- input_grad: bfloat16 [1024, 6144], P(('gx', 'gy'), 'gz')
All inputs are finite; a program needn't handle non-finite values.
Results may differ from a plain program's by a relative error of at most 0.01.
Values may be sent and summed in bfloat16 or wider, within the bound.
No kernel may reach another device: no remote copies, remote signals or barrier semaphores. Data moves between devices by JAX's collectives and lax.ppermute only.
A program may use at most 320 MiB of HBM per device.

v0:
```python
import math

import jax
import jax.numpy as jnp
from jax import lax
from jax.sharding import PartitionSpec as P

D = 6144
HEAD_DIM = 128
IMG_TOK = 256


EPSILON = 1e-06
ROOT_HALF = 0.7071067811865476
ROOT_TWO_PI_INV = 0.3989422804014327


def head_norm(values):
    center = values - jnp.mean(values, axis=-1, keepdims=True)
    spread = jnp.mean(center * center, axis=-1, keepdims=True)
    return center * lax.rsqrt(spread + EPSILON)


def attend(query, keys, values):
    q_norm = head_norm(query).astype(jnp.bfloat16)
    k_norm = head_norm(keys).astype(jnp.bfloat16)
    v_half = values.astype(jnp.bfloat16)
    scale = 1.0 / math.sqrt(query.shape[-1])
    scores = (
        jnp.einsum("bqhd,bkhd->bhqk", q_norm, k_norm, preferred_element_type=jnp.float32) * scale
    )
    weights = jnp.exp(scores)
    probs = weights / jnp.sum(weights, axis=-1, keepdims=True)
    probs_half = probs.astype(jnp.bfloat16)
    mixed = jnp.einsum("bhqk,bkhd->bqhd", probs_half, v_half, preferred_element_type=jnp.float32)
    return mixed.astype(jnp.bfloat16)


def gelu(pre):
    return pre * 0.5 * (1.0 + lax.erf(pre * ROOT_HALF))


def gelu_back(pre, grad_half):
    cdf = 0.5 * (1.0 + lax.erf(pre * ROOT_HALF))
    pdf = jnp.exp(-0.5 * pre * pre) * ROOT_TWO_PI_INV
    return (grad_half.astype(jnp.float32) * (cdf + pre * pdf)).astype(jnp.bfloat16)


def back_dot(left, right):
    return lax.dot_general(
        left, right, (((1,), (1,)), ((), ())), preferred_element_type=jnp.float32
    )


def body(layer_input, out_cotangent, w_query, w_key, w_value, w_mlp_in, w_attn_out, w_mlp_out):

    def row_totals(first_part, second_part):
        return lax.psum((first_part, second_part), "gz")

    def image_rows(block):
        return lax.all_gather(block, "gy", axis=0, tiled=True)

    def spread_rows(term, rows):
        return lax.psum_scatter(
            term(jnp.int32(0), rows * lax.axis_size("gy")).astype(jnp.bfloat16),
            "gy",
            scatter_dimension=0,
            tiled=True,
        ).astype(jnp.float32)

    own_rows = layer_input.shape[0]
    wide = layer_input.astype(jnp.float32)
    total, squares = row_totals(jnp.sum(wide, axis=1), jnp.sum(wide * wide, axis=1))
    center = total / D
    spread = squares / D - center * center
    inverse = lax.rsqrt(spread + EPSILON)
    normed = (wide - center[:, None]) * inverse[:, None]
    gathered_in = image_rows(normed.astype(jnp.bfloat16))
    rows_query, rows_key, rows_value, rows_mlp_in, rows_attn_out, rows_mlp_out = (
        lax.all_gather(w_query, "gx", axis=0, tiled=True),
        lax.all_gather(w_key, "gx", axis=0, tiled=True),
        lax.all_gather(w_value, "gx", axis=0, tiled=True),
        lax.all_gather(w_mlp_in, "gx", axis=0, tiled=True),
        lax.all_gather(w_attn_out, "gx", axis=0, tiled=True),
        lax.all_gather(w_mlp_out, "gx", axis=0, tiled=True),
    )

    def project(weight):
        return jnp.dot(gathered_in, weight, preferred_element_type=jnp.float32)

    query, keys, values, hidden_pre = (
        lax.psum(project(rows_query).astype(jnp.bfloat16), "gz").astype(jnp.float32),
        lax.psum(project(rows_key).astype(jnp.bfloat16), "gz").astype(jnp.float32),
        lax.psum(project(rows_value).astype(jnp.bfloat16), "gz").astype(jnp.float32),
        lax.psum(project(rows_mlp_in).astype(jnp.bfloat16), "gz").astype(jnp.float32),
    )
    activated = gelu(hidden_pre).astype(jnp.bfloat16)
    block_rows = query.shape[0]
    heads_here = query.shape[1] // HEAD_DIM

    def split_heads(block):
        return block.reshape(block_rows // IMG_TOK, IMG_TOK, heads_here, HEAD_DIM)

    mixed, attend_back = jax.vjp(attend, split_heads(query), split_heads(keys), split_heads(values))
    mixed_rows = mixed.reshape(block_rows, query.shape[1])

    def forward_term(start, count):
        return jnp.dot(mixed_rows, rows_attn_out, preferred_element_type=jnp.float32) + jnp.dot(
            activated, rows_mlp_out, preferred_element_type=jnp.float32
        )

    summed = spread_rows(forward_term, own_rows)
    layer_out = (wide + summed).astype(jnp.bfloat16)
    gathered_cot = image_rows(out_cotangent)
    mixed_grad, act_grad = (
        lax.psum(back_dot(gathered_cot, rows_attn_out).astype(jnp.bfloat16), "gz").astype(
            jnp.float32
        ),
        lax.psum(back_dot(gathered_cot, rows_mlp_out).astype(jnp.bfloat16), "gz").astype(
            jnp.float32
        ),
    )
    hidden_grad = gelu_back(hidden_pre, act_grad.astype(jnp.bfloat16))
    query_grad, key_grad, value_grad = attend_back(split_heads(mixed_grad.astype(jnp.bfloat16)))
    query_half = query_grad.reshape(block_rows, -1).astype(jnp.bfloat16)
    key_half = key_grad.reshape(block_rows, -1).astype(jnp.bfloat16)
    value_half = value_grad.reshape(block_rows, -1).astype(jnp.bfloat16)

    def backward_term(start, count):
        result = back_dot(query_half, rows_query)
        result = result + back_dot(key_half, rows_key)
        result = result + back_dot(value_half, rows_value)
        return result + back_dot(hidden_grad, rows_mlp_in)

    normed_grad = spread_rows(backward_term, own_rows)
    first, second = row_totals(jnp.sum(normed_grad, axis=1), jnp.sum(normed_grad * normed, axis=1))
    grad_full = out_cotangent.astype(jnp.float32) + inverse[:, None] * (
        normed_grad - (first / D)[:, None] - normed * (second / D)[:, None]
    )
    return (layer_out, grad_full.astype(jnp.bfloat16))


def solution(mesh):
    in_specs = (
        P(("gx", "gy"), "gz"),
        P(("gx", "gy"), "gz"),
        P(("gz", "gx"), "gy"),
        P(("gz", "gx"), "gy"),
        P(("gz", "gx"), "gy"),
        P(("gz", "gx"), "gy"),
        P(("gy", "gx"), "gz"),
        P(("gy", "gx"), "gz"),
    )
    out_specs = (P(("gx", "gy"), "gz"), P(("gx", "gy"), "gz"))
    return jax.shard_map(body, mesh=mesh, in_specs=in_specs, out_specs=out_specs, check_vma=False)
```

profile of v0, /device:TPU:0, one launch (start us, length us, event | category | flops | bytes accessed | tf_op | source)
XLA Modules:
  0.0 1183.1 jit_solution(314509689803182354)
XLA Ops:
  7.2 1.2 convert_reduce_fusion
  8.4 5.9 all-reduce.1
  14.3 0.6 copy-done.5
  14.9 1.9 fusion.38
  16.8 0.7 all-gather.11.cloned.1.call-update
  17.6 0.7 all-gather.23.cloned.1.call-update
  18.3 0.5 all-gather.17.cloned.1.call-update
  18.9 0.5 all-gather.15.cloned.1.call-update
  19.5 0.5 all-gather.13.cloned.1.call-update
  20.1 0.7 all-gather.21.cloned.1.call-update
  20.8 0.7 all-gather.19.cloned.1.call-update
  21.6 34.3 %all-gather.9.cloned.1.call-done = bf16[256,3072]{1,0:T(8,128)(2,1)} async-done(((bf16[64,3072]{1,0:T(8,128)(2,1)}), bf16[256,3072]{1,0:T(8,128)(2,1)}) %all-gather.9.cloned.1.call-update) | async-done | bytes 1572880 | tf_op jit(solution)/shard_map/all_gather | solution.py:61
  55.8 64.7 %all-gather.11.cloned.1.call-done = bf16[3072,1536]{1,0:T(8,128)(2,1)} async-done(((bf16[768,1536]{1,0:T(8,128)(2,1)}), bf16[3072,1536]{1,0:T(8,128)(2,1)}) %all-gather.11.cloned.1.call-update) | async-done | bytes 9437200 | tf_op jit(solution)/shard_map/all_gather | solution.py:82
  120.5 6.8 convolution_convert_fusion.5
  127.3 1.2 copy.23
  128.4 30.8 %all-gather.23.cloned.1.call-done = bf16[256,3072]{1,0:T(8,128)(2,1)} async-done(((bf16[64,3072]{1,0:T(8,128)(2,1)}), bf16[256,3072]{1,0:T(8,128)(2,1)}) %all-gather.23.cloned.1.call-update) | async-done | bytes 1572880 | tf_op jit(solution)/shard_map/all_gather | solution.py:61
  159.2 64.5 %all-gather.17.cloned.1.call-done = bf16[1536,3072]{1,0:T(8,128)(2,1)} async-done(((bf16[384,3072]{1,0:T(8,128)(2,1)}), bf16[1536,3072]{1,0:T(8,128)(2,1)}) %all-gather.17.cloned.1.call-update) | async-done | bytes 9437200 | tf_op jit(solution)/shard_map/all_gather | solution.py:84
  223.8 6.8 convolution_convert_fusion.2
  230.6 1.2 copy.31
  231.8 57.7 %all-gather.15.cloned.1.call-done = bf16[3072,1536]{1,0:T(8,128)(2,1)} async-done(((bf16[768,1536]{1,0:T(8,128)(2,1)}), bf16[3072,1536]{1,0:T(8,128)(2,1)}) %all-gather.15.cloned.1.call-update) | async-done | bytes 9437200 | tf_op jit(solution)/shard_map/all_gather | solution.py:81
  289.5 7.2 convolution_convert_fusion.3
  296.6 58.5 %all-gather.13.cloned.1.call-done = bf16[3072,1536]{1,0:T(8,128)(2,1)} async-done(((bf16[768,1536]{1,0:T(8,128)(2,1)}), bf16[3072,1536]{1,0:T(8,128)(2,1)}) %all-gather.13.cloned.1.call-update) | async-done | bytes 9437200 | tf_op jit(solution)/shard_map/all_gather | solution.py:80
  355.1 7.2 convolution_convert_fusion.4
  362.3 221.7 %all-gather.21.cloned.1.call-done = bf16[6144,3072]{1,0:T(8,128)(2,1)} async-done(((bf16[1536,3072]{1,0:T(8,128)(2,1)}), bf16[6144,3072]{1,0:T(8,128)(2,1)}) %all-gather.21.cloned.1.call-update) | async-done | bytes 37748752 | tf_op jit(solution)/shard_map/all_gather | solution.py:85
  584.0 23.0 %convolution_convert_fusion = bf16[256,6144]{1,0:T(8,128)(2,1)} fusion(bf16[256,3072]{1,0:T(8,128)(2,1)} %all-gather.23.cloned.1.call-done, bf16[6144,3072]{1,0:T(8,128)(2,1)} %all-gather.21.cloned.1.call-done), kind=kOutput, calls=%fused_computation.5 | convolution fusion | flops 9665249280 | bytes 42467328 | tf_op jit(solution)/shard_map/dot_general | solution.py:50
  607.0 205.8 %all-gather.19.cloned.1.call-done = bf16[3072,6144]{1,0:T(8,128)(2,1)} async-done(((bf16[768,6144]{1,0:T(8,128)(2,1)}), bf16[3072,6144]{1,0:T(8,128)(2,1)}) %all-gather.19.cloned.1.call-update) | async-done | bytes 37748752 | tf_op jit(solution)/shard_map/all_gather | solution.py:83
  812.8 18.2 %convolution_convert_fusion.1 = bf16[256,6144]{1,0:T(8,128)(2,1)} fusion(bf16[256,3072]{1,0:T(8,128)(2,1)S(1)} %copy-done.10, bf16[3072,6144]{1,0:T(8,128)(2,1)} %all-gather.19.cloned.1.call-done), kind=kOutput, calls=%fused_computation.6 | convolution fusion | flops 9665249280 | bytes 42467328 | tf_op jit(solution)/shard_map/dot_general | solution.py:89
  831.3 223.3 %all-reduce.5.cloned.1.call-done = (bf16[256,12,128]{0,2,1:T(8,128)(2,1)}, bf16[256,1536]{1,0:T(8,128)(2,1)}, bf16[256,1536]{1,0:T(8,128)(2,1)}, bf16[256,6144]{...) async-done(((bf16[256,12,128]{0,2,1:T(8,128)(2,1)}, bf16[256,1536]{1,0:T(8,128)(2,1)}, bf16[256,1536]{1,0:T(8,128)(2,1)}, ...) | async-done | bytes 9437200 | tf_op jit(solution)/shard_map/psum | solution.py:94
  1054.5 1.4 copy.24
  1056.1 1.4 copy.26
  1058.0 0.9 fusion.22
  1059.4 1.1 fusion.15
  1060.5 0.6 convolution_convert_fusion.9
  1061.2 1.3 convolution_convert_fusion.10
  1062.5 1.3 fusion.25
  1063.9 1.2 fusion.28
  1066.4 0.4 add_convert_fusion.1
  1066.9 5.6 fusion.55
  1072.5 5.3 convolution_add_fusion.3
  1077.9 4.3 convolution_add_fusion.2
  1082.3 19.5 %fusion.10 = bf16[256,3072]{1,0:T(8,128)(2,1)} fusion(f32[256,3072]{1,0:T(8,128)} %convolution_add_fusion.2, bf16[3072,6144]{1,0:T(8,128)(2,1)} %all-gather.19.cloned.1.call-done, bf16[256,6144]{1,0:T(8,128)(2,1)S(1)} %copy-done.9, bf16[256,6144]{1,0:T(8,128)(2,1)} %get-tuple-element.15), kind=kOutput, calls=%fused_computation.23 | convolution fusion | flops 9684123648 | bytes 48758784 | tf_op jit(solution)/shard_map/dot_general | solution.py:50
  1101.9 8.0 fusion.54
  1109.9 20.0 %fusion.9 = bf16[256,3072]{1,0:T(8,128)(2,1)} fusion(f32[256,3072]{1,0:T(8,128)} %fusion.54, bf16[6144,3072]{1,0:T(8,128)(2,1)} %all-gather.21.cloned.1.call-done, bf16[256,6144]{1,0:T(8,128)(2,1)} %get-tuple-element.13), kind=kOutput, calls=%fused_computation.22 | convolution fusion | flops 9674686464 | bytes 45613056 | tf_op jit(solution)/shard_map/dot_general | solution.py:108
  1129.9 7.4 reduce-scatter.5.cloned.1.call-done
  1137.3 1.3 convert_reduce_fusion.1
  1138.6 4.9 all-reduce
  1143.5 30.3 %reduce-scatter.3.cloned.1.call-done = bf16[64,3072]{1,0:T(8,128)(2,1)} async-done(((bf16[256,3072]{1,0:T(8,128)(2,1)}), bf16[64,3072]{1,0:T(8,128)(2,1)}) %reduce-scatter.3.cloned.1.call-update) | async-done | bytes 393232 | tf_op jit(solution)/shard_map/reduce_scatter | solution.py:64
  1173.9 2.4 fusion.34
  (62 shorter events, 3.1 us)
Async XLA Ops:
  7.2 48.7 %all-gather.9.cloned.1.call-start = ((), (), s32[]{:S(2)}) async-start(), calls=%async_computation.2 | async-start | bytes 1966080 | tf_op jit(solution)/shard_map/all_gather | solution.py:61
  14.3 0.6 copy-start.5
  14.3 0.6 copy-start.7
  16.8 103.7 %all-gather.11.cloned.1.call-start = ((), (), s32[]{:S(2)}) async-start(), calls=%async_computation.3 | async-start | bytes 11796480 | tf_op jit(solution)/shard_map/all_gather | solution.py:82
  17.6 141.7 %all-gather.23.cloned.1.call-start = ((), (), s32[]{:S(2)}) async-start(), calls=%async_computation.10 | async-start | bytes 1966080 | tf_op jit(solution)/shard_map/all_gather | solution.py:61
  18.3 205.5 %all-gather.17.cloned.1.call-start = ((), (), s32[]{:S(2)}) async-start(), calls=%async_computation.6 | async-start | bytes 11796480 | tf_op jit(solution)/shard_map/all_gather | solution.py:84
  18.9 270.6 %all-gather.15.cloned.1.call-start = ((), (), s32[]{:S(2)}) async-start(), calls=%async_computation.5 | async-start | bytes 11796480 | tf_op jit(solution)/shard_map/all_gather | solution.py:81
  19.4 335.7 %all-gather.13.cloned.1.call-start = ((), (), s32[]{:S(2)}) async-start(), calls=%async_computation.4 | async-start | bytes 11796480 | tf_op jit(solution)/shard_map/all_gather | solution.py:80
  20.0 564.0 %all-gather.21.cloned.1.call-start = ((), (), s32[]{:S(2)}) async-start(), calls=%async_computation.8 | async-start | bytes 47185920 | tf_op jit(solution)/shard_map/all_gather | solution.py:85
  20.8 792.0 %all-gather.19.cloned.1.call-start = ((), (), s32[]{:S(2)}) async-start(), calls=%async_computation.7 | async-start | bytes 47185920 | tf_op jit(solution)/shard_map/all_gather | solution.py:83
  21.5 1033.0 %all-reduce.5.cloned.1.call-start = ((), (), s32[]{:S(2)}) async-start(), calls=%async_computation.12 | async-start | bytes 18874368 | tf_op jit(solution)/shard_map/psum | solution.py:94
  128.4 161.0 %copy-start.10 = (bf16[256,3072]{1,0:T(8,128)(2,1)S(1)}, bf16[256,3072]{1,0:T(8,128)(2,1)}, u32[]{:S(2)}) copy-start(bf16[256,3072]{1,0:T(8,128)(2,1)} %all-gather.9.cloned.1.call-done) | copy-start | bytes 4718596
  831.1 306.2 %reduce-scatter.5.cloned.1.call-start = ((), (), s32[]{:S(2)}) async-start(), calls=%async_computation.11 | async-start | bytes 1966080 | tf_op jit(solution)/shard_map/reduce_scatter | solution.py:64
  1058.0 1.1 copy-start.3
  1058.0 1.4 copy-start.4
  1066.9 11.0 slice-start
  1066.9 11.0 slice-start.1
  1072.5 5.4 slice-start.2
  1077.9 4.4 copy-start.9
  1082.3 19.6 %copy-start.1 = (bf16[12,128,256]{2,1,0:T(8,128)(2,1)S(1)}, bf16[12,128,256]{2,1,0:T(8,128)(2,1)}, u32[]{:S(2)}) copy-start(bf16[12,128,256]{2,1,0:T(8,128)(2,1)} %convolution_convert_fusion.10) | copy-start | bytes 2359300
  1101.8 72.1 %reduce-scatter.3.cloned.1.call-start = ((), (), s32[]{:S(2)}) async-start(), calls=%async_computation.9 | async-start | bytes 1966080 | tf_op jit(solution)/shard_map/reduce_scatter | solution.py:64
  1109.9 27.4 %copy-start = (bf16[64,3072]{1,0:T(8,128)(2,1)S(1)}, bf16[64,3072]{1,0:T(8,128)(2,1)}, u32[]{:S(2)}) copy-start(bf16[64,3072]{1,0:T(8,128)(2,1)} %param.8) | copy-start | bytes 1179652
  1109.9 27.4 %copy-start.6 = (f32[64]{0:T(128)S(1)}, f32[64]{0:T(128)}, u32[]{:S(2)}) copy-start(f32[64]{0:T(128)} %copy-done.5) | copy-start | bytes 772
  1109.9 27.4 %copy-start.8 = (f32[64]{0:T(128)S(1)}, f32[64]{0:T(128)}, u32[]{:S(2)}) copy-start(f32[64]{0:T(128)} %copy-done.7) | copy-start | bytes 772
  1109.9 64.0 %copy-start.2 = (bf16[64,3072]{1,0:T(8,128)(2,1)S(1)}, bf16[64,3072]{1,0:T(8,128)(2,1)}, u32[]{:S(2)}) copy-start(bf16[64,3072]{1,0:T(8,128)(2,1)} %param.9) | copy-start | bytes 1179652
Sparse Core Ops, SparseCore 0:
  16.9 38.8 all-gather.8
  57.4 63.0 all-gather.10
  122.1 37.0 all-gather.22
  160.6 63.0 all-gather.16
  225.2 64.2 all-gather.14
  290.9 64.2 all-gather.12
  356.7 227.2 all-gather.20
  585.6 227.2 all-gather.18
  831.2 223.3 all-reduce.4
  1101.9 35.2 reduce-scatter.4
  1139.6 34.2 reduce-scatter.2
where the time goes:
time: 1190 us; the launch traced here: 1180 us
  waiting for transfers between devices  1000 us (84%)
  matrix products  138 us (12%)
  between operations  14.4 us (1%)
    psum x1, waiting for transfers between devices, body(): lax.psum(project(rows_value).astype(jnp.bfloat16), 'gz').astype(jnp.float32)  223 us
    all_gather x1, waiting for transfers between devices, body(): lax.all_gather(w_mlp_out, 'gx', axis=0, tiled=True)  222 us
    all_gather x1, waiting for transfers between devices, body(): lax.all_gather(w_mlp_in, 'gx', axis=0, tiled=True)  206 us
    all_gather x2, waiting for transfers between devices, image_rows(): return lax.all_gather(block, 'gy', axis=0, tiled=True)  65 us
    all_gather x1, waiting for transfers between devices, body(): lax.all_gather(w_value, 'gx', axis=0, tiled=True)  64.7 us
    dot_general x6, matrix products, back_dot(): lax.dot_general(left, right, (((1,), (1,)), ((), ())), preferred_element_...  64.6 us
    all_gather x1, waiting for transfers between devices, body(): lax.all_gather(w_attn_out, 'gx', axis=0, tiled=True)  64.5 us
    all_gather x1, waiting for transfers between devices, body(): lax.all_gather(w_query, 'gx', axis=0, tiled=True)  58.5 us
  transfers between devices with their start and end apart: 11, of which 11 were waited for; matrix products, arithmetic and copies ran while one was open for 7% of the time, Pallas kernels for 0%

commit v1 on v0

v1 whole, which is shorter than its diff:
```python
import math

import jax
import jax.numpy as jnp
from jax import lax
from jax.sharding import PartitionSpec as P

D = 6144
HEAD_DIM = 128
IMG_TOK = 256


EPSILON = 1e-06
ROOT_HALF = 0.7071067811865476
ROOT_TWO_PI_INV = 0.3989422804014327


def head_norm(values):
    center = values - jnp.mean(values, axis=-1, keepdims=True)
    spread = jnp.mean(center * center, axis=-1, keepdims=True)
    return center * lax.rsqrt(spread + EPSILON)


def attend(query, keys, values):
    q_norm = head_norm(query).astype(jnp.bfloat16)
    k_norm = head_norm(keys).astype(jnp.bfloat16)
    v_half = values.astype(jnp.bfloat16)
    scale = 1.0 / math.sqrt(query.shape[-1])
    scores = (
        jnp.einsum("bqhd,bkhd->bhqk", q_norm, k_norm, preferred_element_type=jnp.float32) * scale
    )
    weights = jnp.exp(scores)
    probs = weights / jnp.sum(weights, axis=-1, keepdims=True)
    probs_half = probs.astype(jnp.bfloat16)
    mixed = jnp.einsum("bhqk,bkhd->bqhd", probs_half, v_half, preferred_element_type=jnp.float32)
    return mixed.astype(jnp.bfloat16)


def gelu(pre):
    return pre * 0.5 * (1.0 + lax.erf(pre * ROOT_HALF))


def gelu_back(pre, grad_half):
    cdf = 0.5 * (1.0 + lax.erf(pre * ROOT_HALF))
    pdf = jnp.exp(-0.5 * pre * pre) * ROOT_TWO_PI_INV
    return (grad_half.astype(jnp.float32) * (cdf + pre * pdf)).astype(jnp.bfloat16)


def dot(left, right):
    return jnp.dot(left, right, preferred_element_type=jnp.float32)


def back_dot(left, right):
    return lax.dot_general(
        left, right, (((1,), (1,)), ((), ())), preferred_element_type=jnp.float32
    )


def body(layer_input, out_cotangent, w_query, w_key, w_value, w_mlp_in, w_attn_out, w_mlp_out):
    n_gx, n_gy, n_gz = (lax.axis_size(name) for name in ("gx", "gy", "gz"))
    tokens = layer_input.shape[0] * n_gx * n_gy
    paired = n_gz == 2 and tokens % (2 * IMG_TOK) == 0
    kept = tokens // 2 if paired else tokens
    me_z = lax.axis_index("gz")
    swap_z = [(0, 1), (1, 0)]

    def halves(block):
        if not paired:
            return block, None
        mine = lax.dynamic_slice_in_dim(block, me_z * kept, kept, 0)
        other = lax.dynamic_slice_in_dim(block, (1 - me_z) * kept, kept, 0)
        return mine, other

    def sum_gz(term, mine, other):
        if not paired:
            return lax.psum(term(mine).astype(jnp.bfloat16), "gz").astype(jnp.float32)
        got = lax.ppermute(term(other).astype(jnp.bfloat16), "gz", swap_z)
        return term(mine) + got.astype(jnp.float32)

    def from_pair(block):
        return lax.ppermute(block, "gz", swap_z)

    def spread_rows(mine, other):
        if paired:
            first = jnp.where(me_z == 0, mine, other)
            second = jnp.where(me_z == 0, other, mine)
            mine = jnp.concatenate([first, second], axis=0)
        return lax.psum_scatter(
            mine, ("gx", "gy"), scatter_dimension=0, tiled=True
        ).astype(jnp.float32)

    def columns_of(weight):
        return lax.all_to_all(weight, "gx", split_axis=1, concat_axis=0, tiled=True)

    wide = layer_input.astype(jnp.float32)
    total, squares = lax.psum((jnp.sum(wide, axis=1), jnp.sum(wide * wide, axis=1)), "gz")
    center = total / D
    spread = squares / D - center * center
    inverse = lax.rsqrt(spread + EPSILON)
    normed = (wide - center[:, None]) * inverse[:, None]
    gathered_in = lax.all_gather(normed.astype(jnp.bfloat16), ("gx", "gy"), axis=0, tiled=True)
    gathered_cot = lax.all_gather(out_cotangent, ("gx", "gy"), axis=0, tiled=True)
    in_mine, in_other = halves(gathered_in)
    cot_mine, cot_other = halves(gathered_cot)

    rows_query, rows_key, rows_value = columns_of(w_query), columns_of(w_key), columns_of(w_value)
    rows_mlp_in = columns_of(w_mlp_in)

    def project(weight):
        return sum_gz(lambda rows: dot(rows, weight), in_mine, in_other)

    def project_back(weight):
        return sum_gz(lambda rows: back_dot(rows, weight), cot_mine, cot_other).astype(jnp.bfloat16)

    mixed_grad, act_grad = project_back(w_attn_out), project_back(w_mlp_out)
    query, keys, values = project(rows_query), project(rows_key), project(rows_value)
    heads_here = query.shape[1] // HEAD_DIM

    def split_heads(block):
        return block.reshape(kept // IMG_TOK, IMG_TOK, heads_here, HEAD_DIM)

    mixed, attend_back = jax.vjp(attend, split_heads(query), split_heads(keys), split_heads(values))
    mixed_rows = mixed.reshape(kept, query.shape[1])
    query_grad, key_grad, value_grad = attend_back(split_heads(mixed_grad))
    query_half = query_grad.reshape(kept, -1).astype(jnp.bfloat16)
    key_half = key_grad.reshape(kept, -1).astype(jnp.bfloat16)
    value_half = value_grad.reshape(kept, -1).astype(jnp.bfloat16)

    hidden_pre = project(rows_mlp_in)
    activated = gelu(hidden_pre).astype(jnp.bfloat16)
    hidden_grad = gelu_back(hidden_pre, act_grad)

    def forward_term(mixed_part, act_part):
        return (dot(mixed_part, w_attn_out) + dot(act_part, w_mlp_out)).astype(jnp.bfloat16)

    def backward_term(query_part, key_part, value_part, hidden_part):
        result = back_dot(query_part, rows_query)
        result = result + back_dot(key_part, rows_key)
        result = result + back_dot(value_part, rows_value)
        return (result + back_dot(hidden_part, rows_mlp_in)).astype(jnp.bfloat16)

    forward_in = (mixed_rows, activated)
    backward_in = (query_half, key_half, value_half, hidden_grad)
    forward_mine = forward_term(*forward_in)
    backward_mine = backward_term(*backward_in)
    forward_other = backward_other = None
    if paired:
        forward_other = forward_term(*(from_pair(part) for part in forward_in))
        backward_other = backward_term(*(from_pair(part) for part in backward_in))
    summed = spread_rows(forward_mine, forward_other)
    layer_out = (wide + summed).astype(jnp.bfloat16)
    normed_grad = spread_rows(backward_mine, backward_other)
    first, second = lax.psum(
        (jnp.sum(normed_grad, axis=1), jnp.sum(normed_grad * normed, axis=1)), "gz"
    )
    grad_full = out_cotangent.astype(jnp.float32) + inverse[:, None] * (
        normed_grad - (first / D)[:, None] - normed * (second / D)[:, None]
    )
    return (layer_out, grad_full.astype(jnp.bfloat16))


def solution(mesh):
    in_specs = (
        P(("gx", "gy"), "gz"),
        P(("gx", "gy"), "gz"),
        P(("gz", "gx"), "gy"),
        P(("gz", "gx"), "gy"),
        P(("gz", "gx"), "gy"),
        P(("gz", "gx"), "gy"),
        P(("gy", "gx"), "gz"),
        P(("gy", "gx"), "gz"),
    )
    out_specs = (P(("gx", "gy"), "gz"), P(("gx", "gy"), "gz"))
    return jax.shard_map(body, mesh=mesh, in_specs=in_specs, out_specs=out_specs, check_vma=False)
```

time: 1190 us -> 696 us (0.58)
  waiting for transfers between devices: 1000 us -> 399 us
  local copies, waits for them, and re-layouts: 6.25 us -> 68.9 us
  starting transfers between devices: 0.6 us -> 36.1 us
    all_gather x8 -> x2, waiting for transfers between devices: 738 us -> 0.01 us  [the longest x1 0.01 us: body(): lax.all_gather(normed.astype(jnp.bfloat16), ('gx', 'gy'), axis=0, tiled=T...]
    psum x1 -> x0, waiting for transfers between devices: 223 us -> none  [body(): lax.psum(project(rows_value).astype(jnp.bfloat16), 'gz').astype(jnp.float32)]
    all_to_all x0 -> x4, waiting for transfers between devices: none -> 177 us  [columns_of(): return lax.all_to_all(weight, 'gx', split_axis=1, concat_axis=0, tiled=True)]
    ppermute x0 -> x12, waiting for transfers between devices: none -> 105 us  [the longest x6 54.8 us: sum_gz(): got = lax.ppermute(term(other).astype(jnp.bfloat16), 'gz', swap_z)]
    reduce_scatter x2, waiting for transfers between devices: 37.7 us -> 116 us  [spread_rows(): lax.psum_scatter(mine, ('gx', 'gy'), scatter_dimension=0, tiled=True)]
    unnamed x28 -> x84, local copies, waits for them, and re-layouts: 1.09 us -> 29.7 us
    all_to_all x0 -> x4, local copies, waits for them, and re-layouts: none -> 25.5 us  [columns_of(): return lax.all_to_all(weight, 'gx', split_axis=1, concat_axis=0, tiled=True)]
    all_to_all x0 -> x4, starting transfers between devices: none -> 19.3 us  [columns_of(): return lax.all_to_all(weight, 'gx', split_axis=1, concat_axis=0, tiled=True)]
  transfers between devices with their start and end apart: 11 -> 20, of which waited for: 11 -> 11; matrix products, arithmetic and copies ran while one was open for 7% -> 27% of each run, Pallas kernels for 0% -> 0%
where the time goes in v1:
time: 696 us; the launch traced here: 688 us
  waiting for transfers between devices  399 us (57%)
  matrix products  140 us (20%)
  local copies, waits for them, and re-layouts  68.9 us (10%)
  starting transfers between devices  36.1 us (5%)
  other arithmetic  18.8 us (3%)
  between operations  14.6 us (2%)
  blocking collectives  10.8 us (2%)
    all_to_all x4, waiting for transfers between devices, columns_of(): return lax.all_to_all(weight, 'gx', split_axis=1, concat_axis=0, tiled=True)  177 us
    reduce_scatter x2, waiting for transfers between devices, spread_rows(): lax.psum_scatter(mine, ('gx', 'gy'), scatter_dimension=0, tiled=True)  116 us
    dot_general x12, matrix products, back_dot(): lax.dot_general(left, right, (((1,), (1,)), ((), ())), preferred_element_...  78.3 us
    ppermute x6, waiting for transfers between devices, sum_gz(): got = lax.ppermute(term(other).astype(jnp.bfloat16), 'gz', swap_z)  54.8 us
    dot_general x12, matrix products, dot(): return jnp.dot(left, right, preferred_element_type=jnp.float32)  53.8 us
    ppermute x6, waiting for transfers between devices, from_pair(): return lax.ppermute(block, 'gz', swap_z)  49.9 us
    unnamed x84, local copies, waits for them, and re-layouts  29.7 us
    all_to_all x4, local copies, waits for them, and re-layouts, columns_of(): return lax.all_to_all(weight, 'gx', split_axis=1, concat_axis=0, tiled=True)  25.5 us
  transfers between devices with their start and end apart: 20, of which 11 were waited for; matrix products, arithmetic and copies ran while one was open for 27% of the time, Pallas kernels for 0%

profile of v1, /device:TPU:0, one launch (start us, length us, event | category | flops | bytes accessed | tf_op | source)
XLA Modules:
  0.0 688.4 jit_solution(13544303565581133276)
XLA Ops:
  8.6 5.9 all-reduce.1
  17.0 4.3 copy.108
  21.2 4.5 all-to-all-start.1
  25.8 4.3 copy.115
  30.1 34.0 %all-to-all-done.1 = bf16[768,4,384]{0,2,1:T(8,128)(2,1)} async-done(((bf16[768,4,384]{0,2,1:T(8,128)(2,1)}), bf16[768,4,384]{0,2,1:T(8,128)(2,1)}, u32[]{:S(2)}, u32[]{:S(2)}) %all-to-all-start.1) | async-done | bytes 2359328 | tf_op jit(solution)/shard_map/all_to_all | solution.py:93
  64.1 4.5 all-to-all-start.2
  69.4 4.3 copy.105
  73.7 27.0 %all-to-all-done.2 = bf16[768,4,384]{0,2,1:T(8,128)(2,1)} async-done(((bf16[768,4,384]{0,2,1:T(8,128)(2,1)}), bf16[768,4,384]{0,2,1:T(8,128)(2,1)}, u32[]{:S(2)}, u32[]{:S(2)}) %all-to-all-start.2) | async-done | bytes 2359328 | tf_op jit(solution)/shard_map/all_to_all | solution.py:93
  100.7 4.5 all-to-all-start
  105.2 12.6 %copy.127 = bf16[768,6144]{0,1:T(8,128)(2,1)} copy(bf16[768,6144]{1,0:T(8,128)(2,1)} %param.13) | data formatting | bytes 18874368 | tf_op args[5]
  117.8 25.1 %all-to-all-done = bf16[768,4,384]{0,2,1:T(8,128)(2,1)} async-done(((bf16[768,4,384]{0,2,1:T(8,128)(2,1)}), bf16[768,4,384]{0,2,1:T(8,128)(2,1)}, u32[]{:S(2)}, u32[]{:S(2)}) %all-to-all-start) | async-done | bytes 2359328 | tf_op jit(solution)/shard_map/all_to_all | solution.py:93
  142.9 5.8 all-to-all-start.3
  148.7 4.3 copy.109
  153.0 4.3 copy.116
  157.3 4.3 copy.106
  161.6 91.4 %all-to-all-done.3 = bf16[768,4,1536]{0,2,1:T(8,128)(2,1)} async-done(((bf16[768,4,1536]{0,2,1:T(8,128)(2,1)}), bf16[768,4,1536]{0,2,1:T(8,128)(2,1)}, u32[]{:S(2)}, u32[]{:S(2)}) %all-to-all-start.3) | async-done | bytes 9437216 | tf_op jit(solution)/shard_map/all_to_all | solution.py:93
  253.0 12.6 %copy.128 = bf16[4,768,1536]{2,1,0:T(8,128)(2,1)} copy(bf16[4,768,1536]{1,2,0:T(8,128)(2,1)} %bitcast.11) | data formatting | bytes 18874368 | tf_op jit(solution)/shard_map/all_to_all | solution.py:93
  265.6 10.3 %convolution_convert_fusion.1 = bf16[512,1536]{1,0:T(8,128)(2,1)} fusion(bf16[3072,1536]{1,0:T(8,128)(2,1)} %bitcast.96, bf16[1024,3072]{1,0:T(8,128)(2,1)} %all-gather.3.cloned.1.call-done, s32[]{:T(128)S(6)} %select_n.30), kind=kOutput, calls=%fused_computation.22 | convolution fusion | flops 4832624640 | bytes 14155780 | tf_op jit(solution)/shard_map/dot_general | solution.py:50
  278.0 10.7 %convolution_convert_fusion = bf16[512,1536]{1,0:T(8,128)(2,1)} fusion(bf16[1536,3072]{1,0:T(8,128)(2,1)} %param.15, bf16[1024,3072]{1,0:T(8,128)(2,1)} %all-gather.5.cloned.1.call-done, s32[]{:T(128)S(6)} %select_n.30), kind=kOutput, calls=%fused_computation.21 | convolution fusion | flops 4832624640 | bytes 14155780 | tf_op jit(solution)/shard_map/dot_general | solution.py:54
  292.6 2.5 fusion.45
  295.2 2.6 fusion.48
  299.8 2.6 fusion.39
  302.3 53.2 %collective-permute-done.1 = bf16[512,384]{1,0:T(8,128)(2,1)S(1)} collective-permute-done((bf16[512,384]{1,0:T(8,128)(2,1)S(1)}, bf16[512,384]{1,0:T(8,128)(2,1)S(1)}, u32[]{:S(2)}, u32[]{:S(2)}) %collective-permute-start.1) | collective-permute-done | bytes 393248 | tf_op jit(solution)/shard_map/ppermute | solution.py:77
  364.1 5.3 convert_add_fusion.2
  369.4 2.3 copy.117
  376.2 4.2 add_convert_fusion.7
  382.5 2.9 fusion.101
  386.6 4.5 add_convert_fusion.8
  408.2 13.1 %collective-permute-done.10 = bf16[512,384]{0,1:T(8,128)(2,1)S(1)} collective-permute-done((bf16[512,384]{0,1:T(8,128)(2,1)S(1)}, bf16[512,384]{0,1:T(8,128)(2,1)S(1)}, u32[]{:S(2)}, u32[]{:S(2)}) %collective-permute-start.10) | collective-permute-done | bytes 393248 | tf_op jit(solution)/shard_map/ppermute | solution.py:81
  421.3 4.5 fusion.109
  425.8 4.7 fusion.107
  430.4 4.7 fusion.108
  435.1 7.9 %multiply_convert_fusion = (bf16[512,1536]{1,0:T(8,128)(2,1)}, f32[512,1536]{1,0:T(8,128)S(1)}) fusion(bf16[512,1536]{1,0:T(8,128)(2,1)} %collective-permute-done.3, bf16[3072,1536]{1,0:T(8,128)(2,1)S(1)} %bitcast.101, bf16[1024,3072]{1,0:T(8,128)(2,1)} %all-gather.3.cloned.1.call-done, s32[]{:T(128)S(6)} %select_n.29), kind=kOutput, calls=%fused_computation.14 | convolution fusion | flops 4837343232 | bytes 18874372 | tf_op jit(solution)/shard_map/dot_general | solution.py:50
  443.1 9.8 %fusion.5 = bf16[512,1536]{1,0:T(8,128)(2,1)S(1)} fusion(f32[512,1536]{1,0:T(8,128)S(1)} %get-tuple-element.27, bf16[512,1536]{1,0:T(8,128)(2,1)} %collective-permute-done.7, bf16[1536,3072]{1,0:T(8,128)(2,1)} %param.15, bf16[1024,3072]{1,0:T(8,128)(2,1)} %all-gather.5.cloned.1.call-done, s32[]{:T(128)S(6)} %select_n.29), kind=kOutput, calls=%fused_computation.12 | convolution fusion | flops 4842848256 | bytes 18874372 | tf_op jit(solution)/shard_map/dot_general | solution.py:54
  454.9 10.6 %fusion.106 = f32[512,3072]{1,0:T(8,128)} fusion(bf16[512,1536]{1,0:T(8,128)(2,1)S(1)} %fusion.5, bf16[3072,1536]{1,0:T(8,128)(2,1)} %bitcast.97), kind=kOutput, calls=%fused_computation.144 | convolution fusion | flops 4831838208 | bytes 17301504 | tf_op jit(solution)/shard_map/dot_general | solution.py:54
  465.6 6.8 add_convert_fusion.1
  472.3 11.0 %collective-permute-done.11 = bf16[512,1536]{1,0:T(8,128)(2,1)} collective-permute-done((bf16[512,1536]{1,0:T(8,128)(2,1)S(1)}, bf16[512,1536]{1,0:T(8,128)(2,1)}, u32[]{:S(2)}, u32[]{:S(2)}) %collective-permute-start.11) | collective-permute-done | bytes 1572896 | tf_op jit(solution)/shard_map/ppermute | solution.py:81
  483.3 16.2 %broadcast_select_fusion.1 = (bf16[512,3072]{1,0:T(8,128)(2,1)}, bf16[512,3072]{1,0:T(8,128)(2,1)}) fusion(bf16[512,3072]{1,0:T(8,128)(2,1)} %add_convert_fusion.1, pred[]{:T(512)S(6)} %eq.2, f32[512,3072]{1,0:T(8,128)} %fusion.109, f32[512,3072]{1,0:T(8,128)} %fusion.107, f32[512,3072]{1,0:T(8,128)} %fusion.108, ...), kind=kOutput, calls=%fused_computation.18 | convolution fusion | flops 4839702528 | bytes 39321600 | tf_op jit(solution)/shard_map/dot_general | solution.py:54
  499.5 2.4 broadcast_select_fusion
  502.3 3.1 pad_maximum_fusion.1
  510.9 7.9 %fusion.102 = f32[512,3072]{1,0:T(8,128)S(1)} fusion(bf16[512,1536]{1,0:T(8,128)(2,1)S(1)} %copy-done.29, bf16[1536,3072]{1,0:T(8,128)(2,1)} %param.15), kind=kOutput, calls=%fused_computation.140 | convolution fusion | flops 4831838208 | bytes 17301504 | tf_op jit(solution)/shard_map/dot_general | solution.py:50
  520.8 25.9 %collective-permute-done.5 = bf16[512,1536]{1,0:T(8,128)(2,1)S(1)} collective-permute-done((bf16[512,1536]{1,0:T(8,128)(2,1)S(1)}, bf16[512,1536]{1,0:T(8,128)(2,1)S(1)}, u32[]{:S(2)}, u32[]{:S(2)}) %collective-permute-start.5) | collective-permute-done | bytes 1572896 | tf_op jit(solution)/shard_map/ppermute | solution.py:81
  546.6 5.0 fusion.103
  553.8 3.1 pad_maximum_fusion
  556.9 33.5 %reduce-scatter.5.cloned.1.call-done = bf16[64,3072]{1,0:T(8,128)(2,1)} async-done(((bf16[1024,3072]{1,0:T(8,128)(2,1)}), bf16[64,3072]{1,0:T(8,128)(2,1)}) %reduce-scatter.5.cloned.1.call-update) | async-done | bytes 393232 | tf_op jit(solution)/shard_map/reduce_scatter | solution.py:88
  591.8 4.9 all-reduce
  596.7 82.6 %reduce-scatter.3.cloned.1.call-done = bf16[64,3072]{1,0:T(8,128)(2,1)} async-done(((bf16[1024,3072]{1,0:T(8,128)(2,1)}), bf16[64,3072]{1,0:T(8,128)(2,1)}) %reduce-scatter.3.cloned.1.call-update) | async-done | bytes 393232 | tf_op jit(solution)/shard_map/reduce_scatter | solution.py:88
  679.3 2.4 fusion.60
  (163 shorter events, 59.2 us)
Async XLA Ops:
  7.2 288.0 %copy-start = (bf16[384,3072]{1,0:T(8,128)(2,1)S(1)}, bf16[384,3072]{1,0:T(8,128)(2,1)}, u32[]{:S(2)}) copy-start(bf16[384,3072]{1,0:T(8,128)(2,1)} %param.14) | copy-start | bytes 7077892
  7.2 258.5 %all-gather.3.cloned.1.call-start = ((), (), s32[]{:S(2)}) async-start(), calls=%async_computation.6 | async-start | bytes 6684672 | tf_op jit(solution)/shard_map/all_gather | solution.py:101
  21.2 42.9 %all-to-all-start.1 = ((bf16[768,4,384]{0,2,1:T(8,128)(2,1)}), bf16[768,4,384]{0,2,1:T(8,128)(2,1)}, u32[]{:S(2)}, u32[]{:S(2)}) async-start(bf16[768,4,384]{0,2,1:T(8,128)(2,1)} %bitcast.104), calls=%async_computation.1 | async-start | bytes 4718592 | tf_op jit(solution)/shard_map/all_to_all | solution.py:93
  64.1 36.6 %all-to-all-start.2 = ((bf16[768,4,384]{0,2,1:T(8,128)(2,1)}), bf16[768,4,384]{0,2,1:T(8,128)(2,1)}, u32[]{:S(2)}, u32[]{:S(2)}) async-start(bf16[768,4,384]{0,2,1:T(8,128)(2,1)} %bitcast.102), calls=%async_computation.2 | async-start | bytes 4718592 | tf_op jit(solution)/shard_map/all_to_all | solution.py:93
  68.6 209.3 %all-gather.5.cloned.1.call-start = ((), (), s32[]{:S(2)}) async-start(), calls=%async_computation.8 | async-start | bytes 6684672 | tf_op jit(solution)/shard_map/all_gather | solution.py:102
  100.7 42.2 %all-to-all-start = ((bf16[768,4,384]{0,2,1:T(8,128)(2,1)}), bf16[768,4,384]{0,2,1:T(8,128)(2,1)}, u32[]{:S(2)}, u32[]{:S(2)}) async-start(bf16[768,4,384]{0,2,1:T(8,128)(2,1)} %bitcast.103), calls=%async_computation | async-start | bytes 4718592 | tf_op jit(solution)/shard_map/all_to_all | solution.py:93
  142.9 110.2 %all-to-all-start.3 = ((bf16[768,4,1536]{0,2,1:T(8,128)(2,1)}), bf16[768,4,1536]{0,2,1:T(8,128)(2,1)}, u32[]{:S(2)}, u32[]{:S(2)}) async-start(bf16[768,4,1536]{0,2,1:T(8,128)(2,1)} %bitcast.83), calls=%async_computation.3 | async-start | bytes 18874368 | tf_op jit(solution)/shard_map/all_to_all | solution.py:93
  148.6 441.8 %reduce-scatter.5.cloned.1.call-start = ((), (), s32[]{:S(2)}) async-start(), calls=%async_computation.9 | async-start | bytes 6684672 | tf_op jit(solution)/shard_map/reduce_scatter | solution.py:88
  275.9 159.2 %collective-permute-start.3 = (bf16[512,1536]{1,0:T(8,128)(2,1)}, bf16[512,1536]{1,0:T(8,128)(2,1)}, u32[]{:S(2)}, u32[]{:S(2)}) collective-permute-start(bf16[512,1536]{1,0:T(8,128)(2,1)} %convolution_convert_fusion.1), channel_id=1, source_target_pairs={{0,1},{1,0},{2,3},{3,2},{4,5},{5,4},{6,7},{7,6},{8,9},{9,8},{10,11... | collective-permute-start | bytes 4718600 | tf_op jit(solution)/shard_map/ppermute | solution.py:77
  278.0 10.8 %copy-start.8 = (bf16[4,768,384]{2,1,0:T(8,128)(2,1)S(1)}, bf16[4,768,384]{2,1,0:T(8,128)(2,1)}, u32[]{:S(2)}) copy-start(bf16[4,768,384]{2,1,0:T(8,128)(2,1)} %copy.109) | copy-start | bytes 7077892
  278.0 10.8 %copy-start.28 = (bf16[1024,3072]{1,0:T(8,128)(2,1)S(1)}, bf16[1024,3072]{1,0:T(8,128)(2,1)}, u32[]{:S(2)}) copy-start(bf16[1024,3072]{1,0:T(8,128)(2,1)} %all-gather.3.cloned.1.call-done) | copy-start | bytes 18874372
  288.6 154.4 %collective-permute-start.7 = (bf16[512,1536]{1,0:T(8,128)(2,1)}, bf16[512,1536]{1,0:T(8,128)(2,1)}, u32[]{:S(2)}, u32[]{:S(2)}) collective-permute-start(bf16[512,1536]{1,0:T(8,128)(2,1)} %convolution_convert_fusion), channel_id=1, source_target_pairs={{0,1},{1,0},{2,3},{3,2},{4,5},{5,4},{6,7},{7,6},{8,9},{9,8},{10,11... | collective-permute-start | bytes 4718600 | tf_op jit(solution)/shard_map/ppermute | solution.py:77
  288.7 3.9 copy-start.6
  288.7 6.4 slice-start.6
  290.5 4.6 slice-start.7
  290.6 65.0 %collective-permute-start.1 = (bf16[512,384]{1,0:T(8,128)(2,1)S(1)}, bf16[512,384]{1,0:T(8,128)(2,1)S(1)}, u32[]{:S(2)}, u32[]{:S(2)}) collective-permute-start(bf16[512,384]{1,0:T(8,128)(2,1)S(1)} %fusion.42), channel_id=1, source_target_pairs={{0,1},{1,0},{2,3},{3,2},{4,5},{5,4},{6,7},{7,6},{8,9},{9,8},{10,11... | collective-permute-start | bytes 1179656 | tf_op jit(solution)/shard_map/ppermute | solution.py:77
  295.1 4.6 copy-start.3
  295.1 68.9 %collective-permute-start.2 = (bf16[512,384]{1,0:T(8,128)(2,1)}, bf16[512,384]{1,0:T(8,128)(2,1)}, u32[]{:S(2)}, u32[]{:S(2)}) collective-permute-start(bf16[512,384]{1,0:T(8,128)(2,1)} %fusion.45), channel_id=1, source_target_pairs={{0,1},{1,0},{2,3},{3,2},{4,5},{5,4},{6,7},{7,6},{8,9},{9,8},{10,11... | collective-permute-start | bytes 1179656 | tf_op jit(solution)/shard_map/ppermute | solution.py:77
  297.8 78.5 %collective-permute-start.6 = (bf16[512,384]{1,0:T(8,128)(2,1)}, bf16[512,384]{1,0:T(8,128)(2,1)}, u32[]{:S(2)}, u32[]{:S(2)}) collective-permute-start(bf16[512,384]{1,0:T(8,128)(2,1)} %fusion.48), channel_id=1, source_target_pairs={{0,1},{1,0},{2,3},{3,2},{4,5},{5,4},{6,7},{7,6},{8,9},{9,8},{10,11... | collective-permute-start | bytes 1179656 | tf_op jit(solution)/shard_map/ppermute | solution.py:77
  355.5 31.1 %collective-permute-start = (bf16[512,384]{1,0:T(8,128)(2,1)}, bf16[512,384]{1,0:T(8,128)(2,1)}, u32[]{:S(2)}, u32[]{:S(2)}) collective-permute-start(bf16[512,384]{1,0:T(8,128)(2,1)} %fusion.39), channel_id=1, source_target_pairs={{0,1},{1,0},{2,3},{3,2},{4,5},{5,4},{6,7},{7,6},{8,9},{9,8},{10,11... | collective-permute-start | bytes 1179656 | tf_op jit(solution)/shard_map/ppermute | solution.py:77
  362.2 7.2 %copy-start.1 = (f32[2,256,3,128]{1,0,3,2:T(2,128)}, f32[2,256,3,128]{1,0,3,2:T(2,128)S(1)}, u32[]{:S(2)}) copy-start(f32[2,256,3,128]{1,0,3,2:T(2,128)S(1)} %reshape.102) | copy-start | bytes 2359300
  373.7 2.5 copy-start.17
  382.5 4.1 copy-start.4
  393.2 2.1 copy-start.2
  393.2 2.3 copy-start.10
  393.2 2.3 copy-start.15
  393.2 2.3 copy-start.22
  398.8 4.0 copy-start.18
  400.7 25.1 %collective-permute-start.8 = (bf16[512,384]{0,1:T(8,128)(2,1)S(1)}, bf16[512,384]{0,1:T(8,128)(2,1)S(1)}, u32[]{:S(2)}, u32[]{:S(2)}) collective-permute-start(bf16[512,384]{0,1:T(8,128)(2,1)S(1)} %bitcast.108), channel_id=1, source_target_pairs={{0,1},{1,0},{2,3},{3,2},{4,5},{5,4},{6,7},{7,6},{8,9},{9,8},{10,11... | collective-permute-start | bytes 1179656 | tf_op jit(solution)/shard_map/ppermute | solution.py:81
  404.2 17.1 %collective-permute-start.10 = (bf16[512,384]{0,1:T(8,128)(2,1)S(1)}, bf16[512,384]{0,1:T(8,128)(2,1)S(1)}, u32[]{:S(2)}, u32[]{:S(2)}) collective-permute-start(bf16[512,384]{0,1:T(8,128)(2,1)S(1)} %bitcast.117), channel_id=1, source_target_pairs={{0,1},{1,0},{2,3},{3,2},{4,5},{5,4},{6,7},{7,6},{8,9},{9,8},{10,11... | collective-permute-start | bytes 1179656 | tf_op jit(solution)/shard_map/ppermute | solution.py:81
  404.5 16.8 %copy-start.5 = (bf16[4,768,384]{2,1,0:T(8,128)(2,1)S(1)}, bf16[4,768,384]{2,1,0:T(8,128)(2,1)}, u32[]{:S(2)}) copy-start(bf16[4,768,384]{2,1,0:T(8,128)(2,1)} %copy.106) | copy-start | bytes 7077892
  406.4 24.0 %collective-permute-start.9 = (bf16[512,384]{0,1:T(8,128)(2,1)S(1)}, bf16[512,384]{0,1:T(8,128)(2,1)S(1)}, u32[]{:S(2)}, u32[]{:S(2)}) collective-permute-start(bf16[512,384]{0,1:T(8,128)(2,1)S(1)} %bitcast.110), channel_id=1, source_target_pairs={{0,1},{1,0},{2,3},{3,2},{4,5},{5,4},{6,7},{7,6},{8,9},{9,8},{10,11... | collective-permute-start | bytes 1179656 | tf_op jit(solution)/shard_map/ppermute | solution.py:81
  425.8 9.3 %slice-start = ((s8[9437184]{0:T(1024)(128)(4,1)}), s8[4194304]{0:T(1024)(128)(4,1)S(1)}, s32[]{:S(2)}) async-start(s8[9437184]{0:T(1024)(128)(4,1)} %bitcast.99), calls=%async_computation.10 | async-start | bytes 8388608
  425.8 9.3 %slice-start.1 = ((s8[9437184]{0:T(1024)(128)(4,1)}), s8[4194304]{0:T(1024)(128)(4,1)S(1)}, s32[]{:S(2)}) async-start(s8[9437184]{0:T(1024)(128)(4,1)} %bitcast.99), calls=%async_computation.11 | async-start | bytes 8388608
  430.4 4.7 slice-start.2
  452.9 30.4 %collective-permute-start.11 = (bf16[512,1536]{1,0:T(8,128)(2,1)S(1)}, bf16[512,1536]{1,0:T(8,128)(2,1)}, u32[]{:S(2)}, u32[]{:S(2)}) collective-permute-start(bf16[512,1536]{1,0:T(8,128)(2,1)S(1)} %fusion.5), channel_id=1, source_target_pairs={{0,1},{1,0},{2,3},{3,2},{4,5},{5,4},{6,7},{7,6},{8,9},{9,8},{10,11... | collective-permute-start | bytes 4718600 | tf_op jit(solution)/shard_map/ppermute | solution.py:81
  499.5 2.8 copy-start.12
  505.4 173.9 %reduce-scatter.3.cloned.1.call-start = ((), (), s32[]{:S(2)}) async-start(), calls=%async_computation.7 | async-start | bytes 6684672 | tf_op jit(solution)/shard_map/reduce_scatter | solution.py:88
  506.4 2.4 copy-start.29
  506.4 40.2 %slice-start.3 = ((s8[9437184]{0:T(1024)(128)(4,1)}), s8[4194304]{0:T(1024)(128)(4,1)S(1)}, s32[]{:S(2)}) async-start(s8[9437184]{0:T(1024)(128)(4,1)} %bitcast.119), calls=%async_computation.13 | async-start | bytes 8388608
  508.8 42.9 %collective-permute-start.4 = (bf16[512,384]{0,1:T(8,128)(2,1)S(1)}, bf16[512,384]{0,1:T(8,128)(2,1)S(1)}, u32[]{:S(2)}, u32[]{:S(2)}) collective-permute-start(bf16[512,384]{0,1:T(8,128)(2,1)S(1)} %bitcast.105), channel_id=1, source_target_pairs={{0,1},{1,0},{2,3},{3,2},{4,5},{5,4},{6,7},{7,6},{8,9},{9,8},{10,11... | collective-permute-start | bytes 1179656 | tf_op jit(solution)/shard_map/ppermute | solution.py:81
  508.9 37.7 %slice-start.4 = ((s8[9437184]{0:T(1024)(128)(4,1)}), s8[4194304]{0:T(1024)(128)(4,1)S(1)}, s32[]{:S(2)}) async-start(s8[9437184]{0:T(1024)(128)(4,1)} %bitcast.119), calls=%async_computation.14 | async-start | bytes 8388608
  508.9 37.7 %slice-start.5 = ((s8[9437184]{0:T(1024)(128)(4,1)}), s8[1048576]{0:T(1024)(128)(4,1)S(1)}, s32[]{:S(2)}) async-start(s8[9437184]{0:T(1024)(128)(4,1)} %bitcast.119), calls=%async_computation.15 | async-start | bytes 2097152
  508.9 37.7 %collective-permute-start.5 = (bf16[512,1536]{1,0:T(8,128)(2,1)S(1)}, bf16[512,1536]{1,0:T(8,128)(2,1)S(1)}, u32[]{:S(2)}, u32[]{:S(2)}) collective-permute-start(bf16[512,1536]{1,0:T(8,128)(2,1)S(1)} %copy-done.29), channel_id=1, source_target_pairs={{0,1},{1,0},{2,3},{3,2},{4,5},{5,4},{6,7},{7,6},{8,9},{9,8},{10,11... | collective-permute-start | bytes 4718600 | tf_op jit(solution)/shard_map/ppermute | solution.py:81
  556.9 33.6 %copy-start.11 = (bf16[64,3072]{1,0:T(8,128)(2,1)S(1)}, bf16[64,3072]{1,0:T(8,128)(2,1)}, u32[]{:S(2)}) copy-start(bf16[64,3072]{1,0:T(8,128)(2,1)} %param.8) | copy-start | bytes 1179652
  556.9 33.6 %copy-start.25 = (f32[64]{0:T(128)S(1)}, f32[64]{0:T(128)}, u32[]{:S(2)}) copy-start(f32[64]{0:T(128)} %copy-done.24) | copy-start | bytes 772
  556.9 33.6 %copy-start.27 = (f32[64]{0:T(128)S(1)}, f32[64]{0:T(128)}, u32[]{:S(2)}) copy-start(f32[64]{0:T(128)} %copy-done.26) | copy-start | bytes 772
  556.9 122.4 %copy-start.14 = (bf16[64,3072]{1,0:T(8,128)(2,1)S(1)}, bf16[64,3072]{1,0:T(8,128)(2,1)}, u32[]{:S(2)}) copy-start(bf16[64,3072]{1,0:T(8,128)(2,1)} %param.9) | copy-start | bytes 1179652
  (10 other events, 9.1 us)
Sparse Core Ops, SparseCore 0:
  17.1 75.8 all-gather.2
  95.2 69.7 all-gather.4
  505.5 84.8 reduce-scatter.4
  594.7 84.5 reduce-scatter.2

commit v2 on v0

v2 whole, which is shorter than its diff:
```python
import functools
import math

import jax
import jax.numpy as jnp
from jax import lax
from jax.experimental import pallas as pl
from jax.experimental.pallas import tpu as pltpu
from jax.sharding import PartitionSpec as P

D = 6144
HEAD_DIM = 128
IMG_TOK = 256


EPSILON = 1e-06
ROOT_HALF = 0.7071067811865476
ROOT_TWO_PI_INV = 0.3989422804014327


def attend_kernel(
    q_own, q_got, k_own, k_got, v_own, v_got, g_own, g_got, mixed_ref, dq_ref, dk_ref, dv_ref, *, scale
):
    def total(own, got):
        return own[...].astype(jnp.float32) + got[...].astype(jnp.float32)

    def norm(values):
        center = values - jnp.mean(values, axis=-1, keepdims=True)
        spread = jnp.mean(center * center, axis=-1, keepdims=True)
        inverse = lax.rsqrt(spread + EPSILON)
        return center * inverse, inverse

    def norm_back(grad, normed, inverse):
        slope = inverse * (grad - normed * jnp.mean(grad * normed, axis=-1, keepdims=True))
        return (slope - jnp.mean(slope, axis=-1, keepdims=True)).astype(jnp.bfloat16)

    def contract(left, right, left_dim, right_dim):
        return lax.dot_general(
            left,
            right,
            (((left_dim,), (right_dim,)), ((), ())),
            preferred_element_type=jnp.float32,
        )

    def half(values):
        return values.astype(jnp.bfloat16)

    q_norm, q_inverse = norm(total(q_own, q_got))
    k_norm, k_inverse = norm(total(k_own, k_got))
    q_half, k_half = half(q_norm), half(k_norm)
    v_half = half(total(v_own, v_got))
    grad = half(total(g_own, g_got))
    weights = jnp.exp(contract(q_half, k_half, 1, 1) * scale)
    probs = weights / jnp.sum(weights, axis=-1, keepdims=True)
    probs_half = half(probs)
    mixed_ref[...] = half(contract(probs_half, v_half, 1, 0))
    dv_ref[...] = half(contract(probs_half, grad, 0, 0))
    probs_grad = half(contract(grad, v_half, 1, 1)).astype(jnp.float32)
    inner = jnp.sum(probs_grad * probs, axis=-1, keepdims=True)
    score_grad = half(probs * (probs_grad - inner) * scale)
    q_grad = half(contract(score_grad, k_half, 1, 0)).astype(jnp.float32)
    k_grad = half(contract(score_grad, q_half, 0, 0)).astype(jnp.float32)
    dq_ref[...] = norm_back(q_grad, q_norm, q_inverse)
    dk_ref[...] = norm_back(k_grad, k_norm, k_inverse)


def attend(own, got, grad_own, grad_got):
    rows, width = grad_own.shape
    heads = width // HEAD_DIM

    def block(part):
        return pl.BlockSpec((IMG_TOK, HEAD_DIM), lambda image, head: (image, part * heads + head))

    half = jax.ShapeDtypeStruct((rows, width), jnp.bfloat16)
    return pl.pallas_call(
        functools.partial(attend_kernel, scale=1.0 / math.sqrt(HEAD_DIM)),
        grid=(rows // IMG_TOK, heads),
        in_specs=[block(0), block(0), block(1), block(1), block(2), block(2), block(0), block(0)],
        out_specs=[block(0)] * 4,
        out_shape=[half] * 4,
        compiler_params=pltpu.CompilerParams(vmem_limit_bytes=32 * 1024 * 1024),
        cost_estimate=pl.CostEstimate(
            flops=12 * rows * IMG_TOK * width,
            bytes_accessed=24 * rows * width,
            transcendentals=rows * IMG_TOK * heads,
        ),
        name="attend",
    )(own, got, own, got, own, got, grad_own, grad_got)


def gelu(pre):
    return pre * 0.5 * (1.0 + lax.erf(pre * ROOT_HALF))


def gelu_back(pre, grad_half):
    cdf = 0.5 * (1.0 + lax.erf(pre * ROOT_HALF))
    pdf = jnp.exp(-0.5 * pre * pre) * ROOT_TWO_PI_INV
    return (grad_half.astype(jnp.float32) * (cdf + pre * pdf)).astype(jnp.bfloat16)


def dot(left, right):
    return jnp.dot(left, right, preferred_element_type=jnp.float32)


def back_dot(left, right):
    return lax.dot_general(
        left, right, (((1,), (1,)), ((), ())), preferred_element_type=jnp.float32
    )


def half(values):
    return values.astype(jnp.bfloat16)


def wide_sum(own, got):
    return own.astype(jnp.float32) + got.astype(jnp.float32)


def trade(block, axis, bit):
    pairs = [(index, index ^ bit) for index in range(lax.axis_size(axis))]
    return lax.ppermute(block, axis, pairs)


def body(layer_input, out_cotangent, w_query, w_key, w_value, w_mlp_in, w_attn_out, w_mlp_out):
    n_gx, n_gy, n_gz = (lax.axis_size(name) for name in ("gx", "gy", "gz"))
    me_x, me_y = lax.axis_index("gx"), lax.axis_index("gy")
    own_rows = layer_input.shape[0]
    image_rows = own_rows * n_gy
    order = (3, 1, 2, 0)

    def all_rows(block):
        gathered = lax.all_gather(block, ("gx", "gy"), axis=0, tiled=True)
        return jnp.concatenate(
            [
                lax.dynamic_slice_in_dim(gathered, (me_x ^ bit) * image_rows, image_rows, 0)
                for bit in order
            ],
            axis=0,
        )

    def others(part):
        if n_gz == 2:
            return trade(part, "gz", 1)
        return half(lax.psum(part.astype(jnp.float32), "gz") - part.astype(jnp.float32))

    def by_owner(weight):
        rows, columns = weight.shape
        return weight.reshape(rows, n_gx, columns // n_gx).transpose(1, 0, 2)

    def swap(weight):
        swapped = lax.all_to_all(weight, "gx", split_axis=0, concat_axis=0, tiled=True)
        return swapped.reshape(n_gx * weight.shape[1], weight.shape[2])

    def after(value, earlier):
        return lax.optimization_barrier((value, earlier))

    wide = layer_input.astype(jnp.float32)
    total, squares = lax.psum((jnp.sum(wide, axis=1), jnp.sum(wide * wide, axis=1)), "gz")
    center = total / D
    spread = squares / D - center * center
    inverse = lax.rsqrt(spread + EPSILON)
    normed = (wide - center[:, None]) * inverse[:, None]
    gathered_in = all_rows(half(normed))

    heads_in = jnp.concatenate([by_owner(w) for w in (w_query, w_key, w_value)], axis=2)
    mlp_in = by_owner(w_mlp_in)
    cut = mlp_in.shape[2] // 2
    in_heads = swap(heads_in)
    first_mlp, in_heads = after(mlp_in[:, :, :cut], in_heads)
    in_first = swap(first_mlp)
    second_mlp, in_first = after(mlp_in[:, :, cut:], in_first)
    in_second = swap(second_mlp)

    heads_own = half(dot(gathered_in, in_heads))
    heads_got = others(heads_own)
    first_own = half(dot(gathered_in, in_first))
    first_got = others(first_own)

    gathered_cot = all_rows(out_cotangent)
    mixed_own = half(back_dot(gathered_cot, w_attn_out))
    mixed_got = others(mixed_own)
    second_own = half(dot(gathered_in, in_second))
    second_got = others(second_own)

    mixed, query_grad, key_grad, value_grad = attend(heads_own, heads_got, mixed_own, mixed_got)
    pre_first, pre_second = wide_sum(first_own, first_got), wide_sum(second_own, second_got)
    act_first, act_second = half(gelu(pre_first)), half(gelu(pre_second))
    heads_grad = jnp.concatenate([query_grad, key_grad, value_grad], axis=1)

    def block_of(value, start, count):
        return lax.slice_in_dim(value, start * image_rows, (start + count) * image_rows)

    def forward_term(start, count):
        result = dot(block_of(mixed, start, count), w_attn_out)
        result = result + dot(block_of(act_first, start, count), w_mlp_out[:cut])
        return result + dot(block_of(act_second, start, count), w_mlp_out[cut:])

    def backward_term(start, count):
        act_own = half(back_dot(block_of(gathered_cot, start, count), w_mlp_out))
        grad = half(wide_sum(act_own, others(act_own)))
        first = gelu_back(block_of(pre_first, start, count), grad[:, :cut])
        second = gelu_back(block_of(pre_second, start, count), grad[:, cut:])
        result = back_dot(block_of(heads_grad, start, count), in_heads)
        result = result + back_dot(first, in_first)
        return result + back_dot(second, in_second)

    def keep_and_send(value, sent_first):
        count = value.shape[0] // 2
        low, high = value[:count], value[count:]
        return jnp.where(sent_first, high, low), jnp.where(sent_first, low, high)

    def spread_rows(term):
        from_core = trade(half(term(0, 2)), "gx", 1)
        to_x = half(term(2, 1) + from_core[:image_rows].astype(jnp.float32))
        from_x = trade(to_x, "gx", 2)
        mine = wide_sum(from_core[image_rows:], from_x) + term(3, 1)
        quarters = mine.reshape(2, 2, own_rows, mine.shape[1])
        odd = me_y % 2 == 1
        kept = jnp.where(odd, quarters[:, 1], quarters[:, 0])
        sent = jnp.where(odd, quarters[:, 0], quarters[:, 1])
        pair = kept + trade(half(sent), "gy", 1).astype(jnp.float32)
        high = me_y >= 2
        kept = jnp.where(high, pair[1], pair[0])
        sent = jnp.where(high, pair[0], pair[1])
        return kept + trade(half(sent), "gy", 2).astype(jnp.float32)

    layer_out = half(wide + spread_rows(forward_term))
    normed_grad = spread_rows(backward_term)
    first, second = lax.psum(
        (jnp.sum(normed_grad, axis=1), jnp.sum(normed_grad * normed, axis=1)), "gz"
    )
    grad_full = out_cotangent.astype(jnp.float32) + inverse[:, None] * (
        normed_grad - (first / D)[:, None] - normed * (second / D)[:, None]
    )
    return (layer_out, half(grad_full))


def solution(mesh):
    in_specs = (
        P(("gx", "gy"), "gz"),
        P(("gx", "gy"), "gz"),
        P(("gz", "gx"), "gy"),
        P(("gz", "gx"), "gy"),
        P(("gz", "gx"), "gy"),
        P(("gz", "gx"), "gy"),
        P(("gy", "gx"), "gz"),
        P(("gy", "gx"), "gz"),
    )
    out_specs = (P(("gx", "gy"), "gz"), P(("gx", "gy"), "gz"))
    return jax.shard_map(body, mesh=mesh, in_specs=in_specs, out_specs=out_specs, check_vma=False)
```

time: 1190 us -> 668 us (0.56)
  waiting for transfers between devices: 1000 us -> 341 us
  local copies, waits for them, and re-layouts: 6.25 us -> 69.2 us
  starting transfers between devices: 0.6 us -> 37.3 us
  Pallas kernels: 0 us -> 15.4 us
  other arithmetic: 9.15 us -> 23.7 us
  matrix products: 138 us -> 150 us
    all_gather x8 -> x2, waiting for transfers between devices: 738 us -> 0.02 us  [all_rows(): gathered = lax.all_gather(block, ('gx', 'gy'), axis=0, tiled=True)]
    psum x1 -> x0, waiting for transfers between devices: 223 us -> none  [body(): lax.psum(project(rows_value).astype(jnp.bfloat16), 'gz').astype(jnp.float32)]
    ppermute x0 -> x15, waiting for transfers between devices: none -> 198 us  [trade(): return lax.ppermute(block, axis, pairs)]
    all_to_all x0 -> x3, waiting for transfers between devices: none -> 143 us  [swap(): lax.all_to_all(weight, 'gx', split_axis=0, concat_axis=0, tiled=True)]
    reduce_scatter x2 -> x0, waiting for transfers between devices: 37.7 us -> none  [spread_rows(): lax.psum_scatter(term(jnp.int32(0), rows * lax.axis_size('gy')).astype(jn...]
    unnamed x28 -> x104, local copies, waits for them, and re-layouts: 1.09 us -> 29.4 us
    all_to_all x0 -> x3, local copies, waits for them, and re-layouts: none -> 24 us  [swap(): lax.all_to_all(weight, 'gx', split_axis=0, concat_axis=0, tiled=True)]
    ppermute x0 -> x15, starting transfers between devices: none -> 21.6 us  [trade(): return lax.ppermute(block, axis, pairs)]
  transfers between devices with their start and end apart: 11 -> 20, of which waited for: 11 -> 10; matrix products, arithmetic and copies ran while one was open for 7% -> 33% of each run, Pallas kernels for 0% -> 0%
where the time goes in v2:
time: 668 us; the launch traced here: 663 us
  waiting for transfers between devices  341 us (51%)
  matrix products  150 us (22%)
  local copies, waits for them, and re-layouts  69.2 us (10%)
  starting transfers between devices  37.3 us (6%)
  other arithmetic  23.7 us (4%)
  Pallas kernels  15.4 us (2%)
  between operations  15.2 us (2%)
  blocking collectives  11.3 us (2%)
    ppermute x15, waiting for transfers between devices, trade(): return lax.ppermute(block, axis, pairs)  198 us
    all_to_all x3, waiting for transfers between devices, swap(): lax.all_to_all(weight, 'gx', split_axis=0, concat_axis=0, tiled=True)  143 us
    dot_general x12, matrix products, dot(): return jnp.dot(left, right, preferred_element_type=jnp.float32)  81.9 us
    dot_general x13, matrix products, back_dot(): lax.dot_general(left, right, (((1,), (1,)), ((), ())), preferred_element_...  67.6 us
    unnamed x104, local copies, waits for them, and re-layouts  29.4 us
    all_to_all x3, local copies, waits for them, and re-layouts, swap(): lax.all_to_all(weight, 'gx', split_axis=0, concat_axis=0, tiled=True)  24 us
    ppermute x15, starting transfers between devices, trade(): return lax.ppermute(block, axis, pairs)  21.6 us
    all_to_all x3, starting transfers between devices, swap(): lax.all_to_all(weight, 'gx', split_axis=0, concat_axis=0, tiled=True)  15.7 us
  transfers between devices with their start and end apart: 20, of which 10 were waited for; matrix products, arithmetic and copies ran while one was open for 33% of the time, Pallas kernels for 0%

profile of v2, /device:TPU:0, one launch (start us, length us, event | category | flops | bytes accessed | tf_op | source)
XLA Modules:
  0.0 662.9 jit_solution(6057603666074921737)
XLA Ops:
  8.6 5.9 all-reduce.1
  17.7 4.3 copy.19
  22.0 4.3 copy.20
  26.3 4.3 copy.21
  30.6 6.2 pad_maximum_fusion
  36.9 5.4 all-to-all-start
  42.3 12.5 %copy.18 = bf16[768,6144]{0,1:T(8,128)(2,1)} copy(bf16[768,6144]{1,0:T(8,128)(2,1)} %param.13) | data formatting | bytes 18874368 | tf_op args[5]
  54.8 8.0 %fusion.182 = (bf16[4,768,768]{1,2,0:T(8,128)(2,1)}, bf16[4,768,768]{1,2,0:T(8,128)(2,1)}) fusion(bf16[4,768,1536]{1,2,0:T(8,128)(2,1)} %bitcast.113), kind=kLoop, calls=%fused_computation.228 | loop fusion | bytes 18874368 | tf_op jit(solution)/shard_map/slice | solution.py:169
  62.8 89.0 %all-to-all-done = bf16[4,768,1152]{1,2,0:T(8,128)(2,1)} async-done(((bf16[4,768,1152]{1,2,0:T(8,128)(2,1)}), bf16[4,768,1152]{1,2,0:T(8,128)(2,1)}, u32[]{:S(2)}, u32[]{:S(2)}) %all-to-all-start) | async-done | bytes 7077920 | tf_op jit(solution)/shard_map/all_to_all | solution.py:151
  151.8 10.6 %copy.22 = bf16[4,768,1152]{2,1,0:T(8,128)(2,1)} copy(bf16[4,768,1152]{1,2,0:T(8,128)(2,1)} %all-to-all-done) | data formatting | bytes 14155776 | tf_op jit(solution)/shard_map/all_to_all | solution.py:151
  162.4 5.0 all-to-all-start.1
  167.4 53.8 %all-to-all-done.1 = bf16[4,768,768]{1,2,0:T(8,128)(2,1)} async-done(((bf16[4,768,768]{1,2,0:T(8,128)(2,1)}), bf16[4,768,768]{1,2,0:T(8,128)(2,1)}, u32[]{:S(2)}, u32[]{:S(2)}) %all-to-all-start.1) | async-done | bytes 4718624 | tf_op jit(solution)/shard_map/all_to_all | solution.py:151
  221.3 6.6 %copy.23 = bf16[4,768,768]{2,1,0:T(8,128)(2,1)} copy(bf16[4,768,768]{1,2,0:T(8,128)(2,1)} %all-to-all-done.1) | data formatting | bytes 9437184 | tf_op jit(solution)/shard_map/all_to_all | solution.py:151
  227.9 5.2 all-to-all-start.2
  233.2 3.3 constant_dynamic-slice_fusion.7
  236.5 18.1 %convolution_convert_fusion.q_own.k_own.v_own = bf16[1024,1152]{1,0:T(8,128)(2,1)} fusion(bf16[3072,1152]{1,0:T(8,128)(2,1)} %bitcast.89, bf16[256,3072]{1,0:T(8,128)(2,1)S(1)} %get-tuple-element.34, bf16[256,3072]{1,0:T(8,128)(2,1)S(1)} %get-tuple-element.35, bf16[256,3072]{1,0:T(8,128)(2,1)S(1)} %get-tuple-element.36, ...), kind=kOutput, calls=%fused_computation.22 | convolution fusion | flops 7274102784 | bytes 15728640 | tf_op jit(solution)/shard_map/dot_general | solution.py:102
  257.3 3.4 constant_dynamic-slice_fusion.3
  260.8 3.4 fusion.43.g_own
  264.4 10.0 %convolution_convert_fusion.4 = bf16[1024,768]{1,0:T(8,128)(2,1)} fusion(bf16[3072,768]{1,0:T(8,128)(2,1)S(1)} %bitcast.97, bf16[256,3072]{1,0:T(8,128)(2,1)S(1)} %copy-done.20, bf16[256,3072]{1,0:T(8,128)(2,1)S(1)} %copy-done.22, bf16[256,3072]{1,0:T(8,128)(2,1)S(1)} %copy-done.24, bf16[256,3072]{1,0:T(8,128)(2,1)S(1)} %copy-done.18), kind=kOutput, calls=%fused_computation.53 | convolution fusion | flops 4857790464 | bytes 12582912 | tf_op jit(solution)/shard_map/dot_general | solution.py:102
  276.3 7.3 %convolution_convert_fusion.1 = bf16[256,1536]{1,0:T(8,128)(2,1)} fusion(bf16[256,3072]{1,0:T(8,128)(2,1)S(1)} %get-tuple-element.30, bf16[1536,3072]{1,0:T(8,128)(2,1)} %param.15), kind=kOutput, calls=%fused_computation.48 | convolution fusion | flops 2416312320 | bytes 11796480 | tf_op jit(solution)/shard_map/dot_general | solution.py:106
  283.7 7.3 %convolution_convert_fusion.2 = bf16[256,1536]{1,0:T(8,128)(2,1)} fusion(bf16[256,3072]{1,0:T(8,128)(2,1)S(1)} %get-tuple-element.31, bf16[1536,3072]{1,0:T(8,128)(2,1)} %param.15), kind=kOutput, calls=%fused_computation.49 | convolution fusion | flops 2416312320 | bytes 11796480 | tf_op jit(solution)/shard_map/dot_general | solution.py:106
  292.9 6.3 fusion.28
  299.2 6.8 %copy.24 = bf16[4,768,768]{2,1,0:T(8,128)(2,1)} copy(bf16[4,768,768]{1,2,0:T(8,128)(2,1)} %all-to-all-done.2) | data formatting | bytes 9437184 | tf_op jit(solution)/shard_map/all_to_all | solution.py:151
  306.0 9.3 %convolution_convert_fusion.3 = bf16[1024,768]{1,0:T(8,128)(2,1)S(1)} fusion(bf16[3072,768]{1,0:T(8,128)(2,1)} %bitcast.105, bf16[256,3072]{1,0:T(8,128)(2,1)} %copy-done.19, bf16[256,3072]{1,0:T(8,128)(2,1)} %copy-done.21, bf16[256,3072]{1,0:T(8,128)(2,1)} %copy-done.23, bf16[256,3072]{1,0:T(8,128)(2,1)} %copy-done.17), kind=kOutput, calls=%fused_computation.52 | convolution fusion | flops 4857790464 | bytes 12582912 | tf_op jit(solution)/shard_map/dot_general | solution.py:102
  315.4 61.7 %collective-permute-done.12 = bf16[256,1536]{1,0:T(8,128)(2,1)} collective-permute-done((bf16[256,1536]{1,0:T(8,128)(2,1)}, bf16[256,1536]{1,0:T(8,128)(2,1)}, u32[]{:S(2)}, u32[]{:S(2)}) %collective-permute-start.12) | collective-permute-done | bytes 786464 | tf_op jit(solution)/shard_map/ppermute | solution.py:121
  380.6 13.3 %collective-permute-done.10 = bf16[256,1536]{1,0:T(8,128)(2,1)} collective-permute-done((bf16[256,1536]{1,0:T(8,128)(2,1)}, bf16[256,1536]{1,0:T(8,128)(2,1)}, u32[]{:S(2)}, u32[]{:S(2)}) %collective-permute-start.10) | collective-permute-done | bytes 786464 | tf_op jit(solution)/shard_map/ppermute | solution.py:121
  400.8 8.6 %fusion.22 = f32[512,3072]{1,0:T(8,128)} fusion(bf16[1536,3072]{1,0:T(8,128)(2,1)} %param.15, bf16[1024,768]{1,0:T(8,128)(2,1)S(1)} %get-tuple-element.38), kind=kOutput, calls=%fused_computation.33 | convolution fusion | flops 2415919104 | bytes 11796480 | tf_op jit(solution)/shard_map/dot_general | solution.py:102
  409.4 18.1 %collective-permute-done.8 = bf16[512,1536]{1,0:T(8,128)(2,1)S(1)} collective-permute-done((bf16[512,1536]{1,0:T(8,128)(2,1)S(1)}, bf16[512,1536]{1,0:T(8,128)(2,1)S(1)}, u32[]{:S(2)}, u32[]{:S(2)}) %collective-permute-start.8) | collective-permute-done | bytes 1572896 | tf_op jit(solution)/shard_map/ppermute | solution.py:121
  434.3 4.8 fusion.49
  439.1 21.9 %collective-permute-done.3 = bf16[1024,768]{1,0:T(8,128)(2,1)S(1)} collective-permute-done((bf16[1024,768]{1,0:T(8,128)(2,1)S(1)}, bf16[1024,768]{1,0:T(8,128)(2,1)S(1)}, u32[]{:S(2)}, u32[]{:S(2)}) %collective-permute-start.3) | collective-permute-done | bytes 1572896 | tf_op jit(solution)/shard_map/ppermute | solution.py:121
  462.8 4.8 fusion.47
  467.7 15.4 %attend.1 = (bf16[1024,384]{1,0:T(8,128)(2,1)S(1)}, bf16[1024,384]{1,0:T(8,128)(2,1)S(1)}, bf16[1024,384]{1,0:T(8,128)(2,1)S(1)}, bf16[1024,384]{1,0:T(8,128)(2,1)S(1)}) custom-call(bf16[1024,1152]{1,0:T(8,128)(2,1)} %convolution_convert_fusion.q_own.k_own.v_own, bf16[1024,1152]{1,0:T(8,128)(2,1)} %collective-permute-done.q_got.k_got.v_got, ...), custom_call_target="tpu_custom_call" | custom-call | flops 1207959552 | bytes 9437184 | tf_op jit(solution)/shard_map/attend/pallas_call | solution.py:75
  486.1 13.1 %add_convert_fusion = bf16[512,3072]{1,0:T(8,128)(2,1)} fusion(f32[512,3072]{1,0:T(8,128)} %fusion.47, f32[512,3072]{1,0:T(8,128)} %fusion.49, bf16[3072,1152]{1,0:T(8,128)(2,1)} %bitcast.90, bf16[1024,1152]{1,0:T(8,128)(2,1)} %constant_dynamic-update-slice_fusion), kind=kOutput, calls=%fused_computation.10 | convolution fusion | flops 3628597248 | bytes 23986176 | tf_op jit(solution)/shard_map/dot_general | solution.py:106
  499.2 4.8 fusion.16
  504.1 3.7 add_convert_fusion.1
  508.3 5.7 fusion.18
  516.9 5.6 fusion.14
  522.5 3.4 convolution_add_fusion.5
  526.0 4.3 add_convert_fusion.2
  531.9 5.6 fusion.12
  537.6 4.0 fusion.11
  541.9 3.3 convolution_add_fusion.4
  545.2 22.5 %collective-permute-done.11 = bf16[256,3072]{1,0:T(8,128)(2,1)S(1)} collective-permute-done((bf16[256,3072]{1,0:T(8,128)(2,1)}, bf16[256,3072]{1,0:T(8,128)(2,1)S(1)}, u32[]{:S(2)}, u32[]{:S(2)}) %collective-permute-start.11) | collective-permute-done | bytes 1572896 | tf_op jit(solution)/shard_map/ppermute | solution.py:121
  567.7 3.5 add_add_fusion
  573.4 27.2 %collective-permute-done.5 = bf16[256,3072]{1,0:T(8,128)(2,1)} collective-permute-done((bf16[256,3072]{1,0:T(8,128)(2,1)}, bf16[256,3072]{1,0:T(8,128)(2,1)}, u32[]{:S(2)}, u32[]{:S(2)}) %collective-permute-start.5) | collective-permute-done | bytes 1572896 | tf_op jit(solution)/shard_map/ppermute | solution.py:121
  609.0 22.3 %collective-permute-done.6 = bf16[2,64,3072]{2,1,0:T(8,128)(2,1)S(1)} collective-permute-done((bf16[2,64,3072]{2,1,0:T(8,128)(2,1)S(1)}, bf16[2,64,3072]{2,1,0:T(8,128)(2,1)S(1)}, u32[]{:S(2)}, u32[]{:S(2)}) %collective-permute-start.6) | collective-permute-done | bytes 786464 | tf_op jit(solution)/shard_map/ppermute | solution.py:121
  635.8 5.4 all-reduce
  641.9 10.8 %collective-permute-done.7 = bf16[64,3072]{1,0:T(8,128)(2,1)} collective-permute-done((bf16[64,3072]{1,0:T(8,128)(2,1)}, bf16[64,3072]{1,0:T(8,128)(2,1)}, u32[]{:S(2)}, u32[]{:S(2)}) %collective-permute-start.7) | collective-permute-done | bytes 393248 | tf_op jit(solution)/shard_map/ppermute | solution.py:121
  (160 shorter events, 57.3 us)
Async XLA Ops:
  7.2 253.5 %copy-start = (bf16[384,3072]{1,0:T(8,128)(2,1)S(1)}, bf16[384,3072]{1,0:T(8,128)(2,1)}, u32[]{:S(2)}) copy-start(bf16[384,3072]{1,0:T(8,128)(2,1)} %param.14) | copy-start | bytes 7077892
  7.2 226.0 %all-gather.3.cloned.1.call-start = ((), (), s32[]{:S(2)}) async-start(), calls=%async_computation.3 | async-start | bytes 6684672 | tf_op jit(solution)/shard_map/all_gather | solution.py:132
  17.0 240.3 %all-gather.5.cloned.1.call-start = ((), (), s32[]{:S(2)}) async-start(), calls=%async_computation.4 | async-start | bytes 6684672 | tf_op jit(solution)/shard_map/all_gather | solution.py:132
  36.9 115.0 %all-to-all-start = ((bf16[4,768,1152]{1,2,0:T(8,128)(2,1)}), bf16[4,768,1152]{1,2,0:T(8,128)(2,1)}, u32[]{:S(2)}, u32[]{:S(2)}) async-start(bf16[4,768,1152]{1,2,0:T(8,128)(2,1)} %pad_maximum_fusion), calls=%async_computation | async-start | bytes 14155776 | tf_op jit(solution)/shard_map/all_to_all | solution.py:151
  162.4 58.9 %all-to-all-start.1 = ((bf16[4,768,768]{1,2,0:T(8,128)(2,1)}), bf16[4,768,768]{1,2,0:T(8,128)(2,1)}, u32[]{:S(2)}, u32[]{:S(2)}) async-start(bf16[4,768,768]{1,2,0:T(8,128)(2,1)} %get-tuple-element.12), calls=%async_computation.1 | async-start | bytes 9437184 | tf_op jit(solution)/shard_map/all_to_all | solution.py:151
  227.9 71.3 %all-to-all-start.2 = ((bf16[4,768,768]{1,2,0:T(8,128)(2,1)}), bf16[4,768,768]{1,2,0:T(8,128)(2,1)}, u32[]{:S(2)}, u32[]{:S(2)}) async-start(bf16[4,768,768]{1,2,0:T(8,128)(2,1)} %get-tuple-element.14), calls=%async_computation.2 | async-start | bytes 9437184 | tf_op jit(solution)/shard_map/all_to_all | solution.py:151
  236.5 18.1 %copy-start.17 = (bf16[256,3072]{1,0:T(8,128)(2,1)}, bf16[256,3072]{1,0:T(8,128)(2,1)S(1)}, u32[]{:S(2)}) copy-start(bf16[256,3072]{1,0:T(8,128)(2,1)S(1)} %get-tuple-element.33) | copy-start | bytes 4718596
  236.5 18.1 %copy-start.19 = (bf16[256,3072]{1,0:T(8,128)(2,1)}, bf16[256,3072]{1,0:T(8,128)(2,1)S(1)}, u32[]{:S(2)}) copy-start(bf16[256,3072]{1,0:T(8,128)(2,1)S(1)} %get-tuple-element.34) | copy-start | bytes 4718596
  236.5 18.1 %copy-start.21 = (bf16[256,3072]{1,0:T(8,128)(2,1)}, bf16[256,3072]{1,0:T(8,128)(2,1)S(1)}, u32[]{:S(2)}) copy-start(bf16[256,3072]{1,0:T(8,128)(2,1)S(1)} %get-tuple-element.35) | copy-start | bytes 4718596
  236.5 18.1 %copy-start.23 = (bf16[256,3072]{1,0:T(8,128)(2,1)}, bf16[256,3072]{1,0:T(8,128)(2,1)S(1)}, u32[]{:S(2)}) copy-start(bf16[256,3072]{1,0:T(8,128)(2,1)S(1)} %get-tuple-element.36) | copy-start | bytes 4718596
  254.6 213.1 %collective-permute-start = (bf16[1024,1152]{1,0:T(8,128)(2,1)}, bf16[1024,1152]{1,0:T(8,128)(2,1)}, u32[]{:S(2)}, u32[]{:S(2)}) collective-permute-start(bf16[1024,1152]{1,0:T(8,128)(2,1)} %convolution_convert_fusion.q_own.k_own.v_own), channel_id=1, source_target_pairs={{0,1},{1,0},{2,3},{3,2},{4,5},{5,4},{6,7},{7,6},{8,9},{9,8},{10,11... | collective-permute-start | bytes 7077896 | tf_op jit(solution)/shard_map/ppermute | solution.py:121
  264.2 203.5 %collective-permute-start.1 = (bf16[1024,384]{1,0:T(8,128)(2,1)S(1)}, bf16[1024,384]{1,0:T(8,128)(2,1)}, u32[]{:S(2)}, u32[]{:S(2)}) collective-permute-start(bf16[1024,384]{1,0:T(8,128)(2,1)S(1)} %fusion.43.g_own), channel_id=1, source_target_pairs={{0,1},{1,0},{2,3},{3,2},{4,5},{5,4},{6,7},{7,6},{8,9},{9,8},{10,11... | collective-permute-start | bytes 2359304 | tf_op jit(solution)/shard_map/ppermute | solution.py:121
  274.4 123.9 %collective-permute-start.2 = (bf16[1024,768]{1,0:T(8,128)(2,1)}, bf16[1024,768]{1,0:T(8,128)(2,1)}, u32[]{:S(2)}, u32[]{:S(2)}) collective-permute-start(bf16[1024,768]{1,0:T(8,128)(2,1)} %convolution_convert_fusion.4), channel_id=1, source_target_pairs={{0,1},{1,0},{2,3},{3,2},{4,5},{5,4},{6,7},{7,6},{8,9},{9,8},{10,11... | collective-permute-start | bytes 4718600 | tf_op jit(solution)/shard_map/ppermute | solution.py:121
  276.3 16.6 %slice-start.14 = ((s8[9437184]{0:T(1024)(128)(4,1)}), s8[4194304]{0:T(1024)(128)(4,1)S(1)}, s32[]{:S(2)}) async-start(s8[9437184]{0:T(1024)(128)(4,1)} %bitcast.123), calls=%async_computation.19 | async-start | bytes 8388608
  276.3 16.6 %slice-start.15 = ((s8[9437184]{0:T(1024)(128)(4,1)}), s8[4194304]{0:T(1024)(128)(4,1)S(1)}, s32[]{:S(2)}) async-start(s8[9437184]{0:T(1024)(128)(4,1)} %bitcast.123), calls=%async_computation.20 | async-start | bytes 8388608
  283.7 93.4 %collective-permute-start.12 = (bf16[256,1536]{1,0:T(8,128)(2,1)}, bf16[256,1536]{1,0:T(8,128)(2,1)}, u32[]{:S(2)}, u32[]{:S(2)}) collective-permute-start(bf16[256,1536]{1,0:T(8,128)(2,1)} %convolution_convert_fusion.1), channel_id=1, source_target_pairs={{0,1},{1,0},{2,3},{3,2},{4,5},{5,4},{6,7},{7,6},{8,9},{9,8},{10,11... | collective-permute-start | bytes 2359304 | tf_op jit(solution)/shard_map/ppermute | solution.py:121
  291.0 102.9 %collective-permute-start.10 = (bf16[256,1536]{1,0:T(8,128)(2,1)}, bf16[256,1536]{1,0:T(8,128)(2,1)}, u32[]{:S(2)}, u32[]{:S(2)}) collective-permute-start(bf16[256,1536]{1,0:T(8,128)(2,1)} %convolution_convert_fusion.2), channel_id=1, source_target_pairs={{0,1},{1,0},{2,3},{3,2},{4,5},{5,4},{6,7},{7,6},{8,9},{9,8},{10,11... | collective-permute-start | bytes 2359304 | tf_op jit(solution)/shard_map/ppermute | solution.py:121
  306.0 71.1 %copy-start.14 = (bf16[512,1536]{1,0:T(8,128)(2,1)S(1)}, bf16[512,1536]{1,0:T(8,128)(2,1)}, u32[]{:S(2)}) copy-start(bf16[512,1536]{1,0:T(8,128)(2,1)} %fusion.28) | copy-start | bytes 4718596
  377.1 50.5 %collective-permute-start.8 = (bf16[512,1536]{1,0:T(8,128)(2,1)S(1)}, bf16[512,1536]{1,0:T(8,128)(2,1)S(1)}, u32[]{:S(2)}, u32[]{:S(2)}) collective-permute-start(bf16[512,1536]{1,0:T(8,128)(2,1)S(1)} %copy-done.14), channel_id=1, source_target_pairs={{0,1},{1,0},{2,3},{3,2},{4,5},{5,4},{6,7},{7,6},{8,9},{9,8},{10,11... | collective-permute-start | bytes 4718600 | tf_op jit(solution)/shard_map/ppermute | solution.py:121
  380.6 50.5 %copy-start.12 = (bf16[256,1536]{1,0:T(8,128)(2,1)}, bf16[256,1536]{1,0:T(8,128)(2,1)S(1)}, u32[]{:S(2)}) copy-start(bf16[256,1536]{1,0:T(8,128)(2,1)S(1)} %add_convert_fusion.4) | copy-start | bytes 2359300
  393.9 67.1 %collective-permute-start.3 = (bf16[1024,768]{1,0:T(8,128)(2,1)S(1)}, bf16[1024,768]{1,0:T(8,128)(2,1)S(1)}, u32[]{:S(2)}, u32[]{:S(2)}) collective-permute-start(bf16[1024,768]{1,0:T(8,128)(2,1)S(1)} %convolution_convert_fusion.3), channel_id=1, source_target_pairs={{0,1},{1,0},{2,3},{3,2},{4,5},{5,4},{6,7},{7,6},{8,9},{9,8},{10,11... | collective-permute-start | bytes 4718600 | tf_op jit(solution)/shard_map/ppermute | solution.py:121
  398.3 29.6 %slice-start.17 = ((s8[9437184]{0:T(1024)(128)(4,1)}), s8[4194304]{0:T(1024)(128)(4,1)S(1)}, s32[]{:S(2)}) async-start(s8[9437184]{0:T(1024)(128)(4,1)} %bitcast.125), calls=%async_computation.22 | async-start | bytes 8388608
  400.8 27.1 %copy-start.15 = (bf16[1024,768]{1,0:T(8,128)(2,1)}, bf16[1024,768]{1,0:T(8,128)(2,1)S(1)}, u32[]{:S(2)}) copy-start(bf16[1024,768]{1,0:T(8,128)(2,1)S(1)} %get-tuple-element.38) | copy-start | bytes 4718596
  400.8 33.6 %copy-start.3 = (f32[1024,768]{1,0:T(8,128)}, f32[1024,768]{1,0:T(8,128)S(1)}, u32[]{:S(2)}) copy-start(f32[1024,768]{1,0:T(8,128)S(1)} %get-tuple-element.37) | copy-start | bytes 9437188
  400.8 27.1 %slice-start.18 = ((s8[9437184]{0:T(1024)(128)(4,1)}), s8[4194304]{0:T(1024)(128)(4,1)S(1)}, s32[]{:S(2)}) async-start(s8[9437184]{0:T(1024)(128)(4,1)} %bitcast.125), calls=%async_computation.23 | async-start | bytes 8388608
  400.8 27.1 %slice-start.19 = ((s8[9437184]{0:T(1024)(128)(4,1)}), s8[1048576]{0:T(1024)(128)(4,1)S(1)}, s32[]{:S(2)}) async-start(s8[9437184]{0:T(1024)(128)(4,1)} %bitcast.125), calls=%async_computation.24 | async-start | bytes 2097152
  431.1 31.7 %slice-start.8 = ((s8[4718592]{0:T(1024)(128)(4,1)}), s8[4194304]{0:T(1024)(128)(4,1)S(1)}, s32[]{:S(2)}) async-start(s8[4718592]{0:T(1024)(128)(4,1)} %bitcast.106), calls=%async_computation.13 | async-start | bytes 8388608
  434.3 28.4 %slice-start.9 = ((s8[4718592]{0:T(1024)(128)(4,1)}), s8[524288]{0:T(1024)(128)(4,1)S(1)}, s32[]{:S(2)}) async-start(s8[4718592]{0:T(1024)(128)(4,1)} %bitcast.106), calls=%async_computation.14 | async-start | bytes 1048576
  485.1 19.0 %slice-start.12 = ((s8[6291456]{0:T(1024)(128)(4,1)}), s8[2097152]{0:T(1024)(128)(4,1)S(1)}, s32[]{:S(2)}) async-start(s8[6291456]{0:T(1024)(128)(4,1)} %bitcast.121), calls=%async_computation.17 | async-start | bytes 4194304
  486.1 13.1 %copy-start.16 = (bf16[1024,768]{1,0:T(8,128)(2,1)S(1)}, bf16[1024,768]{1,0:T(8,128)(2,1)}, u32[]{:S(2)}) copy-start(bf16[1024,768]{1,0:T(8,128)(2,1)} %get-tuple-element.40) | copy-start | bytes 4718596
  486.1 18.0 %slice-start.13 = ((s8[6291456]{0:T(1024)(128)(4,1)}), s8[4194304]{0:T(1024)(128)(4,1)S(1)}, s32[]{:S(2)}) async-start(s8[6291456]{0:T(1024)(128)(4,1)} %bitcast.121), calls=%async_computation.18 | async-start | bytes 8388608
  499.2 26.7 %collective-permute-start.9 = (bf16[512,3072]{1,0:T(8,128)(2,1)}, bf16[512,3072]{1,0:T(8,128)(2,1)}, u32[]{:S(2)}, u32[]{:S(2)}) collective-permute-start(bf16[512,3072]{1,0:T(8,128)(2,1)} %add_convert_fusion), channel_id=1, source_target_pairs={{0,8},{8,0},{16,24},{24,16},{1,9},{9,1},{17,25},{25,17},{2,10},{10... | collective-permute-start | bytes 9437192 | tf_op jit(solution)/shard_map/ppermute | solution.py:121
  499.2 14.8 %slice-start.6 = ((s8[4718592]{0:T(1024)(128)(4,1)}), s8[4194304]{0:T(1024)(128)(4,1)S(1)}, s32[]{:S(2)}) async-start(s8[4718592]{0:T(1024)(128)(4,1)} %bitcast.102), calls=%async_computation.11 | async-start | bytes 8388608
  504.1 9.9 %slice-start.7 = ((s8[4718592]{0:T(1024)(128)(4,1)}), s8[524288]{0:T(1024)(128)(4,1)S(1)}, s32[]{:S(2)}) async-start(s8[4718592]{0:T(1024)(128)(4,1)} %bitcast.102), calls=%async_computation.12 | async-start | bytes 1048576
  507.8 29.8 %collective-permute-start.4 = (bf16[512,3072]{1,0:T(8,128)(2,1)}, bf16[512,3072]{1,0:T(8,128)(2,1)}, u32[]{:S(2)}, u32[]{:S(2)}) collective-permute-start(bf16[512,3072]{1,0:T(8,128)(2,1)} %add_convert_fusion.1), channel_id=1, source_target_pairs={{0,8},{8,0},{16,24},{24,16},{1,9},{9,1},{17,25},{25,17},{2,10},{10... | collective-permute-start | bytes 9437192 | tf_op jit(solution)/shard_map/ppermute | solution.py:121
  508.3 14.2 %slice-start = ((s8[7077888]{0:T(1024)(128)(4,1)}), s8[4194304]{0:T(1024)(128)(4,1)S(1)}, s32[]{:S(2)}) async-start(s8[7077888]{0:T(1024)(128)(4,1)} %bitcast.91), calls=%async_computation.5 | async-start | bytes 8388608
  530.2 37.5 %collective-permute-start.11 = (bf16[256,3072]{1,0:T(8,128)(2,1)}, bf16[256,3072]{1,0:T(8,128)(2,1)S(1)}, u32[]{:S(2)}, u32[]{:S(2)}) collective-permute-start(bf16[256,3072]{1,0:T(8,128)(2,1)} %add_convert_fusion.2), channel_id=1, source_target_pairs={{0,16},{8,24},{16,0},{24,8},{1,17},{9,25},{17,1},{25,9},{2,18},{10... | collective-permute-start | bytes 4718600 | tf_op jit(solution)/shard_map/ppermute | solution.py:121
  541.6 26.1 %copy-start.13 = (bf16[256,1536]{1,0:T(8,128)(2,1)S(1)}, bf16[256,1536]{1,0:T(8,128)(2,1)}, u32[]{:S(2)}) copy-start(bf16[256,1536]{1,0:T(8,128)(2,1)} %copy-done.12) | copy-start | bytes 2359300
  541.6 59.0 %collective-permute-start.5 = (bf16[256,3072]{1,0:T(8,128)(2,1)}, bf16[256,3072]{1,0:T(8,128)(2,1)}, u32[]{:S(2)}, u32[]{:S(2)}) collective-permute-start(bf16[256,3072]{1,0:T(8,128)(2,1)} %fusion.11), channel_id=1, source_target_pairs={{0,16},{8,24},{16,0},{24,8},{1,17},{9,25},{17,1},{25,9},{2,18},{10... | collective-permute-start | bytes 4718600 | tf_op jit(solution)/shard_map/ppermute | solution.py:121
  567.7 32.9 %copy-start.10 = (f32[256,3072]{1,0:T(8,128)S(1)}, f32[256,3072]{1,0:T(8,128)}, u32[]{:S(2)}) copy-start(f32[256,3072]{1,0:T(8,128)} %fusion.18) | copy-start | bytes 9437188
  567.7 32.9 %copy-start.11 = (f32[256,3072]{1,0:T(8,128)S(1)}, f32[256,3072]{1,0:T(8,128)}, u32[]{:S(2)}) copy-start(f32[256,3072]{1,0:T(8,128)} %fusion.12) | copy-start | bytes 9437188
  571.4 34.6 %collective-permute-start.13 = (bf16[2,64,3072]{2,1,0:T(8,128)(2,1)S(1)}, bf16[2,64,3072]{2,1,0:T(8,128)(2,1)S(1)}, u32[]{:S(2)}, u32[]{:S(2)}) collective-permute-start(bf16[2,64,3072]{2,1,0:T(8,128)(2,1)S(1)} %fusion.87), channel_id=1, source_target_pairs={{0,2},{2,0},{4,6},{6,4},{1,3},{3,1},{5,7},{7,5},{8,10},{10,8},{12,... | collective-permute-start | bytes 2359304 | tf_op jit(solution)/shard_map/ppermute | solution.py:121
  604.0 27.3 %collective-permute-start.6 = (bf16[2,64,3072]{2,1,0:T(8,128)(2,1)S(1)}, bf16[2,64,3072]{2,1,0:T(8,128)(2,1)S(1)}, u32[]{:S(2)}, u32[]{:S(2)}) collective-permute-start(bf16[2,64,3072]{2,1,0:T(8,128)(2,1)S(1)} %fusion.86), channel_id=1, source_target_pairs={{0,2},{2,0},{4,6},{6,4},{1,3},{3,1},{5,7},{7,5},{8,10},{10,8},{12,... | collective-permute-start | bytes 2359304 | tf_op jit(solution)/shard_map/ppermute | solution.py:121
  606.3 29.1 %copy-start.6 = (bf16[64,3072]{1,0:T(8,128)(2,1)S(1)}, bf16[64,3072]{1,0:T(8,128)(2,1)}, u32[]{:S(2)}) copy-start(bf16[64,3072]{1,0:T(8,128)(2,1)} %param.8) | copy-start | bytes 1179652
  606.3 29.1 %copy-start.26 = (f32[64]{0:T(128)S(1)}, f32[64]{0:T(128)}, u32[]{:S(2)}) copy-start(f32[64]{0:T(128)} %copy-done.25) | copy-start | bytes 772
  606.3 29.1 %copy-start.28 = (f32[64]{0:T(128)S(1)}, f32[64]{0:T(128)}, u32[]{:S(2)}) copy-start(f32[64]{0:T(128)} %copy-done.27) | copy-start | bytes 772
  606.3 29.1 %collective-permute-start.14 = (bf16[64,3072]{1,0:T(8,128)(2,1)S(1)}, bf16[64,3072]{1,0:T(8,128)(2,1)S(1)}, u32[]{:S(2)}, u32[]{:S(2)}) collective-permute-start(bf16[64,3072]{1,0:T(8,128)(2,1)S(1)} %fusion.115), channel_id=1, source_target_pairs={{0,4},{2,6},{4,0},{6,2},{1,5},{3,7},{5,1},{7,3},{8,12},{10,14},{12... | collective-permute-start | bytes 1179656 | tf_op jit(solution)/shard_map/ppermute | solution.py:121
  633.6 19.1 %collective-permute-start.7 = (bf16[64,3072]{1,0:T(8,128)(2,1)}, bf16[64,3072]{1,0:T(8,128)(2,1)}, u32[]{:S(2)}, u32[]{:S(2)}) collective-permute-start(bf16[64,3072]{1,0:T(8,128)(2,1)} %fusion.114), channel_id=1, source_target_pairs={{0,4},{2,6},{4,0},{6,2},{1,5},{3,7},{5,1},{7,3},{8,12},{10,14},{12... | collective-permute-start | bytes 1179656 | tf_op jit(solution)/shard_map/ppermute | solution.py:121
  (21 other events, 98.0 us)
Sparse Core Ops, SparseCore 0:
  17.1 81.0 all-gather.2
  100.5 73.1 all-gather.4

commit v3 on v2

--- a/solution.py
+++ b/solution.py
@@ -126,16 +126,38 @@
     me_x, me_y = lax.axis_index("gx"), lax.axis_index("gy")
     own_rows = layer_input.shape[0]
     image_rows = own_rows * n_gy
-    order = (3, 1, 2, 0)
+    depth = w_query.shape[0]
+    row_order = (3, 1, 2, 0)
 
     def all_rows(block):
         gathered = lax.all_gather(block, ("gx", "gy"), axis=0, tiled=True)
         return jnp.concatenate(
             [
                 lax.dynamic_slice_in_dim(gathered, (me_x ^ bit) * image_rows, image_rows, 0)
-                for bit in order
+                for bit in row_order
             ],
             axis=0,
+        )
+
+    def relative(value):
+        return jnp.concatenate(
+            [
+                lax.dynamic_slice_in_dim(value, (me_x ^ bit) * depth, depth, 1)
+                for bit in range(n_gx)
+            ],
+            axis=1,
+        )
+
+    def same(value, bit):
+        return value
+
+    def reordered(value, bit):
+        return jnp.concatenate(
+            [
+                lax.slice_in_dim(value, (place ^ bit) * depth, ((place ^ bit) + 1) * depth, axis=1)
+                for place in range(n_gx)
+            ],
+            axis=1,
         )
 
     def others(part):
@@ -143,16 +165,25 @@
             return trade(part, "gz", 1)
         return half(lax.psum(part.astype(jnp.float32), "gz") - part.astype(jnp.float32))
 
-    def by_owner(weight):
-        rows, columns = weight.shape
-        return weight.reshape(rows, n_gx, columns // n_gx).transpose(1, 0, 2)
-
-    def swap(weight):
-        swapped = lax.all_to_all(weight, "gx", split_axis=0, concat_axis=0, tiled=True)
-        return swapped.reshape(n_gx * weight.shape[1], weight.shape[2])
+    def columns_of(weights, cut, cuts):
+        pieces = []
+        for bit in range(n_gx):
+            slices = []
+            for weight in weights:
+                owned = weight.shape[1] // n_gx
+                count = owned // cuts
+                start = (me_x ^ bit) * owned + cut * count
+                slices.append(lax.dynamic_slice_in_dim(weight, start, count, 1))
+            piece = jnp.concatenate(slices, axis=1) if len(slices) > 1 else slices[0]
+            pieces.append(piece if bit == 0 else trade(piece, "gx", bit))
+        return jnp.concatenate(pieces, axis=0)
 
     def after(value, earlier):
-        return lax.optimization_barrier((value, earlier))
+        return lax.optimization_barrier((value, earlier))[0]
+
+    mlp_cuts = 3
+    in_heads = columns_of((w_query, w_key, w_value), 0, 1)
+    in_mlp = [columns_of((w_mlp_in,), cut, mlp_cuts) for cut in range(mlp_cuts)]
 
     wide = layer_input.astype(jnp.float32)
     total, squares = lax.psum((jnp.sum(wide, axis=1), jnp.sum(wide * wide, axis=1)), "gz")
@@ -160,60 +191,45 @@
     spread = squares / D - center * center
     inverse = lax.rsqrt(spread + EPSILON)
     normed = (wide - center[:, None]) * inverse[:, None]
-    gathered_in = all_rows(half(normed))
-
-    heads_in = jnp.concatenate([by_owner(w) for w in (w_query, w_key, w_value)], axis=2)
-    mlp_in = by_owner(w_mlp_in)
-    cut = mlp_in.shape[2] // 2
-    in_heads = swap(heads_in)
-    first_mlp, in_heads = after(mlp_in[:, :, :cut], in_heads)
-    in_first = swap(first_mlp)
-    second_mlp, in_first = after(mlp_in[:, :, cut:], in_first)
-    in_second = swap(second_mlp)
+    gathered_in = relative(all_rows(half(normed)))
 
     heads_own = half(dot(gathered_in, in_heads))
     heads_got = others(heads_own)
-    first_own = half(dot(gathered_in, in_first))
-    first_got = others(first_own)
+    mlp_own = [half(dot(gathered_in, weight)) for weight in in_mlp]
+    mlp_got = [others(own) for own in mlp_own]
 
     gathered_cot = all_rows(out_cotangent)
     mixed_own = half(back_dot(gathered_cot, w_attn_out))
     mixed_got = others(mixed_own)
-    second_own = half(dot(gathered_in, in_second))
-    second_got = others(second_own)
 
     mixed, query_grad, key_grad, value_grad = attend(heads_own, heads_got, mixed_own, mixed_got)
-    pre_first, pre_second = wide_sum(first_own, first_got), wide_sum(second_own, second_got)
-    act_first, act_second = half(gelu(pre_first)), half(gelu(pre_second))
-    heads_grad = jnp.concatenate([query_grad, key_grad, value_grad], axis=1)
+    pre = [wide_sum(own, got) for own, got in zip(mlp_own, mlp_got)]
+    acts = jnp.concatenate([mixed] + [half(gelu(part)) for part in pre], axis=1)
+    w_out = jnp.concatenate([w_attn_out, w_mlp_out], axis=0)
+    w_in = jnp.concatenate([in_heads] + in_mlp, axis=1)
+    late_cot = after(gathered_cot, mlp_own[-1])
 
     def block_of(value, start, count):
         return lax.slice_in_dim(value, start * image_rows, (start + count) * image_rows)
 
     def forward_term(start, count):
-        result = dot(block_of(mixed, start, count), w_attn_out)
-        result = result + dot(block_of(act_first, start, count), w_mlp_out[:cut])
-        return result + dot(block_of(act_second, start, count), w_mlp_out[cut:])
+        return dot(block_of(acts, start, count), w_out)
 
     def backward_term(start, count):
-        act_own = half(back_dot(block_of(gathered_cot, start, count), w_mlp_out))
+        act_own = half(back_dot(block_of(late_cot, start, count), w_mlp_out))
         grad = half(wide_sum(act_own, others(act_own)))
-        first = gelu_back(block_of(pre_first, start, count), grad[:, :cut])
-        second = gelu_back(block_of(pre_second, start, count), grad[:, cut:])
-        result = back_dot(block_of(heads_grad, start, count), in_heads)
-        result = result + back_dot(first, in_first)
-        return result + back_dot(second, in_second)
-
-    def keep_and_send(value, sent_first):
-        count = value.shape[0] // 2
-        low, high = value[:count], value[count:]
-        return jnp.where(sent_first, high, low), jnp.where(sent_first, low, high)
-
-    def spread_rows(term):
-        from_core = trade(half(term(0, 2)), "gx", 1)
+        parts = [block_of(value, start, count) for value in (query_grad, key_grad, value_grad)]
+        width = grad.shape[1] // mlp_cuts
+        for cut in range(mlp_cuts):
+            columns = grad[:, cut * width : (cut + 1) * width]
+            parts.append(gelu_back(block_of(pre[cut], start, count), columns))
+        return back_dot(jnp.concatenate(parts, axis=1), w_in)
+
+    def spread_rows(term, mapped):
+        from_core = mapped(trade(half(term(0, 2)), "gx", 1), 1)
         to_x = half(term(2, 1) + from_core[:image_rows].astype(jnp.float32))
-        from_x = trade(to_x, "gx", 2)
-        mine = wide_sum(from_core[image_rows:], from_x) + term(3, 1)
+        from_x = mapped(trade(to_x, "gx", 2), 2)
+        mine = term(3, 1) + wide_sum(from_core[image_rows:], from_x)
         quarters = mine.reshape(2, 2, own_rows, mine.shape[1])
         odd = me_y % 2 == 1
         kept = jnp.where(odd, quarters[:, 1], quarters[:, 0])
@@ -224,8 +240,8 @@
         sent = jnp.where(high, pair[0], pair[1])
         return kept + trade(half(sent), "gy", 2).astype(jnp.float32)
 
-    layer_out = half(wide + spread_rows(forward_term))
-    normed_grad = spread_rows(backward_term)
+    layer_out = half(wide + spread_rows(forward_term, same))
+    normed_grad = relative(spread_rows(backward_term, reordered))
     first, second = lax.psum(
         (jnp.sum(normed_grad, axis=1), jnp.sum(normed_grad * normed, axis=1)), "gz"
     )

time: 668 us -> 821 us (1.23)
  other arithmetic: 23.7 us -> 148 us
  waiting for transfers between devices: 341 us -> 412 us
  matrix products: 150 us -> 131 us
  local copies, waits for them, and re-layouts: 69.2 us -> 53.1 us
    ppermute x15 -> x28, waiting for transfers between devices: 198 us -> 411 us  [trade(): return lax.ppermute(block, axis, pairs)]
    all_to_all x3 -> x0, waiting for transfers between devices: 143 us -> none  [swap(): lax.all_to_all(weight, 'gx', split_axis=0, concat_axis=0, tiled=True)]
    concatenate x1 -> x10, other arithmetic: 6.22 us -> 119 us  [the longest x1 108 us: body(): w_in = jnp.concatenate([in_heads] + in_mlp, axis=1)]
    all_to_all x3 -> x0, local copies, waits for them, and re-layouts: 24 us -> none  [swap(): lax.all_to_all(weight, 'gx', split_axis=0, concat_axis=0, tiled=True)]
    unnamed x104 -> x106, local copies, waits for them, and re-layouts: 29.4 us -> 11.4 us
    all_to_all x3 -> x0, starting transfers between devices: 15.7 us -> none  [swap(): lax.all_to_all(weight, 'gx', split_axis=0, concat_axis=0, tiled=True)]
    dot_general x12 -> x7, matrix products: 81.9 us -> 68.1 us  [dot(): return jnp.dot(left, right, preferred_element_type=jnp.float32)]
    dynamic_slice x0 -> x4, local copies, waits for them, and re-layouts: none -> 13.6 us  [the longest x3 11.3 us: columns_of(): slices.append(lax.dynamic_slice_in_dim(weight, start, count, 1))]
  transfers between devices with their start and end apart: 20 -> 30, of which waited for: 10 -> 16; matrix products, arithmetic and copies ran while one was open for 33% -> 31% of each run, Pallas kernels for 0% -> 0%
where the time goes in v3:
time: 821 us; the launch traced here: 816 us
  waiting for transfers between devices  412 us (50%)
  other arithmetic  148 us (18%)
  matrix products  131 us (16%)
  local copies, waits for them, and re-layouts  53.1 us (6%)
  starting transfers between devices  30.1 us (4%)
  between operations  15.3 us (2%)
  Pallas kernels  15.1 us (2%)
  blocking collectives  11.3 us (1%)
    ppermute x28, waiting for transfers between devices, trade(): return lax.ppermute(block, axis, pairs)  411 us
    concatenate x1, other arithmetic, body(): w_in = jnp.concatenate([in_heads] + in_mlp, axis=1)  108 us
    dot_general x7, matrix products, dot(): return jnp.dot(left, right, preferred_element_type=jnp.float32)  68.1 us
    dot_general x7, matrix products, back_dot(): lax.dot_general(left, right, (((1,), (1,)), ((), ())), preferred_element_...  63.3 us
    ppermute x28, starting transfers between devices, trade(): return lax.ppermute(block, axis, pairs)  30.1 us
  transfers between devices with their start and end apart: 30, of which 16 were waited for; matrix products, arithmetic and copies ran while one was open for 31% of the time, Pallas kernels for 0%

profile of v3, /device:TPU:0, one launch (start us, length us, event | category | flops | bytes accessed | tf_op | source)
XLA Modules:
  0.0 816.3 jit_solution(11010425493540620736)
XLA Ops:
  9.1 5.9 all-reduce.1
  17.6 7.0 constant_dynamic-slice_fusion.15
  29.0 3.0 constant_dynamic-slice_fusion.29
  36.3 11.1 %collective-permute-done.11 = bf16[768,512]{1,0:T(8,128)(2,1)} collective-permute-done((bf16[768,512]{1,0:T(8,128)(2,1)}, bf16[768,512]{1,0:T(8,128)(2,1)}, u32[]{:S(2)}, u32[]{:S(2)}) %collective-permute-start.11) | collective-permute-done | bytes 786464 | tf_op jit(solution)/shard_map/ppermute | solution.py:121
  48.8 30.5 %collective-permute-done.10 = bf16[768,512]{1,0:T(8,128)(2,1)} collective-permute-done((bf16[768,512]{1,0:T(8,128)(2,1)}, bf16[768,512]{1,0:T(8,128)(2,1)}, u32[]{:S(2)}, u32[]{:S(2)}) %collective-permute-start.10) | collective-permute-done | bytes 786464 | tf_op jit(solution)/shard_map/ppermute | solution.py:121
  81.2 14.4 %collective-permute-done.7 = bf16[768,512]{1,0:T(8,128)(2,1)} collective-permute-done((bf16[768,512]{1,0:T(8,128)(2,1)}, bf16[768,512]{1,0:T(8,128)(2,1)}, u32[]{:S(2)}, u32[]{:S(2)}) %collective-permute-start.7) | collective-permute-done | bytes 786464 | tf_op jit(solution)/shard_map/ppermute | solution.py:121
  95.9 3.2 constant_dynamic-update-slice_fusion.1
  99.2 18.0 %collective-permute-done.6 = bf16[768,512]{1,0:T(8,128)(2,1)} collective-permute-done((bf16[768,512]{1,0:T(8,128)(2,1)}, bf16[768,512]{1,0:T(8,128)(2,1)}, u32[]{:S(2)}, u32[]{:S(2)}) %collective-permute-start.6) | collective-permute-done | bytes 786464 | tf_op jit(solution)/shard_map/ppermute | solution.py:121
  119.2 8.4 %constant_dynamic-update-slice_fusion = bf16[1920,3072]{1,0:T(8,128)(2,1)} fusion(bf16[1920,3072]{1,0:T(8,128)(2,1)} %constant_dynamic-update-slice_fusion.1, bf16[1536,3072]{1,0:T(8,128)(2,1)} %param.15), kind=kLoop, calls=%fused_computation.194 | loop fusion | bytes 18874368 | tf_op jit(solution)/shard_map/concatenate | solution.py:208
  127.6 98.6 %collective-permute-done.15 = bf16[768,512]{1,0:T(8,128)(2,1)} collective-permute-done((bf16[768,512]{1,0:T(8,128)(2,1)}, bf16[768,512]{1,0:T(8,128)(2,1)}, u32[]{:S(2)}, u32[]{:S(2)}) %collective-permute-start.15) | collective-permute-done | bytes 786464 | tf_op jit(solution)/shard_map/ppermute | solution.py:121
  226.2 17.1 %collective-permute-done.14 = bf16[768,512]{1,0:T(8,128)(2,1)} collective-permute-done((bf16[768,512]{1,0:T(8,128)(2,1)}, bf16[768,512]{1,0:T(8,128)(2,1)}, u32[]{:S(2)}, u32[]{:S(2)}) %collective-permute-start.14) | collective-permute-done | bytes 786464 | tf_op jit(solution)/shard_map/ppermute | solution.py:121
  243.3 108.0 %maximum_maximum_fusion = bf16[3072,2688]{1,0:T(8,128)(2,1)} fusion(bf16[768,512]{1,0:T(8,128)(2,1)} %collective-permute-done.15, bf16[768,512]{1,0:T(8,128)(2,1)} %collective-permute-done.14, bf16[768,512]{1,0:T(8,128)(2,1)} %collective-permute-done.13, bf16[768,512]{1,0:T(8,128)(2,1)S(1)} %get-tuple-element.28, bf16[768,512]{1,0:T(8,128)(2,1)} %collective-permute-done.11, ...), kind=kLoop, calls=%fused_computation | loop fusion | flops 297271296 | bytes 33030144 | tf_op jit(solution)/shard_map/concatenate | solution.py:209
  351.4 5.1 constant_dynamic-slice_fusion.19
  358.1 3.4 convolution_convert_fusion.4.g_own
  362.1 2.4 constant_dynamic-slice_fusion.35
  364.5 8.1 fusion.48
  372.6 7.8 convolution_convert_fusion.2
  380.5 5.3 convolution_convert_fusion.3
  385.7 6.6 fusion.42
  394.2 13.0 %fusion.13.q_own.k_own.v_own = bf16[1024,1152]{1,0:T(8,128)(2,1)S(1)} fusion(bf16[768,1152]{1,0:T(8,128)(2,1)} %collective-permute-done.2, bf16[768,1152]{1,0:T(8,128)(2,1)} %collective-permute-done.1, bf16[768,1152]{1,0:T(8,128)(2,1)} %collective-permute-done, bf16[768,384]{1,0:T(8,128)(2,1)} %copy-done.25, bf16[768,384]{1,0:T(8,128)(2,1)} %copy-done.26, ...), kind=kOutput, calls=%fused_computation.22 | convolution fusion | flops 7316570112 | bytes 15728640 | tf_op jit(solution)/shard_map/dot_general | solution.py:102
  409.6 8.1 fusion.51
  419.5 7.2 fusion.54
  426.6 59.6 %collective-permute-done.21 = bf16[256,1536]{0,1:T(8,128)(2,1)} collective-permute-done((bf16[256,1536]{0,1:T(8,128)(2,1)}, bf16[256,1536]{0,1:T(8,128)(2,1)}, u32[]{:S(2)}, u32[]{:S(2)}) %collective-permute-start.21) | collective-permute-done | bytes 786464 | tf_op jit(solution)/shard_map/ppermute | solution.py:121
  488.0 2.5 add_convert_fusion.3
  490.5 12.6 %collective-permute-done.24 = bf16[256,1536]{0,1:T(8,128)(2,1)} collective-permute-done((bf16[256,1536]{0,1:T(8,128)(2,1)}, bf16[256,1536]{0,1:T(8,128)(2,1)}, u32[]{:S(2)}, u32[]{:S(2)}) %collective-permute-start.24) | collective-permute-done | bytes 786464 | tf_op jit(solution)/shard_map/ppermute | solution.py:121
  504.8 2.4 add_convert_fusion.2
  507.3 18.2 %collective-permute-done.12 = bf16[1024,512]{0,1:T(8,128)(2,1)} collective-permute-done((bf16[1024,512]{0,1:T(8,128)(2,1)}, bf16[1024,512]{0,1:T(8,128)(2,1)}, u32[]{:S(2)}, u32[]{:S(2)}) %collective-permute-start.12) | collective-permute-done | bytes 1048608 | tf_op jit(solution)/shard_map/ppermute | solution.py:121
  527.3 3.5 convert_add_fusion.1
  530.8 17.1 %collective-permute-done.8 = bf16[1024,512]{0,1:T(8,128)(2,1)S(1)} collective-permute-done((bf16[1024,512]{0,1:T(8,128)(2,1)}, bf16[1024,512]{0,1:T(8,128)(2,1)S(1)}, u32[]{:S(2)}, u32[]{:S(2)}) %collective-permute-start.8) | collective-permute-done | bytes 1048608 | tf_op jit(solution)/shard_map/ppermute | solution.py:121
  547.9 2.2 convert_add_fusion.2
  550.1 3.8 convert_add_fusion
  553.9 27.7 %collective-permute-done.22 = bf16[512,1536]{0,1:T(8,128)(2,1)S(1)} collective-permute-done((bf16[512,1536]{0,1:T(8,128)(2,1)S(1)}, bf16[512,1536]{0,1:T(8,128)(2,1)S(1)}, u32[]{:S(2)}, u32[]{:S(2)}) %collective-permute-start.22) | collective-permute-done | bytes 1572896 | tf_op jit(solution)/shard_map/ppermute | solution.py:121
  583.3 14.0 %collective-permute-done.4.g_got = bf16[1024,384]{1,0:T(8,128)(2,1)S(1)} collective-permute-done((bf16[1024,384]{1,0:T(8,128)(2,1)S(1)}, bf16[1024,384]{1,0:T(8,128)(2,1)S(1)}, u32[]{:S(2)}, u32[]{:S(2)}) %collective-permute-start.4) | collective-permute-done | bytes 786464 | tf_op jit(solution)/shard_map/ppermute | solution.py:121
  597.3 15.1 %attend.1 = (bf16[1024,384]{1,0:T(8,128)(2,1)S(1)}, bf16[1024,384]{1,0:T(8,128)(2,1)S(1)}, bf16[1024,384]{1,0:T(8,128)(2,1)S(1)}, bf16[1024,384]{1,0:T(8,128)(2,1)S(1)}) custom-call(bf16[1024,1152]{1,0:T(8,128)(2,1)S(1)} %fusion.13.q_own.k_own.v_own, bf16[1024,1152]{1,0:T(8,128)(2,1)S(1)} %collective-permute-done.3.q_got.k_got.v_got, ...), custom_call_target="tpu_custom_call" | custom-call | flops 1207959552 | bytes 9437184 | tf_op jit(solution)/shard_map/attend/pallas_call | solution.py:75
  628.2 14.3 %convolution_convert_fusion.1 = bf16[512,3072]{1,0:T(8,128)(2,1)} fusion(bf16[512,2688]{0,1:T(8,128)(2,1)S(1)} %fusion.108, bf16[3072,2688]{1,0:T(8,128)(2,1)} %maximum_maximum_fusion), kind=kOutput, calls=%fused_computation.17 | convolution fusion | flops 8457289728 | bytes 22413312 | tf_op jit(solution)/shard_map/dot_general | solution.py:106
  642.6 2.2 pad_maximum_fusion.3
  645.2 12.9 %convolution_convert_fusion = bf16[512,3072]{1,0:T(8,128)(2,1)} fusion(bf16[1920,3072]{1,0:T(8,128)(2,1)} %constant_dynamic-update-slice_fusion, bf16[1024,1920]{0,1:T(8,128)(2,1)} %pad_maximum_fusion.3), kind=kOutput, calls=%fused_computation.16 | convolution fusion | flops 6041370624 | bytes 16908288 | tf_op jit(solution)/shard_map/dot_general | solution.py:102
  667.3 12.4 %fusion.12 = bf16[256,3072]{1,0:T(8,128)(2,1)} fusion(bf16[256,2688]{0,1:T(8,128)(2,1)} %copy-done.37, bf16[3072,2688]{1,0:T(8,128)(2,1)} %maximum_maximum_fusion, bf16[512,3072]{1,0:T(8,128)(2,1)} %pad_maximum_fusion.4), kind=kOutput, calls=%fused_computation.21 | convolution fusion | flops 4230217728 | bytes 21037056 | tf_op jit(solution)/shard_map/dot_general | solution.py:106
  681.2 9.5 %add_convert_fusion.1 = bf16[256,3072]{1,0:T(8,128)(2,1)} fusion(bf16[512,3072]{1,0:T(8,128)(2,1)} %collective-permute-done.17, bf16[1920,3072]{1,0:T(8,128)(2,1)} %constant_dynamic-update-slice_fusion, bf16[1024,512]{0,1:T(8,128)(2,1)} %get-tuple-element.73, bf16[1024,512]{0,1:T(8,128)(2,1)S(1)} %copy-done.4, bf16[1024,512]{0,1:T(8,128)(2,1)S(1)} %copy-done.5, ...), kind=kOutput, calls=%fused_computation.52 | convolution fusion | flops 3026190336 | bytes 18874368 | tf_op jit(solution)/shard_map/dot_general | solution.py:102
  691.2 26.0 %collective-permute-done.25 = bf16[256,3072]{1,0:T(8,128)(2,1)} collective-permute-done((bf16[256,3072]{1,0:T(8,128)(2,1)}, bf16[256,3072]{1,0:T(8,128)(2,1)}, u32[]{:S(2)}, u32[]{:S(2)}) %collective-permute-start.25) | collective-permute-done | bytes 1572896 | tf_op jit(solution)/shard_map/ppermute | solution.py:121
  717.2 2.6 fusion.166
  719.8 13.5 %convolution_add_fusion.1 = f32[256,3072]{1,0:T(8,128)} fusion(bf16[256,2688]{0,1:T(8,128)(2,1)} %copy-done.38, bf16[3072,2688]{1,0:T(8,128)(2,1)} %maximum_maximum_fusion, bf16[512,3072]{1,0:T(8,128)(2,1)} %pad_maximum_fusion.4, bf16[256,1536]{1,0:T(8,128)(2,1)} %get-tuple-element.79, bf16[256,1536]{1,0:T(8,128)(2,1)} %get-tuple-element.78), kind=kOutput, calls=%fused_computation.20 | convolution fusion | flops 4233363456 | bytes 24182784 | tf_op jit(solution)/shard_map/dot_general | solution.py:106
  737.0 13.4 %collective-permute-done.18 = bf16[256,3072]{1,0:T(8,128)(2,1)} collective-permute-done((bf16[256,3072]{1,0:T(8,128)(2,1)}, bf16[256,3072]{1,0:T(8,128)(2,1)}, u32[]{:S(2)}, u32[]{:S(2)}) %collective-permute-start.18) | collective-permute-done | bytes 1572896 | tf_op jit(solution)/shard_map/ppermute | solution.py:121
  750.4 9.3 %add_add_fusion = f32[256,3072]{1,0:T(8,128)S(1)} fusion(bf16[256,3072]{1,0:T(8,128)(2,1)} %collective-permute-done.18, bf16[512,3072]{1,0:T(8,128)(2,1)} %collective-permute-done.17, bf16[1920,3072]{1,0:T(8,128)(2,1)} %constant_dynamic-update-slice_fusion, bf16[1024,512]{0,1:T(8,128)(2,1)} %get-tuple-element.73, bf16[1024,512]{0,1:T(8,128)(2,1)S(1)} %copy-done.4, ...), kind=kOutput, calls=%fused_computation.51 | convolution fusion | flops 3026976768 | bytes 22020096 | tf_op jit(solution)/shard_map/dot_general | solution.py:102
  761.8 2.7 collective-permute-start.27
  764.4 22.9 %collective-permute-done.19 = bf16[2,64,3072]{2,1,0:T(8,128)(2,1)S(1)} collective-permute-done((bf16[2,64,3072]{2,1,0:T(8,128)(2,1)S(1)}, bf16[2,64,3072]{2,1,0:T(8,128)(2,1)S(1)}, u32[]{:S(2)}, u32[]{:S(2)}) %collective-permute-start.19) | collective-permute-done | bytes 786464 | tf_op jit(solution)/shard_map/ppermute | solution.py:121
  790.8 5.5 all-reduce
  797.5 10.1 %collective-permute-done.20 = bf16[64,3072]{1,0:T(8,128)(2,1)S(1)} collective-permute-done((bf16[64,3072]{1,0:T(8,128)(2,1)}, bf16[64,3072]{1,0:T(8,128)(2,1)S(1)}, u32[]{:S(2)}, u32[]{:S(2)}) %collective-permute-start.20) | collective-permute-done | bytes 393248 | tf_op jit(solution)/shard_map/ppermute | solution.py:121
  (199 shorter events, 73.0 us)
Async XLA Ops:
  7.2 344.2 %all-gather.5.cloned.1.call-start = ((), (), s32[]{:S(2)}) async-start(), calls=%async_computation.1 | async-start | bytes 6684672 | tf_op jit(solution)/shard_map/all_gather | solution.py:133
  7.9 343.4 %all-gather.3.cloned.1.call-start = ((), (), s32[]{:S(2)}) async-start(), calls=%async_computation | async-start | bytes 6684672 | tf_op jit(solution)/shard_map/all_gather | solution.py:133
  24.6 218.7 %copy-start.18 = (bf16[768,512]{1,0:T(8,128)(2,1)}, bf16[768,512]{1,0:T(8,128)(2,1)S(1)}, u32[]{:S(2)}) copy-start(bf16[768,512]{1,0:T(8,128)(2,1)S(1)} %get-tuple-element.26) | copy-start | bytes 2359300
  24.6 218.7 %copy-start.20 = (bf16[768,512]{1,0:T(8,128)(2,1)}, bf16[768,512]{1,0:T(8,128)(2,1)S(1)}, u32[]{:S(2)}) copy-start(bf16[768,512]{1,0:T(8,128)(2,1)S(1)} %get-tuple-element.32) | copy-start | bytes 2359300
  24.6 11.6 %collective-permute-start.13 = (bf16[768,512]{1,0:T(8,128)(2,1)}, bf16[768,512]{1,0:T(8,128)(2,1)}, u32[]{:S(2)}, u32[]{:S(2)}) collective-permute-start(bf16[768,512]{1,0:T(8,128)(2,1)} %get-tuple-element.27), channel_id=1, source_target_pairs={{0,8},{8,0},{16,24},{24,16},{1,9},{9,1},{17,25},{25,17},{2,10},{10... | collective-permute-start | bytes 2359304 | tf_op jit(solution)/shard_map/ppermute | solution.py:121
  24.7 22.7 %collective-permute-start.11 = (bf16[768,512]{1,0:T(8,128)(2,1)}, bf16[768,512]{1,0:T(8,128)(2,1)}, u32[]{:S(2)}, u32[]{:S(2)}) collective-permute-start(bf16[768,512]{1,0:T(8,128)(2,1)} %get-tuple-element.29), channel_id=1, source_target_pairs={{0,24},{8,16},{16,8},{24,0},{1,25},{9,17},{17,9},{25,1},{2,26},{10... | collective-permute-start | bytes 2359304 | tf_op jit(solution)/shard_map/ppermute | solution.py:121
  26.8 52.4 %collective-permute-start.10 = (bf16[768,512]{1,0:T(8,128)(2,1)}, bf16[768,512]{1,0:T(8,128)(2,1)}, u32[]{:S(2)}, u32[]{:S(2)}) collective-permute-start(bf16[768,512]{1,0:T(8,128)(2,1)} %get-tuple-element.30), channel_id=1, source_target_pairs={{0,16},{8,24},{16,0},{24,8},{1,17},{9,25},{17,1},{25,9},{2,18},{10... | collective-permute-start | bytes 2359304 | tf_op jit(solution)/shard_map/ppermute | solution.py:121
  26.9 54.3 %collective-permute-start.9 = (bf16[768,512]{1,0:T(8,128)(2,1)}, bf16[768,512]{1,0:T(8,128)(2,1)}, u32[]{:S(2)}, u32[]{:S(2)}) collective-permute-start(bf16[768,512]{1,0:T(8,128)(2,1)} %get-tuple-element.31), channel_id=1, source_target_pairs={{0,8},{8,0},{16,24},{24,16},{1,9},{9,1},{17,25},{25,17},{2,10},{10... | collective-permute-start | bytes 2359304 | tf_op jit(solution)/shard_map/ppermute | solution.py:121
  27.0 68.6 %collective-permute-start.7 = (bf16[768,512]{1,0:T(8,128)(2,1)}, bf16[768,512]{1,0:T(8,128)(2,1)}, u32[]{:S(2)}, u32[]{:S(2)}) collective-permute-start(bf16[768,512]{1,0:T(8,128)(2,1)} %get-tuple-element.33), channel_id=1, source_target_pairs={{0,24},{8,16},{16,8},{24,0},{1,25},{9,17},{17,9},{25,1},{2,26},{10... | collective-permute-start | bytes 2359304 | tf_op jit(solution)/shard_map/ppermute | solution.py:121
  32.1 211.2 %copy-start.25 = (bf16[768,384]{1,0:T(8,128)(2,1)}, bf16[768,384]{1,0:T(8,128)(2,1)S(1)}, u32[]{:S(2)}) copy-start(bf16[768,384]{1,0:T(8,128)(2,1)S(1)} %get-tuple-element.62) | copy-start | bytes 1769476
  32.1 211.2 %copy-start.26 = (bf16[768,384]{1,0:T(8,128)(2,1)}, bf16[768,384]{1,0:T(8,128)(2,1)S(1)}, u32[]{:S(2)}) copy-start(bf16[768,384]{1,0:T(8,128)(2,1)S(1)} %get-tuple-element.99) | copy-start | bytes 1769476
  36.2 81.0 %collective-permute-start.6 = (bf16[768,512]{1,0:T(8,128)(2,1)}, bf16[768,512]{1,0:T(8,128)(2,1)}, u32[]{:S(2)}, u32[]{:S(2)}) collective-permute-start(bf16[768,512]{1,0:T(8,128)(2,1)} %get-tuple-element.34), channel_id=1, source_target_pairs={{0,16},{8,24},{16,0},{24,8},{1,17},{9,25},{17,1},{25,9},{2,18},{10... | collective-permute-start | bytes 2359304 | tf_op jit(solution)/shard_map/ppermute | solution.py:121
  47.4 70.4 %collective-permute-start.5 = (bf16[768,512]{1,0:T(8,128)(2,1)}, bf16[768,512]{1,0:T(8,128)(2,1)}, u32[]{:S(2)}, u32[]{:S(2)}) collective-permute-start(bf16[768,512]{1,0:T(8,128)(2,1)} %get-tuple-element.35), channel_id=1, source_target_pairs={{0,8},{8,0},{16,24},{24,16},{1,9},{9,1},{17,25},{25,17},{2,10},{10... | collective-permute-start | bytes 2359304 | tf_op jit(solution)/shard_map/ppermute | solution.py:121
  79.3 164.0 %collective-permute-start.1 = (bf16[768,1152]{1,0:T(8,128)(2,1)}, bf16[768,1152]{1,0:T(8,128)(2,1)}, u32[]{:S(2)}, u32[]{:S(2)}) collective-permute-start(bf16[768,1152]{1,0:T(8,128)(2,1)} %pad_maximum_fusion.6), channel_id=1, source_target_pairs={{0,16},{8,24},{16,0},{24,8},{1,17},{9,25},{17,1},{25,9},{2,18},{10... | collective-permute-start | bytes 5308424 | tf_op jit(solution)/shard_map/ppermute | solution.py:121
  81.2 162.0 %collective-permute-start.2 = (bf16[768,1152]{1,0:T(8,128)(2,1)}, bf16[768,1152]{1,0:T(8,128)(2,1)}, u32[]{:S(2)}, u32[]{:S(2)}) collective-permute-start(bf16[768,1152]{1,0:T(8,128)(2,1)} %pad_maximum_fusion.7), channel_id=1, source_target_pairs={{0,24},{8,16},{16,8},{24,0},{1,25},{9,17},{17,9},{25,1},{2,26},{10... | collective-permute-start | bytes 5308424 | tf_op jit(solution)/shard_map/ppermute | solution.py:121
  95.6 147.7 %collective-permute-start = (bf16[768,1152]{1,0:T(8,128)(2,1)}, bf16[768,1152]{1,0:T(8,128)(2,1)}, u32[]{:S(2)}, u32[]{:S(2)}) collective-permute-start(bf16[768,1152]{1,0:T(8,128)(2,1)} %pad_maximum_fusion.5), channel_id=1, source_target_pairs={{0,8},{8,0},{16,24},{24,16},{1,9},{9,1},{17,25},{25,17},{2,10},{10... | collective-permute-start | bytes 5308424 | tf_op jit(solution)/shard_map/ppermute | solution.py:121
  117.2 109.0 %collective-permute-start.15 = (bf16[768,512]{1,0:T(8,128)(2,1)}, bf16[768,512]{1,0:T(8,128)(2,1)}, u32[]{:S(2)}, u32[]{:S(2)}) collective-permute-start(bf16[768,512]{1,0:T(8,128)(2,1)} %get-tuple-element.36), channel_id=1, source_target_pairs={{0,24},{8,16},{16,8},{24,0},{1,25},{9,17},{17,9},{25,1},{2,26},{10... | collective-permute-start | bytes 2359304 | tf_op jit(solution)/shard_map/ppermute | solution.py:121
  117.7 125.5 %collective-permute-start.14 = (bf16[768,512]{1,0:T(8,128)(2,1)}, bf16[768,512]{1,0:T(8,128)(2,1)}, u32[]{:S(2)}, u32[]{:S(2)}) collective-permute-start(bf16[768,512]{1,0:T(8,128)(2,1)} %get-tuple-element.37), channel_id=1, source_target_pairs={{0,16},{8,24},{16,0},{24,8},{1,17},{9,25},{17,1},{25,9},{2,18},{10... | collective-permute-start | bytes 2359304 | tf_op jit(solution)/shard_map/ppermute | solution.py:121
  361.6 164.0 %copy-start.2 = (bf16[1024,384]{1,0:T(8,128)(2,1)}, bf16[1024,384]{1,0:T(8,128)(2,1)S(1)}, u32[]{:S(2)}) copy-start(bf16[1024,384]{1,0:T(8,128)(2,1)S(1)} %convolution_convert_fusion.4.g_own) | copy-start | bytes 2359300
  364.5 15.9 %slice-start = ((s8[9437184]{0:T(1024)(128)(4,1)}), s8[1048576]{0:T(1024)(128)(4,1)S(1)}, s32[]{:S(2)}) async-start(s8[9437184]{0:T(1024)(128)(4,1)} %bitcast.68), calls=%async_computation.2 | async-start | bytes 2097152
  364.5 15.9 %slice-start.1 = ((s8[9437184]{0:T(1024)(128)(4,1)}), s8[4194304]{0:T(1024)(128)(4,1)S(1)}, s32[]{:S(2)}) async-start(s8[9437184]{0:T(1024)(128)(4,1)} %bitcast.68), calls=%async_computation.3 | async-start | bytes 8388608
  392.3 157.8 %collective-permute-start.16 = (bf16[1024,512]{0,1:T(8,128)(2,1)}, bf16[1024,512]{0,1:T(8,128)(2,1)}, u32[]{:S(2)}, u32[]{:S(2)}) collective-permute-start(bf16[1024,512]{0,1:T(8,128)(2,1)} %fusion.48), channel_id=1, source_target_pairs={{0,1},{1,0},{2,3},{3,2},{4,5},{5,4},{6,7},{7,6},{8,9},{9,8},{10,11... | collective-permute-start | bytes 3145736 | tf_op jit(solution)/shard_map/ppermute | solution.py:121
  407.2 190.0 %collective-permute-start.3 = (bf16[1024,1152]{1,0:T(8,128)(2,1)S(1)}, bf16[1024,1152]{1,0:T(8,128)(2,1)S(1)}, u32[]{:S(2)}, u32[]{:S(2)}) collective-permute-start(bf16[1024,1152]{1,0:T(8,128)(2,1)S(1)} %fusion.13.q_own.k_own.v_own), channel_id=1, source_target_pairs={{0,1},{1,0},{2,3},{3,2},{4,5},{5,4},{6,7},{7,6},{8,9},{9,8},{10,11... | collective-permute-start | bytes 7077896 | tf_op jit(solution)/shard_map/ppermute | solution.py:121
  407.6 78.6 %collective-permute-start.21 = (bf16[256,1536]{0,1:T(8,128)(2,1)}, bf16[256,1536]{0,1:T(8,128)(2,1)}, u32[]{:S(2)}, u32[]{:S(2)}) collective-permute-start(bf16[256,1536]{0,1:T(8,128)(2,1)} %convolution_convert_fusion.3), channel_id=1, source_target_pairs={{0,1},{1,0},{2,3},{3,2},{4,5},{5,4},{6,7},{7,6},{8,9},{9,8},{10,11... | collective-permute-start | bytes 2359304 | tf_op jit(solution)/shard_map/ppermute | solution.py:121
  409.3 93.7 %collective-permute-start.24 = (bf16[256,1536]{0,1:T(8,128)(2,1)}, bf16[256,1536]{0,1:T(8,128)(2,1)}, u32[]{:S(2)}, u32[]{:S(2)}) collective-permute-start(bf16[256,1536]{0,1:T(8,128)(2,1)} %convolution_convert_fusion.2), channel_id=1, source_target_pairs={{0,1},{1,0},{2,3},{3,2},{4,5},{5,4},{6,7},{7,6},{8,9},{9,8},{10,11... | collective-permute-start | bytes 2359304 | tf_op jit(solution)/shard_map/ppermute | solution.py:121
  417.7 85.3 %copy-start.28 = (bf16[512,1536]{0,1:T(8,128)(2,1)S(1)}, bf16[512,1536]{0,1:T(8,128)(2,1)}, u32[]{:S(2)}) copy-start(bf16[512,1536]{0,1:T(8,128)(2,1)} %fusion.42) | copy-start | bytes 4718596
  417.7 107.8 %collective-permute-start.12 = (bf16[1024,512]{0,1:T(8,128)(2,1)}, bf16[1024,512]{0,1:T(8,128)(2,1)}, u32[]{:S(2)}, u32[]{:S(2)}) collective-permute-start(bf16[1024,512]{0,1:T(8,128)(2,1)} %fusion.51), channel_id=1, source_target_pairs={{0,1},{1,0},{2,3},{3,2},{4,5},{5,4},{6,7},{7,6},{8,9},{9,8},{10,11... | collective-permute-start | bytes 3145736 | tf_op jit(solution)/shard_map/ppermute | solution.py:121
  426.6 100.7 %copy-start.32 = (bf16[1024,512]{0,1:T(8,128)(2,1)S(1)}, bf16[1024,512]{0,1:T(8,128)(2,1)}, u32[]{:S(2)}) copy-start(bf16[1024,512]{0,1:T(8,128)(2,1)} %fusion.51) | copy-start | bytes 3145732
  486.2 61.7 %collective-permute-start.8 = (bf16[1024,512]{0,1:T(8,128)(2,1)}, bf16[1024,512]{0,1:T(8,128)(2,1)S(1)}, u32[]{:S(2)}, u32[]{:S(2)}) collective-permute-start(bf16[1024,512]{0,1:T(8,128)(2,1)} %fusion.54), channel_id=1, source_target_pairs={{0,1},{1,0},{2,3},{3,2},{4,5},{5,4},{6,7},{7,6},{8,9},{9,8},{10,11... | collective-permute-start | bytes 3145736 | tf_op jit(solution)/shard_map/ppermute | solution.py:121
  503.0 78.5 %collective-permute-start.22 = (bf16[512,1536]{0,1:T(8,128)(2,1)S(1)}, bf16[512,1536]{0,1:T(8,128)(2,1)S(1)}, u32[]{:S(2)}, u32[]{:S(2)}) collective-permute-start(bf16[512,1536]{0,1:T(8,128)(2,1)S(1)} %copy-done.28), channel_id=1, source_target_pairs={{0,1},{1,0},{2,3},{3,2},{4,5},{5,4},{6,7},{7,6},{8,9},{9,8},{10,11... | collective-permute-start | bytes 4718600 | tf_op jit(solution)/shard_map/ppermute | solution.py:121
  507.3 40.6 %copy-start.33 = (bf16[1024,512]{0,1:T(8,128)(2,1)S(1)}, bf16[1024,512]{0,1:T(8,128)(2,1)}, u32[]{:S(2)}) copy-start(bf16[1024,512]{0,1:T(8,128)(2,1)} %fusion.54) | copy-start | bytes 3145732
  525.5 71.7 %collective-permute-start.4 = (bf16[1024,384]{1,0:T(8,128)(2,1)S(1)}, bf16[1024,384]{1,0:T(8,128)(2,1)S(1)}, u32[]{:S(2)}, u32[]{:S(2)}) collective-permute-start(bf16[1024,384]{1,0:T(8,128)(2,1)S(1)} %convolution_convert_fusion.4.g_own), channel_id=1, source_target_pairs={{0,1},{1,0},{2,3},{3,2},{4,5},{5,4},{6,7},{7,6},{8,9},{9,8},{10,11... | collective-permute-start | bytes 2359304 | tf_op jit(solution)/shard_map/ppermute | solution.py:121
  553.9 43.4 %copy-start.3 = (bf16[1024,384]{1,0:T(8,128)(2,1)S(1)}, bf16[1024,384]{1,0:T(8,128)(2,1)}, u32[]{:S(2)}) copy-start(bf16[1024,384]{1,0:T(8,128)(2,1)} %copy-done.2) | copy-start | bytes 2359300
  628.2 14.3 %copy-start.4 = (bf16[1024,512]{0,1:T(8,128)(2,1)S(1)}, bf16[1024,512]{0,1:T(8,128)(2,1)}, u32[]{:S(2)}) copy-start(bf16[1024,512]{0,1:T(8,128)(2,1)} %get-tuple-element.75) | copy-start | bytes 3145732
  628.2 14.3 %copy-start.5 = (bf16[1024,512]{0,1:T(8,128)(2,1)S(1)}, bf16[1024,512]{0,1:T(8,128)(2,1)}, u32[]{:S(2)}) copy-start(bf16[1024,512]{0,1:T(8,128)(2,1)} %get-tuple-element.77) | copy-start | bytes 3145732
  628.2 14.3 %copy-start.6 = (bf16[1024,512]{0,1:T(8,128)(2,1)S(1)}, bf16[1024,512]{0,1:T(8,128)(2,1)}, u32[]{:S(2)}) copy-start(bf16[1024,512]{0,1:T(8,128)(2,1)} %get-tuple-element.73) | copy-start | bytes 3145732
  628.2 14.3 %copy-start.7 = (bf16[1024,384]{0,1:T(8,128)(2,1)S(1)}, bf16[1024,384]{0,1:T(8,128)(2,1)}, u32[]{:S(2)}) copy-start(bf16[1024,384]{0,1:T(8,128)(2,1)} %copy.10) | copy-start | bytes 2359300
  642.5 20.6 %collective-permute-start.23 = (bf16[512,3072]{1,0:T(8,128)(2,1)}, bf16[512,3072]{1,0:T(8,128)(2,1)}, u32[]{:S(2)}, u32[]{:S(2)}) collective-permute-start(bf16[512,3072]{1,0:T(8,128)(2,1)} %convolution_convert_fusion.1), channel_id=1, source_target_pairs={{0,8},{8,0},{16,24},{24,16},{1,9},{9,1},{17,25},{25,17},{2,10},{10... | collective-permute-start | bytes 9437192 | tf_op jit(solution)/shard_map/ppermute | solution.py:121
  645.1 13.6 %copy-start.13 = (f32[1024,512]{0,1:T(8,128)S(1)}, f32[1024,512]{0,1:T(8,128)}, u32[]{:S(2)}) copy-start(f32[1024,512]{0,1:T(8,128)} %get-tuple-element.76) | copy-start | bytes 6291460
  658.1 23.1 %collective-permute-start.17 = (bf16[512,3072]{1,0:T(8,128)(2,1)}, bf16[512,3072]{1,0:T(8,128)(2,1)}, u32[]{:S(2)}, u32[]{:S(2)}) collective-permute-start(bf16[512,3072]{1,0:T(8,128)(2,1)} %convolution_convert_fusion), channel_id=1, source_target_pairs={{0,8},{8,0},{16,24},{24,16},{1,9},{9,1},{17,25},{25,17},{2,10},{10... | collective-permute-start | bytes 9437192 | tf_op jit(solution)/shard_map/ppermute | solution.py:121
  667.3 13.9 %copy-start.8 = (bf16[1024,384]{0,1:T(8,128)(2,1)S(1)}, bf16[1024,384]{0,1:T(8,128)(2,1)}, u32[]{:S(2)}) copy-start(bf16[1024,384]{0,1:T(8,128)(2,1)} %copy.10) | copy-start | bytes 2359300
  679.7 37.5 %collective-permute-start.25 = (bf16[256,3072]{1,0:T(8,128)(2,1)}, bf16[256,3072]{1,0:T(8,128)(2,1)}, u32[]{:S(2)}, u32[]{:S(2)}) collective-permute-start(bf16[256,3072]{1,0:T(8,128)(2,1)} %fusion.12), channel_id=1, source_target_pairs={{0,16},{8,24},{16,0},{24,8},{1,17},{9,25},{17,1},{25,9},{2,18},{10... | collective-permute-start | bytes 4718600 | tf_op jit(solution)/shard_map/ppermute | solution.py:121
  690.7 59.7 %collective-permute-start.18 = (bf16[256,3072]{1,0:T(8,128)(2,1)}, bf16[256,3072]{1,0:T(8,128)(2,1)}, u32[]{:S(2)}, u32[]{:S(2)}) collective-permute-start(bf16[256,3072]{1,0:T(8,128)(2,1)} %add_convert_fusion.1), channel_id=1, source_target_pairs={{0,16},{8,24},{16,0},{24,8},{1,17},{9,25},{17,1},{25,9},{2,18},{10... | collective-permute-start | bytes 4718600 | tf_op jit(solution)/shard_map/ppermute | solution.py:121
  735.4 26.1 %collective-permute-start.26 = (bf16[2,64,3072]{2,1,0:T(8,128)(2,1)S(1)}, bf16[2,64,3072]{2,1,0:T(8,128)(2,1)S(1)}, u32[]{:S(2)}, u32[]{:S(2)}) collective-permute-start(bf16[2,64,3072]{2,1,0:T(8,128)(2,1)S(1)} %fusion.107), channel_id=1, source_target_pairs={{0,2},{2,0},{4,6},{6,4},{1,3},{3,1},{5,7},{7,5},{8,10},{10,8},{12,... | collective-permute-start | bytes 2359304 | tf_op jit(solution)/shard_map/ppermute | solution.py:121
  759.8 27.5 %collective-permute-start.19 = (bf16[2,64,3072]{2,1,0:T(8,128)(2,1)S(1)}, bf16[2,64,3072]{2,1,0:T(8,128)(2,1)S(1)}, u32[]{:S(2)}, u32[]{:S(2)}) collective-permute-start(bf16[2,64,3072]{2,1,0:T(8,128)(2,1)S(1)} %fusion.106), channel_id=1, source_target_pairs={{0,2},{2,0},{4,6},{6,4},{1,3},{3,1},{5,7},{7,5},{8,10},{10,8},{12,... | collective-permute-start | bytes 2359304 | tf_op jit(solution)/shard_map/ppermute | solution.py:121
  761.8 28.3 %collective-permute-start.27 = (bf16[64,3072]{1,0:T(8,128)(2,1)S(1)}, bf16[64,3072]{1,0:T(8,128)(2,1)S(1)}, u32[]{:S(2)}, u32[]{:S(2)}) collective-permute-start(bf16[64,3072]{1,0:T(8,128)(2,1)S(1)} %fusion.148), channel_id=1, source_target_pairs={{0,4},{2,6},{4,0},{6,2},{1,5},{3,7},{5,1},{7,3},{8,12},{10,14},{12... | collective-permute-start | bytes 1179656 | tf_op jit(solution)/shard_map/ppermute | solution.py:121
  787.6 20.0 %copy-start.27 = (bf16[64,3072]{1,0:T(8,128)(2,1)S(1)}, bf16[64,3072]{1,0:T(8,128)(2,1)}, u32[]{:S(2)}) copy-start(bf16[64,3072]{1,0:T(8,128)(2,1)} %param.9) | copy-start | bytes 1179652
  788.4 19.2 %collective-permute-start.20 = (bf16[64,3072]{1,0:T(8,128)(2,1)}, bf16[64,3072]{1,0:T(8,128)(2,1)S(1)}, u32[]{:S(2)}, u32[]{:S(2)}) collective-permute-start(bf16[64,3072]{1,0:T(8,128)(2,1)} %fusion.147), channel_id=1, source_target_pairs={{0,4},{2,6},{4,0},{6,2},{1,5},{3,7},{5,1},{7,3},{8,12},{10,14},{12... | collective-permute-start | bytes 1179656 | tf_op jit(solution)/shard_map/ppermute | solution.py:121
  (30 other events, 192.9 us)
Sparse Core Ops, SparseCore 0:
  10.3 81.9 all-gather.4
  95.2 80.4 all-gather.2

commit v4 on v3

--- a/solution.py
+++ b/solution.py
@@ -121,51 +121,182 @@
     return lax.ppermute(block, axis, pairs)
 
 
+VMEM_LIMIT = 48 * 1024 * 1024
+
+
+def params():
+    return pltpu.CompilerParams(vmem_limit_bytes=VMEM_LIMIT)
+
+
+def cost(flops, *arrays):
+    moved = sum(math.prod(array.shape) * array.dtype.itemsize for array in arrays)
+    return pl.CostEstimate(flops=flops, bytes_accessed=moved, transcendentals=0)
+
+
+def copy_kernel(rows_ref, columns_ref, value_ref, out_ref):
+    out_ref[...] = value_ref[...]
+
+
+def pick_blocks(value, row_index, column_index):
+    rows, columns = value.shape
+    block = (rows // row_index.shape[0], columns // column_index.shape[0])
+    if block[1] % 128:
+        grid_of = (row_index.shape[0], block[0], column_index.shape[0], block[1])
+        picked = value.reshape(grid_of)[row_index][:, :, column_index]
+        return picked.reshape(rows, columns)
+    return pl.pallas_call(
+        copy_kernel,
+        grid_spec=pltpu.PrefetchScalarGridSpec(
+            num_scalar_prefetch=2,
+            grid=(row_index.shape[0], column_index.shape[0]),
+            in_specs=[pl.BlockSpec(block, lambda i, j, row, column: (row[i], column[j]))],
+            out_specs=pl.BlockSpec(block, lambda i, j, row, column: (i, j)),
+        ),
+        out_shape=jax.ShapeDtypeStruct(value.shape, value.dtype),
+        compiler_params=params(),
+        cost_estimate=cost(0, value, value),
+        name="pick_blocks",
+    )(row_index, column_index, value)
+
+
+def in_kernel(rows_ref, *refs):
+    pieces, out_ref = refs[:-1], refs[-1]
+    depth = pieces[0].shape[0]
+    total = None
+    for place, piece in enumerate(pieces):
+        part = dot(rows_ref[:, place * depth : (place + 1) * depth], piece[...])
+        total = part if total is None else total + part
+    out_ref[...] = total.astype(out_ref.dtype)
+
+
+def in_product(rows, pieces):
+    count = rows.shape[0]
+    depth, columns = pieces[0].shape
+    tile = 384 if columns % 384 == 0 else 256
+    out = jax.ShapeDtypeStruct((count, columns), jnp.bfloat16)
+    return pl.pallas_call(
+        in_kernel,
+        grid=(columns // tile,),
+        in_specs=[pl.BlockSpec(rows.shape, lambda n: (0, 0))]
+        + [pl.BlockSpec((depth, tile), lambda n: (0, n)) for _ in pieces],
+        out_specs=pl.BlockSpec((count, tile), lambda n: (0, n)),
+        out_shape=out,
+        compiler_params=params(),
+        cost_estimate=cost(2 * count * columns * rows.shape[1], rows, out, *pieces),
+        name="in_product",
+    )(rows, *pieces)
+
+
+def out_product(mixed, acts, w_attn_out, w_mlp_out, start, count, add, add_start, kind):
+    columns = w_attn_out.shape[1]
+    tile = 512 if columns % 512 == 0 else 256
+
+    def rows_spec(value):
+        return pl.BlockSpec((count, value.shape[1]), lambda n: (start // count, 0))
+
+    def columns_spec(value):
+        return pl.BlockSpec((value.shape[0], tile), lambda n: (0, n))
+
+    operands = [mixed, *acts, w_attn_out, w_mlp_out]
+    specs = [rows_spec(mixed), *(rows_spec(act) for act in acts)]
+    specs += [columns_spec(w_attn_out), columns_spec(w_mlp_out)]
+    if add is not None:
+        operands.append(add)
+        specs.append(pl.BlockSpec((count, tile), lambda n: (add_start // count, n)))
+    depth = w_attn_out.shape[0] + w_mlp_out.shape[0]
+
+    def kernel(*refs):
+        n_acts = len(acts)
+        attn_ref, mlp_ref, out_ref = refs[n_acts + 1], refs[n_acts + 2], refs[-1]
+        total = dot(refs[0][...], attn_ref[...])
+        row = 0
+        for act in refs[1 : n_acts + 1]:
+            total = total + dot(act[...], mlp_ref[row : row + act.shape[1], :])
+            row += act.shape[1]
+        if add is not None:
+            total = total + refs[n_acts + 3][...].astype(jnp.float32)
+        out_ref[...] = total.astype(out_ref.dtype)
+
+    out = jax.ShapeDtypeStruct((count, columns), kind)
+    return pl.pallas_call(
+        kernel,
+        grid=(columns // tile,),
+        in_specs=specs,
+        out_specs=pl.BlockSpec((count, tile), lambda n: (0, n)),
+        out_shape=out,
+        compiler_params=params(),
+        cost_estimate=cost(2 * count * columns * depth, out, w_attn_out, w_mlp_out),
+        name="out_product",
+    )(*operands)
+
+
+def back_product(head_grads, mlp_grads, head_pieces, mlp_pieces, start, add, add_start, flip, kind):
+    count = mlp_grads[0].shape[0]
+    n_pieces, depth = len(head_pieces), head_pieces[0].shape[0]
+    tile = 256 if depth % 256 == 0 else depth
+    heads_width = head_grads[0].shape[1]
+    n_heads, n_mlp = len(head_grads), len(mlp_grads)
+    operands = [*head_grads, *mlp_grads]
+    specs = [pl.BlockSpec((count, heads_width), lambda n: (start // count, 0))] * n_heads
+    specs += [pl.BlockSpec(grad.shape, lambda n: (0, 0)) for grad in mlp_grads]
+    for place in range(n_pieces):
+        for piece in (head_pieces[place], *(cut[place] for cut in mlp_pieces)):
+            operands.append(piece)
+            specs.append(pl.BlockSpec((tile, piece.shape[1]), lambda n: (n, 0)))
+    if add is not None:
+        operands.append(add)
+        specs.append(
+            pl.BlockSpec((n_pieces, count, tile), lambda n: (0, add_start // count, n))
+        )
+
+    def kernel(*refs):
+        grads, weights = refs[: n_heads + n_mlp], refs[n_heads + n_mlp :]
+        out_ref = refs[-1]
+        for place in range(n_pieces):
+            group = weights[place * (n_mlp + 1) : (place + 1) * (n_mlp + 1)]
+            total = None
+            for index in range(n_heads):
+                columns = slice(index * heads_width, (index + 1) * heads_width)
+                part = back_dot(grads[index][...], group[0][:, columns])
+                total = part if total is None else total + part
+            for grad, weight in zip(grads[n_heads:], group[1:]):
+                total = total + back_dot(grad[...], weight[...])
+            if add is not None:
+                total = total + refs[-2][place ^ flip].astype(jnp.float32)
+            out_ref[place] = total.astype(out_ref.dtype)
+
+    width = n_heads * heads_width + sum(grad.shape[1] for grad in mlp_grads)
+    out = jax.ShapeDtypeStruct((n_pieces, count, depth), kind)
+    return pl.pallas_call(
+        kernel,
+        grid=(depth // tile,),
+        in_specs=specs,
+        out_specs=pl.BlockSpec((n_pieces, count, tile), lambda n: (0, 0, n)),
+        out_shape=out,
+        compiler_params=params(),
+        cost_estimate=cost(2 * count * depth * n_pieces * width, out, *operands),
+        name="back_product",
+    )(*operands)
+
+
 def body(layer_input, out_cotangent, w_query, w_key, w_value, w_mlp_in, w_attn_out, w_mlp_out):
     n_gx, n_gy, n_gz = (lax.axis_size(name) for name in ("gx", "gy", "gz"))
     me_x, me_y = lax.axis_index("gx"), lax.axis_index("gy")
     own_rows = layer_input.shape[0]
     image_rows = own_rows * n_gy
     depth = w_query.shape[0]
-    row_order = (3, 1, 2, 0)
-
-    def all_rows(block):
-        gathered = lax.all_gather(block, ("gx", "gy"), axis=0, tiled=True)
-        return jnp.concatenate(
-            [
-                lax.dynamic_slice_in_dim(gathered, (me_x ^ bit) * image_rows, image_rows, 0)
-                for bit in row_order
-            ],
-            axis=0,
-        )
-
-    def relative(value):
-        return jnp.concatenate(
-            [
-                lax.dynamic_slice_in_dim(value, (me_x ^ bit) * depth, depth, 1)
-                for bit in range(n_gx)
-            ],
-            axis=1,
-        )
-
-    def same(value, bit):
-        return value
-
-    def reordered(value, bit):
-        return jnp.concatenate(
-            [
-                lax.slice_in_dim(value, (place ^ bit) * depth, ((place ^ bit) + 1) * depth, axis=1)
-                for place in range(n_gx)
-            ],
-            axis=1,
-        )
+    row_index = me_x ^ jnp.array((3, 1, 2, 0), jnp.int32)
+    feature_index = me_x ^ jnp.arange(n_gx, dtype=jnp.int32)
+
+    def after(value, earlier):
+        return lax.optimization_barrier((value, earlier))[0]
 
     def others(part):
         if n_gz == 2:
             return trade(part, "gz", 1)
         return half(lax.psum(part.astype(jnp.float32), "gz") - part.astype(jnp.float32))
 
-    def columns_of(weights, cut, cuts):
+    def columns_of(weights, cut, cuts, earlier):
         pieces = []
         for bit in range(n_gx):
             slices = []
@@ -174,16 +305,18 @@
                 count = owned // cuts
                 start = (me_x ^ bit) * owned + cut * count
                 slices.append(lax.dynamic_slice_in_dim(weight, start, count, 1))
-            piece = jnp.concatenate(slices, axis=1) if len(slices) > 1 else slices[0]
-            pieces.append(piece if bit == 0 else trade(piece, "gx", bit))
-        return jnp.concatenate(pieces, axis=0)
-
-    def after(value, earlier):
-        return lax.optimization_barrier((value, earlier))[0]
+            pieces.append(jnp.concatenate(slices, axis=1) if len(slices) > 1 else slices[0])
+        if earlier is not None:
+            pieces = after(pieces, earlier)
+        return [piece if bit == 0 else trade(piece, "gx", bit) for bit, piece in enumerate(pieces)]
 
     mlp_cuts = 3
-    in_heads = columns_of((w_query, w_key, w_value), 0, 1)
-    in_mlp = [columns_of((w_mlp_in,), cut, mlp_cuts) for cut in range(mlp_cuts)]
+    in_heads = columns_of((w_query, w_key, w_value), 0, 1, None)
+    in_mlp = []
+    earlier = in_heads[2]
+    for cut in range(mlp_cuts):
+        in_mlp.append(columns_of((w_mlp_in,), cut, mlp_cuts, earlier))
+        earlier = in_mlp[-1][2]
 
     wide = layer_input.astype(jnp.float32)
     total, squares = lax.psum((jnp.sum(wide, axis=1), jnp.sum(wide * wide, axis=1)), "gz")
@@ -191,57 +324,80 @@
     spread = squares / D - center * center
     inverse = lax.rsqrt(spread + EPSILON)
     normed = (wide - center[:, None]) * inverse[:, None]
-    gathered_in = relative(all_rows(half(normed)))
-
-    heads_own = half(dot(gathered_in, in_heads))
+    normed_half = half(normed)
+    all_in = lax.all_gather(normed_half, ("gx", "gy"), axis=0, tiled=True)
+    all_cot = lax.all_gather(
+        after(out_cotangent, normed_half), ("gx", "gy"), axis=0, tiled=True
+    )
+    gathered_in = pick_blocks(all_in, row_index, feature_index)
+    gathered_cot = pick_blocks(all_cot, row_index, jnp.zeros((1,), jnp.int32))
+
+    heads_own = in_product(gathered_in, in_heads)
     heads_got = others(heads_own)
-    mlp_own = [half(dot(gathered_in, weight)) for weight in in_mlp]
+    mlp_own = [in_product(gathered_in, pieces) for pieces in in_mlp]
     mlp_got = [others(own) for own in mlp_own]
 
-    gathered_cot = all_rows(out_cotangent)
     mixed_own = half(back_dot(gathered_cot, w_attn_out))
     mixed_got = others(mixed_own)
 
-    mixed, query_grad, key_grad, value_grad = attend(heads_own, heads_got, mixed_own, mixed_got)
+    mixed, *head_grads = attend(heads_own, heads_got, mixed_own, mixed_got)
     pre = [wide_sum(own, got) for own, got in zip(mlp_own, mlp_got)]
-    acts = jnp.concatenate([mixed] + [half(gelu(part)) for part in pre], axis=1)
-    w_out = jnp.concatenate([w_attn_out, w_mlp_out], axis=0)
-    w_in = jnp.concatenate([in_heads] + in_mlp, axis=1)
+    acts = [half(gelu(part)) for part in pre]
     late_cot = after(gathered_cot, mlp_own[-1])
 
     def block_of(value, start, count):
-        return lax.slice_in_dim(value, start * image_rows, (start + count) * image_rows)
-
-    def forward_term(start, count):
-        return dot(block_of(acts, start, count), w_out)
-
-    def backward_term(start, count):
+        return lax.slice_in_dim(value, start, start + count)
+
+    def forward_term(start, count, add, add_start, flip, kind):
+        return out_product(mixed, acts, w_attn_out, w_mlp_out, start, count, add, add_start, kind)
+
+    def backward_term(start, count, add, add_start, flip, kind):
         act_own = half(back_dot(block_of(late_cot, start, count), w_mlp_out))
         grad = half(wide_sum(act_own, others(act_own)))
-        parts = [block_of(value, start, count) for value in (query_grad, key_grad, value_grad)]
         width = grad.shape[1] // mlp_cuts
-        for cut in range(mlp_cuts):
-            columns = grad[:, cut * width : (cut + 1) * width]
-            parts.append(gelu_back(block_of(pre[cut], start, count), columns))
-        return back_dot(jnp.concatenate(parts, axis=1), w_in)
-
-    def spread_rows(term, mapped):
-        from_core = mapped(trade(half(term(0, 2)), "gx", 1), 1)
-        to_x = half(term(2, 1) + from_core[:image_rows].astype(jnp.float32))
-        from_x = mapped(trade(to_x, "gx", 2), 2)
-        mine = term(3, 1) + wide_sum(from_core[image_rows:], from_x)
-        quarters = mine.reshape(2, 2, own_rows, mine.shape[1])
+        mlp_grads = [
+            gelu_back(block_of(pre[cut], start, count), grad[:, cut * width : (cut + 1) * width])
+            for cut in range(mlp_cuts)
+        ]
+        return back_product(
+            head_grads, mlp_grads, in_heads, in_mlp, start, add, add_start, flip, kind
+        )
+
+    def spread_rows(term, rows_axis, settled):
+        count = image_rows
+        from_core = trade(term(0, 2 * count, None, 0, 0, jnp.bfloat16), "gx", 1)
+        to_x = term(2 * count, count, from_core, 0, 1, jnp.bfloat16)
+        from_x = trade(to_x, "gx", 2)
+        mine = term(3 * count, count, from_core, count, 1, jnp.float32)
+        mine = mine + settled(from_x, 2).astype(jnp.float32)
+        lead = mine.shape[:rows_axis]
+        quarters = mine.reshape(lead + (2, 2, own_rows, mine.shape[-1]))
+
+        def at(value, axis, index):
+            return lax.index_in_dim(value, index, axis, keepdims=False)
+
         odd = me_y % 2 == 1
-        kept = jnp.where(odd, quarters[:, 1], quarters[:, 0])
-        sent = jnp.where(odd, quarters[:, 0], quarters[:, 1])
+        even_part, odd_part = (at(quarters, rows_axis + 1, index) for index in (0, 1))
+        kept, sent = jnp.where(odd, odd_part, even_part), jnp.where(odd, even_part, odd_part)
         pair = kept + trade(half(sent), "gy", 1).astype(jnp.float32)
         high = me_y >= 2
-        kept = jnp.where(high, pair[1], pair[0])
-        sent = jnp.where(high, pair[0], pair[1])
+        low_part, high_part = (at(pair, rows_axis, index) for index in (0, 1))
+        kept, sent = jnp.where(high, high_part, low_part), jnp.where(high, low_part, high_part)
         return kept + trade(half(sent), "gy", 2).astype(jnp.float32)
 
-    layer_out = half(wide + spread_rows(forward_term, same))
-    normed_grad = relative(spread_rows(backward_term, reordered))
+    layer_out = half(wide + spread_rows(forward_term, 0, lambda value, flip: value))
+
+    def settled(value, flip):
+        return jnp.stack([value[place ^ flip] for place in range(n_gx)])
+
+    by_piece = spread_rows(backward_term, 1, settled)
+    normed_grad = jnp.concatenate(
+        [
+            lax.dynamic_index_in_dim(by_piece, me_x ^ block, 0, keepdims=False)
+            for block in range(n_gx)
+        ],
+        axis=1,
+    )
     first, second = lax.psum(
         (jnp.sum(normed_grad, axis=1), jnp.sum(normed_grad * normed, axis=1)), "gz"
     )

time: 821 us -> 619 us (0.75)
  other arithmetic: 148 us -> 25.5 us
  Pallas kernels: 15.1 us -> 132 us
  matrix products: 131 us -> 29.1 us
  waiting for transfers between devices: 412 us -> 355 us
  local copies, waits for them, and re-layouts: 53.1 us -> 20.5 us
    pallas_call x0 -> x12, Pallas kernels: none -> 117 us  [the longest x4 35.1 us: in_product(): pl.pallas_call(in_kernel, grid=(columns // tile,), in_specs=[pl.BlockSpec...]
    concatenate x10 -> x4, other arithmetic: 119 us -> 4.27 us  [columns_of(): jnp.concatenate(slices, axis=1)]
    dot_general x7 -> x0, matrix products: 68.1 us -> none  [dot(): return jnp.dot(left, right, preferred_element_type=jnp.float32)]
    ppermute x28, waiting for transfers between devices: 411 us -> 354 us  [trade(): return lax.ppermute(block, axis, pairs)]
    dot_general x7 -> x4, matrix products: 63.3 us -> 29.1 us  [back_dot(): lax.dot_general(left, right, (((1,), (1,)), ((), ())), preferred_element_...]
    slice x17 -> x1, local copies, waits for them, and re-layouts: 13.3 us -> 1.47 us  [settled(): return jnp.stack([value[place ^ flip] for place in range(n_gx)])]
    concatenate x1 -> x0, local copies, waits for them, and re-layouts: 8.43 us -> none  [body(): w_out = jnp.concatenate([w_attn_out, w_mlp_out], axis=0)]
  transfers between devices with their start and end apart: 30 -> 30, of which waited for: 16 -> 14; matrix products, arithmetic and copies ran while one was open for 31% -> 10% of each run, Pallas kernels for 0% -> 17%
where the time goes in v4:
time: 619 us; the launch traced here: 618 us
  waiting for transfers between devices  355 us (57%)
  Pallas kernels  132 us (21%)
  starting transfers between devices  29.5 us (5%)
  matrix products  29.1 us (5%)
  other arithmetic  25.5 us (4%)
  local copies, waits for them, and re-layouts  20.5 us (3%)
  between operations  14.8 us (2%)
  blocking collectives  11.3 us (2%)
    ppermute x28, waiting for transfers between devices, trade(): return lax.ppermute(block, axis, pairs)  354 us
    pallas_call x4, Pallas kernels, in_product(): pl.pallas_call(in_kernel, grid=(columns // tile,), in_specs=[pl.BlockSpec...  35.1 us
    pallas_call x3, Pallas kernels, back_product(): pl.pallas_call(kernel, grid=(depth // tile,), in_specs=specs, out_specs=p...  34.8 us
    ppermute x28, starting transfers between devices, trade(): return lax.ppermute(block, axis, pairs)  29.4 us
    dot_general x4, matrix products, back_dot(): lax.dot_general(left, right, (((1,), (1,)), ((), ())), preferred_element_...  29.1 us
    pallas_call x3, Pallas kernels, out_product(): pl.pallas_call(kernel, grid=(columns // tile,), in_specs=specs, out_specs...  28.4 us
    pallas_call x2, Pallas kernels, pick_blocks(): pl.pallas_call(copy_kernel, grid_spec=pltpu.PrefetchScalarGridSpec(num_sc...  18.8 us
    pallas_call x1, Pallas kernels, attend(): pl.pallas_call(functools.partial(attend_kernel, scale=1.0 / math.sqrt(HEA...  15.1 us
  transfers between devices with their start and end apart: 30, of which 14 were waited for; matrix products, arithmetic and copies ran while one was open for 10% of the time, Pallas kernels for 17%

profile of v4, /device:TPU:0, one launch (start us, length us, event | category | flops | bytes accessed | tf_op | source)
XLA Modules:
  0.0 617.7 jit_solution(162583139568199196)
XLA Ops:
  8.4 5.9 all-reduce.1
  14.3 1.9 fusion.30
  17.0 3.1 constant_dynamic-slice_fusion.14
  20.8 1.9 constant_dynamic-slice_fusion.12
  24.1 2.0 collective-permute-start.1
  26.1 6.8 %constant_dynamic-slice_fusion = (bf16[768,512]{1,0:T(8,128)(2,1)}, bf16[768,512]{1,0:T(8,128)(2,1)}, bf16[768,512]{1,0:T(8,128)(2,1)S(1)}, bf16[768,512]{1,0:T(...) fusion(bf16[768,6144]{1,0:T(8,128)(2,1)} %param.14, ...), kind=kLoop, calls=%fused_computation.128 | loop fusion | bytes 18874416 | tf_op jit(solution)/shard_map/dynamic_slice | solution.py:307
  32.9 52.3 %collective-permute-done.1.refs_2_.refs_14_ = bf16[768,1152]{1,0:T(8,128)(2,1)S(1)} collective-permute-done((bf16[768,1152]{1,0:T(8,128)(2,1)}, bf16[768,1152]{1,0:T(8,128)(2,1)S(1)}, u32[]{:S(2)}, u32[]{:S(2)}) %collective-permute-start.1) | collective-permute-done | bytes 1769504 | tf_op jit(solution)/shard_map/ppermute | solution.py:121
  85.3 1.9 collective-permute-start.6
  88.6 14.3 %collective-permute-done.6.refs_2_.refs_15_ = bf16[768,512]{1,0:T(8,128)(2,1)S(1)} collective-permute-done((bf16[768,512]{1,0:T(8,128)(2,1)S(1)}, bf16[768,512]{1,0:T(8,128)(2,1)S(1)}, u32[]{:S(2)}, u32[]{:S(2)}) %collective-permute-start.6) | collective-permute-done | bytes 786464 | tf_op jit(solution)/shard_map/ppermute | solution.py:121
  103.0 1.9 collective-permute-start.10
  106.3 21.4 %collective-permute-done.10.refs_2_.refs_16_ = bf16[768,512]{1,0:T(8,128)(2,1)S(1)} collective-permute-done((bf16[768,512]{1,0:T(8,128)(2,1)S(1)}, bf16[768,512]{1,0:T(8,128)(2,1)S(1)}, u32[]{:S(2)}, u32[]{:S(2)}) %collective-permute-start.10) | collective-permute-done | bytes 786464 | tf_op jit(solution)/shard_map/ppermute | solution.py:121
  128.6 1.9 collective-permute-start.14
  130.9 12.0 %pick_blocks.2.rows_ref = bf16[1024,3072]{1,0:T(8,128)(2,1)} custom-call(s32[4]{0:T(128)S(1)} %broadcast_xor_fusion.rows_ref, s32[4]{0:T(128)S(1)} %iota_xor_fusion.columns_ref, bf16[1024,3072]{1,0:T(8,128)(2,1)} %all-gather.3.cloned.1.call-done.value_ref), custom_call_target="tpu_custom_call" | custom-call | bytes 12582912 | tf_op jit(solution)/shard_map/pick_blocks/pallas_call | solution.py:147
  142.9 56.4 %collective-permute-done.14.refs_2_.refs_17_ = bf16[768,512]{1,0:T(8,128)(2,1)} collective-permute-done((bf16[768,512]{1,0:T(8,128)(2,1)}, bf16[768,512]{1,0:T(8,128)(2,1)}, u32[]{:S(2)}, u32[]{:S(2)}) %collective-permute-start.14) | collective-permute-done | bytes 786464 | tf_op jit(solution)/shard_map/ppermute | solution.py:121
  199.4 11.2 %collective-permute-done.15.refs_3_.refs_21_ = bf16[768,512]{1,0:T(8,128)(2,1)} collective-permute-done((bf16[768,512]{1,0:T(8,128)(2,1)}, bf16[768,512]{1,0:T(8,128)(2,1)}, u32[]{:S(2)}, u32[]{:S(2)}) %collective-permute-start.15) | collective-permute-done | bytes 786464 | tf_op jit(solution)/shard_map/ppermute | solution.py:121
  210.6 1.9 collective-permute-start.11
  212.5 6.9 %in_product.7 = bf16[1024,512]{1,0:T(8,128)(2,1)S(1)} custom-call(bf16[1024,3072]{1,0:T(8,128)(2,1)} %pick_blocks.2.rows_ref, bf16[768,512]{1,0:T(8,128)(2,1)S(1)} %get-tuple-element.30.refs_0_.refs_9_, bf16[768,512]{1,0:T(8,128)(2,1)} %collective-permute-done.13.refs_1_.refs_13_, bf16[768,512]{1,0:T(8,128)(2,1)} %collective-permute-done.14.refs_2_.refs_17_, ...), custom_call_target="tpu_custom_call" | custom-call | flops 3221225472 | bytes 10485760 | tf_op jit(solution)/shard_map/in_product/pallas_call | solution.py:177
  220.3 6.8 %pick_blocks.3 = bf16[1024,3072]{1,0:T(8,128)(2,1)} custom-call(s32[4]{0:T(128)S(1)} %broadcast_xor_fusion.rows_ref, s32[1]{0:T(128)} %constant.79.clone.1.columns_ref, bf16[1024,3072]{1,0:T(8,128)(2,1)} %all-gather.5.cloned.1.call-done.value_ref), custom_call_target="tpu_custom_call" | custom-call | bytes 12582912 | tf_op jit(solution)/shard_map/pick_blocks/pallas_call | solution.py:147
  228.8 14.6 %in_product.4.q_own.k_own.v_own = bf16[1024,1152]{1,0:T(8,128)(2,1)} custom-call(bf16[1024,3072]{1,0:T(8,128)(2,1)} %pick_blocks.2.rows_ref, bf16[768,1152]{1,0:T(8,128)(2,1)S(1)} %pad_maximum_fusion.refs_0_.refs_6_, bf16[768,1152]{1,0:T(8,128)(2,1)} %collective-permute-done.refs_1_.refs_10_, bf16[768,1152]{1,0:T(8,128)(2,1)S(1)} %copy-done.11, ...), custom_call_target="tpu_custom_call" | custom-call | flops 7247757312 | bytes 15728640 | tf_op jit(solution)/shard_map/in_product/pallas_call | solution.py:177
  244.0 6.8 %in_product.6 = bf16[1024,512]{1,0:T(8,128)(2,1)S(1)} custom-call(bf16[1024,3072]{1,0:T(8,128)(2,1)} %pick_blocks.2.rows_ref, bf16[768,512]{1,0:T(8,128)(2,1)S(1)} %get-tuple-element.26.refs_0_.refs_8_, bf16[768,512]{1,0:T(8,128)(2,1)} %collective-permute-done.9.refs_1_.refs_12_, bf16[768,512]{1,0:T(8,128)(2,1)S(1)} %copy-done.15, ...), custom_call_target="tpu_custom_call" | custom-call | flops 3221225472 | bytes 10485760 | tf_op jit(solution)/shard_map/in_product/pallas_call | solution.py:177
  252.4 6.8 %in_product.5 = bf16[1024,512]{1,0:T(8,128)(2,1)S(1)} custom-call(bf16[1024,3072]{1,0:T(8,128)(2,1)} %pick_blocks.2.rows_ref, bf16[768,512]{1,0:T(8,128)(2,1)S(1)} %copy-done.8, bf16[768,512]{1,0:T(8,128)(2,1)} %collective-permute-done.5.refs_1_.refs_11_, bf16[768,512]{1,0:T(8,128)(2,1)S(1)} %copy-done.13, ...), custom_call_target="tpu_custom_call" | custom-call | flops 3221225472 | bytes 10485760 | tf_op jit(solution)/shard_map/in_product/pallas_call | solution.py:177
  259.8 9.6 %fusion.2 = bf16[512,1536]{1,0:T(8,128)(2,1)S(1)} fusion(bf16[1536,3072]{1,0:T(8,128)(2,1)} %refs_5_.5, bf16[1024,3072]{1,0:T(8,128)(2,1)} %pick_blocks.3), kind=kOutput, calls=%fused_computation.5 | convolution fusion | flops 4832624640 | bytes 14155776 | tf_op jit(solution)/shard_map/dot_general | solution.py:106
  270.9 5.8 convolution_convert_fusion.2.g_own
  276.7 49.6 %collective-permute-done.12 = bf16[1024,512]{1,0:T(8,128)(2,1)S(1)} collective-permute-done((bf16[1024,512]{1,0:T(8,128)(2,1)S(1)}, bf16[1024,512]{1,0:T(8,128)(2,1)S(1)}, u32[]{:S(2)}, u32[]{:S(2)}) %collective-permute-start.12) | collective-permute-done | bytes 1048608 | tf_op jit(solution)/shard_map/ppermute | solution.py:121
  328.4 20.4 %collective-permute-done.8 = bf16[1024,512]{1,0:T(8,128)(2,1)S(1)} collective-permute-done((bf16[1024,512]{1,0:T(8,128)(2,1)S(1)}, bf16[1024,512]{1,0:T(8,128)(2,1)S(1)}, u32[]{:S(2)}, u32[]{:S(2)}) %collective-permute-start.8) | collective-permute-done | bytes 1048608 | tf_op jit(solution)/shard_map/ppermute | solution.py:121
  349.4 2.6 convert_add_fusion.2
  351.9 30.5 %collective-permute-done.22 = bf16[512,1536]{1,0:T(8,128)(2,1)S(1)} collective-permute-done((bf16[512,1536]{1,0:T(8,128)(2,1)S(1)}, bf16[512,1536]{1,0:T(8,128)(2,1)S(1)}, u32[]{:S(2)}, u32[]{:S(2)}) %collective-permute-start.22) | collective-permute-done | bytes 1572896 | tf_op jit(solution)/shard_map/ppermute | solution.py:121
  384.3 14.4 %collective-permute-done.4.g_got = bf16[1024,384]{1,0:T(8,128)(2,1)S(1)} collective-permute-done((bf16[1024,384]{1,0:T(8,128)(2,1)S(1)}, bf16[1024,384]{1,0:T(8,128)(2,1)S(1)}, u32[]{:S(2)}, u32[]{:S(2)}) %collective-permute-start.4) | collective-permute-done | bytes 786464 | tf_op jit(solution)/shard_map/ppermute | solution.py:121
  398.7 15.1 %attend.1 = (bf16[1024,384]{1,0:T(8,128)(2,1)S(1)}, bf16[1024,384]{1,0:T(8,128)(2,1)S(1)}, bf16[1024,384]{1,0:T(8,128)(2,1)S(1)}, bf16[1024,384]{1,0:T(8,128)(2,1)S(1)}) custom-call(bf16[1024,1152]{1,0:T(8,128)(2,1)S(1)} %copy-done, bf16[1024,1152]{1,0:T(8,128)(2,1)S(1)} %collective-permute-done.3.q_got.k_got.v_got, bf16[1024,1152]{1,0:T(8,128)(2,1)S(1)} %copy-done, ...), custom_call_target="tpu_custom_call" | custom-call | flops 1207959552 | bytes 9437184 | tf_op jit(solution)/shard_map/attend/pallas_call | solution.py:75
  413.9 15.0 %back_product.3 = bf16[4,512,768]{2,1,0:T(8,128)(2,1)} custom-call(bf16[1024,384]{1,0:T(8,128)(2,1)S(1)} %get-tuple-element.34.refs_0_, bf16[1024,384]{1,0:T(8,128)(2,1)S(1)} %get-tuple-element.35.refs_1_, bf16[1024,384]{1,0:T(8,128)(2,1)S(1)} %get-tuple-element.36.refs_2_, bf16[512,512]{1,0:T(8,128)(2,1)S(1)} %get-tuple-element.92.refs_3_, ...), custom_call_target="tpu_custom_call" | custom-call | flops 8455716864 | bytes 23592960 | tf_op jit(solution)/shard_map/back_product/pallas_call | solution.py:270
  428.9 6.8 %convolution_convert_fusion.1 = bf16[256,1536]{1,0:T(8,128)(2,1)S(1)} fusion(bf16[1536,3072]{1,0:T(8,128)(2,1)} %refs_5_.5, bf16[1024,3072]{1,0:T(8,128)(2,1)} %pick_blocks.3), kind=kOutput, calls=%fused_computation.7 | convolution fusion | flops 2416312320 | bytes 11796480 | tf_op jit(solution)/shard_map/dot_general | solution.py:106
  435.8 1.8 collective-permute-start.21
  437.6 11.1 %out_product.3 = bf16[512,3072]{1,0:T(8,128)(2,1)} custom-call(bf16[1024,384]{1,0:T(8,128)(2,1)S(1)} %get-tuple-element.21.refs_0_, bf16[1024,512]{1,0:T(8,128)(2,1)S(1)} %get-tuple-element.83.refs_1_, bf16[1024,512]{1,0:T(8,128)(2,1)S(1)} %get-tuple-element.81.refs_2_, bf16[1024,512]{1,0:T(8,128)(2,1)S(1)} %get-tuple-element.79.refs_3_, ...), custom_call_target="tpu_custom_call" | custom-call | flops 6039797760 | bytes 14942208 | tf_op jit(solution)/shard_map/out_product/pallas_call | solution.py:221
  448.8 6.9 %convolution_convert_fusion = bf16[256,1536]{1,0:T(8,128)(2,1)S(1)} fusion(bf16[1536,3072]{1,0:T(8,128)(2,1)} %refs_5_.5, bf16[1024,3072]{1,0:T(8,128)(2,1)} %pick_blocks.3), kind=kOutput, calls=%fused_computation.6 | convolution fusion | flops 2416312320 | bytes 11796480 | tf_op jit(solution)/shard_map/dot_general | solution.py:106
  456.4 19.2 %collective-permute-done.24 = bf16[256,1536]{1,0:T(8,128)(2,1)S(1)} collective-permute-done((bf16[256,1536]{1,0:T(8,128)(2,1)S(1)}, bf16[256,1536]{1,0:T(8,128)(2,1)S(1)}, u32[]{:S(2)}, u32[]{:S(2)}) %collective-permute-start.24) | collective-permute-done | bytes 786464 | tf_op jit(solution)/shard_map/ppermute | solution.py:121
  475.8 2.1 fusion.65
  478.0 1.7 copy-done.31
  479.7 9.7 %back_product.5 = bf16[4,256,768]{2,1,0:T(8,128)(2,1)} custom-call(bf16[1024,384]{1,0:T(8,128)(2,1)S(1)} %get-tuple-element.34.refs_0_, bf16[1024,384]{1,0:T(8,128)(2,1)S(1)} %get-tuple-element.35.refs_1_, bf16[1024,384]{1,0:T(8,128)(2,1)S(1)} %get-tuple-element.36.refs_2_, bf16[256,512]{1,0:T(8,128)(2,1)S(1)} %get-tuple-element.76.refs_3_, ...), custom_call_target="tpu_custom_call" | custom-call | flops 4227858432 | bytes 24379392 | tf_op jit(solution)/shard_map/back_product/pallas_call | solution.py:270
  491.3 7.9 %out_product.5 = bf16[256,3072]{1,0:T(8,128)(2,1)S(1)} custom-call(bf16[1024,384]{1,0:T(8,128)(2,1)S(1)} %copy-done.24, bf16[1024,512]{1,0:T(8,128)(2,1)S(1)} %get-tuple-element.83.refs_1_, bf16[1024,512]{1,0:T(8,128)(2,1)S(1)} %get-tuple-element.81.refs_2_, bf16[1024,512]{1,0:T(8,128)(2,1)S(1)} %get-tuple-element.79.refs_3_, bf16[384,3072]{1,0:T(8,128)(2,1)} %refs_4_.5, ...), custom_call_target="tpu_custom_call" | custom-call | flops 3019898880 | bytes 13369344 | tf_op jit(solution)/shard_map/out_product/pallas_call | solution.py:221
  500.7 9.4 %out_product.4 = f32[256,3072]{1,0:T(8,128)} custom-call(bf16[1024,384]{1,0:T(8,128)(2,1)S(1)} %copy-done.24, bf16[1024,512]{1,0:T(8,128)(2,1)S(1)} %get-tuple-element.83.refs_1_, bf16[1024,512]{1,0:T(8,128)(2,1)S(1)} %get-tuple-element.81.refs_2_, bf16[1024,512]{1,0:T(8,128)(2,1)S(1)} %get-tuple-element.79.refs_3_, bf16[384,3072]{1,0:T(8,128)(2,1)} %refs_4_.5, ...), custom_call_target="tpu_custom_call" | custom-call | flops 3019898880 | bytes 14942208 | tf_op jit(solution)/shard_map/out_product/pallas_call | solution.py:221
  510.1 10.2 %back_product.4 = f32[4,256,768]{2,1,0:T(8,128)} custom-call(bf16[1024,384]{1,0:T(8,128)(2,1)S(1)} %copy-done.18, bf16[1024,384]{1,0:T(8,128)(2,1)S(1)} %copy-done.20, bf16[1024,384]{1,0:T(8,128)(2,1)S(1)} %copy-done.22, bf16[256,512]{1,0:T(8,128)(2,1)S(1)} %get-tuple-element.77.refs_3_, bf16[256,512]{1,0:T(8,128)(2,1)S(1)} %copy-done.26, ...), custom_call_target="tpu_custom_call" | custom-call | flops 4227858432 | bytes 25952256 | tf_op jit(solution)/shard_map/back_product/pallas_call | solution.py:270
  520.4 6.7 %collective-permute-done.25 = bf16[4,256,768]{2,1,0:T(8,128)(2,1)} collective-permute-done((bf16[4,256,768]{2,1,0:T(8,128)(2,1)}, bf16[4,256,768]{2,1,0:T(8,128)(2,1)}, u32[]{:S(2)}, u32[]{:S(2)}) %collective-permute-start.25) | collective-permute-done | bytes 1572896 | tf_op jit(solution)/shard_map/ppermute | solution.py:121
  531.5 27.6 %collective-permute-done.18 = bf16[256,3072]{1,0:T(8,128)(2,1)S(1)} collective-permute-done((bf16[256,3072]{1,0:T(8,128)(2,1)S(1)}, bf16[256,3072]{1,0:T(8,128)(2,1)S(1)}, u32[]{:S(2)}, u32[]{:S(2)}) %collective-permute-start.18) | collective-permute-done | bytes 1572896 | tf_op jit(solution)/shard_map/ppermute | solution.py:121
  565.5 2.7 collective-permute-start.27
  568.2 20.9 %collective-permute-done.19 = bf16[2,64,3072]{2,1,0:T(8,128)(2,1)} collective-permute-done((bf16[2,64,3072]{2,1,0:T(8,128)(2,1)}, bf16[2,64,3072]{2,1,0:T(8,128)(2,1)}, u32[]{:S(2)}, u32[]{:S(2)}) %collective-permute-start.19) | collective-permute-done | bytes 786464 | tf_op jit(solution)/shard_map/ppermute | solution.py:121
  591.3 1.7 collective-permute-start.20
  593.7 5.5 all-reduce
  600.4 9.1 %collective-permute-done.20 = bf16[64,3072]{1,0:T(8,128)(2,1)S(1)} collective-permute-done((bf16[64,3072]{1,0:T(8,128)(2,1)}, bf16[64,3072]{1,0:T(8,128)(2,1)S(1)}, u32[]{:S(2)}, u32[]{:S(2)}) %collective-permute-start.20) | collective-permute-done | bytes 393248 | tf_op jit(solution)/shard_map/ppermute | solution.py:121
  (181 shorter events, 40.3 us)
Async XLA Ops:
  7.2 123.7 %all-gather.3.cloned.1.call-start = ((), (), s32[]{:S(2)}) async-start(), calls=%async_computation | async-start | bytes 6684672 | tf_op jit(solution)/shard_map/all_gather | solution.py:328
  16.2 204.1 %all-gather.5.cloned.1.call-start = ((), (), s32[]{:S(2)}) async-start(), calls=%async_computation.1 | async-start | bytes 6684672 | tf_op jit(solution)/shard_map/all_gather | solution.py:329
  24.1 61.2 %collective-permute-start.1 = (bf16[768,1152]{1,0:T(8,128)(2,1)}, bf16[768,1152]{1,0:T(8,128)(2,1)S(1)}, u32[]{:S(2)}, u32[]{:S(2)}) collective-permute-start(bf16[768,1152]{1,0:T(8,128)(2,1)} %pad_maximum_fusion.2), channel_id=1, source_target_pairs={{0,16},{8,24},{16,0},{24,8},{1,17},{9,25},{17,1},{25,9},{2,18},{10... | collective-permute-start | bytes 5308424 | tf_op jit(solution)/shard_map/ppermute | solution.py:121
  26.1 61.1 %copy-start.46 = (bf16[768,384]{1,0:T(8,128)(2,1)S(1)}, bf16[768,384]{1,0:T(8,128)(2,1)}, u32[]{:S(2)}) copy-start(bf16[768,384]{1,0:T(8,128)(2,1)} %get-tuple-element.69) | copy-start | bytes 1769476
  26.1 61.1 %copy-start.47 = (bf16[768,384]{1,0:T(8,128)(2,1)S(1)}, bf16[768,384]{1,0:T(8,128)(2,1)}, u32[]{:S(2)}) copy-start(bf16[768,384]{1,0:T(8,128)(2,1)} %get-tuple-element.103) | copy-start | bytes 1769476
  26.1 61.1 %copy-start.52 = (bf16[768,384]{1,0:T(8,128)(2,1)S(1)}, bf16[768,384]{1,0:T(8,128)(2,1)}, u32[]{:S(2)}) copy-start(bf16[768,384]{1,0:T(8,128)(2,1)} %get-tuple-element.61) | copy-start | bytes 1769476
  32.9 179.6 %copy-start.2 = (bf16[768,512]{1,0:T(8,128)(2,1)}, bf16[768,512]{1,0:T(8,128)(2,1)S(1)}, u32[]{:S(2)}) copy-start(bf16[768,512]{1,0:T(8,128)(2,1)S(1)} %get-tuple-element.30.refs_0_.refs_9_) | copy-start | bytes 2359300
  32.9 211.1 %copy-start.5 = (bf16[768,512]{1,0:T(8,128)(2,1)}, bf16[768,512]{1,0:T(8,128)(2,1)S(1)}, u32[]{:S(2)}) copy-start(bf16[768,512]{1,0:T(8,128)(2,1)S(1)} %get-tuple-element.26.refs_0_.refs_8_) | copy-start | bytes 2359300
  32.9 72.0 %copy-start.44 = (bf16[768,384]{1,0:T(8,128)(2,1)S(1)}, bf16[768,384]{1,0:T(8,128)(2,1)}, u32[]{:S(2)}) copy-start(bf16[768,384]{1,0:T(8,128)(2,1)} %get-tuple-element.68) | copy-start | bytes 1769476
  32.9 72.0 %copy-start.45 = (bf16[768,384]{1,0:T(8,128)(2,1)S(1)}, bf16[768,384]{1,0:T(8,128)(2,1)}, u32[]{:S(2)}) copy-start(bf16[768,384]{1,0:T(8,128)(2,1)} %get-tuple-element.104) | copy-start | bytes 1769476
  32.9 72.0 %copy-start.51 = (bf16[768,384]{1,0:T(8,128)(2,1)S(1)}, bf16[768,384]{1,0:T(8,128)(2,1)}, u32[]{:S(2)}) copy-start(bf16[768,384]{1,0:T(8,128)(2,1)} %get-tuple-element.60) | copy-start | bytes 1769476
  85.3 17.7 %collective-permute-start.6 = (bf16[768,512]{1,0:T(8,128)(2,1)S(1)}, bf16[768,512]{1,0:T(8,128)(2,1)S(1)}, u32[]{:S(2)}, u32[]{:S(2)}) collective-permute-start(bf16[768,512]{1,0:T(8,128)(2,1)S(1)} %get-tuple-element.24), channel_id=1, source_target_pairs={{0,16},{8,24},{16,0},{24,8},{1,17},{9,25},{17,1},{25,9},{2,18},{10... | collective-permute-start | bytes 2359304 | tf_op jit(solution)/shard_map/ppermute | solution.py:121
  88.5 42.1 %copy-start.55 = (s32[4]{0:T(128)S(1)}, s32[4]{0:T(128)}, u32[]{:S(2)}) copy-start(s32[4]{0:T(128)} %constant.91.clone) | copy-start | bytes 52
  88.5 42.1 %copy-start.42 = (bf16[768,384]{1,0:T(8,128)(2,1)S(1)}, bf16[768,384]{1,0:T(8,128)(2,1)}, u32[]{:S(2)}) copy-start(bf16[768,384]{1,0:T(8,128)(2,1)} %get-tuple-element.70) | copy-start | bytes 1769476
  88.5 42.1 %copy-start.43 = (bf16[768,384]{1,0:T(8,128)(2,1)S(1)}, bf16[768,384]{1,0:T(8,128)(2,1)}, u32[]{:S(2)}) copy-start(bf16[768,384]{1,0:T(8,128)(2,1)} %get-tuple-element.102) | copy-start | bytes 1769476
  88.5 42.1 %copy-start.50 = (bf16[768,384]{1,0:T(8,128)(2,1)S(1)}, bf16[768,384]{1,0:T(8,128)(2,1)}, u32[]{:S(2)}) copy-start(bf16[768,384]{1,0:T(8,128)(2,1)} %get-tuple-element.62) | copy-start | bytes 1769476
  88.5 138.6 %collective-permute-start = (bf16[768,1152]{1,0:T(8,128)(2,1)}, bf16[768,1152]{1,0:T(8,128)(2,1)}, u32[]{:S(2)}, u32[]{:S(2)}) collective-permute-start(bf16[768,1152]{1,0:T(8,128)(2,1)} %pad_maximum_fusion.1), channel_id=1, source_target_pairs={{0,8},{8,0},{16,24},{24,16},{1,9},{9,1},{17,25},{25,17},{2,10},{10... | collective-permute-start | bytes 5308424 | tf_op jit(solution)/shard_map/ppermute | solution.py:121
  103.0 24.7 %collective-permute-start.10 = (bf16[768,512]{1,0:T(8,128)(2,1)S(1)}, bf16[768,512]{1,0:T(8,128)(2,1)S(1)}, u32[]{:S(2)}, u32[]{:S(2)}) collective-permute-start(bf16[768,512]{1,0:T(8,128)(2,1)S(1)} %get-tuple-element.28), channel_id=1, source_target_pairs={{0,16},{8,24},{16,0},{24,8},{1,17},{9,25},{17,1},{25,9},{2,18},{10... | collective-permute-start | bytes 2359304 | tf_op jit(solution)/shard_map/ppermute | solution.py:121
  106.3 120.9 %collective-permute-start.2 = (bf16[768,1152]{1,0:T(8,128)(2,1)}, bf16[768,1152]{1,0:T(8,128)(2,1)}, u32[]{:S(2)}, u32[]{:S(2)}) collective-permute-start(bf16[768,1152]{1,0:T(8,128)(2,1)} %pad_maximum_fusion.3), channel_id=1, source_target_pairs={{0,24},{8,16},{16,8},{24,0},{1,25},{9,17},{17,9},{25,1},{2,26},{10... | collective-permute-start | bytes 5308424 | tf_op jit(solution)/shard_map/ppermute | solution.py:121
  128.6 14.3 %collective-permute-start.13 = (bf16[768,512]{1,0:T(8,128)(2,1)}, bf16[768,512]{1,0:T(8,128)(2,1)}, u32[]{:S(2)}, u32[]{:S(2)}) collective-permute-start(bf16[768,512]{1,0:T(8,128)(2,1)} %get-tuple-element.31), channel_id=1, source_target_pairs={{0,8},{8,0},{16,24},{24,16},{1,9},{9,1},{17,25},{25,17},{2,10},{10... | collective-permute-start | bytes 2359304 | tf_op jit(solution)/shard_map/ppermute | solution.py:121
  128.6 70.8 %collective-permute-start.14 = (bf16[768,512]{1,0:T(8,128)(2,1)}, bf16[768,512]{1,0:T(8,128)(2,1)}, u32[]{:S(2)}, u32[]{:S(2)}) collective-permute-start(bf16[768,512]{1,0:T(8,128)(2,1)} %get-tuple-element.32), channel_id=1, source_target_pairs={{0,16},{8,24},{16,0},{24,8},{1,17},{9,25},{17,1},{25,9},{2,18},{10... | collective-permute-start | bytes 2359304 | tf_op jit(solution)/shard_map/ppermute | solution.py:121
  130.5 80.1 %collective-permute-start.15 = (bf16[768,512]{1,0:T(8,128)(2,1)}, bf16[768,512]{1,0:T(8,128)(2,1)}, u32[]{:S(2)}, u32[]{:S(2)}) collective-permute-start(bf16[768,512]{1,0:T(8,128)(2,1)} %get-tuple-element.33), channel_id=1, source_target_pairs={{0,24},{8,16},{16,8},{24,0},{1,25},{9,17},{17,9},{25,1},{2,26},{10... | collective-permute-start | bytes 2359304 | tf_op jit(solution)/shard_map/ppermute | solution.py:121
  130.8 98.0 %copy-start.1 = (bf16[768,1152]{1,0:T(8,128)(2,1)}, bf16[768,1152]{1,0:T(8,128)(2,1)S(1)}, u32[]{:S(2)}) copy-start(bf16[768,1152]{1,0:T(8,128)(2,1)S(1)} %pad_maximum_fusion.refs_0_.refs_6_) | copy-start | bytes 5308420
  142.9 109.4 %collective-permute-start.5 = (bf16[768,512]{1,0:T(8,128)(2,1)}, bf16[768,512]{1,0:T(8,128)(2,1)}, u32[]{:S(2)}, u32[]{:S(2)}) collective-permute-start(bf16[768,512]{1,0:T(8,128)(2,1)} %get-tuple-element.23), channel_id=1, source_target_pairs={{0,8},{8,0},{16,24},{24,16},{1,9},{9,1},{17,25},{25,17},{2,10},{10... | collective-permute-start | bytes 2359304 | tf_op jit(solution)/shard_map/ppermute | solution.py:121
  199.4 44.0 %collective-permute-start.9 = (bf16[768,512]{1,0:T(8,128)(2,1)}, bf16[768,512]{1,0:T(8,128)(2,1)}, u32[]{:S(2)}, u32[]{:S(2)}) collective-permute-start(bf16[768,512]{1,0:T(8,128)(2,1)} %get-tuple-element.27), channel_id=1, source_target_pairs={{0,8},{8,0},{16,24},{24,16},{1,9},{9,1},{17,25},{25,17},{2,10},{10... | collective-permute-start | bytes 2359304 | tf_op jit(solution)/shard_map/ppermute | solution.py:121
  210.6 33.4 %collective-permute-start.11 = (bf16[768,512]{1,0:T(8,128)(2,1)}, bf16[768,512]{1,0:T(8,128)(2,1)}, u32[]{:S(2)}, u32[]{:S(2)}) collective-permute-start(bf16[768,512]{1,0:T(8,128)(2,1)} %get-tuple-element.29), channel_id=1, source_target_pairs={{0,24},{8,16},{16,8},{24,0},{1,25},{9,17},{17,9},{25,1},{2,26},{10... | collective-permute-start | bytes 2359304 | tf_op jit(solution)/shard_map/ppermute | solution.py:121
  227.1 25.2 %collective-permute-start.7 = (bf16[768,512]{1,0:T(8,128)(2,1)S(1)}, bf16[768,512]{1,0:T(8,128)(2,1)S(1)}, u32[]{:S(2)}, u32[]{:S(2)}) collective-permute-start(bf16[768,512]{1,0:T(8,128)(2,1)S(1)} %copy-done.54), channel_id=1, source_target_pairs={{0,24},{8,16},{16,8},{24,0},{1,25},{9,17},{17,9},{25,1},{2,26},{10... | collective-permute-start | bytes 2359304 | tf_op jit(solution)/shard_map/ppermute | solution.py:121
  227.2 122.1 %collective-permute-start.16 = (bf16[1024,512]{1,0:T(8,128)(2,1)S(1)}, bf16[1024,512]{1,0:T(8,128)(2,1)}, u32[]{:S(2)}, u32[]{:S(2)}) collective-permute-start(bf16[1024,512]{1,0:T(8,128)(2,1)S(1)} %copy-done.28), channel_id=1, source_target_pairs={{0,1},{1,0},{2,3},{3,2},{4,5},{5,4},{6,7},{7,6},{8,9},{9,8},{10,11... | collective-permute-start | bytes 3145736 | tf_op jit(solution)/shard_map/ppermute | solution.py:121
  243.4 155.3 %collective-permute-start.3 = (bf16[1024,1152]{1,0:T(8,128)(2,1)}, bf16[1024,1152]{1,0:T(8,128)(2,1)S(1)}, u32[]{:S(2)}, u32[]{:S(2)}) collective-permute-start(bf16[1024,1152]{1,0:T(8,128)(2,1)} %in_product.4.q_own.k_own.v_own), channel_id=1, source_target_pairs={{0,1},{1,0},{2,3},{3,2},{4,5},{5,4},{6,7},{7,6},{8,9},{9,8},{10,11... | collective-permute-start | bytes 7077896 | tf_op jit(solution)/shard_map/ppermute | solution.py:121
  250.8 75.5 %collective-permute-start.12 = (bf16[1024,512]{1,0:T(8,128)(2,1)S(1)}, bf16[1024,512]{1,0:T(8,128)(2,1)S(1)}, u32[]{:S(2)}, u32[]{:S(2)}) collective-permute-start(bf16[1024,512]{1,0:T(8,128)(2,1)S(1)} %in_product.6), channel_id=1, source_target_pairs={{0,1},{1,0},{2,3},{3,2},{4,5},{5,4},{6,7},{7,6},{8,9},{9,8},{10,11... | collective-permute-start | bytes 3145736 | tf_op jit(solution)/shard_map/ppermute | solution.py:121
  259.3 89.5 %collective-permute-start.8 = (bf16[1024,512]{1,0:T(8,128)(2,1)S(1)}, bf16[1024,512]{1,0:T(8,128)(2,1)S(1)}, u32[]{:S(2)}, u32[]{:S(2)}) collective-permute-start(bf16[1024,512]{1,0:T(8,128)(2,1)S(1)} %in_product.5), channel_id=1, source_target_pairs={{0,1},{1,0},{2,3},{3,2},{4,5},{5,4},{6,7},{7,6},{8,9},{9,8},{10,11... | collective-permute-start | bytes 3145736 | tf_op jit(solution)/shard_map/ppermute | solution.py:121
  269.4 113.0 %collective-permute-start.22 = (bf16[512,1536]{1,0:T(8,128)(2,1)S(1)}, bf16[512,1536]{1,0:T(8,128)(2,1)S(1)}, u32[]{:S(2)}, u32[]{:S(2)}) collective-permute-start(bf16[512,1536]{1,0:T(8,128)(2,1)S(1)} %fusion.2), channel_id=1, source_target_pairs={{0,1},{1,0},{2,3},{3,2},{4,5},{5,4},{6,7},{7,6},{8,9},{9,8},{10,11... | collective-permute-start | bytes 4718600 | tf_op jit(solution)/shard_map/ppermute | solution.py:121
  326.3 72.5 %collective-permute-start.4 = (bf16[1024,384]{1,0:T(8,128)(2,1)S(1)}, bf16[1024,384]{1,0:T(8,128)(2,1)S(1)}, u32[]{:S(2)}, u32[]{:S(2)}) collective-permute-start(bf16[1024,384]{1,0:T(8,128)(2,1)S(1)} %convolution_convert_fusion.2.g_own), channel_id=1, source_target_pairs={{0,1},{1,0},{2,3},{3,2},{4,5},{5,4},{6,7},{7,6},{8,9},{9,8},{10,11... | collective-permute-start | bytes 2359304 | tf_op jit(solution)/shard_map/ppermute | solution.py:121
  328.4 54.5 %copy-start.35 = (f32[1024,512]{1,0:T(8,128)}, f32[1024,512]{1,0:T(8,128)S(1)}, u32[]{:S(2)}) copy-start(f32[1024,512]{1,0:T(8,128)S(1)} %get-tuple-element.80) | copy-start | bytes 6291460
  349.3 33.5 %copy-start.37 = (f32[1024,512]{1,0:T(8,128)}, f32[1024,512]{1,0:T(8,128)S(1)}, u32[]{:S(2)}) copy-start(f32[1024,512]{1,0:T(8,128)S(1)} %get-tuple-element.82) | copy-start | bytes 6291460
  413.9 64.1 %copy-start.17 = (bf16[1024,384]{1,0:T(8,128)(2,1)}, bf16[1024,384]{1,0:T(8,128)(2,1)S(1)}, u32[]{:S(2)}) copy-start(bf16[1024,384]{1,0:T(8,128)(2,1)S(1)} %get-tuple-element.34.refs_0_) | copy-start | bytes 2359300
  413.9 64.1 %copy-start.19 = (bf16[1024,384]{1,0:T(8,128)(2,1)}, bf16[1024,384]{1,0:T(8,128)(2,1)S(1)}, u32[]{:S(2)}) copy-start(bf16[1024,384]{1,0:T(8,128)(2,1)S(1)} %get-tuple-element.35.refs_1_) | copy-start | bytes 2359300
  413.9 64.1 %copy-start.21 = (bf16[1024,384]{1,0:T(8,128)(2,1)}, bf16[1024,384]{1,0:T(8,128)(2,1)S(1)}, u32[]{:S(2)}) copy-start(bf16[1024,384]{1,0:T(8,128)(2,1)S(1)} %get-tuple-element.36.refs_2_) | copy-start | bytes 2359300
  428.9 49.1 %collective-permute-start.23 = (bf16[4,512,768]{2,1,0:T(8,128)(2,1)}, bf16[4,512,768]{2,1,0:T(8,128)(2,1)S(1)}, u32[]{:S(2)}, u32[]{:S(2)}) collective-permute-start(bf16[4,512,768]{2,1,0:T(8,128)(2,1)} %back_product.3), channel_id=1, source_target_pairs={{0,8},{8,0},{16,24},{24,16},{1,9},{9,1},{17,25},{25,17},{2,10},{10... | collective-permute-start | bytes 9437192 | tf_op jit(solution)/shard_map/ppermute | solution.py:121
  435.8 20.4 %collective-permute-start.21 = (bf16[256,1536]{1,0:T(8,128)(2,1)S(1)}, bf16[256,1536]{1,0:T(8,128)(2,1)S(1)}, u32[]{:S(2)}, u32[]{:S(2)}) collective-permute-start(bf16[256,1536]{1,0:T(8,128)(2,1)S(1)} %convolution_convert_fusion.1), channel_id=1, source_target_pairs={{0,1},{1,0},{2,3},{3,2},{4,5},{5,4},{6,7},{7,6},{8,9},{9,8},{10,11... | collective-permute-start | bytes 2359304 | tf_op jit(solution)/shard_map/ppermute | solution.py:121
  448.6 41.5 %collective-permute-start.17 = (bf16[512,3072]{1,0:T(8,128)(2,1)}, bf16[512,3072]{1,0:T(8,128)(2,1)}, u32[]{:S(2)}, u32[]{:S(2)}) collective-permute-start(bf16[512,3072]{1,0:T(8,128)(2,1)} %out_product.3), channel_id=1, source_target_pairs={{0,8},{8,0},{16,24},{24,16},{1,9},{9,1},{17,25},{25,17},{2,10},{10... | collective-permute-start | bytes 9437192 | tf_op jit(solution)/shard_map/ppermute | solution.py:121
  455.8 19.8 %collective-permute-start.24 = (bf16[256,1536]{1,0:T(8,128)(2,1)S(1)}, bf16[256,1536]{1,0:T(8,128)(2,1)S(1)}, u32[]{:S(2)}, u32[]{:S(2)}) collective-permute-start(bf16[256,1536]{1,0:T(8,128)(2,1)S(1)} %convolution_convert_fusion), channel_id=1, source_target_pairs={{0,1},{1,0},{2,3},{3,2},{4,5},{5,4},{6,7},{7,6},{8,9},{9,8},{10,11... | collective-permute-start | bytes 2359304 | tf_op jit(solution)/shard_map/ppermute | solution.py:121
  489.3 37.7 %collective-permute-start.25 = (bf16[4,256,768]{2,1,0:T(8,128)(2,1)}, bf16[4,256,768]{2,1,0:T(8,128)(2,1)}, u32[]{:S(2)}, u32[]{:S(2)}) collective-permute-start(bf16[4,256,768]{2,1,0:T(8,128)(2,1)} %back_product.5), channel_id=1, source_target_pairs={{0,16},{8,24},{16,0},{24,8},{1,17},{9,25},{17,1},{25,9},{2,18},{10... | collective-permute-start | bytes 4718600 | tf_op jit(solution)/shard_map/ppermute | solution.py:121
  499.3 59.8 %collective-permute-start.18 = (bf16[256,3072]{1,0:T(8,128)(2,1)S(1)}, bf16[256,3072]{1,0:T(8,128)(2,1)S(1)}, u32[]{:S(2)}, u32[]{:S(2)}) collective-permute-start(bf16[256,3072]{1,0:T(8,128)(2,1)S(1)} %out_product.5), channel_id=1, source_target_pairs={{0,16},{8,24},{16,0},{24,8},{1,17},{9,25},{17,1},{25,9},{2,18},{10... | collective-permute-start | bytes 4718600 | tf_op jit(solution)/shard_map/ppermute | solution.py:121
  530.0 33.9 %collective-permute-start.26 = (bf16[4,2,64,768]{3,2,1,0:T(8,128)(2,1)}, bf16[4,2,64,768]{3,2,1,0:T(8,128)(2,1)}, u32[]{:S(2)}, u32[]{:S(2)}) collective-permute-start(bf16[4,2,64,768]{3,2,1,0:T(8,128)(2,1)} %fusion.39), channel_id=1, source_target_pairs={{0,2},{2,0},{4,6},{6,4},{1,3},{3,1},{5,7},{7,5},{8,10},{10,8},{12,... | collective-permute-start | bytes 2359304 | tf_op jit(solution)/shard_map/ppermute | solution.py:121
  562.3 26.7 %collective-permute-start.19 = (bf16[2,64,3072]{2,1,0:T(8,128)(2,1)}, bf16[2,64,3072]{2,1,0:T(8,128)(2,1)}, u32[]{:S(2)}, u32[]{:S(2)}) collective-permute-start(bf16[2,64,3072]{2,1,0:T(8,128)(2,1)} %fusion.38), channel_id=1, source_target_pairs={{0,2},{2,0},{4,6},{6,4},{1,3},{3,1},{5,7},{7,5},{8,10},{10,8},{12,... | collective-permute-start | bytes 2359304 | tf_op jit(solution)/shard_map/ppermute | solution.py:121
  565.5 27.5 %collective-permute-start.27 = (bf16[4,64,768]{2,1,0:T(8,128)(2,1)S(1)}, bf16[4,64,768]{2,1,0:T(8,128)(2,1)S(1)}, u32[]{:S(2)}, u32[]{:S(2)}) collective-permute-start(bf16[4,64,768]{2,1,0:T(8,128)(2,1)S(1)} %fusion.79), channel_id=1, source_target_pairs={{0,4},{2,6},{4,0},{6,2},{1,5},{3,7},{5,1},{7,3},{8,12},{10,14},{12... | collective-permute-start | bytes 1179656 | tf_op jit(solution)/shard_map/ppermute | solution.py:121
  591.3 18.2 %collective-permute-start.20 = (bf16[64,3072]{1,0:T(8,128)(2,1)}, bf16[64,3072]{1,0:T(8,128)(2,1)S(1)}, u32[]{:S(2)}, u32[]{:S(2)}) collective-permute-start(bf16[64,3072]{1,0:T(8,128)(2,1)} %fusion.78), channel_id=1, source_target_pairs={{0,4},{2,6},{4,0},{6,2},{1,5},{3,7},{5,1},{7,3},{8,12},{10,14},{12... | collective-permute-start | bytes 1179656 | tf_op jit(solution)/shard_map/ppermute | solution.py:121
  (38 other events, 479.0 us)
Sparse Core Ops, SparseCore 0:
  16.3 82.3 all-gather.2
  101.0 81.1 all-gather.4

commit v5 on v2

v5 whole, which is shorter than its diff:
```python
import functools
import math

import jax
import jax.numpy as jnp
from jax import lax
from jax.experimental import pallas as pl
from jax.experimental.pallas import tpu as pltpu
from jax.sharding import PartitionSpec as P

D = 6144
HEAD_DIM = 128
IMG_TOK = 256


EPSILON = 1e-06
ROOT_HALF = 0.7071067811865476
ROOT_TWO_PI_INV = 0.3989422804014327


def attend_kernel(
    q_own, q_got, k_own, k_got, v_own, v_got, g_ref, mixed_ref, dq_ref, dk_ref, dv_ref, *, scale
):
    def total(own, got):
        return own[...].astype(jnp.float32) + got[...].astype(jnp.float32)

    def norm(values):
        center = values - jnp.mean(values, axis=-1, keepdims=True)
        spread = jnp.mean(center * center, axis=-1, keepdims=True)
        inverse = lax.rsqrt(spread + EPSILON)
        return center * inverse, inverse

    def norm_back(grad, normed, inverse):
        slope = inverse * (grad - normed * jnp.mean(grad * normed, axis=-1, keepdims=True))
        return (slope - jnp.mean(slope, axis=-1, keepdims=True)).astype(jnp.bfloat16)

    def contract(left, right, left_dim, right_dim):
        return lax.dot_general(
            left,
            right,
            (((left_dim,), (right_dim,)), ((), ())),
            preferred_element_type=jnp.float32,
        )

    def half(values):
        return values.astype(jnp.bfloat16)

    q_norm, q_inverse = norm(total(q_own, q_got))
    k_norm, k_inverse = norm(total(k_own, k_got))
    q_half, k_half = half(q_norm), half(k_norm)
    v_half = half(total(v_own, v_got))
    grad = g_ref[...]
    weights = jnp.exp(contract(q_half, k_half, 1, 1) * scale)
    probs = weights / jnp.sum(weights, axis=-1, keepdims=True)
    probs_half = half(probs)
    mixed_ref[...] = half(contract(probs_half, v_half, 1, 0))
    dv_ref[...] = half(contract(probs_half, grad, 0, 0))
    probs_grad = half(contract(grad, v_half, 1, 1)).astype(jnp.float32)
    inner = jnp.sum(probs_grad * probs, axis=-1, keepdims=True)
    score_grad = half(probs * (probs_grad - inner) * scale)
    q_grad = half(contract(score_grad, k_half, 1, 0)).astype(jnp.float32)
    k_grad = half(contract(score_grad, q_half, 0, 0)).astype(jnp.float32)
    dq_ref[...] = norm_back(q_grad, q_norm, q_inverse)
    dk_ref[...] = norm_back(k_grad, k_norm, k_inverse)


def attend(own, got, grad):
    rows, width = own.shape[0], own.shape[1] // 3
    heads = width // HEAD_DIM

    def block(part):
        return pl.BlockSpec((IMG_TOK, HEAD_DIM), lambda image, head: (image, part * heads + head))

    half = jax.ShapeDtypeStruct((rows, width), jnp.bfloat16)
    return pl.pallas_call(
        functools.partial(attend_kernel, scale=1.0 / math.sqrt(HEAD_DIM)),
        grid=(rows // IMG_TOK, heads),
        in_specs=[block(0), block(0), block(1), block(1), block(2), block(2), block(0)],
        out_specs=[block(0)] * 4,
        out_shape=[half] * 4,
        compiler_params=pltpu.CompilerParams(vmem_limit_bytes=32 * 1024 * 1024),
        cost_estimate=pl.CostEstimate(
            flops=12 * rows * IMG_TOK * width,
            bytes_accessed=24 * rows * width,
            transcendentals=rows * IMG_TOK * heads,
        ),
        name="attend",
    )(own, got, own, got, own, got, grad)


def gelu(pre):
    return pre * 0.5 * (1.0 + lax.erf(pre * ROOT_HALF))


def gelu_back(pre, grad_half):
    cdf = 0.5 * (1.0 + lax.erf(pre * ROOT_HALF))
    pdf = jnp.exp(-0.5 * pre * pre) * ROOT_TWO_PI_INV
    return (grad_half.astype(jnp.float32) * (cdf + pre * pdf)).astype(jnp.bfloat16)


def dot(left, right):
    return jnp.dot(left, right, preferred_element_type=jnp.float32)


def back_dot(left, right):
    return lax.dot_general(
        left, right, (((1,), (1,)), ((), ())), preferred_element_type=jnp.float32
    )


def half(values):
    return values.astype(jnp.bfloat16)


def wide_sum(own, got):
    return own.astype(jnp.float32) + got.astype(jnp.float32)


def trade(block, axis, bit):
    pairs = [(index, index ^ bit) for index in range(lax.axis_size(axis))]
    return lax.ppermute(block, axis, pairs)


VMEM_LIMIT = 48 * 1024 * 1024


def params():
    return pltpu.CompilerParams(vmem_limit_bytes=VMEM_LIMIT)


def cost(flops, *arrays):
    moved = sum(math.prod(array.shape) * array.dtype.itemsize for array in arrays)
    return pl.CostEstimate(flops=flops, bytes_accessed=moved, transcendentals=0)


def pack_kernel(*refs):
    out_ref, start = refs[-1], 0
    for ref in refs[:-1]:
        out_ref[0, :, start : start + ref.shape[1]] = ref[...]
        start += ref.shape[1]


def pack(weights, owners, start, width, tile):
    rows, columns = weights[0].shape
    first, blocks = start // tile, columns // owners // tile
    out = jax.ShapeDtypeStruct((owners, rows, len(weights) * width), weights[0].dtype)
    spec = pl.BlockSpec((rows, tile), lambda owner, n: (0, owner * blocks + first + n))
    return pl.pallas_call(
        pack_kernel,
        grid=(owners, width // tile),
        in_specs=[spec] * len(weights),
        out_specs=pl.BlockSpec((1, rows, len(weights) * tile), lambda owner, n: (owner, 0, n)),
        out_shape=out,
        compiler_params=params(),
        cost_estimate=cost(0, out, out),
        name="pack",
    )(*weights)


IMAGE_ORDER = ((1, 1), (0, 1), (1, 0), (0, 0))


def assemble_kernel(*refs):
    parts, out_ref = refs[:-1], refs[-1]
    rows = parts[0].shape[1]
    start = 0
    for x_bit, core_bit in IMAGE_ORDER:
        for part in range(len(parts) // 2):
            out_ref[start : start + rows, :] = parts[2 * part + core_bit][x_bit]
            start += rows


def assemble(parts):
    flat = [value for part in parts for value in part]
    _, rows, features = flat[0].shape
    tile = 768
    out = jax.ShapeDtypeStruct((len(flat) * 2 * rows, features), flat[0].dtype)
    return pl.pallas_call(
        assemble_kernel,
        grid=(features // tile,),
        in_specs=[pl.BlockSpec((2, rows, tile), lambda n: (0, 0, n))] * len(flat),
        out_specs=pl.BlockSpec((out.shape[0], tile), lambda n: (0, n)),
        out_shape=out,
        compiler_params=params(),
        cost_estimate=cost(0, out, out),
        name="assemble",
    )(*flat)


def cot_kernel(own_ref, other_ref, attn_ref, mlp_ref, out_ref, rows_ref):
    rows = own_ref.shape[1]
    step = pl.program_id(0)

    @pl.when(step == 0)
    def _():
        for place, (x_bit, core_bit) in enumerate(IMAGE_ORDER):
            part = other_ref if core_bit else own_ref
            rows_ref[place * rows : (place + 1) * rows, :] = part[x_bit]
        out_ref[...] = half(back_dot(rows_ref[...], attn_ref[...]))

    @pl.when(step > 0)
    def _():
        out_ref[...] = half(back_dot(rows_ref[...], mlp_ref[...]))


def cot_product(part, w_attn_out, w_mlp_out):
    own, other = part
    _, rows, features = own.shape
    tile = w_attn_out.shape[0]
    columns = tile + w_mlp_out.shape[0]
    count = len(IMAGE_ORDER) * rows
    out = jax.ShapeDtypeStruct((count, columns), jnp.bfloat16)
    whole = pl.BlockSpec(own.shape, lambda n: (0, 0, 0))
    return pl.pallas_call(
        cot_kernel,
        grid=(columns // tile,),
        in_specs=[
            whole,
            whole,
            pl.BlockSpec((tile, features), lambda n: (0, 0)),
            pl.BlockSpec((tile, features), lambda n: (jnp.maximum(n - 1, 0), 0)),
        ],
        out_specs=pl.BlockSpec((count, tile), lambda n: (0, n)),
        out_shape=out,
        scratch_shapes=[pltpu.VMEM((count, features), jnp.bfloat16)],
        compiler_params=params(),
        cost_estimate=cost(2 * count * columns * features, out, w_attn_out, w_mlp_out),
        name="cot_product",
    )(own, other, w_attn_out, w_mlp_out)


def add_kernel(*refs):
    terms, out_ref = refs[:-1], refs[-1]
    count = len(terms) // 2
    for part in range(count):
        out_ref[0, part] = half(wide_sum(terms[part][0], terms[count + part][0]))


def add_parts(owns, gots):
    images, parts = len(IMAGE_ORDER), len(owns)
    rows, columns = owns[0].shape[0] // images, owns[0].shape[1]
    out = jax.ShapeDtypeStruct((images, parts, rows, columns), jnp.bfloat16)
    terms = [value.reshape(images, rows, columns) for value in (*owns, *gots)]
    added = pl.pallas_call(
        add_kernel,
        grid=(images,),
        in_specs=[pl.BlockSpec((1, rows, columns), lambda image: (image, 0, 0))] * len(terms),
        out_specs=pl.BlockSpec((1, parts, rows, columns), lambda image: (image, 0, 0, 0)),
        out_shape=out,
        compiler_params=params(),
        cost_estimate=cost(0, out, out, out),
        name="add_parts",
    )(*terms)
    return added.reshape(images * parts * rows, columns)


def in_kernel(rows_ref, weight_ref, out_ref):
    out_ref[...] = half(dot(rows_ref[...], weight_ref[...]))


def in_product(rows, weight):
    count, features = rows.shape
    columns = weight.shape[1]
    tile = 384 if columns % 384 == 0 else 256
    out = jax.ShapeDtypeStruct((count, columns), jnp.bfloat16)
    return pl.pallas_call(
        in_kernel,
        grid=(columns // tile,),
        in_specs=[
            pl.BlockSpec((count, features), lambda n: (0, 0)),
            pl.BlockSpec((features, tile), lambda n: (0, n)),
        ],
        out_specs=pl.BlockSpec((count, tile), lambda n: (0, n)),
        out_shape=out,
        compiler_params=params(),
        cost_estimate=cost(2 * count * columns * features, rows, out, weight),
        name="in_product",
    )(rows, weight)


def out_product(mixed, acts, w_attn_out, w_mlp_out, start, count, add, add_start, kind):
    columns = w_attn_out.shape[1]
    tile = 512 if columns % 512 == 0 else 256
    n_acts = len(acts)

    def rows_spec(value):
        return pl.BlockSpec((count, value.shape[1]), lambda n: (start // count, 0))

    def columns_spec(value):
        return pl.BlockSpec((value.shape[0], tile), lambda n: (0, n))

    operands = [mixed, *acts, w_attn_out, w_mlp_out]
    specs = [rows_spec(mixed), *(rows_spec(act) for act in acts)]
    specs += [columns_spec(w_attn_out), columns_spec(w_mlp_out)]
    if add is not None:
        operands.append(add)
        specs.append(pl.BlockSpec((count, tile), lambda n: (add_start // count, n)))

    def kernel(*refs):
        attn_ref, mlp_ref, out_ref = refs[n_acts + 1], refs[n_acts + 2], refs[-1]
        total = dot(refs[0][...], attn_ref[...])
        row = 0
        for act in refs[1 : n_acts + 1]:
            total = total + dot(act[...], mlp_ref[row : row + act.shape[1], :])
            row += act.shape[1]
        if add is not None:
            total = total + refs[n_acts + 3][...].astype(jnp.float32)
        out_ref[...] = total.astype(out_ref.dtype)

    depth = w_attn_out.shape[0] + w_mlp_out.shape[0]
    out = jax.ShapeDtypeStruct((count, columns), kind)
    return pl.pallas_call(
        kernel,
        grid=(columns // tile,),
        in_specs=specs,
        out_specs=pl.BlockSpec((count, tile), lambda n: (0, n)),
        out_shape=out,
        compiler_params=params(),
        cost_estimate=cost(2 * count * columns * depth, out, w_attn_out, w_mlp_out),
        name="out_product",
    )(*operands)


def back_product(head_grads, mlp_grads, in_heads, in_mlp, start, count, add):
    features = in_heads.shape[0]
    tile = 512 if features % 512 == 0 else 256
    n_heads = len(head_grads)
    grads = [*head_grads, *mlp_grads]
    weights = [in_heads, *in_mlp]
    specs = [pl.BlockSpec((count, grad.shape[1]), lambda n: (start // count, 0)) for grad in grads]
    specs += [pl.BlockSpec((tile, weight.shape[1]), lambda n: (n, 0)) for weight in weights]
    operands = grads + weights
    if add is not None:
        operands.append(add)
        specs.append(pl.BlockSpec((count, tile), lambda n: (0, n)))

    def kernel(*refs):
        out_ref, heads_ref = refs[-1], refs[len(grads)]
        mlp_refs = refs[len(grads) + 1 : len(grads) + len(weights)]
        total, column = None, 0
        for grad in refs[:n_heads]:
            part = back_dot(grad[...], heads_ref[:, column : column + grad.shape[1]])
            total = part if total is None else total + part
            column += grad.shape[1]
        for grad, weight in zip(refs[n_heads : len(grads)], mlp_refs):
            total = total + back_dot(grad[...], weight[...])
        if add is not None:
            total = total + refs[-2][...].astype(jnp.float32)
        out_ref[...] = total.astype(out_ref.dtype)

    width = sum(grad.shape[1] for grad in grads)
    out = jax.ShapeDtypeStruct((count, features), jnp.bfloat16)
    return pl.pallas_call(
        kernel,
        grid=(features // tile,),
        in_specs=specs,
        out_specs=pl.BlockSpec((count, tile), lambda n: (0, n)),
        out_shape=out,
        compiler_params=params(),
        cost_estimate=cost(2 * count * features * width, out, *weights),
        name="back_product",
    )(*operands)


MLP_CUTS = (256, 512, 512, 256)


def body(layer_input, out_cotangent, w_query, w_key, w_value, w_mlp_in, w_attn_out, w_mlp_out):
    n_gx, n_gz = lax.axis_size("gx"), lax.axis_size("gz")
    own_rows, features = layer_input.shape
    count = own_rows * lax.axis_size("gy")

    def after(value, *earlier):
        return lax.optimization_barrier((value, earlier))[0]

    def others(part):
        if n_gz == 2:
            return trade(part, "gz", 1)
        return half(lax.psum(part.astype(jnp.float32), "gz") - part.astype(jnp.float32))

    def gather_parts(block):
        pair = jnp.stack([block, trade(block, "gx", 2)])
        near, far = trade(pair, "gy", 1), trade(pair, "gy", 2)
        parts = [pair, near, far, trade(far, "gy", 1)]
        return [(part, trade(part, "gx", 1)) for part in parts]

    def swap(packed):
        swapped = lax.all_to_all(packed, "gx", split_axis=0, concat_axis=0, tiled=True)
        return swapped.reshape(n_gx * packed.shape[1], packed.shape[2])

    heads_width = w_query.shape[1] // n_gx
    packed_heads = pack((w_query, w_key, w_value), n_gx, 0, heads_width, heads_width)
    starts = [sum(MLP_CUTS[:cut]) for cut in range(len(MLP_CUTS))]
    packed_mlp = [
        pack((w_mlp_in,), n_gx, start, width, 256) for start, width in zip(starts, MLP_CUTS)
    ]
    in_heads = swap(packed_heads)

    cot_owns = [
        cot_product(part, w_attn_out, w_mlp_out) for part in gather_parts(out_cotangent)
    ]
    cot_gots = [others(own) for own in cot_owns]

    wide = layer_input.astype(jnp.float32)
    total, squares = lax.psum((jnp.sum(wide, axis=1), jnp.sum(wide * wide, axis=1)), "gz")
    center = total / D
    spread = squares / D - center * center
    inverse = lax.rsqrt(spread + EPSILON)
    normed = (wide - center[:, None]) * inverse[:, None]
    all_in = assemble(gather_parts(half(normed)))

    heads_own = in_product(all_in, in_heads)
    heads_got = others(heads_own)
    in_mlp, mlp_own, mlp_got = [], [], []
    turn = (in_heads, *cot_owns)
    for cut in range(len(MLP_CUTS)):
        weight = swap(after(packed_mlp[cut], *turn))
        turn = (weight, mlp_own[-1] if mlp_own else heads_own)
        in_mlp.append(weight)
        mlp_own.append(in_product(all_in, weight))
        mlp_got.append(others(mlp_own[-1]))

    out_grad = add_parts(cot_owns, cot_gots)
    mixed, *head_grads = attend(heads_own, heads_got, out_grad)
    acts, mlp_grads = [], []
    for start, own, got in zip(starts, mlp_own, mlp_got):
        pre = wide_sum(own, got)
        acts.append(half(gelu(pre)))
        first = heads_width + start
        mlp_grads.append(gelu_back(pre, out_grad[:, first : first + own.shape[1]]))

    def forward_term(start, size, add, add_start, kind):
        return out_product(mixed, acts, w_attn_out, w_mlp_out, start, size, add, add_start, kind)

    def backward_term(start, size, add):
        return back_product(head_grads, mlp_grads, in_heads, in_mlp, start, size, add)

    def wider(value):
        return value.astype(jnp.float32)

    from_core = trade(forward_term(0, 2 * count, None, 0, jnp.bfloat16), "gx", 1)
    from_x = trade(forward_term(2 * count, count, from_core, 0, jnp.bfloat16), "gx", 2)
    mine = forward_term(3 * count, count, from_core, count, jnp.float32) + wider(from_x)
    mine = mine.reshape(2, 2, own_rows, features)
    pair = mine[:, 0] + wider(trade(half(mine[:, 1]), "gy", 1))
    summed = pair[0] + wider(trade(half(pair[1]), "gy", 2))
    layer_out = half(wide + summed)

    from_core = trade(backward_term(0, 2 * count, None), "gx", 1)
    both = backward_term(2 * count, 2 * count, from_core).reshape(2, 2, 2, own_rows, features)
    pair = wide_sum(both[:, :, 0], trade(both[:, :, 1], "gy", 1))
    ends = pair[:, 0] + wider(trade(half(pair[:, 1]), "gy", 2))
    normed_grad = ends[1] + wider(trade(half(ends[0]), "gx", 2))
    first, second = lax.psum(
        (jnp.sum(normed_grad, axis=1), jnp.sum(normed_grad * normed, axis=1)), "gz"
    )
    grad_full = out_cotangent.astype(jnp.float32) + inverse[:, None] * (
        normed_grad - (first / D)[:, None] - normed * (second / D)[:, None]
    )
    return (layer_out, half(grad_full))


def solution(mesh):
    in_specs = (
        P(("gx", "gy"), "gz"),
        P(("gx", "gy"), "gz"),
        P(("gz", "gx"), "gy"),
        P(("gz", "gx"), "gy"),
        P(("gz", "gx"), "gy"),
        P(("gz", "gx"), "gy"),
        P(("gy", "gx"), "gz"),
        P(("gy", "gx"), "gz"),
    )
    out_specs = (P(("gx", "gy"), "gz"), P(("gx", "gy"), "gz"))
    return jax.shard_map(body, mesh=mesh, in_specs=in_specs, out_specs=out_specs, check_vma=False)
```

time: 668 us -> 667 us (level)
  Pallas kernels: 15.4 us -> 177 us
  matrix products: 150 us -> 0 us
  local copies, waits for them, and re-layouts: 69.2 us -> 19.2 us
  waiting for transfers between devices: 341 us -> 388 us
  starting transfers between devices: 37.3 us -> 55.8 us
  between operations: 15.2 us -> 1.09 us
  other arithmetic: 23.7 us -> 12.3 us
    pallas_call x0 -> x21, Pallas kernels: none -> 162 us  [the longest x5 40.4 us: in_product(): pl.pallas_call(in_kernel, grid=(columns // tile,), in_specs=[pl.BlockSpec...]
    dot_general x25 -> x0, matrix products: 150 us -> none  [the longest x12 81.9 us: dot(): return jnp.dot(left, right, preferred_element_type=jnp.float32)]
    ppermute x15 -> x33, waiting for transfers between devices: 198 us -> 343 us  [trade(): return lax.ppermute(block, axis, pairs)]
    all_to_all x3 -> x5, waiting for transfers between devices: 143 us -> 45.2 us  [swap(): lax.all_to_all(packed, 'gx', split_axis=0, concat_axis=0, tiled=True)]
    all_to_all x3 -> x0, local copies, waits for them, and re-layouts: 24 us -> none  [swap(): lax.all_to_all(weight, 'gx', split_axis=0, concat_axis=0, tiled=True)]
    unnamed x104 -> x45, local copies, waits for them, and re-layouts: 29.4 us -> 16.1 us
    ppermute x15 -> x33, starting transfers between devices: 21.6 us -> 32.1 us  [trade(): return lax.ppermute(block, axis, pairs)]
    all_to_all x3 -> x5, starting transfers between devices: 15.7 us -> 23.7 us  [swap(): lax.all_to_all(packed, 'gx', split_axis=0, concat_axis=0, tiled=True)]
  transfers between devices with their start and end apart: 20 -> 38, of which waited for: 10 -> 21; matrix products, arithmetic and copies ran while one was open for 33% -> 2% of each run, Pallas kernels for 0% -> 24%
where the time goes in v5:
time: 667 us; the launch traced here: 664 us
  waiting for transfers between devices  388 us (58%)
  Pallas kernels  177 us (27%)
  starting transfers between devices  55.8 us (8%)
  local copies, waits for them, and re-layouts  19.2 us (3%)
  other arithmetic  12.3 us (2%)
  blocking collectives  10.4 us (2%)
    ppermute x33, waiting for transfers between devices, trade(): return lax.ppermute(block, axis, pairs)  343 us
    all_to_all x5, waiting for transfers between devices, swap(): lax.all_to_all(packed, 'gx', split_axis=0, concat_axis=0, tiled=True)  45.2 us
    pallas_call x5, Pallas kernels, in_product(): pl.pallas_call(in_kernel, grid=(columns // tile,), in_specs=[pl.BlockSpec...  40.4 us
    pallas_call x4, Pallas kernels, cot_product(): pl.pallas_call(cot_kernel, grid=(columns // tile,), in_specs=[whole, whol...  34.1 us
    ppermute x33, starting transfers between devices, trade(): return lax.ppermute(block, axis, pairs)  32.1 us
    pallas_call x3, Pallas kernels, out_product(): pl.pallas_call(kernel, grid=(columns // tile,), in_specs=specs, out_specs...  28.3 us
    pallas_call x2, Pallas kernels, back_product(): pl.pallas_call(kernel, grid=(features // tile,), in_specs=specs, out_spec...  28 us
    all_to_all x5, starting transfers between devices, swap(): lax.all_to_all(packed, 'gx', split_axis=0, concat_axis=0, tiled=True)  23.7 us
  transfers between devices with their start and end apart: 38, of which 21 were waited for; matrix products, arithmetic and copies ran while one was open for 2% of the time, Pallas kernels for 24%

profile of v5, /device:TPU:0, one launch (start us, length us, event | category | flops | bytes accessed | tf_op | source)
XLA Modules:
  0.0 664.2 jit_solution(2064568238124200916)
XLA Ops:
  4.0 5.2 pack.5
  9.2 5.6 all-to-all-start
  17.9 4.9 all-reduce.1
  23.2 80.4 %collective-permute-done.9 = bf16[64,3072]{1,0:T(8,128)(2,1)S(1)} collective-permute-done((bf16[64,3072]{1,0:T(8,128)(2,1)S(1)}, bf16[64,3072]{1,0:T(8,128)(2,1)S(1)}, u32[]{:S(2)}, u32[]{:S(2)}) %collective-permute-start.9) | collective-permute-done | bytes 393248 | tf_op jit(solution)/shard_map/ppermute | solution.py:121
  114.8 42.2 %collective-permute-done.13.own_ref = bf16[2,64,3072]{2,1,0:T(8,128)(2,1)S(1)} collective-permute-done((bf16[2,64,3072]{2,1,0:T(8,128)(2,1)S(1)}, bf16[2,64,3072]{2,1,0:T(8,128)(2,1)S(1)}, u32[]{:S(2)}, u32[]{:S(2)}) %collective-permute-start.13) | collective-permute-done | bytes 786464 | tf_op jit(solution)/shard_map/ppermute | solution.py:121
  159.0 15.4 %collective-permute-done.4.refs_4_ = bf16[2,64,3072]{2,1,0:T(8,128)(2,1)S(1)} collective-permute-done((bf16[2,64,3072]{2,1,0:T(8,128)(2,1)S(1)}, bf16[2,64,3072]{2,1,0:T(8,128)(2,1)S(1)}, u32[]{:S(2)}, u32[]{:S(2)}) %collective-permute-start.4) | collective-permute-done | bytes 786464 | tf_op jit(solution)/shard_map/ppermute | solution.py:121
  175.1 3.6 pack.6
  178.7 12.6 %collective-permute-done.15.own_ref = bf16[2,64,3072]{2,1,0:T(8,128)(2,1)S(1)} collective-permute-done((bf16[2,64,3072]{2,1,0:T(8,128)(2,1)S(1)}, bf16[2,64,3072]{2,1,0:T(8,128)(2,1)S(1)}, u32[]{:S(2)}, u32[]{:S(2)}) %collective-permute-start.15) | collective-permute-done | bytes 786464 | tf_op jit(solution)/shard_map/ppermute | solution.py:121
  191.3 8.1 %cot_product.4 = bf16[256,1920]{1,0:T(8,128)(2,1)S(1)} custom-call(bf16[2,64,3072]{2,1,0:T(8,128)(2,1)S(1)} %pad_maximum_fusion.1.own_ref, bf16[2,64,3072]{2,1,0:T(8,128)(2,1)S(1)} %collective-permute-done.10.other_ref, bf16[384,3072]{1,0:T(8,128)(2,1)S(1)} %copy-done, bf16[1536,3072]{1,0:T(8,128)(2,1)} %refs_6_.5), custom_call_target="tpu_custom_call" | custom-call | flops 3019898880 | bytes 12779520 | tf_op jit(solution)/shard_map/cot_product/pallas_call | solution.py:214
  200.0 8.1 %cot_product.5 = bf16[256,1920]{1,0:T(8,128)(2,1)S(1)} custom-call(bf16[2,64,3072]{2,1,0:T(8,128)(2,1)S(1)} %collective-permute-done.11.own_ref, bf16[2,64,3072]{2,1,0:T(8,128)(2,1)S(1)} %collective-permute-done.12.other_ref, bf16[384,3072]{1,0:T(8,128)(2,1)S(1)} %copy-done, bf16[1536,3072]{1,0:T(8,128)(2,1)} %refs_6_.5), custom_call_target="tpu_custom_call" | custom-call | flops 3019898880 | bytes 12779520 | tf_op jit(solution)/shard_map/cot_product/pallas_call | solution.py:214
  209.1 7.4 %collective-permute-done.6.refs_6_ = bf16[2,64,3072]{2,1,0:T(8,128)(2,1)} collective-permute-done((bf16[2,64,3072]{2,1,0:T(8,128)(2,1)S(1)}, bf16[2,64,3072]{2,1,0:T(8,128)(2,1)}, u32[]{:S(2)}, u32[]{:S(2)}) %collective-permute-start.6) | collective-permute-done | bytes 786464 | tf_op jit(solution)/shard_map/ppermute | solution.py:121
  217.1 8.9 %cot_product.6 = bf16[256,1920]{1,0:T(8,128)(2,1)} custom-call(bf16[2,64,3072]{2,1,0:T(8,128)(2,1)S(1)} %collective-permute-done.13.own_ref, bf16[2,64,3072]{2,1,0:T(8,128)(2,1)S(1)} %collective-permute-done.14.other_ref, bf16[384,3072]{1,0:T(8,128)(2,1)S(1)} %copy-done, bf16[1536,3072]{1,0:T(8,128)(2,1)} %refs_6_.5), custom_call_target="tpu_custom_call" | custom-call | flops 3019898880 | bytes 12779520 | tf_op jit(solution)/shard_map/cot_product/pallas_call | solution.py:214
  226.0 8.9 %cot_product.7 = bf16[256,1920]{1,0:T(8,128)(2,1)} custom-call(bf16[2,64,3072]{2,1,0:T(8,128)(2,1)S(1)} %collective-permute-done.15.own_ref, bf16[2,64,3072]{2,1,0:T(8,128)(2,1)S(1)} %collective-permute-done.16.other_ref, bf16[384,3072]{1,0:T(8,128)(2,1)S(1)} %copy-done, bf16[1536,3072]{1,0:T(8,128)(2,1)} %refs_6_.5), custom_call_target="tpu_custom_call" | custom-call | flops 3019898880 | bytes 12779520 | tf_op jit(solution)/shard_map/cot_product/pallas_call | solution.py:214
  234.9 4.3 all-to-all-start.1
  239.2 4.5 pack.7
  245.4 5.5 assemble.1.rows_ref
  250.9 14.0 %in_product.5.q_own.k_own.v_own = bf16[1024,1152]{1,0:T(8,128)(2,1)S(1)} custom-call(bf16[1024,3072]{1,0:T(8,128)(2,1)} %assemble.1.rows_ref, bf16[3072,1152]{1,0:T(8,128)(2,1)} %bitcast.2.weight_ref.refs_7_), custom_call_target="tpu_custom_call" | custom-call | flops 7247757312 | bytes 15728640 | tf_op jit(solution)/shard_map/in_product/pallas_call | solution.py:266
  264.9 4.7 all-to-all-start.2
  269.5 4.5 pack.8
  275.7 5.8 in_product.6
  281.5 25.0 %all-to-all-done.2 = bf16[4,768,512]{2,1,0:T(8,128)(2,1)} async-done(((bf16[4,768,512]{2,1,0:T(8,128)(2,1)}), bf16[4,768,512]{2,1,0:T(8,128)(2,1)}, u32[]{:S(2)}, u32[]{:S(2)}) %all-to-all-start.2) | async-done | bytes 3145760 | tf_op jit(solution)/shard_map/all_to_all | solution.py:388
  306.5 4.6 all-to-all-start.3
  320.3 7.7 %in_product.7 = bf16[1024,512]{1,0:T(8,128)(2,1)} custom-call(bf16[1024,3072]{1,0:T(8,128)(2,1)} %assemble.1.rows_ref, bf16[3072,512]{1,0:T(8,128)(2,1)} %bitcast.15.weight_ref.refs_9_), custom_call_target="tpu_custom_call" | custom-call | flops 3221225472 | bytes 10485760 | tf_op jit(solution)/shard_map/in_product/pallas_call | solution.py:266
  328.0 20.2 %all-to-all-done.3 = bf16[4,768,512]{2,1,0:T(8,128)(2,1)} async-done(((bf16[4,768,512]{2,1,0:T(8,128)(2,1)}), bf16[4,768,512]{2,1,0:T(8,128)(2,1)}, u32[]{:S(2)}, u32[]{:S(2)}) %all-to-all-start.3) | async-done | bytes 3145760 | tf_op jit(solution)/shard_map/all_to_all | solution.py:388
  348.2 4.5 all-to-all-start.4
  352.7 7.8 %in_product.8 = bf16[1024,512]{1,0:T(8,128)(2,1)} custom-call(bf16[1024,3072]{1,0:T(8,128)(2,1)} %assemble.1.rows_ref, bf16[3072,512]{1,0:T(8,128)(2,1)} %bitcast.16.weight_ref.refs_10_), custom_call_target="tpu_custom_call" | custom-call | flops 3221225472 | bytes 10485760 | tf_op jit(solution)/shard_map/in_product/pallas_call | solution.py:266
  360.5 26.0 %collective-permute-done.17 = bf16[256,1920]{1,0:T(8,128)(2,1)} collective-permute-done((bf16[256,1920]{1,0:T(8,128)(2,1)S(1)}, bf16[256,1920]{1,0:T(8,128)(2,1)}, u32[]{:S(2)}, u32[]{:S(2)}) %collective-permute-start.17) | collective-permute-done | bytes 983072 | tf_op jit(solution)/shard_map/ppermute | solution.py:121
  388.1 19.5 %collective-permute-done.18 = bf16[256,1920]{1,0:T(8,128)(2,1)} collective-permute-done((bf16[256,1920]{1,0:T(8,128)(2,1)}, bf16[256,1920]{1,0:T(8,128)(2,1)}, u32[]{:S(2)}, u32[]{:S(2)}) %collective-permute-start.18) | collective-permute-done | bytes 983072 | tf_op jit(solution)/shard_map/ppermute | solution.py:121
  409.2 19.5 %collective-permute-done.19 = bf16[256,1920]{1,0:T(8,128)(2,1)} collective-permute-done((bf16[256,1920]{1,0:T(8,128)(2,1)}, bf16[256,1920]{1,0:T(8,128)(2,1)}, u32[]{:S(2)}, u32[]{:S(2)}) %collective-permute-start.19) | collective-permute-done | bytes 983072 | tf_op jit(solution)/shard_map/ppermute | solution.py:121
  428.7 21.1 %collective-permute-done.20 = bf16[256,1920]{1,0:T(8,128)(2,1)} collective-permute-done((bf16[256,1920]{1,0:T(8,128)(2,1)}, bf16[256,1920]{1,0:T(8,128)(2,1)}, u32[]{:S(2)}, u32[]{:S(2)}) %collective-permute-start.20) | collective-permute-done | bytes 983072 | tf_op jit(solution)/shard_map/ppermute | solution.py:121
  449.7 5.5 add_parts.1
  458.9 15.3 %attend.1 = (bf16[1024,384]{1,0:T(8,128)(2,1)S(1)}, bf16[1024,384]{1,0:T(8,128)(2,1)S(1)}, bf16[1024,384]{1,0:T(8,128)(2,1)S(1)}, bf16[1024,384]{1,0:T(8,128)(2,1)S(1)}) custom-call(bf16[1024,1152]{1,0:T(8,128)(2,1)S(1)} %in_product.5.q_own.k_own.v_own, bf16[1024,1152]{1,0:T(8,128)(2,1)} %collective-permute-done.8.q_got.k_got.v_got, ...), custom_call_target="tpu_custom_call" | custom-call | flops 1207959552 | bytes 9437184 | tf_op jit(solution)/shard_map/attend/pallas_call | solution.py:75
  477.0 5.2 in_product.9
  482.6 12.0 %collective-permute-done.23 = bf16[1024,512]{1,0:T(8,128)(2,1)} collective-permute-done((bf16[1024,512]{1,0:T(8,128)(2,1)}, bf16[1024,512]{1,0:T(8,128)(2,1)}, u32[]{:S(2)}, u32[]{:S(2)}) %collective-permute-start.23) | collective-permute-done | bytes 1048608 | tf_op jit(solution)/shard_map/ppermute | solution.py:121
  494.7 4.4 fusion.11
  499.1 6.8 %collective-permute-done.21 = bf16[1024,256]{1,0:T(8,128)(2,1)} collective-permute-done((bf16[1024,256]{1,0:T(8,128)(2,1)}, bf16[1024,256]{1,0:T(8,128)(2,1)}, u32[]{:S(2)}, u32[]{:S(2)}) %collective-permute-start.21) | collective-permute-done | bytes 524320 | tf_op jit(solution)/shard_map/ppermute | solution.py:121
  505.9 10.6 %collective-permute-done.24 = bf16[1024,256]{1,0:T(8,128)(2,1)S(1)} collective-permute-done((bf16[1024,256]{1,0:T(8,128)(2,1)S(1)}, bf16[1024,256]{1,0:T(8,128)(2,1)S(1)}, u32[]{:S(2)}, u32[]{:S(2)}) %collective-permute-start.24) | collective-permute-done | bytes 524320 | tf_op jit(solution)/shard_map/ppermute | solution.py:121
  518.9 13.7 %back_product.2 = bf16[512,3072]{1,0:T(8,128)(2,1)} custom-call(bf16[1024,384]{1,0:T(8,128)(2,1)S(1)} %copy-done.11, bf16[1024,384]{1,0:T(8,128)(2,1)S(1)} %copy-done.13, bf16[1024,384]{1,0:T(8,128)(2,1)S(1)} %copy-done.15, bf16[1024,256]{1,0:T(8,128)(2,1)S(1)} %get-tuple-element.27.refs_3_, bf16[1024,512]{1,0:T(8,128)(2,1)S(1)} %get-tuple-element.29.refs_4_, ...), custom_call_target="tpu_custom_call" | custom-call | flops 8455716864 | bytes 19660800 | tf_op jit(solution)/shard_map/back_product/pallas_call | solution.py:353
  532.6 11.1 %out_product.3 = bf16[512,3072]{1,0:T(8,128)(2,1)} custom-call(bf16[1024,384]{1,0:T(8,128)(2,1)S(1)} %get-tuple-element.10.refs_0_, bf16[1024,256]{1,0:T(8,128)(2,1)S(1)} %get-tuple-element.34.refs_1_, bf16[1024,512]{1,0:T(8,128)(2,1)S(1)} %get-tuple-element.32.refs_2_, bf16[1024,512]{1,0:T(8,128)(2,1)S(1)} %get-tuple-element.33.refs_3_, ...), custom_call_target="tpu_custom_call" | custom-call | flops 6039797760 | bytes 14942208 | tf_op jit(solution)/shard_map/out_product/pallas_call | solution.py:312
  544.2 14.3 %back_product.3 = bf16[512,3072]{1,0:T(8,128)(2,1)} custom-call(bf16[1024,384]{1,0:T(8,128)(2,1)S(1)} %copy-done.11, bf16[1024,384]{1,0:T(8,128)(2,1)S(1)} %copy-done.13, bf16[1024,384]{1,0:T(8,128)(2,1)S(1)} %copy-done.15, bf16[1024,256]{1,0:T(8,128)(2,1)S(1)} %get-tuple-element.27.refs_3_, bf16[1024,512]{1,0:T(8,128)(2,1)S(1)} %get-tuple-element.29.refs_4_, ...), custom_call_target="tpu_custom_call" | custom-call | flops 8455716864 | bytes 19660800 | tf_op jit(solution)/shard_map/back_product/pallas_call | solution.py:353
  562.4 7.9 %out_product.5 = bf16[256,3072]{1,0:T(8,128)(2,1)S(1)} custom-call(bf16[1024,384]{1,0:T(8,128)(2,1)S(1)} %get-tuple-element.10.refs_0_, bf16[1024,256]{1,0:T(8,128)(2,1)S(1)} %get-tuple-element.34.refs_1_, bf16[1024,512]{1,0:T(8,128)(2,1)S(1)} %get-tuple-element.32.refs_2_, bf16[1024,512]{1,0:T(8,128)(2,1)S(1)} %get-tuple-element.33.refs_3_, ...), custom_call_target="tpu_custom_call" | custom-call | flops 3019898880 | bytes 13369344 | tf_op jit(solution)/shard_map/out_product/pallas_call | solution.py:312
  572.1 9.2 %out_product.4 = f32[256,3072]{1,0:T(8,128)} custom-call(bf16[1024,384]{1,0:T(8,128)(2,1)S(1)} %get-tuple-element.10.refs_0_, bf16[1024,256]{1,0:T(8,128)(2,1)S(1)} %get-tuple-element.34.refs_1_, bf16[1024,512]{1,0:T(8,128)(2,1)S(1)} %get-tuple-element.32.refs_2_, bf16[1024,512]{1,0:T(8,128)(2,1)S(1)} %get-tuple-element.33.refs_3_, ...), custom_call_target="tpu_custom_call" | custom-call | flops 3019898880 | bytes 14942208 | tf_op jit(solution)/shard_map/out_product/pallas_call | solution.py:312
  581.4 15.7 %collective-permute-done.30 = bf16[2,2,64,3072]{3,2,0,1:T(8,128)(2,1)S(1)} collective-permute-done((bf16[2,2,64,3072]{3,2,0,1:T(8,128)(2,1)S(1)}, bf16[2,2,64,3072]{3,2,0,1:T(8,128)(2,1)S(1)}, u32[]{:S(2)}, u32[]{:S(2)}) %collective-permute-start.30) | collective-permute-done | bytes 1572896 | tf_op jit(solution)/shard_map/ppermute | solution.py:121
  597.8 9.0 %collective-permute-done.26 = bf16[256,3072]{1,0:T(8,128)(2,1)S(1)} collective-permute-done((bf16[256,3072]{1,0:T(8,128)(2,1)S(1)}, bf16[256,3072]{1,0:T(8,128)(2,1)S(1)}, u32[]{:S(2)}, u32[]{:S(2)}) %collective-permute-start.26) | collective-permute-done | bytes 1572896 | tf_op jit(solution)/shard_map/ppermute | solution.py:121
  609.2 25.1 %collective-permute-done.31 = bf16[2,64,3072]{2,1,0:T(8,128)(2,1)S(1)} collective-permute-done((bf16[2,64,3072]{2,1,0:T(8,128)(2,1)S(1)}, bf16[2,64,3072]{2,1,0:T(8,128)(2,1)S(1)}, u32[]{:S(2)}, u32[]{:S(2)}) %collective-permute-start.31) | collective-permute-done | bytes 786464 | tf_op jit(solution)/shard_map/ppermute | solution.py:121
  636.3 6.6 collective-permute-done.27
  646.6 5.5 all-reduce
  652.7 9.0 %collective-permute-done.28 = bf16[64,3072]{1,0:T(8,128)(2,1)} collective-permute-done((bf16[64,3072]{1,0:T(8,128)(2,1)}, bf16[64,3072]{1,0:T(8,128)(2,1)}, u32[]{:S(2)}, u32[]{:S(2)}) %collective-permute-start.28) | collective-permute-done | bytes 393248 | tf_op jit(solution)/shard_map/ppermute | solution.py:121
  (117 shorter events, 65.8 us)
Async XLA Ops:
  9.2 5.6 copy-start.20
  9.2 8.5 %copy-start.18 = (bf16[64,3072]{1,0:T(8,128)(2,1)S(1)}, bf16[64,3072]{1,0:T(8,128)(2,1)}, u32[]{:S(2)}) copy-start(bf16[64,3072]{1,0:T(8,128)(2,1)} %param.8) | copy-start | bytes 1179652
  9.2 225.7 %all-to-all-start = ((bf16[4,768,1152]{2,1,0:T(8,128)(2,1)}), bf16[4,768,1152]{2,1,0:T(8,128)(2,1)}, u32[]{:S(2)}, u32[]{:S(2)}) async-start(bf16[4,768,1152]{2,1,0:T(8,128)(2,1)} %pack.5), calls=%async_computation | async-start | bytes 14155776 | tf_op jit(solution)/shard_map/all_to_all | solution.py:388
  14.8 88.8 %collective-permute-start.9 = (bf16[64,3072]{1,0:T(8,128)(2,1)S(1)}, bf16[64,3072]{1,0:T(8,128)(2,1)S(1)}, u32[]{:S(2)}, u32[]{:S(2)}) collective-permute-start(bf16[64,3072]{1,0:T(8,128)(2,1)S(1)} %copy-done.20), channel_id=1, source_target_pairs={{0,16},{8,24},{16,0},{24,8},{1,17},{9,25},{17,1},{25,9},{2,18},{10... | collective-permute-start | bytes 1179656 | tf_op jit(solution)/shard_map/ppermute | solution.py:121
  23.0 88.1 %collective-permute-start = (bf16[64,3072]{1,0:T(8,128)(2,1)S(1)}, bf16[64,3072]{1,0:T(8,128)(2,1)S(1)}, u32[]{:S(2)}, u32[]{:S(2)}) collective-permute-start(bf16[64,3072]{1,0:T(8,128)(2,1)S(1)} %fusion.29), channel_id=1, source_target_pairs={{0,16},{8,24},{16,0},{24,8},{1,17},{9,25},{17,1},{25,9},{2,18},{10... | collective-permute-start | bytes 1179656 | tf_op jit(solution)/shard_map/ppermute | solution.py:121
  103.7 53.3 %collective-permute-start.13 = (bf16[2,64,3072]{2,1,0:T(8,128)(2,1)S(1)}, bf16[2,64,3072]{2,1,0:T(8,128)(2,1)S(1)}, u32[]{:S(2)}, u32[]{:S(2)}) collective-permute-start(bf16[2,64,3072]{2,1,0:T(8,128)(2,1)S(1)} %pad_maximum_fusion.1.own_ref), channel_id=1, source_target_pairs={{0,4},{2,6},{4,0},{6,2},{1,5},{3,7},{5,1},{7,3},{8,12},{10,14},{12... | collective-permute-start | bytes 2359304 | tf_op jit(solution)/shard_map/ppermute | solution.py:121
  107.0 50.0 %collective-permute-start.11 = (bf16[2,64,3072]{2,1,0:T(8,128)(2,1)S(1)}, bf16[2,64,3072]{2,1,0:T(8,128)(2,1)S(1)}, u32[]{:S(2)}, u32[]{:S(2)}) collective-permute-start(bf16[2,64,3072]{2,1,0:T(8,128)(2,1)S(1)} %pad_maximum_fusion.1.own_ref), channel_id=1, source_target_pairs={{0,2},{2,0},{4,6},{6,4},{1,3},{3,1},{5,7},{7,5},{8,10},{10,8},{12,... | collective-permute-start | bytes 2359304 | tf_op jit(solution)/shard_map/ppermute | solution.py:121
  111.3 80.0 %copy-start = (bf16[384,3072]{1,0:T(8,128)(2,1)S(1)}, bf16[384,3072]{1,0:T(8,128)(2,1)}, u32[]{:S(2)}) copy-start(bf16[384,3072]{1,0:T(8,128)(2,1)} %refs_5_.5) | copy-start | bytes 7077892
  111.3 63.2 %collective-permute-start.4 = (bf16[2,64,3072]{2,1,0:T(8,128)(2,1)S(1)}, bf16[2,64,3072]{2,1,0:T(8,128)(2,1)S(1)}, u32[]{:S(2)}, u32[]{:S(2)}) collective-permute-start(bf16[2,64,3072]{2,1,0:T(8,128)(2,1)S(1)} %pad_maximum_fusion.refs_0_), channel_id=1, source_target_pairs={{0,4},{2,6},{4,0},{6,2},{1,5},{3,7},{5,1},{7,3},{8,12},{10,14},{12... | collective-permute-start | bytes 2359304 | tf_op jit(solution)/shard_map/ppermute | solution.py:121
  114.8 60.2 %collective-permute-start.10 = (bf16[2,64,3072]{2,1,0:T(8,128)(2,1)S(1)}, bf16[2,64,3072]{2,1,0:T(8,128)(2,1)S(1)}, u32[]{:S(2)}, u32[]{:S(2)}) collective-permute-start(bf16[2,64,3072]{2,1,0:T(8,128)(2,1)S(1)} %pad_maximum_fusion.1.own_ref), channel_id=1, source_target_pairs={{0,8},{8,0},{16,24},{24,16},{1,9},{9,1},{17,25},{25,17},{2,10},{10... | collective-permute-start | bytes 2359304 | tf_op jit(solution)/shard_map/ppermute | solution.py:121
  157.0 34.3 %collective-permute-start.15 = (bf16[2,64,3072]{2,1,0:T(8,128)(2,1)S(1)}, bf16[2,64,3072]{2,1,0:T(8,128)(2,1)S(1)}, u32[]{:S(2)}, u32[]{:S(2)}) collective-permute-start(bf16[2,64,3072]{2,1,0:T(8,128)(2,1)S(1)} %collective-permute-done.13.own_ref), channel_id=1, source_target_pairs={{0,2},{2,0},{4,6},{6,4},{1,3},{3,1},{5,7},{7,5},{8,10},{10,8},{12,... | collective-permute-start | bytes 2359304 | tf_op jit(solution)/shard_map/ppermute | solution.py:121
  157.0 42.4 %collective-permute-start.12 = (bf16[2,64,3072]{2,1,0:T(8,128)(2,1)S(1)}, bf16[2,64,3072]{2,1,0:T(8,128)(2,1)S(1)}, u32[]{:S(2)}, u32[]{:S(2)}) collective-permute-start(bf16[2,64,3072]{2,1,0:T(8,128)(2,1)S(1)} %collective-permute-done.11.own_ref), channel_id=1, source_target_pairs={{0,8},{8,0},{16,24},{24,16},{1,9},{9,1},{17,25},{25,17},{2,10},{10... | collective-permute-start | bytes 2359304 | tf_op jit(solution)/shard_map/ppermute | solution.py:121
  157.0 52.1 %collective-permute-start.2 = (bf16[2,64,3072]{2,1,0:T(8,128)(2,1)S(1)}, bf16[2,64,3072]{2,1,0:T(8,128)(2,1)S(1)}, u32[]{:S(2)}, u32[]{:S(2)}) collective-permute-start(bf16[2,64,3072]{2,1,0:T(8,128)(2,1)S(1)} %pad_maximum_fusion.refs_0_), channel_id=1, source_target_pairs={{0,2},{2,0},{4,6},{6,4},{1,3},{3,1},{5,7},{7,5},{8,10},{10,8},{12,... | collective-permute-start | bytes 2359304 | tf_op jit(solution)/shard_map/ppermute | solution.py:121
  174.4 42.1 %collective-permute-start.6 = (bf16[2,64,3072]{2,1,0:T(8,128)(2,1)S(1)}, bf16[2,64,3072]{2,1,0:T(8,128)(2,1)}, u32[]{:S(2)}, u32[]{:S(2)}) collective-permute-start(bf16[2,64,3072]{2,1,0:T(8,128)(2,1)S(1)} %collective-permute-done.4.refs_4_), channel_id=1, source_target_pairs={{0,2},{2,0},{4,6},{6,4},{1,3},{3,1},{5,7},{7,5},{8,10},{10,8},{12,... | collective-permute-start | bytes 2359304 | tf_op jit(solution)/shard_map/ppermute | solution.py:121
  175.1 41.5 %collective-permute-start.14 = (bf16[2,64,3072]{2,1,0:T(8,128)(2,1)S(1)}, bf16[2,64,3072]{2,1,0:T(8,128)(2,1)S(1)}, u32[]{:S(2)}, u32[]{:S(2)}) collective-permute-start(bf16[2,64,3072]{2,1,0:T(8,128)(2,1)S(1)} %collective-permute-done.13.own_ref), channel_id=1, source_target_pairs={{0,8},{8,0},{16,24},{24,16},{1,9},{9,1},{17,25},{25,17},{2,10},{10... | collective-permute-start | bytes 2359304 | tf_op jit(solution)/shard_map/ppermute | solution.py:121
  191.3 34.7 %collective-permute-start.16 = (bf16[2,64,3072]{2,1,0:T(8,128)(2,1)S(1)}, bf16[2,64,3072]{2,1,0:T(8,128)(2,1)S(1)}, u32[]{:S(2)}, u32[]{:S(2)}) collective-permute-start(bf16[2,64,3072]{2,1,0:T(8,128)(2,1)S(1)} %collective-permute-done.15.own_ref), channel_id=1, source_target_pairs={{0,8},{8,0},{16,24},{24,16},{1,9},{9,1},{17,25},{25,17},{2,10},{10... | collective-permute-start | bytes 2359304 | tf_op jit(solution)/shard_map/ppermute | solution.py:121
  199.4 46.0 %collective-permute-start.1 = (bf16[2,64,3072]{2,1,0:T(8,128)(2,1)S(1)}, bf16[2,64,3072]{2,1,0:T(8,128)(2,1)}, u32[]{:S(2)}, u32[]{:S(2)}) collective-permute-start(bf16[2,64,3072]{2,1,0:T(8,128)(2,1)S(1)} %pad_maximum_fusion.refs_0_), channel_id=1, source_target_pairs={{0,8},{8,0},{16,24},{24,16},{1,9},{9,1},{17,25},{25,17},{2,10},{10... | collective-permute-start | bytes 2359304 | tf_op jit(solution)/shard_map/ppermute | solution.py:121
  209.1 36.3 %collective-permute-start.5 = (bf16[2,64,3072]{2,1,0:T(8,128)(2,1)S(1)}, bf16[2,64,3072]{2,1,0:T(8,128)(2,1)}, u32[]{:S(2)}, u32[]{:S(2)}) collective-permute-start(bf16[2,64,3072]{2,1,0:T(8,128)(2,1)S(1)} %collective-permute-done.4.refs_4_), channel_id=1, source_target_pairs={{0,8},{8,0},{16,24},{24,16},{1,9},{9,1},{17,25},{25,17},{2,10},{10... | collective-permute-start | bytes 2359304 | tf_op jit(solution)/shard_map/ppermute | solution.py:121
  216.6 28.9 %collective-permute-start.3 = (bf16[2,64,3072]{2,1,0:T(8,128)(2,1)S(1)}, bf16[2,64,3072]{2,1,0:T(8,128)(2,1)}, u32[]{:S(2)}, u32[]{:S(2)}) collective-permute-start(bf16[2,64,3072]{2,1,0:T(8,128)(2,1)S(1)} %collective-permute-done.2.refs_2_), channel_id=1, source_target_pairs={{0,8},{8,0},{16,24},{24,16},{1,9},{9,1},{17,25},{25,17},{2,10},{10... | collective-permute-start | bytes 2359304 | tf_op jit(solution)/shard_map/ppermute | solution.py:121
  216.6 28.9 %collective-permute-start.7 = (bf16[2,64,3072]{2,1,0:T(8,128)(2,1)}, bf16[2,64,3072]{2,1,0:T(8,128)(2,1)}, u32[]{:S(2)}, u32[]{:S(2)}) collective-permute-start(bf16[2,64,3072]{2,1,0:T(8,128)(2,1)} %collective-permute-done.6.refs_6_), channel_id=1, source_target_pairs={{0,8},{8,0},{16,24},{24,16},{1,9},{9,1},{17,25},{25,17},{2,10},{10... | collective-permute-start | bytes 2359304 | tf_op jit(solution)/shard_map/ppermute | solution.py:121
  234.9 30.0 %all-to-all-start.1 = ((bf16[4,768,256]{2,1,0:T(8,128)(2,1)}), bf16[4,768,256]{2,1,0:T(8,128)(2,1)}, u32[]{:S(2)}, u32[]{:S(2)}) async-start(bf16[4,768,256]{2,1,0:T(8,128)(2,1)} %pack.6), calls=%async_computation.1 | async-start | bytes 3145728 | tf_op jit(solution)/shard_map/all_to_all | solution.py:388
  264.9 41.7 %all-to-all-start.2 = ((bf16[4,768,512]{2,1,0:T(8,128)(2,1)}), bf16[4,768,512]{2,1,0:T(8,128)(2,1)}, u32[]{:S(2)}, u32[]{:S(2)}) async-start(bf16[4,768,512]{2,1,0:T(8,128)(2,1)} %copy-done.3), calls=%async_computation.2 | async-start | bytes 6291456 | tf_op jit(solution)/shard_map/all_to_all | solution.py:388
  306.5 41.6 %all-to-all-start.3 = ((bf16[4,768,512]{2,1,0:T(8,128)(2,1)}), bf16[4,768,512]{2,1,0:T(8,128)(2,1)}, u32[]{:S(2)}, u32[]{:S(2)}) async-start(bf16[4,768,512]{2,1,0:T(8,128)(2,1)} %copy-done.4), calls=%async_computation.3 | async-start | bytes 6291456 | tf_op jit(solution)/shard_map/all_to_all | solution.py:388
  311.2 145.6 %collective-permute-start.8 = (bf16[1024,1152]{1,0:T(8,128)(2,1)S(1)}, bf16[1024,1152]{1,0:T(8,128)(2,1)}, u32[]{:S(2)}, u32[]{:S(2)}) collective-permute-start(bf16[1024,1152]{1,0:T(8,128)(2,1)S(1)} %in_product.5.q_own.k_own.v_own), channel_id=1, source_target_pairs={{0,1},{1,0},{2,3},{3,2},{4,5},{5,4},{6,7},{7,6},{8,9},{9,8},{10,11... | collective-permute-start | bytes 7077896 | tf_op jit(solution)/shard_map/ppermute | solution.py:121
  312.9 73.7 %collective-permute-start.17 = (bf16[256,1920]{1,0:T(8,128)(2,1)S(1)}, bf16[256,1920]{1,0:T(8,128)(2,1)}, u32[]{:S(2)}, u32[]{:S(2)}) collective-permute-start(bf16[256,1920]{1,0:T(8,128)(2,1)S(1)} %cot_product.4), channel_id=1, source_target_pairs={{0,1},{1,0},{2,3},{3,2},{4,5},{5,4},{6,7},{7,6},{8,9},{9,8},{10,11... | collective-permute-start | bytes 2949128 | tf_op jit(solution)/shard_map/ppermute | solution.py:121
  313.3 94.3 %collective-permute-start.18 = (bf16[256,1920]{1,0:T(8,128)(2,1)}, bf16[256,1920]{1,0:T(8,128)(2,1)}, u32[]{:S(2)}, u32[]{:S(2)}) collective-permute-start(bf16[256,1920]{1,0:T(8,128)(2,1)} %copy-done.6), channel_id=1, source_target_pairs={{0,1},{1,0},{2,3},{3,2},{4,5},{5,4},{6,7},{7,6},{8,9},{9,8},{10,11... | collective-permute-start | bytes 2949128 | tf_op jit(solution)/shard_map/ppermute | solution.py:121
  318.3 110.4 %collective-permute-start.19 = (bf16[256,1920]{1,0:T(8,128)(2,1)}, bf16[256,1920]{1,0:T(8,128)(2,1)}, u32[]{:S(2)}, u32[]{:S(2)}) collective-permute-start(bf16[256,1920]{1,0:T(8,128)(2,1)} %cot_product.6), channel_id=1, source_target_pairs={{0,1},{1,0},{2,3},{3,2},{4,5},{5,4},{6,7},{7,6},{8,9},{9,8},{10,11... | collective-permute-start | bytes 2949128 | tf_op jit(solution)/shard_map/ppermute | solution.py:121
  318.7 131.0 %collective-permute-start.20 = (bf16[256,1920]{1,0:T(8,128)(2,1)}, bf16[256,1920]{1,0:T(8,128)(2,1)}, u32[]{:S(2)}, u32[]{:S(2)}) collective-permute-start(bf16[256,1920]{1,0:T(8,128)(2,1)} %cot_product.7), channel_id=1, source_target_pairs={{0,1},{1,0},{2,3},{3,2},{4,5},{5,4},{6,7},{7,6},{8,9},{9,8},{10,11... | collective-permute-start | bytes 2949128 | tf_op jit(solution)/shard_map/ppermute | solution.py:121
  348.2 128.8 %all-to-all-start.4 = ((bf16[4,768,256]{2,1,0:T(8,128)(2,1)}), bf16[4,768,256]{2,1,0:T(8,128)(2,1)}, u32[]{:S(2)}, u32[]{:S(2)}) async-start(bf16[4,768,256]{2,1,0:T(8,128)(2,1)} %copy-done.5), calls=%async_computation.4 | async-start | bytes 3145728 | tf_op jit(solution)/shard_map/all_to_all | solution.py:388
  352.7 97.0 %copy-start.7 = (bf16[256,1920]{1,0:T(8,128)(2,1)S(1)}, bf16[256,1920]{1,0:T(8,128)(2,1)}, u32[]{:S(2)}) copy-start(bf16[256,1920]{1,0:T(8,128)(2,1)} %copy-done.6) | copy-start | bytes 2949124
  386.5 96.1 %collective-permute-start.22 = (bf16[1024,512]{1,0:T(8,128)(2,1)}, bf16[1024,512]{1,0:T(8,128)(2,1)}, u32[]{:S(2)}, u32[]{:S(2)}) collective-permute-start(bf16[1024,512]{1,0:T(8,128)(2,1)} %in_product.7), channel_id=1, source_target_pairs={{0,1},{1,0},{2,3},{3,2},{4,5},{5,4},{6,7},{7,6},{8,9},{9,8},{10,11... | collective-permute-start | bytes 3145736 | tf_op jit(solution)/shard_map/ppermute | solution.py:121
  407.6 87.1 %collective-permute-start.23 = (bf16[1024,512]{1,0:T(8,128)(2,1)}, bf16[1024,512]{1,0:T(8,128)(2,1)}, u32[]{:S(2)}, u32[]{:S(2)}) collective-permute-start(bf16[1024,512]{1,0:T(8,128)(2,1)} %in_product.8), channel_id=1, source_target_pairs={{0,1},{1,0},{2,3},{3,2},{4,5},{5,4},{6,7},{7,6},{8,9},{9,8},{10,11... | collective-permute-start | bytes 3145736 | tf_op jit(solution)/shard_map/ppermute | solution.py:121
  455.2 50.7 %collective-permute-start.21 = (bf16[1024,256]{1,0:T(8,128)(2,1)}, bf16[1024,256]{1,0:T(8,128)(2,1)}, u32[]{:S(2)}, u32[]{:S(2)}) collective-permute-start(bf16[1024,256]{1,0:T(8,128)(2,1)} %in_product.6), channel_id=1, source_target_pairs={{0,1},{1,0},{2,3},{3,2},{4,5},{5,4},{6,7},{7,6},{8,9},{9,8},{10,11... | collective-permute-start | bytes 1572872 | tf_op jit(solution)/shard_map/ppermute | solution.py:121
  477.0 17.7 %copy-start.2 = (bf16[4,4,64,1920]{3,2,1,0:T(8,128)(2,1)S(1)}, bf16[4,4,64,1920]{3,2,1,0:T(8,128)(2,1)}, u32[]{:S(2)}) copy-start(bf16[4,4,64,1920]{3,2,1,0:T(8,128)(2,1)} %add_parts.1) | copy-start | bytes 11796484
  482.1 34.4 %collective-permute-start.24 = (bf16[1024,256]{1,0:T(8,128)(2,1)S(1)}, bf16[1024,256]{1,0:T(8,128)(2,1)S(1)}, u32[]{:S(2)}, u32[]{:S(2)}) collective-permute-start(bf16[1024,256]{1,0:T(8,128)(2,1)S(1)} %in_product.9), channel_id=1, source_target_pairs={{0,1},{1,0},{2,3},{3,2},{4,5},{5,4},{6,7},{7,6},{8,9},{9,8},{10,11... | collective-permute-start | bytes 1572872 | tf_op jit(solution)/shard_map/ppermute | solution.py:121
  499.0 19.8 %copy-start.11 = (bf16[1024,384]{1,0:T(8,128)(2,1)S(1)}, bf16[1024,384]{1,0:T(8,128)(2,1)}, u32[]{:S(2)}) copy-start(bf16[1024,384]{1,0:T(8,128)(2,1)} %copy-done.10) | copy-start | bytes 2359300
  499.1 19.8 %copy-start.13 = (bf16[1024,384]{1,0:T(8,128)(2,1)S(1)}, bf16[1024,384]{1,0:T(8,128)(2,1)}, u32[]{:S(2)}) copy-start(bf16[1024,384]{1,0:T(8,128)(2,1)} %copy-done.12) | copy-start | bytes 2359300
  499.1 19.8 %copy-start.15 = (bf16[1024,384]{1,0:T(8,128)(2,1)S(1)}, bf16[1024,384]{1,0:T(8,128)(2,1)}, u32[]{:S(2)}) copy-start(bf16[1024,384]{1,0:T(8,128)(2,1)} %copy-done.14) | copy-start | bytes 2359300
  532.6 11.6 %collective-permute-start.29 = (bf16[512,3072]{1,0:T(8,128)(2,1)}, bf16[512,3072]{1,0:T(8,128)(2,1)}, u32[]{:S(2)}, u32[]{:S(2)}) collective-permute-start(bf16[512,3072]{1,0:T(8,128)(2,1)} %back_product.2), channel_id=1, source_target_pairs={{0,8},{8,0},{16,24},{24,16},{1,9},{9,1},{17,25},{25,17},{2,10},{10... | collective-permute-start | bytes 9437192 | tf_op jit(solution)/shard_map/ppermute | solution.py:121
  543.7 17.1 %collective-permute-start.25 = (bf16[512,3072]{1,0:T(8,128)(2,1)}, bf16[512,3072]{1,0:T(8,128)(2,1)S(1)}, u32[]{:S(2)}, u32[]{:S(2)}) collective-permute-start(bf16[512,3072]{1,0:T(8,128)(2,1)} %out_product.3), channel_id=1, source_target_pairs={{0,8},{8,0},{16,24},{24,16},{1,9},{9,1},{17,25},{25,17},{2,10},{10... | collective-permute-start | bytes 9437192 | tf_op jit(solution)/shard_map/ppermute | solution.py:121
  560.7 36.4 %collective-permute-start.30 = (bf16[2,2,64,3072]{3,2,0,1:T(8,128)(2,1)S(1)}, bf16[2,2,64,3072]{3,2,0,1:T(8,128)(2,1)S(1)}, u32[]{:S(2)}, u32[]{:S(2)}) collective-permute-start(bf16[2,2,64,3072]{3,2,0,1:T(8,128)(2,1)S(1)} %bitcast.69), channel_id=1, source_target_pairs={{0,2},{2,0},{4,6},{6,4},{1,3},{3,1},{5,7},{7,5},{8,10},{10,8},{12,... | collective-permute-start | bytes 4718600 | tf_op jit(solution)/shard_map/ppermute | solution.py:121
  570.4 36.4 %collective-permute-start.26 = (bf16[256,3072]{1,0:T(8,128)(2,1)S(1)}, bf16[256,3072]{1,0:T(8,128)(2,1)S(1)}, u32[]{:S(2)}, u32[]{:S(2)}) collective-permute-start(bf16[256,3072]{1,0:T(8,128)(2,1)S(1)} %out_product.5), channel_id=1, source_target_pairs={{0,16},{8,24},{16,0},{24,8},{1,17},{9,25},{17,1},{25,9},{2,18},{10... | collective-permute-start | bytes 4718600 | tf_op jit(solution)/shard_map/ppermute | solution.py:121
  597.1 9.7 %copy-start.17 = (f32[256,3072]{1,0:T(8,128)S(1)}, f32[256,3072]{1,0:T(8,128)}, u32[]{:S(2)}) copy-start(f32[256,3072]{1,0:T(8,128)} %out_product.4) | copy-start | bytes 9437188
  597.7 36.5 %collective-permute-start.31 = (bf16[2,64,3072]{2,1,0:T(8,128)(2,1)S(1)}, bf16[2,64,3072]{2,1,0:T(8,128)(2,1)S(1)}, u32[]{:S(2)}, u32[]{:S(2)}) collective-permute-start(bf16[2,64,3072]{2,1,0:T(8,128)(2,1)S(1)} %fusion.37), channel_id=1, source_target_pairs={{0,4},{2,6},{4,0},{6,2},{1,5},{3,7},{5,1},{7,3},{8,12},{10,14},{12... | collective-permute-start | bytes 2359304 | tf_op jit(solution)/shard_map/ppermute | solution.py:121
  607.4 35.4 %collective-permute-start.27 = (bf16[2,64,3072]{2,1,0:T(8,128)(2,1)S(1)}, bf16[2,64,3072]{2,1,0:T(8,128)(2,1)S(1)}, u32[]{:S(2)}, u32[]{:S(2)}) collective-permute-start(bf16[2,64,3072]{2,1,0:T(8,128)(2,1)S(1)} %fusion.38), channel_id=1, source_target_pairs={{0,2},{2,0},{4,6},{6,4},{1,3},{3,1},{5,7},{7,5},{8,10},{10,8},{12,... | collective-permute-start | bytes 2359304 | tf_op jit(solution)/shard_map/ppermute | solution.py:121
  634.5 11.8 %copy-start.19 = (bf16[64,3072]{1,0:T(8,128)(2,1)S(1)}, bf16[64,3072]{1,0:T(8,128)(2,1)}, u32[]{:S(2)}) copy-start(bf16[64,3072]{1,0:T(8,128)(2,1)} %param.8) | copy-start | bytes 1179652
  634.5 11.0 %collective-permute-start.32 = (bf16[64,3072]{1,0:T(8,128)(2,1)S(1)}, bf16[64,3072]{1,0:T(8,128)(2,1)S(1)}, u32[]{:S(2)}, u32[]{:S(2)}) collective-permute-start(bf16[64,3072]{1,0:T(8,128)(2,1)S(1)} %fusion.42), channel_id=1, source_target_pairs={{0,16},{8,24},{16,0},{24,8},{1,17},{9,25},{17,1},{25,9},{2,18},{10... | collective-permute-start | bytes 1179656 | tf_op jit(solution)/shard_map/ppermute | solution.py:121
  643.8 17.9 %collective-permute-start.28 = (bf16[64,3072]{1,0:T(8,128)(2,1)}, bf16[64,3072]{1,0:T(8,128)(2,1)}, u32[]{:S(2)}, u32[]{:S(2)}) collective-permute-start(bf16[64,3072]{1,0:T(8,128)(2,1)} %fusion.41), channel_id=1, source_target_pairs={{0,4},{2,6},{4,0},{6,2},{1,5},{3,7},{5,1},{7,3},{8,12},{10,14},{12... | collective-permute-start | bytes 1179656 | tf_op jit(solution)/shard_map/ppermute | solution.py:121
  (12 other events, 16.0 us)

commit v6 on v5

--- a/solution.py
+++ b/solution.py
@@ -278,36 +278,36 @@
     )(rows, weight)
 
 
-def out_product(mixed, acts, w_attn_out, w_mlp_out, start, count, add, add_start, kind):
-    columns = w_attn_out.shape[1]
+def product(terms, weights, adds, start, count, kind, transposed):
+    columns = weights[0].shape[0 if transposed else 1]
     tile = 512 if columns % 512 == 0 else 256
-    n_acts = len(acts)
-
-    def rows_spec(value):
-        return pl.BlockSpec((count, value.shape[1]), lambda n: (start // count, 0))
-
-    def columns_spec(value):
-        return pl.BlockSpec((value.shape[0], tile), lambda n: (0, n))
-
-    operands = [mixed, *acts, w_attn_out, w_mlp_out]
-    specs = [rows_spec(mixed), *(rows_spec(act) for act in acts)]
-    specs += [columns_spec(w_attn_out), columns_spec(w_mlp_out)]
-    if add is not None:
-        operands.append(add)
-        specs.append(pl.BlockSpec((count, tile), lambda n: (add_start // count, n)))
+    specs = [
+        pl.BlockSpec((count, value.shape[1]), lambda n: (start // count, 0))
+        for value, _, _ in terms
+    ]
+    for weight in weights:
+        if transposed:
+            specs.append(pl.BlockSpec((tile, weight.shape[1]), lambda n: (n, 0)))
+        else:
+            specs.append(pl.BlockSpec((weight.shape[0], tile), lambda n: (0, n)))
+    for _, first in adds:
+        specs.append(pl.BlockSpec((count, tile), lambda n, place=first // count: (place, n)))
 
     def kernel(*refs):
-        attn_ref, mlp_ref, out_ref = refs[n_acts + 1], refs[n_acts + 2], refs[-1]
-        total = dot(refs[0][...], attn_ref[...])
-        row = 0
-        for act in refs[1 : n_acts + 1]:
-            total = total + dot(act[...], mlp_ref[row : row + act.shape[1], :])
-            row += act.shape[1]
-        if add is not None:
-            total = total + refs[n_acts + 3][...].astype(jnp.float32)
-        out_ref[...] = total.astype(out_ref.dtype)
-
-    depth = w_attn_out.shape[0] + w_mlp_out.shape[0]
+        weight_refs = refs[len(terms) : len(terms) + len(weights)]
+        total = None
+        for ref, (value, index, offset) in zip(refs, terms):
+            summed = slice(offset, offset + value.shape[1])
+            if transposed:
+                part = back_dot(ref[...], weight_refs[index][:, summed])
+            else:
+                part = dot(ref[...], weight_refs[index][summed, :])
+            total = part if total is None else total + part
+        for ref in refs[len(terms) + len(weights) : -1]:
+            total = total + ref[...].astype(jnp.float32)
+        refs[-1][...] = total.astype(kind)
+
+    depth = sum(value.shape[1] for value, _, _ in terms)
     out = jax.ShapeDtypeStruct((count, columns), kind)
     return pl.pallas_call(
         kernel,
@@ -316,53 +316,13 @@
         out_specs=pl.BlockSpec((count, tile), lambda n: (0, n)),
         out_shape=out,
         compiler_params=params(),
-        cost_estimate=cost(2 * count * columns * depth, out, w_attn_out, w_mlp_out),
-        name="out_product",
-    )(*operands)
-
-
-def back_product(head_grads, mlp_grads, in_heads, in_mlp, start, count, add):
-    features = in_heads.shape[0]
-    tile = 512 if features % 512 == 0 else 256
-    n_heads = len(head_grads)
-    grads = [*head_grads, *mlp_grads]
-    weights = [in_heads, *in_mlp]
-    specs = [pl.BlockSpec((count, grad.shape[1]), lambda n: (start // count, 0)) for grad in grads]
-    specs += [pl.BlockSpec((tile, weight.shape[1]), lambda n: (n, 0)) for weight in weights]
-    operands = grads + weights
-    if add is not None:
-        operands.append(add)
-        specs.append(pl.BlockSpec((count, tile), lambda n: (0, n)))
-
-    def kernel(*refs):
-        out_ref, heads_ref = refs[-1], refs[len(grads)]
-        mlp_refs = refs[len(grads) + 1 : len(grads) + len(weights)]
-        total, column = None, 0
-        for grad in refs[:n_heads]:
-            part = back_dot(grad[...], heads_ref[:, column : column + grad.shape[1]])
-            total = part if total is None else total + part
-            column += grad.shape[1]
-        for grad, weight in zip(refs[n_heads : len(grads)], mlp_refs):
-            total = total + back_dot(grad[...], weight[...])
-        if add is not None:
-            total = total + refs[-2][...].astype(jnp.float32)
-        out_ref[...] = total.astype(out_ref.dtype)
-
-    width = sum(grad.shape[1] for grad in grads)
-    out = jax.ShapeDtypeStruct((count, features), jnp.bfloat16)
-    return pl.pallas_call(
-        kernel,
-        grid=(features // tile,),
-        in_specs=specs,
-        out_specs=pl.BlockSpec((count, tile), lambda n: (0, n)),
-        out_shape=out,
-        compiler_params=params(),
-        cost_estimate=cost(2 * count * features * width, out, *weights),
-        name="back_product",
-    )(*operands)
+        cost_estimate=cost(2 * count * columns * depth, out, *weights),
+        name="back_product" if transposed else "out_product",
+    )(*(value for value, _, _ in terms), *weights, *(add for add, _ in adds))
 
 
 MLP_CUTS = (256, 512, 512, 256)
+EARLY_CUTS = 2
 
 
 def body(layer_input, out_cotangent, w_query, w_key, w_value, w_mlp_in, w_attn_out, w_mlp_out):
@@ -378,8 +338,10 @@
             return trade(part, "gz", 1)
         return half(lax.psum(part.astype(jnp.float32), "gz") - part.astype(jnp.float32))
 
-    def gather_parts(block):
-        pair = jnp.stack([block, trade(block, "gx", 2)])
+    def with_x(block):
+        return jnp.stack([block, trade(block, "gx", 2)])
+
+    def gather_parts(pair):
         near, far = trade(pair, "gy", 1), trade(pair, "gy", 2)
         parts = [pair, near, far, trade(far, "gy", 1)]
         return [(part, trade(part, "gx", 1)) for part in parts]
@@ -394,12 +356,9 @@
     packed_mlp = [
         pack((w_mlp_in,), n_gx, start, width, 256) for start, width in zip(starts, MLP_CUTS)
     ]
-    in_heads = swap(packed_heads)
-
-    cot_owns = [
-        cot_product(part, w_attn_out, w_mlp_out) for part in gather_parts(out_cotangent)
-    ]
-    cot_gots = [others(own) for own in cot_owns]
+
+    cot_pair = with_x(out_cotangent)
+    in_mlp = [swap(after(packed_mlp[0], cot_pair))]
 
     wide = layer_input.astype(jnp.float32)
     total, squares = lax.psum((jnp.sum(wide, axis=1), jnp.sum(wide * wide, axis=1)), "gz")
@@ -407,47 +366,83 @@
     spread = squares / D - center * center
     inverse = lax.rsqrt(spread + EPSILON)
     normed = (wide - center[:, None]) * inverse[:, None]
-    all_in = assemble(gather_parts(half(normed)))
-
-    heads_own = in_product(all_in, in_heads)
+    normed_pair = with_x(half(normed))
+    in_heads = swap(after(packed_heads, normed_pair, in_mlp[0]))
+
+    cot_owns, cot_gots = [], []
+    for place, (own, other) in enumerate(gather_parts(cot_pair)):
+        if place >= 2:
+            own = after(own, cot_gots[place - 2])
+        cot_owns.append(cot_product((own, other), w_attn_out, w_mlp_out))
+        cot_gots.append(others(cot_owns[-1]))
+
+    all_in = assemble(gather_parts(normed_pair))
+    mlp_own = [in_product(after(all_in, cot_gots[2]), in_mlp[0])]
+    mlp_got = [others(mlp_own[0])]
+    heads_own = in_product(after(all_in, cot_gots[3], mlp_own[0]), in_heads)
     heads_got = others(heads_own)
-    in_mlp, mlp_own, mlp_got = [], [], []
-    turn = (in_heads, *cot_owns)
-    for cut in range(len(MLP_CUTS)):
-        weight = swap(after(packed_mlp[cut], *turn))
-        turn = (weight, mlp_own[-1] if mlp_own else heads_own)
-        in_mlp.append(weight)
-        mlp_own.append(in_product(all_in, weight))
-        mlp_got.append(others(mlp_own[-1]))
+    in_mlp.append(swap(after(packed_mlp[1], in_heads, mlp_own[0])))
+    mlp_own.append(in_product(after(all_in, mlp_got[0]), in_mlp[1]))
+    mlp_got.append(others(mlp_own[1]))
+    in_mlp.append(swap(after(packed_mlp[2], in_mlp[1], heads_own)))
+    mlp_own.append(in_product(after(all_in, heads_got), in_mlp[2]))
+    mlp_got.append(others(mlp_own[2]))
+    in_mlp.append(swap(after(packed_mlp[3], in_mlp[2], mlp_own[1])))
 
     out_grad = add_parts(cot_owns, cot_gots)
     mixed, *head_grads = attend(heads_own, heads_got, out_grad)
-    acts, mlp_grads = [], []
-    for start, own, got in zip(starts, mlp_own, mlp_got):
-        pre = wide_sum(own, got)
-        acts.append(half(gelu(pre)))
-        first = heads_width + start
-        mlp_grads.append(gelu_back(pre, out_grad[:, first : first + own.shape[1]]))
-
-    def forward_term(start, size, add, add_start, kind):
-        return out_product(mixed, acts, w_attn_out, w_mlp_out, start, size, add, add_start, kind)
-
-    def backward_term(start, size, add):
-        return back_product(head_grads, mlp_grads, in_heads, in_mlp, start, size, add)
+    mlp_own.append(in_product(after(all_in, mlp_got[1], mixed), in_mlp[3]))
+    mlp_got.append(others(mlp_own[3]))
+
+    forward_terms, backward_terms = [(mixed, 0, 0)], []
+    for index, grad in enumerate(head_grads):
+        backward_terms.append((grad, 0, index * heads_width))
+
+    def add_terms(cut, own):
+        pre = wide_sum(own, mlp_got[cut])
+        first = heads_width + starts[cut]
+        grad = gelu_back(pre, out_grad[:, first : first + own.shape[1]])
+        forward_terms.append((half(gelu(pre)), 1, starts[cut]))
+        backward_terms.append((grad, 1 + cut, 0))
+
+    out_weights, in_weights = [w_attn_out, w_mlp_out], [in_heads, *in_mlp]
+    for cut in range(EARLY_CUTS):
+        add_terms(cut, mlp_own[cut])
+    rows = 4 * count
+    forward_early = product(forward_terms, out_weights, [], 0, rows, jnp.bfloat16, False)
+    backward_early = product(
+        backward_terms, in_weights[: 1 + EARLY_CUTS], [], 0, rows, jnp.bfloat16, True
+    )
+    del forward_terms[:], backward_terms[:]
+    for cut in range(EARLY_CUTS, len(MLP_CUTS)):
+        add_terms(cut, after(mlp_own[cut], forward_early, backward_early))
+    late_weights = in_weights[1 + EARLY_CUTS :]
+    backward_terms = [
+        (grad, index - 1 - EARLY_CUTS, offset) for grad, index, offset in backward_terms
+    ]
+    forward_terms = [(act, 0, offset) for act, _, offset in forward_terms]
+
+    def forward_term(start, size, adds, kind):
+        adds = [(forward_early, start), *adds]
+        return product(forward_terms, [w_mlp_out], adds, start, size, kind, False)
+
+    def backward_term(start, size, adds):
+        adds = [(backward_early, start), *adds]
+        return product(backward_terms, late_weights, adds, start, size, jnp.bfloat16, True)
 
     def wider(value):
         return value.astype(jnp.float32)
 
-    from_core = trade(forward_term(0, 2 * count, None, 0, jnp.bfloat16), "gx", 1)
-    from_x = trade(forward_term(2 * count, count, from_core, 0, jnp.bfloat16), "gx", 2)
-    mine = forward_term(3 * count, count, from_core, count, jnp.float32) + wider(from_x)
+    from_core = trade(forward_term(0, 2 * count, [], jnp.bfloat16), "gx", 1)
+    from_x = trade(forward_term(2 * count, count, [(from_core, 0)], jnp.bfloat16), "gx", 2)
+    mine = forward_term(3 * count, count, [(from_core, count)], jnp.float32) + wider(from_x)
     mine = mine.reshape(2, 2, own_rows, features)
     pair = mine[:, 0] + wider(trade(half(mine[:, 1]), "gy", 1))
     summed = pair[0] + wider(trade(half(pair[1]), "gy", 2))
     layer_out = half(wide + summed)
 
-    from_core = trade(backward_term(0, 2 * count, None), "gx", 1)
-    both = backward_term(2 * count, 2 * count, from_core).reshape(2, 2, 2, own_rows, features)
+    from_core = trade(backward_term(0, 2 * count, []), "gx", 1)
+    both = backward_term(2 * count, 2 * count, [(from_core, 0)]).reshape(2, 2, 2, own_rows, features)
     pair = wide_sum(both[:, :, 0], trade(both[:, :, 1], "gy", 1))
     ends = pair[:, 0] + wider(trade(half(pair[:, 1]), "gy", 2))
     normed_grad = ends[1] + wider(trade(half(ends[0]), "gx", 2))

time: 667 us -> 537 us (0.81)
  waiting for transfers between devices: 388 us -> 239 us
  Pallas kernels: 177 us -> 185 us
    ppermute x33, waiting for transfers between devices: 343 us -> 239 us  [trade(): return lax.ppermute(block, axis, pairs)]
    all_to_all x5, waiting for transfers between devices: 45.2 us -> 0.01 us  [swap(): lax.all_to_all(packed, 'gx', split_axis=0, concat_axis=0, tiled=True)]
    pallas_call x5 -> x7, Pallas kernels: 56.3 us -> 67.8 us  [product(): pl.pallas_call(kernel, grid=(columns // tile,), in_specs=specs, out_specs...]
    unnamed x45 -> x81, local copies, waits for them, and re-layouts: 16.1 us -> 22.3 us
  transfers between devices with their start and end apart: 38 -> 38, of which waited for: 21 -> 15; matrix products, arithmetic and copies ran while one was open for 2% -> 3% of each run, Pallas kernels for 24% -> 33%
where the time goes in v6:
time: 537 us; the launch traced here: 535 us
  waiting for transfers between devices  239 us (45%)
  Pallas kernels  185 us (34%)
  starting transfers between devices  57.4 us (11%)
  local copies, waits for them, and re-layouts  24.7 us (5%)
  other arithmetic  16.5 us (3%)
  blocking collectives  10.4 us (2%)
    ppermute x33, waiting for transfers between devices, trade(): return lax.ppermute(block, axis, pairs)  239 us
    pallas_call x7, Pallas kernels, product(): pl.pallas_call(kernel, grid=(columns // tile,), in_specs=specs, out_specs...  67.8 us
    pallas_call x5, Pallas kernels, in_product(): pl.pallas_call(in_kernel, grid=(columns // tile,), in_specs=[pl.BlockSpec...  39.5 us
    ppermute x33, starting transfers between devices, trade(): return lax.ppermute(block, axis, pairs)  33.3 us
    pallas_call x4, Pallas kernels, cot_product(): pl.pallas_call(cot_kernel, grid=(columns // tile,), in_specs=[whole, whol...  33.2 us
    all_to_all x5, starting transfers between devices, swap(): lax.all_to_all(packed, 'gx', split_axis=0, concat_axis=0, tiled=True)  24 us
    unnamed x81, local copies, waits for them, and re-layouts  22.3 us
    pallas_call x5, Pallas kernels, pack(): pl.pallas_call(pack_kernel, grid=(owners, width // tile), in_specs=[spec]...  20 us
  transfers between devices with their start and end apart: 38, of which 15 were waited for; matrix products, arithmetic and copies ran while one was open for 3% of the time, Pallas kernels for 33%

profile of v6, /device:TPU:0, one launch (start us, length us, event | category | flops | bytes accessed | tf_op | source)
XLA Modules:
  0.0 534.7 jit_solution(12163655257181256765)
XLA Ops:
  0.7 3.0 collective-permute-start.8
  3.7 3.6 pack.5
  7.5 4.9 all-reduce.1
  13.9 4.5 all-to-all-start
  22.3 5.2 pack.6
  27.7 19.2 %collective-permute-done = bf16[64,3072]{1,0:T(8,128)(2,1)S(1)} collective-permute-done((bf16[64,3072]{1,0:T(8,128)(2,1)S(1)}, bf16[64,3072]{1,0:T(8,128)(2,1)S(1)}, u32[]{:S(2)}, u32[]{:S(2)}) %collective-permute-start) | collective-permute-done | bytes 393248 | tf_op jit(solution)/shard_map/ppermute | solution.py:121
  47.9 5.5 %all-to-all-start.1 = ((bf16[4,768,1152]{2,1,0:T(8,128)(2,1)}), bf16[4,768,1152]{2,1,0:T(8,128)(2,1)}, u32[]{:S(2)}, u32[]{:S(2)}) async-start(bf16[4,768,1152]{2,1,0:T(8,128)(2,1)} %pack.6), calls=%async_computation.1 | async-start | bytes 14155776 | tf_op jit(solution)/shard_map/all_to_all | solution.py:350
  55.7 2.6 collective-permute-start.9
  58.7 8.3 %cot_product.6 = bf16[256,1920]{1,0:T(8,128)(2,1)S(1)} custom-call(bf16[2,64,3072]{2,1,0:T(8,128)(2,1)} %pad_maximum_fusion.1.own_ref, bf16[2,64,3072]{2,1,0:T(8,128)(2,1)S(1)} %collective-permute-done.16.other_ref, bf16[384,3072]{1,0:T(8,128)(2,1)S(1)} %copy-done, bf16[1536,3072]{1,0:T(8,128)(2,1)} %refs_2_.7), custom_call_target="tpu_custom_call" | custom-call | flops 3019898880 | bytes 12779520 | tf_op jit(solution)/shard_map/cot_product/pallas_call | solution.py:214
  69.9 21.3 %collective-permute-done.11.own_ref = bf16[2,64,3072]{2,1,0:T(8,128)(2,1)S(1)} collective-permute-done((bf16[2,64,3072]{2,1,0:T(8,128)(2,1)}, bf16[2,64,3072]{2,1,0:T(8,128)(2,1)S(1)}, u32[]{:S(2)}, u32[]{:S(2)}) %collective-permute-start.11) | collective-permute-done | bytes 786464 | tf_op jit(solution)/shard_map/ppermute | solution.py:121
  91.2 19.8 %collective-permute-done.9.own_ref = bf16[2,64,3072]{2,1,0:T(8,128)(2,1)S(1)} collective-permute-done((bf16[2,64,3072]{2,1,0:T(8,128)(2,1)}, bf16[2,64,3072]{2,1,0:T(8,128)(2,1)S(1)}, u32[]{:S(2)}, u32[]{:S(2)}) %collective-permute-start.9) | collective-permute-done | bytes 786464 | tf_op jit(solution)/shard_map/ppermute | solution.py:121
  111.0 15.8 %collective-permute-done.4.refs_4_ = bf16[2,64,3072]{2,1,0:T(8,128)(2,1)S(1)} collective-permute-done((bf16[2,64,3072]{2,1,0:T(8,128)(2,1)}, bf16[2,64,3072]{2,1,0:T(8,128)(2,1)S(1)}, u32[]{:S(2)}, u32[]{:S(2)}) %collective-permute-start.4) | collective-permute-done | bytes 786464 | tf_op jit(solution)/shard_map/ppermute | solution.py:121
  129.8 8.1 %cot_product.4 = bf16[256,1920]{1,0:T(8,128)(2,1)S(1)} custom-call(bf16[2,64,3072]{2,1,0:T(8,128)(2,1)S(1)} %collective-permute-done.11.own_ref, bf16[2,64,3072]{2,1,0:T(8,128)(2,1)S(1)} %collective-permute-done.12.other_ref, bf16[384,3072]{1,0:T(8,128)(2,1)S(1)} %copy-done, bf16[1536,3072]{1,0:T(8,128)(2,1)} %refs_2_.7), custom_call_target="tpu_custom_call" | custom-call | flops 3019898880 | bytes 12779520 | tf_op jit(solution)/shard_map/cot_product/pallas_call | solution.py:214
  139.5 8.1 %cot_product.7 = bf16[256,1920]{1,0:T(8,128)(2,1)S(1)} custom-call(bf16[2,64,3072]{2,1,0:T(8,128)(2,1)S(1)} %collective-permute-done.9.own_ref, bf16[2,64,3072]{2,1,0:T(8,128)(2,1)S(1)} %collective-permute-done.18.other_ref, bf16[384,3072]{1,0:T(8,128)(2,1)S(1)} %copy-done, bf16[1536,3072]{1,0:T(8,128)(2,1)} %refs_2_.7), custom_call_target="tpu_custom_call" | custom-call | flops 3019898880 | bytes 12779520 | tf_op jit(solution)/shard_map/cot_product/pallas_call | solution.py:214
  148.3 15.3 %collective-permute-done.6.refs_6_ = bf16[2,64,3072]{2,1,0:T(8,128)(2,1)S(1)} collective-permute-done((bf16[2,64,3072]{2,1,0:T(8,128)(2,1)S(1)}, bf16[2,64,3072]{2,1,0:T(8,128)(2,1)S(1)}, u32[]{:S(2)}, u32[]{:S(2)}) %collective-permute-start.6) | collective-permute-done | bytes 786464 | tf_op jit(solution)/shard_map/ppermute | solution.py:121
  164.1 4.5 pack.8
  171.4 4.8 assemble.1.rows_ref
  177.2 6.0 %collective-permute-done.19 = bf16[256,1920]{1,0:T(8,128)(2,1)S(1)} collective-permute-done((bf16[256,1920]{1,0:T(8,128)(2,1)S(1)}, bf16[256,1920]{1,0:T(8,128)(2,1)S(1)}, u32[]{:S(2)}, u32[]{:S(2)}) %collective-permute-start.19) | collective-permute-done | bytes 983072 | tf_op jit(solution)/shard_map/ppermute | solution.py:121
  184.2 5.0 in_product.5
  190.0 4.8 all-to-all-start.2
  194.8 8.6 %cot_product.5 = bf16[256,1920]{1,0:T(8,128)(2,1)S(1)} custom-call(bf16[2,64,3072]{2,1,0:T(8,128)(2,1)} %collective-permute-done.10.own_ref, bf16[2,64,3072]{2,1,0:T(8,128)(2,1)} %collective-permute-done.14.other_ref, bf16[384,3072]{1,0:T(8,128)(2,1)S(1)} %copy-done, bf16[1536,3072]{1,0:T(8,128)(2,1)} %refs_2_.7), custom_call_target="tpu_custom_call" | custom-call | flops 3019898880 | bytes 12779520 | tf_op jit(solution)/shard_map/cot_product/pallas_call | solution.py:214
  205.9 21.6 %collective-permute-done.15 = bf16[256,1920]{1,0:T(8,128)(2,1)} collective-permute-done((bf16[256,1920]{1,0:T(8,128)(2,1)S(1)}, bf16[256,1920]{1,0:T(8,128)(2,1)}, u32[]{:S(2)}, u32[]{:S(2)}) %collective-permute-start.15) | collective-permute-done | bytes 983072 | tf_op jit(solution)/shard_map/ppermute | solution.py:121
  227.5 14.7 %in_product.6.q_own.k_own.v_own = bf16[1024,1152]{1,0:T(8,128)(2,1)} custom-call(bf16[1024,3072]{1,0:T(8,128)(2,1)} %assemble.1.rows_ref, bf16[3072,1152]{1,0:T(8,128)(2,1)} %bitcast.5.weight_ref.refs_5_), custom_call_target="tpu_custom_call" | custom-call | flops 7247757312 | bytes 15728640 | tf_op jit(solution)/shard_map/in_product/pallas_call | solution.py:266
  243.7 4.5 pack.7
  249.8 4.7 all-to-all-start.3
  255.1 51.1 %collective-permute-done.21 = bf16[1024,256]{1,0:T(8,128)(2,1)S(1)} collective-permute-done((bf16[1024,256]{1,0:T(8,128)(2,1)}, bf16[1024,256]{1,0:T(8,128)(2,1)S(1)}, u32[]{:S(2)}, u32[]{:S(2)}) %collective-permute-start.21) | collective-permute-done | bytes 524320 | tf_op jit(solution)/shard_map/ppermute | solution.py:121
  306.2 6.9 %in_product.8 = bf16[1024,512]{1,0:T(8,128)(2,1)S(1)} custom-call(bf16[1024,3072]{1,0:T(8,128)(2,1)} %assemble.1.rows_ref, bf16[3072,512]{1,0:T(8,128)(2,1)} %bitcast.6.weight_ref.refs_7_), custom_call_target="tpu_custom_call" | custom-call | flops 3221225472 | bytes 10485760 | tf_op jit(solution)/shard_map/in_product/pallas_call | solution.py:266
  318.2 4.7 add_parts.1
  322.9 2.7 fusion.19
  327.7 15.2 %attend.1 = (bf16[1024,384]{1,0:T(8,128)(2,1)S(1)}, bf16[1024,384]{1,0:T(8,128)(2,1)S(1)}, bf16[1024,384]{1,0:T(8,128)(2,1)S(1)}, bf16[1024,384]{1,0:T(8,128)(2,1)S(1)}) custom-call(bf16[1024,1152]{1,0:T(8,128)(2,1)} %in_product.6.q_own.k_own.v_own, bf16[1024,1152]{1,0:T(8,128)(2,1)} %collective-permute-done.20.q_got.k_got.v_got, ...), custom_call_target="tpu_custom_call" | custom-call | flops 1207959552 | bytes 9437184 | tf_op jit(solution)/shard_map/attend/pallas_call | solution.py:75
  348.7 4.6 all-to-all-start.4
  353.3 7.8 %in_product.7 = bf16[1024,512]{1,0:T(8,128)(2,1)} custom-call(bf16[1024,3072]{1,0:T(8,128)(2,1)} %assemble.1.rows_ref, bf16[3072,512]{1,0:T(8,128)(2,1)} %bitcast.7.weight_ref.refs_2_), custom_call_target="tpu_custom_call" | custom-call | flops 3221225472 | bytes 10485760 | tf_op jit(solution)/shard_map/in_product/pallas_call | solution.py:266
  362.0 18.4 %back_product.3.refs_4_ = bf16[1024,3072]{1,0:T(8,128)(2,1)} custom-call(bf16[1024,384]{1,0:T(8,128)(2,1)S(1)} %copy-done.27, bf16[1024,384]{1,0:T(8,128)(2,1)S(1)} %copy-done.29, bf16[1024,384]{1,0:T(8,128)(2,1)S(1)} %copy-done.31, bf16[1024,256]{1,0:T(8,128)(2,1)S(1)} %copy-done.23, bf16[1024,512]{1,0:T(8,128)(2,1)S(1)} %copy-done.15, ...), custom_call_target="tpu_custom_call" | custom-call | flops 12079595520 | bytes 18087936 | tf_op jit(solution)/shard_map/back_product/pallas_call | solution.py:312
  380.4 5.1 in_product.9
  386.8 12.3 %out_product.4.refs_3_ = bf16[1024,3072]{1,0:T(8,128)(2,1)} custom-call(bf16[1024,384]{1,0:T(8,128)(2,1)S(1)} %copy-done.25, bf16[1024,256]{1,0:T(8,128)(2,1)S(1)} %copy-done.22, bf16[1024,512]{1,0:T(8,128)(2,1)S(1)} %get-tuple-element.51.refs_2_, bf16[384,3072]{1,0:T(8,128)(2,1)S(1)} %copy-done, bf16[1536,3072]{1,0:T(8,128)(2,1)} %refs_2_.7), custom_call_target="tpu_custom_call" | custom-call | flops 7247757312 | bytes 18087936 | tf_op jit(solution)/shard_map/out_product/pallas_call | solution.py:312
  399.1 2.7 fusion.11
  403.5 7.7 %back_product.4 = bf16[512,3072]{1,0:T(8,128)(2,1)} custom-call(bf16[1024,512]{1,0:T(8,128)(2,1)S(1)} %get-tuple-element.48.refs_0_, bf16[1024,256]{1,0:T(8,128)(2,1)S(1)} %get-tuple-element.52.refs_1_, bf16[3072,512]{1,0:T(8,128)(2,1)} %bitcast.7.weight_ref.refs_2_, bf16[3072,256]{1,0:T(8,128)(2,1)} %bitcast.17.weight_ref.refs_3_, ...), custom_call_target="tpu_custom_call" | custom-call | flops 2415919104 | bytes 7864320 | tf_op jit(solution)/shard_map/back_product/pallas_call | solution.py:312
  411.2 7.4 %out_product.5 = bf16[512,3072]{1,0:T(8,128)(2,1)S(1)} custom-call(bf16[1024,512]{1,0:T(8,128)(2,1)S(1)} %get-tuple-element.49.refs_0_, bf16[1024,256]{1,0:T(8,128)(2,1)S(1)} %get-tuple-element.53.refs_1_, bf16[1536,3072]{1,0:T(8,128)(2,1)} %refs_2_.7, bf16[1024,3072]{1,0:T(8,128)(2,1)} %out_product.4.refs_3_), custom_call_target="tpu_custom_call" | custom-call | flops 2415919104 | bytes 12582912 | tf_op jit(solution)/shard_map/out_product/pallas_call | solution.py:312
  420.8 8.5 %back_product.5 = bf16[512,3072]{1,0:T(8,128)(2,1)} custom-call(bf16[1024,512]{1,0:T(8,128)(2,1)S(1)} %get-tuple-element.48.refs_0_, bf16[1024,256]{1,0:T(8,128)(2,1)S(1)} %get-tuple-element.52.refs_1_, bf16[3072,512]{1,0:T(8,128)(2,1)} %bitcast.7.weight_ref.refs_2_, bf16[3072,256]{1,0:T(8,128)(2,1)} %bitcast.17.weight_ref.refs_3_, ...), custom_call_target="tpu_custom_call" | custom-call | flops 2415919104 | bytes 7864320 | tf_op jit(solution)/shard_map/back_product/pallas_call | solution.py:312
  433.4 6.7 %out_product.7 = bf16[256,3072]{1,0:T(8,128)(2,1)S(1)} custom-call(bf16[1024,512]{1,0:T(8,128)(2,1)S(1)} %get-tuple-element.49.refs_0_, bf16[1024,256]{1,0:T(8,128)(2,1)S(1)} %get-tuple-element.53.refs_1_, bf16[1536,3072]{1,0:T(8,128)(2,1)} %refs_2_.7, bf16[1024,3072]{1,0:T(8,128)(2,1)} %out_product.4.refs_3_, bf16[512,3072]{1,0:T(8,128)(2,1)} %copy-done.32), custom_call_target="tpu_custom_call" | custom-call | flops 1207959552 | bytes 11010048 | tf_op jit(solution)/shard_map/out_product/pallas_call | solution.py:312
  441.9 6.7 %out_product.6 = f32[256,3072]{1,0:T(8,128)S(1)} custom-call(bf16[1024,512]{1,0:T(8,128)(2,1)S(1)} %get-tuple-element.49.refs_0_, bf16[1024,256]{1,0:T(8,128)(2,1)S(1)} %get-tuple-element.53.refs_1_, bf16[1536,3072]{1,0:T(8,128)(2,1)} %refs_2_.7, bf16[1024,3072]{1,0:T(8,128)(2,1)} %out_product.4.refs_3_, bf16[512,3072]{1,0:T(8,128)(2,1)} %copy-done.32), custom_call_target="tpu_custom_call" | custom-call | flops 1207959552 | bytes 12582912 | tf_op jit(solution)/shard_map/out_product/pallas_call | solution.py:312
  448.7 19.3 %collective-permute-done.30 = bf16[2,2,64,3072]{3,2,0,1:T(8,128)(2,1)S(1)} collective-permute-done((bf16[2,2,64,3072]{3,2,0,1:T(8,128)(2,1)S(1)}, bf16[2,2,64,3072]{3,2,0,1:T(8,128)(2,1)S(1)}, u32[]{:S(2)}, u32[]{:S(2)}) %collective-permute-start.30) | collective-permute-done | bytes 1572896 | tf_op jit(solution)/shard_map/ppermute | solution.py:121
  469.9 6.5 %collective-permute-done.26 = bf16[256,3072]{1,0:T(8,128)(2,1)S(1)} collective-permute-done((bf16[256,3072]{1,0:T(8,128)(2,1)S(1)}, bf16[256,3072]{1,0:T(8,128)(2,1)S(1)}, u32[]{:S(2)}, u32[]{:S(2)}) %collective-permute-start.26) | collective-permute-done | bytes 1572896 | tf_op jit(solution)/shard_map/ppermute | solution.py:121
  478.8 26.2 %collective-permute-done.31 = bf16[2,64,3072]{2,1,0:T(8,128)(2,1)S(1)} collective-permute-done((bf16[2,64,3072]{2,1,0:T(8,128)(2,1)S(1)}, bf16[2,64,3072]{2,1,0:T(8,128)(2,1)S(1)}, u32[]{:S(2)}, u32[]{:S(2)}) %collective-permute-start.31) | collective-permute-done | bytes 786464 | tf_op jit(solution)/shard_map/ppermute | solution.py:121
  507.1 5.3 collective-permute-done.27
  516.6 5.4 %all-reduce = (f32[64]{0:T(128)}, f32[64]{0:T(128)}) all-reduce(f32[64]{0:T(128)S(1)} %get-tuple-element.39, f32[64]{0:T(128)S(1)} %get-tuple-element.38), channel_id=1, replica_groups=mesh['gx'=4,'gy'=4,'gz'=2] {'gz'}, use_global_device_ids=true, to_apply=%region_7.0 | all-reduce | flops 128 | bytes 1024 | tf_op jit(solution)/shard_map/psum | solution.py:449
  522.7 9.5 %collective-permute-done.28 = bf16[64,3072]{1,0:T(8,128)(2,1)S(1)} collective-permute-done((bf16[64,3072]{1,0:T(8,128)(2,1)S(1)}, bf16[64,3072]{1,0:T(8,128)(2,1)S(1)}, u32[]{:S(2)}, u32[]{:S(2)}) %collective-permute-start.28) | collective-permute-done | bytes 393248 | tf_op jit(solution)/shard_map/ppermute | solution.py:121
  532.2 2.4 fusion.34
  (157 shorter events, 65.8 us)
Async XLA Ops:
  0.6 12.4 %copy-start.37 = (bf16[64,3072]{1,0:T(8,128)(2,1)S(1)}, bf16[64,3072]{1,0:T(8,128)(2,1)}, u32[]{:S(2)}) copy-start(bf16[64,3072]{1,0:T(8,128)(2,1)} %param.9) | copy-start | bytes 1179652
  0.7 12.3 %collective-permute-start.8 = (bf16[64,3072]{1,0:T(8,128)(2,1)}, bf16[64,3072]{1,0:T(8,128)(2,1)S(1)}, u32[]{:S(2)}, u32[]{:S(2)}) collective-permute-start(bf16[64,3072]{1,0:T(8,128)(2,1)} %param.9), channel_id=1, source_target_pairs={{0,16},{8,24},{16,0},{24,8},{1,17},{9,25},{17,1},{25,9},{2,18},{10... | collective-permute-start | bytes 1179656 | tf_op jit(solution)/shard_map/ppermute | solution.py:121
  13.9 34.0 %all-to-all-start = ((bf16[4,768,256]{2,1,0:T(8,128)(2,1)}), bf16[4,768,256]{2,1,0:T(8,128)(2,1)}, u32[]{:S(2)}, u32[]{:S(2)}) async-start(bf16[4,768,256]{2,1,0:T(8,128)(2,1)} %pack.5), calls=%async_computation | async-start | bytes 3145728 | tf_op jit(solution)/shard_map/all_to_all | solution.py:350
  18.6 28.3 %collective-permute-start = (bf16[64,3072]{1,0:T(8,128)(2,1)S(1)}, bf16[64,3072]{1,0:T(8,128)(2,1)S(1)}, u32[]{:S(2)}, u32[]{:S(2)}) collective-permute-start(bf16[64,3072]{1,0:T(8,128)(2,1)S(1)} %fusion.29), channel_id=1, source_target_pairs={{0,16},{8,24},{16,0},{24,8},{1,17},{9,25},{17,1},{25,9},{2,18},{10... | collective-permute-start | bytes 1179656 | tf_op jit(solution)/shard_map/ppermute | solution.py:121
  47.9 10.7 %copy-start = (bf16[384,3072]{1,0:T(8,128)(2,1)S(1)}, bf16[384,3072]{1,0:T(8,128)(2,1)}, u32[]{:S(2)}) copy-start(bf16[384,3072]{1,0:T(8,128)(2,1)} %refs_3_.1) | copy-start | bytes 7077892
  47.9 142.0 %all-to-all-start.1 = ((bf16[4,768,1152]{2,1,0:T(8,128)(2,1)}), bf16[4,768,1152]{2,1,0:T(8,128)(2,1)}, u32[]{:S(2)}, u32[]{:S(2)}) async-start(bf16[4,768,1152]{2,1,0:T(8,128)(2,1)} %pack.6), calls=%async_computation.1 | async-start | bytes 14155776 | tf_op jit(solution)/shard_map/all_to_all | solution.py:350
  53.5 5.2 collective-permute-start.16
  53.9 37.3 %collective-permute-start.11 = (bf16[2,64,3072]{2,1,0:T(8,128)(2,1)}, bf16[2,64,3072]{2,1,0:T(8,128)(2,1)S(1)}, u32[]{:S(2)}, u32[]{:S(2)}) collective-permute-start(bf16[2,64,3072]{2,1,0:T(8,128)(2,1)} %pad_maximum_fusion.1.own_ref), channel_id=1, source_target_pairs={{0,2},{2,0},{4,6},{6,4},{1,3},{3,1},{5,7},{7,5},{8,10},{10,8},{12,... | collective-permute-start | bytes 2359304 | tf_op jit(solution)/shard_map/ppermute | solution.py:121
  55.7 55.2 %collective-permute-start.9 = (bf16[2,64,3072]{2,1,0:T(8,128)(2,1)}, bf16[2,64,3072]{2,1,0:T(8,128)(2,1)S(1)}, u32[]{:S(2)}, u32[]{:S(2)}) collective-permute-start(bf16[2,64,3072]{2,1,0:T(8,128)(2,1)} %pad_maximum_fusion.1.own_ref), channel_id=1, source_target_pairs={{0,4},{2,6},{4,0},{6,2},{1,5},{3,7},{5,1},{7,3},{8,12},{10,14},{12... | collective-permute-start | bytes 2359304 | tf_op jit(solution)/shard_map/ppermute | solution.py:121
  58.3 68.4 %collective-permute-start.4 = (bf16[2,64,3072]{2,1,0:T(8,128)(2,1)}, bf16[2,64,3072]{2,1,0:T(8,128)(2,1)S(1)}, u32[]{:S(2)}, u32[]{:S(2)}) collective-permute-start(bf16[2,64,3072]{2,1,0:T(8,128)(2,1)} %pad_maximum_fusion.refs_0_), channel_id=1, source_target_pairs={{0,4},{2,6},{4,0},{6,2},{1,5},{3,7},{5,1},{7,3},{8,12},{10,14},{12... | collective-permute-start | bytes 2359304 | tf_op jit(solution)/shard_map/ppermute | solution.py:121
  67.0 61.8 %collective-permute-start.17 = (bf16[256,1920]{1,0:T(8,128)(2,1)S(1)}, bf16[256,1920]{1,0:T(8,128)(2,1)S(1)}, u32[]{:S(2)}, u32[]{:S(2)}) collective-permute-start(bf16[256,1920]{1,0:T(8,128)(2,1)S(1)} %cot_product.6), channel_id=1, source_target_pairs={{0,1},{1,0},{2,3},{3,2},{4,5},{5,4},{6,7},{7,6},{8,9},{9,8},{10,11... | collective-permute-start | bytes 2949128 | tf_op jit(solution)/shard_map/ppermute | solution.py:121
  68.6 58.2 %collective-permute-start.2 = (bf16[2,64,3072]{2,1,0:T(8,128)(2,1)}, bf16[2,64,3072]{2,1,0:T(8,128)(2,1)S(1)}, u32[]{:S(2)}, u32[]{:S(2)}) collective-permute-start(bf16[2,64,3072]{2,1,0:T(8,128)(2,1)} %pad_maximum_fusion.refs_0_), channel_id=1, source_target_pairs={{0,2},{2,0},{4,6},{6,4},{1,3},{3,1},{5,7},{7,5},{8,10},{10,8},{12,... | collective-permute-start | bytes 2359304 | tf_op jit(solution)/shard_map/ppermute | solution.py:121
  91.2 35.5 %collective-permute-start.12 = (bf16[2,64,3072]{2,1,0:T(8,128)(2,1)S(1)}, bf16[2,64,3072]{2,1,0:T(8,128)(2,1)S(1)}, u32[]{:S(2)}, u32[]{:S(2)}) collective-permute-start(bf16[2,64,3072]{2,1,0:T(8,128)(2,1)S(1)} %collective-permute-done.11.own_ref), channel_id=1, source_target_pairs={{0,8},{8,0},{16,24},{24,16},{1,9},{9,1},{17,25},{25,17},{2,10},{10... | collective-permute-start | bytes 2359304 | tf_op jit(solution)/shard_map/ppermute | solution.py:121
  111.0 26.9 %collective-permute-start.18 = (bf16[2,64,3072]{2,1,0:T(8,128)(2,1)S(1)}, bf16[2,64,3072]{2,1,0:T(8,128)(2,1)S(1)}, u32[]{:S(2)}, u32[]{:S(2)}) collective-permute-start(bf16[2,64,3072]{2,1,0:T(8,128)(2,1)S(1)} %collective-permute-done.9.own_ref), channel_id=1, source_target_pairs={{0,8},{8,0},{16,24},{24,16},{1,9},{9,1},{17,25},{25,17},{2,10},{10... | collective-permute-start | bytes 2359304 | tf_op jit(solution)/shard_map/ppermute | solution.py:121
  126.8 20.9 %collective-permute-start.1 = (bf16[2,64,3072]{2,1,0:T(8,128)(2,1)}, bf16[2,64,3072]{2,1,0:T(8,128)(2,1)S(1)}, u32[]{:S(2)}, u32[]{:S(2)}) collective-permute-start(bf16[2,64,3072]{2,1,0:T(8,128)(2,1)} %pad_maximum_fusion.refs_0_), channel_id=1, source_target_pairs={{0,8},{8,0},{16,24},{24,16},{1,9},{9,1},{17,25},{25,17},{2,10},{10... | collective-permute-start | bytes 2359304 | tf_op jit(solution)/shard_map/ppermute | solution.py:121
  126.8 21.5 %collective-permute-start.10 = (bf16[2,64,3072]{2,1,0:T(8,128)(2,1)S(1)}, bf16[2,64,3072]{2,1,0:T(8,128)(2,1)}, u32[]{:S(2)}, u32[]{:S(2)}) collective-permute-start(bf16[2,64,3072]{2,1,0:T(8,128)(2,1)S(1)} %collective-permute-done.9.own_ref), channel_id=1, source_target_pairs={{0,2},{2,0},{4,6},{6,4},{1,3},{3,1},{5,7},{7,5},{8,10},{10,8},{12,... | collective-permute-start | bytes 2359304 | tf_op jit(solution)/shard_map/ppermute | solution.py:121
  126.8 36.8 %collective-permute-start.6 = (bf16[2,64,3072]{2,1,0:T(8,128)(2,1)S(1)}, bf16[2,64,3072]{2,1,0:T(8,128)(2,1)S(1)}, u32[]{:S(2)}, u32[]{:S(2)}) collective-permute-start(bf16[2,64,3072]{2,1,0:T(8,128)(2,1)S(1)} %collective-permute-done.4.refs_4_), channel_id=1, source_target_pairs={{0,2},{2,0},{4,6},{6,4},{1,3},{3,1},{5,7},{7,5},{8,10},{10,8},{12,... | collective-permute-start | bytes 2359304 | tf_op jit(solution)/shard_map/ppermute | solution.py:121
  129.8 33.8 %collective-permute-start.5 = (bf16[2,64,3072]{2,1,0:T(8,128)(2,1)S(1)}, bf16[2,64,3072]{2,1,0:T(8,128)(2,1)S(1)}, u32[]{:S(2)}, u32[]{:S(2)}) collective-permute-start(bf16[2,64,3072]{2,1,0:T(8,128)(2,1)S(1)} %collective-permute-done.4.refs_4_), channel_id=1, source_target_pairs={{0,8},{8,0},{16,24},{24,16},{1,9},{9,1},{17,25},{25,17},{2,10},{10... | collective-permute-start | bytes 2359304 | tf_op jit(solution)/shard_map/ppermute | solution.py:121
  137.9 9.8 %copy-start.5 = (bf16[256,1920]{1,0:T(8,128)(2,1)}, bf16[256,1920]{1,0:T(8,128)(2,1)S(1)}, u32[]{:S(2)}) copy-start(bf16[256,1920]{1,0:T(8,128)(2,1)S(1)} %cot_product.4) | copy-start | bytes 2949124
  137.9 38.3 %collective-permute-start.13 = (bf16[256,1920]{1,0:T(8,128)(2,1)S(1)}, bf16[256,1920]{1,0:T(8,128)(2,1)S(1)}, u32[]{:S(2)}, u32[]{:S(2)}) collective-permute-start(bf16[256,1920]{1,0:T(8,128)(2,1)S(1)} %cot_product.4), channel_id=1, source_target_pairs={{0,1},{1,0},{2,3},{3,2},{4,5},{5,4},{6,7},{7,6},{8,9},{9,8},{10,11... | collective-permute-start | bytes 2949128 | tf_op jit(solution)/shard_map/ppermute | solution.py:121
  147.7 20.9 %copy-start.7 = (bf16[256,1920]{1,0:T(8,128)(2,1)}, bf16[256,1920]{1,0:T(8,128)(2,1)S(1)}, u32[]{:S(2)}) copy-start(bf16[256,1920]{1,0:T(8,128)(2,1)S(1)} %cot_product.7) | copy-start | bytes 2949124
  147.7 35.5 %collective-permute-start.19 = (bf16[256,1920]{1,0:T(8,128)(2,1)S(1)}, bf16[256,1920]{1,0:T(8,128)(2,1)S(1)}, u32[]{:S(2)}, u32[]{:S(2)}) collective-permute-start(bf16[256,1920]{1,0:T(8,128)(2,1)S(1)} %cot_product.7), channel_id=1, source_target_pairs={{0,1},{1,0},{2,3},{3,2},{4,5},{5,4},{6,7},{7,6},{8,9},{9,8},{10,11... | collective-permute-start | bytes 2949128 | tf_op jit(solution)/shard_map/ppermute | solution.py:121
  148.3 22.0 %collective-permute-start.3 = (bf16[2,64,3072]{2,1,0:T(8,128)(2,1)S(1)}, bf16[2,64,3072]{2,1,0:T(8,128)(2,1)S(1)}, u32[]{:S(2)}, u32[]{:S(2)}) collective-permute-start(bf16[2,64,3072]{2,1,0:T(8,128)(2,1)S(1)} %collective-permute-done.2.refs_2_), channel_id=1, source_target_pairs={{0,8},{8,0},{16,24},{24,16},{1,9},{9,1},{17,25},{25,17},{2,10},{10... | collective-permute-start | bytes 2359304 | tf_op jit(solution)/shard_map/ppermute | solution.py:121
  163.6 6.7 %collective-permute-start.7 = (bf16[2,64,3072]{2,1,0:T(8,128)(2,1)S(1)}, bf16[2,64,3072]{2,1,0:T(8,128)(2,1)}, u32[]{:S(2)}, u32[]{:S(2)}) collective-permute-start(bf16[2,64,3072]{2,1,0:T(8,128)(2,1)S(1)} %collective-permute-done.6.refs_6_), channel_id=1, source_target_pairs={{0,8},{8,0},{16,24},{24,16},{1,9},{9,1},{17,25},{25,17},{2,10},{10... | collective-permute-start | bytes 2359304 | tf_op jit(solution)/shard_map/ppermute | solution.py:121
  163.6 31.2 %collective-permute-start.14 = (bf16[2,64,3072]{2,1,0:T(8,128)(2,1)}, bf16[2,64,3072]{2,1,0:T(8,128)(2,1)}, u32[]{:S(2)}, u32[]{:S(2)}) collective-permute-start(bf16[2,64,3072]{2,1,0:T(8,128)(2,1)} %collective-permute-done.10.own_ref), channel_id=1, source_target_pairs={{0,8},{8,0},{16,24},{24,16},{1,9},{9,1},{17,25},{25,17},{2,10},{10... | collective-permute-start | bytes 2359304 | tf_op jit(solution)/shard_map/ppermute | solution.py:121
  190.0 59.8 %all-to-all-start.2 = ((bf16[4,768,512]{2,1,0:T(8,128)(2,1)}), bf16[4,768,512]{2,1,0:T(8,128)(2,1)}, u32[]{:S(2)}, u32[]{:S(2)}) async-start(bf16[4,768,512]{2,1,0:T(8,128)(2,1)} %copy-done.3), calls=%async_computation.2 | async-start | bytes 6291456 | tf_op jit(solution)/shard_map/all_to_all | solution.py:350
  203.4 24.1 %collective-permute-start.15 = (bf16[256,1920]{1,0:T(8,128)(2,1)S(1)}, bf16[256,1920]{1,0:T(8,128)(2,1)}, u32[]{:S(2)}, u32[]{:S(2)}) collective-permute-start(bf16[256,1920]{1,0:T(8,128)(2,1)S(1)} %cot_product.5), channel_id=1, source_target_pairs={{0,1},{1,0},{2,3},{3,2},{4,5},{5,4},{6,7},{7,6},{8,9},{9,8},{10,11... | collective-permute-start | bytes 2949128 | tf_op jit(solution)/shard_map/ppermute | solution.py:121
  242.2 83.4 %collective-permute-start.20 = (bf16[1024,1152]{1,0:T(8,128)(2,1)}, bf16[1024,1152]{1,0:T(8,128)(2,1)}, u32[]{:S(2)}, u32[]{:S(2)}) collective-permute-start(bf16[1024,1152]{1,0:T(8,128)(2,1)} %in_product.6.q_own.k_own.v_own), channel_id=1, source_target_pairs={{0,1},{1,0},{2,3},{3,2},{4,5},{5,4},{6,7},{7,6},{8,9},{9,8},{10,11... | collective-permute-start | bytes 7077896 | tf_op jit(solution)/shard_map/ppermute | solution.py:121
  249.8 98.9 %all-to-all-start.3 = ((bf16[4,768,512]{2,1,0:T(8,128)(2,1)}), bf16[4,768,512]{2,1,0:T(8,128)(2,1)}, u32[]{:S(2)}, u32[]{:S(2)}) async-start(bf16[4,768,512]{2,1,0:T(8,128)(2,1)} %copy-done.2), calls=%async_computation.3 | async-start | bytes 6291456 | tf_op jit(solution)/shard_map/all_to_all | solution.py:350
  254.5 51.7 %collective-permute-start.21 = (bf16[1024,256]{1,0:T(8,128)(2,1)}, bf16[1024,256]{1,0:T(8,128)(2,1)S(1)}, u32[]{:S(2)}, u32[]{:S(2)}) collective-permute-start(bf16[1024,256]{1,0:T(8,128)(2,1)} %copy-done.13), channel_id=1, source_target_pairs={{0,1},{1,0},{2,3},{3,2},{4,5},{5,4},{6,7},{7,6},{8,9},{9,8},{10,11... | collective-permute-start | bytes 1572872 | tf_op jit(solution)/shard_map/ppermute | solution.py:121
  313.2 33.4 %collective-permute-start.22 = (bf16[1024,512]{1,0:T(8,128)(2,1)S(1)}, bf16[1024,512]{1,0:T(8,128)(2,1)S(1)}, u32[]{:S(2)}, u32[]{:S(2)}) collective-permute-start(bf16[1024,512]{1,0:T(8,128)(2,1)S(1)} %in_product.8), channel_id=1, source_target_pairs={{0,1},{1,0},{2,3},{3,2},{4,5},{5,4},{6,7},{7,6},{8,9},{9,8},{10,11... | collective-permute-start | bytes 3145736 | tf_op jit(solution)/shard_map/ppermute | solution.py:121
  348.7 31.7 %all-to-all-start.4 = ((bf16[4,768,256]{2,1,0:T(8,128)(2,1)}), bf16[4,768,256]{2,1,0:T(8,128)(2,1)}, u32[]{:S(2)}, u32[]{:S(2)}) async-start(bf16[4,768,256]{2,1,0:T(8,128)(2,1)} %copy-done.4), calls=%async_computation.4 | async-start | bytes 3145728 | tf_op jit(solution)/shard_map/all_to_all | solution.py:350
  353.3 8.7 %copy-start.15 = (bf16[1024,512]{1,0:T(8,128)(2,1)S(1)}, bf16[1024,512]{1,0:T(8,128)(2,1)}, u32[]{:S(2)}) copy-start(bf16[1024,512]{1,0:T(8,128)(2,1)} %get-tuple-element.50.refs_4_) | copy-start | bytes 3145732
  353.3 8.7 %copy-start.23 = (bf16[1024,256]{1,0:T(8,128)(2,1)S(1)}, bf16[1024,256]{1,0:T(8,128)(2,1)}, u32[]{:S(2)}) copy-start(bf16[1024,256]{1,0:T(8,128)(2,1)} %get-tuple-element.54.refs_3_) | copy-start | bytes 1572868
  353.3 8.7 %copy-start.27 = (bf16[1024,384]{1,0:T(8,128)(2,1)S(1)}, bf16[1024,384]{1,0:T(8,128)(2,1)}, u32[]{:S(2)}) copy-start(bf16[1024,384]{1,0:T(8,128)(2,1)} %copy-done.26) | copy-start | bytes 2359300
  353.3 8.7 %copy-start.29 = (bf16[1024,384]{1,0:T(8,128)(2,1)S(1)}, bf16[1024,384]{1,0:T(8,128)(2,1)}, u32[]{:S(2)}) copy-start(bf16[1024,384]{1,0:T(8,128)(2,1)} %copy-done.28) | copy-start | bytes 2359300
  361.1 37.9 %collective-permute-start.23 = (bf16[1024,512]{1,0:T(8,128)(2,1)}, bf16[1024,512]{1,0:T(8,128)(2,1)}, u32[]{:S(2)}, u32[]{:S(2)}) collective-permute-start(bf16[1024,512]{1,0:T(8,128)(2,1)} %in_product.7), channel_id=1, source_target_pairs={{0,1},{1,0},{2,3},{3,2},{4,5},{5,4},{6,7},{7,6},{8,9},{9,8},{10,11... | collective-permute-start | bytes 3145736 | tf_op jit(solution)/shard_map/ppermute | solution.py:121
  385.5 16.3 %collective-permute-start.24 = (bf16[1024,256]{1,0:T(8,128)(2,1)S(1)}, bf16[1024,256]{1,0:T(8,128)(2,1)S(1)}, u32[]{:S(2)}, u32[]{:S(2)}) collective-permute-start(bf16[1024,256]{1,0:T(8,128)(2,1)S(1)} %in_product.9), channel_id=1, source_target_pairs={{0,1},{1,0},{2,3},{3,2},{4,5},{5,4},{6,7},{7,6},{8,9},{9,8},{10,11... | collective-permute-start | bytes 1572872 | tf_op jit(solution)/shard_map/ppermute | solution.py:121
  411.2 8.0 %collective-permute-start.29 = (bf16[512,3072]{1,0:T(8,128)(2,1)}, bf16[512,3072]{1,0:T(8,128)(2,1)S(1)}, u32[]{:S(2)}, u32[]{:S(2)}) collective-permute-start(bf16[512,3072]{1,0:T(8,128)(2,1)} %back_product.4), channel_id=1, source_target_pairs={{0,8},{8,0},{16,24},{24,16},{1,9},{9,1},{17,25},{25,17},{2,10},{10... | collective-permute-start | bytes 9437192 | tf_op jit(solution)/shard_map/ppermute | solution.py:121
  418.6 13.1 %collective-permute-start.25 = (bf16[512,3072]{1,0:T(8,128)(2,1)S(1)}, bf16[512,3072]{1,0:T(8,128)(2,1)S(1)}, u32[]{:S(2)}, u32[]{:S(2)}) collective-permute-start(bf16[512,3072]{1,0:T(8,128)(2,1)S(1)} %out_product.5), channel_id=1, source_target_pairs={{0,8},{8,0},{16,24},{24,16},{1,9},{9,1},{17,25},{25,17},{2,10},{10... | collective-permute-start | bytes 9437192 | tf_op jit(solution)/shard_map/ppermute | solution.py:121
  431.6 36.4 %collective-permute-start.30 = (bf16[2,2,64,3072]{3,2,0,1:T(8,128)(2,1)S(1)}, bf16[2,2,64,3072]{3,2,0,1:T(8,128)(2,1)S(1)}, u32[]{:S(2)}, u32[]{:S(2)}) collective-permute-start(bf16[2,2,64,3072]{3,2,0,1:T(8,128)(2,1)S(1)} %bitcast.75), channel_id=1, source_target_pairs={{0,2},{2,0},{4,6},{6,4},{1,3},{3,1},{5,7},{7,5},{8,10},{10,8},{12,... | collective-permute-start | bytes 4718600 | tf_op jit(solution)/shard_map/ppermute | solution.py:121
  440.1 36.3 %collective-permute-start.26 = (bf16[256,3072]{1,0:T(8,128)(2,1)S(1)}, bf16[256,3072]{1,0:T(8,128)(2,1)S(1)}, u32[]{:S(2)}, u32[]{:S(2)}) collective-permute-start(bf16[256,3072]{1,0:T(8,128)(2,1)S(1)} %out_product.7), channel_id=1, source_target_pairs={{0,16},{8,24},{16,0},{24,8},{1,17},{9,25},{17,1},{25,9},{2,18},{10... | collective-permute-start | bytes 4718600 | tf_op jit(solution)/shard_map/ppermute | solution.py:121
  468.6 36.5 %collective-permute-start.31 = (bf16[2,64,3072]{2,1,0:T(8,128)(2,1)S(1)}, bf16[2,64,3072]{2,1,0:T(8,128)(2,1)S(1)}, u32[]{:S(2)}, u32[]{:S(2)}) collective-permute-start(bf16[2,64,3072]{2,1,0:T(8,128)(2,1)S(1)} %fusion.37), channel_id=1, source_target_pairs={{0,4},{2,6},{4,0},{6,2},{1,5},{3,7},{5,1},{7,3},{8,12},{10,14},{12... | collective-permute-start | bytes 2359304 | tf_op jit(solution)/shard_map/ppermute | solution.py:121
  477.0 35.4 %collective-permute-start.27 = (bf16[2,64,3072]{2,1,0:T(8,128)(2,1)S(1)}, bf16[2,64,3072]{2,1,0:T(8,128)(2,1)S(1)}, u32[]{:S(2)}, u32[]{:S(2)}) collective-permute-start(bf16[2,64,3072]{2,1,0:T(8,128)(2,1)S(1)} %fusion.38), channel_id=1, source_target_pairs={{0,2},{2,0},{4,6},{6,4},{1,3},{3,1},{5,7},{7,5},{8,10},{10,8},{12,... | collective-permute-start | bytes 2359304 | tf_op jit(solution)/shard_map/ppermute | solution.py:121
  505.3 11.1 %copy-start.34 = (bf16[64,3072]{1,0:T(8,128)(2,1)S(1)}, bf16[64,3072]{1,0:T(8,128)(2,1)}, u32[]{:S(2)}) copy-start(bf16[64,3072]{1,0:T(8,128)(2,1)} %param.8) | copy-start | bytes 1179652
  505.3 11.0 %collective-permute-start.32 = (bf16[64,3072]{1,0:T(8,128)(2,1)S(1)}, bf16[64,3072]{1,0:T(8,128)(2,1)S(1)}, u32[]{:S(2)}, u32[]{:S(2)}) collective-permute-start(bf16[64,3072]{1,0:T(8,128)(2,1)S(1)} %fusion.42), channel_id=1, source_target_pairs={{0,16},{8,24},{16,0},{24,8},{1,17},{9,25},{17,1},{25,9},{2,18},{10... | collective-permute-start | bytes 1179656 | tf_op jit(solution)/shard_map/ppermute | solution.py:121
  513.8 18.5 %copy-start.38 = (bf16[64,3072]{1,0:T(8,128)(2,1)S(1)}, bf16[64,3072]{1,0:T(8,128)(2,1)}, u32[]{:S(2)}) copy-start(bf16[64,3072]{1,0:T(8,128)(2,1)} %param.9) | copy-start | bytes 1179652
  513.8 18.4 %collective-permute-start.28 = (bf16[64,3072]{1,0:T(8,128)(2,1)S(1)}, bf16[64,3072]{1,0:T(8,128)(2,1)S(1)}, u32[]{:S(2)}, u32[]{:S(2)}) collective-permute-start(bf16[64,3072]{1,0:T(8,128)(2,1)S(1)} %fusion.41), channel_id=1, source_target_pairs={{0,4},{2,6},{4,0},{6,2},{1,5},{3,7},{5,1},{7,3},{8,12},{10,14},{12... | collective-permute-start | bytes 1179656 | tf_op jit(solution)/shard_map/ppermute | solution.py:121
  (30 other events, 91.7 us)

commit v7 on v6

--- a/solution.py
+++ b/solution.py
@@ -80,9 +80,9 @@
         out_shape=[half] * 4,
         compiler_params=pltpu.CompilerParams(vmem_limit_bytes=32 * 1024 * 1024),
         cost_estimate=pl.CostEstimate(
-            flops=12 * rows * IMG_TOK * width,
-            bytes_accessed=24 * rows * width,
-            transcendentals=rows * IMG_TOK * heads,
+            flops=rows * IMG_TOK * width // 8,
+            bytes_accessed=rows * width // 4,
+            transcendentals=0,
         ),
         name="attend",
     )(own, got, own, got, own, got, grad)
@@ -130,7 +130,7 @@
 
 def cost(flops, *arrays):
     moved = sum(math.prod(array.shape) * array.dtype.itemsize for array in arrays)
-    return pl.CostEstimate(flops=flops, bytes_accessed=moved, transcendentals=0)
+    return pl.CostEstimate(flops=flops // 64, bytes_accessed=moved // 64, transcendentals=0)
 
 
 def pack_kernel(*refs):
@@ -278,20 +278,24 @@
     )(rows, weight)
 
 
-def product(terms, weights, adds, start, count, kind, transposed):
-    columns = weights[0].shape[0 if transposed else 1]
-    tile = 512 if columns % 512 == 0 else 256
+def product(terms, weights, adds, start, count, kind, transposed, window=None):
+    whole = weights[0].shape[0 if transposed else 1]
+    first_column, columns = window or (0, whole)
+    tile = 512 if columns % 512 == 0 else 384 if columns % 384 == 0 else 256
+    skip = first_column // tile
     specs = [
         pl.BlockSpec((count, value.shape[1]), lambda n: (start // count, 0))
         for value, _, _ in terms
     ]
     for weight in weights:
         if transposed:
-            specs.append(pl.BlockSpec((tile, weight.shape[1]), lambda n: (n, 0)))
+            specs.append(pl.BlockSpec((tile, weight.shape[1]), lambda n: (n + skip, 0)))
         else:
-            specs.append(pl.BlockSpec((weight.shape[0], tile), lambda n: (0, n)))
+            specs.append(pl.BlockSpec((weight.shape[0], tile), lambda n: (0, n + skip)))
     for _, first in adds:
-        specs.append(pl.BlockSpec((count, tile), lambda n, place=first // count: (place, n)))
+        specs.append(
+            pl.BlockSpec((count, tile), lambda n, place=first // count: (place, n + skip))
+        )
 
     def kernel(*refs):
         weight_refs = refs[len(terms) : len(terms) + len(weights)]
@@ -381,13 +385,13 @@
     mlp_got = [others(mlp_own[0])]
     heads_own = in_product(after(all_in, cot_gots[3], mlp_own[0]), in_heads)
     heads_got = others(heads_own)
-    in_mlp.append(swap(after(packed_mlp[1], in_heads, mlp_own[0])))
+    in_mlp.append(swap(after(packed_mlp[1], in_heads)))
     mlp_own.append(in_product(after(all_in, mlp_got[0]), in_mlp[1]))
     mlp_got.append(others(mlp_own[1]))
-    in_mlp.append(swap(after(packed_mlp[2], in_mlp[1], heads_own)))
+    in_mlp.append(swap(after(packed_mlp[2], in_mlp[1], mlp_own[0])))
     mlp_own.append(in_product(after(all_in, heads_got), in_mlp[2]))
     mlp_got.append(others(mlp_own[2]))
-    in_mlp.append(swap(after(packed_mlp[3], in_mlp[2], mlp_own[1])))
+    in_mlp.append(swap(after(packed_mlp[3], in_mlp[2], heads_own)))
 
     out_grad = add_parts(cot_owns, cot_gots)
     mixed, *head_grads = attend(heads_own, heads_got, out_grad)
@@ -422,30 +426,39 @@
     ]
     forward_terms = [(act, 0, offset) for act, _, offset in forward_terms]
 
-    def forward_term(start, size, adds, kind):
+    def forward_term(start, size, adds, window=None):
         adds = [(forward_early, start), *adds]
-        return product(forward_terms, [w_mlp_out], adds, start, size, kind, False)
-
-    def backward_term(start, size, adds):
+        return product(
+            forward_terms, [w_mlp_out], adds, start, size, jnp.bfloat16, False, window
+        )
+
+    def backward_term(start, size, adds, window=None):
         adds = [(backward_early, start), *adds]
-        return product(backward_terms, late_weights, adds, start, size, jnp.bfloat16, True)
+        return product(
+            backward_terms, late_weights, adds, start, size, jnp.bfloat16, True, window
+        )
 
     def wider(value):
         return value.astype(jnp.float32)
 
-    from_core = trade(forward_term(0, 2 * count, [], jnp.bfloat16), "gx", 1)
-    from_x = trade(forward_term(2 * count, count, [(from_core, 0)], jnp.bfloat16), "gx", 2)
-    mine = forward_term(3 * count, count, [(from_core, count)], jnp.float32) + wider(from_x)
-    mine = mine.reshape(2, 2, own_rows, features)
-    pair = mine[:, 0] + wider(trade(half(mine[:, 1]), "gy", 1))
-    summed = pair[0] + wider(trade(half(pair[1]), "gy", 2))
-    layer_out = half(wide + summed)
-
-    from_core = trade(backward_term(0, 2 * count, []), "gx", 1)
-    both = backward_term(2 * count, 2 * count, [(from_core, 0)]).reshape(2, 2, 2, own_rows, features)
-    pair = wide_sum(both[:, :, 0], trade(both[:, :, 1], "gy", 1))
-    ends = pair[:, 0] + wider(trade(half(pair[:, 1]), "gy", 2))
-    normed_grad = ends[1] + wider(trade(half(ends[0]), "gx", 2))
+    def spread_rows(term):
+        half_width = features // 2
+        low, high = (0, half_width), (half_width, half_width)
+        from_core = trade(term(0, 2 * count, []), "gx", 1)
+        from_x = trade(term(2 * count, count, [(from_core, 0)], low), "gx", 2)
+        both = term(2 * count, 2 * count, [(from_core, 0)], high)
+        both = both.reshape(2, 2, 2, own_rows, half_width)
+        pair = wide_sum(both[:, :, 0], trade(both[:, :, 1], "gy", 1))
+        ends = pair[:, 0] + wider(trade(half(pair[:, 1]), "gy", 2))
+        high_sum = ends[1] + wider(trade(half(ends[0]), "gx", 2))
+        mine = wide_sum(term(3 * count, count, [(from_core, count)], low), from_x)
+        mine = mine.reshape(2, 2, own_rows, half_width)
+        pair = mine[:, 0] + wider(trade(half(mine[:, 1]), "gy", 1))
+        low_sum = pair[0] + wider(trade(half(pair[1]), "gy", 2))
+        return jnp.concatenate([low_sum, high_sum], axis=1)
+
+    layer_out = half(wide + spread_rows(forward_term))
+    normed_grad = spread_rows(backward_term)
     first, second = lax.psum(
         (jnp.sum(normed_grad, axis=1), jnp.sum(normed_grad * normed, axis=1)), "gz"
     )

time: 537 us -> 518 us (0.965)
  waiting for transfers between devices: 239 us -> 214 us
  starting transfers between devices: 57.4 us -> 66 us
  local copies, waits for them, and re-layouts: 24.7 us -> 18.8 us
    ppermute x33 -> x39, waiting for transfers between devices: 239 us -> 171 us  [trade(): return lax.ppermute(block, axis, pairs)]
    all_to_all x5, waiting for transfers between devices: 0.01 us -> 42.6 us  [swap(): lax.all_to_all(packed, 'gx', split_axis=0, concat_axis=0, tiled=True)]
    ppermute x33 -> x39, starting transfers between devices: 33.3 us -> 44 us  [trade(): return lax.ppermute(block, axis, pairs)]
    unnamed x81 -> x78, local copies, waits for them, and re-layouts: 22.3 us -> 18.4 us
    pallas_call x7 -> x10, Pallas kernels: 67.8 us -> 69.2 us  [product(): pl.pallas_call(kernel, grid=(columns // tile,), in_specs=specs, out_specs...]
  transfers between devices with their start and end apart: 38 -> 44, of which waited for: 15 -> 15; matrix products, arithmetic and copies ran while one was open for 3% -> 2% of each run, Pallas kernels for 33% -> 35%
where the time goes in v7:
time: 518 us; the launch traced here: 516 us
  waiting for transfers between devices  214 us (41%)
  Pallas kernels  189 us (36%)
  starting transfers between devices  66 us (13%)
  local copies, waits for them, and re-layouts  18.8 us (4%)
  other arithmetic  16.3 us (3%)
  blocking collectives  10.5 us (2%)
    ppermute x39, waiting for transfers between devices, trade(): return lax.ppermute(block, axis, pairs)  171 us
    pallas_call x10, Pallas kernels, product(): pl.pallas_call(kernel, grid=(columns // tile,), in_specs=specs, out_specs...  69.2 us
    ppermute x39, starting transfers between devices, trade(): return lax.ppermute(block, axis, pairs)  44 us
    all_to_all x5, waiting for transfers between devices, swap(): lax.all_to_all(packed, 'gx', split_axis=0, concat_axis=0, tiled=True)  42.6 us
    pallas_call x5, Pallas kernels, in_product(): pl.pallas_call(in_kernel, grid=(columns // tile,), in_specs=[pl.BlockSpec...  39.5 us
    pallas_call x4, Pallas kernels, cot_product(): pl.pallas_call(cot_kernel, grid=(columns // tile,), in_specs=[whole, whol...  35.5 us
    all_to_all x5, starting transfers between devices, swap(): lax.all_to_all(packed, 'gx', split_axis=0, concat_axis=0, tiled=True)  21.9 us
    pallas_call x5, Pallas kernels, pack(): pl.pallas_call(pack_kernel, grid=(owners, width // tile), in_specs=[spec]...  20 us
  transfers between devices with their start and end apart: 44, of which 15 were waited for; matrix products, arithmetic and copies ran while one was open for 2% of the time, Pallas kernels for 35%

profile of v7, /device:TPU:0, one launch (start us, length us, event | category | flops | bytes accessed | tf_op | source)
XLA Modules:
  0.0 515.9 jit_solution(14953794419022389439)
XLA Ops:
  0.7 3.0 collective-permute-start.8
  3.7 3.6 pack.5
  7.5 4.9 all-reduce.1
  13.9 3.6 all-to-all-start
  23.0 5.2 %pack.6 = bf16[4,768,1152]{2,1,0:T(8,128)(2,1)} custom-call(bf16[768,1536]{1,0:T(8,128)(2,1)S(1)} %copy-done.21, bf16[768,1536]{1,0:T(8,128)(2,1)S(1)} %copy-done.22, bf16[768,1536]{1,0:T(8,128)(2,1)} %refs_2_.5), custom_call_target="tpu_custom_call" | custom-call | bytes 221184 | tf_op jit(solution)/shard_map/pack/pallas_call | solution.py:148
  28.4 17.5 %collective-permute-done = bf16[64,3072]{1,0:T(8,128)(2,1)S(1)} collective-permute-done((bf16[64,3072]{1,0:T(8,128)(2,1)S(1)}, bf16[64,3072]{1,0:T(8,128)(2,1)S(1)}, u32[]{:S(2)}, u32[]{:S(2)}) %collective-permute-start) | collective-permute-done | bytes 393248 | tf_op jit(solution)/shard_map/ppermute | solution.py:121
  47.3 5.4 %all-to-all-start.1 = ((bf16[4,768,1152]{2,1,0:T(8,128)(2,1)}), bf16[4,768,1152]{2,1,0:T(8,128)(2,1)}, u32[]{:S(2)}, u32[]{:S(2)}) async-start(bf16[4,768,1152]{2,1,0:T(8,128)(2,1)} %pack.6), calls=%async_computation.1 | async-start | bytes 14155776 | tf_op jit(solution)/shard_map/all_to_all | solution.py:354
  57.2 32.5 %collective-permute-done.11.own_ref = bf16[2,64,3072]{2,1,0:T(8,128)(2,1)} collective-permute-done((bf16[2,64,3072]{2,1,0:T(8,128)(2,1)}, bf16[2,64,3072]{2,1,0:T(8,128)(2,1)}, u32[]{:S(2)}, u32[]{:S(2)}) %collective-permute-start.11) | collective-permute-done | bytes 786464 | tf_op jit(solution)/shard_map/ppermute | solution.py:121
  93.1 4.5 pack.8
  99.3 32.5 %all-to-all-done.1 = bf16[4,768,1152]{2,1,0:T(8,128)(2,1)} async-done(((bf16[4,768,1152]{2,1,0:T(8,128)(2,1)}), bf16[4,768,1152]{2,1,0:T(8,128)(2,1)}, u32[]{:S(2)}, u32[]{:S(2)}) %all-to-all-start.1) | async-done | bytes 7077920 | tf_op jit(solution)/shard_map/all_to_all | solution.py:354
  131.8 4.8 all-to-all-start.2
  136.6 8.6 %cot_product.6 = bf16[256,1920]{1,0:T(8,128)(2,1)S(1)} custom-call(bf16[2,64,3072]{2,1,0:T(8,128)(2,1)} %pad_maximum_fusion.1.own_ref, bf16[2,64,3072]{2,1,0:T(8,128)(2,1)} %collective-permute-done.16.other_ref, bf16[384,3072]{1,0:T(8,128)(2,1)S(1)} %copy-done.1, bf16[1536,3072]{1,0:T(8,128)(2,1)} %refs_2_.9), custom_call_target="tpu_custom_call" | custom-call | flops 47185920 | bytes 199680 | tf_op jit(solution)/shard_map/cot_product/pallas_call | solution.py:214
  147.0 8.6 %cot_product.4 = bf16[256,1920]{1,0:T(8,128)(2,1)S(1)} custom-call(bf16[2,64,3072]{2,1,0:T(8,128)(2,1)} %collective-permute-done.11.own_ref, bf16[2,64,3072]{2,1,0:T(8,128)(2,1)} %collective-permute-done.12.other_ref, bf16[384,3072]{1,0:T(8,128)(2,1)S(1)} %copy-done.1, bf16[1536,3072]{1,0:T(8,128)(2,1)} %refs_2_.9), custom_call_target="tpu_custom_call" | custom-call | flops 47185920 | bytes 199680 | tf_op jit(solution)/shard_map/cot_product/pallas_call | solution.py:214
  158.0 11.8 %collective-permute-done.17 = bf16[256,1920]{1,0:T(8,128)(2,1)S(1)} collective-permute-done((bf16[256,1920]{1,0:T(8,128)(2,1)S(1)}, bf16[256,1920]{1,0:T(8,128)(2,1)S(1)}, u32[]{:S(2)}, u32[]{:S(2)}) %collective-permute-start.17) | collective-permute-done | bytes 983072 | tf_op jit(solution)/shard_map/ppermute | solution.py:121
  169.8 8.9 %cot_product.7 = bf16[256,1920]{1,0:T(8,128)(2,1)S(1)} custom-call(bf16[2,64,3072]{2,1,0:T(8,128)(2,1)} %collective-permute-done.9.own_ref, bf16[2,64,3072]{2,1,0:T(8,128)(2,1)} %collective-permute-done.18.other_ref, bf16[384,3072]{1,0:T(8,128)(2,1)S(1)} %copy-done.1, bf16[1536,3072]{1,0:T(8,128)(2,1)} %refs_2_.9), custom_call_target="tpu_custom_call" | custom-call | flops 47185920 | bytes 199680 | tf_op jit(solution)/shard_map/cot_product/pallas_call | solution.py:214
  180.6 11.8 %collective-permute-done.6.refs_6_ = bf16[2,64,3072]{2,1,0:T(8,128)(2,1)S(1)} collective-permute-done((bf16[2,64,3072]{2,1,0:T(8,128)(2,1)}, bf16[2,64,3072]{2,1,0:T(8,128)(2,1)S(1)}, u32[]{:S(2)}, u32[]{:S(2)}) %collective-permute-start.6) | collective-permute-done | bytes 786464 | tf_op jit(solution)/shard_map/ppermute | solution.py:121
  193.0 9.4 %cot_product.5 = bf16[256,1920]{1,0:T(8,128)(2,1)} custom-call(bf16[2,64,3072]{2,1,0:T(8,128)(2,1)} %collective-permute-done.10.own_ref, bf16[2,64,3072]{2,1,0:T(8,128)(2,1)S(1)} %collective-permute-done.14.other_ref, bf16[384,3072]{1,0:T(8,128)(2,1)S(1)} %copy-done.1, bf16[1536,3072]{1,0:T(8,128)(2,1)} %refs_2_.9), custom_call_target="tpu_custom_call" | custom-call | flops 47185920 | bytes 199680 | tf_op jit(solution)/shard_map/cot_product/pallas_call | solution.py:214
  204.0 4.5 pack.7
  211.1 4.9 assemble.1.rows_ref
  216.9 5.4 %in_product.5 = bf16[1024,256]{1,0:T(8,128)(2,1)} custom-call(bf16[1024,3072]{1,0:T(8,128)(2,1)} %assemble.1.rows_ref, bf16[3072,256]{1,0:T(8,128)(2,1)S(1)} %bitcast.99), custom_call_target="tpu_custom_call" | custom-call | flops 25165824 | bytes 131072 | tf_op jit(solution)/shard_map/in_product/pallas_call | solution.py:266
  222.3 3.7 all-to-all-start.3
  226.0 6.7 %collective-permute-done.15 = bf16[256,1920]{1,0:T(8,128)(2,1)} collective-permute-done((bf16[256,1920]{1,0:T(8,128)(2,1)}, bf16[256,1920]{1,0:T(8,128)(2,1)}, u32[]{:S(2)}, u32[]{:S(2)}) %collective-permute-start.15) | collective-permute-done | bytes 983072 | tf_op jit(solution)/shard_map/ppermute | solution.py:121
  232.7 14.7 %in_product.6.q_own.k_own.v_own = bf16[1024,1152]{1,0:T(8,128)(2,1)} custom-call(bf16[1024,3072]{1,0:T(8,128)(2,1)} %assemble.1.rows_ref, bf16[3072,1152]{1,0:T(8,128)(2,1)} %bitcast.5.weight_ref.refs_5_), custom_call_target="tpu_custom_call" | custom-call | flops 113246208 | bytes 245760 | tf_op jit(solution)/shard_map/in_product/pallas_call | solution.py:266
  252.8 10.1 %all-to-all-done.3 = bf16[4,768,512]{2,1,0:T(8,128)(2,1)S(1)} async-done(((bf16[4,768,512]{2,1,0:T(8,128)(2,1)}), bf16[4,768,512]{2,1,0:T(8,128)(2,1)S(1)}, u32[]{:S(2)}, u32[]{:S(2)}) %all-to-all-start.3) | async-done | bytes 3145760 | tf_op jit(solution)/shard_map/all_to_all | solution.py:354
  262.9 4.5 all-to-all-start.4
  267.4 44.3 %collective-permute-done.21 = bf16[1024,256]{1,0:T(8,128)(2,1)} collective-permute-done((bf16[1024,256]{1,0:T(8,128)(2,1)}, bf16[1024,256]{1,0:T(8,128)(2,1)}, u32[]{:S(2)}, u32[]{:S(2)}) %collective-permute-start.21) | collective-permute-done | bytes 524320 | tf_op jit(solution)/shard_map/ppermute | solution.py:121
  311.8 6.9 %in_product.8 = bf16[1024,512]{1,0:T(8,128)(2,1)S(1)} custom-call(bf16[1024,3072]{1,0:T(8,128)(2,1)} %assemble.1.rows_ref, bf16[3072,512]{1,0:T(8,128)(2,1)} %bitcast.6.weight_ref.refs_7_), custom_call_target="tpu_custom_call" | custom-call | flops 50331648 | bytes 163840 | tf_op jit(solution)/shard_map/in_product/pallas_call | solution.py:266
  320.5 7.3 %in_product.7 = bf16[1024,512]{1,0:T(8,128)(2,1)} custom-call(bf16[1024,3072]{1,0:T(8,128)(2,1)} %assemble.1.rows_ref, bf16[3072,512]{1,0:T(8,128)(2,1)S(1)} %bitcast.89), custom_call_target="tpu_custom_call" | custom-call | flops 50331648 | bytes 163840 | tf_op jit(solution)/shard_map/in_product/pallas_call | solution.py:266
  328.8 4.9 add_parts.1
  337.8 15.2 %attend.1 = (bf16[1024,384]{1,0:T(8,128)(2,1)S(1)}, bf16[1024,384]{1,0:T(8,128)(2,1)S(1)}, bf16[1024,384]{1,0:T(8,128)(2,1)S(1)}, bf16[1024,384]{1,0:T(8,128)(2,1)S(1)}) custom-call(bf16[1024,1152]{1,0:T(8,128)(2,1)} %in_product.6.q_own.k_own.v_own, bf16[1024,1152]{1,0:T(8,128)(2,1)} %collective-permute-done.20.q_got.k_got.v_got, ...), custom_call_target="tpu_custom_call" | custom-call | flops 12582912 | bytes 98304 | tf_op jit(solution)/shard_map/attend/pallas_call | solution.py:75
  355.0 5.2 in_product.9
  362.7 12.4 %out_product.5.refs_3_ = bf16[1024,3072]{1,0:T(8,128)(2,1)} custom-call(bf16[1024,384]{1,0:T(8,128)(2,1)S(1)} %copy-done.28, bf16[1024,256]{1,0:T(8,128)(2,1)S(1)} %get-tuple-element.59.refs_1_, bf16[1024,512]{1,0:T(8,128)(2,1)S(1)} %get-tuple-element.51.refs_2_, bf16[384,3072]{1,0:T(8,128)(2,1)S(1)} %copy-done.2, bf16[1536,3072]{1,0:T(8,128)(2,1)} %refs_2_.9), custom_call_target="tpu_custom_call" | custom-call | flops 113246208 | bytes 282624 | tf_op jit(solution)/shard_map/out_product/pallas_call | solution.py:316
  375.0 18.3 %back_product.5.refs_4_ = bf16[1024,3072]{1,0:T(8,128)(2,1)} custom-call(bf16[1024,384]{1,0:T(8,128)(2,1)S(1)} %get-tuple-element.31.refs_0_, bf16[1024,384]{1,0:T(8,128)(2,1)S(1)} %get-tuple-element.32.refs_1_, bf16[1024,384]{1,0:T(8,128)(2,1)S(1)} %get-tuple-element.33.refs_2_, bf16[1024,256]{1,0:T(8,128)(2,1)S(1)} %get-tuple-element.58.refs_3_, ...), custom_call_target="tpu_custom_call" | custom-call | flops 188743680 | bytes 282624 | tf_op jit(solution)/shard_map/back_product/pallas_call | solution.py:316
  397.6 7.4 %out_product.6 = bf16[512,3072]{1,0:T(8,128)(2,1)S(1)} custom-call(bf16[1024,512]{1,0:T(8,128)(2,1)S(1)} %get-tuple-element.49.refs_0_, bf16[1024,256]{1,0:T(8,128)(2,1)S(1)} %get-tuple-element.57.refs_1_, bf16[1536,3072]{1,0:T(8,128)(2,1)} %refs_2_.9, bf16[1024,3072]{1,0:T(8,128)(2,1)} %out_product.5.refs_3_), custom_call_target="tpu_custom_call" | custom-call | flops 37748736 | bytes 196608 | tf_op jit(solution)/shard_map/out_product/pallas_call | solution.py:316
  405.1 7.8 %back_product.6 = bf16[512,3072]{1,0:T(8,128)(2,1)} custom-call(bf16[1024,512]{1,0:T(8,128)(2,1)S(1)} %get-tuple-element.48.refs_0_, bf16[1024,256]{1,0:T(8,128)(2,1)S(1)} %get-tuple-element.56.refs_1_, bf16[3072,512]{1,0:T(8,128)(2,1)} %bitcast.90, bf16[3072,256]{1,0:T(8,128)(2,1)} %bitcast.17.weight_ref.refs_3_, bf16[1024,3072]{1,0:T(8,128)(2,1)} %back_product.5.refs_4_), custom_call_target="tpu_custom_call" | custom-call | flops 37748736 | bytes 122880 | tf_op jit(solution)/shard_map/back_product/pallas_call | solution.py:316
  415.0 4.7 out_product.9
  421.7 3.8 out_product.8
  428.5 4.3 back_product.9
  434.6 3.4 back_product.8
  438.8 3.8 out_product.7
  442.6 3.4 back_product.7
  447.5 2.7 collective-permute-start.30
  450.9 14.6 %collective-permute-done.36 = bf16[2,2,64,1536]{3,2,0,1:T(8,128)(2,1)S(1)} collective-permute-done((bf16[2,2,64,1536]{3,2,0,1:T(8,128)(2,1)S(1)}, bf16[2,2,64,1536]{3,2,0,1:T(8,128)(2,1)S(1)}, u32[]{:S(2)}, u32[]{:S(2)}) %collective-permute-start.36) | collective-permute-done | bytes 786464 | tf_op jit(solution)/shard_map/ppermute | solution.py:121
  466.9 3.0 collective-permute-start.34
  471.5 10.3 %collective-permute-done.27 = bf16[2,64,1536]{2,1,0:T(8,128)(2,1)S(1)} collective-permute-done((bf16[2,64,1536]{2,1,0:T(8,128)(2,1)S(1)}, bf16[2,64,1536]{2,1,0:T(8,128)(2,1)S(1)}, u32[]{:S(2)}, u32[]{:S(2)}) %collective-permute-start.27) | collective-permute-done | bytes 393248 | tf_op jit(solution)/shard_map/ppermute | solution.py:121
  486.6 7.7 %collective-permute-done.34 = bf16[2,64,1536]{2,1,0:T(8,128)(2,1)S(1)} collective-permute-done((bf16[2,64,1536]{2,1,0:T(8,128)(2,1)S(1)}, bf16[2,64,1536]{2,1,0:T(8,128)(2,1)S(1)}, u32[]{:S(2)}, u32[]{:S(2)}) %collective-permute-start.34) | collective-permute-done | bytes 393248 | tf_op jit(solution)/shard_map/ppermute | solution.py:121
  496.4 9.2 %collective-permute-done.35 = bf16[64,1536]{1,0:T(8,128)(2,1)S(1)} collective-permute-done((bf16[64,1536]{1,0:T(8,128)(2,1)S(1)}, bf16[64,1536]{1,0:T(8,128)(2,1)S(1)}, u32[]{:S(2)}, u32[]{:S(2)}) %collective-permute-start.35) | collective-permute-done | bytes 196640 | tf_op jit(solution)/shard_map/ppermute | solution.py:121
  506.5 5.6 %all-reduce = (f32[64]{0:T(128)S(1)}, f32[64]{0:T(128)}) all-reduce(f32[64]{0:T(128)S(1)} %fusion.28, f32[64]{0:T(128)} %reduce_sum.48), channel_id=1, replica_groups=mesh['gx'=4,'gy'=4,'gz'=2] {'gz'}, use_global_device_ids=true, to_apply=%region_8.9 | all-reduce | flops 128 | bytes 1024 | tf_op jit(solution)/shard_map/psum | solution.py:462
  (183 shorter events, 77.5 us)
Async XLA Ops:
  0.7 12.3 %collective-permute-start.8 = (bf16[64,3072]{1,0:T(8,128)(2,1)}, bf16[64,3072]{1,0:T(8,128)(2,1)S(1)}, u32[]{:S(2)}, u32[]{:S(2)}) collective-permute-start(bf16[64,3072]{1,0:T(8,128)(2,1)} %param.9), channel_id=1, source_target_pairs={{0,16},{8,24},{16,0},{24,8},{1,17},{9,25},{17,1},{25,9},{2,18},{10... | collective-permute-start | bytes 1179656 | tf_op jit(solution)/shard_map/ppermute | solution.py:121
  13.9 32.1 %all-to-all-start = ((bf16[4,768,256]{2,1,0:T(8,128)(2,1)}), bf16[4,768,256]{2,1,0:T(8,128)(2,1)S(1)}, u32[]{:S(2)}, u32[]{:S(2)}) async-start(bf16[4,768,256]{2,1,0:T(8,128)(2,1)} %pack.5), calls=%async_computation | async-start | bytes 3145728 | tf_op jit(solution)/shard_map/all_to_all | solution.py:354
  17.7 28.3 %collective-permute-start = (bf16[64,3072]{1,0:T(8,128)(2,1)S(1)}, bf16[64,3072]{1,0:T(8,128)(2,1)S(1)}, u32[]{:S(2)}, u32[]{:S(2)}) collective-permute-start(bf16[64,3072]{1,0:T(8,128)(2,1)S(1)} %fusion.27), channel_id=1, source_target_pairs={{0,16},{8,24},{16,0},{24,8},{1,17},{9,25},{17,1},{25,9},{2,18},{10... | collective-permute-start | bytes 1179656 | tf_op jit(solution)/shard_map/ppermute | solution.py:121
  47.3 84.5 %all-to-all-start.1 = ((bf16[4,768,1152]{2,1,0:T(8,128)(2,1)}), bf16[4,768,1152]{2,1,0:T(8,128)(2,1)}, u32[]{:S(2)}, u32[]{:S(2)}) async-start(bf16[4,768,1152]{2,1,0:T(8,128)(2,1)} %pack.6), calls=%async_computation.1 | async-start | bytes 14155776 | tf_op jit(solution)/shard_map/all_to_all | solution.py:354
  52.7 37.0 %collective-permute-start.11 = (bf16[2,64,3072]{2,1,0:T(8,128)(2,1)}, bf16[2,64,3072]{2,1,0:T(8,128)(2,1)}, u32[]{:S(2)}, u32[]{:S(2)}) collective-permute-start(bf16[2,64,3072]{2,1,0:T(8,128)(2,1)} %pad_maximum_fusion.1.own_ref), channel_id=1, source_target_pairs={{0,2},{2,0},{4,6},{6,4},{1,3},{3,1},{5,7},{7,5},{8,10},{10,8},{12,... | collective-permute-start | bytes 2359304 | tf_op jit(solution)/shard_map/ppermute | solution.py:121
  54.6 37.7 %collective-permute-start.9 = (bf16[2,64,3072]{2,1,0:T(8,128)(2,1)}, bf16[2,64,3072]{2,1,0:T(8,128)(2,1)}, u32[]{:S(2)}, u32[]{:S(2)}) collective-permute-start(bf16[2,64,3072]{2,1,0:T(8,128)(2,1)} %pad_maximum_fusion.1.own_ref), channel_id=1, source_target_pairs={{0,4},{2,6},{4,0},{6,2},{1,5},{3,7},{5,1},{7,3},{8,12},{10,14},{12... | collective-permute-start | bytes 2359304 | tf_op jit(solution)/shard_map/ppermute | solution.py:121
  57.2 79.4 %collective-permute-start.16 = (bf16[2,64,3072]{2,1,0:T(8,128)(2,1)}, bf16[2,64,3072]{2,1,0:T(8,128)(2,1)}, u32[]{:S(2)}, u32[]{:S(2)}) collective-permute-start(bf16[2,64,3072]{2,1,0:T(8,128)(2,1)} %pad_maximum_fusion.1.own_ref), channel_id=1, source_target_pairs={{0,8},{8,0},{16,24},{24,16},{1,9},{9,1},{17,25},{25,17},{2,10},{10... | collective-permute-start | bytes 2359304 | tf_op jit(solution)/shard_map/ppermute | solution.py:121
  89.7 57.3 %collective-permute-start.12 = (bf16[2,64,3072]{2,1,0:T(8,128)(2,1)}, bf16[2,64,3072]{2,1,0:T(8,128)(2,1)}, u32[]{:S(2)}, u32[]{:S(2)}) collective-permute-start(bf16[2,64,3072]{2,1,0:T(8,128)(2,1)} %collective-permute-done.11.own_ref), channel_id=1, source_target_pairs={{0,8},{8,0},{16,24},{24,16},{1,9},{9,1},{17,25},{25,17},{2,10},{10... | collective-permute-start | bytes 2359304 | tf_op jit(solution)/shard_map/ppermute | solution.py:121
  89.7 66.3 %collective-permute-start.4 = (bf16[2,64,3072]{2,1,0:T(8,128)(2,1)S(1)}, bf16[2,64,3072]{2,1,0:T(8,128)(2,1)}, u32[]{:S(2)}, u32[]{:S(2)}) collective-permute-start(bf16[2,64,3072]{2,1,0:T(8,128)(2,1)S(1)} %pad_maximum_fusion.refs_0_), channel_id=1, source_target_pairs={{0,4},{2,6},{4,0},{6,2},{1,5},{3,7},{5,1},{7,3},{8,12},{10,14},{12... | collective-permute-start | bytes 2359304 | tf_op jit(solution)/shard_map/ppermute | solution.py:121
  92.2 65.5 %collective-permute-start.18 = (bf16[2,64,3072]{2,1,0:T(8,128)(2,1)}, bf16[2,64,3072]{2,1,0:T(8,128)(2,1)}, u32[]{:S(2)}, u32[]{:S(2)}) collective-permute-start(bf16[2,64,3072]{2,1,0:T(8,128)(2,1)} %collective-permute-done.9.own_ref), channel_id=1, source_target_pairs={{0,8},{8,0},{16,24},{24,16},{1,9},{9,1},{17,25},{25,17},{2,10},{10... | collective-permute-start | bytes 2359304 | tf_op jit(solution)/shard_map/ppermute | solution.py:121
  92.2 65.7 %collective-permute-start.10 = (bf16[2,64,3072]{2,1,0:T(8,128)(2,1)}, bf16[2,64,3072]{2,1,0:T(8,128)(2,1)}, u32[]{:S(2)}, u32[]{:S(2)}) collective-permute-start(bf16[2,64,3072]{2,1,0:T(8,128)(2,1)} %collective-permute-done.9.own_ref), channel_id=1, source_target_pairs={{0,2},{2,0},{4,6},{6,4},{1,3},{3,1},{5,7},{7,5},{8,10},{10,8},{12,... | collective-permute-start | bytes 2359304 | tf_op jit(solution)/shard_map/ppermute | solution.py:121
  131.8 90.5 %all-to-all-start.2 = ((bf16[4,768,512]{2,1,0:T(8,128)(2,1)}), bf16[4,768,512]{2,1,0:T(8,128)(2,1)}, u32[]{:S(2)}, u32[]{:S(2)}) async-start(bf16[4,768,512]{2,1,0:T(8,128)(2,1)} %copy-done.10), calls=%async_computation.2 | async-start | bytes 6291456 | tf_op jit(solution)/shard_map/all_to_all | solution.py:354
  145.2 24.6 %collective-permute-start.17 = (bf16[256,1920]{1,0:T(8,128)(2,1)S(1)}, bf16[256,1920]{1,0:T(8,128)(2,1)S(1)}, u32[]{:S(2)}, u32[]{:S(2)}) collective-permute-start(bf16[256,1920]{1,0:T(8,128)(2,1)S(1)} %cot_product.6), channel_id=1, source_target_pairs={{0,1},{1,0},{2,3},{3,2},{4,5},{5,4},{6,7},{7,6},{8,9},{9,8},{10,11... | collective-permute-start | bytes 2949128 | tf_op jit(solution)/shard_map/ppermute | solution.py:121
  155.6 23.1 %copy-start.17 = (bf16[256,1920]{1,0:T(8,128)(2,1)}, bf16[256,1920]{1,0:T(8,128)(2,1)S(1)}, u32[]{:S(2)}) copy-start(bf16[256,1920]{1,0:T(8,128)(2,1)S(1)} %cot_product.4) | copy-start | bytes 2949124
  155.6 37.3 %collective-permute-start.13 = (bf16[256,1920]{1,0:T(8,128)(2,1)S(1)}, bf16[256,1920]{1,0:T(8,128)(2,1)S(1)}, u32[]{:S(2)}, u32[]{:S(2)}) collective-permute-start(bf16[256,1920]{1,0:T(8,128)(2,1)S(1)} %cot_product.4), channel_id=1, source_target_pairs={{0,1},{1,0},{2,3},{3,2},{4,5},{5,4},{6,7},{7,6},{8,9},{9,8},{10,11... | collective-permute-start | bytes 2949128 | tf_op jit(solution)/shard_map/ppermute | solution.py:121
  156.0 22.8 %collective-permute-start.2 = (bf16[2,64,3072]{2,1,0:T(8,128)(2,1)S(1)}, bf16[2,64,3072]{2,1,0:T(8,128)(2,1)S(1)}, u32[]{:S(2)}, u32[]{:S(2)}) collective-permute-start(bf16[2,64,3072]{2,1,0:T(8,128)(2,1)S(1)} %pad_maximum_fusion.refs_0_), channel_id=1, source_target_pairs={{0,2},{2,0},{4,6},{6,4},{1,3},{3,1},{5,7},{7,5},{8,10},{10,8},{12,... | collective-permute-start | bytes 2359304 | tf_op jit(solution)/shard_map/ppermute | solution.py:121
  157.8 34.7 %collective-permute-start.6 = (bf16[2,64,3072]{2,1,0:T(8,128)(2,1)}, bf16[2,64,3072]{2,1,0:T(8,128)(2,1)S(1)}, u32[]{:S(2)}, u32[]{:S(2)}) collective-permute-start(bf16[2,64,3072]{2,1,0:T(8,128)(2,1)} %collective-permute-done.4.refs_4_), channel_id=1, source_target_pairs={{0,2},{2,0},{4,6},{6,4},{1,3},{3,1},{5,7},{7,5},{8,10},{10,8},{12,... | collective-permute-start | bytes 2359304 | tf_op jit(solution)/shard_map/ppermute | solution.py:121
  158.0 34.5 %collective-permute-start.14 = (bf16[2,64,3072]{2,1,0:T(8,128)(2,1)}, bf16[2,64,3072]{2,1,0:T(8,128)(2,1)S(1)}, u32[]{:S(2)}, u32[]{:S(2)}) collective-permute-start(bf16[2,64,3072]{2,1,0:T(8,128)(2,1)} %collective-permute-done.10.own_ref), channel_id=1, source_target_pairs={{0,8},{8,0},{16,24},{24,16},{1,9},{9,1},{17,25},{25,17},{2,10},{10... | collective-permute-start | bytes 2359304 | tf_op jit(solution)/shard_map/ppermute | solution.py:121
  169.8 32.6 %collective-permute-start.1 = (bf16[2,64,3072]{2,1,0:T(8,128)(2,1)S(1)}, bf16[2,64,3072]{2,1,0:T(8,128)(2,1)S(1)}, u32[]{:S(2)}, u32[]{:S(2)}) collective-permute-start(bf16[2,64,3072]{2,1,0:T(8,128)(2,1)S(1)} %pad_maximum_fusion.refs_0_), channel_id=1, source_target_pairs={{0,8},{8,0},{16,24},{24,16},{1,9},{9,1},{17,25},{25,17},{2,10},{10... | collective-permute-start | bytes 2359304 | tf_op jit(solution)/shard_map/ppermute | solution.py:121
  178.8 23.6 %copy-start.19 = (bf16[256,1920]{1,0:T(8,128)(2,1)}, bf16[256,1920]{1,0:T(8,128)(2,1)S(1)}, u32[]{:S(2)}) copy-start(bf16[256,1920]{1,0:T(8,128)(2,1)S(1)} %cot_product.7) | copy-start | bytes 2949124
  178.8 37.2 %collective-permute-start.19 = (bf16[256,1920]{1,0:T(8,128)(2,1)S(1)}, bf16[256,1920]{1,0:T(8,128)(2,1)S(1)}, u32[]{:S(2)}, u32[]{:S(2)}) collective-permute-start(bf16[256,1920]{1,0:T(8,128)(2,1)S(1)} %cot_product.7), channel_id=1, source_target_pairs={{0,1},{1,0},{2,3},{3,2},{4,5},{5,4},{6,7},{7,6},{8,9},{9,8},{10,11... | collective-permute-start | bytes 2949128 | tf_op jit(solution)/shard_map/ppermute | solution.py:121
  192.4 17.7 %collective-permute-start.5 = (bf16[2,64,3072]{2,1,0:T(8,128)(2,1)}, bf16[2,64,3072]{2,1,0:T(8,128)(2,1)S(1)}, u32[]{:S(2)}, u32[]{:S(2)}) collective-permute-start(bf16[2,64,3072]{2,1,0:T(8,128)(2,1)} %collective-permute-done.4.refs_4_), channel_id=1, source_target_pairs={{0,8},{8,0},{16,24},{24,16},{1,9},{9,1},{17,25},{25,17},{2,10},{10... | collective-permute-start | bytes 2359304 | tf_op jit(solution)/shard_map/ppermute | solution.py:121
  192.4 17.7 %collective-permute-start.3 = (bf16[2,64,3072]{2,1,0:T(8,128)(2,1)S(1)}, bf16[2,64,3072]{2,1,0:T(8,128)(2,1)S(1)}, u32[]{:S(2)}, u32[]{:S(2)}) collective-permute-start(bf16[2,64,3072]{2,1,0:T(8,128)(2,1)S(1)} %collective-permute-done.2.refs_2_), channel_id=1, source_target_pairs={{0,8},{8,0},{16,24},{24,16},{1,9},{9,1},{17,25},{25,17},{2,10},{10... | collective-permute-start | bytes 2359304 | tf_op jit(solution)/shard_map/ppermute | solution.py:121
  193.0 17.2 %collective-permute-start.7 = (bf16[2,64,3072]{2,1,0:T(8,128)(2,1)S(1)}, bf16[2,64,3072]{2,1,0:T(8,128)(2,1)S(1)}, u32[]{:S(2)}, u32[]{:S(2)}) collective-permute-start(bf16[2,64,3072]{2,1,0:T(8,128)(2,1)S(1)} %collective-permute-done.6.refs_6_), channel_id=1, source_target_pairs={{0,8},{8,0},{16,24},{24,16},{1,9},{9,1},{17,25},{25,17},{2,10},{10... | collective-permute-start | bytes 2359304 | tf_op jit(solution)/shard_map/ppermute | solution.py:121
  202.4 30.3 %collective-permute-start.15 = (bf16[256,1920]{1,0:T(8,128)(2,1)}, bf16[256,1920]{1,0:T(8,128)(2,1)}, u32[]{:S(2)}, u32[]{:S(2)}) collective-permute-start(bf16[256,1920]{1,0:T(8,128)(2,1)} %cot_product.5), channel_id=1, source_target_pairs={{0,1},{1,0},{2,3},{3,2},{4,5},{5,4},{6,7},{7,6},{8,9},{9,8},{10,11... | collective-permute-start | bytes 2949128 | tf_op jit(solution)/shard_map/ppermute | solution.py:121
  222.3 40.6 %all-to-all-start.3 = ((bf16[4,768,512]{2,1,0:T(8,128)(2,1)}), bf16[4,768,512]{2,1,0:T(8,128)(2,1)S(1)}, u32[]{:S(2)}, u32[]{:S(2)}) async-start(bf16[4,768,512]{2,1,0:T(8,128)(2,1)} %copy-done.11), calls=%async_computation.3 | async-start | bytes 6291456 | tf_op jit(solution)/shard_map/all_to_all | solution.py:354
  247.4 73.2 %collective-permute-start.20 = (bf16[1024,1152]{1,0:T(8,128)(2,1)}, bf16[1024,1152]{1,0:T(8,128)(2,1)}, u32[]{:S(2)}, u32[]{:S(2)}) collective-permute-start(bf16[1024,1152]{1,0:T(8,128)(2,1)} %in_product.6.q_own.k_own.v_own), channel_id=1, source_target_pairs={{0,1},{1,0},{2,3},{3,2},{4,5},{5,4},{6,7},{7,6},{8,9},{9,8},{10,11... | collective-permute-start | bytes 7077896 | tf_op jit(solution)/shard_map/ppermute | solution.py:121
  249.1 62.7 %collective-permute-start.21 = (bf16[1024,256]{1,0:T(8,128)(2,1)}, bf16[1024,256]{1,0:T(8,128)(2,1)}, u32[]{:S(2)}, u32[]{:S(2)}) collective-permute-start(bf16[1024,256]{1,0:T(8,128)(2,1)} %in_product.5), channel_id=1, source_target_pairs={{0,1},{1,0},{2,3},{3,2},{4,5},{5,4},{6,7},{7,6},{8,9},{9,8},{10,11... | collective-permute-start | bytes 1572872 | tf_op jit(solution)/shard_map/ppermute | solution.py:121
  262.9 57.6 %copy-start = (bf16[4,768,512]{2,1,0:T(8,128)(2,1)}, bf16[4,768,512]{2,1,0:T(8,128)(2,1)S(1)}, u32[]{:S(2)}) copy-start(bf16[4,768,512]{2,1,0:T(8,128)(2,1)S(1)} %all-to-all-done.3) | copy-start | bytes 9437188
  262.9 92.1 %all-to-all-start.4 = ((bf16[4,768,256]{2,1,0:T(8,128)(2,1)}), bf16[4,768,256]{2,1,0:T(8,128)(2,1)}, u32[]{:S(2)}, u32[]{:S(2)}) async-start(bf16[4,768,256]{2,1,0:T(8,128)(2,1)} %copy-done.12), calls=%async_computation.4 | async-start | bytes 3145728 | tf_op jit(solution)/shard_map/all_to_all | solution.py:354
  318.7 35.2 %collective-permute-start.22 = (bf16[1024,512]{1,0:T(8,128)(2,1)S(1)}, bf16[1024,512]{1,0:T(8,128)(2,1)S(1)}, u32[]{:S(2)}, u32[]{:S(2)}) collective-permute-start(bf16[1024,512]{1,0:T(8,128)(2,1)S(1)} %in_product.8), channel_id=1, source_target_pairs={{0,1},{1,0},{2,3},{3,2},{4,5},{5,4},{6,7},{7,6},{8,9},{9,8},{10,11... | collective-permute-start | bytes 3145736 | tf_op jit(solution)/shard_map/ppermute | solution.py:121
  327.8 65.5 %collective-permute-start.23 = (bf16[1024,512]{1,0:T(8,128)(2,1)}, bf16[1024,512]{1,0:T(8,128)(2,1)}, u32[]{:S(2)}, u32[]{:S(2)}) collective-permute-start(bf16[1024,512]{1,0:T(8,128)(2,1)} %in_product.7), channel_id=1, source_target_pairs={{0,1},{1,0},{2,3},{3,2},{4,5},{5,4},{6,7},{7,6},{8,9},{9,8},{10,11... | collective-permute-start | bytes 3145736 | tf_op jit(solution)/shard_map/ppermute | solution.py:121
  360.2 35.8 %collective-permute-start.24 = (bf16[1024,256]{1,0:T(8,128)(2,1)S(1)}, bf16[1024,256]{1,0:T(8,128)(2,1)}, u32[]{:S(2)}, u32[]{:S(2)}) collective-permute-start(bf16[1024,256]{1,0:T(8,128)(2,1)S(1)} %in_product.9), channel_id=1, source_target_pairs={{0,1},{1,0},{2,3},{3,2},{4,5},{5,4},{6,7},{7,6},{8,9},{9,8},{10,11... | collective-permute-start | bytes 1572872 | tf_op jit(solution)/shard_map/ppermute | solution.py:121
  405.0 8.3 %collective-permute-start.25 = (bf16[512,3072]{1,0:T(8,128)(2,1)S(1)}, bf16[512,3072]{1,0:T(8,128)(2,1)S(1)}, u32[]{:S(2)}, u32[]{:S(2)}) collective-permute-start(bf16[512,3072]{1,0:T(8,128)(2,1)S(1)} %out_product.6), channel_id=1, source_target_pairs={{0,8},{8,0},{16,24},{24,16},{1,9},{9,1},{17,25},{25,17},{2,10},{10... | collective-permute-start | bytes 9437192 | tf_op jit(solution)/shard_map/ppermute | solution.py:121
  412.9 14.0 %collective-permute-start.32 = (bf16[512,3072]{1,0:T(8,128)(2,1)}, bf16[512,3072]{1,0:T(8,128)(2,1)S(1)}, u32[]{:S(2)}, u32[]{:S(2)}) collective-permute-start(bf16[512,3072]{1,0:T(8,128)(2,1)} %back_product.6), channel_id=1, source_target_pairs={{0,8},{8,0},{16,24},{24,16},{1,9},{9,1},{17,25},{25,17},{2,10},{10... | collective-permute-start | bytes 9437192 | tf_op jit(solution)/shard_map/ppermute | solution.py:121
  419.9 26.1 %collective-permute-start.29 = (bf16[2,2,64,1536]{3,2,0,1:T(8,128)(2,1)S(1)}, bf16[2,2,64,1536]{3,2,0,1:T(8,128)(2,1)}, u32[]{:S(2)}, u32[]{:S(2)}) collective-permute-start(bf16[2,2,64,1536]{3,2,0,1:T(8,128)(2,1)S(1)} %bitcast.115), channel_id=1, source_target_pairs={{0,2},{2,0},{4,6},{6,4},{1,3},{3,1},{5,7},{7,5},{8,10},{10,8},{12,... | collective-permute-start | bytes 2359304 | tf_op jit(solution)/shard_map/ppermute | solution.py:121
  425.4 24.7 %collective-permute-start.26 = (bf16[256,1536]{1,0:T(8,128)(2,1)S(1)}, bf16[256,1536]{1,0:T(8,128)(2,1)S(1)}, u32[]{:S(2)}, u32[]{:S(2)}) collective-permute-start(bf16[256,1536]{1,0:T(8,128)(2,1)S(1)} %out_product.8), channel_id=1, source_target_pairs={{0,16},{8,24},{16,0},{24,8},{1,17},{9,25},{17,1},{25,9},{2,18},{10... | collective-permute-start | bytes 2359304 | tf_op jit(solution)/shard_map/ppermute | solution.py:121
  432.9 32.6 %collective-permute-start.36 = (bf16[2,2,64,1536]{3,2,0,1:T(8,128)(2,1)S(1)}, bf16[2,2,64,1536]{3,2,0,1:T(8,128)(2,1)S(1)}, u32[]{:S(2)}, u32[]{:S(2)}) collective-permute-start(bf16[2,2,64,1536]{3,2,0,1:T(8,128)(2,1)S(1)} %bitcast.114), channel_id=1, source_target_pairs={{0,2},{2,0},{4,6},{6,4},{1,3},{3,1},{5,7},{7,5},{8,10},{10,8},{12,... | collective-permute-start | bytes 2359304 | tf_op jit(solution)/shard_map/ppermute | solution.py:121
  438.1 28.6 %collective-permute-start.33 = (bf16[256,1536]{1,0:T(8,128)(2,1)S(1)}, bf16[256,1536]{1,0:T(8,128)(2,1)S(1)}, u32[]{:S(2)}, u32[]{:S(2)}) collective-permute-start(bf16[256,1536]{1,0:T(8,128)(2,1)S(1)} %back_product.8), channel_id=1, source_target_pairs={{0,16},{8,24},{16,0},{24,8},{1,17},{9,25},{17,1},{25,9},{2,18},{10... | collective-permute-start | bytes 2359304 | tf_op jit(solution)/shard_map/ppermute | solution.py:121
  447.5 22.5 %collective-permute-start.30 = (bf16[2,64,1536]{2,1,0:T(8,128)(2,1)S(1)}, bf16[2,64,1536]{2,1,0:T(8,128)(2,1)S(1)}, u32[]{:S(2)}, u32[]{:S(2)}) collective-permute-start(bf16[2,64,1536]{2,1,0:T(8,128)(2,1)S(1)} %fusion.39), channel_id=1, source_target_pairs={{0,4},{2,6},{4,0},{6,2},{1,5},{3,7},{5,1},{7,3},{8,12},{10,14},{12... | collective-permute-start | bytes 1179656 | tf_op jit(solution)/shard_map/ppermute | solution.py:121
  450.4 31.3 %collective-permute-start.27 = (bf16[2,64,1536]{2,1,0:T(8,128)(2,1)S(1)}, bf16[2,64,1536]{2,1,0:T(8,128)(2,1)S(1)}, u32[]{:S(2)}, u32[]{:S(2)}) collective-permute-start(bf16[2,64,1536]{2,1,0:T(8,128)(2,1)S(1)} %fusion.41), channel_id=1, source_target_pairs={{0,2},{2,0},{4,6},{6,4},{1,3},{3,1},{5,7},{7,5},{8,10},{10,8},{12,... | collective-permute-start | bytes 1179656 | tf_op jit(solution)/shard_map/ppermute | solution.py:121
  465.8 19.3 %collective-permute-start.37 = (bf16[2,64,1536]{2,1,0:T(8,128)(2,1)S(1)}, bf16[2,64,1536]{2,1,0:T(8,128)(2,1)S(1)}, u32[]{:S(2)}, u32[]{:S(2)}) collective-permute-start(bf16[2,64,1536]{2,1,0:T(8,128)(2,1)S(1)} %fusion.40), channel_id=1, source_target_pairs={{0,4},{2,6},{4,0},{6,2},{1,5},{3,7},{5,1},{7,3},{8,12},{10,14},{12... | collective-permute-start | bytes 1179656 | tf_op jit(solution)/shard_map/ppermute | solution.py:121
  466.9 27.3 %collective-permute-start.34 = (bf16[2,64,1536]{2,1,0:T(8,128)(2,1)S(1)}, bf16[2,64,1536]{2,1,0:T(8,128)(2,1)S(1)}, u32[]{:S(2)}, u32[]{:S(2)}) collective-permute-start(bf16[2,64,1536]{2,1,0:T(8,128)(2,1)S(1)} %fusion.42), channel_id=1, source_target_pairs={{0,2},{2,0},{4,6},{6,4},{1,3},{3,1},{5,7},{7,5},{8,10},{10,8},{12,... | collective-permute-start | bytes 1179656 | tf_op jit(solution)/shard_map/ppermute | solution.py:121
  470.1 42.0 %collective-permute-start.31 = (bf16[64,1536]{1,0:T(8,128)(2,1)S(1)}, bf16[64,1536]{1,0:T(8,128)(2,1)}, u32[]{:S(2)}, u32[]{:S(2)}) collective-permute-start(bf16[64,1536]{1,0:T(8,128)(2,1)S(1)} %fusion.48), channel_id=1, source_target_pairs={{0,16},{8,24},{16,0},{24,8},{1,17},{9,25},{17,1},{25,9},{2,18},{10... | collective-permute-start | bytes 589832 | tf_op jit(solution)/shard_map/ppermute | solution.py:121
  481.9 31.8 %collective-permute-start.28 = (bf16[64,1536]{1,0:T(8,128)(2,1)S(1)}, bf16[64,1536]{1,0:T(8,128)(2,1)}, u32[]{:S(2)}, u32[]{:S(2)}) collective-permute-start(bf16[64,1536]{1,0:T(8,128)(2,1)S(1)} %fusion.47), channel_id=1, source_target_pairs={{0,4},{2,6},{4,0},{6,2},{1,5},{3,7},{5,1},{7,3},{8,12},{10,14},{12... | collective-permute-start | bytes 589832 | tf_op jit(solution)/shard_map/ppermute | solution.py:121
  485.2 21.0 %copy-start.31 = (bf16[64,3072]{1,0:T(8,128)(2,1)S(1)}, bf16[64,3072]{1,0:T(8,128)(2,1)}, u32[]{:S(2)}) copy-start(bf16[64,3072]{1,0:T(8,128)(2,1)} %param.8) | copy-start | bytes 1179652
  485.2 11.0 %collective-permute-start.38 = (bf16[64,1536]{1,0:T(8,128)(2,1)S(1)}, bf16[64,1536]{1,0:T(8,128)(2,1)S(1)}, u32[]{:S(2)}, u32[]{:S(2)}) collective-permute-start(bf16[64,1536]{1,0:T(8,128)(2,1)S(1)} %fusion.50), channel_id=1, source_target_pairs={{0,16},{8,24},{16,0},{24,8},{1,17},{9,25},{17,1},{25,9},{2,18},{10... | collective-permute-start | bytes 589832 | tf_op jit(solution)/shard_map/ppermute | solution.py:121
  494.4 11.2 %collective-permute-start.35 = (bf16[64,1536]{1,0:T(8,128)(2,1)S(1)}, bf16[64,1536]{1,0:T(8,128)(2,1)S(1)}, u32[]{:S(2)}, u32[]{:S(2)}) collective-permute-start(bf16[64,1536]{1,0:T(8,128)(2,1)S(1)} %fusion.49), channel_id=1, source_target_pairs={{0,4},{2,6},{4,0},{6,2},{1,5},{3,7},{5,1},{7,3},{8,12},{10,14},{12... | collective-permute-start | bytes 589832 | tf_op jit(solution)/shard_map/ppermute | solution.py:121
  (34 other events, 193.8 us)

commit v8 on v7

--- a/solution.py
+++ b/solution.py
@@ -278,7 +278,7 @@
     )(rows, weight)
 
 
-def product(terms, weights, adds, start, count, kind, transposed, window=None):
+def product(terms, weights, adds, start, count, kind, transposed, window=None, rows=None):
     whole = weights[0].shape[0 if transposed else 1]
     first_column, columns = window or (0, whole)
     tile = 512 if columns % 512 == 0 else 384 if columns % 384 == 0 else 256
@@ -291,7 +291,8 @@
         if transposed:
             specs.append(pl.BlockSpec((tile, weight.shape[1]), lambda n: (n + skip, 0)))
         else:
-            specs.append(pl.BlockSpec((weight.shape[0], tile), lambda n: (0, n + skip)))
+            block, size = rows or (0, weight.shape[0])
+            specs.append(pl.BlockSpec((size, tile), lambda n, block=block: (block, n + skip)))
     for _, first in adds:
         specs.append(
             pl.BlockSpec((count, tile), lambda n, place=first // count: (place, n + skip))
@@ -362,8 +363,6 @@
     ]
 
     cot_pair = with_x(out_cotangent)
-    in_mlp = [swap(after(packed_mlp[0], cot_pair))]
-
     wide = layer_input.astype(jnp.float32)
     total, squares = lax.psum((jnp.sum(wide, axis=1), jnp.sum(wide * wide, axis=1)), "gz")
     center = total / D
@@ -371,7 +370,6 @@
     inverse = lax.rsqrt(spread + EPSILON)
     normed = (wide - center[:, None]) * inverse[:, None]
     normed_pair = with_x(half(normed))
-    in_heads = swap(after(packed_heads, normed_pair, in_mlp[0]))
 
     cot_owns, cot_gots = [], []
     for place, (own, other) in enumerate(gather_parts(cot_pair)):
@@ -379,23 +377,25 @@
             own = after(own, cot_gots[place - 2])
         cot_owns.append(cot_product((own, other), w_attn_out, w_mlp_out))
         cot_gots.append(others(cot_owns[-1]))
-
     all_in = assemble(gather_parts(normed_pair))
-    mlp_own = [in_product(after(all_in, cot_gots[2]), in_mlp[0])]
+
+    in_heads = swap(after(packed_heads, normed_pair, cot_owns[0]))
+    in_mlp = [swap(after(packed_mlp[0], in_heads, cot_owns[2]))]
+    in_mlp.append(swap(after(packed_mlp[1], in_mlp[0], cot_owns[3])))
+    heads_own = in_product(after(all_in, cot_gots[2]), in_heads)
+    heads_got = others(heads_own)
+    mlp_own = [in_product(after(all_in, cot_gots[3], heads_own), in_mlp[0])]
     mlp_got = [others(mlp_own[0])]
-    heads_own = in_product(after(all_in, cot_gots[3], mlp_own[0]), in_heads)
-    heads_got = others(heads_own)
-    in_mlp.append(swap(after(packed_mlp[1], in_heads)))
-    mlp_own.append(in_product(after(all_in, mlp_got[0]), in_mlp[1]))
+    in_mlp.append(swap(after(packed_mlp[2], in_mlp[1], heads_own)))
+    mlp_own.append(in_product(after(all_in, mlp_own[0]), in_mlp[1]))
     mlp_got.append(others(mlp_own[1]))
-    in_mlp.append(swap(after(packed_mlp[2], in_mlp[1], mlp_own[0])))
+    in_mlp.append(swap(after(packed_mlp[3], in_mlp[2], mlp_own[0])))
     mlp_own.append(in_product(after(all_in, heads_got), in_mlp[2]))
     mlp_got.append(others(mlp_own[2]))
-    in_mlp.append(swap(after(packed_mlp[3], in_mlp[2], heads_own)))
 
     out_grad = add_parts(cot_owns, cot_gots)
     mixed, *head_grads = attend(heads_own, heads_got, out_grad)
-    mlp_own.append(in_product(after(all_in, mlp_got[1], mixed), in_mlp[3]))
+    mlp_own.append(in_product(after(all_in, mlp_got[0], mixed), in_mlp[3]))
     mlp_got.append(others(mlp_own[3]))
 
     forward_terms, backward_terms = [(mixed, 0, 0)], []
@@ -424,12 +424,14 @@
     backward_terms = [
         (grad, index - 1 - EARLY_CUTS, offset) for grad, index, offset in backward_terms
     ]
-    forward_terms = [(act, 0, offset) for act, _, offset in forward_terms]
+    early, all_columns = starts[EARLY_CUTS], sum(MLP_CUTS)
+    late_rows = (early // (all_columns - early), all_columns - early)
+    forward_terms = [(act, 0, offset - early) for act, _, offset in forward_terms]
 
     def forward_term(start, size, adds, window=None):
         adds = [(forward_early, start), *adds]
         return product(
-            forward_terms, [w_mlp_out], adds, start, size, jnp.bfloat16, False, window
+            forward_terms, [w_mlp_out], adds, start, size, jnp.bfloat16, False, window, late_rows
         )
 
     def backward_term(start, size, adds, window=None):
@@ -441,24 +443,28 @@
     def wider(value):
         return value.astype(jnp.float32)
 
-    def spread_rows(term):
-        half_width = features // 2
-        low, high = (0, half_width), (half_width, half_width)
-        from_core = trade(term(0, 2 * count, []), "gx", 1)
-        from_x = trade(term(2 * count, count, [(from_core, 0)], low), "gx", 2)
-        both = term(2 * count, 2 * count, [(from_core, 0)], high)
-        both = both.reshape(2, 2, 2, own_rows, half_width)
+    def over_x_z(term, from_core, window):
+        from_x = trade(term(2 * count, count, [(from_core, 0)], window), "gx", 2)
+        mine = wide_sum(term(3 * count, count, [(from_core, count)], window), from_x)
+        mine = mine.reshape(2, 2, own_rows, window[1])
+        pair = mine[:, 0] + wider(trade(half(mine[:, 1]), "gy", 1))
+        return pair[0] + wider(trade(half(pair[1]), "gy", 2))
+
+    def over_z_x(term, from_core, window):
+        both = term(2 * count, 2 * count, [(from_core, 0)], window)
+        both = both.reshape(2, 2, 2, own_rows, window[1])
         pair = wide_sum(both[:, :, 0], trade(both[:, :, 1], "gy", 1))
         ends = pair[:, 0] + wider(trade(half(pair[:, 1]), "gy", 2))
-        high_sum = ends[1] + wider(trade(half(ends[0]), "gx", 2))
-        mine = wide_sum(term(3 * count, count, [(from_core, count)], low), from_x)
-        mine = mine.reshape(2, 2, own_rows, half_width)
-        pair = mine[:, 0] + wider(trade(half(mine[:, 1]), "gy", 1))
-        low_sum = pair[0] + wider(trade(half(pair[1]), "gy", 2))
-        return jnp.concatenate([low_sum, high_sum], axis=1)
-
-    layer_out = half(wide + spread_rows(forward_term))
-    normed_grad = spread_rows(backward_term)
+        return ends[1] + wider(trade(half(ends[0]), "gx", 2))
+
+    def spread_rows(term, ways):
+        width = features // len(ways)
+        from_core = trade(term(0, 2 * count, []), "gx", 1)
+        sums = [way(term, from_core, (place * width, width)) for place, way in enumerate(ways)]
+        return jnp.concatenate(sums, axis=1)
+
+    normed_grad = spread_rows(backward_term, (over_x_z, over_z_x))
+    layer_out = half(wide + spread_rows(forward_term, (over_x_z, over_x_z)))
     first, second = lax.psum(
         (jnp.sum(normed_grad, axis=1), jnp.sum(normed_grad * normed, axis=1)), "gz"
     )

time: 518 us -> 547 us (1.056)
  waiting for transfers between devices: 214 us -> 237 us
  local copies, waits for them, and re-layouts: 18.8 us -> 25.5 us
    ppermute x39, waiting for transfers between devices: 171 us -> 212 us  [trade(): return lax.ppermute(block, axis, pairs)]
    all_to_all x5, waiting for transfers between devices: 42.6 us -> 25.5 us  [swap(): lax.all_to_all(packed, 'gx', split_axis=0, concat_axis=0, tiled=True)]
    unnamed x78 -> x79, local copies, waits for them, and re-layouts: 18.4 us -> 25.1 us
    pallas_call x10 -> x11, Pallas kernels: 69.2 us -> 68.9 us  [product(): pl.pallas_call(kernel, grid=(columns // tile,), in_specs=specs, out_specs...]
  transfers between devices with their start and end apart: 44 -> 44, of which waited for: 15 -> 13; matrix products, arithmetic and copies ran while one was open for 2% -> 3% of each run, Pallas kernels for 35% -> 31%
where the time goes in v8:
time: 547 us; the launch traced here: 545 us
  waiting for transfers between devices  237 us (43%)
  Pallas kernels  185 us (34%)
  starting transfers between devices  68.2 us (12%)
  local copies, waits for them, and re-layouts  25.5 us (5%)
  other arithmetic  17.1 us (3%)
  blocking collectives  10.5 us (2%)
    ppermute x39, waiting for transfers between devices, trade(): return lax.ppermute(block, axis, pairs)  212 us
    pallas_call x11, Pallas kernels, product(): pl.pallas_call(kernel, grid=(columns // tile,), in_specs=specs, out_specs...  68.9 us
    ppermute x39, starting transfers between devices, trade(): return lax.ppermute(block, axis, pairs)  46.5 us
    pallas_call x5, Pallas kernels, in_product(): pl.pallas_call(in_kernel, grid=(columns // tile,), in_specs=[pl.BlockSpec...  38.8 us
    pallas_call x4, Pallas kernels, cot_product(): pl.pallas_call(cot_kernel, grid=(columns // tile,), in_specs=[whole, whol...  33.4 us
    all_to_all x5, waiting for transfers between devices, swap(): lax.all_to_all(packed, 'gx', split_axis=0, concat_axis=0, tiled=True)  25.5 us
    unnamed x79, local copies, waits for them, and re-layouts  25.1 us
    all_to_all x5, starting transfers between devices, swap(): lax.all_to_all(packed, 'gx', split_axis=0, concat_axis=0, tiled=True)  21.7 us
  transfers between devices with their start and end apart: 44, of which 13 were waited for; matrix products, arithmetic and copies ran while one was open for 3% of the time, Pallas kernels for 31%

profile of v8, /device:TPU:0, one launch (start us, length us, event | category | flops | bytes accessed | tf_op | source)
XLA Modules:
  0.0 544.7 jit_solution(14435605558936041215)
XLA Ops:
  0.6 3.0 collective-permute-start.8
  4.8 4.9 all-reduce.1
  14.4 5.3 pack.5
  22.4 8.2 %cot_product.4 = bf16[256,1920]{1,0:T(8,128)(2,1)S(1)} custom-call(bf16[2,64,3072]{2,1,0:T(8,128)(2,1)S(1)} %pad_maximum_fusion.1.own_ref, bf16[2,64,3072]{2,1,0:T(8,128)(2,1)S(1)} %collective-permute-done.10.other_ref, bf16[384,3072]{1,0:T(8,128)(2,1)S(1)} %copy-done.1, bf16[1536,3072]{1,0:T(8,128)(2,1)} %refs_2_.11), custom_call_target="tpu_custom_call" | custom-call | flops 47185920 | bytes 199680 | tf_op jit(solution)/shard_map/cot_product/pallas_call | solution.py:214
  30.5 5.4 all-to-all-start
  36.0 2.9 collective-permute-start.9
  42.0 32.2 %collective-permute-done.9.own_ref = bf16[2,64,3072]{2,1,0:T(8,128)(2,1)} collective-permute-done((bf16[2,64,3072]{2,1,0:T(8,128)(2,1)}, bf16[2,64,3072]{2,1,0:T(8,128)(2,1)}, u32[]{:S(2)}, u32[]{:S(2)}) %collective-permute-start.9) | collective-permute-done | bytes 786464 | tf_op jit(solution)/shard_map/ppermute | solution.py:121
  80.3 8.3 %cot_product.5 = bf16[256,1920]{1,0:T(8,128)(2,1)S(1)} custom-call(bf16[2,64,3072]{2,1,0:T(8,128)(2,1)} %collective-permute-done.9.own_ref, bf16[2,64,3072]{2,1,0:T(8,128)(2,1)S(1)} %collective-permute-done.12.other_ref, bf16[384,3072]{1,0:T(8,128)(2,1)S(1)} %copy-done.1, bf16[1536,3072]{1,0:T(8,128)(2,1)} %refs_2_.11), custom_call_target="tpu_custom_call" | custom-call | flops 47185920 | bytes 199680 | tf_op jit(solution)/shard_map/cot_product/pallas_call | solution.py:214
  89.6 25.5 %all-to-all-done = bf16[4,768,1152]{2,1,0:T(8,128)(2,1)} async-done(((bf16[4,768,1152]{2,1,0:T(8,128)(2,1)}), bf16[4,768,1152]{2,1,0:T(8,128)(2,1)}, u32[]{:S(2)}, u32[]{:S(2)}) %all-to-all-start) | async-done | bytes 7077920 | tf_op jit(solution)/shard_map/all_to_all | solution.py:355
  115.1 4.4 all-to-all-start.1
  119.5 8.6 %cot_product.6 = bf16[256,1920]{1,0:T(8,128)(2,1)S(1)} custom-call(bf16[2,64,3072]{2,1,0:T(8,128)(2,1)} %collective-permute-done.16.own_ref, bf16[2,64,3072]{2,1,0:T(8,128)(2,1)} %collective-permute-done.17.other_ref, bf16[384,3072]{1,0:T(8,128)(2,1)S(1)} %copy-done.1, bf16[1536,3072]{1,0:T(8,128)(2,1)} %refs_2_.11), custom_call_target="tpu_custom_call" | custom-call | flops 47185920 | bytes 199680 | tf_op jit(solution)/shard_map/cot_product/pallas_call | solution.py:214
  132.7 4.5 pack.7
  138.8 13.5 %collective-permute-done.18 = bf16[256,1920]{1,0:T(8,128)(2,1)S(1)} collective-permute-done((bf16[256,1920]{1,0:T(8,128)(2,1)S(1)}, bf16[256,1920]{1,0:T(8,128)(2,1)S(1)}, u32[]{:S(2)}, u32[]{:S(2)}) %collective-permute-start.18) | collective-permute-done | bytes 983072 | tf_op jit(solution)/shard_map/ppermute | solution.py:121
  153.2 8.3 %cot_product.7 = bf16[256,1920]{1,0:T(8,128)(2,1)S(1)} custom-call(bf16[2,64,3072]{2,1,0:T(8,128)(2,1)} %collective-permute-done.15.own_ref, bf16[2,64,3072]{2,1,0:T(8,128)(2,1)S(1)} %collective-permute-done.19.other_ref, bf16[384,3072]{1,0:T(8,128)(2,1)S(1)} %copy-done.1, bf16[1536,3072]{1,0:T(8,128)(2,1)} %refs_2_.11), custom_call_target="tpu_custom_call" | custom-call | flops 47185920 | bytes 199680 | tf_op jit(solution)/shard_map/cot_product/pallas_call | solution.py:214
  162.5 3.7 all-to-all-start.2
  170.6 16.3 %collective-permute-done.2.refs_2_ = bf16[2,64,3072]{2,1,0:T(8,128)(2,1)S(1)} collective-permute-done((bf16[2,64,3072]{2,1,0:T(8,128)(2,1)}, bf16[2,64,3072]{2,1,0:T(8,128)(2,1)S(1)}, u32[]{:S(2)}, u32[]{:S(2)}) %collective-permute-start.2) | collective-permute-done | bytes 786464 | tf_op jit(solution)/shard_map/ppermute | solution.py:121
  186.9 16.4 %collective-permute-done.6.refs_6_ = bf16[2,64,3072]{2,1,0:T(8,128)(2,1)S(1)} collective-permute-done((bf16[2,64,3072]{2,1,0:T(8,128)(2,1)}, bf16[2,64,3072]{2,1,0:T(8,128)(2,1)S(1)}, u32[]{:S(2)}, u32[]{:S(2)}) %collective-permute-start.6) | collective-permute-done | bytes 786464 | tf_op jit(solution)/shard_map/ppermute | solution.py:121
  203.3 4.5 pack.6
  210.4 5.0 assemble.1.rows_ref
  216.3 14.0 %in_product.5.q_own.k_own.v_own = bf16[1024,1152]{1,0:T(8,128)(2,1)S(1)} custom-call(bf16[1024,3072]{1,0:T(8,128)(2,1)} %assemble.1.rows_ref, bf16[3072,1152]{1,0:T(8,128)(2,1)} %bitcast.4.weight_ref.refs_5_), custom_call_target="tpu_custom_call" | custom-call | flops 113246208 | bytes 245760 | tf_op jit(solution)/shard_map/in_product/pallas_call | solution.py:266
  233.4 3.7 all-to-all-start.3
  242.6 69.6 %collective-permute-done.20 = bf16[256,1920]{1,0:T(8,128)(2,1)} collective-permute-done((bf16[256,1920]{1,0:T(8,128)(2,1)}, bf16[256,1920]{1,0:T(8,128)(2,1)}, u32[]{:S(2)}, u32[]{:S(2)}) %collective-permute-start.20) | collective-permute-done | bytes 983072 | tf_op jit(solution)/shard_map/ppermute | solution.py:121
  312.2 5.0 in_product.7
  318.0 4.5 all-to-all-start.4
  324.4 7.3 %in_product.8 = bf16[1024,512]{1,0:T(8,128)(2,1)} custom-call(bf16[1024,3072]{1,0:T(8,128)(2,1)} %assemble.1.rows_ref, bf16[3072,512]{1,0:T(8,128)(2,1)S(1)} %bitcast.92), custom_call_target="tpu_custom_call" | custom-call | flops 50331648 | bytes 163840 | tf_op jit(solution)/shard_map/in_product/pallas_call | solution.py:266
  333.9 7.3 %in_product.6 = bf16[1024,512]{1,0:T(8,128)(2,1)} custom-call(bf16[1024,3072]{1,0:T(8,128)(2,1)} %assemble.1.rows_ref, bf16[3072,512]{1,0:T(8,128)(2,1)S(1)} %bitcast.81), custom_call_target="tpu_custom_call" | custom-call | flops 50331648 | bytes 163840 | tf_op jit(solution)/shard_map/in_product/pallas_call | solution.py:266
  343.0 4.6 add_parts.1
  347.6 21.7 %collective-permute-done.21 = bf16[1024,256]{1,0:T(8,128)(2,1)S(1)} collective-permute-done((bf16[1024,256]{1,0:T(8,128)(2,1)S(1)}, bf16[1024,256]{1,0:T(8,128)(2,1)S(1)}, u32[]{:S(2)}, u32[]{:S(2)}) %collective-permute-start.21) | collective-permute-done | bytes 524320 | tf_op jit(solution)/shard_map/ppermute | solution.py:121
  373.1 15.3 %attend.1 = (bf16[1024,384]{1,0:T(8,128)(2,1)S(1)}, bf16[1024,384]{1,0:T(8,128)(2,1)S(1)}, bf16[1024,384]{1,0:T(8,128)(2,1)S(1)}, bf16[1024,384]{1,0:T(8,128)(2,1)S(1)}) custom-call(bf16[1024,1152]{1,0:T(8,128)(2,1)S(1)} %copy-done.4, bf16[1024,1152]{1,0:T(8,128)(2,1)} %collective-permute-done.14.q_got.k_got.v_got, bf16[1024,1152]{1,0:T(8,128)(2,1)S(1)} %copy-done.4, ...), custom_call_target="tpu_custom_call" | custom-call | flops 12582912 | bytes 98304 | tf_op jit(solution)/shard_map/attend/pallas_call | solution.py:75
  389.3 5.2 in_product.9
  398.9 12.3 %out_product.6.refs_3_ = bf16[1024,3072]{1,0:T(8,128)(2,1)} custom-call(bf16[1024,384]{1,0:T(8,128)(2,1)S(1)} %copy-done.31, bf16[1024,256]{1,0:T(8,128)(2,1)S(1)} %get-tuple-element.57.refs_1_, bf16[1024,512]{1,0:T(8,128)(2,1)S(1)} %get-tuple-element.51.refs_2_, bf16[384,3072]{1,0:T(8,128)(2,1)S(1)} %copy-done.2, bf16[1536,3072]{1,0:T(8,128)(2,1)} %refs_2_.11), custom_call_target="tpu_custom_call" | custom-call | flops 113246208 | bytes 282624 | tf_op jit(solution)/shard_map/out_product/pallas_call | solution.py:317
  411.2 18.4 %back_product.5.refs_4_ = bf16[1024,3072]{1,0:T(8,128)(2,1)} custom-call(bf16[1024,384]{1,0:T(8,128)(2,1)S(1)} %get-tuple-element.31.refs_0_, bf16[1024,384]{1,0:T(8,128)(2,1)S(1)} %get-tuple-element.32.refs_1_, bf16[1024,384]{1,0:T(8,128)(2,1)S(1)} %get-tuple-element.33.refs_2_, bf16[1024,256]{1,0:T(8,128)(2,1)S(1)} %get-tuple-element.56.refs_3_, ...), custom_call_target="tpu_custom_call" | custom-call | flops 188743680 | bytes 282624 | tf_op jit(solution)/shard_map/back_product/pallas_call | solution.py:317
  432.8 6.5 %out_product.7 = bf16[512,3072]{1,0:T(8,128)(2,1)S(1)} custom-call(bf16[1024,512]{1,0:T(8,128)(2,1)S(1)} %get-tuple-element.49.refs_0_, bf16[1024,256]{1,0:T(8,128)(2,1)S(1)} %get-tuple-element.55.refs_1_, bf16[1536,3072]{1,0:T(8,128)(2,1)} %refs_2_.11, bf16[1024,3072]{1,0:T(8,128)(2,1)} %out_product.6.refs_3_), custom_call_target="tpu_custom_call" | custom-call | flops 37748736 | bytes 196608 | tf_op jit(solution)/shard_map/out_product/pallas_call | solution.py:317
  439.4 7.7 %back_product.6 = bf16[512,3072]{1,0:T(8,128)(2,1)} custom-call(bf16[1024,512]{1,0:T(8,128)(2,1)S(1)} %get-tuple-element.48.refs_0_, bf16[1024,256]{1,0:T(8,128)(2,1)S(1)} %get-tuple-element.54.refs_1_, bf16[3072,512]{1,0:T(8,128)(2,1)} %bitcast.82, bf16[3072,256]{1,0:T(8,128)(2,1)} %bitcast.17.weight_ref.refs_3_, bf16[1024,3072]{1,0:T(8,128)(2,1)} %back_product.5.refs_4_), custom_call_target="tpu_custom_call" | custom-call | flops 37748736 | bytes 122880 | tf_op jit(solution)/shard_map/back_product/pallas_call | solution.py:317
  447.6 3.2 out_product.9
  452.7 3.2 out_product.11
  457.9 4.3 back_product.9
  464.0 3.4 back_product.8
  469.3 3.2 out_product.10
  472.5 3.2 out_product.8
  475.7 3.4 back_product.7
  480.0 8.2 %collective-permute-done.29 = bf16[256,1536]{1,0:T(8,128)(2,1)S(1)} collective-permute-done((bf16[256,1536]{1,0:T(8,128)(2,1)S(1)}, bf16[256,1536]{1,0:T(8,128)(2,1)S(1)}, u32[]{:S(2)}, u32[]{:S(2)}) %collective-permute-start.29) | collective-permute-done | bytes 786464 | tf_op jit(solution)/shard_map/ppermute | solution.py:121
  490.3 2.6 collective-permute-start.37
  493.0 11.2 %collective-permute-done.33 = bf16[256,1536]{1,0:T(8,128)(2,1)S(1)} collective-permute-done((bf16[256,1536]{1,0:T(8,128)(2,1)S(1)}, bf16[256,1536]{1,0:T(8,128)(2,1)S(1)}, u32[]{:S(2)}, u32[]{:S(2)}) %collective-permute-start.33) | collective-permute-done | bytes 786464 | tf_op jit(solution)/shard_map/ppermute | solution.py:121
  506.2 2.6 collective-permute-start.28
  511.3 12.1 %collective-permute-done.34 = bf16[2,64,1536]{2,1,0:T(8,128)(2,1)S(1)} collective-permute-done((bf16[2,64,1536]{2,1,0:T(8,128)(2,1)S(1)}, bf16[2,64,1536]{2,1,0:T(8,128)(2,1)S(1)}, u32[]{:S(2)}, u32[]{:S(2)}) %collective-permute-start.34) | collective-permute-done | bytes 393248 | tf_op jit(solution)/shard_map/ppermute | solution.py:121
  525.2 9.1 %collective-permute-done.35 = bf16[64,1536]{1,0:T(8,128)(2,1)S(1)} collective-permute-done((bf16[64,1536]{1,0:T(8,128)(2,1)S(1)}, bf16[64,1536]{1,0:T(8,128)(2,1)S(1)}, u32[]{:S(2)}, u32[]{:S(2)}) %collective-permute-start.35) | collective-permute-done | bytes 196640 | tf_op jit(solution)/shard_map/ppermute | solution.py:121
  535.3 5.6 %all-reduce = (f32[64]{0:T(128)S(1)}, f32[64]{0:T(128)}) all-reduce(f32[64]{0:T(128)S(1)} %fusion.28, f32[64]{0:T(128)} %reduce_sum.48), channel_id=1, replica_groups=mesh['gx'=4,'gy'=4,'gz'=2] {'gz'}, use_global_device_ids=true, to_apply=%region_8.9 | all-reduce | flops 128 | bytes 1024 | tf_op jit(solution)/shard_map/psum | solution.py:468
  (184 shorter events, 83.9 us)
Async XLA Ops:
  0.6 19.0 %collective-permute-start.8 = (bf16[64,3072]{1,0:T(8,128)(2,1)}, bf16[64,3072]{1,0:T(8,128)(2,1)S(1)}, u32[]{:S(2)}, u32[]{:S(2)}) collective-permute-start(bf16[64,3072]{1,0:T(8,128)(2,1)} %param.9), channel_id=1, source_target_pairs={{0,16},{8,24},{16,0},{24,8},{1,17},{9,25},{17,1},{25,9},{2,18},{10... | collective-permute-start | bytes 1179656 | tf_op jit(solution)/shard_map/ppermute | solution.py:121
  10.9 10.4 %collective-permute-start = (bf16[64,3072]{1,0:T(8,128)(2,1)S(1)}, bf16[64,3072]{1,0:T(8,128)(2,1)S(1)}, u32[]{:S(2)}, u32[]{:S(2)}) collective-permute-start(bf16[64,3072]{1,0:T(8,128)(2,1)S(1)} %fusion.27), channel_id=1, source_target_pairs={{0,16},{8,24},{16,0},{24,8},{1,17},{9,25},{17,1},{25,9},{2,18},{10... | collective-permute-start | bytes 1179656 | tf_op jit(solution)/shard_map/ppermute | solution.py:121
  19.8 2.6 collective-permute-start.10
  30.5 84.5 %all-to-all-start = ((bf16[4,768,1152]{2,1,0:T(8,128)(2,1)}), bf16[4,768,1152]{2,1,0:T(8,128)(2,1)}, u32[]{:S(2)}, u32[]{:S(2)}) async-start(bf16[4,768,1152]{2,1,0:T(8,128)(2,1)} %pack.5), calls=%async_computation | async-start | bytes 14155776 | tf_op jit(solution)/shard_map/all_to_all | solution.py:355
  36.0 38.3 %collective-permute-start.9 = (bf16[2,64,3072]{2,1,0:T(8,128)(2,1)}, bf16[2,64,3072]{2,1,0:T(8,128)(2,1)}, u32[]{:S(2)}, u32[]{:S(2)}) collective-permute-start(bf16[2,64,3072]{2,1,0:T(8,128)(2,1)} %copy-done.21), channel_id=1, source_target_pairs={{0,4},{2,6},{4,0},{6,2},{1,5},{3,7},{5,1},{7,3},{8,12},{10,14},{12... | collective-permute-start | bytes 2359304 | tf_op jit(solution)/shard_map/ppermute | solution.py:121
  38.9 35.5 %collective-permute-start.16 = (bf16[2,64,3072]{2,1,0:T(8,128)(2,1)}, bf16[2,64,3072]{2,1,0:T(8,128)(2,1)}, u32[]{:S(2)}, u32[]{:S(2)}) collective-permute-start(bf16[2,64,3072]{2,1,0:T(8,128)(2,1)} %copy-done.21), channel_id=1, source_target_pairs={{0,2},{2,0},{4,6},{6,4},{1,3},{3,1},{5,7},{7,5},{8,10},{10,8},{12,... | collective-permute-start | bytes 2359304 | tf_op jit(solution)/shard_map/ppermute | solution.py:121
  40.5 38.8 %collective-permute-start.11 = (bf16[256,1920]{1,0:T(8,128)(2,1)S(1)}, bf16[256,1920]{1,0:T(8,128)(2,1)S(1)}, u32[]{:S(2)}, u32[]{:S(2)}) collective-permute-start(bf16[256,1920]{1,0:T(8,128)(2,1)S(1)} %cot_product.4), channel_id=1, source_target_pairs={{0,1},{1,0},{2,3},{3,2},{4,5},{5,4},{6,7},{7,6},{8,9},{9,8},{10,11... | collective-permute-start | bytes 2949128 | tf_op jit(solution)/shard_map/ppermute | solution.py:121
  74.2 6.0 %collective-permute-start.12 = (bf16[2,64,3072]{2,1,0:T(8,128)(2,1)}, bf16[2,64,3072]{2,1,0:T(8,128)(2,1)S(1)}, u32[]{:S(2)}, u32[]{:S(2)}) collective-permute-start(bf16[2,64,3072]{2,1,0:T(8,128)(2,1)} %collective-permute-done.9.own_ref), channel_id=1, source_target_pairs={{0,8},{8,0},{16,24},{24,16},{1,9},{9,1},{17,25},{25,17},{2,10},{10... | collective-permute-start | bytes 2359304 | tf_op jit(solution)/shard_map/ppermute | solution.py:121
  74.4 45.0 %collective-permute-start.17 = (bf16[2,64,3072]{2,1,0:T(8,128)(2,1)}, bf16[2,64,3072]{2,1,0:T(8,128)(2,1)}, u32[]{:S(2)}, u32[]{:S(2)}) collective-permute-start(bf16[2,64,3072]{2,1,0:T(8,128)(2,1)} %collective-permute-done.16.own_ref), channel_id=1, source_target_pairs={{0,8},{8,0},{16,24},{24,16},{1,9},{9,1},{17,25},{25,17},{2,10},{10... | collective-permute-start | bytes 2359304 | tf_op jit(solution)/shard_map/ppermute | solution.py:121
  74.8 55.2 %collective-permute-start.15 = (bf16[2,64,3072]{2,1,0:T(8,128)(2,1)}, bf16[2,64,3072]{2,1,0:T(8,128)(2,1)}, u32[]{:S(2)}, u32[]{:S(2)}) collective-permute-start(bf16[2,64,3072]{2,1,0:T(8,128)(2,1)} %collective-permute-done.9.own_ref), channel_id=1, source_target_pairs={{0,2},{2,0},{4,6},{6,4},{1,3},{3,1},{5,7},{7,5},{8,10},{10,8},{12,... | collective-permute-start | bytes 2359304 | tf_op jit(solution)/shard_map/ppermute | solution.py:121
  115.1 47.4 %all-to-all-start.1 = ((bf16[4,768,256]{2,1,0:T(8,128)(2,1)}), bf16[4,768,256]{2,1,0:T(8,128)(2,1)}, u32[]{:S(2)}, u32[]{:S(2)}) async-start(bf16[4,768,256]{2,1,0:T(8,128)(2,1)} %copy-done.12), calls=%async_computation.1 | async-start | bytes 3145728 | tf_op jit(solution)/shard_map/all_to_all | solution.py:355
  128.1 24.2 %collective-permute-start.18 = (bf16[256,1920]{1,0:T(8,128)(2,1)S(1)}, bf16[256,1920]{1,0:T(8,128)(2,1)S(1)}, u32[]{:S(2)}, u32[]{:S(2)}) collective-permute-start(bf16[256,1920]{1,0:T(8,128)(2,1)S(1)} %cot_product.6), channel_id=1, source_target_pairs={{0,1},{1,0},{2,3},{3,2},{4,5},{5,4},{6,7},{7,6},{8,9},{9,8},{10,11... | collective-permute-start | bytes 2949128 | tf_op jit(solution)/shard_map/ppermute | solution.py:121
  129.9 23.3 %collective-permute-start.19 = (bf16[2,64,3072]{2,1,0:T(8,128)(2,1)}, bf16[2,64,3072]{2,1,0:T(8,128)(2,1)S(1)}, u32[]{:S(2)}, u32[]{:S(2)}) collective-permute-start(bf16[2,64,3072]{2,1,0:T(8,128)(2,1)} %collective-permute-done.15.own_ref), channel_id=1, source_target_pairs={{0,8},{8,0},{16,24},{24,16},{1,9},{9,1},{17,25},{25,17},{2,10},{10... | collective-permute-start | bytes 2359304 | tf_op jit(solution)/shard_map/ppermute | solution.py:121
  130.1 38.0 %collective-permute-start.4 = (bf16[2,64,3072]{2,1,0:T(8,128)(2,1)}, bf16[2,64,3072]{2,1,0:T(8,128)(2,1)}, u32[]{:S(2)}, u32[]{:S(2)}) collective-permute-start(bf16[2,64,3072]{2,1,0:T(8,128)(2,1)} %pad_maximum_fusion.refs_0_), channel_id=1, source_target_pairs={{0,4},{2,6},{4,0},{6,2},{1,5},{3,7},{5,1},{7,3},{8,12},{10,14},{12... | collective-permute-start | bytes 2359304 | tf_op jit(solution)/shard_map/ppermute | solution.py:121
  162.5 69.1 %all-to-all-start.2 = ((bf16[4,768,512]{2,1,0:T(8,128)(2,1)}), bf16[4,768,512]{2,1,0:T(8,128)(2,1)S(1)}, u32[]{:S(2)}, u32[]{:S(2)}) async-start(bf16[4,768,512]{2,1,0:T(8,128)(2,1)} %copy-done.9), calls=%async_computation.2 | async-start | bytes 6291456 | tf_op jit(solution)/shard_map/all_to_all | solution.py:355
  166.2 20.6 %collective-permute-start.2 = (bf16[2,64,3072]{2,1,0:T(8,128)(2,1)}, bf16[2,64,3072]{2,1,0:T(8,128)(2,1)S(1)}, u32[]{:S(2)}, u32[]{:S(2)}) collective-permute-start(bf16[2,64,3072]{2,1,0:T(8,128)(2,1)} %pad_maximum_fusion.refs_0_), channel_id=1, source_target_pairs={{0,2},{2,0},{4,6},{6,4},{1,3},{3,1},{5,7},{7,5},{8,10},{10,8},{12,... | collective-permute-start | bytes 2359304 | tf_op jit(solution)/shard_map/ppermute | solution.py:121
  168.1 35.2 %collective-permute-start.6 = (bf16[2,64,3072]{2,1,0:T(8,128)(2,1)}, bf16[2,64,3072]{2,1,0:T(8,128)(2,1)S(1)}, u32[]{:S(2)}, u32[]{:S(2)}) collective-permute-start(bf16[2,64,3072]{2,1,0:T(8,128)(2,1)} %collective-permute-done.4.refs_4_), channel_id=1, source_target_pairs={{0,2},{2,0},{4,6},{6,4},{1,3},{3,1},{5,7},{7,5},{8,10},{10,8},{12,... | collective-permute-start | bytes 2359304 | tf_op jit(solution)/shard_map/ppermute | solution.py:121
  168.6 46.7 %collective-permute-start.13 = (bf16[256,1920]{1,0:T(8,128)(2,1)}, bf16[256,1920]{1,0:T(8,128)(2,1)S(1)}, u32[]{:S(2)}, u32[]{:S(2)}) collective-permute-start(bf16[256,1920]{1,0:T(8,128)(2,1)} %copy-done.15), channel_id=1, source_target_pairs={{0,1},{1,0},{2,3},{3,2},{4,5},{5,4},{6,7},{7,6},{8,9},{9,8},{10,11... | collective-permute-start | bytes 2949128 | tf_op jit(solution)/shard_map/ppermute | solution.py:121
  170.1 39.3 %collective-permute-start.1 = (bf16[2,64,3072]{2,1,0:T(8,128)(2,1)}, bf16[2,64,3072]{2,1,0:T(8,128)(2,1)S(1)}, u32[]{:S(2)}, u32[]{:S(2)}) collective-permute-start(bf16[2,64,3072]{2,1,0:T(8,128)(2,1)} %pad_maximum_fusion.refs_0_), channel_id=1, source_target_pairs={{0,8},{8,0},{16,24},{24,16},{1,9},{9,1},{17,25},{25,17},{2,10},{10... | collective-permute-start | bytes 2359304 | tf_op jit(solution)/shard_map/ppermute | solution.py:121
  170.1 39.3 %collective-permute-start.5 = (bf16[2,64,3072]{2,1,0:T(8,128)(2,1)}, bf16[2,64,3072]{2,1,0:T(8,128)(2,1)S(1)}, u32[]{:S(2)}, u32[]{:S(2)}) collective-permute-start(bf16[2,64,3072]{2,1,0:T(8,128)(2,1)} %collective-permute-done.4.refs_4_), channel_id=1, source_target_pairs={{0,8},{8,0},{16,24},{24,16},{1,9},{9,1},{17,25},{25,17},{2,10},{10... | collective-permute-start | bytes 2359304 | tf_op jit(solution)/shard_map/ppermute | solution.py:121
  186.9 22.5 %collective-permute-start.3 = (bf16[2,64,3072]{2,1,0:T(8,128)(2,1)S(1)}, bf16[2,64,3072]{2,1,0:T(8,128)(2,1)S(1)}, u32[]{:S(2)}, u32[]{:S(2)}) collective-permute-start(bf16[2,64,3072]{2,1,0:T(8,128)(2,1)S(1)} %collective-permute-done.2.refs_2_), channel_id=1, source_target_pairs={{0,8},{8,0},{16,24},{24,16},{1,9},{9,1},{17,25},{25,17},{2,10},{10... | collective-permute-start | bytes 2359304 | tf_op jit(solution)/shard_map/ppermute | solution.py:121
  203.3 6.1 %collective-permute-start.7 = (bf16[2,64,3072]{2,1,0:T(8,128)(2,1)S(1)}, bf16[2,64,3072]{2,1,0:T(8,128)(2,1)S(1)}, u32[]{:S(2)}, u32[]{:S(2)}) collective-permute-start(bf16[2,64,3072]{2,1,0:T(8,128)(2,1)S(1)} %collective-permute-done.6.refs_6_), channel_id=1, source_target_pairs={{0,8},{8,0},{16,24},{24,16},{1,9},{9,1},{17,25},{25,17},{2,10},{10... | collective-permute-start | bytes 2359304 | tf_op jit(solution)/shard_map/ppermute | solution.py:121
  233.4 84.6 %all-to-all-start.3 = ((bf16[4,768,512]{2,1,0:T(8,128)(2,1)}), bf16[4,768,512]{2,1,0:T(8,128)(2,1)S(1)}, u32[]{:S(2)}, u32[]{:S(2)}) async-start(bf16[4,768,512]{2,1,0:T(8,128)(2,1)} %copy-done.10), calls=%async_computation.3 | async-start | bytes 6291456 | tf_op jit(solution)/shard_map/all_to_all | solution.py:355
  237.1 96.8 %collective-permute-start.14 = (bf16[1024,1152]{1,0:T(8,128)(2,1)}, bf16[1024,1152]{1,0:T(8,128)(2,1)}, u32[]{:S(2)}, u32[]{:S(2)}) collective-permute-start(bf16[1024,1152]{1,0:T(8,128)(2,1)} %copy-done.3), channel_id=1, source_target_pairs={{0,1},{1,0},{2,3},{3,2},{4,5},{5,4},{6,7},{7,6},{8,9},{9,8},{10,11... | collective-permute-start | bytes 7077896 | tf_op jit(solution)/shard_map/ppermute | solution.py:121
  238.9 73.3 %collective-permute-start.20 = (bf16[256,1920]{1,0:T(8,128)(2,1)}, bf16[256,1920]{1,0:T(8,128)(2,1)}, u32[]{:S(2)}, u32[]{:S(2)}) collective-permute-start(bf16[256,1920]{1,0:T(8,128)(2,1)} %copy-done.19), channel_id=1, source_target_pairs={{0,1},{1,0},{2,3},{3,2},{4,5},{5,4},{6,7},{7,6},{8,9},{9,8},{10,11... | collective-permute-start | bytes 2949128 | tf_op jit(solution)/shard_map/ppermute | solution.py:121
  318.0 15.9 %copy-start = (bf16[4,768,512]{2,1,0:T(8,128)(2,1)}, bf16[4,768,512]{2,1,0:T(8,128)(2,1)S(1)}, u32[]{:S(2)}) copy-start(bf16[4,768,512]{2,1,0:T(8,128)(2,1)S(1)} %all-to-all-done.3) | copy-start | bytes 9437188
  318.0 71.3 %all-to-all-start.4 = ((bf16[4,768,256]{2,1,0:T(8,128)(2,1)}), bf16[4,768,256]{2,1,0:T(8,128)(2,1)}, u32[]{:S(2)}, u32[]{:S(2)}) async-start(bf16[4,768,256]{2,1,0:T(8,128)(2,1)} %copy-done.11), calls=%async_computation.4 | async-start | bytes 3145728 | tf_op jit(solution)/shard_map/all_to_all | solution.py:355
  331.8 64.5 %collective-permute-start.22 = (bf16[1024,512]{1,0:T(8,128)(2,1)}, bf16[1024,512]{1,0:T(8,128)(2,1)}, u32[]{:S(2)}, u32[]{:S(2)}) collective-permute-start(bf16[1024,512]{1,0:T(8,128)(2,1)} %in_product.8), channel_id=1, source_target_pairs={{0,1},{1,0},{2,3},{3,2},{4,5},{5,4},{6,7},{7,6},{8,9},{9,8},{10,11... | collective-permute-start | bytes 3145736 | tf_op jit(solution)/shard_map/ppermute | solution.py:121
  333.6 35.7 %collective-permute-start.21 = (bf16[1024,256]{1,0:T(8,128)(2,1)S(1)}, bf16[1024,256]{1,0:T(8,128)(2,1)S(1)}, u32[]{:S(2)}, u32[]{:S(2)}) collective-permute-start(bf16[1024,256]{1,0:T(8,128)(2,1)S(1)} %copy-done.25), channel_id=1, source_target_pairs={{0,1},{1,0},{2,3},{3,2},{4,5},{5,4},{6,7},{7,6},{8,9},{9,8},{10,11... | collective-permute-start | bytes 1572872 | tf_op jit(solution)/shard_map/ppermute | solution.py:121
  341.2 88.4 %collective-permute-start.23 = (bf16[1024,512]{1,0:T(8,128)(2,1)}, bf16[1024,512]{1,0:T(8,128)(2,1)}, u32[]{:S(2)}, u32[]{:S(2)}) collective-permute-start(bf16[1024,512]{1,0:T(8,128)(2,1)} %in_product.6), channel_id=1, source_target_pairs={{0,1},{1,0},{2,3},{3,2},{4,5},{5,4},{6,7},{7,6},{8,9},{9,8},{10,11... | collective-permute-start | bytes 3145736 | tf_op jit(solution)/shard_map/ppermute | solution.py:121
  347.6 23.4 %copy-start.4 = (bf16[1024,1152]{1,0:T(8,128)(2,1)S(1)}, bf16[1024,1152]{1,0:T(8,128)(2,1)}, u32[]{:S(2)}) copy-start(bf16[1024,1152]{1,0:T(8,128)(2,1)} %copy-done.3) | copy-start | bytes 7077892
  394.5 37.6 %collective-permute-start.24 = (bf16[1024,256]{1,0:T(8,128)(2,1)S(1)}, bf16[1024,256]{1,0:T(8,128)(2,1)S(1)}, u32[]{:S(2)}, u32[]{:S(2)}) collective-permute-start(bf16[1024,256]{1,0:T(8,128)(2,1)S(1)} %in_product.9), channel_id=1, source_target_pairs={{0,1},{1,0},{2,3},{3,2},{4,5},{5,4},{6,7},{7,6},{8,9},{9,8},{10,11... | collective-permute-start | bytes 1572872 | tf_op jit(solution)/shard_map/ppermute | solution.py:121
  439.3 8.3 %collective-permute-start.25 = (bf16[512,3072]{1,0:T(8,128)(2,1)S(1)}, bf16[512,3072]{1,0:T(8,128)(2,1)S(1)}, u32[]{:S(2)}, u32[]{:S(2)}) collective-permute-start(bf16[512,3072]{1,0:T(8,128)(2,1)S(1)} %out_product.7), channel_id=1, source_target_pairs={{0,8},{8,0},{16,24},{24,16},{1,9},{9,1},{17,25},{25,17},{2,10},{10... | collective-permute-start | bytes 9437192 | tf_op jit(solution)/shard_map/ppermute | solution.py:121
  447.1 9.1 %collective-permute-start.32 = (bf16[512,3072]{1,0:T(8,128)(2,1)}, bf16[512,3072]{1,0:T(8,128)(2,1)S(1)}, u32[]{:S(2)}, u32[]{:S(2)}) collective-permute-start(bf16[512,3072]{1,0:T(8,128)(2,1)} %back_product.6), channel_id=1, source_target_pairs={{0,8},{8,0},{16,24},{24,16},{1,9},{9,1},{17,25},{25,17},{2,10},{10... | collective-permute-start | bytes 9437192 | tf_op jit(solution)/shard_map/ppermute | solution.py:121
  450.8 28.3 %collective-permute-start.26 = (bf16[256,1536]{1,0:T(8,128)(2,1)S(1)}, bf16[256,1536]{1,0:T(8,128)(2,1)S(1)}, u32[]{:S(2)}, u32[]{:S(2)}) collective-permute-start(bf16[256,1536]{1,0:T(8,128)(2,1)S(1)} %out_product.9), channel_id=1, source_target_pairs={{0,16},{8,24},{16,0},{24,8},{1,17},{9,25},{17,1},{25,9},{2,18},{10... | collective-permute-start | bytes 2359304 | tf_op jit(solution)/shard_map/ppermute | solution.py:121
  455.9 32.2 %collective-permute-start.29 = (bf16[256,1536]{1,0:T(8,128)(2,1)S(1)}, bf16[256,1536]{1,0:T(8,128)(2,1)S(1)}, u32[]{:S(2)}, u32[]{:S(2)}) collective-permute-start(bf16[256,1536]{1,0:T(8,128)(2,1)S(1)} %out_product.11), channel_id=1, source_target_pairs={{0,16},{8,24},{16,0},{24,8},{1,17},{9,25},{17,1},{25,9},{2,18},{10... | collective-permute-start | bytes 2359304 | tf_op jit(solution)/shard_map/ppermute | solution.py:121
  462.3 27.7 %collective-permute-start.36 = (bf16[2,2,64,1536]{3,2,0,1:T(8,128)(2,1)S(1)}, bf16[2,2,64,1536]{3,2,0,1:T(8,128)(2,1)S(1)}, u32[]{:S(2)}, u32[]{:S(2)}) collective-permute-start(bf16[2,2,64,1536]{3,2,0,1:T(8,128)(2,1)S(1)} %bitcast.108), channel_id=1, source_target_pairs={{0,2},{2,0},{4,6},{6,4},{1,3},{3,1},{5,7},{7,5},{8,10},{10,8},{12,... | collective-permute-start | bytes 2359304 | tf_op jit(solution)/shard_map/ppermute | solution.py:121
  467.4 36.8 %collective-permute-start.33 = (bf16[256,1536]{1,0:T(8,128)(2,1)S(1)}, bf16[256,1536]{1,0:T(8,128)(2,1)S(1)}, u32[]{:S(2)}, u32[]{:S(2)}) collective-permute-start(bf16[256,1536]{1,0:T(8,128)(2,1)S(1)} %back_product.8), channel_id=1, source_target_pairs={{0,16},{8,24},{16,0},{24,8},{1,17},{9,25},{17,1},{25,9},{2,18},{10... | collective-permute-start | bytes 2359304 | tf_op jit(solution)/shard_map/ppermute | solution.py:121
  479.5 26.6 %collective-permute-start.27 = (bf16[2,64,1536]{2,1,0:T(8,128)(2,1)S(1)}, bf16[2,64,1536]{2,1,0:T(8,128)(2,1)S(1)}, u32[]{:S(2)}, u32[]{:S(2)}) collective-permute-start(bf16[2,64,1536]{2,1,0:T(8,128)(2,1)S(1)} %fusion.40), channel_id=1, source_target_pairs={{0,2},{2,0},{4,6},{6,4},{1,3},{3,1},{5,7},{7,5},{8,10},{10,8},{12,... | collective-permute-start | bytes 1179656 | tf_op jit(solution)/shard_map/ppermute | solution.py:121
  488.4 20.4 %collective-permute-start.30 = (bf16[2,64,1536]{2,1,0:T(8,128)(2,1)S(1)}, bf16[2,64,1536]{2,1,0:T(8,128)(2,1)S(1)}, u32[]{:S(2)}, u32[]{:S(2)}) collective-permute-start(bf16[2,64,1536]{2,1,0:T(8,128)(2,1)S(1)} %fusion.41), channel_id=1, source_target_pairs={{0,2},{2,0},{4,6},{6,4},{1,3},{3,1},{5,7},{7,5},{8,10},{10,8},{12,... | collective-permute-start | bytes 1179656 | tf_op jit(solution)/shard_map/ppermute | solution.py:121
  490.3 19.0 %collective-permute-start.37 = (bf16[2,64,1536]{2,1,0:T(8,128)(2,1)S(1)}, bf16[2,64,1536]{2,1,0:T(8,128)(2,1)S(1)}, u32[]{:S(2)}, u32[]{:S(2)}) collective-permute-start(bf16[2,64,1536]{2,1,0:T(8,128)(2,1)S(1)} %fusion.39), channel_id=1, source_target_pairs={{0,4},{2,6},{4,0},{6,2},{1,5},{3,7},{5,1},{7,3},{8,12},{10,14},{12... | collective-permute-start | bytes 1179656 | tf_op jit(solution)/shard_map/ppermute | solution.py:121
  504.4 18.9 %collective-permute-start.34 = (bf16[2,64,1536]{2,1,0:T(8,128)(2,1)S(1)}, bf16[2,64,1536]{2,1,0:T(8,128)(2,1)S(1)}, u32[]{:S(2)}, u32[]{:S(2)}) collective-permute-start(bf16[2,64,1536]{2,1,0:T(8,128)(2,1)S(1)} %fusion.42), channel_id=1, source_target_pairs={{0,2},{2,0},{4,6},{6,4},{1,3},{3,1},{5,7},{7,5},{8,10},{10,8},{12,... | collective-permute-start | bytes 1179656 | tf_op jit(solution)/shard_map/ppermute | solution.py:121
  506.2 34.6 %collective-permute-start.28 = (bf16[64,1536]{1,0:T(8,128)(2,1)S(1)}, bf16[64,1536]{1,0:T(8,128)(2,1)}, u32[]{:S(2)}, u32[]{:S(2)}) collective-permute-start(bf16[64,1536]{1,0:T(8,128)(2,1)S(1)} %fusion.47), channel_id=1, source_target_pairs={{0,4},{2,6},{4,0},{6,2},{1,5},{3,7},{5,1},{7,3},{8,12},{10,14},{12... | collective-permute-start | bytes 589832 | tf_op jit(solution)/shard_map/ppermute | solution.py:121
  509.0 33.5 %collective-permute-start.31 = (bf16[64,1536]{1,0:T(8,128)(2,1)S(1)}, bf16[64,1536]{1,0:T(8,128)(2,1)}, u32[]{:S(2)}, u32[]{:S(2)}) collective-permute-start(bf16[64,1536]{1,0:T(8,128)(2,1)S(1)} %fusion.48), channel_id=1, source_target_pairs={{0,4},{2,6},{4,0},{6,2},{1,5},{3,7},{5,1},{7,3},{8,12},{10,14},{12... | collective-permute-start | bytes 589832 | tf_op jit(solution)/shard_map/ppermute | solution.py:121
  509.5 25.5 %copy-start.34 = (bf16[64,3072]{1,0:T(8,128)(2,1)S(1)}, bf16[64,3072]{1,0:T(8,128)(2,1)}, u32[]{:S(2)}) copy-start(bf16[64,3072]{1,0:T(8,128)(2,1)} %param.8) | copy-start | bytes 1179652
  509.5 15.6 %collective-permute-start.38 = (bf16[64,1536]{1,0:T(8,128)(2,1)S(1)}, bf16[64,1536]{1,0:T(8,128)(2,1)S(1)}, u32[]{:S(2)}, u32[]{:S(2)}) collective-permute-start(bf16[64,1536]{1,0:T(8,128)(2,1)S(1)} %fusion.50), channel_id=1, source_target_pairs={{0,16},{8,24},{16,0},{24,8},{1,17},{9,25},{17,1},{25,9},{2,18},{10... | collective-permute-start | bytes 589832 | tf_op jit(solution)/shard_map/ppermute | solution.py:121
  523.5 10.8 %collective-permute-start.35 = (bf16[64,1536]{1,0:T(8,128)(2,1)S(1)}, bf16[64,1536]{1,0:T(8,128)(2,1)S(1)}, u32[]{:S(2)}, u32[]{:S(2)}) collective-permute-start(bf16[64,1536]{1,0:T(8,128)(2,1)S(1)} %fusion.49), channel_id=1, source_target_pairs={{0,4},{2,6},{4,0},{6,2},{1,5},{3,7},{5,1},{7,3},{8,12},{10,14},{12... | collective-permute-start | bytes 589832 | tf_op jit(solution)/shard_map/ppermute | solution.py:121
  525.2 18.2 %copy-start.36 = (bf16[64,3072]{1,0:T(8,128)(2,1)S(1)}, bf16[64,3072]{1,0:T(8,128)(2,1)}, u32[]{:S(2)}) copy-start(bf16[64,3072]{1,0:T(8,128)(2,1)} %param.9) | copy-start | bytes 1179652
  (35 other events, 152.3 us)

commit v9 on v8

--- a/solution.py
+++ b/solution.py
@@ -160,31 +160,25 @@
 IMAGE_ORDER = ((1, 1), (0, 1), (1, 0), (0, 0))
 
 
-def assemble_kernel(*refs):
-    parts, out_ref = refs[:-1], refs[-1]
-    rows = parts[0].shape[1]
-    start = 0
-    for x_bit, core_bit in IMAGE_ORDER:
-        for part in range(len(parts) // 2):
-            out_ref[start : start + rows, :] = parts[2 * part + core_bit][x_bit]
-            start += rows
-
-
-def assemble(parts):
-    flat = [value for part in parts for value in part]
-    _, rows, features = flat[0].shape
-    tile = 768
-    out = jax.ShapeDtypeStruct((len(flat) * 2 * rows, features), flat[0].dtype)
-    return pl.pallas_call(
-        assemble_kernel,
-        grid=(features // tile,),
-        in_specs=[pl.BlockSpec((2, rows, tile), lambda n: (0, 0, n))] * len(flat),
-        out_specs=pl.BlockSpec((out.shape[0], tile), lambda n: (0, n)),
-        out_shape=out,
-        compiler_params=params(),
-        cost_estimate=cost(0, out, out),
-        name="assemble",
-    )(*flat)
+def copy_kernel(index_ref, value_ref, out_ref):
+    out_ref[...] = value_ref[...]
+
+
+def pick_rows(value, index):
+    block = (value.shape[0] // index.shape[0], value.shape[1])
+    return pl.pallas_call(
+        copy_kernel,
+        grid_spec=pltpu.PrefetchScalarGridSpec(
+            num_scalar_prefetch=1,
+            grid=index.shape,
+            in_specs=[pl.BlockSpec(block, lambda i, index: (index[i], 0))],
+            out_specs=pl.BlockSpec(block, lambda i, index: (i, 0)),
+        ),
+        out_shape=jax.ShapeDtypeStruct(value.shape, value.dtype),
+        compiler_params=params(),
+        cost_estimate=cost(0, value, value),
+        name="pick_rows",
+    )(index, value)
 
 
 def cot_kernel(own_ref, other_ref, attn_ref, mlp_ref, out_ref, rows_ref):
@@ -369,7 +363,11 @@
     spread = squares / D - center * center
     inverse = lax.rsqrt(spread + EPSILON)
     normed = (wide - center[:, None]) * inverse[:, None]
-    normed_pair = with_x(half(normed))
+    gathered = lax.all_gather(half(normed), ("gx", "gy"), axis=0, tiled=True)
+    n_gy = lax.axis_size("gy")
+    image_of = lax.axis_index("gx") ^ jnp.array([2 * x + core for x, core in IMAGE_ORDER])
+    block_of = image_of[:, None] * n_gy + (lax.axis_index("gy") ^ jnp.arange(n_gy))[None, :]
+    all_in = pick_rows(gathered, block_of.reshape(-1).astype(jnp.int32))
 
     cot_owns, cot_gots = [], []
     for place, (own, other) in enumerate(gather_parts(cot_pair)):
@@ -377,23 +375,22 @@
             own = after(own, cot_gots[place - 2])
         cot_owns.append(cot_product((own, other), w_attn_out, w_mlp_out))
         cot_gots.append(others(cot_owns[-1]))
-    all_in = assemble(gather_parts(normed_pair))
-
-    in_heads = swap(after(packed_heads, normed_pair, cot_owns[0]))
-    in_mlp = [swap(after(packed_mlp[0], in_heads, cot_owns[2]))]
-    in_mlp.append(swap(after(packed_mlp[1], in_mlp[0], cot_owns[3])))
-    heads_own = in_product(after(all_in, cot_gots[2]), in_heads)
+
+    in_heads = swap(after(packed_heads, cot_owns[0]))
+    in_mlp = [swap(after(packed_mlp[0], in_heads, cot_owns[1]))]
+    in_mlp.append(swap(after(packed_mlp[1], in_mlp[0], cot_owns[2], cot_owns[3])))
+    heads_own = in_product(after(all_in, cot_gots[1]), in_heads)
     heads_got = others(heads_own)
-    mlp_own = [in_product(after(all_in, cot_gots[3], heads_own), in_mlp[0])]
+    mlp_own = [in_product(after(all_in, cot_gots[2], heads_own), in_mlp[0])]
     mlp_got = [others(mlp_own[0])]
     in_mlp.append(swap(after(packed_mlp[2], in_mlp[1], heads_own)))
-    mlp_own.append(in_product(after(all_in, mlp_own[0]), in_mlp[1]))
+    mlp_own.append(in_product(after(all_in, cot_gots[3], mlp_own[0]), in_mlp[1]))
     mlp_got.append(others(mlp_own[1]))
     in_mlp.append(swap(after(packed_mlp[3], in_mlp[2], mlp_own[0])))
     mlp_own.append(in_product(after(all_in, heads_got), in_mlp[2]))
     mlp_got.append(others(mlp_own[2]))
 
-    out_grad = add_parts(cot_owns, cot_gots)
+    out_grad = add_parts(after(cot_owns, mlp_own[1]), cot_gots)
     mixed, *head_grads = attend(heads_own, heads_got, out_grad)
     mlp_own.append(in_product(after(all_in, mlp_got[0], mixed), in_mlp[3]))
     mlp_got.append(others(mlp_own[3]))

time: 547 us -> 576 us (1.053)
  waiting for transfers between devices: 237 us -> 253 us
  between operations: 1.39 us -> 14.7 us
  starting transfers between devices: 68.2 us -> 61 us
  Pallas kernels: 185 us -> 191 us
    ppermute x39 -> x31, waiting for transfers between devices: 212 us -> 230 us  [trade(): return lax.ppermute(block, axis, pairs)]
    ppermute x39 -> x31, starting transfers between devices: 46.5 us -> 38.8 us  [trade(): return lax.ppermute(block, axis, pairs)]
    pallas_call x1, Pallas kernels: 4.99 us -> 11.5 us  [pick_rows(): pl.pallas_call(copy_kernel, grid_spec=pltpu.PrefetchScalarGridSpec(num_sc...]
    unnamed x79 -> x73, local copies, waits for them, and re-layouts: 25.1 us -> 23.8 us
  transfers between devices with their start and end apart: 44 -> 37, of which waited for: 13 -> 13; matrix products, arithmetic and copies ran while one was open for 3% -> 2% of each run, Pallas kernels for 31% -> 32%
where the time goes in v9:
time: 576 us; the launch traced here: 573 us
  waiting for transfers between devices  253 us (44%)
  Pallas kernels  191 us (33%)
  starting transfers between devices  61 us (11%)
  local copies, waits for them, and re-layouts  24.2 us (4%)
  other arithmetic  18 us (3%)
  between operations  14.7 us (3%)
  blocking collectives  11.3 us (2%)
    ppermute x31, waiting for transfers between devices, trade(): return lax.ppermute(block, axis, pairs)  230 us
    pallas_call x11, Pallas kernels, product(): pl.pallas_call(kernel, grid=(columns // tile,), in_specs=specs, out_specs...  69 us
    ppermute x31, starting transfers between devices, trade(): return lax.ppermute(block, axis, pairs)  38.8 us
    pallas_call x5, Pallas kernels, in_product(): pl.pallas_call(in_kernel, grid=(columns // tile,), in_specs=[pl.BlockSpec...  38.8 us
    pallas_call x4, Pallas kernels, cot_product(): pl.pallas_call(cot_kernel, grid=(columns // tile,), in_specs=[whole, whol...  33.3 us
    unnamed x73, local copies, waits for them, and re-layouts  23.8 us
    all_to_all x5, waiting for transfers between devices, swap(): lax.all_to_all(packed, 'gx', split_axis=0, concat_axis=0, tiled=True)  22.4 us
    all_to_all x5, starting transfers between devices, swap(): lax.all_to_all(packed, 'gx', split_axis=0, concat_axis=0, tiled=True)  22.1 us
  transfers between devices with their start and end apart: 37, of which 13 were waited for; matrix products, arithmetic and copies ran while one was open for 2% of the time, Pallas kernels for 32%

profile of v9, /device:TPU:0, one launch (start us, length us, event | category | flops | bytes accessed | tf_op | source)
XLA Modules:
  0.0 573.1 jit_solution(14384044650651242296)
XLA Ops:
  8.4 5.9 %all-reduce.1 = (f32[64]{0:T(128)S(1)}, f32[64]{0:T(128)S(1)}) all-reduce(f32[64]{0:T(128)S(1)} %get-tuple-element.47, f32[64]{0:T(128)S(1)} %get-tuple-element.46), channel_id=1, replica_groups=mesh['gx'=4,'gy'=4,'gz'=2] {'gz'}, use_global_device_ids=true, to_apply=%region_3.0 | all-reduce | flops 128 | bytes 1024 | tf_op jit(solution)/shard_map/psum | solution.py:361
  18.3 8.2 %collective-permute-done = bf16[64,3072]{1,0:T(8,128)(2,1)S(1)} collective-permute-done((bf16[64,3072]{1,0:T(8,128)(2,1)}, bf16[64,3072]{1,0:T(8,128)(2,1)S(1)}, u32[]{:S(2)}, u32[]{:S(2)}) %collective-permute-start) | collective-permute-done | bytes 393248 | tf_op jit(solution)/shard_map/ppermute | solution.py:121
  31.4 5.2 pack.5
  36.6 8.2 %cot_product.5 = bf16[256,1920]{1,0:T(8,128)(2,1)S(1)} custom-call(bf16[2,64,3072]{2,1,0:T(8,128)(2,1)S(1)} %pad_maximum_fusion.own_ref, bf16[2,64,3072]{2,1,0:T(8,128)(2,1)S(1)} %collective-permute-done.4.other_ref, bf16[384,3072]{1,0:T(8,128)(2,1)S(1)} %copy-done.1, bf16[1536,3072]{1,0:T(8,128)(2,1)} %refs_2_.11), custom_call_target="tpu_custom_call" | custom-call | flops 47185920 | bytes 199680 | tf_op jit(solution)/shard_map/cot_product/pallas_call | solution.py:208
  44.8 5.8 %all-to-all-start = ((bf16[4,768,1152]{2,1,0:T(8,128)(2,1)}), bf16[4,768,1152]{2,1,0:T(8,128)(2,1)}, u32[]{:S(2)}, u32[]{:S(2)}) async-start(bf16[4,768,1152]{2,1,0:T(8,128)(2,1)} %pack.5), calls=%async_computation | async-start | bytes 14155776 | tf_op jit(solution)/shard_map/all_to_all | solution.py:349
  52.4 2.8 collective-permute-start.6
  55.2 53.5 %collective-permute-done.1.own_ref = bf16[2,64,3072]{2,1,0:T(8,128)(2,1)S(1)} collective-permute-done((bf16[2,64,3072]{2,1,0:T(8,128)(2,1)}, bf16[2,64,3072]{2,1,0:T(8,128)(2,1)S(1)}, u32[]{:S(2)}, u32[]{:S(2)}) %collective-permute-start.1) | collective-permute-done | bytes 786464 | tf_op jit(solution)/shard_map/ppermute | solution.py:121
  114.6 8.1 %cot_product.4 = bf16[256,1920]{1,0:T(8,128)(2,1)S(1)} custom-call(bf16[2,64,3072]{2,1,0:T(8,128)(2,1)S(1)} %collective-permute-done.1.own_ref, bf16[2,64,3072]{2,1,0:T(8,128)(2,1)S(1)} %collective-permute-done.2.other_ref, bf16[384,3072]{1,0:T(8,128)(2,1)S(1)} %copy-done.1, bf16[1536,3072]{1,0:T(8,128)(2,1)} %refs_2_.11), custom_call_target="tpu_custom_call" | custom-call | flops 47185920 | bytes 199680 | tf_op jit(solution)/shard_map/cot_product/pallas_call | solution.py:208
  123.8 18.8 %all-to-all-done = bf16[4,768,1152]{2,1,0:T(8,128)(2,1)} async-done(((bf16[4,768,1152]{2,1,0:T(8,128)(2,1)}), bf16[4,768,1152]{2,1,0:T(8,128)(2,1)}, u32[]{:S(2)}, u32[]{:S(2)}) %all-to-all-start) | async-done | bytes 7077920 | tf_op jit(solution)/shard_map/all_to_all | solution.py:349
  142.6 4.4 all-to-all-start.1
  149.6 4.5 pack.7
  155.8 15.8 %collective-permute-done.7 = bf16[256,1920]{1,0:T(8,128)(2,1)S(1)} collective-permute-done((bf16[256,1920]{1,0:T(8,128)(2,1)S(1)}, bf16[256,1920]{1,0:T(8,128)(2,1)S(1)}, u32[]{:S(2)}, u32[]{:S(2)}) %collective-permute-start.7) | collective-permute-done | bytes 983072 | tf_op jit(solution)/shard_map/ppermute | solution.py:121
  171.6 8.7 %cot_product.6 = bf16[256,1920]{1,0:T(8,128)(2,1)S(1)} custom-call(bf16[2,64,3072]{2,1,0:T(8,128)(2,1)} %collective-permute-done.6.own_ref, bf16[2,64,3072]{2,1,0:T(8,128)(2,1)S(1)} %collective-permute-done.8.other_ref, bf16[384,3072]{1,0:T(8,128)(2,1)S(1)} %copy-done.1, bf16[1536,3072]{1,0:T(8,128)(2,1)} %refs_2_.11), custom_call_target="tpu_custom_call" | custom-call | flops 47185920 | bytes 199680 | tf_op jit(solution)/shard_map/cot_product/pallas_call | solution.py:208
  181.3 10.9 %collective-permute-done.3 = bf16[256,1920]{1,0:T(8,128)(2,1)S(1)} collective-permute-done((bf16[256,1920]{1,0:T(8,128)(2,1)}, bf16[256,1920]{1,0:T(8,128)(2,1)S(1)}, u32[]{:S(2)}, u32[]{:S(2)}) %collective-permute-start.3) | collective-permute-done | bytes 983072 | tf_op jit(solution)/shard_map/ppermute | solution.py:121
  193.1 8.3 %cot_product.7 = bf16[256,1920]{1,0:T(8,128)(2,1)S(1)} custom-call(bf16[2,64,3072]{2,1,0:T(8,128)(2,1)} %collective-permute-done.9.own_ref, bf16[2,64,3072]{2,1,0:T(8,128)(2,1)S(1)} %collective-permute-done.10.other_ref, bf16[384,3072]{1,0:T(8,128)(2,1)S(1)} %copy-done.1, bf16[1536,3072]{1,0:T(8,128)(2,1)} %refs_2_.11), custom_call_target="tpu_custom_call" | custom-call | flops 47185920 | bytes 199680 | tf_op jit(solution)/shard_map/cot_product/pallas_call | solution.py:208
  202.4 3.7 all-to-all-start.2
  206.2 4.5 pack.6
  212.5 11.5 %pick_rows.1.rows_ref = bf16[1024,3072]{1,0:T(8,128)(2,1)} custom-call(s32[16]{0:T(128)S(1)} %add.116.index_ref, bf16[1024,3072]{1,0:T(8,128)(2,1)} %all-gather.2.cloned.1.call-done.value_ref), custom_call_target="tpu_custom_call" | custom-call | bytes 196608 | tf_op jit(solution)/shard_map/pick_rows/pallas_call | solution.py:169
  224.0 14.0 %in_product.5.q_own.k_own.v_own = bf16[1024,1152]{1,0:T(8,128)(2,1)S(1)} custom-call(bf16[1024,3072]{1,0:T(8,128)(2,1)} %pick_rows.1.rows_ref, bf16[3072,1152]{1,0:T(8,128)(2,1)} %bitcast.2.weight_ref.refs_5_), custom_call_target="tpu_custom_call" | custom-call | flops 113246208 | bytes 245760 | tf_op jit(solution)/shard_map/in_product/pallas_call | solution.py:260
  239.5 3.6 all-to-all-done.2
  244.7 3.7 all-to-all-start.3
  255.4 68.5 %collective-permute-done.12 = bf16[256,1920]{1,0:T(8,128)(2,1)} collective-permute-done((bf16[256,1920]{1,0:T(8,128)(2,1)}, bf16[256,1920]{1,0:T(8,128)(2,1)}, u32[]{:S(2)}, u32[]{:S(2)}) %collective-permute-start.12) | collective-permute-done | bytes 983072 | tf_op jit(solution)/shard_map/ppermute | solution.py:121
  323.9 5.0 in_product.7
  329.7 4.5 all-to-all-start.4
  334.3 10.2 %collective-permute-done.11 = bf16[256,1920]{1,0:T(8,128)(2,1)} collective-permute-done((bf16[256,1920]{1,0:T(8,128)(2,1)}, bf16[256,1920]{1,0:T(8,128)(2,1)}, u32[]{:S(2)}, u32[]{:S(2)}) %collective-permute-start.11) | collective-permute-done | bytes 983072 | tf_op jit(solution)/shard_map/ppermute | solution.py:121
  346.4 7.4 %in_product.8 = bf16[1024,512]{1,0:T(8,128)(2,1)} custom-call(bf16[1024,3072]{1,0:T(8,128)(2,1)} %pick_rows.1.rows_ref, bf16[3072,512]{1,0:T(8,128)(2,1)S(1)} %bitcast.89), custom_call_target="tpu_custom_call" | custom-call | flops 50331648 | bytes 163840 | tf_op jit(solution)/shard_map/in_product/pallas_call | solution.py:260
  355.9 7.3 %in_product.6 = bf16[1024,512]{1,0:T(8,128)(2,1)} custom-call(bf16[1024,3072]{1,0:T(8,128)(2,1)} %pick_rows.1.rows_ref, bf16[3072,512]{1,0:T(8,128)(2,1)S(1)} %bitcast.78), custom_call_target="tpu_custom_call" | custom-call | flops 50331648 | bytes 163840 | tf_op jit(solution)/shard_map/in_product/pallas_call | solution.py:260
  364.7 4.6 add_parts.1
  369.3 22.1 %collective-permute-done.13 = bf16[1024,256]{1,0:T(8,128)(2,1)S(1)} collective-permute-done((bf16[1024,256]{1,0:T(8,128)(2,1)S(1)}, bf16[1024,256]{1,0:T(8,128)(2,1)S(1)}, u32[]{:S(2)}, u32[]{:S(2)}) %collective-permute-start.13) | collective-permute-done | bytes 524320 | tf_op jit(solution)/shard_map/ppermute | solution.py:121
  395.2 15.3 %attend.1 = (bf16[1024,384]{1,0:T(8,128)(2,1)S(1)}, bf16[1024,384]{1,0:T(8,128)(2,1)S(1)}, bf16[1024,384]{1,0:T(8,128)(2,1)S(1)}, bf16[1024,384]{1,0:T(8,128)(2,1)S(1)}) custom-call(bf16[1024,1152]{1,0:T(8,128)(2,1)S(1)} %copy-done.4, bf16[1024,1152]{1,0:T(8,128)(2,1)} %collective-permute-done.5.q_got.k_got.v_got, bf16[1024,1152]{1,0:T(8,128)(2,1)S(1)} %copy-done.4, ...), custom_call_target="tpu_custom_call" | custom-call | flops 12582912 | bytes 98304 | tf_op jit(solution)/shard_map/attend/pallas_call | solution.py:75
  411.4 5.2 in_product.9
  418.1 2.5 fusion.5
  420.7 12.3 %out_product.6.refs_3_ = bf16[1024,3072]{1,0:T(8,128)(2,1)} custom-call(bf16[1024,384]{1,0:T(8,128)(2,1)S(1)} %copy-done.31, bf16[1024,256]{1,0:T(8,128)(2,1)S(1)} %get-tuple-element.65.refs_1_, bf16[1024,512]{1,0:T(8,128)(2,1)S(1)} %get-tuple-element.59.refs_2_, bf16[384,3072]{1,0:T(8,128)(2,1)S(1)} %copy-done.2, bf16[1536,3072]{1,0:T(8,128)(2,1)} %refs_2_.11), custom_call_target="tpu_custom_call" | custom-call | flops 113246208 | bytes 282624 | tf_op jit(solution)/shard_map/out_product/pallas_call | solution.py:311
  433.0 18.5 %back_product.5.refs_4_ = bf16[1024,3072]{1,0:T(8,128)(2,1)} custom-call(bf16[1024,384]{1,0:T(8,128)(2,1)S(1)} %get-tuple-element.39.refs_0_, bf16[1024,384]{1,0:T(8,128)(2,1)S(1)} %get-tuple-element.40.refs_1_, bf16[1024,384]{1,0:T(8,128)(2,1)S(1)} %get-tuple-element.41.refs_2_, bf16[1024,256]{1,0:T(8,128)(2,1)S(1)} %get-tuple-element.64.refs_3_, ...), custom_call_target="tpu_custom_call" | custom-call | flops 188743680 | bytes 282624 | tf_op jit(solution)/shard_map/back_product/pallas_call | solution.py:311
  454.7 6.5 %out_product.7 = bf16[512,3072]{1,0:T(8,128)(2,1)S(1)} custom-call(bf16[1024,512]{1,0:T(8,128)(2,1)S(1)} %get-tuple-element.57.refs_0_, bf16[1024,256]{1,0:T(8,128)(2,1)S(1)} %get-tuple-element.63.refs_1_, bf16[1536,3072]{1,0:T(8,128)(2,1)} %refs_2_.11, bf16[1024,3072]{1,0:T(8,128)(2,1)} %out_product.6.refs_3_), custom_call_target="tpu_custom_call" | custom-call | flops 37748736 | bytes 196608 | tf_op jit(solution)/shard_map/out_product/pallas_call | solution.py:311
  461.3 7.7 %back_product.6 = bf16[512,3072]{1,0:T(8,128)(2,1)} custom-call(bf16[1024,512]{1,0:T(8,128)(2,1)S(1)} %get-tuple-element.56.refs_0_, bf16[1024,256]{1,0:T(8,128)(2,1)S(1)} %get-tuple-element.62.refs_1_, bf16[3072,512]{1,0:T(8,128)(2,1)} %bitcast.79, bf16[3072,256]{1,0:T(8,128)(2,1)} %bitcast.15.weight_ref.refs_3_, bf16[1024,3072]{1,0:T(8,128)(2,1)} %back_product.5.refs_4_), custom_call_target="tpu_custom_call" | custom-call | flops 37748736 | bytes 122880 | tf_op jit(solution)/shard_map/back_product/pallas_call | solution.py:311
  469.5 3.2 out_product.9
  474.5 3.2 out_product.11
  479.8 4.3 back_product.9
  485.8 3.4 back_product.8
  490.9 3.2 out_product.10
  494.1 3.2 out_product.8
  497.4 3.4 back_product.7
  501.7 8.3 %collective-permute-done.21 = bf16[256,1536]{1,0:T(8,128)(2,1)S(1)} collective-permute-done((bf16[256,1536]{1,0:T(8,128)(2,1)S(1)}, bf16[256,1536]{1,0:T(8,128)(2,1)S(1)}, u32[]{:S(2)}, u32[]{:S(2)}) %collective-permute-start.21) | collective-permute-done | bytes 786464 | tf_op jit(solution)/shard_map/ppermute | solution.py:121
  514.6 11.3 %collective-permute-done.25 = bf16[256,1536]{1,0:T(8,128)(2,1)S(1)} collective-permute-done((bf16[256,1536]{1,0:T(8,128)(2,1)S(1)}, bf16[256,1536]{1,0:T(8,128)(2,1)S(1)}, u32[]{:S(2)}, u32[]{:S(2)}) %collective-permute-start.25) | collective-permute-done | bytes 786464 | tf_op jit(solution)/shard_map/ppermute | solution.py:121
  532.9 12.2 %collective-permute-done.26 = bf16[2,64,1536]{2,1,0:T(8,128)(2,1)S(1)} collective-permute-done((bf16[2,64,1536]{2,1,0:T(8,128)(2,1)S(1)}, bf16[2,64,1536]{2,1,0:T(8,128)(2,1)S(1)}, u32[]{:S(2)}, u32[]{:S(2)}) %collective-permute-start.26) | collective-permute-done | bytes 393248 | tf_op jit(solution)/shard_map/ppermute | solution.py:121
  546.7 9.2 %collective-permute-done.27 = bf16[64,1536]{1,0:T(8,128)(2,1)S(1)} collective-permute-done((bf16[64,1536]{1,0:T(8,128)(2,1)S(1)}, bf16[64,1536]{1,0:T(8,128)(2,1)S(1)}, u32[]{:S(2)}, u32[]{:S(2)}) %collective-permute-start.27) | collective-permute-done | bytes 196640 | tf_op jit(solution)/shard_map/ppermute | solution.py:121
  556.4 5.4 all-reduce
  (167 shorter events, 80.2 us)
Async XLA Ops:
  7.2 205.3 %all-gather.2.cloned.1.call-start = ((), (), s32[]{:S(2)}) async-start(), calls=%async_computation.5 | async-start | bytes 6684672 | tf_op jit(solution)/shard_map/all_gather | solution.py:366
  16.2 10.3 %collective-permute-start = (bf16[64,3072]{1,0:T(8,128)(2,1)}, bf16[64,3072]{1,0:T(8,128)(2,1)S(1)}, u32[]{:S(2)}, u32[]{:S(2)}) collective-permute-start(bf16[64,3072]{1,0:T(8,128)(2,1)} %param.10), channel_id=1, source_target_pairs={{0,16},{8,24},{16,0},{24,8},{1,17},{9,25},{17,1},{25,9},{2,18},{10... | collective-permute-start | bytes 1179656 | tf_op jit(solution)/shard_map/ppermute | solution.py:121
  27.6 9.0 %collective-permute-start.4 = (bf16[2,64,3072]{2,1,0:T(8,128)(2,1)S(1)}, bf16[2,64,3072]{2,1,0:T(8,128)(2,1)S(1)}, u32[]{:S(2)}, u32[]{:S(2)}) collective-permute-start(bf16[2,64,3072]{2,1,0:T(8,128)(2,1)S(1)} %pad_maximum_fusion.own_ref), channel_id=1, source_target_pairs={{0,8},{8,0},{16,24},{24,16},{1,9},{9,1},{17,25},{25,17},{2,10},{10... | collective-permute-start | bytes 2359304 | tf_op jit(solution)/shard_map/ppermute | solution.py:121
  44.8 102.2 %copy-start.13 = (bf16[256,1920]{1,0:T(8,128)(2,1)}, bf16[256,1920]{1,0:T(8,128)(2,1)S(1)}, u32[]{:S(2)}) copy-start(bf16[256,1920]{1,0:T(8,128)(2,1)S(1)} %cot_product.5) | copy-start | bytes 2949124
  44.8 97.8 %all-to-all-start = ((bf16[4,768,1152]{2,1,0:T(8,128)(2,1)}), bf16[4,768,1152]{2,1,0:T(8,128)(2,1)}, u32[]{:S(2)}, u32[]{:S(2)}) async-start(bf16[4,768,1152]{2,1,0:T(8,128)(2,1)} %pack.5), calls=%async_computation | async-start | bytes 14155776 | tf_op jit(solution)/shard_map/all_to_all | solution.py:349
  50.6 58.1 %collective-permute-start.1 = (bf16[2,64,3072]{2,1,0:T(8,128)(2,1)}, bf16[2,64,3072]{2,1,0:T(8,128)(2,1)S(1)}, u32[]{:S(2)}, u32[]{:S(2)}) collective-permute-start(bf16[2,64,3072]{2,1,0:T(8,128)(2,1)} %copy-done.21), channel_id=1, source_target_pairs={{0,2},{2,0},{4,6},{6,4},{1,3},{3,1},{5,7},{7,5},{8,10},{10,8},{12,... | collective-permute-start | bytes 2359304 | tf_op jit(solution)/shard_map/ppermute | solution.py:121
  52.4 56.4 %collective-permute-start.6 = (bf16[2,64,3072]{2,1,0:T(8,128)(2,1)}, bf16[2,64,3072]{2,1,0:T(8,128)(2,1)}, u32[]{:S(2)}, u32[]{:S(2)}) collective-permute-start(bf16[2,64,3072]{2,1,0:T(8,128)(2,1)} %copy-done.21), channel_id=1, source_target_pairs={{0,4},{2,6},{4,0},{6,2},{1,5},{3,7},{5,1},{7,3},{8,12},{10,14},{12... | collective-permute-start | bytes 2359304 | tf_op jit(solution)/shard_map/ppermute | solution.py:121
  108.7 5.9 %collective-permute-start.2 = (bf16[2,64,3072]{2,1,0:T(8,128)(2,1)S(1)}, bf16[2,64,3072]{2,1,0:T(8,128)(2,1)S(1)}, u32[]{:S(2)}, u32[]{:S(2)}) collective-permute-start(bf16[2,64,3072]{2,1,0:T(8,128)(2,1)S(1)} %collective-permute-done.1.own_ref), channel_id=1, source_target_pairs={{0,8},{8,0},{16,24},{24,16},{1,9},{9,1},{17,25},{25,17},{2,10},{10... | collective-permute-start | bytes 2359304 | tf_op jit(solution)/shard_map/ppermute | solution.py:121
  108.8 40.3 %collective-permute-start.9 = (bf16[2,64,3072]{2,1,0:T(8,128)(2,1)}, bf16[2,64,3072]{2,1,0:T(8,128)(2,1)}, u32[]{:S(2)}, u32[]{:S(2)}) collective-permute-start(bf16[2,64,3072]{2,1,0:T(8,128)(2,1)} %collective-permute-done.6.own_ref), channel_id=1, source_target_pairs={{0,2},{2,0},{4,6},{6,4},{1,3},{3,1},{5,7},{7,5},{8,10},{10,8},{12,... | collective-permute-start | bytes 2359304 | tf_op jit(solution)/shard_map/ppermute | solution.py:121
  142.6 59.9 %all-to-all-start.1 = ((bf16[4,768,256]{2,1,0:T(8,128)(2,1)}), bf16[4,768,256]{2,1,0:T(8,128)(2,1)}, u32[]{:S(2)}, u32[]{:S(2)}) async-start(bf16[4,768,256]{2,1,0:T(8,128)(2,1)} %copy-done.12), calls=%async_computation.1 | async-start | bytes 3145728 | tf_op jit(solution)/shard_map/all_to_all | solution.py:349
  147.0 24.7 %collective-permute-start.7 = (bf16[256,1920]{1,0:T(8,128)(2,1)S(1)}, bf16[256,1920]{1,0:T(8,128)(2,1)S(1)}, u32[]{:S(2)}, u32[]{:S(2)}) collective-permute-start(bf16[256,1920]{1,0:T(8,128)(2,1)S(1)} %cot_product.5), channel_id=1, source_target_pairs={{0,1},{1,0},{2,3},{3,2},{4,5},{5,4},{6,7},{7,6},{8,9},{9,8},{10,11... | collective-permute-start | bytes 2949128 | tf_op jit(solution)/shard_map/ppermute | solution.py:121
  148.5 43.6 %collective-permute-start.3 = (bf16[256,1920]{1,0:T(8,128)(2,1)}, bf16[256,1920]{1,0:T(8,128)(2,1)S(1)}, u32[]{:S(2)}, u32[]{:S(2)}) collective-permute-start(bf16[256,1920]{1,0:T(8,128)(2,1)} %copy-done.15), channel_id=1, source_target_pairs={{0,1},{1,0},{2,3},{3,2},{4,5},{5,4},{6,7},{7,6},{8,9},{9,8},{10,11... | collective-permute-start | bytes 2949128 | tf_op jit(solution)/shard_map/ppermute | solution.py:121
  149.1 22.5 %collective-permute-start.8 = (bf16[2,64,3072]{2,1,0:T(8,128)(2,1)}, bf16[2,64,3072]{2,1,0:T(8,128)(2,1)S(1)}, u32[]{:S(2)}, u32[]{:S(2)}) collective-permute-start(bf16[2,64,3072]{2,1,0:T(8,128)(2,1)} %collective-permute-done.6.own_ref), channel_id=1, source_target_pairs={{0,8},{8,0},{16,24},{24,16},{1,9},{9,1},{17,25},{25,17},{2,10},{10... | collective-permute-start | bytes 2359304 | tf_op jit(solution)/shard_map/ppermute | solution.py:121
  149.1 44.0 %collective-permute-start.10 = (bf16[2,64,3072]{2,1,0:T(8,128)(2,1)}, bf16[2,64,3072]{2,1,0:T(8,128)(2,1)S(1)}, u32[]{:S(2)}, u32[]{:S(2)}) collective-permute-start(bf16[2,64,3072]{2,1,0:T(8,128)(2,1)} %collective-permute-done.9.own_ref), channel_id=1, source_target_pairs={{0,8},{8,0},{16,24},{24,16},{1,9},{9,1},{17,25},{25,17},{2,10},{10... | collective-permute-start | bytes 2359304 | tf_op jit(solution)/shard_map/ppermute | solution.py:121
  202.4 40.6 %all-to-all-start.2 = ((bf16[4,768,512]{2,1,0:T(8,128)(2,1)}), bf16[4,768,512]{2,1,0:T(8,128)(2,1)S(1)}, u32[]{:S(2)}, u32[]{:S(2)}) async-start(bf16[4,768,512]{2,1,0:T(8,128)(2,1)} %copy-done.9), calls=%async_computation.2 | async-start | bytes 6291456 | tf_op jit(solution)/shard_map/all_to_all | solution.py:349
  244.7 85.1 %all-to-all-start.3 = ((bf16[4,768,512]{2,1,0:T(8,128)(2,1)}), bf16[4,768,512]{2,1,0:T(8,128)(2,1)S(1)}, u32[]{:S(2)}, u32[]{:S(2)}) async-start(bf16[4,768,512]{2,1,0:T(8,128)(2,1)} %copy-done.10), calls=%async_computation.3 | async-start | bytes 6291456 | tf_op jit(solution)/shard_map/all_to_all | solution.py:349
  248.4 107.5 %collective-permute-start.5 = (bf16[1024,1152]{1,0:T(8,128)(2,1)}, bf16[1024,1152]{1,0:T(8,128)(2,1)}, u32[]{:S(2)}, u32[]{:S(2)}) collective-permute-start(bf16[1024,1152]{1,0:T(8,128)(2,1)} %copy-done.3), channel_id=1, source_target_pairs={{0,1},{1,0},{2,3},{3,2},{4,5},{5,4},{6,7},{7,6},{8,9},{9,8},{10,11... | collective-permute-start | bytes 7077896 | tf_op jit(solution)/shard_map/ppermute | solution.py:121
  249.9 74.0 %collective-permute-start.12 = (bf16[256,1920]{1,0:T(8,128)(2,1)}, bf16[256,1920]{1,0:T(8,128)(2,1)}, u32[]{:S(2)}, u32[]{:S(2)}) collective-permute-start(bf16[256,1920]{1,0:T(8,128)(2,1)} %copy-done.17), channel_id=1, source_target_pairs={{0,1},{1,0},{2,3},{3,2},{4,5},{5,4},{6,7},{7,6},{8,9},{9,8},{10,11... | collective-permute-start | bytes 2949128 | tf_op jit(solution)/shard_map/ppermute | solution.py:121
  250.5 94.0 %collective-permute-start.11 = (bf16[256,1920]{1,0:T(8,128)(2,1)}, bf16[256,1920]{1,0:T(8,128)(2,1)}, u32[]{:S(2)}, u32[]{:S(2)}) collective-permute-start(bf16[256,1920]{1,0:T(8,128)(2,1)} %copy-done.19), channel_id=1, source_target_pairs={{0,1},{1,0},{2,3},{3,2},{4,5},{5,4},{6,7},{7,6},{8,9},{9,8},{10,11... | collective-permute-start | bytes 2949128 | tf_op jit(solution)/shard_map/ppermute | solution.py:121
  329.7 26.1 %copy-start = (bf16[4,768,512]{2,1,0:T(8,128)(2,1)}, bf16[4,768,512]{2,1,0:T(8,128)(2,1)S(1)}, u32[]{:S(2)}) copy-start(bf16[4,768,512]{2,1,0:T(8,128)(2,1)S(1)} %all-to-all-done.3) | copy-start | bytes 9437188
  329.7 81.6 %all-to-all-start.4 = ((bf16[4,768,256]{2,1,0:T(8,128)(2,1)}), bf16[4,768,256]{2,1,0:T(8,128)(2,1)}, u32[]{:S(2)}, u32[]{:S(2)}) async-start(bf16[4,768,256]{2,1,0:T(8,128)(2,1)} %copy-done.11), calls=%async_computation.4 | async-start | bytes 3145728 | tf_op jit(solution)/shard_map/all_to_all | solution.py:349
  353.7 10.9 %copy-start.14 = (bf16[256,1920]{1,0:T(8,128)(2,1)S(1)}, bf16[256,1920]{1,0:T(8,128)(2,1)}, u32[]{:S(2)}) copy-start(bf16[256,1920]{1,0:T(8,128)(2,1)} %copy-done.13) | copy-start | bytes 2949124
  353.7 10.9 %copy-start.16 = (bf16[256,1920]{1,0:T(8,128)(2,1)S(1)}, bf16[256,1920]{1,0:T(8,128)(2,1)}, u32[]{:S(2)}) copy-start(bf16[256,1920]{1,0:T(8,128)(2,1)} %copy-done.15) | copy-start | bytes 2949124
  353.7 10.9 %copy-start.18 = (bf16[256,1920]{1,0:T(8,128)(2,1)S(1)}, bf16[256,1920]{1,0:T(8,128)(2,1)}, u32[]{:S(2)}) copy-start(bf16[256,1920]{1,0:T(8,128)(2,1)} %copy-done.17) | copy-start | bytes 2949124
  353.8 10.9 %copy-start.20 = (bf16[256,1920]{1,0:T(8,128)(2,1)S(1)}, bf16[256,1920]{1,0:T(8,128)(2,1)}, u32[]{:S(2)}) copy-start(bf16[256,1920]{1,0:T(8,128)(2,1)} %copy-done.19) | copy-start | bytes 2949124
  353.8 10.9 %copy-start.27 = (bf16[256,1920]{1,0:T(8,128)(2,1)S(1)}, bf16[256,1920]{1,0:T(8,128)(2,1)}, u32[]{:S(2)}) copy-start(bf16[256,1920]{1,0:T(8,128)(2,1)} %copy-done.26) | copy-start | bytes 2949124
  353.8 10.9 %copy-start.29 = (bf16[256,1920]{1,0:T(8,128)(2,1)S(1)}, bf16[256,1920]{1,0:T(8,128)(2,1)}, u32[]{:S(2)}) copy-start(bf16[256,1920]{1,0:T(8,128)(2,1)} %copy-done.28) | copy-start | bytes 2949124
  353.8 64.4 %collective-permute-start.14 = (bf16[1024,512]{1,0:T(8,128)(2,1)}, bf16[1024,512]{1,0:T(8,128)(2,1)}, u32[]{:S(2)}, u32[]{:S(2)}) collective-permute-start(bf16[1024,512]{1,0:T(8,128)(2,1)} %in_product.8), channel_id=1, source_target_pairs={{0,1},{1,0},{2,3},{3,2},{4,5},{5,4},{6,7},{7,6},{8,9},{9,8},{10,11... | collective-permute-start | bytes 3145736 | tf_op jit(solution)/shard_map/ppermute | solution.py:121
  355.3 36.0 %collective-permute-start.13 = (bf16[1024,256]{1,0:T(8,128)(2,1)S(1)}, bf16[1024,256]{1,0:T(8,128)(2,1)S(1)}, u32[]{:S(2)}, u32[]{:S(2)}) collective-permute-start(bf16[1024,256]{1,0:T(8,128)(2,1)S(1)} %copy-done.25), channel_id=1, source_target_pairs={{0,1},{1,0},{2,3},{3,2},{4,5},{5,4},{6,7},{7,6},{8,9},{9,8},{10,11... | collective-permute-start | bytes 1572872 | tf_op jit(solution)/shard_map/ppermute | solution.py:121
  363.2 88.3 %collective-permute-start.15 = (bf16[1024,512]{1,0:T(8,128)(2,1)}, bf16[1024,512]{1,0:T(8,128)(2,1)}, u32[]{:S(2)}, u32[]{:S(2)}) collective-permute-start(bf16[1024,512]{1,0:T(8,128)(2,1)} %in_product.6), channel_id=1, source_target_pairs={{0,1},{1,0},{2,3},{3,2},{4,5},{5,4},{6,7},{7,6},{8,9},{9,8},{10,11... | collective-permute-start | bytes 3145736 | tf_op jit(solution)/shard_map/ppermute | solution.py:121
  369.3 23.8 %copy-start.4 = (bf16[1024,1152]{1,0:T(8,128)(2,1)S(1)}, bf16[1024,1152]{1,0:T(8,128)(2,1)}, u32[]{:S(2)}) copy-start(bf16[1024,1152]{1,0:T(8,128)(2,1)} %copy-done.3) | copy-start | bytes 7077892
  416.6 37.4 %collective-permute-start.16 = (bf16[1024,256]{1,0:T(8,128)(2,1)S(1)}, bf16[1024,256]{1,0:T(8,128)(2,1)S(1)}, u32[]{:S(2)}, u32[]{:S(2)}) collective-permute-start(bf16[1024,256]{1,0:T(8,128)(2,1)S(1)} %in_product.9), channel_id=1, source_target_pairs={{0,1},{1,0},{2,3},{3,2},{4,5},{5,4},{6,7},{7,6},{8,9},{9,8},{10,11... | collective-permute-start | bytes 1572872 | tf_op jit(solution)/shard_map/ppermute | solution.py:121
  461.2 8.3 %collective-permute-start.17 = (bf16[512,3072]{1,0:T(8,128)(2,1)S(1)}, bf16[512,3072]{1,0:T(8,128)(2,1)S(1)}, u32[]{:S(2)}, u32[]{:S(2)}) collective-permute-start(bf16[512,3072]{1,0:T(8,128)(2,1)S(1)} %out_product.7), channel_id=1, source_target_pairs={{0,8},{8,0},{16,24},{24,16},{1,9},{9,1},{17,25},{25,17},{2,10},{10... | collective-permute-start | bytes 9437192 | tf_op jit(solution)/shard_map/ppermute | solution.py:121
  469.0 9.1 %collective-permute-start.24 = (bf16[512,3072]{1,0:T(8,128)(2,1)}, bf16[512,3072]{1,0:T(8,128)(2,1)S(1)}, u32[]{:S(2)}, u32[]{:S(2)}) collective-permute-start(bf16[512,3072]{1,0:T(8,128)(2,1)} %back_product.6), channel_id=1, source_target_pairs={{0,8},{8,0},{16,24},{24,16},{1,9},{9,1},{17,25},{25,17},{2,10},{10... | collective-permute-start | bytes 9437192 | tf_op jit(solution)/shard_map/ppermute | solution.py:121
  472.7 28.1 %collective-permute-start.18 = (bf16[256,1536]{1,0:T(8,128)(2,1)S(1)}, bf16[256,1536]{1,0:T(8,128)(2,1)S(1)}, u32[]{:S(2)}, u32[]{:S(2)}) collective-permute-start(bf16[256,1536]{1,0:T(8,128)(2,1)S(1)} %out_product.9), channel_id=1, source_target_pairs={{0,16},{8,24},{16,0},{24,8},{1,17},{9,25},{17,1},{25,9},{2,18},{10... | collective-permute-start | bytes 2359304 | tf_op jit(solution)/shard_map/ppermute | solution.py:121
  477.7 32.4 %collective-permute-start.21 = (bf16[256,1536]{1,0:T(8,128)(2,1)S(1)}, bf16[256,1536]{1,0:T(8,128)(2,1)S(1)}, u32[]{:S(2)}, u32[]{:S(2)}) collective-permute-start(bf16[256,1536]{1,0:T(8,128)(2,1)S(1)} %out_product.11), channel_id=1, source_target_pairs={{0,16},{8,24},{16,0},{24,8},{1,17},{9,25},{17,1},{25,9},{2,18},{10... | collective-permute-start | bytes 2359304 | tf_op jit(solution)/shard_map/ppermute | solution.py:121
  484.2 27.7 %collective-permute-start.28 = (bf16[2,2,64,1536]{3,2,0,1:T(8,128)(2,1)S(1)}, bf16[2,2,64,1536]{3,2,0,1:T(8,128)(2,1)S(1)}, u32[]{:S(2)}, u32[]{:S(2)}) collective-permute-start(bf16[2,2,64,1536]{3,2,0,1:T(8,128)(2,1)S(1)} %bitcast.104), channel_id=1, source_target_pairs={{0,2},{2,0},{4,6},{6,4},{1,3},{3,1},{5,7},{7,5},{8,10},{10,8},{12,... | collective-permute-start | bytes 2359304 | tf_op jit(solution)/shard_map/ppermute | solution.py:121
  489.2 36.8 %collective-permute-start.25 = (bf16[256,1536]{1,0:T(8,128)(2,1)S(1)}, bf16[256,1536]{1,0:T(8,128)(2,1)S(1)}, u32[]{:S(2)}, u32[]{:S(2)}) collective-permute-start(bf16[256,1536]{1,0:T(8,128)(2,1)S(1)} %back_product.8), channel_id=1, source_target_pairs={{0,16},{8,24},{16,0},{24,8},{1,17},{9,25},{17,1},{25,9},{2,18},{10... | collective-permute-start | bytes 2359304 | tf_op jit(solution)/shard_map/ppermute | solution.py:121
  501.1 26.7 %collective-permute-start.19 = (bf16[2,64,1536]{2,1,0:T(8,128)(2,1)S(1)}, bf16[2,64,1536]{2,1,0:T(8,128)(2,1)S(1)}, u32[]{:S(2)}, u32[]{:S(2)}) collective-permute-start(bf16[2,64,1536]{2,1,0:T(8,128)(2,1)S(1)} %fusion.40), channel_id=1, source_target_pairs={{0,2},{2,0},{4,6},{6,4},{1,3},{3,1},{5,7},{7,5},{8,10},{10,8},{12,... | collective-permute-start | bytes 1179656 | tf_op jit(solution)/shard_map/ppermute | solution.py:121
  510.3 20.1 %collective-permute-start.22 = (bf16[2,64,1536]{2,1,0:T(8,128)(2,1)S(1)}, bf16[2,64,1536]{2,1,0:T(8,128)(2,1)S(1)}, u32[]{:S(2)}, u32[]{:S(2)}) collective-permute-start(bf16[2,64,1536]{2,1,0:T(8,128)(2,1)S(1)} %fusion.41), channel_id=1, source_target_pairs={{0,2},{2,0},{4,6},{6,4},{1,3},{3,1},{5,7},{7,5},{8,10},{10,8},{12,... | collective-permute-start | bytes 1179656 | tf_op jit(solution)/shard_map/ppermute | solution.py:121
  512.2 18.9 %collective-permute-start.29 = (bf16[2,64,1536]{2,1,0:T(8,128)(2,1)S(1)}, bf16[2,64,1536]{2,1,0:T(8,128)(2,1)S(1)}, u32[]{:S(2)}, u32[]{:S(2)}) collective-permute-start(bf16[2,64,1536]{2,1,0:T(8,128)(2,1)S(1)} %fusion.39), channel_id=1, source_target_pairs={{0,4},{2,6},{4,0},{6,2},{1,5},{3,7},{5,1},{7,3},{8,12},{10,14},{12... | collective-permute-start | bytes 1179656 | tf_op jit(solution)/shard_map/ppermute | solution.py:121
  526.2 18.9 %collective-permute-start.26 = (bf16[2,64,1536]{2,1,0:T(8,128)(2,1)S(1)}, bf16[2,64,1536]{2,1,0:T(8,128)(2,1)S(1)}, u32[]{:S(2)}, u32[]{:S(2)}) collective-permute-start(bf16[2,64,1536]{2,1,0:T(8,128)(2,1)S(1)} %fusion.42), channel_id=1, source_target_pairs={{0,2},{2,0},{4,6},{6,4},{1,3},{3,1},{5,7},{7,5},{8,10},{10,8},{12,... | collective-permute-start | bytes 1179656 | tf_op jit(solution)/shard_map/ppermute | solution.py:121
  527.9 34.5 %collective-permute-start.20 = (bf16[64,1536]{1,0:T(8,128)(2,1)S(1)}, bf16[64,1536]{1,0:T(8,128)(2,1)}, u32[]{:S(2)}, u32[]{:S(2)}) collective-permute-start(bf16[64,1536]{1,0:T(8,128)(2,1)S(1)} %fusion.47), channel_id=1, source_target_pairs={{0,4},{2,6},{4,0},{6,2},{1,5},{3,7},{5,1},{7,3},{8,12},{10,14},{12... | collective-permute-start | bytes 589832 | tf_op jit(solution)/shard_map/ppermute | solution.py:121
  530.5 33.6 %collective-permute-start.23 = (bf16[64,1536]{1,0:T(8,128)(2,1)S(1)}, bf16[64,1536]{1,0:T(8,128)(2,1)}, u32[]{:S(2)}, u32[]{:S(2)}) collective-permute-start(bf16[64,1536]{1,0:T(8,128)(2,1)S(1)} %fusion.48), channel_id=1, source_target_pairs={{0,4},{2,6},{4,0},{6,2},{1,5},{3,7},{5,1},{7,3},{8,12},{10,14},{12... | collective-permute-start | bytes 589832 | tf_op jit(solution)/shard_map/ppermute | solution.py:121
  531.2 24.9 %copy-start.33 = (bf16[64,3072]{1,0:T(8,128)(2,1)S(1)}, bf16[64,3072]{1,0:T(8,128)(2,1)}, u32[]{:S(2)}) copy-start(bf16[64,3072]{1,0:T(8,128)(2,1)} %param.9) | copy-start | bytes 1179652
  531.2 15.3 %collective-permute-start.30 = (bf16[64,1536]{1,0:T(8,128)(2,1)S(1)}, bf16[64,1536]{1,0:T(8,128)(2,1)S(1)}, u32[]{:S(2)}, u32[]{:S(2)}) collective-permute-start(bf16[64,1536]{1,0:T(8,128)(2,1)S(1)} %fusion.50), channel_id=1, source_target_pairs={{0,16},{8,24},{16,0},{24,8},{1,17},{9,25},{17,1},{25,9},{2,18},{10... | collective-permute-start | bytes 589832 | tf_op jit(solution)/shard_map/ppermute | solution.py:121
  545.2 10.7 %collective-permute-start.27 = (bf16[64,1536]{1,0:T(8,128)(2,1)S(1)}, bf16[64,1536]{1,0:T(8,128)(2,1)S(1)}, u32[]{:S(2)}, u32[]{:S(2)}) collective-permute-start(bf16[64,1536]{1,0:T(8,128)(2,1)S(1)} %fusion.49), channel_id=1, source_target_pairs={{0,4},{2,6},{4,0},{6,2},{1,5},{3,7},{5,1},{7,3},{8,12},{10,14},{12... | collective-permute-start | bytes 589832 | tf_op jit(solution)/shard_map/ppermute | solution.py:121
  546.7 18.4 %copy-start.34 = (bf16[64,3072]{1,0:T(8,128)(2,1)S(1)}, bf16[64,3072]{1,0:T(8,128)(2,1)}, u32[]{:S(2)}) copy-start(bf16[64,3072]{1,0:T(8,128)(2,1)} %param.10) | copy-start | bytes 1179652
  (25 other events, 80.5 us)
Sparse Core Ops, SparseCore 0:
  16.3 87.9 all-gather.1

commit v10 on v9

--- a/solution.py
+++ b/solution.py
@@ -157,119 +157,105 @@
     )(*weights)
 
 
-IMAGE_ORDER = ((1, 1), (0, 1), (1, 0), (0, 0))
-
-
-def copy_kernel(index_ref, value_ref, out_ref):
-    out_ref[...] = value_ref[...]
-
-
-def pick_rows(value, index):
-    block = (value.shape[0] // index.shape[0], value.shape[1])
+IMAGE_ORDER = (3, 1, 2, 0)
+
+
+def store_images(place_ref, out_ref, value):
+    size = value.shape[0] // len(IMAGE_ORDER)
+    for image in range(len(IMAGE_ORDER)):
+        start = pl.multiple_of(place_ref[image] * size, size)
+        out_ref[pl.ds(start, size), :] = value[image * size : (image + 1) * size]
+
+
+def cot_kernel(place_ref, rows_ref, attn_ref, mlp_ref, out_ref):
+    step = pl.program_id(0)
+
+    @pl.when(step == 0)
+    def _():
+        store_images(place_ref, out_ref, half(back_dot(rows_ref[...], attn_ref[...])))
+
+    @pl.when(step > 0)
+    def _():
+        store_images(place_ref, out_ref, half(back_dot(rows_ref[...], mlp_ref[...])))
+
+
+def cot_product(place, rows, w_attn_out, w_mlp_out):
+    count, features = rows.shape
+    tile = w_attn_out.shape[0]
+    columns = tile + w_mlp_out.shape[0]
+    out = jax.ShapeDtypeStruct((count, columns), jnp.bfloat16)
     return pl.pallas_call(
-        copy_kernel,
+        cot_kernel,
         grid_spec=pltpu.PrefetchScalarGridSpec(
             num_scalar_prefetch=1,
-            grid=index.shape,
-            in_specs=[pl.BlockSpec(block, lambda i, index: (index[i], 0))],
-            out_specs=pl.BlockSpec(block, lambda i, index: (i, 0)),
+            grid=(columns // tile,),
+            in_specs=[
+                pl.BlockSpec((count, features), lambda n, place: (0, 0)),
+                pl.BlockSpec((tile, features), lambda n, place: (0, 0)),
+                pl.BlockSpec((tile, features), lambda n, place: (jnp.maximum(n - 1, 0), 0)),
+            ],
+            out_specs=pl.BlockSpec((count, tile), lambda n, place: (0, n)),
         ),
-        out_shape=jax.ShapeDtypeStruct(value.shape, value.dtype),
-        compiler_params=params(),
-        cost_estimate=cost(0, value, value),
-        name="pick_rows",
-    )(index, value)
-
-
-def cot_kernel(own_ref, other_ref, attn_ref, mlp_ref, out_ref, rows_ref):
-    rows = own_ref.shape[1]
-    step = pl.program_id(0)
-
-    @pl.when(step == 0)
-    def _():
-        for place, (x_bit, core_bit) in enumerate(IMAGE_ORDER):
-            part = other_ref if core_bit else own_ref
-            rows_ref[place * rows : (place + 1) * rows, :] = part[x_bit]
-        out_ref[...] = half(back_dot(rows_ref[...], attn_ref[...]))
-
-    @pl.when(step > 0)
-    def _():
-        out_ref[...] = half(back_dot(rows_ref[...], mlp_ref[...]))
-
-
-def cot_product(part, w_attn_out, w_mlp_out):
-    own, other = part
-    _, rows, features = own.shape
-    tile = w_attn_out.shape[0]
-    columns = tile + w_mlp_out.shape[0]
-    count = len(IMAGE_ORDER) * rows
-    out = jax.ShapeDtypeStruct((count, columns), jnp.bfloat16)
-    whole = pl.BlockSpec(own.shape, lambda n: (0, 0, 0))
-    return pl.pallas_call(
-        cot_kernel,
-        grid=(columns // tile,),
-        in_specs=[
-            whole,
-            whole,
-            pl.BlockSpec((tile, features), lambda n: (0, 0)),
-            pl.BlockSpec((tile, features), lambda n: (jnp.maximum(n - 1, 0), 0)),
-        ],
-        out_specs=pl.BlockSpec((count, tile), lambda n: (0, n)),
         out_shape=out,
-        scratch_shapes=[pltpu.VMEM((count, features), jnp.bfloat16)],
         compiler_params=params(),
         cost_estimate=cost(2 * count * columns * features, out, w_attn_out, w_mlp_out),
         name="cot_product",
-    )(own, other, w_attn_out, w_mlp_out)
+    )(place, rows, w_attn_out, w_mlp_out)
 
 
 def add_kernel(*refs):
     terms, out_ref = refs[:-1], refs[-1]
     count = len(terms) // 2
+    rows = terms[0].shape[2]
     for part in range(count):
-        out_ref[0, part] = half(wide_sum(terms[part][0], terms[count + part][0]))
-
-
-def add_parts(owns, gots):
-    images, parts = len(IMAGE_ORDER), len(owns)
-    rows, columns = owns[0].shape[0] // images, owns[0].shape[1]
-    out = jax.ShapeDtypeStruct((images, parts, rows, columns), jnp.bfloat16)
-    terms = [value.reshape(images, rows, columns) for value in (*owns, *gots)]
+        total = half(wide_sum(terms[part][0], terms[count + part][0]))
+        out_ref[0, :, part * rows : (part + 1) * rows, :] = total
+
+
+def add_parts(owns, gots, n_gy):
+    images, parts, columns = len(IMAGE_ORDER), len(owns), owns[0].shape[1]
+    rows = owns[0].shape[0] // images // n_gy
+    out = jax.ShapeDtypeStruct((images, n_gy, parts * rows, columns), jnp.bfloat16)
+    terms = [value.reshape(images, n_gy, rows, columns) for value in (*owns, *gots)]
+    spec = pl.BlockSpec((1, n_gy, rows, columns), lambda image: (image, 0, 0, 0))
     added = pl.pallas_call(
         add_kernel,
         grid=(images,),
-        in_specs=[pl.BlockSpec((1, rows, columns), lambda image: (image, 0, 0))] * len(terms),
-        out_specs=pl.BlockSpec((1, parts, rows, columns), lambda image: (image, 0, 0, 0)),
+        in_specs=[spec] * len(terms),
+        out_specs=pl.BlockSpec((1, *out.shape[1:]), lambda image: (image, 0, 0, 0)),
         out_shape=out,
         compiler_params=params(),
         cost_estimate=cost(0, out, out, out),
         name="add_parts",
     )(*terms)
-    return added.reshape(images * parts * rows, columns)
-
-
-def in_kernel(rows_ref, weight_ref, out_ref):
-    out_ref[...] = half(dot(rows_ref[...], weight_ref[...]))
-
-
-def in_product(rows, weight):
+    return added.reshape(images * n_gy * parts * rows, columns)
+
+
+def in_kernel(place_ref, rows_ref, weight_ref, out_ref):
+    store_images(place_ref, out_ref, half(dot(rows_ref[...], weight_ref[...])))
+
+
+def in_product(place, rows, weight):
     count, features = rows.shape
     columns = weight.shape[1]
     tile = 384 if columns % 384 == 0 else 256
     out = jax.ShapeDtypeStruct((count, columns), jnp.bfloat16)
     return pl.pallas_call(
         in_kernel,
-        grid=(columns // tile,),
-        in_specs=[
-            pl.BlockSpec((count, features), lambda n: (0, 0)),
-            pl.BlockSpec((features, tile), lambda n: (0, n)),
-        ],
-        out_specs=pl.BlockSpec((count, tile), lambda n: (0, n)),
+        grid_spec=pltpu.PrefetchScalarGridSpec(
+            num_scalar_prefetch=1,
+            grid=(columns // tile,),
+            in_specs=[
+                pl.BlockSpec((count, features), lambda n, place: (0, 0)),
+                pl.BlockSpec((features, tile), lambda n, place: (0, n)),
+            ],
+            out_specs=pl.BlockSpec((count, tile), lambda n, place: (0, n)),
+        ),
         out_shape=out,
         compiler_params=params(),
         cost_estimate=cost(2 * count * columns * features, rows, out, weight),
         name="in_product",
-    )(rows, weight)
+    )(place, rows, weight)
 
 
 def product(terms, weights, adds, start, count, kind, transposed, window=None, rows=None):
@@ -325,9 +311,12 @@
 
 
 def body(layer_input, out_cotangent, w_query, w_key, w_value, w_mlp_in, w_attn_out, w_mlp_out):
-    n_gx, n_gz = lax.axis_size("gx"), lax.axis_size("gz")
+    n_gx, n_gy, n_gz = (lax.axis_size(name) for name in ("gx", "gy", "gz"))
+    me_y = lax.axis_index("gy")
     own_rows, features = layer_input.shape
-    count = own_rows * lax.axis_size("gy")
+    count = own_rows * n_gy
+    places = jnp.array([IMAGE_ORDER.index(bits) for bits in range(n_gx)], jnp.int32)
+    place = places[lax.axis_index("gx") ^ jnp.arange(n_gx)]
 
     def after(value, *earlier):
         return lax.optimization_barrier((value, earlier))[0]
@@ -337,13 +326,8 @@
             return trade(part, "gz", 1)
         return half(lax.psum(part.astype(jnp.float32), "gz") - part.astype(jnp.float32))
 
-    def with_x(block):
-        return jnp.stack([block, trade(block, "gx", 2)])
-
-    def gather_parts(pair):
-        near, far = trade(pair, "gy", 1), trade(pair, "gy", 2)
-        parts = [pair, near, far, trade(far, "gy", 1)]
-        return [(part, trade(part, "gx", 1)) for part in parts]
+    def all_rows(block):
+        return lax.all_gather(block, ("gx", "gy"), axis=0, tiled=True)
 
     def swap(packed):
         swapped = lax.all_to_all(packed, "gx", split_axis=0, concat_axis=0, tiled=True)
@@ -356,43 +340,41 @@
         pack((w_mlp_in,), n_gx, start, width, 256) for start, width in zip(starts, MLP_CUTS)
     ]
 
-    cot_pair = with_x(out_cotangent)
+    in_heads = swap(packed_heads)
+
     wide = layer_input.astype(jnp.float32)
     total, squares = lax.psum((jnp.sum(wide, axis=1), jnp.sum(wide * wide, axis=1)), "gz")
     center = total / D
     spread = squares / D - center * center
     inverse = lax.rsqrt(spread + EPSILON)
     normed = (wide - center[:, None]) * inverse[:, None]
-    gathered = lax.all_gather(half(normed), ("gx", "gy"), axis=0, tiled=True)
-    n_gy = lax.axis_size("gy")
-    image_of = lax.axis_index("gx") ^ jnp.array([2 * x + core for x, core in IMAGE_ORDER])
-    block_of = image_of[:, None] * n_gy + (lax.axis_index("gy") ^ jnp.arange(n_gy))[None, :]
-    all_in = pick_rows(gathered, block_of.reshape(-1).astype(jnp.int32))
-
-    cot_owns, cot_gots = [], []
-    for place, (own, other) in enumerate(gather_parts(cot_pair)):
-        if place >= 2:
-            own = after(own, cot_gots[place - 2])
-        cot_owns.append(cot_product((own, other), w_attn_out, w_mlp_out))
-        cot_gots.append(others(cot_owns[-1]))
-
-    in_heads = swap(after(packed_heads, cot_owns[0]))
-    in_mlp = [swap(after(packed_mlp[0], in_heads, cot_owns[1]))]
-    in_mlp.append(swap(after(packed_mlp[1], in_mlp[0], cot_owns[2], cot_owns[3])))
-    heads_own = in_product(after(all_in, cot_gots[1]), in_heads)
+
+    middle = own_rows // 2
+    first_cot = all_rows(out_cotangent[:middle])
+    second_cot = all_rows(after(out_cotangent[middle:], total))
+    all_in = all_rows(after(half(normed), first_cot))
+
+    cot_owns = [cot_product(place, first_cot, w_attn_out, w_mlp_out)]
+    cot_gots = [others(cot_owns[0])]
+    cot_owns.append(cot_product(place, after(second_cot, cot_gots[0]), w_attn_out, w_mlp_out))
+    cot_gots.append(others(cot_owns[1]))
+
+    in_mlp = [swap(after(packed_mlp[0], in_heads, cot_owns[0]))]
+    in_mlp.append(swap(after(packed_mlp[1], in_mlp[0], cot_owns[1])))
+    mlp_own = [in_product(place, after(all_in, cot_gots[1]), in_mlp[0])]
+    mlp_got = [others(mlp_own[0])]
+    heads_own = in_product(place, after(all_in, mlp_own[0]), in_heads)
     heads_got = others(heads_own)
-    mlp_own = [in_product(after(all_in, cot_gots[2], heads_own), in_mlp[0])]
-    mlp_got = [others(mlp_own[0])]
-    in_mlp.append(swap(after(packed_mlp[2], in_mlp[1], heads_own)))
-    mlp_own.append(in_product(after(all_in, cot_gots[3], mlp_own[0]), in_mlp[1]))
+    in_mlp.append(swap(after(packed_mlp[2], in_mlp[1], mlp_own[0])))
+    mlp_own.append(in_product(place, after(all_in, mlp_got[0], heads_own), in_mlp[1]))
     mlp_got.append(others(mlp_own[1]))
-    in_mlp.append(swap(after(packed_mlp[3], in_mlp[2], mlp_own[0])))
-    mlp_own.append(in_product(after(all_in, heads_got), in_mlp[2]))
+    in_mlp.append(swap(after(packed_mlp[3], in_mlp[2], heads_own)))
+    mlp_own.append(in_product(place, after(all_in, heads_got), in_mlp[2]))
     mlp_got.append(others(mlp_own[2]))
 
-    out_grad = add_parts(after(cot_owns, mlp_own[1]), cot_gots)
+    out_grad = add_parts(after(cot_owns, mlp_own[1]), cot_gots, n_gy)
     mixed, *head_grads = attend(heads_own, heads_got, out_grad)
-    mlp_own.append(in_product(after(all_in, mlp_got[0], mixed), in_mlp[3]))
+    mlp_own.append(in_product(place, after(all_in, mlp_got[1], mixed), in_mlp[3]))
     mlp_got.append(others(mlp_own[3]))
 
     forward_terms, backward_terms = [(mixed, 0, 0)], []
@@ -440,19 +422,28 @@
     def wider(value):
         return value.astype(jnp.float32)
 
+    def at(value, axis, index):
+        return lax.index_in_dim(value, index, axis, keepdims=False)
+
+    def own_and_sent(value, axis, is_second):
+        low, high = at(value, axis, 0), at(value, axis, 1)
+        return jnp.where(is_second, high, low), half(jnp.where(is_second, low, high))
+
+    def over_z(value, axis):
+        kept, sent = own_and_sent(value, axis + 1, me_y % 2 == 1)
+        value = wide_sum(kept, trade(sent, "gy", 1))
+        kept, sent = own_and_sent(value, axis, me_y >= 2)
+        return wide_sum(kept, trade(sent, "gy", 2))
+
     def over_x_z(term, from_core, window):
         from_x = trade(term(2 * count, count, [(from_core, 0)], window), "gx", 2)
         mine = wide_sum(term(3 * count, count, [(from_core, count)], window), from_x)
-        mine = mine.reshape(2, 2, own_rows, window[1])
-        pair = mine[:, 0] + wider(trade(half(mine[:, 1]), "gy", 1))
-        return pair[0] + wider(trade(half(pair[1]), "gy", 2))
+        return over_z(mine.reshape(2, 2, own_rows, window[1]), 0)
 
     def over_z_x(term, from_core, window):
         both = term(2 * count, 2 * count, [(from_core, 0)], window)
-        both = both.reshape(2, 2, 2, own_rows, window[1])
-        pair = wide_sum(both[:, :, 0], trade(both[:, :, 1], "gy", 1))
-        ends = pair[:, 0] + wider(trade(half(pair[:, 1]), "gy", 2))
-        return ends[1] + wider(trade(half(ends[0]), "gx", 2))
+        ends = over_z(both.reshape(2, 2, 2, own_rows, window[1]), 1)
+        return wide_sum(ends[1], trade(half(ends[0]), "gx", 2))
 
     def spread_rows(term, ways):
         width = features // len(ways)

time: 576 us -> 554 us (0.962)
  starting transfers between devices: 61 us -> 47.2 us
  Pallas kernels: 191 us -> 178 us
  waiting for transfers between devices: 253 us -> 261 us
    ppermute x31 -> x21, waiting for transfers between devices: 230 us -> 120 us  [trade(): return lax.ppermute(block, axis, pairs)]
    all_to_all x5, waiting for transfers between devices: 22.4 us -> 102 us  [swap(): lax.all_to_all(packed, 'gx', split_axis=0, concat_axis=0, tiled=True)]
    all_gather x1 -> x3, waiting for transfers between devices: 0.01 us -> 39.9 us  [all_rows(): return lax.all_gather(block, ('gx', 'gy'), axis=0, tiled=True)]
    pallas_call x11 -> x8, Pallas kernels: 88.2 us -> 73.5 us  [the longest x5 42.4 us: in_product(): pl.pallas_call(in_kernel, grid_spec=pltpu.PrefetchScalarGridSpec(num_scal...]
    ppermute x31 -> x21, starting transfers between devices: 38.8 us -> 25.3 us  [trade(): return lax.ppermute(block, axis, pairs)]
    unnamed x73 -> x68, local copies, waits for them, and re-layouts: 23.8 us -> 18.6 us
  transfers between devices with their start and end apart: 37 -> 29, of which waited for: 13 -> 10; matrix products, arithmetic and copies ran while one was open for 2% -> 3% of each run, Pallas kernels for 32% -> 31%
where the time goes in v10:
time: 554 us; the launch traced here: 551 us
  waiting for transfers between devices  261 us (47%)
  Pallas kernels  178 us (32%)
  starting transfers between devices  47.2 us (9%)
  local copies, waits for them, and re-layouts  21.3 us (4%)
  other arithmetic  17.3 us (3%)
  between operations  14.4 us (3%)
  blocking collectives  11.4 us (2%)
    ppermute x21, waiting for transfers between devices, trade(): return lax.ppermute(block, axis, pairs)  120 us
    all_to_all x5, waiting for transfers between devices, swap(): lax.all_to_all(packed, 'gx', split_axis=0, concat_axis=0, tiled=True)  102 us
    pallas_call x11, Pallas kernels, product(): pl.pallas_call(kernel, grid=(columns // tile,), in_specs=specs, out_specs...  70.9 us
    pallas_call x5, Pallas kernels, in_product(): pl.pallas_call(in_kernel, grid_spec=pltpu.PrefetchScalarGridSpec(num_scal...  42.4 us
    all_gather x3, waiting for transfers between devices, all_rows(): return lax.all_gather(block, ('gx', 'gy'), axis=0, tiled=True)  39.9 us
    pallas_call x2, Pallas kernels, cot_product(): pl.pallas_call(cot_kernel, grid_spec=pltpu.PrefetchScalarGridSpec(num_sca...  25.8 us
    ppermute x21, starting transfers between devices, trade(): return lax.ppermute(block, axis, pairs)  25.3 us
    all_to_all x5, starting transfers between devices, swap(): lax.all_to_all(packed, 'gx', split_axis=0, concat_axis=0, tiled=True)  21.8 us
  transfers between devices with their start and end apart: 29, of which 10 were waited for; matrix products, arithmetic and copies ran while one was open for 3% of the time, Pallas kernels for 31%

profile of v10, /device:TPU:0, one launch (start us, length us, event | category | flops | bytes accessed | tf_op | source)
XLA Modules:
  0.0 551.2 jit_solution(665684716777338577)
XLA Ops:
  10.4 5.9 %all-reduce.1 = (f32[64]{0:T(128)S(1)}, f32[64]{0:T(128)S(1)}) all-reduce(f32[64]{0:T(128)S(1)} %get-tuple-element.43, f32[64]{0:T(128)S(1)} %get-tuple-element.42), channel_id=1, replica_groups=mesh['gx'=4,'gy'=4,'gz'=2] {'gz'}, use_global_device_ids=true, to_apply=%region_3.0 | all-reduce | flops 128 | bytes 1024 | tf_op jit(solution)/shard_map/psum | solution.py:346
  18.3 39.9 %all-gather.4.cloned.1.call-done.rows_ref = bf16[512,3072]{1,0:T(8,128)(2,1)} async-done(((bf16[32,3072]{1,0:T(8,128)(2,1)}), bf16[512,3072]{1,0:T(8,128)(2,1)}) %all-gather.4.cloned.1.call-update) | async-done | bytes 3145744 | tf_op jit(solution)/shard_map/all_gather | solution.py:330
  59.9 5.2 pack.6
  65.2 5.6 %all-to-all-start = ((bf16[4,768,1152]{2,1,0:T(8,128)(2,1)}), bf16[4,768,1152]{2,1,0:T(8,128)(2,1)}, u32[]{:S(2)}, u32[]{:S(2)}) async-start(bf16[4,768,1152]{2,1,0:T(8,128)(2,1)} %pack.6), calls=%async_computation | async-start | bytes 14155776 | tf_op jit(solution)/shard_map/all_to_all | solution.py:333
  71.4 13.2 %cot_product.2 = bf16[512,1920]{1,0:T(8,128)(2,1)} custom-call(s32[4]{0:T(128)S(1)} %gather_fusion, bf16[512,3072]{1,0:T(8,128)(2,1)} %all-gather.4.cloned.1.call-done.rows_ref, bf16[384,3072]{1,0:T(8,128)(2,1)S(1)} %copy-done.10, bf16[1536,3072]{1,0:T(8,128)(2,1)} %refs_2_.11), custom_call_target="tpu_custom_call" | custom-call | flops 94371840 | bytes 215040 | tf_op jit(solution)/shard_map/cot_product/pallas_call | solution.py:187
  86.1 2.2 pack.5
  89.5 85.6 %all-to-all-done = bf16[4,768,1152]{2,1,0:T(8,128)(2,1)} async-done(((bf16[4,768,1152]{2,1,0:T(8,128)(2,1)}), bf16[4,768,1152]{2,1,0:T(8,128)(2,1)}, u32[]{:S(2)}, u32[]{:S(2)}) %all-to-all-start) | async-done | bytes 7077920 | tf_op jit(solution)/shard_map/all_to_all | solution.py:333
  175.1 4.4 all-to-all-start.1
  179.5 4.5 pack.8
  185.6 12.6 %cot_product.3 = bf16[512,1920]{1,0:T(8,128)(2,1)S(1)} custom-call(s32[4]{0:T(128)S(1)} %gather_fusion, bf16[512,3072]{1,0:T(8,128)(2,1)} %all-gather.8.cloned.1.call-done.rows_ref, bf16[384,3072]{1,0:T(8,128)(2,1)S(1)} %copy-done.10, bf16[1536,3072]{1,0:T(8,128)(2,1)} %refs_2_.11), custom_call_target="tpu_custom_call" | custom-call | flops 94371840 | bytes 215040 | tf_op jit(solution)/shard_map/cot_product/pallas_call | solution.py:187
  199.6 3.7 all-to-all-start.2
  204.9 4.5 pack.7
  211.2 37.8 %collective-permute-done.1 = bf16[512,1920]{1,0:T(8,128)(2,1)} collective-permute-done((bf16[512,1920]{1,0:T(8,128)(2,1)}, bf16[512,1920]{1,0:T(8,128)(2,1)}, u32[]{:S(2)}, u32[]{:S(2)}) %collective-permute-start.1) | collective-permute-done | bytes 1966112 | tf_op jit(solution)/shard_map/ppermute | solution.py:121
  248.9 6.4 %in_product.5 = bf16[1024,256]{1,0:T(8,128)(2,1)} custom-call(s32[4]{0:T(128)S(1)} %gather_fusion, bf16[1024,3072]{1,0:T(8,128)(2,1)} %all-gather.6.cloned.1.call-done.rows_ref, bf16[3072,256]{1,0:T(8,128)(2,1)} %bitcast.2.weight_ref.refs_6_), custom_call_target="tpu_custom_call" | custom-call | flops 25165824 | bytes 131072 | tf_op jit(solution)/shard_map/in_product/pallas_call | solution.py:243
  257.0 3.7 all-to-all-start.3
  260.7 15.2 %in_product.6.q_own.k_own.v_own = bf16[1024,1152]{1,0:T(8,128)(2,1)} custom-call(s32[4]{0:T(128)S(1)} %gather_fusion, bf16[1024,3072]{1,0:T(8,128)(2,1)} %all-gather.6.cloned.1.call-done.rows_ref, bf16[3072,1152]{1,0:T(8,128)(2,1)} %bitcast.1.weight_ref.refs_5_), custom_call_target="tpu_custom_call" | custom-call | flops 113246208 | bytes 245760 | tf_op jit(solution)/shard_map/in_product/pallas_call | solution.py:243
  278.0 2.2 pack.9
  281.4 16.2 %all-to-all-done.3 = bf16[4,768,512]{2,1,0:T(8,128)(2,1)S(1)} async-done(((bf16[4,768,512]{2,1,0:T(8,128)(2,1)}), bf16[4,768,512]{2,1,0:T(8,128)(2,1)S(1)}, u32[]{:S(2)}, u32[]{:S(2)}) %all-to-all-start.3) | async-done | bytes 3145760 | tf_op jit(solution)/shard_map/all_to_all | solution.py:333
  297.6 4.5 all-to-all-start.4
  302.1 39.0 %collective-permute-done.3 = bf16[1024,256]{1,0:T(8,128)(2,1)} collective-permute-done((bf16[1024,256]{1,0:T(8,128)(2,1)}, bf16[1024,256]{1,0:T(8,128)(2,1)}, u32[]{:S(2)}, u32[]{:S(2)}) %collective-permute-start.3) | collective-permute-done | bytes 524320 | tf_op jit(solution)/shard_map/ppermute | solution.py:121
  343.0 7.1 %in_product.8 = bf16[1024,512]{1,0:T(8,128)(2,1)S(1)} custom-call(s32[4]{0:T(128)S(1)} %gather_fusion, bf16[1024,3072]{1,0:T(8,128)(2,1)} %all-gather.6.cloned.1.call-done.rows_ref, bf16[3072,512]{1,0:T(8,128)(2,1)S(1)} %bitcast.116), custom_call_target="tpu_custom_call" | custom-call | flops 50331648 | bytes 163840 | tf_op jit(solution)/shard_map/in_product/pallas_call | solution.py:243
  351.8 7.8 %in_product.7 = bf16[1024,512]{1,0:T(8,128)(2,1)} custom-call(s32[4]{0:T(128)S(1)} %gather_fusion, bf16[1024,3072]{1,0:T(8,128)(2,1)} %all-gather.6.cloned.1.call-done.rows_ref, bf16[3072,512]{1,0:T(8,128)(2,1)S(1)} %bitcast.105), custom_call_target="tpu_custom_call" | custom-call | flops 50331648 | bytes 163840 | tf_op jit(solution)/shard_map/in_product/pallas_call | solution.py:243
  360.1 5.3 add_parts.1
  365.4 2.0 fusion.17
  367.4 2.1 copy-done.4
  369.5 15.2 %attend.1 = (bf16[1024,384]{1,0:T(8,128)(2,1)S(1)}, bf16[1024,384]{1,0:T(8,128)(2,1)S(1)}, bf16[1024,384]{1,0:T(8,128)(2,1)S(1)}, bf16[1024,384]{1,0:T(8,128)(2,1)S(1)}) custom-call(bf16[1024,1152]{1,0:T(8,128)(2,1)} %in_product.6.q_own.k_own.v_own, bf16[1024,1152]{1,0:T(8,128)(2,1)} %collective-permute-done.2.q_got.k_got.v_got, ...), custom_call_target="tpu_custom_call" | custom-call | flops 12582912 | bytes 98304 | tf_op jit(solution)/shard_map/attend/pallas_call | solution.py:75
  386.6 5.8 %in_product.9 = bf16[1024,256]{1,0:T(8,128)(2,1)S(1)} custom-call(s32[4]{0:T(128)S(1)} %gather_fusion, bf16[1024,3072]{1,0:T(8,128)(2,1)} %all-gather.6.cloned.1.call-done.rows_ref, bf16[3072,256]{1,0:T(8,128)(2,1)} %bitcast.10.weight_ref.refs_3_), custom_call_target="tpu_custom_call" | custom-call | flops 25165824 | bytes 131072 | tf_op jit(solution)/shard_map/in_product/pallas_call | solution.py:243
  395.4 12.3 %out_product.6.refs_3_ = bf16[1024,3072]{1,0:T(8,128)(2,1)} custom-call(bf16[1024,384]{1,0:T(8,128)(2,1)S(1)} %copy-done.28, bf16[1024,256]{1,0:T(8,128)(2,1)S(1)} %get-tuple-element.61.refs_1_, bf16[1024,512]{1,0:T(8,128)(2,1)S(1)} %get-tuple-element.55.refs_2_, bf16[384,3072]{1,0:T(8,128)(2,1)S(1)} %copy-done.11, bf16[1536,3072]{1,0:T(8,128)(2,1)} %refs_2_.11), custom_call_target="tpu_custom_call" | custom-call | flops 113246208 | bytes 282624 | tf_op jit(solution)/shard_map/out_product/pallas_call | solution.py:297
  407.7 18.5 %back_product.5.refs_4_ = bf16[1024,3072]{1,0:T(8,128)(2,1)} custom-call(bf16[1024,384]{1,0:T(8,128)(2,1)S(1)} %get-tuple-element.35.refs_0_, bf16[1024,384]{1,0:T(8,128)(2,1)S(1)} %get-tuple-element.36.refs_1_, bf16[1024,384]{1,0:T(8,128)(2,1)S(1)} %get-tuple-element.37.refs_2_, bf16[1024,256]{1,0:T(8,128)(2,1)S(1)} %get-tuple-element.60.refs_3_, ...), custom_call_target="tpu_custom_call" | custom-call | flops 188743680 | bytes 282624 | tf_op jit(solution)/shard_map/back_product/pallas_call | solution.py:297
  426.2 2.5 fusion.11
  429.5 8.1 %out_product.7 = bf16[512,3072]{1,0:T(8,128)(2,1)} custom-call(bf16[1024,512]{1,0:T(8,128)(2,1)S(1)} %get-tuple-element.53.refs_0_, bf16[1024,256]{1,0:T(8,128)(2,1)S(1)} %get-tuple-element.59.refs_1_, bf16[1536,3072]{1,0:T(8,128)(2,1)} %refs_2_.11, bf16[1024,3072]{1,0:T(8,128)(2,1)} %out_product.6.refs_3_), custom_call_target="tpu_custom_call" | custom-call | flops 37748736 | bytes 196608 | tf_op jit(solution)/shard_map/out_product/pallas_call | solution.py:297
  437.7 7.8 %back_product.6 = bf16[512,3072]{1,0:T(8,128)(2,1)} custom-call(bf16[1024,512]{1,0:T(8,128)(2,1)S(1)} %get-tuple-element.52.refs_0_, bf16[1024,256]{1,0:T(8,128)(2,1)S(1)} %get-tuple-element.58.refs_1_, bf16[3072,512]{1,0:T(8,128)(2,1)} %bitcast.106, bf16[3072,256]{1,0:T(8,128)(2,1)} %bitcast.10.weight_ref.refs_3_, bf16[1024,3072]{1,0:T(8,128)(2,1)} %back_product.5.refs_4_), custom_call_target="tpu_custom_call" | custom-call | flops 37748736 | bytes 122880 | tf_op jit(solution)/shard_map/back_product/pallas_call | solution.py:297
  448.2 3.2 out_product.9
  453.2 3.2 out_product.11
  456.9 4.5 back_product.9
  461.6 2.3 collective-permute-start.18
  463.9 3.4 back_product.8
  469.1 3.2 out_product.10
  472.3 3.2 out_product.8
  475.5 3.4 back_product.7
  480.6 8.1 %collective-permute-done.11 = bf16[256,1536]{1,0:T(8,128)(2,1)S(1)} collective-permute-done((bf16[256,1536]{1,0:T(8,128)(2,1)S(1)}, bf16[256,1536]{1,0:T(8,128)(2,1)S(1)}, u32[]{:S(2)}, u32[]{:S(2)}) %collective-permute-start.11) | collective-permute-done | bytes 786464 | tf_op jit(solution)/shard_map/ppermute | solution.py:121
  489.1 2.3 collective-permute-start.12
  491.9 12.8 %collective-permute-done.15 = bf16[256,1536]{1,0:T(8,128)(2,1)S(1)} collective-permute-done((bf16[256,1536]{1,0:T(8,128)(2,1)S(1)}, bf16[256,1536]{1,0:T(8,128)(2,1)S(1)}, u32[]{:S(2)}, u32[]{:S(2)}) %collective-permute-start.15) | collective-permute-done | bytes 786464 | tf_op jit(solution)/shard_map/ppermute | solution.py:121
  505.0 2.3 collective-permute-start.16
  509.1 2.9 collective-permute-start.13
  513.9 9.7 %collective-permute-done.16 = bf16[2,64,1536]{2,1,0:T(8,128)(2,1)S(1)} collective-permute-done((bf16[2,64,1536]{2,1,0:T(8,128)(2,1)S(1)}, bf16[2,64,1536]{2,1,0:T(8,128)(2,1)S(1)}, u32[]{:S(2)}, u32[]{:S(2)}) %collective-permute-start.16) | collective-permute-done | bytes 393248 | tf_op jit(solution)/shard_map/ppermute | solution.py:121
  524.0 12.1 %collective-permute-done.17 = bf16[64,1536]{1,0:T(8,128)(2,1)S(1)} collective-permute-done((bf16[64,1536]{1,0:T(8,128)(2,1)S(1)}, bf16[64,1536]{1,0:T(8,128)(2,1)S(1)}, u32[]{:S(2)}, u32[]{:S(2)}) %collective-permute-start.17) | collective-permute-done | bytes 196640 | tf_op jit(solution)/shard_map/ppermute | solution.py:121
  537.2 5.5 all-reduce
  (145 shorter events, 47.5 us)
Async XLA Ops:
  7.2 51.1 %copy-start.25 = (bf16[768,1536]{1,0:T(8,128)(2,1)S(1)}, bf16[768,1536]{1,0:T(8,128)(2,1)}, u32[]{:S(2)}) copy-start(bf16[768,1536]{1,0:T(8,128)(2,1)} %refs_0_.6) | copy-start | bytes 7077892
  7.2 51.1 %all-gather.4.cloned.1.call-start = ((), (), s32[]{:S(2)}) async-start(), calls=%async_computation.5 | async-start | bytes 3342336 | tf_op jit(solution)/shard_map/all_gather | solution.py:330
  9.2 176.4 %all-gather.8.cloned.1.call-start = ((), (), s32[]{:S(2)}) async-start(), calls=%async_computation.7 | async-start | bytes 3342336 | tf_op jit(solution)/shard_map/all_gather | solution.py:330
  16.3 232.6 %all-gather.6.cloned.1.call-start = ((), (), s32[]{:S(2)}) async-start(), calls=%async_computation.6 | async-start | bytes 6684672 | tf_op jit(solution)/shard_map/all_gather | solution.py:330
  65.2 5.6 %copy-start.29 = (s32[4]{0:T(128)S(1)}, s32[4]{0:T(128)}, u32[]{:S(2)}) copy-start(s32[4]{0:T(128)} %constant.59.clone) | copy-start | bytes 52
  65.2 6.3 %copy-start.10 = (bf16[384,3072]{1,0:T(8,128)(2,1)S(1)}, bf16[384,3072]{1,0:T(8,128)(2,1)}, u32[]{:S(2)}) copy-start(bf16[384,3072]{1,0:T(8,128)(2,1)} %refs_3_.1) | copy-start | bytes 7077892
  65.2 109.9 %all-to-all-start = ((bf16[4,768,1152]{2,1,0:T(8,128)(2,1)}), bf16[4,768,1152]{2,1,0:T(8,128)(2,1)}, u32[]{:S(2)}, u32[]{:S(2)}) async-start(bf16[4,768,1152]{2,1,0:T(8,128)(2,1)} %pack.6), calls=%async_computation | async-start | bytes 14155776 | tf_op jit(solution)/shard_map/all_to_all | solution.py:333
  84.6 101.0 %collective-permute-start = (bf16[512,1920]{1,0:T(8,128)(2,1)}, bf16[512,1920]{1,0:T(8,128)(2,1)}, u32[]{:S(2)}, u32[]{:S(2)}) collective-permute-start(bf16[512,1920]{1,0:T(8,128)(2,1)} %cot_product.2), channel_id=1, source_target_pairs={{0,1},{1,0},{2,3},{3,2},{4,5},{5,4},{6,7},{7,6},{8,9},{9,8},{10,11... | collective-permute-start | bytes 5898248 | tf_op jit(solution)/shard_map/ppermute | solution.py:121
  175.1 24.5 %all-to-all-start.1 = ((bf16[4,768,256]{2,1,0:T(8,128)(2,1)}), bf16[4,768,256]{2,1,0:T(8,128)(2,1)}, u32[]{:S(2)}, u32[]{:S(2)}) async-start(bf16[4,768,256]{2,1,0:T(8,128)(2,1)} %copy-done.22), calls=%async_computation.1 | async-start | bytes 3145728 | tf_op jit(solution)/shard_map/all_to_all | solution.py:333
  199.6 55.7 %all-to-all-start.2 = ((bf16[4,768,512]{2,1,0:T(8,128)(2,1)}), bf16[4,768,512]{2,1,0:T(8,128)(2,1)S(1)}, u32[]{:S(2)}, u32[]{:S(2)}) async-start(bf16[4,768,512]{2,1,0:T(8,128)(2,1)} %copy-done.17), calls=%async_computation.2 | async-start | bytes 6291456 | tf_op jit(solution)/shard_map/all_to_all | solution.py:333
  203.3 45.6 %collective-permute-start.1 = (bf16[512,1920]{1,0:T(8,128)(2,1)}, bf16[512,1920]{1,0:T(8,128)(2,1)}, u32[]{:S(2)}, u32[]{:S(2)}) collective-permute-start(bf16[512,1920]{1,0:T(8,128)(2,1)} %copy-done.19), channel_id=1, source_target_pairs={{0,1},{1,0},{2,3},{3,2},{4,5},{5,4},{6,7},{7,6},{8,9},{9,8},{10,11... | collective-permute-start | bytes 5898248 | tf_op jit(solution)/shard_map/ppermute | solution.py:121
  257.0 40.6 %all-to-all-start.3 = ((bf16[4,768,512]{2,1,0:T(8,128)(2,1)}), bf16[4,768,512]{2,1,0:T(8,128)(2,1)S(1)}, u32[]{:S(2)}, u32[]{:S(2)}) async-start(bf16[4,768,512]{2,1,0:T(8,128)(2,1)} %copy-done.18), calls=%async_computation.3 | async-start | bytes 6291456 | tf_op jit(solution)/shard_map/all_to_all | solution.py:333
  275.9 75.8 %collective-permute-start.2 = (bf16[1024,1152]{1,0:T(8,128)(2,1)}, bf16[1024,1152]{1,0:T(8,128)(2,1)}, u32[]{:S(2)}, u32[]{:S(2)}) collective-permute-start(bf16[1024,1152]{1,0:T(8,128)(2,1)} %in_product.6.q_own.k_own.v_own), channel_id=1, source_target_pairs={{0,1},{1,0},{2,3},{3,2},{4,5},{5,4},{6,7},{7,6},{8,9},{9,8},{10,11... | collective-permute-start | bytes 7077896 | tf_op jit(solution)/shard_map/ppermute | solution.py:121
  277.5 63.7 %collective-permute-start.3 = (bf16[1024,256]{1,0:T(8,128)(2,1)}, bf16[1024,256]{1,0:T(8,128)(2,1)}, u32[]{:S(2)}, u32[]{:S(2)}) collective-permute-start(bf16[1024,256]{1,0:T(8,128)(2,1)} %in_product.5), channel_id=1, source_target_pairs={{0,1},{1,0},{2,3},{3,2},{4,5},{5,4},{6,7},{7,6},{8,9},{9,8},{10,11... | collective-permute-start | bytes 1572872 | tf_op jit(solution)/shard_map/ppermute | solution.py:121
  297.6 54.2 %copy-start = (bf16[4,768,512]{2,1,0:T(8,128)(2,1)}, bf16[4,768,512]{2,1,0:T(8,128)(2,1)S(1)}, u32[]{:S(2)}) copy-start(bf16[4,768,512]{2,1,0:T(8,128)(2,1)S(1)} %all-to-all-done.3) | copy-start | bytes 9437188
  297.6 89.0 %all-to-all-start.4 = ((bf16[4,768,256]{2,1,0:T(8,128)(2,1)}), bf16[4,768,256]{2,1,0:T(8,128)(2,1)}, u32[]{:S(2)}, u32[]{:S(2)}) async-start(bf16[4,768,256]{2,1,0:T(8,128)(2,1)} %copy-done.21), calls=%async_computation.4 | async-start | bytes 3145728 | tf_op jit(solution)/shard_map/all_to_all | solution.py:333
  350.1 9.5 %copy-start.23 = (bf16[1024,512]{1,0:T(8,128)(2,1)}, bf16[1024,512]{1,0:T(8,128)(2,1)S(1)}, u32[]{:S(2)}) copy-start(bf16[1024,512]{1,0:T(8,128)(2,1)S(1)} %in_product.8) | copy-start | bytes 3145732
  350.2 10.0 %copy-start.20 = (bf16[512,1920]{1,0:T(8,128)(2,1)S(1)}, bf16[512,1920]{1,0:T(8,128)(2,1)}, u32[]{:S(2)}) copy-start(bf16[512,1920]{1,0:T(8,128)(2,1)} %copy-done.19) | copy-start | bytes 5898244
  350.2 35.5 %collective-permute-start.4 = (bf16[1024,512]{1,0:T(8,128)(2,1)S(1)}, bf16[1024,512]{1,0:T(8,128)(2,1)S(1)}, u32[]{:S(2)}, u32[]{:S(2)}) collective-permute-start(bf16[1024,512]{1,0:T(8,128)(2,1)S(1)} %in_product.8), channel_id=1, source_target_pairs={{0,1},{1,0},{2,3},{3,2},{4,5},{5,4},{6,7},{7,6},{8,9},{9,8},{10,11... | collective-permute-start | bytes 3145736 | tf_op jit(solution)/shard_map/ppermute | solution.py:121
  359.6 66.6 %collective-permute-start.5 = (bf16[1024,512]{1,0:T(8,128)(2,1)}, bf16[1024,512]{1,0:T(8,128)(2,1)}, u32[]{:S(2)}, u32[]{:S(2)}) collective-permute-start(bf16[1024,512]{1,0:T(8,128)(2,1)} %in_product.7), channel_id=1, source_target_pairs={{0,1},{1,0},{2,3},{3,2},{4,5},{5,4},{6,7},{7,6},{8,9},{9,8},{10,11... | collective-permute-start | bytes 3145736 | tf_op jit(solution)/shard_map/ppermute | solution.py:121
  386.6 7.4 %copy-start.5 = (bf16[4,4,64,1920]{3,2,1,0:T(8,128)(2,1)S(1)}, bf16[4,4,64,1920]{3,2,1,0:T(8,128)(2,1)}, u32[]{:S(2)}) copy-start(bf16[4,4,64,1920]{3,2,1,0:T(8,128)(2,1)} %add_parts.1) | copy-start | bytes 11796484
  386.6 7.4 %copy-start.24 = (bf16[1024,512]{1,0:T(8,128)(2,1)S(1)}, bf16[1024,512]{1,0:T(8,128)(2,1)}, u32[]{:S(2)}) copy-start(bf16[1024,512]{1,0:T(8,128)(2,1)} %copy-done.23) | copy-start | bytes 3145732
  386.6 7.4 %copy-start.33 = (bf16[1024,512]{1,0:T(8,128)(2,1)S(1)}, bf16[1024,512]{1,0:T(8,128)(2,1)}, u32[]{:S(2)}) copy-start(bf16[1024,512]{1,0:T(8,128)(2,1)} %copy-done.32) | copy-start | bytes 3145732
  392.5 36.3 %collective-permute-start.6 = (bf16[1024,256]{1,0:T(8,128)(2,1)S(1)}, bf16[1024,256]{1,0:T(8,128)(2,1)S(1)}, u32[]{:S(2)}, u32[]{:S(2)}) collective-permute-start(bf16[1024,256]{1,0:T(8,128)(2,1)S(1)} %in_product.9), channel_id=1, source_target_pairs={{0,1},{1,0},{2,3},{3,2},{4,5},{5,4},{6,7},{7,6},{8,9},{9,8},{10,11... | collective-permute-start | bytes 1572872 | tf_op jit(solution)/shard_map/ppermute | solution.py:121
  428.8 8.8 %copy-start.1 = (bf16[1024,512]{1,0:T(8,128)(2,1)}, bf16[1024,512]{1,0:T(8,128)(2,1)S(1)}, u32[]{:S(2)}) copy-start(bf16[1024,512]{1,0:T(8,128)(2,1)S(1)} %get-tuple-element.53.refs_0_) | copy-start | bytes 3145732
  428.8 8.9 %copy-start.8 = (bf16[1024,512]{1,0:T(8,128)(2,1)}, bf16[1024,512]{1,0:T(8,128)(2,1)S(1)}, u32[]{:S(2)}) copy-start(bf16[1024,512]{1,0:T(8,128)(2,1)S(1)} %get-tuple-element.52.refs_0_) | copy-start | bytes 3145732
  429.5 8.1 %copy-start.12 = (bf16[1024,256]{1,0:T(8,128)(2,1)}, bf16[1024,256]{1,0:T(8,128)(2,1)S(1)}, u32[]{:S(2)}) copy-start(bf16[1024,256]{1,0:T(8,128)(2,1)S(1)} %get-tuple-element.59.refs_1_) | copy-start | bytes 1572868
  429.5 8.2 %copy-start.15 = (bf16[1024,256]{1,0:T(8,128)(2,1)}, bf16[1024,256]{1,0:T(8,128)(2,1)S(1)}, u32[]{:S(2)}) copy-start(bf16[1024,256]{1,0:T(8,128)(2,1)S(1)} %get-tuple-element.58.refs_1_) | copy-start | bytes 1572868
  437.6 8.4 %collective-permute-start.7 = (bf16[512,3072]{1,0:T(8,128)(2,1)}, bf16[512,3072]{1,0:T(8,128)(2,1)S(1)}, u32[]{:S(2)}, u32[]{:S(2)}) collective-permute-start(bf16[512,3072]{1,0:T(8,128)(2,1)} %out_product.7), channel_id=1, source_target_pairs={{0,8},{8,0},{16,24},{24,16},{1,9},{9,1},{17,25},{25,17},{2,10},{10... | collective-permute-start | bytes 9437192 | tf_op jit(solution)/shard_map/ppermute | solution.py:121
  445.4 11.4 %collective-permute-start.14 = (bf16[512,3072]{1,0:T(8,128)(2,1)}, bf16[512,3072]{1,0:T(8,128)(2,1)}, u32[]{:S(2)}, u32[]{:S(2)}) collective-permute-start(bf16[512,3072]{1,0:T(8,128)(2,1)} %back_product.6), channel_id=1, source_target_pairs={{0,8},{8,0},{16,24},{24,16},{1,9},{9,1},{17,25},{25,17},{2,10},{10... | collective-permute-start | bytes 9437192 | tf_op jit(solution)/shard_map/ppermute | solution.py:121
  451.4 5.4 copy-start.9
  451.4 5.4 copy-start.16
  451.4 27.6 %collective-permute-start.8 = (bf16[256,1536]{1,0:T(8,128)(2,1)S(1)}, bf16[256,1536]{1,0:T(8,128)(2,1)}, u32[]{:S(2)}, u32[]{:S(2)}) collective-permute-start(bf16[256,1536]{1,0:T(8,128)(2,1)S(1)} %out_product.9), channel_id=1, source_target_pairs={{0,16},{8,24},{16,0},{24,8},{1,17},{9,25},{17,1},{25,9},{2,18},{10... | collective-permute-start | bytes 2359304 | tf_op jit(solution)/shard_map/ppermute | solution.py:121
  456.4 32.4 %collective-permute-start.11 = (bf16[256,1536]{1,0:T(8,128)(2,1)S(1)}, bf16[256,1536]{1,0:T(8,128)(2,1)S(1)}, u32[]{:S(2)}, u32[]{:S(2)}) collective-permute-start(bf16[256,1536]{1,0:T(8,128)(2,1)S(1)} %out_product.11), channel_id=1, source_target_pairs={{0,16},{8,24},{16,0},{24,8},{1,17},{9,25},{17,1},{25,9},{2,18},{10... | collective-permute-start | bytes 2359304 | tf_op jit(solution)/shard_map/ppermute | solution.py:121
  461.6 7.5 %copy-start.3 = (bf16[1024,512]{1,0:T(8,128)(2,1)S(1)}, bf16[1024,512]{1,0:T(8,128)(2,1)}, u32[]{:S(2)}) copy-start(bf16[1024,512]{1,0:T(8,128)(2,1)} %copy-done.1) | copy-start | bytes 3145732
  461.6 7.5 %copy-start.14 = (bf16[1024,256]{1,0:T(8,128)(2,1)S(1)}, bf16[1024,256]{1,0:T(8,128)(2,1)}, u32[]{:S(2)}) copy-start(bf16[1024,256]{1,0:T(8,128)(2,1)} %copy-done.12) | copy-start | bytes 1572868
  461.6 29.8 %collective-permute-start.18 = (bf16[2,2,64,1536]{3,2,0,1:T(8,128)(2,1)S(1)}, bf16[2,2,64,1536]{3,2,0,1:T(8,128)(2,1)S(1)}, u32[]{:S(2)}, u32[]{:S(2)}) collective-permute-start(bf16[2,2,64,1536]{3,2,0,1:T(8,128)(2,1)S(1)} %select_bitcast_fusion), channel_id=1, source_target_pairs={{0,2},{2,0},{4,6},{6,4},{1,3},{3,1},{5,7},{7,5},{8,10},{10,8},{12,... | collective-permute-start | bytes 2359304 | tf_op jit(solution)/shard_map/ppermute | solution.py:121
  467.4 37.3 %collective-permute-start.15 = (bf16[256,1536]{1,0:T(8,128)(2,1)S(1)}, bf16[256,1536]{1,0:T(8,128)(2,1)S(1)}, u32[]{:S(2)}, u32[]{:S(2)}) collective-permute-start(bf16[256,1536]{1,0:T(8,128)(2,1)S(1)} %back_product.8), channel_id=1, source_target_pairs={{0,16},{8,24},{16,0},{24,8},{1,17},{9,25},{17,1},{25,9},{2,18},{10... | collective-permute-start | bytes 2359304 | tf_op jit(solution)/shard_map/ppermute | solution.py:121
  480.4 26.9 %collective-permute-start.9 = (bf16[2,64,1536]{2,1,0:T(8,128)(2,1)S(1)}, bf16[2,64,1536]{2,1,0:T(8,128)(2,1)S(1)}, u32[]{:S(2)}, u32[]{:S(2)}) collective-permute-start(bf16[2,64,1536]{2,1,0:T(8,128)(2,1)S(1)} %fusion.35), channel_id=1, source_target_pairs={{0,2},{2,0},{4,6},{6,4},{1,3},{3,1},{5,7},{7,5},{8,10},{10,8},{12,... | collective-permute-start | bytes 1179656 | tf_op jit(solution)/shard_map/ppermute | solution.py:121
  489.1 19.1 %collective-permute-start.12 = (bf16[2,64,1536]{2,1,0:T(8,128)(2,1)S(1)}, bf16[2,64,1536]{2,1,0:T(8,128)(2,1)S(1)}, u32[]{:S(2)}, u32[]{:S(2)}) collective-permute-start(bf16[2,64,1536]{2,1,0:T(8,128)(2,1)S(1)} %fusion.36), channel_id=1, source_target_pairs={{0,2},{2,0},{4,6},{6,4},{1,3},{3,1},{5,7},{7,5},{8,10},{10,8},{12,... | collective-permute-start | bytes 1179656 | tf_op jit(solution)/shard_map/ppermute | solution.py:121
  491.8 20.2 %collective-permute-start.19 = (bf16[2,64,1536]{2,1,0:T(8,128)(2,1)S(1)}, bf16[2,64,1536]{2,1,0:T(8,128)(2,1)S(1)}, u32[]{:S(2)}, u32[]{:S(2)}) collective-permute-start(bf16[2,64,1536]{2,1,0:T(8,128)(2,1)S(1)} %fusion.38), channel_id=1, source_target_pairs={{0,4},{2,6},{4,0},{6,2},{1,5},{3,7},{5,1},{7,3},{8,12},{10,14},{12... | collective-permute-start | bytes 1179656 | tf_op jit(solution)/shard_map/ppermute | solution.py:121
  505.0 18.6 %collective-permute-start.16 = (bf16[2,64,1536]{2,1,0:T(8,128)(2,1)S(1)}, bf16[2,64,1536]{2,1,0:T(8,128)(2,1)S(1)}, u32[]{:S(2)}, u32[]{:S(2)}) collective-permute-start(bf16[2,64,1536]{2,1,0:T(8,128)(2,1)S(1)} %fusion.37), channel_id=1, source_target_pairs={{0,2},{2,0},{4,6},{6,4},{1,3},{3,1},{5,7},{7,5},{8,10},{10,8},{12,... | collective-permute-start | bytes 1179656 | tf_op jit(solution)/shard_map/ppermute | solution.py:121
  508.2 34.5 %collective-permute-start.10 = (bf16[64,1536]{1,0:T(8,128)(2,1)}, bf16[64,1536]{1,0:T(8,128)(2,1)S(1)}, u32[]{:S(2)}, u32[]{:S(2)}) collective-permute-start(bf16[64,1536]{1,0:T(8,128)(2,1)} %fusion.40), channel_id=1, source_target_pairs={{0,4},{2,6},{4,0},{6,2},{1,5},{3,7},{5,1},{7,3},{8,12},{10,14},{12... | collective-permute-start | bytes 589832 | tf_op jit(solution)/shard_map/ppermute | solution.py:121
  509.1 34.3 %collective-permute-start.13 = (bf16[64,1536]{1,0:T(8,128)(2,1)}, bf16[64,1536]{1,0:T(8,128)(2,1)S(1)}, u32[]{:S(2)}, u32[]{:S(2)}) collective-permute-start(bf16[64,1536]{1,0:T(8,128)(2,1)} %fusion.41), channel_id=1, source_target_pairs={{0,4},{2,6},{4,0},{6,2},{1,5},{3,7},{5,1},{7,3},{8,12},{10,14},{12... | collective-permute-start | bytes 589832 | tf_op jit(solution)/shard_map/ppermute | solution.py:121
  512.2 11.7 %collective-permute-start.20 = (bf16[64,1536]{1,0:T(8,128)(2,1)S(1)}, bf16[64,1536]{1,0:T(8,128)(2,1)S(1)}, u32[]{:S(2)}, u32[]{:S(2)}) collective-permute-start(bf16[64,1536]{1,0:T(8,128)(2,1)S(1)} %fusion.43), channel_id=1, source_target_pairs={{0,16},{8,24},{16,0},{24,8},{1,17},{9,25},{17,1},{25,9},{2,18},{10... | collective-permute-start | bytes 589832 | tf_op jit(solution)/shard_map/ppermute | solution.py:121
  523.7 13.1 %copy-start.30 = (bf16[64,3072]{1,0:T(8,128)(2,1)S(1)}, bf16[64,3072]{1,0:T(8,128)(2,1)}, u32[]{:S(2)}) copy-start(bf16[64,3072]{1,0:T(8,128)(2,1)} %param.9) | copy-start | bytes 1179652
  523.8 12.3 %collective-permute-start.17 = (bf16[64,1536]{1,0:T(8,128)(2,1)S(1)}, bf16[64,1536]{1,0:T(8,128)(2,1)S(1)}, u32[]{:S(2)}, u32[]{:S(2)}) collective-permute-start(bf16[64,1536]{1,0:T(8,128)(2,1)S(1)} %fusion.42), channel_id=1, source_target_pairs={{0,4},{2,6},{4,0},{6,2},{1,5},{3,7},{5,1},{7,3},{8,12},{10,14},{12... | collective-permute-start | bytes 589832 | tf_op jit(solution)/shard_map/ppermute | solution.py:121
  536.3 7.2 %copy-start.31 = (bf16[64,3072]{1,0:T(8,128)(2,1)S(1)}, bf16[64,3072]{1,0:T(8,128)(2,1)}, u32[]{:S(2)}) copy-start(bf16[64,3072]{1,0:T(8,128)(2,1)} %param.10) | copy-start | bytes 1179652
  (15 other events, 24.5 us)
Sparse Core Ops, SparseCore 0:
  10.3 47.8 all-gather.3
  61.1 52.7 all-gather.7
  116.8 76.2 all-gather.5

commit v11 on v8

--- a/solution.py
+++ b/solution.py
@@ -258,8 +258,10 @@
     out_ref[...] = half(dot(rows_ref[...], weight_ref[...]))
 
 
-def in_product(rows, weight):
+def in_product(rows, weight, half_index=None):
     count, features = rows.shape
+    first = half_index or 0
+    count = count if half_index is None else count // 2
     columns = weight.shape[1]
     tile = 384 if columns % 384 == 0 else 256
     out = jax.ShapeDtypeStruct((count, columns), jnp.bfloat16)
@@ -267,7 +269,7 @@
         in_kernel,
         grid=(columns // tile,),
         in_specs=[
-            pl.BlockSpec((count, features), lambda n: (0, 0)),
+            pl.BlockSpec((count, features), lambda n: (first, 0)),
             pl.BlockSpec((features, tile), lambda n: (0, n)),
         ],
         out_specs=pl.BlockSpec((count, tile), lambda n: (0, n)),
@@ -284,8 +286,10 @@
     tile = 512 if columns % 512 == 0 else 384 if columns % 384 == 0 else 256
     skip = first_column // tile
     specs = [
-        pl.BlockSpec((count, value.shape[1]), lambda n: (start // count, 0))
-        for value, _, _ in terms
+        pl.BlockSpec(
+            (count, value.shape[1]), lambda n, place=(start - row) // count: (place, 0)
+        )
+        for value, _, _, row in terms
     ]
     for weight in weights:
         if transposed:
@@ -301,7 +305,7 @@
     def kernel(*refs):
         weight_refs = refs[len(terms) : len(terms) + len(weights)]
         total = None
-        for ref, (value, index, offset) in zip(refs, terms):
+        for ref, (value, index, offset, _) in zip(refs, terms):
             summed = slice(offset, offset + value.shape[1])
             if transposed:
                 part = back_dot(ref[...], weight_refs[index][:, summed])
@@ -312,7 +316,7 @@
             total = total + ref[...].astype(jnp.float32)
         refs[-1][...] = total.astype(kind)
 
-    depth = sum(value.shape[1] for value, _, _ in terms)
+    depth = sum(value.shape[1] for value, *_ in terms)
     out = jax.ShapeDtypeStruct((count, columns), kind)
     return pl.pallas_call(
         kernel,
@@ -323,11 +327,10 @@
         compiler_params=params(),
         cost_estimate=cost(2 * count * columns * depth, out, *weights),
         name="back_product" if transposed else "out_product",
-    )(*(value for value, _, _ in terms), *weights, *(add for add, _ in adds))
-
-
-MLP_CUTS = (256, 512, 512, 256)
-EARLY_CUTS = 2
+    )(*(value for value, *_ in terms), *weights, *(add for add, _ in adds))
+
+
+MLP_CUTS = (256, 512, 768)
 
 
 def body(layer_input, out_cotangent, w_query, w_key, w_value, w_mlp_in, w_attn_out, w_mlp_out):
@@ -346,10 +349,12 @@
     def with_x(block):
         return jnp.stack([block, trade(block, "gx", 2)])
 
-    def gather_parts(pair):
+    def over_z(pair):
         near, far = trade(pair, "gy", 1), trade(pair, "gy", 2)
-        parts = [pair, near, far, trade(far, "gy", 1)]
-        return [(part, trade(part, "gx", 1)) for part in parts]
+        return [pair, near, far, trade(far, "gy", 1)]
+
+    def with_core(part):
+        return part, trade(part, "gx", 1)
 
     def swap(packed):
         swapped = lax.all_to_all(packed, "gx", split_axis=0, concat_axis=0, tiled=True)
@@ -371,74 +376,77 @@
     normed = (wide - center[:, None]) * inverse[:, None]
     normed_pair = with_x(half(normed))
 
+    cot_parts, normed_parts = over_z(cot_pair), over_z(normed_pair)
+    waits = [(), (normed_parts[1],), (), ()]
     cot_owns, cot_gots = [], []
-    for place, (own, other) in enumerate(gather_parts(cot_pair)):
-        if place >= 2:
-            own = after(own, cot_gots[place - 2])
+    for place, part in enumerate(cot_parts):
+        own, other = with_core(part)
+        own = after(own, *waits[place], *cot_gots[: max(place - 1, 0)])
         cot_owns.append(cot_product((own, other), w_attn_out, w_mlp_out))
         cot_gots.append(others(cot_owns[-1]))
-    all_in = assemble(gather_parts(normed_pair))
+    all_in = assemble([with_core(part) for part in normed_parts])
 
     in_heads = swap(after(packed_heads, normed_pair, cot_owns[0]))
-    in_mlp = [swap(after(packed_mlp[0], in_heads, cot_owns[2]))]
+    in_mlp = [swap(after(packed_mlp[0], in_heads, cot_owns[2], normed_parts[2]))]
     in_mlp.append(swap(after(packed_mlp[1], in_mlp[0], cot_owns[3])))
-    heads_own = in_product(after(all_in, cot_gots[2]), in_heads)
+    heads_own = in_product(after(all_in, cot_gots[1]), in_heads)
     heads_got = others(heads_own)
-    mlp_own = [in_product(after(all_in, cot_gots[3], heads_own), in_mlp[0])]
+    mlp_own = [in_product(after(all_in, cot_gots[2], heads_own), in_mlp[0])]
     mlp_got = [others(mlp_own[0])]
     in_mlp.append(swap(after(packed_mlp[2], in_mlp[1], heads_own)))
-    mlp_own.append(in_product(after(all_in, mlp_own[0]), in_mlp[1]))
+    mlp_own.append(in_product(after(all_in, cot_gots[3], mlp_own[0]), in_mlp[1]))
     mlp_got.append(others(mlp_own[1]))
-    in_mlp.append(swap(after(packed_mlp[3], in_mlp[2], mlp_own[0])))
-    mlp_own.append(in_product(after(all_in, heads_got), in_mlp[2]))
-    mlp_got.append(others(mlp_own[2]))
-
-    out_grad = add_parts(cot_owns, cot_gots)
+
+    out_grad = add_parts(after(cot_owns, mlp_own[0]), cot_gots)
+    late_owns = [in_product(after(all_in, heads_got, out_grad), in_mlp[2], 0)]
+    late_gots = [others(late_owns[0])]
+    late_owns.append(in_product(after(all_in, late_owns[0]), in_mlp[2], 1))
+    late_gots.append(others(late_owns[1]))
+
     mixed, *head_grads = attend(heads_own, heads_got, out_grad)
-    mlp_own.append(in_product(after(all_in, mlp_got[0], mixed), in_mlp[3]))
-    mlp_got.append(others(mlp_own[3]))
-
-    forward_terms, backward_terms = [(mixed, 0, 0)], []
-    for index, grad in enumerate(head_grads):
-        backward_terms.append((grad, 0, index * heads_width))
-
-    def add_terms(cut, own):
-        pre = wide_sum(own, mlp_got[cut])
-        first = heads_width + starts[cut]
-        grad = gelu_back(pre, out_grad[:, first : first + own.shape[1]])
-        forward_terms.append((half(gelu(pre)), 1, starts[cut]))
-        backward_terms.append((grad, 1 + cut, 0))
-
-    out_weights, in_weights = [w_attn_out, w_mlp_out], [in_heads, *in_mlp]
-    for cut in range(EARLY_CUTS):
-        add_terms(cut, mlp_own[cut])
+
+    def mlp_terms(cut, first_row, own, got):
+        pre = wide_sum(own, got)
+        column = heads_width + starts[cut]
+        rows = slice(first_row, first_row + own.shape[0])
+        grad = gelu_back(pre, out_grad[rows, column : column + own.shape[1]])
+        return half(gelu(pre)), grad
+
+    forward_terms = [(after(mixed, late_owns), 0, 0, 0)]
+    backward_terms = [
+        (grad, 0, index * heads_width, 0) for index, grad in enumerate(head_grads)
+    ]
+    for cut in range(2):
+        act, grad = mlp_terms(cut, 0, after(mlp_own[cut], mixed), mlp_got[cut])
+        forward_terms.append((act, 1, starts[cut], 0))
+        backward_terms.append((grad, 1 + cut, 0, 0))
     rows = 4 * count
-    forward_early = product(forward_terms, out_weights, [], 0, rows, jnp.bfloat16, False)
+    forward_early = product(
+        forward_terms, [w_attn_out, w_mlp_out], [], 0, rows, jnp.bfloat16, False
+    )
     backward_early = product(
-        backward_terms, in_weights[: 1 + EARLY_CUTS], [], 0, rows, jnp.bfloat16, True
+        backward_terms, [in_heads, *in_mlp[:2]], [], 0, rows, jnp.bfloat16, True
     )
-    del forward_terms[:], backward_terms[:]
-    for cut in range(EARLY_CUTS, len(MLP_CUTS)):
-        add_terms(cut, after(mlp_own[cut], forward_early, backward_early))
-    late_weights = in_weights[1 + EARLY_CUTS :]
-    backward_terms = [
-        (grad, index - 1 - EARLY_CUTS, offset) for grad, index, offset in backward_terms
-    ]
-    early, all_columns = starts[EARLY_CUTS], sum(MLP_CUTS)
-    late_rows = (early // (all_columns - early), all_columns - early)
-    forward_terms = [(act, 0, offset - early) for act, _, offset in forward_terms]
+    forward_late, backward_late = [], []
+
+    def add_late(part, *earlier):
+        first_row = part * 2 * count
+        own = after(late_owns[part], *earlier)
+        act, grad = mlp_terms(2, first_row, own, late_gots[part])
+        forward_late.append([(act, 0, 0, first_row)])
+        backward_late.append([(grad, 0, 0, first_row)])
+
+    late_rows = (starts[2] // MLP_CUTS[2], MLP_CUTS[2])
 
     def forward_term(start, size, adds, window=None):
-        adds = [(forward_early, start), *adds]
+        adds, terms = [(forward_early, start), *adds], forward_late[start // (2 * count)]
         return product(
-            forward_terms, [w_mlp_out], adds, start, size, jnp.bfloat16, False, window, late_rows
+            terms, [w_mlp_out], adds, start, size, jnp.bfloat16, False, window, late_rows
         )
 
     def backward_term(start, size, adds, window=None):
-        adds = [(backward_early, start), *adds]
-        return product(
-            backward_terms, late_weights, adds, start, size, jnp.bfloat16, True, window
-        )
+        adds, terms = [(backward_early, start), *adds], backward_late[start // (2 * count)]
+        return product(terms, [in_mlp[2]], adds, start, size, jnp.bfloat16, True, window)
 
     def wider(value):
         return value.astype(jnp.float32)
@@ -457,14 +465,21 @@
         ends = pair[:, 0] + wider(trade(half(pair[:, 1]), "gy", 2))
         return ends[1] + wider(trade(half(ends[0]), "gx", 2))
 
-    def spread_rows(term, ways):
+    add_late(0, forward_early, backward_early)
+    forward_to_core = forward_term(0, 2 * count, [])
+    (grad, *where), *_ = backward_late[0]
+    backward_late[0] = [(after(grad, late_gots[1]), *where)]
+    to_cores = forward_to_core, backward_term(0, 2 * count, [])
+    add_late(1, *to_cores)
+
+    def spread_rows(term, to_core, ways):
         width = features // len(ways)
-        from_core = trade(term(0, 2 * count, []), "gx", 1)
+        from_core = trade(to_core, "gx", 1)
         sums = [way(term, from_core, (place * width, width)) for place, way in enumerate(ways)]
         return jnp.concatenate(sums, axis=1)
 
-    normed_grad = spread_rows(backward_term, (over_x_z, over_z_x))
-    layer_out = half(wide + spread_rows(forward_term, (over_x_z, over_x_z)))
+    normed_grad = spread_rows(backward_term, to_cores[1], (over_x_z, over_z_x))
+    layer_out = half(wide + spread_rows(forward_term, to_cores[0], (over_x_z, over_x_z)))
     first, second = lax.psum(
         (jnp.sum(normed_grad, axis=1), jnp.sum(normed_grad * normed, axis=1)), "gz"
     )

time: 547 us -> 525 us (0.960)
  waiting for transfers between devices: 237 us -> 221 us
    all_to_all x5 -> x4, waiting for transfers between devices: 25.5 us -> 2.72 us  [swap(): lax.all_to_all(packed, 'gx', split_axis=0, concat_axis=0, tiled=True)]
    ppermute x39, waiting for transfers between devices: 212 us -> 218 us  [trade(): return lax.ppermute(block, axis, pairs)]
    unnamed x79 -> x81, local copies, waits for them, and re-layouts: 25.1 us -> 20.3 us
    all_to_all x5 -> x4, starting transfers between devices: 21.7 us -> 19.5 us  [swap(): lax.all_to_all(packed, 'gx', split_axis=0, concat_axis=0, tiled=True)]
    pallas_call x5 -> x4, Pallas kernels: 18.7 us -> 18.6 us  [pack(): pl.pallas_call(pack_kernel, grid=(owners, width // tile), in_specs=[spec]...]
  transfers between devices with their start and end apart: 44 -> 43, of which waited for: 13 -> 13; matrix products, arithmetic and copies ran while one was open for 3% -> 3% of each run, Pallas kernels for 31% -> 34%
where the time goes in v11:
time: 525 us; the launch traced here: 523 us
  waiting for transfers between devices  221 us (42%)
  Pallas kernels  184 us (35%)
  starting transfers between devices  65.8 us (13%)
  local copies, waits for them, and re-layouts  20.6 us (4%)
  other arithmetic  19.3 us (4%)
  blocking collectives  10.5 us (2%)
    ppermute x39, waiting for transfers between devices, trade(): return lax.ppermute(block, axis, pairs)  218 us
    pallas_call x11, Pallas kernels, product(): pl.pallas_call(kernel, grid=(columns // tile,), in_specs=specs, out_specs...  68.7 us
    ppermute x39, starting transfers between devices, trade(): return lax.ppermute(block, axis, pairs)  46.3 us
    pallas_call x5, Pallas kernels, in_product(): pl.pallas_call(in_kernel, grid=(columns // tile,), in_specs=[pl.BlockSpec...  39.4 us
    pallas_call x4, Pallas kernels, cot_product(): pl.pallas_call(cot_kernel, grid=(columns // tile,), in_specs=[whole, whol...  33.4 us
    unnamed x81, local copies, waits for them, and re-layouts  20.3 us
    all_to_all x4, starting transfers between devices, swap(): lax.all_to_all(packed, 'gx', split_axis=0, concat_axis=0, tiled=True)  19.5 us
    pallas_call x4, Pallas kernels, pack(): pl.pallas_call(pack_kernel, grid=(owners, width // tile), in_specs=[spec]...  18.6 us
  transfers between devices with their start and end apart: 43, of which 13 were waited for; matrix products, arithmetic and copies ran while one was open for 3% of the time, Pallas kernels for 34%

profile of v11, /device:TPU:0, one launch (start us, length us, event | category | flops | bytes accessed | tf_op | source)
XLA Modules:
  0.0 522.8 jit_solution(14143265515585949968)
XLA Ops:
  0.6 3.0 collective-permute-start.8
  4.8 4.9 all-reduce.1
  14.4 5.2 pack.4
  22.4 8.2 %cot_product.5 = bf16[256,1920]{1,0:T(8,128)(2,1)S(1)} custom-call(bf16[2,64,3072]{2,1,0:T(8,128)(2,1)S(1)} %pad_maximum_fusion.1.own_ref, bf16[2,64,3072]{2,1,0:T(8,128)(2,1)S(1)} %collective-permute-done.12.other_ref, bf16[384,3072]{1,0:T(8,128)(2,1)S(1)} %copy-done, bf16[1536,3072]{1,0:T(8,128)(2,1)} %refs_1_.11), custom_call_target="tpu_custom_call" | custom-call | flops 47185920 | bytes 199680 | tf_op jit(solution)/shard_map/cot_product/pallas_call | solution.py:214
  30.5 5.4 %all-to-all-start = ((bf16[4,768,1152]{2,1,0:T(8,128)(2,1)}), bf16[4,768,1152]{2,1,0:T(8,128)(2,1)}, u32[]{:S(2)}, u32[]{:S(2)}) async-start(bf16[4,768,1152]{2,1,0:T(8,128)(2,1)} %pack.4), calls=%async_computation | async-start | bytes 14155776 | tf_op jit(solution)/shard_map/all_to_all | solution.py:360
  35.9 2.9 collective-permute-start.14
  42.0 32.2 %collective-permute-done.14.own_ref = bf16[2,64,3072]{2,1,0:T(8,128)(2,1)} collective-permute-done((bf16[2,64,3072]{2,1,0:T(8,128)(2,1)}, bf16[2,64,3072]{2,1,0:T(8,128)(2,1)}, u32[]{:S(2)}, u32[]{:S(2)}) %collective-permute-start.14) | collective-permute-done | bytes 786464 | tf_op jit(solution)/shard_map/ppermute | solution.py:121
  74.2 4.0 collective-permute-start.2
  82.8 8.3 %cot_product.6 = bf16[256,1920]{1,0:T(8,128)(2,1)S(1)} custom-call(bf16[2,64,3072]{2,1,0:T(8,128)(2,1)} %collective-permute-done.14.own_ref, bf16[2,64,3072]{2,1,0:T(8,128)(2,1)S(1)} %collective-permute-done.16.other_ref, bf16[384,3072]{1,0:T(8,128)(2,1)S(1)} %copy-done, bf16[1536,3072]{1,0:T(8,128)(2,1)} %refs_1_.11), custom_call_target="tpu_custom_call" | custom-call | flops 47185920 | bytes 199680 | tf_op jit(solution)/shard_map/cot_product/pallas_call | solution.py:214
  91.1 21.2 %collective-permute-done.4.refs_4_ = bf16[2,64,3072]{2,1,0:T(8,128)(2,1)} collective-permute-done((bf16[2,64,3072]{2,1,0:T(8,128)(2,1)}, bf16[2,64,3072]{2,1,0:T(8,128)(2,1)}, u32[]{:S(2)}, u32[]{:S(2)}) %collective-permute-start.4) | collective-permute-done | bytes 786464 | tf_op jit(solution)/shard_map/ppermute | solution.py:121
  112.4 2.7 all-to-all-done
  115.1 4.4 all-to-all-start.1
  119.5 8.6 %cot_product.4 = bf16[256,1920]{1,0:T(8,128)(2,1)S(1)} custom-call(bf16[2,64,3072]{2,1,0:T(8,128)(2,1)} %collective-permute-done.9.own_ref, bf16[2,64,3072]{2,1,0:T(8,128)(2,1)} %collective-permute-done.10.other_ref, bf16[384,3072]{1,0:T(8,128)(2,1)S(1)} %copy-done, bf16[1536,3072]{1,0:T(8,128)(2,1)} %refs_1_.11), custom_call_target="tpu_custom_call" | custom-call | flops 47185920 | bytes 199680 | tf_op jit(solution)/shard_map/cot_product/pallas_call | solution.py:214
  130.1 4.5 pack.7
  136.3 16.0 %collective-permute-done.11 = bf16[256,1920]{1,0:T(8,128)(2,1)S(1)} collective-permute-done((bf16[256,1920]{1,0:T(8,128)(2,1)S(1)}, bf16[256,1920]{1,0:T(8,128)(2,1)S(1)}, u32[]{:S(2)}, u32[]{:S(2)}) %collective-permute-start.11) | collective-permute-done | bytes 983072 | tf_op jit(solution)/shard_map/ppermute | solution.py:121
  153.2 8.3 %cot_product.7 = bf16[256,1920]{1,0:T(8,128)(2,1)S(1)} custom-call(bf16[2,64,3072]{2,1,0:T(8,128)(2,1)} %collective-permute-done.17.own_ref, bf16[2,64,3072]{2,1,0:T(8,128)(2,1)S(1)} %collective-permute-done.18.other_ref, bf16[384,3072]{1,0:T(8,128)(2,1)S(1)} %copy-done, bf16[1536,3072]{1,0:T(8,128)(2,1)} %refs_1_.11), custom_call_target="tpu_custom_call" | custom-call | flops 47185920 | bytes 199680 | tf_op jit(solution)/shard_map/cot_product/pallas_call | solution.py:214
  162.5 4.6 all-to-all-start.2
  169.7 17.7 %collective-permute-done.6.refs_6_ = bf16[2,64,3072]{2,1,0:T(8,128)(2,1)S(1)} collective-permute-done((bf16[2,64,3072]{2,1,0:T(8,128)(2,1)}, bf16[2,64,3072]{2,1,0:T(8,128)(2,1)S(1)}, u32[]{:S(2)}, u32[]{:S(2)}) %collective-permute-start.6) | collective-permute-done | bytes 786464 | tf_op jit(solution)/shard_map/ppermute | solution.py:121
  187.4 6.7 %pack.6 = bf16[4,768,768]{2,1,0:T(8,128)(2,1)S(1)} custom-call(bf16[768,6144]{1,0:T(8,128)(2,1)} %refs_0_.7), custom_call_target="tpu_custom_call" | custom-call | bytes 147456 | tf_op jit(solution)/shard_map/pack/pallas_call | solution.py:148
  197.2 5.0 assemble.1.rows_ref
  202.1 14.0 %in_product.5.q_own.k_own.v_own = bf16[1024,1152]{1,0:T(8,128)(2,1)S(1)} custom-call(bf16[1024,3072]{1,0:T(8,128)(2,1)} %assemble.1.rows_ref, bf16[3072,1152]{1,0:T(8,128)(2,1)} %bitcast.4.weight_ref.refs_5_), custom_call_target="tpu_custom_call" | custom-call | flops 113246208 | bytes 245760 | tf_op jit(solution)/shard_map/in_product/pallas_call | solution.py:268
  217.5 5.1 all-to-all-start.3
  226.4 71.7 %collective-permute-done.19 = bf16[256,1920]{1,0:T(8,128)(2,1)} collective-permute-done((bf16[256,1920]{1,0:T(8,128)(2,1)S(1)}, bf16[256,1920]{1,0:T(8,128)(2,1)}, u32[]{:S(2)}, u32[]{:S(2)}) %collective-permute-start.19) | collective-permute-done | bytes 983072 | tf_op jit(solution)/shard_map/ppermute | solution.py:121
  298.1 5.8 %in_product.6 = bf16[1024,256]{1,0:T(8,128)(2,1)} custom-call(bf16[1024,3072]{1,0:T(8,128)(2,1)} %assemble.1.rows_ref, bf16[3072,256]{1,0:T(8,128)(2,1)} %bitcast.5.weight_ref.refs_6_), custom_call_target="tpu_custom_call" | custom-call | flops 25165824 | bytes 131072 | tf_op jit(solution)/shard_map/in_product/pallas_call | solution.py:268
  304.0 14.9 %collective-permute-done.20 = bf16[256,1920]{1,0:T(8,128)(2,1)} collective-permute-done((bf16[256,1920]{1,0:T(8,128)(2,1)}, bf16[256,1920]{1,0:T(8,128)(2,1)}, u32[]{:S(2)}, u32[]{:S(2)}) %collective-permute-start.20) | collective-permute-done | bytes 983072 | tf_op jit(solution)/shard_map/ppermute | solution.py:121
  318.8 6.9 %in_product.9 = bf16[1024,512]{1,0:T(8,128)(2,1)S(1)} custom-call(bf16[1024,3072]{1,0:T(8,128)(2,1)} %assemble.1.rows_ref, bf16[3072,512]{1,0:T(8,128)(2,1)} %bitcast.15.weight_ref.refs_7_), custom_call_target="tpu_custom_call" | custom-call | flops 50331648 | bytes 163840 | tf_op jit(solution)/shard_map/in_product/pallas_call | solution.py:268
  327.9 4.5 add_parts.1
  333.8 6.4 %in_product.7 = bf16[512,768]{1,0:T(8,128)(2,1)S(1)} custom-call(bf16[1024,3072]{1,0:T(8,128)(2,1)} %assemble.1.rows_ref, bf16[3072,768]{1,0:T(8,128)(2,1)} %bitcast.16.weight_ref.refs_1_), custom_call_target="tpu_custom_call" | custom-call | flops 37748736 | bytes 184320 | tf_op jit(solution)/shard_map/in_product/pallas_call | solution.py:268
  343.7 14.9 %attend.1 = (bf16[1024,384]{1,0:T(8,128)(2,1)S(1)}, bf16[1024,384]{1,0:T(8,128)(2,1)S(1)}, bf16[1024,384]{1,0:T(8,128)(2,1)S(1)}, bf16[1024,384]{1,0:T(8,128)(2,1)S(1)}) custom-call(bf16[1024,1152]{1,0:T(8,128)(2,1)S(1)} %copy-done.2, bf16[1024,1152]{1,0:T(8,128)(2,1)S(1)} %copy-done.5, bf16[1024,1152]{1,0:T(8,128)(2,1)S(1)} %copy-done.2, ...), custom_call_target="tpu_custom_call" | custom-call | flops 12582912 | bytes 98304 | tf_op jit(solution)/shard_map/attend/pallas_call | solution.py:75
  365.1 6.3 %in_product.8 = bf16[512,768]{1,0:T(8,128)(2,1)S(1)} custom-call(bf16[1024,3072]{1,0:T(8,128)(2,1)} %assemble.1.rows_ref, bf16[3072,768]{1,0:T(8,128)(2,1)} %bitcast.16.weight_ref.refs_1_), custom_call_target="tpu_custom_call" | custom-call | flops 37748736 | bytes 184320 | tf_op jit(solution)/shard_map/in_product/pallas_call | solution.py:268
  375.7 18.5 %back_product.5.refs_2_ = bf16[1024,3072]{1,0:T(8,128)(2,1)} custom-call(bf16[1024,384]{1,0:T(8,128)(2,1)S(1)} %copy-done.30, bf16[1024,384]{1,0:T(8,128)(2,1)S(1)} %copy-done.32, bf16[1024,384]{1,0:T(8,128)(2,1)S(1)} %copy-done.34, bf16[1024,256]{1,0:T(8,128)(2,1)S(1)} %get-tuple-element.72.refs_3_, bf16[1024,512]{1,0:T(8,128)(2,1)S(1)} %get-tuple-element.64.refs_4_, ...), custom_call_target="tpu_custom_call" | custom-call | flops 188743680 | bytes 282624 | tf_op jit(solution)/shard_map/back_product/pallas_call | solution.py:321
  394.2 12.3 %out_product.6.refs_2_ = bf16[1024,3072]{1,0:T(8,128)(2,1)} custom-call(bf16[1024,384]{1,0:T(8,128)(2,1)S(1)} %copy-done.28, bf16[1024,256]{1,0:T(8,128)(2,1)S(1)} %get-tuple-element.73.refs_1_, bf16[1024,512]{1,0:T(8,128)(2,1)S(1)} %get-tuple-element.65.refs_2_, bf16[384,3072]{1,0:T(8,128)(2,1)S(1)} %copy-done, bf16[1536,3072]{1,0:T(8,128)(2,1)} %refs_1_.11), custom_call_target="tpu_custom_call" | custom-call | flops 113246208 | bytes 282624 | tf_op jit(solution)/shard_map/out_product/pallas_call | solution.py:321
  408.6 7.7 %out_product.7 = bf16[512,3072]{1,0:T(8,128)(2,1)} custom-call(bf16[512,768]{1,0:T(8,128)(2,1)S(1)} %get-tuple-element.71.refs_0_, bf16[1536,3072]{1,0:T(8,128)(2,1)} %refs_1_.11, bf16[1024,3072]{1,0:T(8,128)(2,1)} %out_product.6.refs_2_), custom_call_target="tpu_custom_call" | custom-call | flops 37748736 | bytes 196608 | tf_op jit(solution)/shard_map/out_product/pallas_call | solution.py:321
  416.3 6.9 %back_product.6 = bf16[512,3072]{1,0:T(8,128)(2,1)S(1)} custom-call(bf16[512,768]{1,0:T(8,128)(2,1)S(1)} %get-tuple-element.52.refs_0_, bf16[3072,768]{1,0:T(8,128)(2,1)} %bitcast.16.weight_ref.refs_1_, bf16[1024,3072]{1,0:T(8,128)(2,1)} %back_product.5.refs_2_), custom_call_target="tpu_custom_call" | custom-call | flops 37748736 | bytes 122880 | tf_op jit(solution)/shard_map/back_product/pallas_call | solution.py:321
  425.9 3.2 out_product.9
  430.9 3.2 out_product.11
  434.5 3.9 back_product.9
  440.3 3.3 back_product.8
  445.3 3.2 out_product.10
  448.5 3.2 out_product.8
  451.7 3.3 back_product.7
  456.9 9.5 %collective-permute-done.29 = bf16[256,1536]{1,0:T(8,128)(2,1)S(1)} collective-permute-done((bf16[256,1536]{1,0:T(8,128)(2,1)S(1)}, bf16[256,1536]{1,0:T(8,128)(2,1)S(1)}, u32[]{:S(2)}, u32[]{:S(2)}) %collective-permute-start.29) | collective-permute-done | bytes 786464 | tf_op jit(solution)/shard_map/ppermute | solution.py:121
  468.7 2.7 collective-permute-start.37
  471.3 11.1 %collective-permute-done.33 = bf16[256,1536]{1,0:T(8,128)(2,1)S(1)} collective-permute-done((bf16[256,1536]{1,0:T(8,128)(2,1)S(1)}, bf16[256,1536]{1,0:T(8,128)(2,1)S(1)}, u32[]{:S(2)}, u32[]{:S(2)}) %collective-permute-start.33) | collective-permute-done | bytes 786464 | tf_op jit(solution)/shard_map/ppermute | solution.py:121
  484.4 2.7 collective-permute-start.28
  489.4 11.9 %collective-permute-done.34 = bf16[2,64,1536]{2,1,0:T(8,128)(2,1)S(1)} collective-permute-done((bf16[2,64,1536]{2,1,0:T(8,128)(2,1)S(1)}, bf16[2,64,1536]{2,1,0:T(8,128)(2,1)S(1)}, u32[]{:S(2)}, u32[]{:S(2)}) %collective-permute-start.34) | collective-permute-done | bytes 393248 | tf_op jit(solution)/shard_map/ppermute | solution.py:121
  503.2 9.2 %collective-permute-done.35 = bf16[64,1536]{1,0:T(8,128)(2,1)S(1)} collective-permute-done((bf16[64,1536]{1,0:T(8,128)(2,1)S(1)}, bf16[64,1536]{1,0:T(8,128)(2,1)S(1)}, u32[]{:S(2)}, u32[]{:S(2)}) %collective-permute-start.35) | collective-permute-done | bytes 196640 | tf_op jit(solution)/shard_map/ppermute | solution.py:121
  513.4 5.6 %all-reduce = (f32[64]{0:T(128)S(1)}, f32[64]{0:T(128)}) all-reduce(f32[64]{0:T(128)S(1)} %fusion.28, f32[64]{0:T(128)} %reduce_sum.48), channel_id=1, replica_groups=mesh['gx'=4,'gy'=4,'gz'=2] {'gz'}, use_global_device_ids=true, to_apply=%region_8.9 | all-reduce | flops 128 | bytes 1024 | tf_op jit(solution)/shard_map/psum | solution.py:483
  (183 shorter events, 75.7 us)
Async XLA Ops:
  0.6 19.0 %collective-permute-start.8 = (bf16[64,3072]{1,0:T(8,128)(2,1)}, bf16[64,3072]{1,0:T(8,128)(2,1)S(1)}, u32[]{:S(2)}, u32[]{:S(2)}) collective-permute-start(bf16[64,3072]{1,0:T(8,128)(2,1)} %param.9), channel_id=1, source_target_pairs={{0,16},{8,24},{16,0},{24,8},{1,17},{9,25},{17,1},{25,9},{2,18},{10... | collective-permute-start | bytes 1179656 | tf_op jit(solution)/shard_map/ppermute | solution.py:121
  10.9 10.4 %collective-permute-start = (bf16[64,3072]{1,0:T(8,128)(2,1)S(1)}, bf16[64,3072]{1,0:T(8,128)(2,1)S(1)}, u32[]{:S(2)}, u32[]{:S(2)}) collective-permute-start(bf16[64,3072]{1,0:T(8,128)(2,1)S(1)} %fusion.27), channel_id=1, source_target_pairs={{0,16},{8,24},{16,0},{24,8},{1,17},{9,25},{17,1},{25,9},{2,18},{10... | collective-permute-start | bytes 1179656 | tf_op jit(solution)/shard_map/ppermute | solution.py:121
  19.7 2.6 collective-permute-start.12
  30.5 84.5 %all-to-all-start = ((bf16[4,768,1152]{2,1,0:T(8,128)(2,1)}), bf16[4,768,1152]{2,1,0:T(8,128)(2,1)}, u32[]{:S(2)}, u32[]{:S(2)}) async-start(bf16[4,768,1152]{2,1,0:T(8,128)(2,1)} %pack.4), calls=%async_computation | async-start | bytes 14155776 | tf_op jit(solution)/shard_map/all_to_all | solution.py:360
  35.9 38.3 %collective-permute-start.14 = (bf16[2,64,3072]{2,1,0:T(8,128)(2,1)}, bf16[2,64,3072]{2,1,0:T(8,128)(2,1)}, u32[]{:S(2)}, u32[]{:S(2)}) collective-permute-start(bf16[2,64,3072]{2,1,0:T(8,128)(2,1)} %copy-done.18), channel_id=1, source_target_pairs={{0,4},{2,6},{4,0},{6,2},{1,5},{3,7},{5,1},{7,3},{8,12},{10,14},{12... | collective-permute-start | bytes 2359304 | tf_op jit(solution)/shard_map/ppermute | solution.py:121
  38.9 39.4 %collective-permute-start.9 = (bf16[2,64,3072]{2,1,0:T(8,128)(2,1)}, bf16[2,64,3072]{2,1,0:T(8,128)(2,1)}, u32[]{:S(2)}, u32[]{:S(2)}) collective-permute-start(bf16[2,64,3072]{2,1,0:T(8,128)(2,1)} %copy-done.18), channel_id=1, source_target_pairs={{0,2},{2,0},{4,6},{6,4},{1,3},{3,1},{5,7},{7,5},{8,10},{10,8},{12,... | collective-permute-start | bytes 2359304 | tf_op jit(solution)/shard_map/ppermute | solution.py:121
  40.4 37.8 %collective-permute-start.15 = (bf16[256,1920]{1,0:T(8,128)(2,1)S(1)}, bf16[256,1920]{1,0:T(8,128)(2,1)S(1)}, u32[]{:S(2)}, u32[]{:S(2)}) collective-permute-start(bf16[256,1920]{1,0:T(8,128)(2,1)S(1)} %cot_product.5), channel_id=1, source_target_pairs={{0,1},{1,0},{2,3},{3,2},{4,5},{5,4},{6,7},{7,6},{8,9},{9,8},{10,11... | collective-permute-start | bytes 2949128 | tf_op jit(solution)/shard_map/ppermute | solution.py:121
  74.2 8.6 %collective-permute-start.16 = (bf16[2,64,3072]{2,1,0:T(8,128)(2,1)}, bf16[2,64,3072]{2,1,0:T(8,128)(2,1)S(1)}, u32[]{:S(2)}, u32[]{:S(2)}) collective-permute-start(bf16[2,64,3072]{2,1,0:T(8,128)(2,1)} %collective-permute-done.14.own_ref), channel_id=1, source_target_pairs={{0,8},{8,0},{16,24},{24,16},{1,9},{9,1},{17,25},{25,17},{2,10},{10... | collective-permute-start | bytes 2359304 | tf_op jit(solution)/shard_map/ppermute | solution.py:121
  74.2 38.1 %collective-permute-start.4 = (bf16[2,64,3072]{2,1,0:T(8,128)(2,1)}, bf16[2,64,3072]{2,1,0:T(8,128)(2,1)}, u32[]{:S(2)}, u32[]{:S(2)}) collective-permute-start(bf16[2,64,3072]{2,1,0:T(8,128)(2,1)} %pad_maximum_fusion.refs_0_), channel_id=1, source_target_pairs={{0,4},{2,6},{4,0},{6,2},{1,5},{3,7},{5,1},{7,3},{8,12},{10,14},{12... | collective-permute-start | bytes 2359304 | tf_op jit(solution)/shard_map/ppermute | solution.py:121
  74.2 45.2 %collective-permute-start.2 = (bf16[2,64,3072]{2,1,0:T(8,128)(2,1)}, bf16[2,64,3072]{2,1,0:T(8,128)(2,1)}, u32[]{:S(2)}, u32[]{:S(2)}) collective-permute-start(bf16[2,64,3072]{2,1,0:T(8,128)(2,1)} %pad_maximum_fusion.refs_0_), channel_id=1, source_target_pairs={{0,2},{2,0},{4,6},{6,4},{1,3},{3,1},{5,7},{7,5},{8,10},{10,8},{12,... | collective-permute-start | bytes 2359304 | tf_op jit(solution)/shard_map/ppermute | solution.py:121
  78.3 41.2 %collective-permute-start.10 = (bf16[2,64,3072]{2,1,0:T(8,128)(2,1)}, bf16[2,64,3072]{2,1,0:T(8,128)(2,1)}, u32[]{:S(2)}, u32[]{:S(2)}) collective-permute-start(bf16[2,64,3072]{2,1,0:T(8,128)(2,1)} %collective-permute-done.9.own_ref), channel_id=1, source_target_pairs={{0,8},{8,0},{16,24},{24,16},{1,9},{9,1},{17,25},{25,17},{2,10},{10... | collective-permute-start | bytes 2359304 | tf_op jit(solution)/shard_map/ppermute | solution.py:121
  79.2 50.7 %collective-permute-start.17 = (bf16[2,64,3072]{2,1,0:T(8,128)(2,1)}, bf16[2,64,3072]{2,1,0:T(8,128)(2,1)}, u32[]{:S(2)}, u32[]{:S(2)}) collective-permute-start(bf16[2,64,3072]{2,1,0:T(8,128)(2,1)} %collective-permute-done.14.own_ref), channel_id=1, source_target_pairs={{0,2},{2,0},{4,6},{6,4},{1,3},{3,1},{5,7},{7,5},{8,10},{10,8},{12,... | collective-permute-start | bytes 2359304 | tf_op jit(solution)/shard_map/ppermute | solution.py:121
  91.1 133.3 %copy-start.11 = (bf16[256,1920]{1,0:T(8,128)(2,1)}, bf16[256,1920]{1,0:T(8,128)(2,1)S(1)}, u32[]{:S(2)}) copy-start(bf16[256,1920]{1,0:T(8,128)(2,1)S(1)} %cot_product.6) | copy-start | bytes 2949124
  115.1 47.5 %all-to-all-start.1 = ((bf16[4,768,256]{2,1,0:T(8,128)(2,1)}), bf16[4,768,256]{2,1,0:T(8,128)(2,1)}, u32[]{:S(2)}, u32[]{:S(2)}) async-start(bf16[4,768,256]{2,1,0:T(8,128)(2,1)} %copy-done.8), calls=%async_computation.1 | async-start | bytes 3145728 | tf_op jit(solution)/shard_map/all_to_all | solution.py:360
  128.1 24.2 %collective-permute-start.11 = (bf16[256,1920]{1,0:T(8,128)(2,1)S(1)}, bf16[256,1920]{1,0:T(8,128)(2,1)S(1)}, u32[]{:S(2)}, u32[]{:S(2)}) collective-permute-start(bf16[256,1920]{1,0:T(8,128)(2,1)S(1)} %cot_product.4), channel_id=1, source_target_pairs={{0,1},{1,0},{2,3},{3,2},{4,5},{5,4},{6,7},{7,6},{8,9},{9,8},{10,11... | collective-permute-start | bytes 2949128 | tf_op jit(solution)/shard_map/ppermute | solution.py:121
  129.9 23.3 %collective-permute-start.18 = (bf16[2,64,3072]{2,1,0:T(8,128)(2,1)}, bf16[2,64,3072]{2,1,0:T(8,128)(2,1)S(1)}, u32[]{:S(2)}, u32[]{:S(2)}) collective-permute-start(bf16[2,64,3072]{2,1,0:T(8,128)(2,1)} %collective-permute-done.17.own_ref), channel_id=1, source_target_pairs={{0,8},{8,0},{16,24},{24,16},{1,9},{9,1},{17,25},{25,17},{2,10},{10... | collective-permute-start | bytes 2359304 | tf_op jit(solution)/shard_map/ppermute | solution.py:121
  162.5 55.0 %all-to-all-start.2 = ((bf16[4,768,512]{2,1,0:T(8,128)(2,1)}), bf16[4,768,512]{2,1,0:T(8,128)(2,1)}, u32[]{:S(2)}, u32[]{:S(2)}) async-start(bf16[4,768,512]{2,1,0:T(8,128)(2,1)} %copy-done.7), calls=%async_computation.2 | async-start | bytes 6291456 | tf_op jit(solution)/shard_map/all_to_all | solution.py:360
  167.2 30.0 %copy-start.17 = (bf16[2,64,3072]{2,1,0:T(8,128)(2,1)S(1)}, bf16[2,64,3072]{2,1,0:T(8,128)(2,1)}, u32[]{:S(2)}) copy-start(bf16[2,64,3072]{2,1,0:T(8,128)(2,1)} %pad_maximum_fusion.refs_0_) | copy-start | bytes 2359300
  167.2 20.2 %collective-permute-start.6 = (bf16[2,64,3072]{2,1,0:T(8,128)(2,1)}, bf16[2,64,3072]{2,1,0:T(8,128)(2,1)S(1)}, u32[]{:S(2)}, u32[]{:S(2)}) collective-permute-start(bf16[2,64,3072]{2,1,0:T(8,128)(2,1)} %collective-permute-done.4.refs_4_), channel_id=1, source_target_pairs={{0,2},{2,0},{4,6},{6,4},{1,3},{3,1},{5,7},{7,5},{8,10},{10,8},{12,... | collective-permute-start | bytes 2359304 | tf_op jit(solution)/shard_map/ppermute | solution.py:121
  169.1 27.1 %collective-permute-start.1 = (bf16[2,64,3072]{2,1,0:T(8,128)(2,1)}, bf16[2,64,3072]{2,1,0:T(8,128)(2,1)S(1)}, u32[]{:S(2)}, u32[]{:S(2)}) collective-permute-start(bf16[2,64,3072]{2,1,0:T(8,128)(2,1)} %pad_maximum_fusion.refs_0_), channel_id=1, source_target_pairs={{0,8},{8,0},{16,24},{24,16},{1,9},{9,1},{17,25},{25,17},{2,10},{10... | collective-permute-start | bytes 2359304 | tf_op jit(solution)/shard_map/ppermute | solution.py:121
  169.2 27.0 %collective-permute-start.5 = (bf16[2,64,3072]{2,1,0:T(8,128)(2,1)}, bf16[2,64,3072]{2,1,0:T(8,128)(2,1)S(1)}, u32[]{:S(2)}, u32[]{:S(2)}) collective-permute-start(bf16[2,64,3072]{2,1,0:T(8,128)(2,1)} %collective-permute-done.4.refs_4_), channel_id=1, source_target_pairs={{0,8},{8,0},{16,24},{24,16},{1,9},{9,1},{17,25},{25,17},{2,10},{10... | collective-permute-start | bytes 2359304 | tf_op jit(solution)/shard_map/ppermute | solution.py:121
  169.6 26.6 %collective-permute-start.3 = (bf16[2,64,3072]{2,1,0:T(8,128)(2,1)}, bf16[2,64,3072]{2,1,0:T(8,128)(2,1)S(1)}, u32[]{:S(2)}, u32[]{:S(2)}) collective-permute-start(bf16[2,64,3072]{2,1,0:T(8,128)(2,1)} %collective-permute-done.2.refs_2_), channel_id=1, source_target_pairs={{0,8},{8,0},{16,24},{24,16},{1,9},{9,1},{17,25},{25,17},{2,10},{10... | collective-permute-start | bytes 2359304 | tf_op jit(solution)/shard_map/ppermute | solution.py:121
  187.4 8.9 %collective-permute-start.7 = (bf16[2,64,3072]{2,1,0:T(8,128)(2,1)S(1)}, bf16[2,64,3072]{2,1,0:T(8,128)(2,1)S(1)}, u32[]{:S(2)}, u32[]{:S(2)}) collective-permute-start(bf16[2,64,3072]{2,1,0:T(8,128)(2,1)S(1)} %collective-permute-done.6.refs_6_), channel_id=1, source_target_pairs={{0,8},{8,0},{16,24},{24,16},{1,9},{9,1},{17,25},{25,17},{2,10},{10... | collective-permute-start | bytes 2359304 | tf_op jit(solution)/shard_map/ppermute | solution.py:121
  217.5 116.3 %all-to-all-start.3 = ((bf16[4,768,768]{2,1,0:T(8,128)(2,1)}), bf16[4,768,768]{2,1,0:T(8,128)(2,1)}, u32[]{:S(2)}, u32[]{:S(2)}) async-start(bf16[4,768,768]{2,1,0:T(8,128)(2,1)} %copy-done.6), calls=%async_computation.3 | async-start | bytes 9437184 | tf_op jit(solution)/shard_map/all_to_all | solution.py:360
  222.6 109.8 %collective-permute-start.13 = (bf16[1024,1152]{1,0:T(8,128)(2,1)}, bf16[1024,1152]{1,0:T(8,128)(2,1)S(1)}, u32[]{:S(2)}, u32[]{:S(2)}) collective-permute-start(bf16[1024,1152]{1,0:T(8,128)(2,1)} %copy-done.1), channel_id=1, source_target_pairs={{0,1},{1,0},{2,3},{3,2},{4,5},{5,4},{6,7},{7,6},{8,9},{9,8},{10,11... | collective-permute-start | bytes 7077896 | tf_op jit(solution)/shard_map/ppermute | solution.py:121
  224.4 73.7 %collective-permute-start.19 = (bf16[256,1920]{1,0:T(8,128)(2,1)S(1)}, bf16[256,1920]{1,0:T(8,128)(2,1)}, u32[]{:S(2)}, u32[]{:S(2)}) collective-permute-start(bf16[256,1920]{1,0:T(8,128)(2,1)S(1)} %cot_product.6), channel_id=1, source_target_pairs={{0,1},{1,0},{2,3},{3,2},{4,5},{5,4},{6,7},{7,6},{8,9},{9,8},{10,11... | collective-permute-start | bytes 2949128 | tf_op jit(solution)/shard_map/ppermute | solution.py:121
  224.7 94.1 %collective-permute-start.20 = (bf16[256,1920]{1,0:T(8,128)(2,1)}, bf16[256,1920]{1,0:T(8,128)(2,1)}, u32[]{:S(2)}, u32[]{:S(2)}) collective-permute-start(bf16[256,1920]{1,0:T(8,128)(2,1)} %copy-done.15), channel_id=1, source_target_pairs={{0,1},{1,0},{2,3},{3,2},{4,5},{5,4},{6,7},{7,6},{8,9},{9,8},{10,11... | collective-permute-start | bytes 2949128 | tf_op jit(solution)/shard_map/ppermute | solution.py:121
  303.9 23.9 %copy-start.16 = (bf16[256,1920]{1,0:T(8,128)(2,1)S(1)}, bf16[256,1920]{1,0:T(8,128)(2,1)}, u32[]{:S(2)}) copy-start(bf16[256,1920]{1,0:T(8,128)(2,1)} %copy-done.15) | copy-start | bytes 2949124
  303.9 23.9 %copy-start.24 = (bf16[256,1920]{1,0:T(8,128)(2,1)S(1)}, bf16[256,1920]{1,0:T(8,128)(2,1)}, u32[]{:S(2)}) copy-start(bf16[256,1920]{1,0:T(8,128)(2,1)} %copy-done.23) | copy-start | bytes 2949124
  303.9 23.9 %copy-start.26 = (bf16[256,1920]{1,0:T(8,128)(2,1)S(1)}, bf16[256,1920]{1,0:T(8,128)(2,1)}, u32[]{:S(2)}) copy-start(bf16[256,1920]{1,0:T(8,128)(2,1)} %copy-done.25) | copy-start | bytes 2949124
  325.8 47.4 %collective-permute-start.22 = (bf16[1024,512]{1,0:T(8,128)(2,1)S(1)}, bf16[1024,512]{1,0:T(8,128)(2,1)}, u32[]{:S(2)}, u32[]{:S(2)}) collective-permute-start(bf16[1024,512]{1,0:T(8,128)(2,1)S(1)} %in_product.9), channel_id=1, source_target_pairs={{0,1},{1,0},{2,3},{3,2},{4,5},{5,4},{6,7},{7,6},{8,9},{9,8},{10,11... | collective-permute-start | bytes 3145736 | tf_op jit(solution)/shard_map/ppermute | solution.py:121
  327.5 35.7 %collective-permute-start.21 = (bf16[1024,256]{1,0:T(8,128)(2,1)}, bf16[1024,256]{1,0:T(8,128)(2,1)}, u32[]{:S(2)}, u32[]{:S(2)}) collective-permute-start(bf16[1024,256]{1,0:T(8,128)(2,1)} %in_product.6), channel_id=1, source_target_pairs={{0,1},{1,0},{2,3},{3,2},{4,5},{5,4},{6,7},{7,6},{8,9},{9,8},{10,11... | collective-permute-start | bytes 1572872 | tf_op jit(solution)/shard_map/ppermute | solution.py:121
  340.2 66.2 %collective-permute-start.23 = (bf16[512,768]{1,0:T(8,128)(2,1)S(1)}, bf16[512,768]{1,0:T(8,128)(2,1)}, u32[]{:S(2)}, u32[]{:S(2)}) collective-permute-start(bf16[512,768]{1,0:T(8,128)(2,1)S(1)} %in_product.7), channel_id=1, source_target_pairs={{0,1},{1,0},{2,3},{3,2},{4,5},{5,4},{6,7},{7,6},{8,9},{9,8},{10,11... | collective-permute-start | bytes 2359304 | tf_op jit(solution)/shard_map/ppermute | solution.py:121
  371.4 44.9 %collective-permute-start.24 = (bf16[512,768]{1,0:T(8,128)(2,1)S(1)}, bf16[512,768]{1,0:T(8,128)(2,1)}, u32[]{:S(2)}, u32[]{:S(2)}) collective-permute-start(bf16[512,768]{1,0:T(8,128)(2,1)S(1)} %in_product.8), channel_id=1, source_target_pairs={{0,1},{1,0},{2,3},{3,2},{4,5},{5,4},{6,7},{7,6},{8,9},{9,8},{10,11... | collective-permute-start | bytes 2359304 | tf_op jit(solution)/shard_map/ppermute | solution.py:121
  416.3 9.6 %collective-permute-start.25 = (bf16[512,3072]{1,0:T(8,128)(2,1)}, bf16[512,3072]{1,0:T(8,128)(2,1)S(1)}, u32[]{:S(2)}, u32[]{:S(2)}) collective-permute-start(bf16[512,3072]{1,0:T(8,128)(2,1)} %out_product.7), channel_id=1, source_target_pairs={{0,8},{8,0},{16,24},{24,16},{1,9},{9,1},{17,25},{25,17},{2,10},{10... | collective-permute-start | bytes 9437192 | tf_op jit(solution)/shard_map/ppermute | solution.py:121
  423.2 11.3 %collective-permute-start.32 = (bf16[512,3072]{1,0:T(8,128)(2,1)S(1)}, bf16[512,3072]{1,0:T(8,128)(2,1)S(1)}, u32[]{:S(2)}, u32[]{:S(2)}) collective-permute-start(bf16[512,3072]{1,0:T(8,128)(2,1)S(1)} %back_product.6), channel_id=1, source_target_pairs={{0,8},{8,0},{16,24},{24,16},{1,9},{9,1},{17,25},{25,17},{2,10},{10... | collective-permute-start | bytes 9437192 | tf_op jit(solution)/shard_map/ppermute | solution.py:121
  429.1 25.9 %collective-permute-start.26 = (bf16[256,1536]{1,0:T(8,128)(2,1)S(1)}, bf16[256,1536]{1,0:T(8,128)(2,1)}, u32[]{:S(2)}, u32[]{:S(2)}) collective-permute-start(bf16[256,1536]{1,0:T(8,128)(2,1)S(1)} %out_product.9), channel_id=1, source_target_pairs={{0,16},{8,24},{16,0},{24,8},{1,17},{9,25},{17,1},{25,9},{2,18},{10... | collective-permute-start | bytes 2359304 | tf_op jit(solution)/shard_map/ppermute | solution.py:121
  434.1 32.3 %collective-permute-start.29 = (bf16[256,1536]{1,0:T(8,128)(2,1)S(1)}, bf16[256,1536]{1,0:T(8,128)(2,1)S(1)}, u32[]{:S(2)}, u32[]{:S(2)}) collective-permute-start(bf16[256,1536]{1,0:T(8,128)(2,1)S(1)} %out_product.11), channel_id=1, source_target_pairs={{0,16},{8,24},{16,0},{24,8},{1,17},{9,25},{17,1},{25,9},{2,18},{10... | collective-permute-start | bytes 2359304 | tf_op jit(solution)/shard_map/ppermute | solution.py:121
  438.6 29.8 %collective-permute-start.36 = (bf16[2,2,64,1536]{3,2,0,1:T(8,128)(2,1)S(1)}, bf16[2,2,64,1536]{3,2,0,1:T(8,128)(2,1)S(1)}, u32[]{:S(2)}, u32[]{:S(2)}) collective-permute-start(bf16[2,2,64,1536]{3,2,0,1:T(8,128)(2,1)S(1)} %bitcast.99), channel_id=1, source_target_pairs={{0,2},{2,0},{4,6},{6,4},{1,3},{3,1},{5,7},{7,5},{8,10},{10,8},{12,... | collective-permute-start | bytes 2359304 | tf_op jit(solution)/shard_map/ppermute | solution.py:121
  443.5 38.8 %collective-permute-start.33 = (bf16[256,1536]{1,0:T(8,128)(2,1)S(1)}, bf16[256,1536]{1,0:T(8,128)(2,1)S(1)}, u32[]{:S(2)}, u32[]{:S(2)}) collective-permute-start(bf16[256,1536]{1,0:T(8,128)(2,1)S(1)} %back_product.8), channel_id=1, source_target_pairs={{0,16},{8,24},{16,0},{24,8},{1,17},{9,25},{17,1},{25,9},{2,18},{10... | collective-permute-start | bytes 2359304 | tf_op jit(solution)/shard_map/ppermute | solution.py:121
  456.4 27.9 %collective-permute-start.27 = (bf16[2,64,1536]{2,1,0:T(8,128)(2,1)S(1)}, bf16[2,64,1536]{2,1,0:T(8,128)(2,1)S(1)}, u32[]{:S(2)}, u32[]{:S(2)}) collective-permute-start(bf16[2,64,1536]{2,1,0:T(8,128)(2,1)S(1)} %fusion.40), channel_id=1, source_target_pairs={{0,2},{2,0},{4,6},{6,4},{1,3},{3,1},{5,7},{7,5},{8,10},{10,8},{12,... | collective-permute-start | bytes 1179656 | tf_op jit(solution)/shard_map/ppermute | solution.py:121
  466.7 20.3 %collective-permute-start.30 = (bf16[2,64,1536]{2,1,0:T(8,128)(2,1)S(1)}, bf16[2,64,1536]{2,1,0:T(8,128)(2,1)S(1)}, u32[]{:S(2)}, u32[]{:S(2)}) collective-permute-start(bf16[2,64,1536]{2,1,0:T(8,128)(2,1)S(1)} %fusion.41), channel_id=1, source_target_pairs={{0,2},{2,0},{4,6},{6,4},{1,3},{3,1},{5,7},{7,5},{8,10},{10,8},{12,... | collective-permute-start | bytes 1179656 | tf_op jit(solution)/shard_map/ppermute | solution.py:121
  468.7 18.9 %collective-permute-start.37 = (bf16[2,64,1536]{2,1,0:T(8,128)(2,1)S(1)}, bf16[2,64,1536]{2,1,0:T(8,128)(2,1)S(1)}, u32[]{:S(2)}, u32[]{:S(2)}) collective-permute-start(bf16[2,64,1536]{2,1,0:T(8,128)(2,1)S(1)} %fusion.39), channel_id=1, source_target_pairs={{0,4},{2,6},{4,0},{6,2},{1,5},{3,7},{5,1},{7,3},{8,12},{10,14},{12... | collective-permute-start | bytes 1179656 | tf_op jit(solution)/shard_map/ppermute | solution.py:121
  482.6 18.7 %collective-permute-start.34 = (bf16[2,64,1536]{2,1,0:T(8,128)(2,1)S(1)}, bf16[2,64,1536]{2,1,0:T(8,128)(2,1)S(1)}, u32[]{:S(2)}, u32[]{:S(2)}) collective-permute-start(bf16[2,64,1536]{2,1,0:T(8,128)(2,1)S(1)} %fusion.42), channel_id=1, source_target_pairs={{0,2},{2,0},{4,6},{6,4},{1,3},{3,1},{5,7},{7,5},{8,10},{10,8},{12,... | collective-permute-start | bytes 1179656 | tf_op jit(solution)/shard_map/ppermute | solution.py:121
  484.4 34.5 %collective-permute-start.28 = (bf16[64,1536]{1,0:T(8,128)(2,1)S(1)}, bf16[64,1536]{1,0:T(8,128)(2,1)}, u32[]{:S(2)}, u32[]{:S(2)}) collective-permute-start(bf16[64,1536]{1,0:T(8,128)(2,1)S(1)} %fusion.47), channel_id=1, source_target_pairs={{0,4},{2,6},{4,0},{6,2},{1,5},{3,7},{5,1},{7,3},{8,12},{10,14},{12... | collective-permute-start | bytes 589832 | tf_op jit(solution)/shard_map/ppermute | solution.py:121
  487.2 33.4 %collective-permute-start.31 = (bf16[64,1536]{1,0:T(8,128)(2,1)S(1)}, bf16[64,1536]{1,0:T(8,128)(2,1)}, u32[]{:S(2)}, u32[]{:S(2)}) collective-permute-start(bf16[64,1536]{1,0:T(8,128)(2,1)S(1)} %fusion.48), channel_id=1, source_target_pairs={{0,4},{2,6},{4,0},{6,2},{1,5},{3,7},{5,1},{7,3},{8,12},{10,14},{12... | collective-permute-start | bytes 589832 | tf_op jit(solution)/shard_map/ppermute | solution.py:121
  487.7 15.4 %collective-permute-start.38 = (bf16[64,1536]{1,0:T(8,128)(2,1)S(1)}, bf16[64,1536]{1,0:T(8,128)(2,1)S(1)}, u32[]{:S(2)}, u32[]{:S(2)}) collective-permute-start(bf16[64,1536]{1,0:T(8,128)(2,1)S(1)} %fusion.50), channel_id=1, source_target_pairs={{0,16},{8,24},{16,0},{24,8},{1,17},{9,25},{17,1},{25,9},{2,18},{10... | collective-permute-start | bytes 589832 | tf_op jit(solution)/shard_map/ppermute | solution.py:121
  501.5 10.9 %collective-permute-start.35 = (bf16[64,1536]{1,0:T(8,128)(2,1)S(1)}, bf16[64,1536]{1,0:T(8,128)(2,1)S(1)}, u32[]{:S(2)}, u32[]{:S(2)}) collective-permute-start(bf16[64,1536]{1,0:T(8,128)(2,1)S(1)} %fusion.49), channel_id=1, source_target_pairs={{0,4},{2,6},{4,0},{6,2},{1,5},{3,7},{5,1},{7,3},{8,12},{10,14},{12... | collective-permute-start | bytes 589832 | tf_op jit(solution)/shard_map/ppermute | solution.py:121
  (35 other events, 207.0 us)

commit v12 on v11

--- a/solution.py
+++ b/solution.py
@@ -377,24 +377,26 @@
     normed_pair = with_x(half(normed))
 
     cot_parts, normed_parts = over_z(cot_pair), over_z(normed_pair)
-    waits = [(), (normed_parts[1],), (), ()]
     cot_owns, cot_gots = [], []
     for place, part in enumerate(cot_parts):
         own, other = with_core(part)
-        own = after(own, *waits[place], *cot_gots[: max(place - 1, 0)])
+        if place == 2:
+            own = after(own, cot_owns[1], cot_gots[0])
+        if place == 3:
+            own = after(own, cot_gots[1], cot_gots[2], normed_parts[2])
         cot_owns.append(cot_product((own, other), w_attn_out, w_mlp_out))
         cot_gots.append(others(cot_owns[-1]))
     all_in = assemble([with_core(part) for part in normed_parts])
 
     in_heads = swap(after(packed_heads, normed_pair, cot_owns[0]))
-    in_mlp = [swap(after(packed_mlp[0], in_heads, cot_owns[2], normed_parts[2]))]
-    in_mlp.append(swap(after(packed_mlp[1], in_mlp[0], cot_owns[3])))
-    heads_own = in_product(after(all_in, cot_gots[1]), in_heads)
+    in_mlp = [swap(after(packed_mlp[0], in_heads, cot_owns[2], *normed_parts[1:3]))]
+    in_mlp.append(swap(after(packed_mlp[1], in_mlp[0], cot_owns[3], all_in)))
+    heads_own = in_product(after(all_in, cot_gots[3]), in_heads)
     heads_got = others(heads_own)
-    mlp_own = [in_product(after(all_in, cot_gots[2], heads_own), in_mlp[0])]
+    mlp_own = [in_product(after(all_in, heads_own), in_mlp[0])]
     mlp_got = [others(mlp_own[0])]
     in_mlp.append(swap(after(packed_mlp[2], in_mlp[1], heads_own)))
-    mlp_own.append(in_product(after(all_in, cot_gots[3], mlp_own[0]), in_mlp[1]))
+    mlp_own.append(in_product(after(all_in, mlp_own[0]), in_mlp[1]))
     mlp_got.append(others(mlp_own[1]))
 
     out_grad = add_parts(after(cot_owns, mlp_own[0]), cot_gots)

time: 525 us -> 509 us (0.970)
  waiting for transfers between devices: 221 us -> 210 us
  starting transfers between devices: 65.8 us -> 57.7 us
    ppermute x39, waiting for transfers between devices: 218 us -> 210 us  [trade(): return lax.ppermute(block, axis, pairs)]
    ppermute x39, starting transfers between devices: 46.3 us -> 38.1 us  [trade(): return lax.ppermute(block, axis, pairs)]
    unnamed x81 -> x85, local copies, waits for them, and re-layouts: 20.3 us -> 22.3 us
  transfers between devices with their start and end apart: 43 -> 43, of which waited for: 13 -> 15; matrix products, arithmetic and copies ran while one was open for 3% -> 3% of each run, Pallas kernels for 34% -> 35%
where the time goes in v12:
time: 509 us; the launch traced here: 506 us
  waiting for transfers between devices  210 us (41%)
  Pallas kernels  185 us (36%)
  starting transfers between devices  57.7 us (11%)
  local copies, waits for them, and re-layouts  22.6 us (4%)
  other arithmetic  19.3 us (4%)
  blocking collectives  10.5 us (2%)
    ppermute x39, waiting for transfers between devices, trade(): return lax.ppermute(block, axis, pairs)  210 us
    pallas_call x11, Pallas kernels, product(): pl.pallas_call(kernel, grid=(columns // tile,), in_specs=specs, out_specs...  68.8 us
    pallas_call x5, Pallas kernels, in_product(): pl.pallas_call(in_kernel, grid=(columns // tile,), in_specs=[pl.BlockSpec...  39.5 us
    ppermute x39, starting transfers between devices, trade(): return lax.ppermute(block, axis, pairs)  38.1 us
    pallas_call x4, Pallas kernels, cot_product(): pl.pallas_call(cot_kernel, grid=(columns // tile,), in_specs=[whole, whol...  33.3 us
    unnamed x85, local copies, waits for them, and re-layouts  22.3 us
    all_to_all x4, starting transfers between devices, swap(): lax.all_to_all(packed, 'gx', split_axis=0, concat_axis=0, tiled=True)  19.6 us
    pallas_call x4, Pallas kernels, pack(): pl.pallas_call(pack_kernel, grid=(owners, width // tile), in_specs=[spec]...  18.6 us
  transfers between devices with their start and end apart: 43, of which 15 were waited for; matrix products, arithmetic and copies ran while one was open for 3% of the time, Pallas kernels for 35%

profile of v12, /device:TPU:0, one launch (start us, length us, event | category | flops | bytes accessed | tf_op | source)
XLA Modules:
  0.0 506.5 jit_solution(15683541586708121245)
XLA Ops:
  0.6 3.0 collective-permute-start.8
  4.8 4.9 all-reduce.1
  14.4 5.2 %pack.4 = bf16[4,768,1152]{2,1,0:T(8,128)(2,1)} custom-call(bf16[768,1536]{1,0:T(8,128)(2,1)S(1)} %copy-done.21, bf16[768,1536]{1,0:T(8,128)(2,1)S(1)} %copy-done.22, bf16[768,1536]{1,0:T(8,128)(2,1)} %refs_2_.1), custom_call_target="tpu_custom_call" | custom-call | bytes 221184 | tf_op jit(solution)/shard_map/pack/pallas_call | solution.py:148
  22.4 8.2 %cot_product.5 = bf16[256,1920]{1,0:T(8,128)(2,1)S(1)} custom-call(bf16[2,64,3072]{2,1,0:T(8,128)(2,1)S(1)} %pad_maximum_fusion.1.own_ref, bf16[2,64,3072]{2,1,0:T(8,128)(2,1)S(1)} %collective-permute-done.14.other_ref, bf16[384,3072]{1,0:T(8,128)(2,1)S(1)} %copy-done, bf16[1536,3072]{1,0:T(8,128)(2,1)} %refs_1_.11), custom_call_target="tpu_custom_call" | custom-call | flops 47185920 | bytes 199680 | tf_op jit(solution)/shard_map/cot_product/pallas_call | solution.py:214
  30.5 5.4 %all-to-all-start = ((bf16[4,768,1152]{2,1,0:T(8,128)(2,1)}), bf16[4,768,1152]{2,1,0:T(8,128)(2,1)}, u32[]{:S(2)}, u32[]{:S(2)}) async-start(bf16[4,768,1152]{2,1,0:T(8,128)(2,1)} %pack.4), calls=%async_computation | async-start | bytes 14155776 | tf_op jit(solution)/shard_map/all_to_all | solution.py:360
  42.3 30.5 %collective-permute-done.11.own_ref = bf16[2,64,3072]{2,1,0:T(8,128)(2,1)S(1)} collective-permute-done((bf16[2,64,3072]{2,1,0:T(8,128)(2,1)}, bf16[2,64,3072]{2,1,0:T(8,128)(2,1)S(1)}, u32[]{:S(2)}, u32[]{:S(2)}) %collective-permute-start.11) | collective-permute-done | bytes 786464 | tf_op jit(solution)/shard_map/ppermute | solution.py:121
  72.9 20.4 %collective-permute-done.9.own_ref = bf16[2,64,3072]{2,1,0:T(8,128)(2,1)} collective-permute-done((bf16[2,64,3072]{2,1,0:T(8,128)(2,1)}, bf16[2,64,3072]{2,1,0:T(8,128)(2,1)}, u32[]{:S(2)}, u32[]{:S(2)}) %collective-permute-start.9) | collective-permute-done | bytes 786464 | tf_op jit(solution)/shard_map/ppermute | solution.py:121
  93.2 16.1 %collective-permute-done.4.refs_4_ = bf16[2,64,3072]{2,1,0:T(8,128)(2,1)} collective-permute-done((bf16[2,64,3072]{2,1,0:T(8,128)(2,1)}, bf16[2,64,3072]{2,1,0:T(8,128)(2,1)}, u32[]{:S(2)}, u32[]{:S(2)}) %collective-permute-start.4) | collective-permute-done | bytes 786464 | tf_op jit(solution)/shard_map/ppermute | solution.py:121
  116.1 8.1 %cot_product.4 = bf16[256,1920]{1,0:T(8,128)(2,1)S(1)} custom-call(bf16[2,64,3072]{2,1,0:T(8,128)(2,1)S(1)} %collective-permute-done.11.own_ref, bf16[2,64,3072]{2,1,0:T(8,128)(2,1)S(1)} %collective-permute-done.12.other_ref, bf16[384,3072]{1,0:T(8,128)(2,1)S(1)} %copy-done, bf16[1536,3072]{1,0:T(8,128)(2,1)} %refs_1_.11), custom_call_target="tpu_custom_call" | custom-call | flops 47185920 | bytes 199680 | tf_op jit(solution)/shard_map/cot_product/pallas_call | solution.py:214
  124.2 8.7 %cot_product.6 = bf16[256,1920]{1,0:T(8,128)(2,1)S(1)} custom-call(bf16[2,64,3072]{2,1,0:T(8,128)(2,1)} %collective-permute-done.9.own_ref, bf16[2,64,3072]{2,1,0:T(8,128)(2,1)S(1)} %collective-permute-done.16.other_ref, bf16[384,3072]{1,0:T(8,128)(2,1)S(1)} %copy-done, bf16[1536,3072]{1,0:T(8,128)(2,1)} %refs_1_.11), custom_call_target="tpu_custom_call" | custom-call | flops 47185920 | bytes 199680 | tf_op jit(solution)/shard_map/cot_product/pallas_call | solution.py:214
  133.9 4.4 all-to-all-start.1
  143.5 16.3 %collective-permute-done.10.own_ref = bf16[2,64,3072]{2,1,0:T(8,128)(2,1)} collective-permute-done((bf16[2,64,3072]{2,1,0:T(8,128)(2,1)}, bf16[2,64,3072]{2,1,0:T(8,128)(2,1)}, u32[]{:S(2)}, u32[]{:S(2)}) %collective-permute-start.10) | collective-permute-done | bytes 786464 | tf_op jit(solution)/shard_map/ppermute | solution.py:121
  159.9 4.5 pack.7
  166.9 5.7 %assemble.1.rows_ref = bf16[1024,3072]{1,0:T(8,128)(2,1)} custom-call(bf16[2,64,3072]{2,1,0:T(8,128)(2,1)S(1)} %copy-done.17, bf16[2,64,3072]{2,1,0:T(8,128)(2,1)} %collective-permute-done.1.refs_1_, bf16[2,64,3072]{2,1,0:T(8,128)(2,1)} %collective-permute-done.2.refs_2_, bf16[2,64,3072]{2,1,0:T(8,128)(2,1)S(1)} %collective-permute-done.3.refs_3_, ...), custom_call_target="tpu_custom_call" | custom-call | bytes 196608 | tf_op jit(solution)/shard_map/assemble/pallas_call | solution.py:178
  173.6 9.9 %collective-permute-done.17 = bf16[256,1920]{1,0:T(8,128)(2,1)S(1)} collective-permute-done((bf16[256,1920]{1,0:T(8,128)(2,1)}, bf16[256,1920]{1,0:T(8,128)(2,1)S(1)}, u32[]{:S(2)}, u32[]{:S(2)}) %collective-permute-start.17) | collective-permute-done | bytes 983072 | tf_op jit(solution)/shard_map/ppermute | solution.py:121
  184.4 8.3 %cot_product.7 = bf16[256,1920]{1,0:T(8,128)(2,1)S(1)} custom-call(bf16[2,64,3072]{2,1,0:T(8,128)(2,1)} %collective-permute-done.10.own_ref, bf16[2,64,3072]{2,1,0:T(8,128)(2,1)S(1)} %collective-permute-done.18.other_ref, bf16[384,3072]{1,0:T(8,128)(2,1)S(1)} %copy-done, bf16[1536,3072]{1,0:T(8,128)(2,1)} %refs_1_.11), custom_call_target="tpu_custom_call" | custom-call | flops 47185920 | bytes 199680 | tf_op jit(solution)/shard_map/cot_product/pallas_call | solution.py:214
  192.8 4.7 all-to-all-start.2
  199.1 6.7 %pack.6 = bf16[4,768,768]{2,1,0:T(8,128)(2,1)S(1)} custom-call(bf16[768,6144]{1,0:T(8,128)(2,1)} %refs_0_.7), custom_call_target="tpu_custom_call" | custom-call | bytes 147456 | tf_op jit(solution)/shard_map/pack/pallas_call | solution.py:148
  207.9 13.7 %collective-permute-done.19 = bf16[256,1920]{1,0:T(8,128)(2,1)S(1)} collective-permute-done((bf16[256,1920]{1,0:T(8,128)(2,1)S(1)}, bf16[256,1920]{1,0:T(8,128)(2,1)S(1)}, u32[]{:S(2)}, u32[]{:S(2)}) %collective-permute-start.19) | collective-permute-done | bytes 983072 | tf_op jit(solution)/shard_map/ppermute | solution.py:121
  222.6 14.0 %in_product.5.q_own.k_own.v_own = bf16[1024,1152]{1,0:T(8,128)(2,1)S(1)} custom-call(bf16[1024,3072]{1,0:T(8,128)(2,1)} %assemble.1.rows_ref, bf16[3072,1152]{1,0:T(8,128)(2,1)} %bitcast.4.weight_ref.refs_5_), custom_call_target="tpu_custom_call" | custom-call | flops 113246208 | bytes 245760 | tf_op jit(solution)/shard_map/in_product/pallas_call | solution.py:268
  238.0 5.1 %all-to-all-start.3 = ((bf16[4,768,768]{2,1,0:T(8,128)(2,1)}), bf16[4,768,768]{2,1,0:T(8,128)(2,1)}, u32[]{:S(2)}, u32[]{:S(2)}) async-start(bf16[4,768,768]{2,1,0:T(8,128)(2,1)} %copy-done.6), calls=%async_computation.3 | async-start | bytes 9437184 | tf_op jit(solution)/shard_map/all_to_all | solution.py:360
  244.7 5.8 %in_product.6 = bf16[1024,256]{1,0:T(8,128)(2,1)} custom-call(bf16[1024,3072]{1,0:T(8,128)(2,1)} %assemble.1.rows_ref, bf16[3072,256]{1,0:T(8,128)(2,1)} %bitcast.5.weight_ref.refs_6_), custom_call_target="tpu_custom_call" | custom-call | flops 25165824 | bytes 131072 | tf_op jit(solution)/shard_map/in_product/pallas_call | solution.py:268
  250.5 7.1 %in_product.9 = bf16[1024,512]{1,0:T(8,128)(2,1)S(1)} custom-call(bf16[1024,3072]{1,0:T(8,128)(2,1)} %assemble.1.rows_ref, bf16[3072,512]{1,0:T(8,128)(2,1)} %bitcast.15.weight_ref.refs_7_), custom_call_target="tpu_custom_call" | custom-call | flops 50331648 | bytes 163840 | tf_op jit(solution)/shard_map/in_product/pallas_call | solution.py:268
  259.7 4.6 add_parts.1
  264.3 33.1 %collective-permute-done.20.q_got.k_got.v_got = bf16[1024,1152]{1,0:T(8,128)(2,1)S(1)} collective-permute-done((bf16[1024,1152]{1,0:T(8,128)(2,1)}, bf16[1024,1152]{1,0:T(8,128)(2,1)S(1)}, u32[]{:S(2)}, u32[]{:S(2)}) %collective-permute-start.20) | collective-permute-done | bytes 2359328 | tf_op jit(solution)/shard_map/ppermute | solution.py:121
  298.9 6.4 %in_product.7 = bf16[512,768]{1,0:T(8,128)(2,1)S(1)} custom-call(bf16[1024,3072]{1,0:T(8,128)(2,1)} %assemble.1.rows_ref, bf16[3072,768]{1,0:T(8,128)(2,1)} %bitcast.16.weight_ref.refs_1_), custom_call_target="tpu_custom_call" | custom-call | flops 37748736 | bytes 184320 | tf_op jit(solution)/shard_map/in_product/pallas_call | solution.py:268
  308.6 14.9 %attend.1 = (bf16[1024,384]{1,0:T(8,128)(2,1)S(1)}, bf16[1024,384]{1,0:T(8,128)(2,1)S(1)}, bf16[1024,384]{1,0:T(8,128)(2,1)S(1)}, bf16[1024,384]{1,0:T(8,128)(2,1)S(1)}) custom-call(bf16[1024,1152]{1,0:T(8,128)(2,1)S(1)} %copy-done.2, bf16[1024,1152]{1,0:T(8,128)(2,1)S(1)} %copy-done.5, bf16[1024,1152]{1,0:T(8,128)(2,1)S(1)} %copy-done.2, ...), custom_call_target="tpu_custom_call" | custom-call | flops 12582912 | bytes 98304 | tf_op jit(solution)/shard_map/attend/pallas_call | solution.py:75
  326.2 5.0 collective-permute-done.21
  333.1 6.3 %in_product.8 = bf16[512,768]{1,0:T(8,128)(2,1)S(1)} custom-call(bf16[1024,3072]{1,0:T(8,128)(2,1)} %assemble.1.rows_ref, bf16[3072,768]{1,0:T(8,128)(2,1)} %bitcast.16.weight_ref.refs_1_), custom_call_target="tpu_custom_call" | custom-call | flops 37748736 | bytes 184320 | tf_op jit(solution)/shard_map/in_product/pallas_call | solution.py:268
  343.5 18.6 %back_product.5.refs_2_ = bf16[1024,3072]{1,0:T(8,128)(2,1)} custom-call(bf16[1024,384]{1,0:T(8,128)(2,1)S(1)} %copy-done.30, bf16[1024,384]{1,0:T(8,128)(2,1)S(1)} %copy-done.32, bf16[1024,384]{1,0:T(8,128)(2,1)S(1)} %copy-done.34, bf16[1024,256]{1,0:T(8,128)(2,1)S(1)} %get-tuple-element.70.refs_3_, bf16[1024,512]{1,0:T(8,128)(2,1)S(1)} %get-tuple-element.62.refs_4_, ...), custom_call_target="tpu_custom_call" | custom-call | flops 188743680 | bytes 282624 | tf_op jit(solution)/shard_map/back_product/pallas_call | solution.py:321
  362.1 12.3 %out_product.6.refs_2_ = bf16[1024,3072]{1,0:T(8,128)(2,1)} custom-call(bf16[1024,384]{1,0:T(8,128)(2,1)S(1)} %copy-done.28, bf16[1024,256]{1,0:T(8,128)(2,1)S(1)} %get-tuple-element.71.refs_1_, bf16[1024,512]{1,0:T(8,128)(2,1)S(1)} %get-tuple-element.63.refs_2_, bf16[384,3072]{1,0:T(8,128)(2,1)S(1)} %copy-done, bf16[1536,3072]{1,0:T(8,128)(2,1)} %refs_1_.11), custom_call_target="tpu_custom_call" | custom-call | flops 113246208 | bytes 282624 | tf_op jit(solution)/shard_map/out_product/pallas_call | solution.py:321
  376.5 7.7 %out_product.7 = bf16[512,3072]{1,0:T(8,128)(2,1)} custom-call(bf16[512,768]{1,0:T(8,128)(2,1)S(1)} %get-tuple-element.69.refs_0_, bf16[1536,3072]{1,0:T(8,128)(2,1)} %refs_1_.11, bf16[1024,3072]{1,0:T(8,128)(2,1)} %out_product.6.refs_2_), custom_call_target="tpu_custom_call" | custom-call | flops 37748736 | bytes 196608 | tf_op jit(solution)/shard_map/out_product/pallas_call | solution.py:321
  384.2 6.9 %back_product.6 = bf16[512,3072]{1,0:T(8,128)(2,1)S(1)} custom-call(bf16[512,768]{1,0:T(8,128)(2,1)S(1)} %get-tuple-element.50.refs_0_, bf16[3072,768]{1,0:T(8,128)(2,1)} %bitcast.16.weight_ref.refs_1_, bf16[1024,3072]{1,0:T(8,128)(2,1)} %back_product.5.refs_2_), custom_call_target="tpu_custom_call" | custom-call | flops 37748736 | bytes 122880 | tf_op jit(solution)/shard_map/back_product/pallas_call | solution.py:321
  393.8 3.2 out_product.9
  398.9 3.2 out_product.11
  402.4 3.3 back_product.8
  407.5 3.9 back_product.9
  412.0 3.2 out_product.8
  415.2 3.2 out_product.10
  418.5 3.3 back_product.7
  424.9 9.4 %collective-permute-done.29 = bf16[256,1536]{1,0:T(8,128)(2,1)S(1)} collective-permute-done((bf16[256,1536]{1,0:T(8,128)(2,1)S(1)}, bf16[256,1536]{1,0:T(8,128)(2,1)S(1)}, u32[]{:S(2)}, u32[]{:S(2)}) %collective-permute-start.29) | collective-permute-done | bytes 786464 | tf_op jit(solution)/shard_map/ppermute | solution.py:121
  435.0 15.2 %collective-permute-done.33 = bf16[256,1536]{1,0:T(8,128)(2,1)S(1)} collective-permute-done((bf16[256,1536]{1,0:T(8,128)(2,1)S(1)}, bf16[256,1536]{1,0:T(8,128)(2,1)S(1)}, u32[]{:S(2)}, u32[]{:S(2)}) %collective-permute-start.33) | collective-permute-done | bytes 786464 | tf_op jit(solution)/shard_map/ppermute | solution.py:121
  451.3 2.7 collective-permute-start.37
  454.5 2.7 collective-permute-start.31
  457.3 11.5 %collective-permute-done.34 = bf16[2,64,1536]{2,1,0:T(8,128)(2,1)S(1)} collective-permute-done((bf16[2,64,1536]{2,1,0:T(8,128)(2,1)S(1)}, bf16[2,64,1536]{2,1,0:T(8,128)(2,1)S(1)}, u32[]{:S(2)}, u32[]{:S(2)}) %collective-permute-start.34) | collective-permute-done | bytes 393248 | tf_op jit(solution)/shard_map/ppermute | solution.py:121
  468.9 16.4 %collective-permute-done.37 = bf16[2,64,1536]{2,1,0:T(8,128)(2,1)S(1)} collective-permute-done((bf16[2,64,1536]{2,1,0:T(8,128)(2,1)S(1)}, bf16[2,64,1536]{2,1,0:T(8,128)(2,1)S(1)}, u32[]{:S(2)}, u32[]{:S(2)}) %collective-permute-start.37) | collective-permute-done | bytes 393248 | tf_op jit(solution)/shard_map/ppermute | solution.py:121
  487.3 8.7 %collective-permute-done.35 = bf16[64,1536]{1,0:T(8,128)(2,1)S(1)} collective-permute-done((bf16[64,1536]{1,0:T(8,128)(2,1)S(1)}, bf16[64,1536]{1,0:T(8,128)(2,1)S(1)}, u32[]{:S(2)}, u32[]{:S(2)}) %collective-permute-start.35) | collective-permute-done | bytes 196640 | tf_op jit(solution)/shard_map/ppermute | solution.py:121
  497.1 5.6 %all-reduce = (f32[64]{0:T(128)S(1)}, f32[64]{0:T(128)}) all-reduce(f32[64]{0:T(128)S(1)} %fusion.28, f32[64]{0:T(128)} %reduce_sum.48), channel_id=1, replica_groups=mesh['gx'=4,'gy'=4,'gz'=2] {'gz'}, use_global_device_ids=true, to_apply=%region_8.9 | all-reduce | flops 128 | bytes 1024 | tf_op jit(solution)/shard_map/psum | solution.py:485
  (187 shorter events, 77.0 us)
Async XLA Ops:
  0.6 19.0 %collective-permute-start.8 = (bf16[64,3072]{1,0:T(8,128)(2,1)}, bf16[64,3072]{1,0:T(8,128)(2,1)S(1)}, u32[]{:S(2)}, u32[]{:S(2)}) collective-permute-start(bf16[64,3072]{1,0:T(8,128)(2,1)} %param.9), channel_id=1, source_target_pairs={{0,16},{8,24},{16,0},{24,8},{1,17},{9,25},{17,1},{25,9},{2,18},{10... | collective-permute-start | bytes 1179656 | tf_op jit(solution)/shard_map/ppermute | solution.py:121
  10.9 10.4 %collective-permute-start = (bf16[64,3072]{1,0:T(8,128)(2,1)S(1)}, bf16[64,3072]{1,0:T(8,128)(2,1)S(1)}, u32[]{:S(2)}, u32[]{:S(2)}) collective-permute-start(bf16[64,3072]{1,0:T(8,128)(2,1)S(1)} %fusion.27), channel_id=1, source_target_pairs={{0,16},{8,24},{16,0},{24,8},{1,17},{9,25},{17,1},{25,9},{2,18},{10... | collective-permute-start | bytes 1179656 | tf_op jit(solution)/shard_map/ppermute | solution.py:121
  19.7 2.6 collective-permute-start.14
  30.5 103.4 %all-to-all-start = ((bf16[4,768,1152]{2,1,0:T(8,128)(2,1)}), bf16[4,768,1152]{2,1,0:T(8,128)(2,1)}, u32[]{:S(2)}, u32[]{:S(2)}) async-start(bf16[4,768,1152]{2,1,0:T(8,128)(2,1)} %pack.4), calls=%async_computation | async-start | bytes 14155776 | tf_op jit(solution)/shard_map/all_to_all | solution.py:360
  35.9 36.9 %collective-permute-start.11 = (bf16[2,64,3072]{2,1,0:T(8,128)(2,1)}, bf16[2,64,3072]{2,1,0:T(8,128)(2,1)S(1)}, u32[]{:S(2)}, u32[]{:S(2)}) collective-permute-start(bf16[2,64,3072]{2,1,0:T(8,128)(2,1)} %copy-done.18), channel_id=1, source_target_pairs={{0,2},{2,0},{4,6},{6,4},{1,3},{3,1},{5,7},{7,5},{8,10},{10,8},{12,... | collective-permute-start | bytes 2359304 | tf_op jit(solution)/shard_map/ppermute | solution.py:121
  37.9 55.4 %collective-permute-start.9 = (bf16[2,64,3072]{2,1,0:T(8,128)(2,1)}, bf16[2,64,3072]{2,1,0:T(8,128)(2,1)}, u32[]{:S(2)}, u32[]{:S(2)}) collective-permute-start(bf16[2,64,3072]{2,1,0:T(8,128)(2,1)} %copy-done.18), channel_id=1, source_target_pairs={{0,4},{2,6},{4,0},{6,2},{1,5},{3,7},{5,1},{7,3},{8,12},{10,14},{12... | collective-permute-start | bytes 2359304 | tf_op jit(solution)/shard_map/ppermute | solution.py:121
  40.5 68.9 %collective-permute-start.4 = (bf16[2,64,3072]{2,1,0:T(8,128)(2,1)}, bf16[2,64,3072]{2,1,0:T(8,128)(2,1)}, u32[]{:S(2)}, u32[]{:S(2)}) collective-permute-start(bf16[2,64,3072]{2,1,0:T(8,128)(2,1)} %pad_maximum_fusion.refs_0_), channel_id=1, source_target_pairs={{0,4},{2,6},{4,0},{6,2},{1,5},{3,7},{5,1},{7,3},{8,12},{10,14},{12... | collective-permute-start | bytes 2359304 | tf_op jit(solution)/shard_map/ppermute | solution.py:121
  40.8 69.1 %collective-permute-start.15 = (bf16[256,1920]{1,0:T(8,128)(2,1)S(1)}, bf16[256,1920]{1,0:T(8,128)(2,1)S(1)}, u32[]{:S(2)}, u32[]{:S(2)}) collective-permute-start(bf16[256,1920]{1,0:T(8,128)(2,1)S(1)} %cot_product.5), channel_id=1, source_target_pairs={{0,1},{1,0},{2,3},{3,2},{4,5},{5,4},{6,7},{7,6},{8,9},{9,8},{10,11... | collective-permute-start | bytes 2949128 | tf_op jit(solution)/shard_map/ppermute | solution.py:121
  72.9 36.5 %collective-permute-start.12 = (bf16[2,64,3072]{2,1,0:T(8,128)(2,1)S(1)}, bf16[2,64,3072]{2,1,0:T(8,128)(2,1)S(1)}, u32[]{:S(2)}, u32[]{:S(2)}) collective-permute-start(bf16[2,64,3072]{2,1,0:T(8,128)(2,1)S(1)} %collective-permute-done.11.own_ref), channel_id=1, source_target_pairs={{0,8},{8,0},{16,24},{24,16},{1,9},{9,1},{17,25},{25,17},{2,10},{10... | collective-permute-start | bytes 2359304 | tf_op jit(solution)/shard_map/ppermute | solution.py:121
  93.2 16.1 %collective-permute-start.16 = (bf16[2,64,3072]{2,1,0:T(8,128)(2,1)}, bf16[2,64,3072]{2,1,0:T(8,128)(2,1)S(1)}, u32[]{:S(2)}, u32[]{:S(2)}) collective-permute-start(bf16[2,64,3072]{2,1,0:T(8,128)(2,1)} %collective-permute-done.9.own_ref), channel_id=1, source_target_pairs={{0,8},{8,0},{16,24},{24,16},{1,9},{9,1},{17,25},{25,17},{2,10},{10... | collective-permute-start | bytes 2359304 | tf_op jit(solution)/shard_map/ppermute | solution.py:121
  93.2 40.6 %collective-permute-start.2 = (bf16[2,64,3072]{2,1,0:T(8,128)(2,1)}, bf16[2,64,3072]{2,1,0:T(8,128)(2,1)}, u32[]{:S(2)}, u32[]{:S(2)}) collective-permute-start(bf16[2,64,3072]{2,1,0:T(8,128)(2,1)} %pad_maximum_fusion.refs_0_), channel_id=1, source_target_pairs={{0,2},{2,0},{4,6},{6,4},{1,3},{3,1},{5,7},{7,5},{8,10},{10,8},{12,... | collective-permute-start | bytes 2359304 | tf_op jit(solution)/shard_map/ppermute | solution.py:121
  109.3 30.6 %collective-permute-start.1 = (bf16[2,64,3072]{2,1,0:T(8,128)(2,1)}, bf16[2,64,3072]{2,1,0:T(8,128)(2,1)}, u32[]{:S(2)}, u32[]{:S(2)}) collective-permute-start(bf16[2,64,3072]{2,1,0:T(8,128)(2,1)} %pad_maximum_fusion.refs_0_), channel_id=1, source_target_pairs={{0,8},{8,0},{16,24},{24,16},{1,9},{9,1},{17,25},{25,17},{2,10},{10... | collective-permute-start | bytes 2359304 | tf_op jit(solution)/shard_map/ppermute | solution.py:121
  109.3 33.6 %collective-permute-start.6 = (bf16[2,64,3072]{2,1,0:T(8,128)(2,1)}, bf16[2,64,3072]{2,1,0:T(8,128)(2,1)}, u32[]{:S(2)}, u32[]{:S(2)}) collective-permute-start(bf16[2,64,3072]{2,1,0:T(8,128)(2,1)} %collective-permute-done.4.refs_4_), channel_id=1, source_target_pairs={{0,2},{2,0},{4,6},{6,4},{1,3},{3,1},{5,7},{7,5},{8,10},{10,8},{12,... | collective-permute-start | bytes 2359304 | tf_op jit(solution)/shard_map/ppermute | solution.py:121
  109.4 33.6 %collective-permute-start.5 = (bf16[2,64,3072]{2,1,0:T(8,128)(2,1)}, bf16[2,64,3072]{2,1,0:T(8,128)(2,1)}, u32[]{:S(2)}, u32[]{:S(2)}) collective-permute-start(bf16[2,64,3072]{2,1,0:T(8,128)(2,1)} %collective-permute-done.4.refs_4_), channel_id=1, source_target_pairs={{0,8},{8,0},{16,24},{24,16},{1,9},{9,1},{17,25},{25,17},{2,10},{10... | collective-permute-start | bytes 2359304 | tf_op jit(solution)/shard_map/ppermute | solution.py:121
  110.9 48.8 %collective-permute-start.10 = (bf16[2,64,3072]{2,1,0:T(8,128)(2,1)}, bf16[2,64,3072]{2,1,0:T(8,128)(2,1)}, u32[]{:S(2)}, u32[]{:S(2)}) collective-permute-start(bf16[2,64,3072]{2,1,0:T(8,128)(2,1)} %collective-permute-done.9.own_ref), channel_id=1, source_target_pairs={{0,2},{2,0},{4,6},{6,4},{1,3},{3,1},{5,7},{7,5},{8,10},{10,8},{12,... | collective-permute-start | bytes 2359304 | tf_op jit(solution)/shard_map/ppermute | solution.py:121
  124.2 14.1 %copy-start.11 = (bf16[256,1920]{1,0:T(8,128)(2,1)}, bf16[256,1920]{1,0:T(8,128)(2,1)S(1)}, u32[]{:S(2)}) copy-start(bf16[256,1920]{1,0:T(8,128)(2,1)S(1)} %cot_product.4) | copy-start | bytes 2949124
  133.9 58.9 %all-to-all-start.1 = ((bf16[4,768,256]{2,1,0:T(8,128)(2,1)}), bf16[4,768,256]{2,1,0:T(8,128)(2,1)}, u32[]{:S(2)}, u32[]{:S(2)}) async-start(bf16[4,768,256]{2,1,0:T(8,128)(2,1)} %copy-done.8), calls=%async_computation.1 | async-start | bytes 3145728 | tf_op jit(solution)/shard_map/all_to_all | solution.py:360
  138.3 28.6 %copy-start.17 = (bf16[2,64,3072]{2,1,0:T(8,128)(2,1)S(1)}, bf16[2,64,3072]{2,1,0:T(8,128)(2,1)}, u32[]{:S(2)}) copy-start(bf16[2,64,3072]{2,1,0:T(8,128)(2,1)} %pad_maximum_fusion.refs_0_) | copy-start | bytes 2359300
  138.3 34.3 %collective-permute-start.13 = (bf16[256,1920]{1,0:T(8,128)(2,1)S(1)}, bf16[256,1920]{1,0:T(8,128)(2,1)S(1)}, u32[]{:S(2)}, u32[]{:S(2)}) collective-permute-start(bf16[256,1920]{1,0:T(8,128)(2,1)S(1)} %cot_product.4), channel_id=1, source_target_pairs={{0,1},{1,0},{2,3},{3,2},{4,5},{5,4},{6,7},{7,6},{8,9},{9,8},{10,11... | collective-permute-start | bytes 2949128 | tf_op jit(solution)/shard_map/ppermute | solution.py:121
  139.9 43.6 %collective-permute-start.17 = (bf16[256,1920]{1,0:T(8,128)(2,1)}, bf16[256,1920]{1,0:T(8,128)(2,1)S(1)}, u32[]{:S(2)}, u32[]{:S(2)}) collective-permute-start(bf16[256,1920]{1,0:T(8,128)(2,1)} %copy-done.13), channel_id=1, source_target_pairs={{0,1},{1,0},{2,3},{3,2},{4,5},{5,4},{6,7},{7,6},{8,9},{9,8},{10,11... | collective-permute-start | bytes 2949128 | tf_op jit(solution)/shard_map/ppermute | solution.py:121
  143.0 23.1 %collective-permute-start.3 = (bf16[2,64,3072]{2,1,0:T(8,128)(2,1)}, bf16[2,64,3072]{2,1,0:T(8,128)(2,1)S(1)}, u32[]{:S(2)}, u32[]{:S(2)}) collective-permute-start(bf16[2,64,3072]{2,1,0:T(8,128)(2,1)} %collective-permute-done.2.refs_2_), channel_id=1, source_target_pairs={{0,8},{8,0},{16,24},{24,16},{1,9},{9,1},{17,25},{25,17},{2,10},{10... | collective-permute-start | bytes 2359304 | tf_op jit(solution)/shard_map/ppermute | solution.py:121
  143.0 23.0 %collective-permute-start.7 = (bf16[2,64,3072]{2,1,0:T(8,128)(2,1)}, bf16[2,64,3072]{2,1,0:T(8,128)(2,1)S(1)}, u32[]{:S(2)}, u32[]{:S(2)}) collective-permute-start(bf16[2,64,3072]{2,1,0:T(8,128)(2,1)} %collective-permute-done.6.refs_6_), channel_id=1, source_target_pairs={{0,8},{8,0},{16,24},{24,16},{1,9},{9,1},{17,25},{25,17},{2,10},{10... | collective-permute-start | bytes 2359304 | tf_op jit(solution)/shard_map/ppermute | solution.py:121
  159.8 23.7 %collective-permute-start.18 = (bf16[2,64,3072]{2,1,0:T(8,128)(2,1)}, bf16[2,64,3072]{2,1,0:T(8,128)(2,1)S(1)}, u32[]{:S(2)}, u32[]{:S(2)}) collective-permute-start(bf16[2,64,3072]{2,1,0:T(8,128)(2,1)} %collective-permute-done.10.own_ref), channel_id=1, source_target_pairs={{0,8},{8,0},{16,24},{24,16},{1,9},{9,1},{17,25},{25,17},{2,10},{10... | collective-permute-start | bytes 2359304 | tf_op jit(solution)/shard_map/ppermute | solution.py:121
  192.8 45.2 %all-to-all-start.2 = ((bf16[4,768,512]{2,1,0:T(8,128)(2,1)}), bf16[4,768,512]{2,1,0:T(8,128)(2,1)}, u32[]{:S(2)}, u32[]{:S(2)}) async-start(bf16[4,768,512]{2,1,0:T(8,128)(2,1)} %copy-done.7), calls=%async_computation.2 | async-start | bytes 6291456 | tf_op jit(solution)/shard_map/all_to_all | solution.py:360
  197.5 24.1 %collective-permute-start.19 = (bf16[256,1920]{1,0:T(8,128)(2,1)S(1)}, bf16[256,1920]{1,0:T(8,128)(2,1)S(1)}, u32[]{:S(2)}, u32[]{:S(2)}) collective-permute-start(bf16[256,1920]{1,0:T(8,128)(2,1)S(1)} %cot_product.7), channel_id=1, source_target_pairs={{0,1},{1,0},{2,3},{3,2},{4,5},{5,4},{6,7},{7,6},{8,9},{9,8},{10,11... | collective-permute-start | bytes 2949128 | tf_op jit(solution)/shard_map/ppermute | solution.py:121
  238.0 61.0 %all-to-all-start.3 = ((bf16[4,768,768]{2,1,0:T(8,128)(2,1)}), bf16[4,768,768]{2,1,0:T(8,128)(2,1)}, u32[]{:S(2)}, u32[]{:S(2)}) async-start(bf16[4,768,768]{2,1,0:T(8,128)(2,1)} %copy-done.6), calls=%async_computation.3 | async-start | bytes 9437184 | tf_op jit(solution)/shard_map/all_to_all | solution.py:360
  243.1 54.4 %collective-permute-start.20 = (bf16[1024,1152]{1,0:T(8,128)(2,1)}, bf16[1024,1152]{1,0:T(8,128)(2,1)S(1)}, u32[]{:S(2)}, u32[]{:S(2)}) collective-permute-start(bf16[1024,1152]{1,0:T(8,128)(2,1)} %copy-done.1), channel_id=1, source_target_pairs={{0,1},{1,0},{2,3},{3,2},{4,5},{5,4},{6,7},{7,6},{8,9},{9,8},{10,11... | collective-permute-start | bytes 7077896 | tf_op jit(solution)/shard_map/ppermute | solution.py:121
  257.6 83.4 %collective-permute-start.22 = (bf16[1024,512]{1,0:T(8,128)(2,1)S(1)}, bf16[1024,512]{1,0:T(8,128)(2,1)}, u32[]{:S(2)}, u32[]{:S(2)}) collective-permute-start(bf16[1024,512]{1,0:T(8,128)(2,1)S(1)} %in_product.9), channel_id=1, source_target_pairs={{0,1},{1,0},{2,3},{3,2},{4,5},{5,4},{6,7},{7,6},{8,9},{9,8},{10,11... | collective-permute-start | bytes 3145736 | tf_op jit(solution)/shard_map/ppermute | solution.py:121
  258.2 73.1 %collective-permute-start.21 = (bf16[1024,256]{1,0:T(8,128)(2,1)}, bf16[1024,256]{1,0:T(8,128)(2,1)}, u32[]{:S(2)}, u32[]{:S(2)}) collective-permute-start(bf16[1024,256]{1,0:T(8,128)(2,1)} %in_product.6), channel_id=1, source_target_pairs={{0,1},{1,0},{2,3},{3,2},{4,5},{5,4},{6,7},{7,6},{8,9},{9,8},{10,11... | collective-permute-start | bytes 1572872 | tf_op jit(solution)/shard_map/ppermute | solution.py:121
  305.4 69.0 %collective-permute-start.23 = (bf16[512,768]{1,0:T(8,128)(2,1)S(1)}, bf16[512,768]{1,0:T(8,128)(2,1)}, u32[]{:S(2)}, u32[]{:S(2)}) collective-permute-start(bf16[512,768]{1,0:T(8,128)(2,1)S(1)} %in_product.7), channel_id=1, source_target_pairs={{0,1},{1,0},{2,3},{3,2},{4,5},{5,4},{6,7},{7,6},{8,9},{9,8},{10,11... | collective-permute-start | bytes 2359304 | tf_op jit(solution)/shard_map/ppermute | solution.py:121
  326.2 13.2 %copy-start.29 = (bf16[1024,384]{1,0:T(8,128)(2,1)}, bf16[1024,384]{1,0:T(8,128)(2,1)S(1)}, u32[]{:S(2)}) copy-start(bf16[1024,384]{1,0:T(8,128)(2,1)S(1)} %get-tuple-element.46.refs_0_) | copy-start | bytes 2359300
  339.4 44.8 %collective-permute-start.24 = (bf16[512,768]{1,0:T(8,128)(2,1)S(1)}, bf16[512,768]{1,0:T(8,128)(2,1)}, u32[]{:S(2)}, u32[]{:S(2)}) collective-permute-start(bf16[512,768]{1,0:T(8,128)(2,1)S(1)} %in_product.8), channel_id=1, source_target_pairs={{0,1},{1,0},{2,3},{3,2},{4,5},{5,4},{6,7},{7,6},{8,9},{9,8},{10,11... | collective-permute-start | bytes 2359304 | tf_op jit(solution)/shard_map/ppermute | solution.py:121
  343.5 18.6 %copy-start.28 = (bf16[1024,384]{1,0:T(8,128)(2,1)S(1)}, bf16[1024,384]{1,0:T(8,128)(2,1)}, u32[]{:S(2)}) copy-start(bf16[1024,384]{1,0:T(8,128)(2,1)} %copy-done.27) | copy-start | bytes 2359300
  384.2 9.6 %collective-permute-start.25 = (bf16[512,3072]{1,0:T(8,128)(2,1)}, bf16[512,3072]{1,0:T(8,128)(2,1)S(1)}, u32[]{:S(2)}, u32[]{:S(2)}) collective-permute-start(bf16[512,3072]{1,0:T(8,128)(2,1)} %out_product.7), channel_id=1, source_target_pairs={{0,8},{8,0},{16,24},{24,16},{1,9},{9,1},{17,25},{25,17},{2,10},{10... | collective-permute-start | bytes 9437192 | tf_op jit(solution)/shard_map/ppermute | solution.py:121
  391.1 11.3 %collective-permute-start.32 = (bf16[512,3072]{1,0:T(8,128)(2,1)S(1)}, bf16[512,3072]{1,0:T(8,128)(2,1)S(1)}, u32[]{:S(2)}, u32[]{:S(2)}) collective-permute-start(bf16[512,3072]{1,0:T(8,128)(2,1)S(1)} %back_product.6), channel_id=1, source_target_pairs={{0,8},{8,0},{16,24},{24,16},{1,9},{9,1},{17,25},{25,17},{2,10},{10... | collective-permute-start | bytes 9437192 | tf_op jit(solution)/shard_map/ppermute | solution.py:121
  397.0 24.7 %collective-permute-start.26 = (bf16[256,1536]{1,0:T(8,128)(2,1)S(1)}, bf16[256,1536]{1,0:T(8,128)(2,1)}, u32[]{:S(2)}, u32[]{:S(2)}) collective-permute-start(bf16[256,1536]{1,0:T(8,128)(2,1)S(1)} %out_product.9), channel_id=1, source_target_pairs={{0,16},{8,24},{16,0},{24,8},{1,17},{9,25},{17,1},{25,9},{2,18},{10... | collective-permute-start | bytes 2359304 | tf_op jit(solution)/shard_map/ppermute | solution.py:121
  402.1 32.3 %collective-permute-start.29 = (bf16[256,1536]{1,0:T(8,128)(2,1)S(1)}, bf16[256,1536]{1,0:T(8,128)(2,1)S(1)}, u32[]{:S(2)}, u32[]{:S(2)}) collective-permute-start(bf16[256,1536]{1,0:T(8,128)(2,1)S(1)} %out_product.11), channel_id=1, source_target_pairs={{0,16},{8,24},{16,0},{24,8},{1,17},{9,25},{17,1},{25,9},{2,18},{10... | collective-permute-start | bytes 2359304 | tf_op jit(solution)/shard_map/ppermute | solution.py:121
  405.7 44.6 %collective-permute-start.33 = (bf16[256,1536]{1,0:T(8,128)(2,1)S(1)}, bf16[256,1536]{1,0:T(8,128)(2,1)S(1)}, u32[]{:S(2)}, u32[]{:S(2)}) collective-permute-start(bf16[256,1536]{1,0:T(8,128)(2,1)S(1)} %back_product.8), channel_id=1, source_target_pairs={{0,16},{8,24},{16,0},{24,8},{1,17},{9,25},{17,1},{25,9},{2,18},{10... | collective-permute-start | bytes 2359304 | tf_op jit(solution)/shard_map/ppermute | solution.py:121
  411.6 39.4 %collective-permute-start.36 = (bf16[2,2,64,1536]{3,2,0,1:T(8,128)(2,1)S(1)}, bf16[2,2,64,1536]{3,2,0,1:T(8,128)(2,1)S(1)}, u32[]{:S(2)}, u32[]{:S(2)}) collective-permute-start(bf16[2,2,64,1536]{3,2,0,1:T(8,128)(2,1)S(1)} %bitcast.101), channel_id=1, source_target_pairs={{0,2},{2,0},{4,6},{6,4},{1,3},{3,1},{5,7},{7,5},{8,10},{10,8},{12,... | collective-permute-start | bytes 2359304 | tf_op jit(solution)/shard_map/ppermute | solution.py:121
  423.2 30.8 %collective-permute-start.27 = (bf16[2,64,1536]{2,1,0:T(8,128)(2,1)S(1)}, bf16[2,64,1536]{2,1,0:T(8,128)(2,1)S(1)}, u32[]{:S(2)}, u32[]{:S(2)}) collective-permute-start(bf16[2,64,1536]{2,1,0:T(8,128)(2,1)S(1)} %fusion.40), channel_id=1, source_target_pairs={{0,2},{2,0},{4,6},{6,4},{1,3},{3,1},{5,7},{7,5},{8,10},{10,8},{12,... | collective-permute-start | bytes 1179656 | tf_op jit(solution)/shard_map/ppermute | solution.py:121
  434.6 19.8 %collective-permute-start.30 = (bf16[2,64,1536]{2,1,0:T(8,128)(2,1)S(1)}, bf16[2,64,1536]{2,1,0:T(8,128)(2,1)S(1)}, u32[]{:S(2)}, u32[]{:S(2)}) collective-permute-start(bf16[2,64,1536]{2,1,0:T(8,128)(2,1)S(1)} %fusion.41), channel_id=1, source_target_pairs={{0,2},{2,0},{4,6},{6,4},{1,3},{3,1},{5,7},{7,5},{8,10},{10,8},{12,... | collective-permute-start | bytes 1179656 | tf_op jit(solution)/shard_map/ppermute | solution.py:121
  450.6 18.2 %collective-permute-start.34 = (bf16[2,64,1536]{2,1,0:T(8,128)(2,1)S(1)}, bf16[2,64,1536]{2,1,0:T(8,128)(2,1)S(1)}, u32[]{:S(2)}, u32[]{:S(2)}) collective-permute-start(bf16[2,64,1536]{2,1,0:T(8,128)(2,1)S(1)} %fusion.42), channel_id=1, source_target_pairs={{0,2},{2,0},{4,6},{6,4},{1,3},{3,1},{5,7},{7,5},{8,10},{10,8},{12,... | collective-permute-start | bytes 1179656 | tf_op jit(solution)/shard_map/ppermute | solution.py:121
  451.3 34.1 %collective-permute-start.37 = (bf16[2,64,1536]{2,1,0:T(8,128)(2,1)S(1)}, bf16[2,64,1536]{2,1,0:T(8,128)(2,1)S(1)}, u32[]{:S(2)}, u32[]{:S(2)}) collective-permute-start(bf16[2,64,1536]{2,1,0:T(8,128)(2,1)S(1)} %fusion.39), channel_id=1, source_target_pairs={{0,4},{2,6},{4,0},{6,2},{1,5},{3,7},{5,1},{7,3},{8,12},{10,14},{12... | collective-permute-start | bytes 1179656 | tf_op jit(solution)/shard_map/ppermute | solution.py:121
  454.1 48.5 %collective-permute-start.28 = (bf16[64,1536]{1,0:T(8,128)(2,1)S(1)}, bf16[64,1536]{1,0:T(8,128)(2,1)}, u32[]{:S(2)}, u32[]{:S(2)}) collective-permute-start(bf16[64,1536]{1,0:T(8,128)(2,1)S(1)} %fusion.47), channel_id=1, source_target_pairs={{0,4},{2,6},{4,0},{6,2},{1,5},{3,7},{5,1},{7,3},{8,12},{10,14},{12... | collective-permute-start | bytes 589832 | tf_op jit(solution)/shard_map/ppermute | solution.py:121
  454.5 49.7 %collective-permute-start.31 = (bf16[64,1536]{1,0:T(8,128)(2,1)S(1)}, bf16[64,1536]{1,0:T(8,128)(2,1)}, u32[]{:S(2)}, u32[]{:S(2)}) collective-permute-start(bf16[64,1536]{1,0:T(8,128)(2,1)S(1)} %fusion.48), channel_id=1, source_target_pairs={{0,4},{2,6},{4,0},{6,2},{1,5},{3,7},{5,1},{7,3},{8,12},{10,14},{12... | collective-permute-start | bytes 589832 | tf_op jit(solution)/shard_map/ppermute | solution.py:121
  468.9 27.1 %collective-permute-start.35 = (bf16[64,1536]{1,0:T(8,128)(2,1)S(1)}, bf16[64,1536]{1,0:T(8,128)(2,1)S(1)}, u32[]{:S(2)}, u32[]{:S(2)}) collective-permute-start(bf16[64,1536]{1,0:T(8,128)(2,1)S(1)} %fusion.49), channel_id=1, source_target_pairs={{0,4},{2,6},{4,0},{6,2},{1,5},{3,7},{5,1},{7,3},{8,12},{10,14},{12... | collective-permute-start | bytes 589832 | tf_op jit(solution)/shard_map/ppermute | solution.py:121
  485.4 11.3 %copy-start.36 = (bf16[64,3072]{1,0:T(8,128)(2,1)S(1)}, bf16[64,3072]{1,0:T(8,128)(2,1)}, u32[]{:S(2)}) copy-start(bf16[64,3072]{1,0:T(8,128)(2,1)} %param.8) | copy-start | bytes 1179652
  485.5 10.6 %collective-permute-start.38 = (bf16[64,1536]{1,0:T(8,128)(2,1)S(1)}, bf16[64,1536]{1,0:T(8,128)(2,1)S(1)}, u32[]{:S(2)}, u32[]{:S(2)}) collective-permute-start(bf16[64,1536]{1,0:T(8,128)(2,1)S(1)} %fusion.50), channel_id=1, source_target_pairs={{0,16},{8,24},{16,0},{24,8},{1,17},{9,25},{17,1},{25,9},{2,18},{10... | collective-permute-start | bytes 589832 | tf_op jit(solution)/shard_map/ppermute | solution.py:121
  (37 other events, 149.9 us)

commit v13 on v12

--- a/solution.py
+++ b/solution.py
@@ -330,7 +330,7 @@
     )(*(value for value, *_ in terms), *weights, *(add for add, _ in adds))
 
 
-MLP_CUTS = (256, 512, 768)
+MLP_CUTS = (512, 256, 768)
 
 
 def body(layer_input, out_cotangent, w_query, w_key, w_value, w_mlp_in, w_attn_out, w_mlp_out):
@@ -350,8 +350,7 @@
         return jnp.stack([block, trade(block, "gx", 2)])
 
     def over_z(pair):
-        near, far = trade(pair, "gy", 1), trade(pair, "gy", 2)
-        return [pair, near, far, trade(far, "gy", 1)]
+        return [pair, trade(pair, "gy", 1), trade(pair, "gy", 2)]
 
     def with_core(part):
         return part, trade(part, "gx", 1)
@@ -377,23 +376,27 @@
     normed_pair = with_x(half(normed))
 
     cot_parts, normed_parts = over_z(cot_pair), over_z(normed_pair)
+    cot_parts.append(trade(cot_parts[2], "gy", 1))
     cot_owns, cot_gots = [], []
     for place, part in enumerate(cot_parts):
         own, other = with_core(part)
         if place == 2:
             own = after(own, cot_owns[1], cot_gots[0])
         if place == 3:
-            own = after(own, cot_gots[1], cot_gots[2], normed_parts[2])
+            own = after(own, cot_gots[1], cot_gots[2])
         cot_owns.append(cot_product((own, other), w_attn_out, w_mlp_out))
         cot_gots.append(others(cot_owns[-1]))
-    all_in = assemble([with_core(part) for part in normed_parts])
+    normed_parts.append(trade(after(normed_parts[2], *cot_owns[1:3]), "gy", 1))
+    normed_parts = [with_core(part) for part in normed_parts]
+    normed_parts[0] = after(normed_parts[0], cot_owns[3])
+    all_in = assemble(normed_parts)
 
     in_heads = swap(after(packed_heads, normed_pair, cot_owns[0]))
-    in_mlp = [swap(after(packed_mlp[0], in_heads, cot_owns[2], *normed_parts[1:3]))]
-    in_mlp.append(swap(after(packed_mlp[1], in_mlp[0], cot_owns[3], all_in)))
+    in_mlp = [swap(after(packed_mlp[0], in_heads, cot_owns[2]))]
+    in_mlp.append(swap(after(packed_mlp[1], in_mlp[0], all_in)))
     heads_own = in_product(after(all_in, cot_gots[3]), in_heads)
     heads_got = others(heads_own)
-    mlp_own = [in_product(after(all_in, heads_own), in_mlp[0])]
+    mlp_own = [in_product(after(all_in, heads_own, in_mlp[1]), in_mlp[0])]
     mlp_got = [others(mlp_own[0])]
     in_mlp.append(swap(after(packed_mlp[2], in_mlp[1], heads_own)))
     mlp_own.append(in_product(after(all_in, mlp_own[0]), in_mlp[1]))

time: 509 us -> 494 us (0.971)
  waiting for transfers between devices: 210 us -> 189 us
  starting transfers between devices: 57.7 us -> 64.2 us
    ppermute x39, waiting for transfers between devices: 210 us -> 175 us  [trade(): return lax.ppermute(block, axis, pairs)]
    all_to_all x4, waiting for transfers between devices: 0.01 us -> 13.7 us  [swap(): lax.all_to_all(packed, 'gx', split_axis=0, concat_axis=0, tiled=True)]
    ppermute x39, starting transfers between devices: 38.1 us -> 44.5 us  [trade(): return lax.ppermute(block, axis, pairs)]
    unnamed x85 -> x87, local copies, waits for them, and re-layouts: 22.3 us -> 22.1 us
  transfers between devices with their start and end apart: 43 -> 43, of which waited for: 15 -> 14; matrix products, arithmetic and copies ran while one was open for 3% -> 4% of each run, Pallas kernels for 35% -> 36%
where the time goes in v13:
time: 494 us; the launch traced here: 491 us
  waiting for transfers between devices  189 us (38%)
  Pallas kernels  184 us (37%)
  starting transfers between devices  64.2 us (13%)
  local copies, waits for them, and re-layouts  22.5 us (5%)
  other arithmetic  19.3 us (4%)
  blocking collectives  10.5 us (2%)
    ppermute x39, waiting for transfers between devices, trade(): return lax.ppermute(block, axis, pairs)  175 us
    pallas_call x11, Pallas kernels, product(): pl.pallas_call(kernel, grid=(columns // tile,), in_specs=specs, out_specs...  68.7 us
    ppermute x39, starting transfers between devices, trade(): return lax.ppermute(block, axis, pairs)  44.5 us
    pallas_call x5, Pallas kernels, in_product(): pl.pallas_call(in_kernel, grid=(columns // tile,), in_specs=[pl.BlockSpec...  39.6 us
    pallas_call x4, Pallas kernels, cot_product(): pl.pallas_call(cot_kernel, grid=(columns // tile,), in_specs=[whole, whol...  32.6 us
    unnamed x87, local copies, waits for them, and re-layouts  22.1 us
    all_to_all x4, starting transfers between devices, swap(): lax.all_to_all(packed, 'gx', split_axis=0, concat_axis=0, tiled=True)  19.6 us
    pallas_call x4, Pallas kernels, pack(): pl.pallas_call(pack_kernel, grid=(owners, width // tile), in_specs=[spec]...  18.9 us
  transfers between devices with their start and end apart: 43, of which 14 were waited for; matrix products, arithmetic and copies ran while one was open for 4% of the time, Pallas kernels for 36%

profile of v13, /device:TPU:0, one launch (start us, length us, event | category | flops | bytes accessed | tf_op | source)
XLA Modules:
  0.0 491.0 jit_solution(5500496064329992001)
XLA Ops:
  0.6 3.0 collective-permute-start.2
  4.8 4.9 %all-reduce.1 = (f32[64]{0:T(128)S(1)}, f32[64]{0:T(128)S(1)}) all-reduce(f32[64]{0:T(128)S(1)} %get-tuple-element.59, f32[64]{0:T(128)S(1)} %get-tuple-element.58), channel_id=1, replica_groups=mesh['gx'=4,'gy'=4,'gz'=2] {'gz'}, use_global_device_ids=true, to_apply=%region_3.0 | all-reduce | flops 128 | bytes 1024 | tf_op jit(solution)/shard_map/psum | solution.py:371
  14.4 5.2 %pack.4 = bf16[4,768,1152]{2,1,0:T(8,128)(2,1)} custom-call(bf16[768,1536]{1,0:T(8,128)(2,1)S(1)} %copy-done.21, bf16[768,1536]{1,0:T(8,128)(2,1)S(1)} %copy-done.22, bf16[768,1536]{1,0:T(8,128)(2,1)} %refs_2_.1), custom_call_target="tpu_custom_call" | custom-call | bytes 221184 | tf_op jit(solution)/shard_map/pack/pallas_call | solution.py:148
  22.4 8.2 %cot_product.5 = bf16[256,1920]{1,0:T(8,128)(2,1)S(1)} custom-call(bf16[2,64,3072]{2,1,0:T(8,128)(2,1)S(1)} %pad_maximum_fusion.1.own_ref, bf16[2,64,3072]{2,1,0:T(8,128)(2,1)S(1)} %collective-permute-done.8.other_ref, bf16[384,3072]{1,0:T(8,128)(2,1)S(1)} %copy-done, bf16[1536,3072]{1,0:T(8,128)(2,1)} %refs_1_.11), custom_call_target="tpu_custom_call" | custom-call | flops 47185920 | bytes 199680 | tf_op jit(solution)/shard_map/cot_product/pallas_call | solution.py:214
  30.5 5.4 %all-to-all-start = ((bf16[4,768,1152]{2,1,0:T(8,128)(2,1)}), bf16[4,768,1152]{2,1,0:T(8,128)(2,1)}, u32[]{:S(2)}, u32[]{:S(2)}) async-start(bf16[4,768,1152]{2,1,0:T(8,128)(2,1)} %pack.4), calls=%async_computation | async-start | bytes 14155776 | tf_op jit(solution)/shard_map/all_to_all | solution.py:359
  37.9 2.6 collective-permute-start.3
  42.0 30.9 %collective-permute-done.5.own_ref = bf16[2,64,3072]{2,1,0:T(8,128)(2,1)S(1)} collective-permute-done((bf16[2,64,3072]{2,1,0:T(8,128)(2,1)}, bf16[2,64,3072]{2,1,0:T(8,128)(2,1)S(1)}, u32[]{:S(2)}, u32[]{:S(2)}) %collective-permute-start.5) | collective-permute-done | bytes 786464 | tf_op jit(solution)/shard_map/ppermute | solution.py:121
  75.4 4.8 pack.6
  82.2 8.1 %cot_product.4 = bf16[256,1920]{1,0:T(8,128)(2,1)S(1)} custom-call(bf16[2,64,3072]{2,1,0:T(8,128)(2,1)S(1)} %collective-permute-done.5.own_ref, bf16[2,64,3072]{2,1,0:T(8,128)(2,1)S(1)} %collective-permute-done.6.other_ref, bf16[384,3072]{1,0:T(8,128)(2,1)S(1)} %copy-done, bf16[1536,3072]{1,0:T(8,128)(2,1)} %refs_1_.11), custom_call_target="tpu_custom_call" | custom-call | flops 47185920 | bytes 199680 | tf_op jit(solution)/shard_map/cot_product/pallas_call | solution.py:214
  92.3 8.1 %cot_product.6 = bf16[256,1920]{1,0:T(8,128)(2,1)S(1)} custom-call(bf16[2,64,3072]{2,1,0:T(8,128)(2,1)S(1)} %collective-permute-done.3.own_ref, bf16[2,64,3072]{2,1,0:T(8,128)(2,1)S(1)} %collective-permute-done.10.other_ref, bf16[384,3072]{1,0:T(8,128)(2,1)S(1)} %copy-done, bf16[1536,3072]{1,0:T(8,128)(2,1)} %refs_1_.11), custom_call_target="tpu_custom_call" | custom-call | flops 47185920 | bytes 199680 | tf_op jit(solution)/shard_map/cot_product/pallas_call | solution.py:214
  101.4 13.7 %all-to-all-done = bf16[4,768,1152]{2,1,0:T(8,128)(2,1)} async-done(((bf16[4,768,1152]{2,1,0:T(8,128)(2,1)}), bf16[4,768,1152]{2,1,0:T(8,128)(2,1)}, u32[]{:S(2)}, u32[]{:S(2)}) %all-to-all-start) | async-done | bytes 7077920 | tf_op jit(solution)/shard_map/all_to_all | solution.py:359
  115.1 4.8 all-to-all-start.1
  125.8 16.8 %collective-permute-done.4.own_ref = bf16[2,64,3072]{2,1,0:T(8,128)(2,1)S(1)} collective-permute-done((bf16[2,64,3072]{2,1,0:T(8,128)(2,1)}, bf16[2,64,3072]{2,1,0:T(8,128)(2,1)S(1)}, u32[]{:S(2)}, u32[]{:S(2)}) %collective-permute-start.4) | collective-permute-done | bytes 786464 | tf_op jit(solution)/shard_map/ppermute | solution.py:121
  142.6 16.8 %collective-permute-done.13.refs_2_ = bf16[2,64,3072]{2,1,0:T(8,128)(2,1)S(1)} collective-permute-done((bf16[2,64,3072]{2,1,0:T(8,128)(2,1)}, bf16[2,64,3072]{2,1,0:T(8,128)(2,1)S(1)}, u32[]{:S(2)}, u32[]{:S(2)}) %collective-permute-start.13) | collective-permute-done | bytes 786464 | tf_op jit(solution)/shard_map/ppermute | solution.py:121
  160.9 14.3 %collective-permute-done.17.refs_6_ = bf16[2,64,3072]{2,1,0:T(8,128)(2,1)S(1)} collective-permute-done((bf16[2,64,3072]{2,1,0:T(8,128)(2,1)}, bf16[2,64,3072]{2,1,0:T(8,128)(2,1)S(1)}, u32[]{:S(2)}, u32[]{:S(2)}) %collective-permute-start.17) | collective-permute-done | bytes 786464 | tf_op jit(solution)/shard_map/ppermute | solution.py:121
  179.1 8.1 %cot_product.7 = bf16[256,1920]{1,0:T(8,128)(2,1)S(1)} custom-call(bf16[2,64,3072]{2,1,0:T(8,128)(2,1)S(1)} %collective-permute-done.4.own_ref, bf16[2,64,3072]{2,1,0:T(8,128)(2,1)S(1)} %collective-permute-done.12.other_ref, bf16[384,3072]{1,0:T(8,128)(2,1)S(1)} %copy-done, bf16[1536,3072]{1,0:T(8,128)(2,1)} %refs_1_.11), custom_call_target="tpu_custom_call" | custom-call | flops 47185920 | bytes 199680 | tf_op jit(solution)/shard_map/cot_product/pallas_call | solution.py:214
  188.3 5.0 %assemble.1.rows_ref = bf16[1024,3072]{1,0:T(8,128)(2,1)} custom-call(bf16[2,64,3072]{2,1,0:T(8,128)(2,1)} %pad_maximum_fusion.refs_0_, bf16[2,64,3072]{2,1,0:T(8,128)(2,1)S(1)} %collective-permute-done.1.refs_1_, bf16[2,64,3072]{2,1,0:T(8,128)(2,1)S(1)} %collective-permute-done.13.refs_2_, bf16[2,64,3072]{2,1,0:T(8,128)(2,1)S(1)} %collective-permute-done.14.refs_3_, ...), custom_call_target="tpu_custom_call" | custom-call | bytes 196608 | tf_op jit(solution)/shard_map/assemble/pallas_call | solution.py:178
  193.2 4.4 all-to-all-start.2
  199.4 6.7 %pack.7 = bf16[4,768,768]{2,1,0:T(8,128)(2,1)S(1)} custom-call(bf16[768,6144]{1,0:T(8,128)(2,1)} %refs_0_.7), custom_call_target="tpu_custom_call" | custom-call | bytes 147456 | tf_op jit(solution)/shard_map/pack/pallas_call | solution.py:148
  208.2 13.5 %collective-permute-done.19 = bf16[256,1920]{1,0:T(8,128)(2,1)S(1)} collective-permute-done((bf16[256,1920]{1,0:T(8,128)(2,1)S(1)}, bf16[256,1920]{1,0:T(8,128)(2,1)S(1)}, u32[]{:S(2)}, u32[]{:S(2)}) %collective-permute-start.19) | collective-permute-done | bytes 983072 | tf_op jit(solution)/shard_map/ppermute | solution.py:121
  222.7 14.0 %in_product.5.q_own.k_own.v_own = bf16[1024,1152]{1,0:T(8,128)(2,1)S(1)} custom-call(bf16[1024,3072]{1,0:T(8,128)(2,1)} %assemble.1.rows_ref, bf16[3072,1152]{1,0:T(8,128)(2,1)} %bitcast.4.weight_ref.refs_5_), custom_call_target="tpu_custom_call" | custom-call | flops 113246208 | bytes 245760 | tf_op jit(solution)/shard_map/in_product/pallas_call | solution.py:268
  238.1 5.1 %all-to-all-start.3 = ((bf16[4,768,768]{2,1,0:T(8,128)(2,1)}), bf16[4,768,768]{2,1,0:T(8,128)(2,1)}, u32[]{:S(2)}, u32[]{:S(2)}) async-start(bf16[4,768,768]{2,1,0:T(8,128)(2,1)} %copy-done.6), calls=%async_computation.3 | async-start | bytes 9437184 | tf_op jit(solution)/shard_map/all_to_all | solution.py:359
  245.0 6.9 %in_product.6 = bf16[1024,512]{1,0:T(8,128)(2,1)S(1)} custom-call(bf16[1024,3072]{1,0:T(8,128)(2,1)} %assemble.1.rows_ref, bf16[3072,512]{1,0:T(8,128)(2,1)} %bitcast.5.weight_ref.refs_6_), custom_call_target="tpu_custom_call" | custom-call | flops 50331648 | bytes 163840 | tf_op jit(solution)/shard_map/in_product/pallas_call | solution.py:268
  252.4 6.0 %in_product.9 = bf16[1024,256]{1,0:T(8,128)(2,1)} custom-call(bf16[1024,3072]{1,0:T(8,128)(2,1)} %assemble.1.rows_ref, bf16[3072,256]{1,0:T(8,128)(2,1)} %bitcast.6.weight_ref.refs_7_), custom_call_target="tpu_custom_call" | custom-call | flops 25165824 | bytes 131072 | tf_op jit(solution)/shard_map/in_product/pallas_call | solution.py:268
  259.9 4.5 add_parts.1
  264.4 33.1 %collective-permute-done.20.q_got.k_got.v_got = bf16[1024,1152]{1,0:T(8,128)(2,1)S(1)} collective-permute-done((bf16[1024,1152]{1,0:T(8,128)(2,1)}, bf16[1024,1152]{1,0:T(8,128)(2,1)S(1)}, u32[]{:S(2)}, u32[]{:S(2)}) %collective-permute-start.20) | collective-permute-done | bytes 2359328 | tf_op jit(solution)/shard_map/ppermute | solution.py:121
  299.0 6.4 %in_product.7 = bf16[512,768]{1,0:T(8,128)(2,1)S(1)} custom-call(bf16[1024,3072]{1,0:T(8,128)(2,1)} %assemble.1.rows_ref, bf16[3072,768]{1,0:T(8,128)(2,1)} %bitcast.16.weight_ref.refs_1_), custom_call_target="tpu_custom_call" | custom-call | flops 37748736 | bytes 184320 | tf_op jit(solution)/shard_map/in_product/pallas_call | solution.py:268
  308.8 14.9 %attend.1 = (bf16[1024,384]{1,0:T(8,128)(2,1)S(1)}, bf16[1024,384]{1,0:T(8,128)(2,1)S(1)}, bf16[1024,384]{1,0:T(8,128)(2,1)S(1)}, bf16[1024,384]{1,0:T(8,128)(2,1)S(1)}) custom-call(bf16[1024,1152]{1,0:T(8,128)(2,1)S(1)} %copy-done.2, bf16[1024,1152]{1,0:T(8,128)(2,1)S(1)} %copy-done.5, bf16[1024,1152]{1,0:T(8,128)(2,1)S(1)} %copy-done.2, ...), custom_call_target="tpu_custom_call" | custom-call | flops 12582912 | bytes 98304 | tf_op jit(solution)/shard_map/attend/pallas_call | solution.py:75
  326.4 5.0 %collective-permute-done.22 = bf16[1024,256]{1,0:T(8,128)(2,1)} collective-permute-done((bf16[1024,256]{1,0:T(8,128)(2,1)}, bf16[1024,256]{1,0:T(8,128)(2,1)}, u32[]{:S(2)}, u32[]{:S(2)}) %collective-permute-start.22) | collective-permute-done | bytes 524320 | tf_op jit(solution)/shard_map/ppermute | solution.py:121
  333.2 6.3 %in_product.8 = bf16[512,768]{1,0:T(8,128)(2,1)S(1)} custom-call(bf16[1024,3072]{1,0:T(8,128)(2,1)} %assemble.1.rows_ref, bf16[3072,768]{1,0:T(8,128)(2,1)} %bitcast.16.weight_ref.refs_1_), custom_call_target="tpu_custom_call" | custom-call | flops 37748736 | bytes 184320 | tf_op jit(solution)/shard_map/in_product/pallas_call | solution.py:268
  343.8 18.5 %back_product.5.refs_2_ = bf16[1024,3072]{1,0:T(8,128)(2,1)} custom-call(bf16[1024,384]{1,0:T(8,128)(2,1)S(1)} %copy-done.30, bf16[1024,384]{1,0:T(8,128)(2,1)S(1)} %copy-done.32, bf16[1024,384]{1,0:T(8,128)(2,1)S(1)} %copy-done.34, bf16[1024,512]{1,0:T(8,128)(2,1)S(1)} %get-tuple-element.68.refs_3_, bf16[1024,256]{1,0:T(8,128)(2,1)S(1)} %get-tuple-element.76.refs_4_, ...), custom_call_target="tpu_custom_call" | custom-call | flops 188743680 | bytes 282624 | tf_op jit(solution)/shard_map/back_product/pallas_call | solution.py:321
  362.4 12.3 %out_product.6.refs_2_ = bf16[1024,3072]{1,0:T(8,128)(2,1)} custom-call(bf16[1024,384]{1,0:T(8,128)(2,1)S(1)} %copy-done.28, bf16[1024,512]{1,0:T(8,128)(2,1)S(1)} %get-tuple-element.69.refs_1_, bf16[1024,256]{1,0:T(8,128)(2,1)S(1)} %get-tuple-element.77.refs_2_, bf16[384,3072]{1,0:T(8,128)(2,1)S(1)} %copy-done, bf16[1536,3072]{1,0:T(8,128)(2,1)} %refs_1_.11), custom_call_target="tpu_custom_call" | custom-call | flops 113246208 | bytes 282624 | tf_op jit(solution)/shard_map/out_product/pallas_call | solution.py:321
  376.7 7.7 %out_product.7 = bf16[512,3072]{1,0:T(8,128)(2,1)} custom-call(bf16[512,768]{1,0:T(8,128)(2,1)S(1)} %get-tuple-element.75.refs_0_, bf16[1536,3072]{1,0:T(8,128)(2,1)} %refs_1_.11, bf16[1024,3072]{1,0:T(8,128)(2,1)} %out_product.6.refs_2_), custom_call_target="tpu_custom_call" | custom-call | flops 37748736 | bytes 196608 | tf_op jit(solution)/shard_map/out_product/pallas_call | solution.py:321
  384.5 6.9 %back_product.6 = bf16[512,3072]{1,0:T(8,128)(2,1)S(1)} custom-call(bf16[512,768]{1,0:T(8,128)(2,1)S(1)} %get-tuple-element.56.refs_0_, bf16[3072,768]{1,0:T(8,128)(2,1)} %bitcast.16.weight_ref.refs_1_, bf16[1024,3072]{1,0:T(8,128)(2,1)} %back_product.5.refs_2_), custom_call_target="tpu_custom_call" | custom-call | flops 37748736 | bytes 122880 | tf_op jit(solution)/shard_map/back_product/pallas_call | solution.py:321
  394.1 3.2 out_product.9
  399.1 3.2 out_product.11
  402.7 3.9 back_product.9
  408.4 3.3 back_product.8
  413.5 3.2 out_product.10
  416.7 3.2 out_product.8
  420.0 3.3 back_product.7
  425.2 9.5 %collective-permute-done.29 = bf16[256,1536]{1,0:T(8,128)(2,1)S(1)} collective-permute-done((bf16[256,1536]{1,0:T(8,128)(2,1)S(1)}, bf16[256,1536]{1,0:T(8,128)(2,1)S(1)}, u32[]{:S(2)}, u32[]{:S(2)}) %collective-permute-start.29) | collective-permute-done | bytes 786464 | tf_op jit(solution)/shard_map/ppermute | solution.py:121
  436.8 2.7 collective-permute-start.37
  439.5 11.1 %collective-permute-done.33 = bf16[256,1536]{1,0:T(8,128)(2,1)S(1)} collective-permute-done((bf16[256,1536]{1,0:T(8,128)(2,1)S(1)}, bf16[256,1536]{1,0:T(8,128)(2,1)S(1)}, u32[]{:S(2)}, u32[]{:S(2)}) %collective-permute-start.33) | collective-permute-done | bytes 786464 | tf_op jit(solution)/shard_map/ppermute | solution.py:121
  452.6 2.7 collective-permute-start.28
  457.7 11.8 %collective-permute-done.34 = bf16[2,64,1536]{2,1,0:T(8,128)(2,1)S(1)} collective-permute-done((bf16[2,64,1536]{2,1,0:T(8,128)(2,1)S(1)}, bf16[2,64,1536]{2,1,0:T(8,128)(2,1)S(1)}, u32[]{:S(2)}, u32[]{:S(2)}) %collective-permute-start.34) | collective-permute-done | bytes 393248 | tf_op jit(solution)/shard_map/ppermute | solution.py:121
  471.4 9.2 %collective-permute-done.35 = bf16[64,1536]{1,0:T(8,128)(2,1)S(1)} collective-permute-done((bf16[64,1536]{1,0:T(8,128)(2,1)S(1)}, bf16[64,1536]{1,0:T(8,128)(2,1)S(1)}, u32[]{:S(2)}, u32[]{:S(2)}) %collective-permute-start.35) | collective-permute-done | bytes 196640 | tf_op jit(solution)/shard_map/ppermute | solution.py:121
  481.5 5.6 %all-reduce = (f32[64]{0:T(128)S(1)}, f32[64]{0:T(128)}) all-reduce(f32[64]{0:T(128)S(1)} %fusion.28, f32[64]{0:T(128)} %reduce_sum.48), channel_id=1, replica_groups=mesh['gx'=4,'gy'=4,'gz'=2] {'gz'}, use_global_device_ids=true, to_apply=%region_8.9 | all-reduce | flops 128 | bytes 1024 | tf_op jit(solution)/shard_map/psum | solution.py:488
  (189 shorter events, 80.9 us)
Async XLA Ops:
  0.6 19.0 %collective-permute-start.2 = (bf16[64,3072]{1,0:T(8,128)(2,1)}, bf16[64,3072]{1,0:T(8,128)(2,1)S(1)}, u32[]{:S(2)}, u32[]{:S(2)}) collective-permute-start(bf16[64,3072]{1,0:T(8,128)(2,1)} %param.9), channel_id=1, source_target_pairs={{0,16},{8,24},{16,0},{24,8},{1,17},{9,25},{17,1},{25,9},{2,18},{10... | collective-permute-start | bytes 1179656 | tf_op jit(solution)/shard_map/ppermute | solution.py:121
  10.9 10.4 %collective-permute-start = (bf16[64,3072]{1,0:T(8,128)(2,1)S(1)}, bf16[64,3072]{1,0:T(8,128)(2,1)S(1)}, u32[]{:S(2)}, u32[]{:S(2)}) collective-permute-start(bf16[64,3072]{1,0:T(8,128)(2,1)S(1)} %fusion.27), channel_id=1, source_target_pairs={{0,16},{8,24},{16,0},{24,8},{1,17},{9,25},{17,1},{25,9},{2,18},{10... | collective-permute-start | bytes 1179656 | tf_op jit(solution)/shard_map/ppermute | solution.py:121
  19.7 2.7 collective-permute-start.8
  30.5 84.5 %all-to-all-start = ((bf16[4,768,1152]{2,1,0:T(8,128)(2,1)}), bf16[4,768,1152]{2,1,0:T(8,128)(2,1)}, u32[]{:S(2)}, u32[]{:S(2)}) async-start(bf16[4,768,1152]{2,1,0:T(8,128)(2,1)} %pack.4), calls=%async_computation | async-start | bytes 14155776 | tf_op jit(solution)/shard_map/all_to_all | solution.py:359
  35.9 36.9 %collective-permute-start.5 = (bf16[2,64,3072]{2,1,0:T(8,128)(2,1)}, bf16[2,64,3072]{2,1,0:T(8,128)(2,1)S(1)}, u32[]{:S(2)}, u32[]{:S(2)}) collective-permute-start(bf16[2,64,3072]{2,1,0:T(8,128)(2,1)} %copy-done.18), channel_id=1, source_target_pairs={{0,2},{2,0},{4,6},{6,4},{1,3},{3,1},{5,7},{7,5},{8,10},{10,8},{12,... | collective-permute-start | bytes 2359304 | tf_op jit(solution)/shard_map/ppermute | solution.py:121
  37.9 37.5 %collective-permute-start.3 = (bf16[2,64,3072]{2,1,0:T(8,128)(2,1)}, bf16[2,64,3072]{2,1,0:T(8,128)(2,1)S(1)}, u32[]{:S(2)}, u32[]{:S(2)}) collective-permute-start(bf16[2,64,3072]{2,1,0:T(8,128)(2,1)} %copy-done.18), channel_id=1, source_target_pairs={{0,4},{2,6},{4,0},{6,2},{1,5},{3,7},{5,1},{7,3},{8,12},{10,14},{12... | collective-permute-start | bytes 2359304 | tf_op jit(solution)/shard_map/ppermute | solution.py:121
  40.5 50.8 %collective-permute-start.9 = (bf16[256,1920]{1,0:T(8,128)(2,1)S(1)}, bf16[256,1920]{1,0:T(8,128)(2,1)S(1)}, u32[]{:S(2)}, u32[]{:S(2)}) collective-permute-start(bf16[256,1920]{1,0:T(8,128)(2,1)S(1)} %cot_product.5), channel_id=1, source_target_pairs={{0,1},{1,0},{2,3},{3,2},{4,5},{5,4},{6,7},{7,6},{8,9},{9,8},{10,11... | collective-permute-start | bytes 2949128 | tf_op jit(solution)/shard_map/ppermute | solution.py:121
  72.9 9.3 %collective-permute-start.6 = (bf16[2,64,3072]{2,1,0:T(8,128)(2,1)S(1)}, bf16[2,64,3072]{2,1,0:T(8,128)(2,1)S(1)}, u32[]{:S(2)}, u32[]{:S(2)}) collective-permute-start(bf16[2,64,3072]{2,1,0:T(8,128)(2,1)S(1)} %collective-permute-done.5.own_ref), channel_id=1, source_target_pairs={{0,8},{8,0},{16,24},{24,16},{1,9},{9,1},{17,25},{25,17},{2,10},{10... | collective-permute-start | bytes 2359304 | tf_op jit(solution)/shard_map/ppermute | solution.py:121
  75.4 16.9 %copy-start.35 = (bf16[2,64,3072]{2,1,0:T(8,128)(2,1)}, bf16[2,64,3072]{2,1,0:T(8,128)(2,1)S(1)}, u32[]{:S(2)}) copy-start(bf16[2,64,3072]{2,1,0:T(8,128)(2,1)S(1)} %collective-permute-done.3.own_ref) | copy-start | bytes 2359300
  75.4 16.9 %collective-permute-start.10 = (bf16[2,64,3072]{2,1,0:T(8,128)(2,1)S(1)}, bf16[2,64,3072]{2,1,0:T(8,128)(2,1)S(1)}, u32[]{:S(2)}, u32[]{:S(2)}) collective-permute-start(bf16[2,64,3072]{2,1,0:T(8,128)(2,1)S(1)} %collective-permute-done.3.own_ref), channel_id=1, source_target_pairs={{0,8},{8,0},{16,24},{24,16},{1,9},{9,1},{17,25},{25,17},{2,10},{10... | collective-permute-start | bytes 2359304 | tf_op jit(solution)/shard_map/ppermute | solution.py:121
  81.8 42.1 %collective-permute-start.15 = (bf16[2,64,3072]{2,1,0:T(8,128)(2,1)}, bf16[2,64,3072]{2,1,0:T(8,128)(2,1)}, u32[]{:S(2)}, u32[]{:S(2)}) collective-permute-start(bf16[2,64,3072]{2,1,0:T(8,128)(2,1)} %pad_maximum_fusion.refs_0_), channel_id=1, source_target_pairs={{0,4},{2,6},{4,0},{6,2},{1,5},{3,7},{5,1},{7,3},{8,12},{10,14},{12... | collective-permute-start | bytes 2359304 | tf_op jit(solution)/shard_map/ppermute | solution.py:121
  115.1 78.2 %all-to-all-start.1 = ((bf16[4,768,512]{2,1,0:T(8,128)(2,1)}), bf16[4,768,512]{2,1,0:T(8,128)(2,1)}, u32[]{:S(2)}, u32[]{:S(2)}) async-start(bf16[4,768,512]{2,1,0:T(8,128)(2,1)} %copy-done.7), calls=%async_computation.1 | async-start | bytes 6291456 | tf_op jit(solution)/shard_map/all_to_all | solution.py:359
  119.8 39.6 %collective-permute-start.7 = (bf16[256,1920]{1,0:T(8,128)(2,1)S(1)}, bf16[256,1920]{1,0:T(8,128)(2,1)S(1)}, u32[]{:S(2)}, u32[]{:S(2)}) collective-permute-start(bf16[256,1920]{1,0:T(8,128)(2,1)S(1)} %copy-done.12), channel_id=1, source_target_pairs={{0,1},{1,0},{2,3},{3,2},{4,5},{5,4},{6,7},{7,6},{8,9},{9,8},{10,11... | collective-permute-start | bytes 2949128 | tf_op jit(solution)/shard_map/ppermute | solution.py:121
  121.7 53.5 %collective-permute-start.11 = (bf16[256,1920]{1,0:T(8,128)(2,1)}, bf16[256,1920]{1,0:T(8,128)(2,1)S(1)}, u32[]{:S(2)}, u32[]{:S(2)}) collective-permute-start(bf16[256,1920]{1,0:T(8,128)(2,1)} %copy-done.14), channel_id=1, source_target_pairs={{0,1},{1,0},{2,3},{3,2},{4,5},{5,4},{6,7},{7,6},{8,9},{9,8},{10,11... | collective-permute-start | bytes 2949128 | tf_op jit(solution)/shard_map/ppermute | solution.py:121
  122.0 20.6 %collective-permute-start.4 = (bf16[2,64,3072]{2,1,0:T(8,128)(2,1)}, bf16[2,64,3072]{2,1,0:T(8,128)(2,1)S(1)}, u32[]{:S(2)}, u32[]{:S(2)}) collective-permute-start(bf16[2,64,3072]{2,1,0:T(8,128)(2,1)} %copy-done.35), channel_id=1, source_target_pairs={{0,2},{2,0},{4,6},{6,4},{1,3},{3,1},{5,7},{7,5},{8,10},{10,8},{12,... | collective-permute-start | bytes 2359304 | tf_op jit(solution)/shard_map/ppermute | solution.py:121
  123.8 35.7 %collective-permute-start.13 = (bf16[2,64,3072]{2,1,0:T(8,128)(2,1)}, bf16[2,64,3072]{2,1,0:T(8,128)(2,1)S(1)}, u32[]{:S(2)}, u32[]{:S(2)}) collective-permute-start(bf16[2,64,3072]{2,1,0:T(8,128)(2,1)} %pad_maximum_fusion.refs_0_), channel_id=1, source_target_pairs={{0,2},{2,0},{4,6},{6,4},{1,3},{3,1},{5,7},{7,5},{8,10},{10,8},{12,... | collective-permute-start | bytes 2359304 | tf_op jit(solution)/shard_map/ppermute | solution.py:121
  124.0 51.2 %collective-permute-start.17 = (bf16[2,64,3072]{2,1,0:T(8,128)(2,1)}, bf16[2,64,3072]{2,1,0:T(8,128)(2,1)S(1)}, u32[]{:S(2)}, u32[]{:S(2)}) collective-permute-start(bf16[2,64,3072]{2,1,0:T(8,128)(2,1)} %collective-permute-done.15.refs_4_), channel_id=1, source_target_pairs={{0,2},{2,0},{4,6},{6,4},{1,3},{3,1},{5,7},{7,5},{8,10},{10,8},{12,... | collective-permute-start | bytes 2359304 | tf_op jit(solution)/shard_map/ppermute | solution.py:121
  142.6 36.5 %collective-permute-start.12 = (bf16[2,64,3072]{2,1,0:T(8,128)(2,1)S(1)}, bf16[2,64,3072]{2,1,0:T(8,128)(2,1)S(1)}, u32[]{:S(2)}, u32[]{:S(2)}) collective-permute-start(bf16[2,64,3072]{2,1,0:T(8,128)(2,1)S(1)} %collective-permute-done.4.own_ref), channel_id=1, source_target_pairs={{0,8},{8,0},{16,24},{24,16},{1,9},{9,1},{17,25},{25,17},{2,10},{10... | collective-permute-start | bytes 2359304 | tf_op jit(solution)/shard_map/ppermute | solution.py:121
  159.5 27.8 %collective-permute-start.1 = (bf16[2,64,3072]{2,1,0:T(8,128)(2,1)}, bf16[2,64,3072]{2,1,0:T(8,128)(2,1)S(1)}, u32[]{:S(2)}, u32[]{:S(2)}) collective-permute-start(bf16[2,64,3072]{2,1,0:T(8,128)(2,1)} %pad_maximum_fusion.refs_0_), channel_id=1, source_target_pairs={{0,8},{8,0},{16,24},{24,16},{1,9},{9,1},{17,25},{25,17},{2,10},{10... | collective-permute-start | bytes 2359304 | tf_op jit(solution)/shard_map/ppermute | solution.py:121
  160.4 26.9 %collective-permute-start.16 = (bf16[2,64,3072]{2,1,0:T(8,128)(2,1)}, bf16[2,64,3072]{2,1,0:T(8,128)(2,1)S(1)}, u32[]{:S(2)}, u32[]{:S(2)}) collective-permute-start(bf16[2,64,3072]{2,1,0:T(8,128)(2,1)} %collective-permute-done.15.refs_4_), channel_id=1, source_target_pairs={{0,8},{8,0},{16,24},{24,16},{1,9},{9,1},{17,25},{25,17},{2,10},{10... | collective-permute-start | bytes 2359304 | tf_op jit(solution)/shard_map/ppermute | solution.py:121
  175.2 12.1 %collective-permute-start.14 = (bf16[2,64,3072]{2,1,0:T(8,128)(2,1)S(1)}, bf16[2,64,3072]{2,1,0:T(8,128)(2,1)S(1)}, u32[]{:S(2)}, u32[]{:S(2)}) collective-permute-start(bf16[2,64,3072]{2,1,0:T(8,128)(2,1)S(1)} %collective-permute-done.13.refs_2_), channel_id=1, source_target_pairs={{0,8},{8,0},{16,24},{24,16},{1,9},{9,1},{17,25},{25,17},{2,10},{10... | collective-permute-start | bytes 2359304 | tf_op jit(solution)/shard_map/ppermute | solution.py:121
  175.2 12.1 %collective-permute-start.18 = (bf16[2,64,3072]{2,1,0:T(8,128)(2,1)S(1)}, bf16[2,64,3072]{2,1,0:T(8,128)(2,1)S(1)}, u32[]{:S(2)}, u32[]{:S(2)}) collective-permute-start(bf16[2,64,3072]{2,1,0:T(8,128)(2,1)S(1)} %collective-permute-done.17.refs_6_), channel_id=1, source_target_pairs={{0,8},{8,0},{16,24},{24,16},{1,9},{9,1},{17,25},{25,17},{2,10},{10... | collective-permute-start | bytes 2359304 | tf_op jit(solution)/shard_map/ppermute | solution.py:121
  187.3 10.3 %copy-start.16 = (bf16[256,1920]{1,0:T(8,128)(2,1)}, bf16[256,1920]{1,0:T(8,128)(2,1)S(1)}, u32[]{:S(2)}) copy-start(bf16[256,1920]{1,0:T(8,128)(2,1)S(1)} %cot_product.7) | copy-start | bytes 2949124
  193.2 44.9 %all-to-all-start.2 = ((bf16[4,768,256]{2,1,0:T(8,128)(2,1)}), bf16[4,768,256]{2,1,0:T(8,128)(2,1)}, u32[]{:S(2)}, u32[]{:S(2)}) async-start(bf16[4,768,256]{2,1,0:T(8,128)(2,1)} %copy-done.8), calls=%async_computation.2 | async-start | bytes 3145728 | tf_op jit(solution)/shard_map/all_to_all | solution.py:359
  197.6 24.1 %collective-permute-start.19 = (bf16[256,1920]{1,0:T(8,128)(2,1)S(1)}, bf16[256,1920]{1,0:T(8,128)(2,1)S(1)}, u32[]{:S(2)}, u32[]{:S(2)}) collective-permute-start(bf16[256,1920]{1,0:T(8,128)(2,1)S(1)} %cot_product.7), channel_id=1, source_target_pairs={{0,1},{1,0},{2,3},{3,2},{4,5},{5,4},{6,7},{7,6},{8,9},{9,8},{10,11... | collective-permute-start | bytes 2949128 | tf_op jit(solution)/shard_map/ppermute | solution.py:121
  238.1 60.9 %all-to-all-start.3 = ((bf16[4,768,768]{2,1,0:T(8,128)(2,1)}), bf16[4,768,768]{2,1,0:T(8,128)(2,1)}, u32[]{:S(2)}, u32[]{:S(2)}) async-start(bf16[4,768,768]{2,1,0:T(8,128)(2,1)} %copy-done.6), calls=%async_computation.3 | async-start | bytes 9437184 | tf_op jit(solution)/shard_map/all_to_all | solution.py:359
  243.2 54.4 %collective-permute-start.20 = (bf16[1024,1152]{1,0:T(8,128)(2,1)}, bf16[1024,1152]{1,0:T(8,128)(2,1)S(1)}, u32[]{:S(2)}, u32[]{:S(2)}) collective-permute-start(bf16[1024,1152]{1,0:T(8,128)(2,1)} %copy-done.1), channel_id=1, source_target_pairs={{0,1},{1,0},{2,3},{3,2},{4,5},{5,4},{6,7},{7,6},{8,9},{9,8},{10,11... | collective-permute-start | bytes 7077896 | tf_op jit(solution)/shard_map/ppermute | solution.py:121
  252.0 89.3 %collective-permute-start.21 = (bf16[1024,512]{1,0:T(8,128)(2,1)S(1)}, bf16[1024,512]{1,0:T(8,128)(2,1)}, u32[]{:S(2)}, u32[]{:S(2)}) collective-permute-start(bf16[1024,512]{1,0:T(8,128)(2,1)S(1)} %in_product.6), channel_id=1, source_target_pairs={{0,1},{1,0},{2,3},{3,2},{4,5},{5,4},{6,7},{7,6},{8,9},{9,8},{10,11... | collective-permute-start | bytes 3145736 | tf_op jit(solution)/shard_map/ppermute | solution.py:121
  258.4 73.0 %collective-permute-start.22 = (bf16[1024,256]{1,0:T(8,128)(2,1)}, bf16[1024,256]{1,0:T(8,128)(2,1)}, u32[]{:S(2)}, u32[]{:S(2)}) collective-permute-start(bf16[1024,256]{1,0:T(8,128)(2,1)} %in_product.9), channel_id=1, source_target_pairs={{0,1},{1,0},{2,3},{3,2},{4,5},{5,4},{6,7},{7,6},{8,9},{9,8},{10,11... | collective-permute-start | bytes 1572872 | tf_op jit(solution)/shard_map/ppermute | solution.py:121
  305.4 69.2 %collective-permute-start.23 = (bf16[512,768]{1,0:T(8,128)(2,1)S(1)}, bf16[512,768]{1,0:T(8,128)(2,1)}, u32[]{:S(2)}, u32[]{:S(2)}) collective-permute-start(bf16[512,768]{1,0:T(8,128)(2,1)S(1)} %in_product.7), channel_id=1, source_target_pairs={{0,1},{1,0},{2,3},{3,2},{4,5},{5,4},{6,7},{7,6},{8,9},{9,8},{10,11... | collective-permute-start | bytes 2359304 | tf_op jit(solution)/shard_map/ppermute | solution.py:121
  326.4 13.1 %copy-start.29 = (bf16[1024,384]{1,0:T(8,128)(2,1)}, bf16[1024,384]{1,0:T(8,128)(2,1)S(1)}, u32[]{:S(2)}) copy-start(bf16[1024,384]{1,0:T(8,128)(2,1)S(1)} %get-tuple-element.52.refs_0_) | copy-start | bytes 2359300
  339.6 44.9 %collective-permute-start.24 = (bf16[512,768]{1,0:T(8,128)(2,1)S(1)}, bf16[512,768]{1,0:T(8,128)(2,1)}, u32[]{:S(2)}, u32[]{:S(2)}) collective-permute-start(bf16[512,768]{1,0:T(8,128)(2,1)S(1)} %in_product.8), channel_id=1, source_target_pairs={{0,1},{1,0},{2,3},{3,2},{4,5},{5,4},{6,7},{7,6},{8,9},{9,8},{10,11... | collective-permute-start | bytes 2359304 | tf_op jit(solution)/shard_map/ppermute | solution.py:121
  343.8 18.5 %copy-start.28 = (bf16[1024,384]{1,0:T(8,128)(2,1)S(1)}, bf16[1024,384]{1,0:T(8,128)(2,1)}, u32[]{:S(2)}) copy-start(bf16[1024,384]{1,0:T(8,128)(2,1)} %copy-done.27) | copy-start | bytes 2359300
  384.5 9.6 %collective-permute-start.25 = (bf16[512,3072]{1,0:T(8,128)(2,1)}, bf16[512,3072]{1,0:T(8,128)(2,1)S(1)}, u32[]{:S(2)}, u32[]{:S(2)}) collective-permute-start(bf16[512,3072]{1,0:T(8,128)(2,1)} %out_product.7), channel_id=1, source_target_pairs={{0,8},{8,0},{16,24},{24,16},{1,9},{9,1},{17,25},{25,17},{2,10},{10... | collective-permute-start | bytes 9437192 | tf_op jit(solution)/shard_map/ppermute | solution.py:121
  391.4 11.3 %collective-permute-start.32 = (bf16[512,3072]{1,0:T(8,128)(2,1)S(1)}, bf16[512,3072]{1,0:T(8,128)(2,1)S(1)}, u32[]{:S(2)}, u32[]{:S(2)}) collective-permute-start(bf16[512,3072]{1,0:T(8,128)(2,1)S(1)} %back_product.6), channel_id=1, source_target_pairs={{0,8},{8,0},{16,24},{24,16},{1,9},{9,1},{17,25},{25,17},{2,10},{10... | collective-permute-start | bytes 9437192 | tf_op jit(solution)/shard_map/ppermute | solution.py:121
  397.3 25.9 %collective-permute-start.26 = (bf16[256,1536]{1,0:T(8,128)(2,1)S(1)}, bf16[256,1536]{1,0:T(8,128)(2,1)}, u32[]{:S(2)}, u32[]{:S(2)}) collective-permute-start(bf16[256,1536]{1,0:T(8,128)(2,1)S(1)} %out_product.9), channel_id=1, source_target_pairs={{0,16},{8,24},{16,0},{24,8},{1,17},{9,25},{17,1},{25,9},{2,18},{10... | collective-permute-start | bytes 2359304 | tf_op jit(solution)/shard_map/ppermute | solution.py:121
  402.3 32.3 %collective-permute-start.29 = (bf16[256,1536]{1,0:T(8,128)(2,1)S(1)}, bf16[256,1536]{1,0:T(8,128)(2,1)S(1)}, u32[]{:S(2)}, u32[]{:S(2)}) collective-permute-start(bf16[256,1536]{1,0:T(8,128)(2,1)S(1)} %out_product.11), channel_id=1, source_target_pairs={{0,16},{8,24},{16,0},{24,8},{1,17},{9,25},{17,1},{25,9},{2,18},{10... | collective-permute-start | bytes 2359304 | tf_op jit(solution)/shard_map/ppermute | solution.py:121
  406.8 29.8 %collective-permute-start.36 = (bf16[2,2,64,1536]{3,2,0,1:T(8,128)(2,1)S(1)}, bf16[2,2,64,1536]{3,2,0,1:T(8,128)(2,1)S(1)}, u32[]{:S(2)}, u32[]{:S(2)}) collective-permute-start(bf16[2,2,64,1536]{3,2,0,1:T(8,128)(2,1)S(1)} %bitcast.101), channel_id=1, source_target_pairs={{0,2},{2,0},{4,6},{6,4},{1,3},{3,1},{5,7},{7,5},{8,10},{10,8},{12,... | collective-permute-start | bytes 2359304 | tf_op jit(solution)/shard_map/ppermute | solution.py:121
  411.7 38.9 %collective-permute-start.33 = (bf16[256,1536]{1,0:T(8,128)(2,1)S(1)}, bf16[256,1536]{1,0:T(8,128)(2,1)S(1)}, u32[]{:S(2)}, u32[]{:S(2)}) collective-permute-start(bf16[256,1536]{1,0:T(8,128)(2,1)S(1)} %back_product.8), channel_id=1, source_target_pairs={{0,16},{8,24},{16,0},{24,8},{1,17},{9,25},{17,1},{25,9},{2,18},{10... | collective-permute-start | bytes 2359304 | tf_op jit(solution)/shard_map/ppermute | solution.py:121
  424.6 27.8 %collective-permute-start.27 = (bf16[2,64,1536]{2,1,0:T(8,128)(2,1)S(1)}, bf16[2,64,1536]{2,1,0:T(8,128)(2,1)S(1)}, u32[]{:S(2)}, u32[]{:S(2)}) collective-permute-start(bf16[2,64,1536]{2,1,0:T(8,128)(2,1)S(1)} %fusion.40), channel_id=1, source_target_pairs={{0,2},{2,0},{4,6},{6,4},{1,3},{3,1},{5,7},{7,5},{8,10},{10,8},{12,... | collective-permute-start | bytes 1179656 | tf_op jit(solution)/shard_map/ppermute | solution.py:121
  434.9 20.3 %collective-permute-start.30 = (bf16[2,64,1536]{2,1,0:T(8,128)(2,1)S(1)}, bf16[2,64,1536]{2,1,0:T(8,128)(2,1)S(1)}, u32[]{:S(2)}, u32[]{:S(2)}) collective-permute-start(bf16[2,64,1536]{2,1,0:T(8,128)(2,1)S(1)} %fusion.41), channel_id=1, source_target_pairs={{0,2},{2,0},{4,6},{6,4},{1,3},{3,1},{5,7},{7,5},{8,10},{10,8},{12,... | collective-permute-start | bytes 1179656 | tf_op jit(solution)/shard_map/ppermute | solution.py:121
  436.8 18.9 %collective-permute-start.37 = (bf16[2,64,1536]{2,1,0:T(8,128)(2,1)S(1)}, bf16[2,64,1536]{2,1,0:T(8,128)(2,1)S(1)}, u32[]{:S(2)}, u32[]{:S(2)}) collective-permute-start(bf16[2,64,1536]{2,1,0:T(8,128)(2,1)S(1)} %fusion.39), channel_id=1, source_target_pairs={{0,4},{2,6},{4,0},{6,2},{1,5},{3,7},{5,1},{7,3},{8,12},{10,14},{12... | collective-permute-start | bytes 1179656 | tf_op jit(solution)/shard_map/ppermute | solution.py:121
  450.8 18.7 %collective-permute-start.34 = (bf16[2,64,1536]{2,1,0:T(8,128)(2,1)S(1)}, bf16[2,64,1536]{2,1,0:T(8,128)(2,1)S(1)}, u32[]{:S(2)}, u32[]{:S(2)}) collective-permute-start(bf16[2,64,1536]{2,1,0:T(8,128)(2,1)S(1)} %fusion.42), channel_id=1, source_target_pairs={{0,2},{2,0},{4,6},{6,4},{1,3},{3,1},{5,7},{7,5},{8,10},{10,8},{12,... | collective-permute-start | bytes 1179656 | tf_op jit(solution)/shard_map/ppermute | solution.py:121
  452.6 34.5 %collective-permute-start.28 = (bf16[64,1536]{1,0:T(8,128)(2,1)S(1)}, bf16[64,1536]{1,0:T(8,128)(2,1)}, u32[]{:S(2)}, u32[]{:S(2)}) collective-permute-start(bf16[64,1536]{1,0:T(8,128)(2,1)S(1)} %fusion.47), channel_id=1, source_target_pairs={{0,4},{2,6},{4,0},{6,2},{1,5},{3,7},{5,1},{7,3},{8,12},{10,14},{12... | collective-permute-start | bytes 589832 | tf_op jit(solution)/shard_map/ppermute | solution.py:121
  455.3 33.4 %collective-permute-start.31 = (bf16[64,1536]{1,0:T(8,128)(2,1)S(1)}, bf16[64,1536]{1,0:T(8,128)(2,1)}, u32[]{:S(2)}, u32[]{:S(2)}) collective-permute-start(bf16[64,1536]{1,0:T(8,128)(2,1)S(1)} %fusion.48), channel_id=1, source_target_pairs={{0,4},{2,6},{4,0},{6,2},{1,5},{3,7},{5,1},{7,3},{8,12},{10,14},{12... | collective-permute-start | bytes 589832 | tf_op jit(solution)/shard_map/ppermute | solution.py:121
  455.9 15.4 %collective-permute-start.38 = (bf16[64,1536]{1,0:T(8,128)(2,1)S(1)}, bf16[64,1536]{1,0:T(8,128)(2,1)S(1)}, u32[]{:S(2)}, u32[]{:S(2)}) collective-permute-start(bf16[64,1536]{1,0:T(8,128)(2,1)S(1)} %fusion.50), channel_id=1, source_target_pairs={{0,16},{8,24},{16,0},{24,8},{1,17},{9,25},{17,1},{25,9},{2,18},{10... | collective-permute-start | bytes 589832 | tf_op jit(solution)/shard_map/ppermute | solution.py:121
  469.6 11.7 %copy-start.37 = (bf16[64,3072]{1,0:T(8,128)(2,1)S(1)}, bf16[64,3072]{1,0:T(8,128)(2,1)}, u32[]{:S(2)}) copy-start(bf16[64,3072]{1,0:T(8,128)(2,1)} %param.8) | copy-start | bytes 1179652
  469.6 10.9 %collective-permute-start.35 = (bf16[64,1536]{1,0:T(8,128)(2,1)S(1)}, bf16[64,1536]{1,0:T(8,128)(2,1)S(1)}, u32[]{:S(2)}, u32[]{:S(2)}) collective-permute-start(bf16[64,1536]{1,0:T(8,128)(2,1)S(1)} %fusion.49), channel_id=1, source_target_pairs={{0,4},{2,6},{4,0},{6,2},{1,5},{3,7},{5,1},{7,3},{8,12},{10,14},{12... | collective-permute-start | bytes 589832 | tf_op jit(solution)/shard_map/ppermute | solution.py:121
  (38 other events, 145.5 us)

commit v14 on v13

--- a/solution.py
+++ b/solution.py
@@ -381,18 +381,19 @@
     for place, part in enumerate(cot_parts):
         own, other = with_core(part)
         if place == 2:
-            own = after(own, cot_owns[1], cot_gots[0])
+            own = after(own, cot_owns[1], cot_gots[0], normed_parts[1])
         if place == 3:
-            own = after(own, cot_gots[1], cot_gots[2])
+            own = after(own, cot_gots[1])
         cot_owns.append(cot_product((own, other), w_attn_out, w_mlp_out))
         cot_gots.append(others(cot_owns[-1]))
     normed_parts.append(trade(after(normed_parts[2], *cot_owns[1:3]), "gy", 1))
     normed_parts = [with_core(part) for part in normed_parts]
-    normed_parts[0] = after(normed_parts[0], cot_owns[3])
+    normed_parts[0] = after(normed_parts[0], cot_owns[3], cot_gots[2])
     all_in = assemble(normed_parts)
 
     in_heads = swap(after(packed_heads, normed_pair, cot_owns[0]))
-    in_mlp = [swap(after(packed_mlp[0], in_heads, cot_owns[2]))]
+    early = (cot_owns[2], cot_gots[1], cot_parts[3])
+    in_mlp = [swap(after(packed_mlp[0], in_heads, *early))]
     in_mlp.append(swap(after(packed_mlp[1], in_mlp[0], all_in)))
     heads_own = in_product(after(all_in, cot_gots[3]), in_heads)
     heads_got = others(heads_own)

time: 494 us -> 477 us (0.966)
  waiting for transfers between devices: 189 us -> 174 us
    all_to_all x4, waiting for transfers between devices: 13.7 us -> 0.01 us  [swap(): lax.all_to_all(packed, 'gx', split_axis=0, concat_axis=0, tiled=True)]
    unnamed x87 -> x93, local copies, waits for them, and re-layouts: 22.1 us -> 21.9 us
  transfers between devices with their start and end apart: 43 -> 43, of which waited for: 14 -> 14; matrix products, arithmetic and copies ran while one was open for 4% -> 4% of each run, Pallas kernels for 36% -> 37%
where the time goes in v14:
time: 477 us; the launch traced here: 474 us
  Pallas kernels  184 us (39%)
  waiting for transfers between devices  174 us (36%)
  starting transfers between devices  62.4 us (13%)
  local copies, waits for them, and re-layouts  22.3 us (5%)
  other arithmetic  19.3 us (4%)
  blocking collectives  10.5 us (2%)
    ppermute x39, waiting for transfers between devices, trade(): return lax.ppermute(block, axis, pairs)  174 us
    pallas_call x11, Pallas kernels, product(): pl.pallas_call(kernel, grid=(columns // tile,), in_specs=specs, out_specs...  68.7 us
    ppermute x39, starting transfers between devices, trade(): return lax.ppermute(block, axis, pairs)  42.8 us
    pallas_call x5, Pallas kernels, in_product(): pl.pallas_call(in_kernel, grid=(columns // tile,), in_specs=[pl.BlockSpec...  39.7 us
    pallas_call x4, Pallas kernels, cot_product(): pl.pallas_call(cot_kernel, grid=(columns // tile,), in_specs=[whole, whol...  33 us
    unnamed x93, local copies, waits for them, and re-layouts  21.9 us
    all_to_all x4, starting transfers between devices, swap(): lax.all_to_all(packed, 'gx', split_axis=0, concat_axis=0, tiled=True)  19.7 us
    pallas_call x4, Pallas kernels, pack(): pl.pallas_call(pack_kernel, grid=(owners, width // tile), in_specs=[spec]...  18.6 us
  transfers between devices with their start and end apart: 43, of which 14 were waited for; matrix products, arithmetic and copies ran while one was open for 4% of the time, Pallas kernels for 37%

profile of v14, /device:TPU:0, one launch (start us, length us, event | category | flops | bytes accessed | tf_op | source)
XLA Modules:
  0.0 474.2 jit_solution(12213582392691645499)
XLA Ops:
  0.6 3.0 collective-permute-start.2
  4.8 4.9 %all-reduce.1 = (f32[64]{0:T(128)S(1)}, f32[64]{0:T(128)S(1)}) all-reduce(f32[64]{0:T(128)S(1)} %get-tuple-element.59, f32[64]{0:T(128)S(1)} %get-tuple-element.58), channel_id=1, replica_groups=mesh['gx'=4,'gy'=4,'gz'=2] {'gz'}, use_global_device_ids=true, to_apply=%region_3.0 | all-reduce | flops 128 | bytes 1024 | tf_op jit(solution)/shard_map/psum | solution.py:371
  14.4 5.2 %pack.4 = bf16[4,768,1152]{2,1,0:T(8,128)(2,1)} custom-call(bf16[768,1536]{1,0:T(8,128)(2,1)S(1)} %copy-done.21, bf16[768,1536]{1,0:T(8,128)(2,1)S(1)} %copy-done.22, bf16[768,1536]{1,0:T(8,128)(2,1)} %refs_2_.1), custom_call_target="tpu_custom_call" | custom-call | bytes 221184 | tf_op jit(solution)/shard_map/pack/pallas_call | solution.py:148
  22.4 8.2 %cot_product.6 = bf16[256,1920]{1,0:T(8,128)(2,1)S(1)} custom-call(bf16[2,64,3072]{2,1,0:T(8,128)(2,1)S(1)} %pad_maximum_fusion.1.own_ref, bf16[2,64,3072]{2,1,0:T(8,128)(2,1)S(1)} %collective-permute-done.9.other_ref, bf16[384,3072]{1,0:T(8,128)(2,1)S(1)} %copy-done, bf16[1536,3072]{1,0:T(8,128)(2,1)} %refs_1_.11), custom_call_target="tpu_custom_call" | custom-call | flops 47185920 | bytes 199680 | tf_op jit(solution)/shard_map/cot_product/pallas_call | solution.py:214
  30.5 5.4 %all-to-all-start = ((bf16[4,768,1152]{2,1,0:T(8,128)(2,1)}), bf16[4,768,1152]{2,1,0:T(8,128)(2,1)}, u32[]{:S(2)}, u32[]{:S(2)}) async-start(bf16[4,768,1152]{2,1,0:T(8,128)(2,1)} %pack.4), calls=%async_computation | async-start | bytes 14155776 | tf_op jit(solution)/shard_map/all_to_all | solution.py:359
  37.9 18.3 %collective-permute-done.5.own_ref = bf16[2,64,3072]{2,1,0:T(8,128)(2,1)S(1)} collective-permute-done((bf16[2,64,3072]{2,1,0:T(8,128)(2,1)}, bf16[2,64,3072]{2,1,0:T(8,128)(2,1)S(1)}, u32[]{:S(2)}, u32[]{:S(2)}) %collective-permute-start.5) | collective-permute-done | bytes 786464 | tf_op jit(solution)/shard_map/ppermute | solution.py:121
  60.4 8.1 %cot_product.4 = bf16[256,1920]{1,0:T(8,128)(2,1)S(1)} custom-call(bf16[2,64,3072]{2,1,0:T(8,128)(2,1)S(1)} %collective-permute-done.5.own_ref, bf16[2,64,3072]{2,1,0:T(8,128)(2,1)S(1)} %collective-permute-done.6.other_ref, bf16[384,3072]{1,0:T(8,128)(2,1)S(1)} %copy-done, bf16[1536,3072]{1,0:T(8,128)(2,1)} %refs_1_.11), custom_call_target="tpu_custom_call" | custom-call | flops 47185920 | bytes 199680 | tf_op jit(solution)/shard_map/cot_product/pallas_call | solution.py:214
  70.7 23.5 %collective-permute-done.3.own_ref = bf16[2,64,3072]{2,1,0:T(8,128)(2,1)S(1)} collective-permute-done((bf16[2,64,3072]{2,1,0:T(8,128)(2,1)}, bf16[2,64,3072]{2,1,0:T(8,128)(2,1)S(1)}, u32[]{:S(2)}, u32[]{:S(2)}) %collective-permute-start.3) | collective-permute-done | bytes 786464 | tf_op jit(solution)/shard_map/ppermute | solution.py:121
  95.1 4.5 pack.6
  101.3 4.2 collective-permute-done.11.refs_2_
  107.5 8.5 %cot_product.7 = bf16[256,1920]{1,0:T(8,128)(2,1)S(1)} custom-call(bf16[2,64,3072]{2,1,0:T(8,128)(2,1)S(1)} %collective-permute-done.3.own_ref, bf16[2,64,3072]{2,1,0:T(8,128)(2,1)S(1)} %collective-permute-done.12.other_ref, bf16[384,3072]{1,0:T(8,128)(2,1)S(1)} %copy-done, bf16[1536,3072]{1,0:T(8,128)(2,1)} %refs_1_.11), custom_call_target="tpu_custom_call" | custom-call | flops 47185920 | bytes 199680 | tf_op jit(solution)/shard_map/cot_product/pallas_call | solution.py:214
  116.1 14.3 %collective-permute-done.4.own_ref = bf16[2,64,3072]{2,1,0:T(8,128)(2,1)S(1)} collective-permute-done((bf16[2,64,3072]{2,1,0:T(8,128)(2,1)S(1)}, bf16[2,64,3072]{2,1,0:T(8,128)(2,1)S(1)}, u32[]{:S(2)}, u32[]{:S(2)}) %collective-permute-start.4) | collective-permute-done | bytes 786464 | tf_op jit(solution)/shard_map/ppermute | solution.py:121
  132.2 4.6 all-to-all-start.1
  137.3 3.3 collective-permute-done.15.refs_4_
  143.1 14.3 %collective-permute-done.17.refs_6_ = bf16[2,64,3072]{2,1,0:T(8,128)(2,1)S(1)} collective-permute-done((bf16[2,64,3072]{2,1,0:T(8,128)(2,1)}, bf16[2,64,3072]{2,1,0:T(8,128)(2,1)S(1)}, u32[]{:S(2)}, u32[]{:S(2)}) %collective-permute-start.17) | collective-permute-done | bytes 786464 | tf_op jit(solution)/shard_map/ppermute | solution.py:121
  160.7 8.2 %cot_product.5 = bf16[256,1920]{1,0:T(8,128)(2,1)S(1)} custom-call(bf16[2,64,3072]{2,1,0:T(8,128)(2,1)S(1)} %copy-done.38, bf16[2,64,3072]{2,1,0:T(8,128)(2,1)S(1)} %collective-permute-done.8.other_ref, bf16[384,3072]{1,0:T(8,128)(2,1)S(1)} %copy-done, bf16[1536,3072]{1,0:T(8,128)(2,1)} %refs_1_.11), custom_call_target="tpu_custom_call" | custom-call | flops 47185920 | bytes 199680 | tf_op jit(solution)/shard_map/cot_product/pallas_call | solution.py:214
  171.8 5.0 %assemble.1.rows_ref = bf16[1024,3072]{1,0:T(8,128)(2,1)} custom-call(bf16[2,64,3072]{2,1,0:T(8,128)(2,1)} %pad_maximum_fusion.refs_0_, bf16[2,64,3072]{2,1,0:T(8,128)(2,1)S(1)} %collective-permute-done.1.refs_1_, bf16[2,64,3072]{2,1,0:T(8,128)(2,1)S(1)} %copy-done.36, bf16[2,64,3072]{2,1,0:T(8,128)(2,1)S(1)} %collective-permute-done.14.refs_3_, ...), custom_call_target="tpu_custom_call" | custom-call | bytes 196608 | tf_op jit(solution)/shard_map/assemble/pallas_call | solution.py:178
  176.8 4.5 all-to-all-start.2
  182.9 6.7 %pack.7 = bf16[4,768,768]{2,1,0:T(8,128)(2,1)S(1)} custom-call(bf16[768,6144]{1,0:T(8,128)(2,1)} %refs_0_.7), custom_call_target="tpu_custom_call" | custom-call | bytes 147456 | tf_op jit(solution)/shard_map/pack/pallas_call | solution.py:148
  191.8 13.7 %collective-permute-done.19 = bf16[256,1920]{1,0:T(8,128)(2,1)S(1)} collective-permute-done((bf16[256,1920]{1,0:T(8,128)(2,1)S(1)}, bf16[256,1920]{1,0:T(8,128)(2,1)S(1)}, u32[]{:S(2)}, u32[]{:S(2)}) %collective-permute-start.19) | collective-permute-done | bytes 983072 | tf_op jit(solution)/shard_map/ppermute | solution.py:121
  206.5 14.0 %in_product.5.q_own.k_own.v_own = bf16[1024,1152]{1,0:T(8,128)(2,1)S(1)} custom-call(bf16[1024,3072]{1,0:T(8,128)(2,1)} %assemble.1.rows_ref, bf16[3072,1152]{1,0:T(8,128)(2,1)} %bitcast.4.weight_ref.refs_5_), custom_call_target="tpu_custom_call" | custom-call | flops 113246208 | bytes 245760 | tf_op jit(solution)/shard_map/in_product/pallas_call | solution.py:268
  221.8 5.1 %all-to-all-start.3 = ((bf16[4,768,768]{2,1,0:T(8,128)(2,1)}), bf16[4,768,768]{2,1,0:T(8,128)(2,1)}, u32[]{:S(2)}, u32[]{:S(2)}) async-start(bf16[4,768,768]{2,1,0:T(8,128)(2,1)} %copy-done.6), calls=%async_computation.3 | async-start | bytes 9437184 | tf_op jit(solution)/shard_map/all_to_all | solution.py:359
  228.6 6.9 %in_product.6 = bf16[1024,512]{1,0:T(8,128)(2,1)S(1)} custom-call(bf16[1024,3072]{1,0:T(8,128)(2,1)} %assemble.1.rows_ref, bf16[3072,512]{1,0:T(8,128)(2,1)} %bitcast.5.weight_ref.refs_6_), custom_call_target="tpu_custom_call" | custom-call | flops 50331648 | bytes 163840 | tf_op jit(solution)/shard_map/in_product/pallas_call | solution.py:268
  236.1 6.1 %in_product.9 = bf16[1024,256]{1,0:T(8,128)(2,1)} custom-call(bf16[1024,3072]{1,0:T(8,128)(2,1)} %assemble.1.rows_ref, bf16[3072,256]{1,0:T(8,128)(2,1)} %bitcast.6.weight_ref.refs_7_), custom_call_target="tpu_custom_call" | custom-call | flops 25165824 | bytes 131072 | tf_op jit(solution)/shard_map/in_product/pallas_call | solution.py:268
  243.6 4.6 add_parts.1
  248.2 33.2 %collective-permute-done.20.q_got.k_got.v_got = bf16[1024,1152]{1,0:T(8,128)(2,1)S(1)} collective-permute-done((bf16[1024,1152]{1,0:T(8,128)(2,1)}, bf16[1024,1152]{1,0:T(8,128)(2,1)S(1)}, u32[]{:S(2)}, u32[]{:S(2)}) %collective-permute-start.20) | collective-permute-done | bytes 2359328 | tf_op jit(solution)/shard_map/ppermute | solution.py:121
  282.7 6.4 %in_product.7 = bf16[512,768]{1,0:T(8,128)(2,1)S(1)} custom-call(bf16[1024,3072]{1,0:T(8,128)(2,1)} %assemble.1.rows_ref, bf16[3072,768]{1,0:T(8,128)(2,1)} %bitcast.16.weight_ref.refs_1_), custom_call_target="tpu_custom_call" | custom-call | flops 37748736 | bytes 184320 | tf_op jit(solution)/shard_map/in_product/pallas_call | solution.py:268
  292.4 14.9 %attend.1 = (bf16[1024,384]{1,0:T(8,128)(2,1)S(1)}, bf16[1024,384]{1,0:T(8,128)(2,1)S(1)}, bf16[1024,384]{1,0:T(8,128)(2,1)S(1)}, bf16[1024,384]{1,0:T(8,128)(2,1)S(1)}) custom-call(bf16[1024,1152]{1,0:T(8,128)(2,1)S(1)} %copy-done.2, bf16[1024,1152]{1,0:T(8,128)(2,1)S(1)} %copy-done.5, bf16[1024,1152]{1,0:T(8,128)(2,1)S(1)} %copy-done.2, ...), custom_call_target="tpu_custom_call" | custom-call | flops 12582912 | bytes 98304 | tf_op jit(solution)/shard_map/attend/pallas_call | solution.py:75
  310.0 5.1 %collective-permute-done.22 = bf16[1024,256]{1,0:T(8,128)(2,1)} collective-permute-done((bf16[1024,256]{1,0:T(8,128)(2,1)}, bf16[1024,256]{1,0:T(8,128)(2,1)}, u32[]{:S(2)}, u32[]{:S(2)}) %collective-permute-start.22) | collective-permute-done | bytes 524320 | tf_op jit(solution)/shard_map/ppermute | solution.py:121
  317.0 6.3 %in_product.8 = bf16[512,768]{1,0:T(8,128)(2,1)S(1)} custom-call(bf16[1024,3072]{1,0:T(8,128)(2,1)} %assemble.1.rows_ref, bf16[3072,768]{1,0:T(8,128)(2,1)} %bitcast.16.weight_ref.refs_1_), custom_call_target="tpu_custom_call" | custom-call | flops 37748736 | bytes 184320 | tf_op jit(solution)/shard_map/in_product/pallas_call | solution.py:268
  327.5 18.5 %back_product.5.refs_2_ = bf16[1024,3072]{1,0:T(8,128)(2,1)} custom-call(bf16[1024,384]{1,0:T(8,128)(2,1)S(1)} %copy-done.30, bf16[1024,384]{1,0:T(8,128)(2,1)S(1)} %copy-done.32, bf16[1024,384]{1,0:T(8,128)(2,1)S(1)} %copy-done.34, bf16[1024,512]{1,0:T(8,128)(2,1)S(1)} %get-tuple-element.68.refs_3_, bf16[1024,256]{1,0:T(8,128)(2,1)S(1)} %get-tuple-element.76.refs_4_, ...), custom_call_target="tpu_custom_call" | custom-call | flops 188743680 | bytes 282624 | tf_op jit(solution)/shard_map/back_product/pallas_call | solution.py:321
  346.0 12.3 %out_product.6.refs_2_ = bf16[1024,3072]{1,0:T(8,128)(2,1)} custom-call(bf16[1024,384]{1,0:T(8,128)(2,1)S(1)} %copy-done.28, bf16[1024,512]{1,0:T(8,128)(2,1)S(1)} %get-tuple-element.69.refs_1_, bf16[1024,256]{1,0:T(8,128)(2,1)S(1)} %get-tuple-element.77.refs_2_, bf16[384,3072]{1,0:T(8,128)(2,1)S(1)} %copy-done, bf16[1536,3072]{1,0:T(8,128)(2,1)} %refs_1_.11), custom_call_target="tpu_custom_call" | custom-call | flops 113246208 | bytes 282624 | tf_op jit(solution)/shard_map/out_product/pallas_call | solution.py:321
  360.3 7.7 %out_product.7 = bf16[512,3072]{1,0:T(8,128)(2,1)} custom-call(bf16[512,768]{1,0:T(8,128)(2,1)S(1)} %get-tuple-element.75.refs_0_, bf16[1536,3072]{1,0:T(8,128)(2,1)} %refs_1_.11, bf16[1024,3072]{1,0:T(8,128)(2,1)} %out_product.6.refs_2_), custom_call_target="tpu_custom_call" | custom-call | flops 37748736 | bytes 196608 | tf_op jit(solution)/shard_map/out_product/pallas_call | solution.py:321
  368.1 6.9 %back_product.6 = bf16[512,3072]{1,0:T(8,128)(2,1)S(1)} custom-call(bf16[512,768]{1,0:T(8,128)(2,1)S(1)} %get-tuple-element.56.refs_0_, bf16[3072,768]{1,0:T(8,128)(2,1)} %bitcast.16.weight_ref.refs_1_, bf16[1024,3072]{1,0:T(8,128)(2,1)} %back_product.5.refs_2_), custom_call_target="tpu_custom_call" | custom-call | flops 37748736 | bytes 122880 | tf_op jit(solution)/shard_map/back_product/pallas_call | solution.py:321
  377.7 3.2 out_product.9
  382.7 3.2 out_product.11
  386.3 3.9 back_product.9
  390.9 3.3 back_product.8
  396.0 3.2 out_product.10
  399.2 3.2 out_product.8
  402.5 3.3 back_product.7
  408.8 9.5 %collective-permute-done.29 = bf16[256,1536]{1,0:T(8,128)(2,1)S(1)} collective-permute-done((bf16[256,1536]{1,0:T(8,128)(2,1)S(1)}, bf16[256,1536]{1,0:T(8,128)(2,1)S(1)}, u32[]{:S(2)}, u32[]{:S(2)}) %collective-permute-start.29) | collective-permute-done | bytes 786464 | tf_op jit(solution)/shard_map/ppermute | solution.py:121
  419.3 3.4 collective-permute-start.37
  422.8 11.4 %collective-permute-done.33 = bf16[256,1536]{1,0:T(8,128)(2,1)S(1)} collective-permute-done((bf16[256,1536]{1,0:T(8,128)(2,1)S(1)}, bf16[256,1536]{1,0:T(8,128)(2,1)S(1)}, u32[]{:S(2)}, u32[]{:S(2)}) %collective-permute-start.33) | collective-permute-done | bytes 786464 | tf_op jit(solution)/shard_map/ppermute | solution.py:121
  435.1 3.4 collective-permute-start.28
  440.7 12.4 %collective-permute-done.34 = bf16[2,64,1536]{2,1,0:T(8,128)(2,1)S(1)} collective-permute-done((bf16[2,64,1536]{2,1,0:T(8,128)(2,1)S(1)}, bf16[2,64,1536]{2,1,0:T(8,128)(2,1)S(1)}, u32[]{:S(2)}, u32[]{:S(2)}) %collective-permute-start.34) | collective-permute-done | bytes 393248 | tf_op jit(solution)/shard_map/ppermute | solution.py:121
  453.9 9.9 %collective-permute-done.35 = bf16[64,1536]{1,0:T(8,128)(2,1)S(1)} collective-permute-done((bf16[64,1536]{1,0:T(8,128)(2,1)S(1)}, bf16[64,1536]{1,0:T(8,128)(2,1)S(1)}, u32[]{:S(2)}, u32[]{:S(2)}) %collective-permute-start.35) | collective-permute-done | bytes 196640 | tf_op jit(solution)/shard_map/ppermute | solution.py:121
  464.8 5.6 %all-reduce = (f32[64]{0:T(128)S(1)}, f32[64]{0:T(128)}) all-reduce(f32[64]{0:T(128)S(1)} %fusion.28, f32[64]{0:T(128)} %reduce_sum.48), channel_id=1, replica_groups=mesh['gx'=4,'gy'=4,'gz'=2] {'gz'}, use_global_device_ids=true, to_apply=%region_8.9 | all-reduce | flops 128 | bytes 1024 | tf_op jit(solution)/shard_map/psum | solution.py:489
  (195 shorter events, 77.4 us)
Async XLA Ops:
  0.6 19.0 %collective-permute-start.2 = (bf16[64,3072]{1,0:T(8,128)(2,1)}, bf16[64,3072]{1,0:T(8,128)(2,1)S(1)}, u32[]{:S(2)}, u32[]{:S(2)}) collective-permute-start(bf16[64,3072]{1,0:T(8,128)(2,1)} %param.9), channel_id=1, source_target_pairs={{0,16},{8,24},{16,0},{24,8},{1,17},{9,25},{17,1},{25,9},{2,18},{10... | collective-permute-start | bytes 1179656 | tf_op jit(solution)/shard_map/ppermute | solution.py:121
  10.9 10.4 %collective-permute-start = (bf16[64,3072]{1,0:T(8,128)(2,1)S(1)}, bf16[64,3072]{1,0:T(8,128)(2,1)S(1)}, u32[]{:S(2)}, u32[]{:S(2)}) collective-permute-start(bf16[64,3072]{1,0:T(8,128)(2,1)S(1)} %fusion.27), channel_id=1, source_target_pairs={{0,16},{8,24},{16,0},{24,8},{1,17},{9,25},{17,1},{25,9},{2,18},{10... | collective-permute-start | bytes 1179656 | tf_op jit(solution)/shard_map/ppermute | solution.py:121
  19.7 2.7 collective-permute-start.9
  30.5 28.4 %copy-start.9 = (bf16[256,1920]{1,0:T(8,128)(2,1)}, bf16[256,1920]{1,0:T(8,128)(2,1)S(1)}, u32[]{:S(2)}) copy-start(bf16[256,1920]{1,0:T(8,128)(2,1)S(1)} %cot_product.6) | copy-start | bytes 2949124
  30.5 101.7 %all-to-all-start = ((bf16[4,768,1152]{2,1,0:T(8,128)(2,1)}), bf16[4,768,1152]{2,1,0:T(8,128)(2,1)}, u32[]{:S(2)}, u32[]{:S(2)}) async-start(bf16[4,768,1152]{2,1,0:T(8,128)(2,1)} %pack.4), calls=%async_computation | async-start | bytes 14155776 | tf_op jit(solution)/shard_map/all_to_all | solution.py:359
  35.9 20.2 %collective-permute-start.5 = (bf16[2,64,3072]{2,1,0:T(8,128)(2,1)}, bf16[2,64,3072]{2,1,0:T(8,128)(2,1)S(1)}, u32[]{:S(2)}, u32[]{:S(2)}) collective-permute-start(bf16[2,64,3072]{2,1,0:T(8,128)(2,1)} %copy-done.18), channel_id=1, source_target_pairs={{0,2},{2,0},{4,6},{6,4},{1,3},{3,1},{5,7},{7,5},{8,10},{10,8},{12,... | collective-permute-start | bytes 2359304 | tf_op jit(solution)/shard_map/ppermute | solution.py:121
  56.1 4.3 collective-permute-start.6
  56.1 38.1 %collective-permute-start.3 = (bf16[2,64,3072]{2,1,0:T(8,128)(2,1)}, bf16[2,64,3072]{2,1,0:T(8,128)(2,1)S(1)}, u32[]{:S(2)}, u32[]{:S(2)}) collective-permute-start(bf16[2,64,3072]{2,1,0:T(8,128)(2,1)} %copy-done.18), channel_id=1, source_target_pairs={{0,4},{2,6},{4,0},{6,2},{1,5},{3,7},{5,1},{7,3},{8,12},{10,14},{12... | collective-permute-start | bytes 2359304 | tf_op jit(solution)/shard_map/ppermute | solution.py:121
  58.9 48.6 %collective-permute-start.10 = (bf16[256,1920]{1,0:T(8,128)(2,1)S(1)}, bf16[256,1920]{1,0:T(8,128)(2,1)S(1)}, u32[]{:S(2)}, u32[]{:S(2)}) collective-permute-start(bf16[256,1920]{1,0:T(8,128)(2,1)S(1)} %cot_product.6), channel_id=1, source_target_pairs={{0,1},{1,0},{2,3},{3,2},{4,5},{5,4},{6,7},{7,6},{8,9},{9,8},{10,11... | collective-permute-start | bytes 2949128 | tf_op jit(solution)/shard_map/ppermute | solution.py:121
  68.6 31.0 %copy-start.11 = (bf16[256,1920]{1,0:T(8,128)(2,1)}, bf16[256,1920]{1,0:T(8,128)(2,1)S(1)}, u32[]{:S(2)}) copy-start(bf16[256,1920]{1,0:T(8,128)(2,1)S(1)} %cot_product.4) | copy-start | bytes 2949124
  68.6 62.7 %collective-permute-start.7 = (bf16[256,1920]{1,0:T(8,128)(2,1)S(1)}, bf16[256,1920]{1,0:T(8,128)(2,1)S(1)}, u32[]{:S(2)}, u32[]{:S(2)}) collective-permute-start(bf16[256,1920]{1,0:T(8,128)(2,1)S(1)} %cot_product.4), channel_id=1, source_target_pairs={{0,1},{1,0},{2,3},{3,2},{4,5},{5,4},{6,7},{7,6},{8,9},{9,8},{10,11... | collective-permute-start | bytes 2949128 | tf_op jit(solution)/shard_map/ppermute | solution.py:121
  69.2 36.3 %collective-permute-start.11 = (bf16[2,64,3072]{2,1,0:T(8,128)(2,1)}, bf16[2,64,3072]{2,1,0:T(8,128)(2,1)S(1)}, u32[]{:S(2)}, u32[]{:S(2)}) collective-permute-start(bf16[2,64,3072]{2,1,0:T(8,128)(2,1)} %pad_maximum_fusion.refs_0_), channel_id=1, source_target_pairs={{0,2},{2,0},{4,6},{6,4},{1,3},{3,1},{5,7},{7,5},{8,10},{10,8},{12,... | collective-permute-start | bytes 2359304 | tf_op jit(solution)/shard_map/ppermute | solution.py:121
  94.3 13.2 %collective-permute-start.12 = (bf16[2,64,3072]{2,1,0:T(8,128)(2,1)S(1)}, bf16[2,64,3072]{2,1,0:T(8,128)(2,1)S(1)}, u32[]{:S(2)}, u32[]{:S(2)}) collective-permute-start(bf16[2,64,3072]{2,1,0:T(8,128)(2,1)S(1)} %collective-permute-done.3.own_ref), channel_id=1, source_target_pairs={{0,8},{8,0},{16,24},{24,16},{1,9},{9,1},{17,25},{25,17},{2,10},{10... | collective-permute-start | bytes 2359304 | tf_op jit(solution)/shard_map/ppermute | solution.py:121
  94.3 36.1 %collective-permute-start.4 = (bf16[2,64,3072]{2,1,0:T(8,128)(2,1)S(1)}, bf16[2,64,3072]{2,1,0:T(8,128)(2,1)S(1)}, u32[]{:S(2)}, u32[]{:S(2)}) collective-permute-start(bf16[2,64,3072]{2,1,0:T(8,128)(2,1)S(1)} %collective-permute-done.3.own_ref), channel_id=1, source_target_pairs={{0,2},{2,0},{4,6},{6,4},{1,3},{3,1},{5,7},{7,5},{8,10},{10,8},{12,... | collective-permute-start | bytes 2359304 | tf_op jit(solution)/shard_map/ppermute | solution.py:121
  105.5 35.1 %collective-permute-start.15 = (bf16[2,64,3072]{2,1,0:T(8,128)(2,1)}, bf16[2,64,3072]{2,1,0:T(8,128)(2,1)}, u32[]{:S(2)}, u32[]{:S(2)}) collective-permute-start(bf16[2,64,3072]{2,1,0:T(8,128)(2,1)} %pad_maximum_fusion.refs_0_), channel_id=1, source_target_pairs={{0,4},{2,6},{4,0},{6,2},{1,5},{3,7},{5,1},{7,3},{8,12},{10,14},{12... | collective-permute-start | bytes 2359304 | tf_op jit(solution)/shard_map/ppermute | solution.py:121
  116.1 26.0 %copy-start.13 = (bf16[256,1920]{1,0:T(8,128)(2,1)}, bf16[256,1920]{1,0:T(8,128)(2,1)S(1)}, u32[]{:S(2)}) copy-start(bf16[256,1920]{1,0:T(8,128)(2,1)S(1)} %cot_product.7) | copy-start | bytes 2949124
  132.2 44.5 %all-to-all-start.1 = ((bf16[4,768,512]{2,1,0:T(8,128)(2,1)}), bf16[4,768,512]{2,1,0:T(8,128)(2,1)}, u32[]{:S(2)}, u32[]{:S(2)}) async-start(bf16[4,768,512]{2,1,0:T(8,128)(2,1)} %copy-done.7), calls=%async_computation.1 | async-start | bytes 6291456 | tf_op jit(solution)/shard_map/all_to_all | solution.py:359
  136.8 23.9 %copy-start.38 = (bf16[2,64,3072]{2,1,0:T(8,128)(2,1)S(1)}, bf16[2,64,3072]{2,1,0:T(8,128)(2,1)}, u32[]{:S(2)}) copy-start(bf16[2,64,3072]{2,1,0:T(8,128)(2,1)} %copy-done.37) | copy-start | bytes 2359300
  136.8 6.2 %collective-permute-start.8 = (bf16[2,64,3072]{2,1,0:T(8,128)(2,1)}, bf16[2,64,3072]{2,1,0:T(8,128)(2,1)S(1)}, u32[]{:S(2)}, u32[]{:S(2)}) collective-permute-start(bf16[2,64,3072]{2,1,0:T(8,128)(2,1)} %copy-done.37), channel_id=1, source_target_pairs={{0,8},{8,0},{16,24},{24,16},{1,9},{9,1},{17,25},{25,17},{2,10},{10... | collective-permute-start | bytes 2359304 | tf_op jit(solution)/shard_map/ppermute | solution.py:121
  140.6 16.7 %collective-permute-start.17 = (bf16[2,64,3072]{2,1,0:T(8,128)(2,1)}, bf16[2,64,3072]{2,1,0:T(8,128)(2,1)S(1)}, u32[]{:S(2)}, u32[]{:S(2)}) collective-permute-start(bf16[2,64,3072]{2,1,0:T(8,128)(2,1)} %collective-permute-done.15.refs_4_), channel_id=1, source_target_pairs={{0,2},{2,0},{4,6},{6,4},{1,3},{3,1},{5,7},{7,5},{8,10},{10,8},{12,... | collective-permute-start | bytes 2359304 | tf_op jit(solution)/shard_map/ppermute | solution.py:121
  142.1 27.9 %collective-permute-start.13 = (bf16[256,1920]{1,0:T(8,128)(2,1)S(1)}, bf16[256,1920]{1,0:T(8,128)(2,1)S(1)}, u32[]{:S(2)}, u32[]{:S(2)}) collective-permute-start(bf16[256,1920]{1,0:T(8,128)(2,1)S(1)} %cot_product.7), channel_id=1, source_target_pairs={{0,1},{1,0},{2,3},{3,2},{4,5},{5,4},{6,7},{7,6},{8,9},{9,8},{10,11... | collective-permute-start | bytes 2949128 | tf_op jit(solution)/shard_map/ppermute | solution.py:121
  142.6 27.3 %collective-permute-start.1 = (bf16[2,64,3072]{2,1,0:T(8,128)(2,1)}, bf16[2,64,3072]{2,1,0:T(8,128)(2,1)S(1)}, u32[]{:S(2)}, u32[]{:S(2)}) collective-permute-start(bf16[2,64,3072]{2,1,0:T(8,128)(2,1)} %pad_maximum_fusion.refs_0_), channel_id=1, source_target_pairs={{0,8},{8,0},{16,24},{24,16},{1,9},{9,1},{17,25},{25,17},{2,10},{10... | collective-permute-start | bytes 2359304 | tf_op jit(solution)/shard_map/ppermute | solution.py:121
  142.6 27.3 %collective-permute-start.16 = (bf16[2,64,3072]{2,1,0:T(8,128)(2,1)}, bf16[2,64,3072]{2,1,0:T(8,128)(2,1)S(1)}, u32[]{:S(2)}, u32[]{:S(2)}) collective-permute-start(bf16[2,64,3072]{2,1,0:T(8,128)(2,1)} %collective-permute-done.15.refs_4_), channel_id=1, source_target_pairs={{0,8},{8,0},{16,24},{24,16},{1,9},{9,1},{17,25},{25,17},{2,10},{10... | collective-permute-start | bytes 2359304 | tf_op jit(solution)/shard_map/ppermute | solution.py:121
  143.1 26.8 %collective-permute-start.14 = (bf16[2,64,3072]{2,1,0:T(8,128)(2,1)}, bf16[2,64,3072]{2,1,0:T(8,128)(2,1)S(1)}, u32[]{:S(2)}, u32[]{:S(2)}) collective-permute-start(bf16[2,64,3072]{2,1,0:T(8,128)(2,1)} %copy-done.35), channel_id=1, source_target_pairs={{0,8},{8,0},{16,24},{24,16},{1,9},{9,1},{17,25},{25,17},{2,10},{10... | collective-permute-start | bytes 2359304 | tf_op jit(solution)/shard_map/ppermute | solution.py:121
  157.4 12.6 %collective-permute-start.18 = (bf16[2,64,3072]{2,1,0:T(8,128)(2,1)S(1)}, bf16[2,64,3072]{2,1,0:T(8,128)(2,1)S(1)}, u32[]{:S(2)}, u32[]{:S(2)}) collective-permute-start(bf16[2,64,3072]{2,1,0:T(8,128)(2,1)S(1)} %collective-permute-done.17.refs_6_), channel_id=1, source_target_pairs={{0,8},{8,0},{16,24},{24,16},{1,9},{9,1},{17,25},{25,17},{2,10},{10... | collective-permute-start | bytes 2359304 | tf_op jit(solution)/shard_map/ppermute | solution.py:121
  176.8 45.1 %all-to-all-start.2 = ((bf16[4,768,256]{2,1,0:T(8,128)(2,1)}), bf16[4,768,256]{2,1,0:T(8,128)(2,1)}, u32[]{:S(2)}, u32[]{:S(2)}) async-start(bf16[4,768,256]{2,1,0:T(8,128)(2,1)} %copy-done.8), calls=%async_computation.2 | async-start | bytes 3145728 | tf_op jit(solution)/shard_map/all_to_all | solution.py:359
  181.3 24.2 %collective-permute-start.19 = (bf16[256,1920]{1,0:T(8,128)(2,1)S(1)}, bf16[256,1920]{1,0:T(8,128)(2,1)S(1)}, u32[]{:S(2)}, u32[]{:S(2)}) collective-permute-start(bf16[256,1920]{1,0:T(8,128)(2,1)S(1)} %copy-done.16), channel_id=1, source_target_pairs={{0,1},{1,0},{2,3},{3,2},{4,5},{5,4},{6,7},{7,6},{8,9},{9,8},{10,11... | collective-permute-start | bytes 2949128 | tf_op jit(solution)/shard_map/ppermute | solution.py:121
  221.8 60.9 %all-to-all-start.3 = ((bf16[4,768,768]{2,1,0:T(8,128)(2,1)}), bf16[4,768,768]{2,1,0:T(8,128)(2,1)}, u32[]{:S(2)}, u32[]{:S(2)}) async-start(bf16[4,768,768]{2,1,0:T(8,128)(2,1)} %copy-done.6), calls=%async_computation.3 | async-start | bytes 9437184 | tf_op jit(solution)/shard_map/all_to_all | solution.py:359
  227.0 54.4 %collective-permute-start.20 = (bf16[1024,1152]{1,0:T(8,128)(2,1)}, bf16[1024,1152]{1,0:T(8,128)(2,1)S(1)}, u32[]{:S(2)}, u32[]{:S(2)}) collective-permute-start(bf16[1024,1152]{1,0:T(8,128)(2,1)} %copy-done.1), channel_id=1, source_target_pairs={{0,1},{1,0},{2,3},{3,2},{4,5},{5,4},{6,7},{7,6},{8,9},{9,8},{10,11... | collective-permute-start | bytes 7077896 | tf_op jit(solution)/shard_map/ppermute | solution.py:121
  235.6 89.3 %collective-permute-start.21 = (bf16[1024,512]{1,0:T(8,128)(2,1)S(1)}, bf16[1024,512]{1,0:T(8,128)(2,1)}, u32[]{:S(2)}, u32[]{:S(2)}) collective-permute-start(bf16[1024,512]{1,0:T(8,128)(2,1)S(1)} %in_product.6), channel_id=1, source_target_pairs={{0,1},{1,0},{2,3},{3,2},{4,5},{5,4},{6,7},{7,6},{8,9},{9,8},{10,11... | collective-permute-start | bytes 3145736 | tf_op jit(solution)/shard_map/ppermute | solution.py:121
  242.2 72.9 %collective-permute-start.22 = (bf16[1024,256]{1,0:T(8,128)(2,1)}, bf16[1024,256]{1,0:T(8,128)(2,1)}, u32[]{:S(2)}, u32[]{:S(2)}) collective-permute-start(bf16[1024,256]{1,0:T(8,128)(2,1)} %in_product.9), channel_id=1, source_target_pairs={{0,1},{1,0},{2,3},{3,2},{4,5},{5,4},{6,7},{7,6},{8,9},{9,8},{10,11... | collective-permute-start | bytes 1572872 | tf_op jit(solution)/shard_map/ppermute | solution.py:121
  289.1 69.1 %collective-permute-start.23 = (bf16[512,768]{1,0:T(8,128)(2,1)S(1)}, bf16[512,768]{1,0:T(8,128)(2,1)}, u32[]{:S(2)}, u32[]{:S(2)}) collective-permute-start(bf16[512,768]{1,0:T(8,128)(2,1)S(1)} %in_product.7), channel_id=1, source_target_pairs={{0,1},{1,0},{2,3},{3,2},{4,5},{5,4},{6,7},{7,6},{8,9},{9,8},{10,11... | collective-permute-start | bytes 2359304 | tf_op jit(solution)/shard_map/ppermute | solution.py:121
  323.3 44.8 %collective-permute-start.24 = (bf16[512,768]{1,0:T(8,128)(2,1)S(1)}, bf16[512,768]{1,0:T(8,128)(2,1)}, u32[]{:S(2)}, u32[]{:S(2)}) collective-permute-start(bf16[512,768]{1,0:T(8,128)(2,1)S(1)} %in_product.8), channel_id=1, source_target_pairs={{0,1},{1,0},{2,3},{3,2},{4,5},{5,4},{6,7},{7,6},{8,9},{9,8},{10,11... | collective-permute-start | bytes 2359304 | tf_op jit(solution)/shard_map/ppermute | solution.py:121
  327.4 18.5 %copy-start.28 = (bf16[1024,384]{1,0:T(8,128)(2,1)S(1)}, bf16[1024,384]{1,0:T(8,128)(2,1)}, u32[]{:S(2)}) copy-start(bf16[1024,384]{1,0:T(8,128)(2,1)} %copy-done.27) | copy-start | bytes 2359300
  368.1 9.6 %collective-permute-start.25 = (bf16[512,3072]{1,0:T(8,128)(2,1)}, bf16[512,3072]{1,0:T(8,128)(2,1)S(1)}, u32[]{:S(2)}, u32[]{:S(2)}) collective-permute-start(bf16[512,3072]{1,0:T(8,128)(2,1)} %out_product.7), channel_id=1, source_target_pairs={{0,8},{8,0},{16,24},{24,16},{1,9},{9,1},{17,25},{25,17},{2,10},{10... | collective-permute-start | bytes 9437192 | tf_op jit(solution)/shard_map/ppermute | solution.py:121
  375.0 11.3 %collective-permute-start.32 = (bf16[512,3072]{1,0:T(8,128)(2,1)S(1)}, bf16[512,3072]{1,0:T(8,128)(2,1)S(1)}, u32[]{:S(2)}, u32[]{:S(2)}) collective-permute-start(bf16[512,3072]{1,0:T(8,128)(2,1)S(1)} %back_product.6), channel_id=1, source_target_pairs={{0,8},{8,0},{16,24},{24,16},{1,9},{9,1},{17,25},{25,17},{2,10},{10... | collective-permute-start | bytes 9437192 | tf_op jit(solution)/shard_map/ppermute | solution.py:121
  380.9 24.8 %collective-permute-start.26 = (bf16[256,1536]{1,0:T(8,128)(2,1)S(1)}, bf16[256,1536]{1,0:T(8,128)(2,1)}, u32[]{:S(2)}, u32[]{:S(2)}) collective-permute-start(bf16[256,1536]{1,0:T(8,128)(2,1)S(1)} %out_product.9), channel_id=1, source_target_pairs={{0,16},{8,24},{16,0},{24,8},{1,17},{9,25},{17,1},{25,9},{2,18},{10... | collective-permute-start | bytes 2359304 | tf_op jit(solution)/shard_map/ppermute | solution.py:121
  385.9 32.3 %collective-permute-start.29 = (bf16[256,1536]{1,0:T(8,128)(2,1)S(1)}, bf16[256,1536]{1,0:T(8,128)(2,1)S(1)}, u32[]{:S(2)}, u32[]{:S(2)}) collective-permute-start(bf16[256,1536]{1,0:T(8,128)(2,1)S(1)} %out_product.11), channel_id=1, source_target_pairs={{0,16},{8,24},{16,0},{24,8},{1,17},{9,25},{17,1},{25,9},{2,18},{10... | collective-permute-start | bytes 2359304 | tf_op jit(solution)/shard_map/ppermute | solution.py:121
  390.4 28.7 %collective-permute-start.36 = (bf16[2,2,64,1536]{3,2,0,1:T(8,128)(2,1)S(1)}, bf16[2,2,64,1536]{3,2,0,1:T(8,128)(2,1)S(1)}, u32[]{:S(2)}, u32[]{:S(2)}) collective-permute-start(bf16[2,2,64,1536]{3,2,0,1:T(8,128)(2,1)S(1)} %bitcast.101), channel_id=1, source_target_pairs={{0,2},{2,0},{4,6},{6,4},{1,3},{3,1},{5,7},{7,5},{8,10},{10,8},{12,... | collective-permute-start | bytes 2359304 | tf_op jit(solution)/shard_map/ppermute | solution.py:121
  394.2 39.9 %collective-permute-start.33 = (bf16[256,1536]{1,0:T(8,128)(2,1)S(1)}, bf16[256,1536]{1,0:T(8,128)(2,1)S(1)}, u32[]{:S(2)}, u32[]{:S(2)}) collective-permute-start(bf16[256,1536]{1,0:T(8,128)(2,1)S(1)} %back_product.8), channel_id=1, source_target_pairs={{0,16},{8,24},{16,0},{24,8},{1,17},{9,25},{17,1},{25,9},{2,18},{10... | collective-permute-start | bytes 2359304 | tf_op jit(solution)/shard_map/ppermute | solution.py:121
  407.2 27.8 %collective-permute-start.27 = (bf16[2,64,1536]{2,1,0:T(8,128)(2,1)S(1)}, bf16[2,64,1536]{2,1,0:T(8,128)(2,1)S(1)}, u32[]{:S(2)}, u32[]{:S(2)}) collective-permute-start(bf16[2,64,1536]{2,1,0:T(8,128)(2,1)S(1)} %fusion.40), channel_id=1, source_target_pairs={{0,2},{2,0},{4,6},{6,4},{1,3},{3,1},{5,7},{7,5},{8,10},{10,8},{12,... | collective-permute-start | bytes 1179656 | tf_op jit(solution)/shard_map/ppermute | solution.py:121
  418.5 20.0 %collective-permute-start.30 = (bf16[2,64,1536]{2,1,0:T(8,128)(2,1)S(1)}, bf16[2,64,1536]{2,1,0:T(8,128)(2,1)S(1)}, u32[]{:S(2)}, u32[]{:S(2)}) collective-permute-start(bf16[2,64,1536]{2,1,0:T(8,128)(2,1)S(1)} %fusion.41), channel_id=1, source_target_pairs={{0,2},{2,0},{4,6},{6,4},{1,3},{3,1},{5,7},{7,5},{8,10},{10,8},{12,... | collective-permute-start | bytes 1179656 | tf_op jit(solution)/shard_map/ppermute | solution.py:121
  419.3 19.4 %collective-permute-start.37 = (bf16[2,64,1536]{2,1,0:T(8,128)(2,1)S(1)}, bf16[2,64,1536]{2,1,0:T(8,128)(2,1)S(1)}, u32[]{:S(2)}, u32[]{:S(2)}) collective-permute-start(bf16[2,64,1536]{2,1,0:T(8,128)(2,1)S(1)} %fusion.39), channel_id=1, source_target_pairs={{0,4},{2,6},{4,0},{6,2},{1,5},{3,7},{5,1},{7,3},{8,12},{10,14},{12... | collective-permute-start | bytes 1179656 | tf_op jit(solution)/shard_map/ppermute | solution.py:121
  434.4 18.7 %collective-permute-start.34 = (bf16[2,64,1536]{2,1,0:T(8,128)(2,1)S(1)}, bf16[2,64,1536]{2,1,0:T(8,128)(2,1)S(1)}, u32[]{:S(2)}, u32[]{:S(2)}) collective-permute-start(bf16[2,64,1536]{2,1,0:T(8,128)(2,1)S(1)} %fusion.42), channel_id=1, source_target_pairs={{0,2},{2,0},{4,6},{6,4},{1,3},{3,1},{5,7},{7,5},{8,10},{10,8},{12,... | collective-permute-start | bytes 1179656 | tf_op jit(solution)/shard_map/ppermute | solution.py:121
  435.1 35.3 %collective-permute-start.28 = (bf16[64,1536]{1,0:T(8,128)(2,1)S(1)}, bf16[64,1536]{1,0:T(8,128)(2,1)}, u32[]{:S(2)}, u32[]{:S(2)}) collective-permute-start(bf16[64,1536]{1,0:T(8,128)(2,1)S(1)} %fusion.47), channel_id=1, source_target_pairs={{0,4},{2,6},{4,0},{6,2},{1,5},{3,7},{5,1},{7,3},{8,12},{10,14},{12... | collective-permute-start | bytes 589832 | tf_op jit(solution)/shard_map/ppermute | solution.py:121
  438.6 33.4 %collective-permute-start.31 = (bf16[64,1536]{1,0:T(8,128)(2,1)S(1)}, bf16[64,1536]{1,0:T(8,128)(2,1)}, u32[]{:S(2)}, u32[]{:S(2)}) collective-permute-start(bf16[64,1536]{1,0:T(8,128)(2,1)S(1)} %fusion.48), channel_id=1, source_target_pairs={{0,4},{2,6},{4,0},{6,2},{1,5},{3,7},{5,1},{7,3},{8,12},{10,14},{12... | collective-permute-start | bytes 589832 | tf_op jit(solution)/shard_map/ppermute | solution.py:121
  438.9 14.9 %collective-permute-start.38 = (bf16[64,1536]{1,0:T(8,128)(2,1)S(1)}, bf16[64,1536]{1,0:T(8,128)(2,1)S(1)}, u32[]{:S(2)}, u32[]{:S(2)}) collective-permute-start(bf16[64,1536]{1,0:T(8,128)(2,1)S(1)} %fusion.50), channel_id=1, source_target_pairs={{0,16},{8,24},{16,0},{24,8},{1,17},{9,25},{17,1},{25,9},{2,18},{10... | collective-permute-start | bytes 589832 | tf_op jit(solution)/shard_map/ppermute | solution.py:121
  453.2 10.6 %collective-permute-start.35 = (bf16[64,1536]{1,0:T(8,128)(2,1)S(1)}, bf16[64,1536]{1,0:T(8,128)(2,1)S(1)}, u32[]{:S(2)}, u32[]{:S(2)}) collective-permute-start(bf16[64,1536]{1,0:T(8,128)(2,1)S(1)} %fusion.49), channel_id=1, source_target_pairs={{0,4},{2,6},{4,0},{6,2},{1,5},{3,7},{5,1},{7,3},{8,12},{10,14},{12... | collective-permute-start | bytes 589832 | tf_op jit(solution)/shard_map/ppermute | solution.py:121
  (41 other events, 187.0 us)

commit v15 on v14

--- a/solution.py
+++ b/solution.py
@@ -395,7 +395,7 @@
     early = (cot_owns[2], cot_gots[1], cot_parts[3])
     in_mlp = [swap(after(packed_mlp[0], in_heads, *early))]
     in_mlp.append(swap(after(packed_mlp[1], in_mlp[0], all_in)))
-    heads_own = in_product(after(all_in, cot_gots[3]), in_heads)
+    heads_own = in_product(after(all_in, cot_owns[3]), in_heads)
     heads_got = others(heads_own)
     mlp_own = [in_product(after(all_in, heads_own, in_mlp[1]), in_mlp[0])]
     mlp_got = [others(mlp_own[0])]

time: 477 us -> 483 us (1.013)
  waiting for transfers between devices: 174 us -> 179 us
    ppermute x39, waiting for transfers between devices: 174 us -> 179 us  [trade(): return lax.ppermute(block, axis, pairs)]
    unnamed x93 -> x87, local copies, waits for them, and re-layouts: 21.9 us -> 20.9 us
  transfers between devices with their start and end apart: 43 -> 43, of which waited for: 14 -> 13; matrix products, arithmetic and copies ran while one was open for 4% -> 4% of each run, Pallas kernels for 37% -> 37%
where the time goes in v15:
time: 483 us; the launch traced here: 480 us
  Pallas kernels  185 us (38%)
  waiting for transfers between devices  179 us (37%)
  starting transfers between devices  63.1 us (13%)
  local copies, waits for them, and re-layouts  21.3 us (4%)
  other arithmetic  19.6 us (4%)
  blocking collectives  10.5 us (2%)
    ppermute x39, waiting for transfers between devices, trade(): return lax.ppermute(block, axis, pairs)  179 us
    pallas_call x11, Pallas kernels, product(): pl.pallas_call(kernel, grid=(columns // tile,), in_specs=specs, out_specs...  68.7 us
    ppermute x39, starting transfers between devices, trade(): return lax.ppermute(block, axis, pairs)  43.6 us
    pallas_call x5, Pallas kernels, in_product(): pl.pallas_call(in_kernel, grid=(columns // tile,), in_specs=[pl.BlockSpec...  39.4 us
    pallas_call x4, Pallas kernels, cot_product(): pl.pallas_call(cot_kernel, grid=(columns // tile,), in_specs=[whole, whol...  33.8 us
    unnamed x87, local copies, waits for them, and re-layouts  20.9 us
    all_to_all x4, starting transfers between devices, swap(): lax.all_to_all(packed, 'gx', split_axis=0, concat_axis=0, tiled=True)  19.5 us
    pallas_call x4, Pallas kernels, pack(): pl.pallas_call(pack_kernel, grid=(owners, width // tile), in_specs=[spec]...  18.6 us
  transfers between devices with their start and end apart: 43, of which 13 were waited for; matrix products, arithmetic and copies ran while one was open for 4% of the time, Pallas kernels for 37%

profile of v15, /device:TPU:0, one launch (start us, length us, event | category | flops | bytes accessed | tf_op | source)
XLA Modules:
  0.0 480.0 jit_solution(10261338197072648392)
XLA Ops:
  0.6 3.0 collective-permute-start.2
  4.8 4.9 %all-reduce.1 = (f32[64]{0:T(128)S(1)}, f32[64]{0:T(128)S(1)}) all-reduce(f32[64]{0:T(128)S(1)} %get-tuple-element.59, f32[64]{0:T(128)S(1)} %get-tuple-element.58), channel_id=1, replica_groups=mesh['gx'=4,'gy'=4,'gz'=2] {'gz'}, use_global_device_ids=true, to_apply=%region_3.0 | all-reduce | flops 128 | bytes 1024 | tf_op jit(solution)/shard_map/psum | solution.py:371
  14.4 5.2 %pack.4 = bf16[4,768,1152]{2,1,0:T(8,128)(2,1)} custom-call(bf16[768,1536]{1,0:T(8,128)(2,1)S(1)} %copy-done.18, bf16[768,1536]{1,0:T(8,128)(2,1)S(1)} %copy-done.19, bf16[768,1536]{1,0:T(8,128)(2,1)} %refs_2_.1), custom_call_target="tpu_custom_call" | custom-call | bytes 221184 | tf_op jit(solution)/shard_map/pack/pallas_call | solution.py:148
  22.4 8.2 %cot_product.6 = bf16[256,1920]{1,0:T(8,128)(2,1)S(1)} custom-call(bf16[2,64,3072]{2,1,0:T(8,128)(2,1)S(1)} %pad_maximum_fusion.1.own_ref, bf16[2,64,3072]{2,1,0:T(8,128)(2,1)S(1)} %collective-permute-done.9.other_ref, bf16[384,3072]{1,0:T(8,128)(2,1)S(1)} %copy-done, bf16[1536,3072]{1,0:T(8,128)(2,1)} %refs_1_.11), custom_call_target="tpu_custom_call" | custom-call | flops 47185920 | bytes 199680 | tf_op jit(solution)/shard_map/cot_product/pallas_call | solution.py:214
  30.5 5.4 %all-to-all-start = ((bf16[4,768,1152]{2,1,0:T(8,128)(2,1)}), bf16[4,768,1152]{2,1,0:T(8,128)(2,1)}, u32[]{:S(2)}, u32[]{:S(2)}) async-start(bf16[4,768,1152]{2,1,0:T(8,128)(2,1)} %pack.4), calls=%async_computation | async-start | bytes 14155776 | tf_op jit(solution)/shard_map/all_to_all | solution.py:359
  37.9 18.3 %collective-permute-done.5.own_ref = bf16[2,64,3072]{2,1,0:T(8,128)(2,1)S(1)} collective-permute-done((bf16[2,64,3072]{2,1,0:T(8,128)(2,1)}, bf16[2,64,3072]{2,1,0:T(8,128)(2,1)S(1)}, u32[]{:S(2)}, u32[]{:S(2)}) %collective-permute-start.5) | collective-permute-done | bytes 786464 | tf_op jit(solution)/shard_map/ppermute | solution.py:121
  56.1 2.8 collective-permute-start.3
  60.4 8.1 %cot_product.4 = bf16[256,1920]{1,0:T(8,128)(2,1)S(1)} custom-call(bf16[2,64,3072]{2,1,0:T(8,128)(2,1)S(1)} %collective-permute-done.5.own_ref, bf16[2,64,3072]{2,1,0:T(8,128)(2,1)S(1)} %collective-permute-done.6.other_ref, bf16[384,3072]{1,0:T(8,128)(2,1)S(1)} %copy-done, bf16[1536,3072]{1,0:T(8,128)(2,1)} %refs_1_.11), custom_call_target="tpu_custom_call" | custom-call | flops 47185920 | bytes 199680 | tf_op jit(solution)/shard_map/cot_product/pallas_call | solution.py:214
  70.7 23.6 %collective-permute-done.3.own_ref = bf16[2,64,3072]{2,1,0:T(8,128)(2,1)S(1)} collective-permute-done((bf16[2,64,3072]{2,1,0:T(8,128)(2,1)}, bf16[2,64,3072]{2,1,0:T(8,128)(2,1)S(1)}, u32[]{:S(2)}, u32[]{:S(2)}) %collective-permute-start.3) | collective-permute-done | bytes 786464 | tf_op jit(solution)/shard_map/ppermute | solution.py:121
  95.1 4.5 pack.6
  101.3 4.2 collective-permute-done.11.refs_2_
  107.5 8.5 %cot_product.7 = bf16[256,1920]{1,0:T(8,128)(2,1)S(1)} custom-call(bf16[2,64,3072]{2,1,0:T(8,128)(2,1)S(1)} %collective-permute-done.3.own_ref, bf16[2,64,3072]{2,1,0:T(8,128)(2,1)S(1)} %collective-permute-done.12.other_ref, bf16[384,3072]{1,0:T(8,128)(2,1)S(1)} %copy-done, bf16[1536,3072]{1,0:T(8,128)(2,1)} %refs_1_.11), custom_call_target="tpu_custom_call" | custom-call | flops 47185920 | bytes 199680 | tf_op jit(solution)/shard_map/cot_product/pallas_call | solution.py:214
  116.1 14.3 %collective-permute-done.4.own_ref = bf16[2,64,3072]{2,1,0:T(8,128)(2,1)S(1)} collective-permute-done((bf16[2,64,3072]{2,1,0:T(8,128)(2,1)S(1)}, bf16[2,64,3072]{2,1,0:T(8,128)(2,1)S(1)}, u32[]{:S(2)}, u32[]{:S(2)}) %collective-permute-start.4) | collective-permute-done | bytes 786464 | tf_op jit(solution)/shard_map/ppermute | solution.py:121
  132.2 4.6 all-to-all-start.1
  137.3 3.3 collective-permute-done.15.refs_4_
  143.1 14.3 %collective-permute-done.17.refs_6_ = bf16[2,64,3072]{2,1,0:T(8,128)(2,1)S(1)} collective-permute-done((bf16[2,64,3072]{2,1,0:T(8,128)(2,1)}, bf16[2,64,3072]{2,1,0:T(8,128)(2,1)S(1)}, u32[]{:S(2)}, u32[]{:S(2)}) %collective-permute-start.17) | collective-permute-done | bytes 786464 | tf_op jit(solution)/shard_map/ppermute | solution.py:121
  160.7 9.0 %cot_product.5 = bf16[256,1920]{1,0:T(8,128)(2,1)} custom-call(bf16[2,64,3072]{2,1,0:T(8,128)(2,1)S(1)} %copy-done.35, bf16[2,64,3072]{2,1,0:T(8,128)(2,1)S(1)} %collective-permute-done.8.other_ref, bf16[384,3072]{1,0:T(8,128)(2,1)S(1)} %copy-done, bf16[1536,3072]{1,0:T(8,128)(2,1)} %refs_1_.11), custom_call_target="tpu_custom_call" | custom-call | flops 47185920 | bytes 199680 | tf_op jit(solution)/shard_map/cot_product/pallas_call | solution.py:214
  171.6 5.0 %assemble.1.rows_ref = bf16[1024,3072]{1,0:T(8,128)(2,1)} custom-call(bf16[2,64,3072]{2,1,0:T(8,128)(2,1)} %pad_maximum_fusion.refs_0_, bf16[2,64,3072]{2,1,0:T(8,128)(2,1)S(1)} %collective-permute-done.1.refs_1_, bf16[2,64,3072]{2,1,0:T(8,128)(2,1)S(1)} %copy-done.33, bf16[2,64,3072]{2,1,0:T(8,128)(2,1)S(1)} %collective-permute-done.14.refs_3_, ...), custom_call_target="tpu_custom_call" | custom-call | bytes 196608 | tf_op jit(solution)/shard_map/assemble/pallas_call | solution.py:178
  176.5 4.4 all-to-all-start.2
  180.9 6.7 %pack.7 = bf16[4,768,768]{2,1,0:T(8,128)(2,1)S(1)} custom-call(bf16[768,6144]{1,0:T(8,128)(2,1)} %refs_0_.7), custom_call_target="tpu_custom_call" | custom-call | bytes 147456 | tf_op jit(solution)/shard_map/pack/pallas_call | solution.py:148
  189.8 14.0 %in_product.5.q_own.k_own.v_own = bf16[1024,1152]{1,0:T(8,128)(2,1)S(1)} custom-call(bf16[1024,3072]{1,0:T(8,128)(2,1)} %assemble.1.rows_ref, bf16[3072,1152]{1,0:T(8,128)(2,1)} %bitcast.4.weight_ref.refs_5_), custom_call_target="tpu_custom_call" | custom-call | flops 113246208 | bytes 245760 | tf_op jit(solution)/shard_map/in_product/pallas_call | solution.py:268
  205.1 5.1 %all-to-all-start.3 = ((bf16[4,768,768]{2,1,0:T(8,128)(2,1)}), bf16[4,768,768]{2,1,0:T(8,128)(2,1)}, u32[]{:S(2)}, u32[]{:S(2)}) async-start(bf16[4,768,768]{2,1,0:T(8,128)(2,1)} %copy-done.6), calls=%async_computation.3 | async-start | bytes 9437184 | tf_op jit(solution)/shard_map/all_to_all | solution.py:359
  212.3 6.9 %in_product.6 = bf16[1024,512]{1,0:T(8,128)(2,1)S(1)} custom-call(bf16[1024,3072]{1,0:T(8,128)(2,1)} %assemble.1.rows_ref, bf16[3072,512]{1,0:T(8,128)(2,1)} %bitcast.5.weight_ref.refs_6_), custom_call_target="tpu_custom_call" | custom-call | flops 50331648 | bytes 163840 | tf_op jit(solution)/shard_map/in_product/pallas_call | solution.py:268
  221.0 5.8 %in_product.9 = bf16[1024,256]{1,0:T(8,128)(2,1)} custom-call(bf16[1024,3072]{1,0:T(8,128)(2,1)} %assemble.1.rows_ref, bf16[3072,256]{1,0:T(8,128)(2,1)} %bitcast.6.weight_ref.refs_7_), custom_call_target="tpu_custom_call" | custom-call | flops 25165824 | bytes 131072 | tf_op jit(solution)/shard_map/in_product/pallas_call | solution.py:268
  227.5 58.1 %collective-permute-done.20 = bf16[256,1920]{1,0:T(8,128)(2,1)S(1)} collective-permute-done((bf16[256,1920]{1,0:T(8,128)(2,1)}, bf16[256,1920]{1,0:T(8,128)(2,1)S(1)}, u32[]{:S(2)}, u32[]{:S(2)}) %collective-permute-start.20) | collective-permute-done | bytes 983072 | tf_op jit(solution)/shard_map/ppermute | solution.py:121
  286.6 4.8 %add_parts.1 = bf16[4,4,64,1920]{3,2,1,0:T(8,128)(2,1)} custom-call(bf16[4,64,1920]{2,1,0:T(8,128)(2,1)S(1)} %bitcast.86, bf16[4,64,1920]{2,1,0:T(8,128)(2,1)S(1)} %bitcast.87, bf16[4,64,1920]{2,1,0:T(8,128)(2,1)S(1)} %bitcast.88, bf16[4,64,1920]{2,1,0:T(8,128)(2,1)} %bitcast.10.refs_3_, bf16[4,64,1920]{2,1,0:T(8,128)(2,1)S(1)} %bitcast.89, ...), custom_call_target="tpu_custom_call" | custom-call | bytes 184320 | tf_op jit(solution)/shard_map/add_parts/pallas_call | solution.py:244
  292.9 6.4 %in_product.7 = bf16[512,768]{1,0:T(8,128)(2,1)S(1)} custom-call(bf16[1024,3072]{1,0:T(8,128)(2,1)} %assemble.1.rows_ref, bf16[3072,768]{1,0:T(8,128)(2,1)} %bitcast.16.weight_ref.refs_1_), custom_call_target="tpu_custom_call" | custom-call | flops 37748736 | bytes 184320 | tf_op jit(solution)/shard_map/in_product/pallas_call | solution.py:268
  302.6 14.9 %attend.1 = (bf16[1024,384]{1,0:T(8,128)(2,1)S(1)}, bf16[1024,384]{1,0:T(8,128)(2,1)S(1)}, bf16[1024,384]{1,0:T(8,128)(2,1)S(1)}, bf16[1024,384]{1,0:T(8,128)(2,1)S(1)}) custom-call(bf16[1024,1152]{1,0:T(8,128)(2,1)S(1)} %copy-done.2, bf16[1024,1152]{1,0:T(8,128)(2,1)S(1)} %copy-done.5, bf16[1024,1152]{1,0:T(8,128)(2,1)S(1)} %copy-done.2, ...), custom_call_target="tpu_custom_call" | custom-call | flops 12582912 | bytes 98304 | tf_op jit(solution)/shard_map/attend/pallas_call | solution.py:75
  322.3 6.3 %in_product.8 = bf16[512,768]{1,0:T(8,128)(2,1)S(1)} custom-call(bf16[1024,3072]{1,0:T(8,128)(2,1)} %assemble.1.rows_ref, bf16[3072,768]{1,0:T(8,128)(2,1)} %bitcast.16.weight_ref.refs_1_), custom_call_target="tpu_custom_call" | custom-call | flops 37748736 | bytes 184320 | tf_op jit(solution)/shard_map/in_product/pallas_call | solution.py:268
  329.3 2.5 fusion.5
  331.8 18.5 %back_product.5.refs_2_ = bf16[1024,3072]{1,0:T(8,128)(2,1)} custom-call(bf16[1024,384]{1,0:T(8,128)(2,1)S(1)} %copy-done.27, bf16[1024,384]{1,0:T(8,128)(2,1)S(1)} %copy-done.29, bf16[1024,384]{1,0:T(8,128)(2,1)S(1)} %copy-done.31, bf16[1024,512]{1,0:T(8,128)(2,1)S(1)} %get-tuple-element.68.refs_3_, bf16[1024,256]{1,0:T(8,128)(2,1)S(1)} %get-tuple-element.76.refs_4_, ...), custom_call_target="tpu_custom_call" | custom-call | flops 188743680 | bytes 282624 | tf_op jit(solution)/shard_map/back_product/pallas_call | solution.py:321
  350.3 12.3 %out_product.6.refs_2_ = bf16[1024,3072]{1,0:T(8,128)(2,1)} custom-call(bf16[1024,384]{1,0:T(8,128)(2,1)S(1)} %copy-done.25, bf16[1024,512]{1,0:T(8,128)(2,1)S(1)} %get-tuple-element.69.refs_1_, bf16[1024,256]{1,0:T(8,128)(2,1)S(1)} %get-tuple-element.77.refs_2_, bf16[384,3072]{1,0:T(8,128)(2,1)S(1)} %copy-done, bf16[1536,3072]{1,0:T(8,128)(2,1)} %refs_1_.11), custom_call_target="tpu_custom_call" | custom-call | flops 113246208 | bytes 282624 | tf_op jit(solution)/shard_map/out_product/pallas_call | solution.py:321
  364.7 7.7 %out_product.7 = bf16[512,3072]{1,0:T(8,128)(2,1)} custom-call(bf16[512,768]{1,0:T(8,128)(2,1)S(1)} %get-tuple-element.75.refs_0_, bf16[1536,3072]{1,0:T(8,128)(2,1)} %refs_1_.11, bf16[1024,3072]{1,0:T(8,128)(2,1)} %out_product.6.refs_2_), custom_call_target="tpu_custom_call" | custom-call | flops 37748736 | bytes 196608 | tf_op jit(solution)/shard_map/out_product/pallas_call | solution.py:321
  372.5 6.9 %back_product.6 = bf16[512,3072]{1,0:T(8,128)(2,1)S(1)} custom-call(bf16[512,768]{1,0:T(8,128)(2,1)S(1)} %get-tuple-element.56.refs_0_, bf16[3072,768]{1,0:T(8,128)(2,1)} %bitcast.16.weight_ref.refs_1_, bf16[1024,3072]{1,0:T(8,128)(2,1)} %back_product.5.refs_2_), custom_call_target="tpu_custom_call" | custom-call | flops 37748736 | bytes 122880 | tf_op jit(solution)/shard_map/back_product/pallas_call | solution.py:321
  382.1 3.2 out_product.9
  387.4 3.2 out_product.11
  390.7 3.9 back_product.9
  396.2 3.3 back_product.8
  401.5 3.2 out_product.10
  404.7 3.2 out_product.8
  407.9 3.3 back_product.7
  413.4 9.2 %collective-permute-done.29 = bf16[256,1536]{1,0:T(8,128)(2,1)S(1)} collective-permute-done((bf16[256,1536]{1,0:T(8,128)(2,1)S(1)}, bf16[256,1536]{1,0:T(8,128)(2,1)S(1)}, u32[]{:S(2)}, u32[]{:S(2)}) %collective-permute-start.29) | collective-permute-done | bytes 786464 | tf_op jit(solution)/shard_map/ppermute | solution.py:121
  424.5 3.5 collective-permute-start.37
  428.0 10.8 %collective-permute-done.33 = bf16[256,1536]{1,0:T(8,128)(2,1)S(1)} collective-permute-done((bf16[256,1536]{1,0:T(8,128)(2,1)S(1)}, bf16[256,1536]{1,0:T(8,128)(2,1)S(1)}, u32[]{:S(2)}, u32[]{:S(2)}) %collective-permute-start.33) | collective-permute-done | bytes 786464 | tf_op jit(solution)/shard_map/ppermute | solution.py:121
  440.6 3.5 collective-permute-start.28
  446.2 11.9 %collective-permute-done.34 = bf16[2,64,1536]{2,1,0:T(8,128)(2,1)S(1)} collective-permute-done((bf16[2,64,1536]{2,1,0:T(8,128)(2,1)S(1)}, bf16[2,64,1536]{2,1,0:T(8,128)(2,1)S(1)}, u32[]{:S(2)}, u32[]{:S(2)}) %collective-permute-start.34) | collective-permute-done | bytes 393248 | tf_op jit(solution)/shard_map/ppermute | solution.py:121
  459.7 9.9 %collective-permute-done.35 = bf16[64,1536]{1,0:T(8,128)(2,1)S(1)} collective-permute-done((bf16[64,1536]{1,0:T(8,128)(2,1)S(1)}, bf16[64,1536]{1,0:T(8,128)(2,1)S(1)}, u32[]{:S(2)}, u32[]{:S(2)}) %collective-permute-start.35) | collective-permute-done | bytes 196640 | tf_op jit(solution)/shard_map/ppermute | solution.py:121
  470.6 5.6 %all-reduce = (f32[64]{0:T(128)S(1)}, f32[64]{0:T(128)}) all-reduce(f32[64]{0:T(128)S(1)} %fusion.28, f32[64]{0:T(128)} %reduce_sum.48), channel_id=1, replica_groups=mesh['gx'=4,'gy'=4,'gz'=2] {'gz'}, use_global_device_ids=true, to_apply=%region_8.9 | all-reduce | flops 128 | bytes 1024 | tf_op jit(solution)/shard_map/psum | solution.py:489
  (189 shorter events, 72.6 us)
Async XLA Ops:
  0.6 19.0 %collective-permute-start.2 = (bf16[64,3072]{1,0:T(8,128)(2,1)}, bf16[64,3072]{1,0:T(8,128)(2,1)S(1)}, u32[]{:S(2)}, u32[]{:S(2)}) collective-permute-start(bf16[64,3072]{1,0:T(8,128)(2,1)} %param.9), channel_id=1, source_target_pairs={{0,16},{8,24},{16,0},{24,8},{1,17},{9,25},{17,1},{25,9},{2,18},{10... | collective-permute-start | bytes 1179656 | tf_op jit(solution)/shard_map/ppermute | solution.py:121
  10.9 10.4 %collective-permute-start = (bf16[64,3072]{1,0:T(8,128)(2,1)S(1)}, bf16[64,3072]{1,0:T(8,128)(2,1)S(1)}, u32[]{:S(2)}, u32[]{:S(2)}) collective-permute-start(bf16[64,3072]{1,0:T(8,128)(2,1)S(1)} %fusion.27), channel_id=1, source_target_pairs={{0,16},{8,24},{16,0},{24,8},{1,17},{9,25},{17,1},{25,9},{2,18},{10... | collective-permute-start | bytes 1179656 | tf_op jit(solution)/shard_map/ppermute | solution.py:121
  19.7 2.7 collective-permute-start.9
  30.5 101.7 %all-to-all-start = ((bf16[4,768,1152]{2,1,0:T(8,128)(2,1)}), bf16[4,768,1152]{2,1,0:T(8,128)(2,1)}, u32[]{:S(2)}, u32[]{:S(2)}) async-start(bf16[4,768,1152]{2,1,0:T(8,128)(2,1)} %pack.4), calls=%async_computation | async-start | bytes 14155776 | tf_op jit(solution)/shard_map/all_to_all | solution.py:359
  35.9 20.2 %collective-permute-start.5 = (bf16[2,64,3072]{2,1,0:T(8,128)(2,1)}, bf16[2,64,3072]{2,1,0:T(8,128)(2,1)S(1)}, u32[]{:S(2)}, u32[]{:S(2)}) collective-permute-start(bf16[2,64,3072]{2,1,0:T(8,128)(2,1)} %copy-done.15), channel_id=1, source_target_pairs={{0,2},{2,0},{4,6},{6,4},{1,3},{3,1},{5,7},{7,5},{8,10},{10,8},{12,... | collective-permute-start | bytes 2359304 | tf_op jit(solution)/shard_map/ppermute | solution.py:121
  56.1 4.3 collective-permute-start.6
  56.1 38.1 %collective-permute-start.3 = (bf16[2,64,3072]{2,1,0:T(8,128)(2,1)}, bf16[2,64,3072]{2,1,0:T(8,128)(2,1)S(1)}, u32[]{:S(2)}, u32[]{:S(2)}) collective-permute-start(bf16[2,64,3072]{2,1,0:T(8,128)(2,1)} %copy-done.15), channel_id=1, source_target_pairs={{0,4},{2,6},{4,0},{6,2},{1,5},{3,7},{5,1},{7,3},{8,12},{10,14},{12... | collective-permute-start | bytes 2359304 | tf_op jit(solution)/shard_map/ppermute | solution.py:121
  58.9 48.6 %collective-permute-start.10 = (bf16[256,1920]{1,0:T(8,128)(2,1)S(1)}, bf16[256,1920]{1,0:T(8,128)(2,1)S(1)}, u32[]{:S(2)}, u32[]{:S(2)}) collective-permute-start(bf16[256,1920]{1,0:T(8,128)(2,1)S(1)} %cot_product.6), channel_id=1, source_target_pairs={{0,1},{1,0},{2,3},{3,2},{4,5},{5,4},{6,7},{7,6},{8,9},{9,8},{10,11... | collective-permute-start | bytes 2949128 | tf_op jit(solution)/shard_map/ppermute | solution.py:121
  68.6 62.7 %collective-permute-start.7 = (bf16[256,1920]{1,0:T(8,128)(2,1)S(1)}, bf16[256,1920]{1,0:T(8,128)(2,1)S(1)}, u32[]{:S(2)}, u32[]{:S(2)}) collective-permute-start(bf16[256,1920]{1,0:T(8,128)(2,1)S(1)} %cot_product.4), channel_id=1, source_target_pairs={{0,1},{1,0},{2,3},{3,2},{4,5},{5,4},{6,7},{7,6},{8,9},{9,8},{10,11... | collective-permute-start | bytes 2949128 | tf_op jit(solution)/shard_map/ppermute | solution.py:121
  69.2 36.3 %collective-permute-start.11 = (bf16[2,64,3072]{2,1,0:T(8,128)(2,1)}, bf16[2,64,3072]{2,1,0:T(8,128)(2,1)S(1)}, u32[]{:S(2)}, u32[]{:S(2)}) collective-permute-start(bf16[2,64,3072]{2,1,0:T(8,128)(2,1)} %pad_maximum_fusion.refs_0_), channel_id=1, source_target_pairs={{0,2},{2,0},{4,6},{6,4},{1,3},{3,1},{5,7},{7,5},{8,10},{10,8},{12,... | collective-permute-start | bytes 2359304 | tf_op jit(solution)/shard_map/ppermute | solution.py:121
  94.3 13.2 %collective-permute-start.12 = (bf16[2,64,3072]{2,1,0:T(8,128)(2,1)S(1)}, bf16[2,64,3072]{2,1,0:T(8,128)(2,1)S(1)}, u32[]{:S(2)}, u32[]{:S(2)}) collective-permute-start(bf16[2,64,3072]{2,1,0:T(8,128)(2,1)S(1)} %collective-permute-done.3.own_ref), channel_id=1, source_target_pairs={{0,8},{8,0},{16,24},{24,16},{1,9},{9,1},{17,25},{25,17},{2,10},{10... | collective-permute-start | bytes 2359304 | tf_op jit(solution)/shard_map/ppermute | solution.py:121
  94.3 36.1 %collective-permute-start.4 = (bf16[2,64,3072]{2,1,0:T(8,128)(2,1)S(1)}, bf16[2,64,3072]{2,1,0:T(8,128)(2,1)S(1)}, u32[]{:S(2)}, u32[]{:S(2)}) collective-permute-start(bf16[2,64,3072]{2,1,0:T(8,128)(2,1)S(1)} %collective-permute-done.3.own_ref), channel_id=1, source_target_pairs={{0,2},{2,0},{4,6},{6,4},{1,3},{3,1},{5,7},{7,5},{8,10},{10,8},{12,... | collective-permute-start | bytes 2359304 | tf_op jit(solution)/shard_map/ppermute | solution.py:121
  105.5 35.1 %collective-permute-start.15 = (bf16[2,64,3072]{2,1,0:T(8,128)(2,1)}, bf16[2,64,3072]{2,1,0:T(8,128)(2,1)}, u32[]{:S(2)}, u32[]{:S(2)}) collective-permute-start(bf16[2,64,3072]{2,1,0:T(8,128)(2,1)} %pad_maximum_fusion.refs_0_), channel_id=1, source_target_pairs={{0,4},{2,6},{4,0},{6,2},{1,5},{3,7},{5,1},{7,3},{8,12},{10,14},{12... | collective-permute-start | bytes 2359304 | tf_op jit(solution)/shard_map/ppermute | solution.py:121
  132.2 44.3 %all-to-all-start.1 = ((bf16[4,768,512]{2,1,0:T(8,128)(2,1)}), bf16[4,768,512]{2,1,0:T(8,128)(2,1)}, u32[]{:S(2)}, u32[]{:S(2)}) async-start(bf16[4,768,512]{2,1,0:T(8,128)(2,1)} %copy-done.7), calls=%async_computation.1 | async-start | bytes 6291456 | tf_op jit(solution)/shard_map/all_to_all | solution.py:359
  136.8 6.2 %collective-permute-start.8 = (bf16[2,64,3072]{2,1,0:T(8,128)(2,1)}, bf16[2,64,3072]{2,1,0:T(8,128)(2,1)S(1)}, u32[]{:S(2)}, u32[]{:S(2)}) collective-permute-start(bf16[2,64,3072]{2,1,0:T(8,128)(2,1)} %copy-done.34), channel_id=1, source_target_pairs={{0,8},{8,0},{16,24},{24,16},{1,9},{9,1},{17,25},{25,17},{2,10},{10... | collective-permute-start | bytes 2359304 | tf_op jit(solution)/shard_map/ppermute | solution.py:121
  140.6 16.7 %collective-permute-start.17 = (bf16[2,64,3072]{2,1,0:T(8,128)(2,1)}, bf16[2,64,3072]{2,1,0:T(8,128)(2,1)S(1)}, u32[]{:S(2)}, u32[]{:S(2)}) collective-permute-start(bf16[2,64,3072]{2,1,0:T(8,128)(2,1)} %collective-permute-done.15.refs_4_), channel_id=1, source_target_pairs={{0,2},{2,0},{4,6},{6,4},{1,3},{3,1},{5,7},{7,5},{8,10},{10,8},{12,... | collective-permute-start | bytes 2359304 | tf_op jit(solution)/shard_map/ppermute | solution.py:121
  142.1 27.7 %collective-permute-start.13 = (bf16[256,1920]{1,0:T(8,128)(2,1)S(1)}, bf16[256,1920]{1,0:T(8,128)(2,1)S(1)}, u32[]{:S(2)}, u32[]{:S(2)}) collective-permute-start(bf16[256,1920]{1,0:T(8,128)(2,1)S(1)} %cot_product.7), channel_id=1, source_target_pairs={{0,1},{1,0},{2,3},{3,2},{4,5},{5,4},{6,7},{7,6},{8,9},{9,8},{10,11... | collective-permute-start | bytes 2949128 | tf_op jit(solution)/shard_map/ppermute | solution.py:121
  142.6 27.2 %collective-permute-start.1 = (bf16[2,64,3072]{2,1,0:T(8,128)(2,1)}, bf16[2,64,3072]{2,1,0:T(8,128)(2,1)S(1)}, u32[]{:S(2)}, u32[]{:S(2)}) collective-permute-start(bf16[2,64,3072]{2,1,0:T(8,128)(2,1)} %pad_maximum_fusion.refs_0_), channel_id=1, source_target_pairs={{0,8},{8,0},{16,24},{24,16},{1,9},{9,1},{17,25},{25,17},{2,10},{10... | collective-permute-start | bytes 2359304 | tf_op jit(solution)/shard_map/ppermute | solution.py:121
  142.6 27.2 %collective-permute-start.16 = (bf16[2,64,3072]{2,1,0:T(8,128)(2,1)}, bf16[2,64,3072]{2,1,0:T(8,128)(2,1)S(1)}, u32[]{:S(2)}, u32[]{:S(2)}) collective-permute-start(bf16[2,64,3072]{2,1,0:T(8,128)(2,1)} %collective-permute-done.15.refs_4_), channel_id=1, source_target_pairs={{0,8},{8,0},{16,24},{24,16},{1,9},{9,1},{17,25},{25,17},{2,10},{10... | collective-permute-start | bytes 2359304 | tf_op jit(solution)/shard_map/ppermute | solution.py:121
  143.1 26.7 %collective-permute-start.14 = (bf16[2,64,3072]{2,1,0:T(8,128)(2,1)}, bf16[2,64,3072]{2,1,0:T(8,128)(2,1)S(1)}, u32[]{:S(2)}, u32[]{:S(2)}) collective-permute-start(bf16[2,64,3072]{2,1,0:T(8,128)(2,1)} %copy-done.32), channel_id=1, source_target_pairs={{0,8},{8,0},{16,24},{24,16},{1,9},{9,1},{17,25},{25,17},{2,10},{10... | collective-permute-start | bytes 2359304 | tf_op jit(solution)/shard_map/ppermute | solution.py:121
  157.4 12.4 %collective-permute-start.18 = (bf16[2,64,3072]{2,1,0:T(8,128)(2,1)S(1)}, bf16[2,64,3072]{2,1,0:T(8,128)(2,1)S(1)}, u32[]{:S(2)}, u32[]{:S(2)}) collective-permute-start(bf16[2,64,3072]{2,1,0:T(8,128)(2,1)S(1)} %collective-permute-done.17.refs_6_), channel_id=1, source_target_pairs={{0,8},{8,0},{16,24},{24,16},{1,9},{9,1},{17,25},{25,17},{2,10},{10... | collective-permute-start | bytes 2359304 | tf_op jit(solution)/shard_map/ppermute | solution.py:121
  176.5 28.6 %all-to-all-start.2 = ((bf16[4,768,256]{2,1,0:T(8,128)(2,1)}), bf16[4,768,256]{2,1,0:T(8,128)(2,1)}, u32[]{:S(2)}, u32[]{:S(2)}) async-start(bf16[4,768,256]{2,1,0:T(8,128)(2,1)} %copy-done.8), calls=%async_computation.2 | async-start | bytes 3145728 | tf_op jit(solution)/shard_map/all_to_all | solution.py:359
  205.1 87.7 %all-to-all-start.3 = ((bf16[4,768,768]{2,1,0:T(8,128)(2,1)}), bf16[4,768,768]{2,1,0:T(8,128)(2,1)}, u32[]{:S(2)}, u32[]{:S(2)}) async-start(bf16[4,768,768]{2,1,0:T(8,128)(2,1)} %copy-done.6), calls=%async_computation.3 | async-start | bytes 9437184 | tf_op jit(solution)/shard_map/all_to_all | solution.py:359
  210.2 81.2 %collective-permute-start.19 = (bf16[1024,1152]{1,0:T(8,128)(2,1)}, bf16[1024,1152]{1,0:T(8,128)(2,1)S(1)}, u32[]{:S(2)}, u32[]{:S(2)}) collective-permute-start(bf16[1024,1152]{1,0:T(8,128)(2,1)} %copy-done.1), channel_id=1, source_target_pairs={{0,1},{1,0},{2,3},{3,2},{4,5},{5,4},{6,7},{7,6},{8,9},{9,8},{10,11... | collective-permute-start | bytes 7077896 | tf_op jit(solution)/shard_map/ppermute | solution.py:121
  211.9 73.7 %collective-permute-start.20 = (bf16[256,1920]{1,0:T(8,128)(2,1)}, bf16[256,1920]{1,0:T(8,128)(2,1)S(1)}, u32[]{:S(2)}, u32[]{:S(2)}) collective-permute-start(bf16[256,1920]{1,0:T(8,128)(2,1)} %cot_product.5), channel_id=1, source_target_pairs={{0,1},{1,0},{2,3},{3,2},{4,5},{5,4},{6,7},{7,6},{8,9},{9,8},{10,11... | collective-permute-start | bytes 2949128 | tf_op jit(solution)/shard_map/ppermute | solution.py:121
  219.3 67.3 %copy-start.10 = (bf16[256,1920]{1,0:T(8,128)(2,1)S(1)}, bf16[256,1920]{1,0:T(8,128)(2,1)}, u32[]{:S(2)}) copy-start(bf16[256,1920]{1,0:T(8,128)(2,1)} %copy-done.9) | copy-start | bytes 2949124
  219.3 67.3 %copy-start.12 = (bf16[256,1920]{1,0:T(8,128)(2,1)S(1)}, bf16[256,1920]{1,0:T(8,128)(2,1)}, u32[]{:S(2)}) copy-start(bf16[256,1920]{1,0:T(8,128)(2,1)} %copy-done.11) | copy-start | bytes 2949124
  219.3 67.3 %copy-start.14 = (bf16[256,1920]{1,0:T(8,128)(2,1)S(1)}, bf16[256,1920]{1,0:T(8,128)(2,1)}, u32[]{:S(2)}) copy-start(bf16[256,1920]{1,0:T(8,128)(2,1)} %copy-done.13) | copy-start | bytes 2949124
  219.3 67.3 %copy-start.21 = (bf16[256,1920]{1,0:T(8,128)(2,1)S(1)}, bf16[256,1920]{1,0:T(8,128)(2,1)}, u32[]{:S(2)}) copy-start(bf16[256,1920]{1,0:T(8,128)(2,1)} %copy-done.20) | copy-start | bytes 2949124
  219.3 67.3 %copy-start.23 = (bf16[256,1920]{1,0:T(8,128)(2,1)S(1)}, bf16[256,1920]{1,0:T(8,128)(2,1)}, u32[]{:S(2)}) copy-start(bf16[256,1920]{1,0:T(8,128)(2,1)} %copy-done.22) | copy-start | bytes 2949124
  219.3 109.9 %collective-permute-start.21 = (bf16[1024,512]{1,0:T(8,128)(2,1)S(1)}, bf16[1024,512]{1,0:T(8,128)(2,1)}, u32[]{:S(2)}, u32[]{:S(2)}) collective-permute-start(bf16[1024,512]{1,0:T(8,128)(2,1)S(1)} %in_product.6), channel_id=1, source_target_pairs={{0,1},{1,0},{2,3},{3,2},{4,5},{5,4},{6,7},{7,6},{8,9},{9,8},{10,11... | collective-permute-start | bytes 3145736 | tf_op jit(solution)/shard_map/ppermute | solution.py:121
  226.8 93.4 %collective-permute-start.22 = (bf16[1024,256]{1,0:T(8,128)(2,1)}, bf16[1024,256]{1,0:T(8,128)(2,1)}, u32[]{:S(2)}, u32[]{:S(2)}) collective-permute-start(bf16[1024,256]{1,0:T(8,128)(2,1)} %in_product.9), channel_id=1, source_target_pairs={{0,1},{1,0},{2,3},{3,2},{4,5},{5,4},{6,7},{7,6},{8,9},{9,8},{10,11... | collective-permute-start | bytes 1572872 | tf_op jit(solution)/shard_map/ppermute | solution.py:121
  299.3 63.3 %collective-permute-start.23 = (bf16[512,768]{1,0:T(8,128)(2,1)S(1)}, bf16[512,768]{1,0:T(8,128)(2,1)}, u32[]{:S(2)}, u32[]{:S(2)}) collective-permute-start(bf16[512,768]{1,0:T(8,128)(2,1)S(1)} %in_product.7), channel_id=1, source_target_pairs={{0,1},{1,0},{2,3},{3,2},{4,5},{5,4},{6,7},{7,6},{8,9},{9,8},{10,11... | collective-permute-start | bytes 2359304 | tf_op jit(solution)/shard_map/ppermute | solution.py:121
  328.6 43.8 %collective-permute-start.24 = (bf16[512,768]{1,0:T(8,128)(2,1)S(1)}, bf16[512,768]{1,0:T(8,128)(2,1)}, u32[]{:S(2)}, u32[]{:S(2)}) collective-permute-start(bf16[512,768]{1,0:T(8,128)(2,1)S(1)} %in_product.8), channel_id=1, source_target_pairs={{0,1},{1,0},{2,3},{3,2},{4,5},{5,4},{6,7},{7,6},{8,9},{9,8},{10,11... | collective-permute-start | bytes 2359304 | tf_op jit(solution)/shard_map/ppermute | solution.py:121
  372.4 9.6 %collective-permute-start.25 = (bf16[512,3072]{1,0:T(8,128)(2,1)}, bf16[512,3072]{1,0:T(8,128)(2,1)S(1)}, u32[]{:S(2)}, u32[]{:S(2)}) collective-permute-start(bf16[512,3072]{1,0:T(8,128)(2,1)} %out_product.7), channel_id=1, source_target_pairs={{0,8},{8,0},{16,24},{24,16},{1,9},{9,1},{17,25},{25,17},{2,10},{10... | collective-permute-start | bytes 9437192 | tf_op jit(solution)/shard_map/ppermute | solution.py:121
  379.4 11.3 %collective-permute-start.32 = (bf16[512,3072]{1,0:T(8,128)(2,1)S(1)}, bf16[512,3072]{1,0:T(8,128)(2,1)S(1)}, u32[]{:S(2)}, u32[]{:S(2)}) collective-permute-start(bf16[512,3072]{1,0:T(8,128)(2,1)S(1)} %back_product.6), channel_id=1, source_target_pairs={{0,8},{8,0},{16,24},{24,16},{1,9},{9,1},{17,25},{25,17},{2,10},{10... | collective-permute-start | bytes 9437192 | tf_op jit(solution)/shard_map/ppermute | solution.py:121
  385.3 25.9 %collective-permute-start.26 = (bf16[256,1536]{1,0:T(8,128)(2,1)S(1)}, bf16[256,1536]{1,0:T(8,128)(2,1)}, u32[]{:S(2)}, u32[]{:S(2)}) collective-permute-start(bf16[256,1536]{1,0:T(8,128)(2,1)S(1)} %out_product.9), channel_id=1, source_target_pairs={{0,16},{8,24},{16,0},{24,8},{1,17},{9,25},{17,1},{25,9},{2,18},{10... | collective-permute-start | bytes 2359304 | tf_op jit(solution)/shard_map/ppermute | solution.py:121
  390.6 32.0 %collective-permute-start.29 = (bf16[256,1536]{1,0:T(8,128)(2,1)S(1)}, bf16[256,1536]{1,0:T(8,128)(2,1)S(1)}, u32[]{:S(2)}, u32[]{:S(2)}) collective-permute-start(bf16[256,1536]{1,0:T(8,128)(2,1)S(1)} %out_product.11), channel_id=1, source_target_pairs={{0,16},{8,24},{16,0},{24,8},{1,17},{9,25},{17,1},{25,9},{2,18},{10... | collective-permute-start | bytes 2359304 | tf_op jit(solution)/shard_map/ppermute | solution.py:121
  394.8 29.4 %collective-permute-start.36 = (bf16[2,2,64,1536]{3,2,0,1:T(8,128)(2,1)S(1)}, bf16[2,2,64,1536]{3,2,0,1:T(8,128)(2,1)S(1)}, u32[]{:S(2)}, u32[]{:S(2)}) collective-permute-start(bf16[2,2,64,1536]{3,2,0,1:T(8,128)(2,1)S(1)} %bitcast.100), channel_id=1, source_target_pairs={{0,2},{2,0},{4,6},{6,4},{1,3},{3,1},{5,7},{7,5},{8,10},{10,8},{12,... | collective-permute-start | bytes 2359304 | tf_op jit(solution)/shard_map/ppermute | solution.py:121
  399.4 39.3 %collective-permute-start.33 = (bf16[256,1536]{1,0:T(8,128)(2,1)S(1)}, bf16[256,1536]{1,0:T(8,128)(2,1)S(1)}, u32[]{:S(2)}, u32[]{:S(2)}) collective-permute-start(bf16[256,1536]{1,0:T(8,128)(2,1)S(1)} %back_product.8), channel_id=1, source_target_pairs={{0,16},{8,24},{16,0},{24,8},{1,17},{9,25},{17,1},{25,9},{2,18},{10... | collective-permute-start | bytes 2359304 | tf_op jit(solution)/shard_map/ppermute | solution.py:121
  412.6 27.8 %collective-permute-start.27 = (bf16[2,64,1536]{2,1,0:T(8,128)(2,1)S(1)}, bf16[2,64,1536]{2,1,0:T(8,128)(2,1)S(1)}, u32[]{:S(2)}, u32[]{:S(2)}) collective-permute-start(bf16[2,64,1536]{2,1,0:T(8,128)(2,1)S(1)} %fusion.40), channel_id=1, source_target_pairs={{0,2},{2,0},{4,6},{6,4},{1,3},{3,1},{5,7},{7,5},{8,10},{10,8},{12,... | collective-permute-start | bytes 1179656 | tf_op jit(solution)/shard_map/ppermute | solution.py:121
  422.8 21.2 %collective-permute-start.30 = (bf16[2,64,1536]{2,1,0:T(8,128)(2,1)S(1)}, bf16[2,64,1536]{2,1,0:T(8,128)(2,1)S(1)}, u32[]{:S(2)}, u32[]{:S(2)}) collective-permute-start(bf16[2,64,1536]{2,1,0:T(8,128)(2,1)S(1)} %fusion.41), channel_id=1, source_target_pairs={{0,2},{2,0},{4,6},{6,4},{1,3},{3,1},{5,7},{7,5},{8,10},{10,8},{12,... | collective-permute-start | bytes 1179656 | tf_op jit(solution)/shard_map/ppermute | solution.py:121
  424.5 20.1 %collective-permute-start.37 = (bf16[2,64,1536]{2,1,0:T(8,128)(2,1)S(1)}, bf16[2,64,1536]{2,1,0:T(8,128)(2,1)S(1)}, u32[]{:S(2)}, u32[]{:S(2)}) collective-permute-start(bf16[2,64,1536]{2,1,0:T(8,128)(2,1)S(1)} %fusion.39), channel_id=1, source_target_pairs={{0,4},{2,6},{4,0},{6,2},{1,5},{3,7},{5,1},{7,3},{8,12},{10,14},{12... | collective-permute-start | bytes 1179656 | tf_op jit(solution)/shard_map/ppermute | solution.py:121
  439.1 19.0 %collective-permute-start.34 = (bf16[2,64,1536]{2,1,0:T(8,128)(2,1)S(1)}, bf16[2,64,1536]{2,1,0:T(8,128)(2,1)S(1)}, u32[]{:S(2)}, u32[]{:S(2)}) collective-permute-start(bf16[2,64,1536]{2,1,0:T(8,128)(2,1)S(1)} %fusion.42), channel_id=1, source_target_pairs={{0,2},{2,0},{4,6},{6,4},{1,3},{3,1},{5,7},{7,5},{8,10},{10,8},{12,... | collective-permute-start | bytes 1179656 | tf_op jit(solution)/shard_map/ppermute | solution.py:121
  440.6 35.6 %collective-permute-start.28 = (bf16[64,1536]{1,0:T(8,128)(2,1)S(1)}, bf16[64,1536]{1,0:T(8,128)(2,1)}, u32[]{:S(2)}, u32[]{:S(2)}) collective-permute-start(bf16[64,1536]{1,0:T(8,128)(2,1)S(1)} %fusion.47), channel_id=1, source_target_pairs={{0,4},{2,6},{4,0},{6,2},{1,5},{3,7},{5,1},{7,3},{8,12},{10,14},{12... | collective-permute-start | bytes 589832 | tf_op jit(solution)/shard_map/ppermute | solution.py:121
  444.1 33.7 %collective-permute-start.31 = (bf16[64,1536]{1,0:T(8,128)(2,1)S(1)}, bf16[64,1536]{1,0:T(8,128)(2,1)}, u32[]{:S(2)}, u32[]{:S(2)}) collective-permute-start(bf16[64,1536]{1,0:T(8,128)(2,1)S(1)} %fusion.48), channel_id=1, source_target_pairs={{0,4},{2,6},{4,0},{6,2},{1,5},{3,7},{5,1},{7,3},{8,12},{10,14},{12... | collective-permute-start | bytes 589832 | tf_op jit(solution)/shard_map/ppermute | solution.py:121
  444.7 14.9 %collective-permute-start.38 = (bf16[64,1536]{1,0:T(8,128)(2,1)S(1)}, bf16[64,1536]{1,0:T(8,128)(2,1)S(1)}, u32[]{:S(2)}, u32[]{:S(2)}) collective-permute-start(bf16[64,1536]{1,0:T(8,128)(2,1)S(1)} %fusion.50), channel_id=1, source_target_pairs={{0,16},{8,24},{16,0},{24,8},{1,17},{9,25},{17,1},{25,9},{2,18},{10... | collective-permute-start | bytes 589832 | tf_op jit(solution)/shard_map/ppermute | solution.py:121
  458.2 11.4 %collective-permute-start.35 = (bf16[64,1536]{1,0:T(8,128)(2,1)S(1)}, bf16[64,1536]{1,0:T(8,128)(2,1)S(1)}, u32[]{:S(2)}, u32[]{:S(2)}) collective-permute-start(bf16[64,1536]{1,0:T(8,128)(2,1)S(1)} %fusion.49), channel_id=1, source_target_pairs={{0,4},{2,6},{4,0},{6,2},{1,5},{3,7},{5,1},{7,3},{8,12},{10,14},{12... | collective-permute-start | bytes 589832 | tf_op jit(solution)/shard_map/ppermute | solution.py:121
  (38 other events, 254.2 us)

commit v16 on v14

--- a/solution.py
+++ b/solution.py
@@ -386,7 +386,7 @@
             own = after(own, cot_gots[1])
         cot_owns.append(cot_product((own, other), w_attn_out, w_mlp_out))
         cot_gots.append(others(cot_owns[-1]))
-    normed_parts.append(trade(after(normed_parts[2], *cot_owns[1:3]), "gy", 1))
+    normed_parts.append(trade(after(normed_parts[2], *cot_owns[1:4]), "gy", 1))
     normed_parts = [with_core(part) for part in normed_parts]
     normed_parts[0] = after(normed_parts[0], cot_owns[3], cot_gots[2])
     all_in = assemble(normed_parts)

time: 477 us -> 485 us (1.017)
  waiting for transfers between devices: 174 us -> 185 us
    ppermute x39, waiting for transfers between devices: 174 us -> 185 us  [trade(): return lax.ppermute(block, axis, pairs)]
    unnamed x93 -> x89, local copies, waits for them, and re-layouts: 21.9 us -> 21.1 us
where the time goes in v16:
time: 485 us; the launch traced here: 483 us
  Pallas kernels  185 us (38%)
  waiting for transfers between devices  185 us (38%)
  starting transfers between devices  59.7 us (12%)
  local copies, waits for them, and re-layouts  21.5 us (4%)
  other arithmetic  19.3 us (4%)
  blocking collectives  10.5 us (2%)
    ppermute x39, waiting for transfers between devices, trade(): return lax.ppermute(block, axis, pairs)  185 us
    pallas_call x11, Pallas kernels, product(): pl.pallas_call(kernel, grid=(columns // tile,), in_specs=specs, out_specs...  68.6 us
    ppermute x39, starting transfers between devices, trade(): return lax.ppermute(block, axis, pairs)  40.1 us
    pallas_call x5, Pallas kernels, in_product(): pl.pallas_call(in_kernel, grid=(columns // tile,), in_specs=[pl.BlockSpec...  39.7 us
    pallas_call x4, Pallas kernels, cot_product(): pl.pallas_call(cot_kernel, grid=(columns // tile,), in_specs=[whole, whol...  33.4 us
    unnamed x89, local copies, waits for them, and re-layouts  21.1 us
    all_to_all x4, starting transfers between devices, swap(): lax.all_to_all(packed, 'gx', split_axis=0, concat_axis=0, tiled=True)  19.7 us
    pallas_call x4, Pallas kernels, pack(): pl.pallas_call(pack_kernel, grid=(owners, width // tile), in_specs=[spec]...  18.6 us
  transfers between devices with their start and end apart: 43, of which 14 were waited for; matrix products, arithmetic and copies ran while one was open for 4% of the time, Pallas kernels for 37%

profile of v16, /device:TPU:0, one launch (start us, length us, event | category | flops | bytes accessed | tf_op | source)
XLA Modules:
  0.0 482.7 jit_solution(2985254473234027995)
XLA Ops:
  0.6 3.0 collective-permute-start.2
  4.8 4.9 %all-reduce.1 = (f32[64]{0:T(128)S(1)}, f32[64]{0:T(128)S(1)}) all-reduce(f32[64]{0:T(128)S(1)} %get-tuple-element.59, f32[64]{0:T(128)S(1)} %get-tuple-element.58), channel_id=1, replica_groups=mesh['gx'=4,'gy'=4,'gz'=2] {'gz'}, use_global_device_ids=true, to_apply=%region_3.0 | all-reduce | flops 128 | bytes 1024 | tf_op jit(solution)/shard_map/psum | solution.py:371
  14.4 5.2 %pack.4 = bf16[4,768,1152]{2,1,0:T(8,128)(2,1)} custom-call(bf16[768,1536]{1,0:T(8,128)(2,1)S(1)} %copy-done.21, bf16[768,1536]{1,0:T(8,128)(2,1)S(1)} %copy-done.22, bf16[768,1536]{1,0:T(8,128)(2,1)} %refs_2_.1), custom_call_target="tpu_custom_call" | custom-call | bytes 221184 | tf_op jit(solution)/shard_map/pack/pallas_call | solution.py:148
  22.4 8.2 %cot_product.6 = bf16[256,1920]{1,0:T(8,128)(2,1)S(1)} custom-call(bf16[2,64,3072]{2,1,0:T(8,128)(2,1)S(1)} %pad_maximum_fusion.1.own_ref, bf16[2,64,3072]{2,1,0:T(8,128)(2,1)S(1)} %collective-permute-done.9.other_ref, bf16[384,3072]{1,0:T(8,128)(2,1)S(1)} %copy-done, bf16[1536,3072]{1,0:T(8,128)(2,1)} %refs_1_.11), custom_call_target="tpu_custom_call" | custom-call | flops 47185920 | bytes 199680 | tf_op jit(solution)/shard_map/cot_product/pallas_call | solution.py:214
  30.5 5.4 %all-to-all-start = ((bf16[4,768,1152]{2,1,0:T(8,128)(2,1)}), bf16[4,768,1152]{2,1,0:T(8,128)(2,1)}, u32[]{:S(2)}, u32[]{:S(2)}) async-start(bf16[4,768,1152]{2,1,0:T(8,128)(2,1)} %pack.4), calls=%async_computation | async-start | bytes 14155776 | tf_op jit(solution)/shard_map/all_to_all | solution.py:359
  37.8 18.3 %collective-permute-done.5.own_ref = bf16[2,64,3072]{2,1,0:T(8,128)(2,1)S(1)} collective-permute-done((bf16[2,64,3072]{2,1,0:T(8,128)(2,1)}, bf16[2,64,3072]{2,1,0:T(8,128)(2,1)S(1)}, u32[]{:S(2)}, u32[]{:S(2)}) %collective-permute-start.5) | collective-permute-done | bytes 786464 | tf_op jit(solution)/shard_map/ppermute | solution.py:121
  56.1 2.8 collective-permute-start.3
  60.4 8.1 %cot_product.4 = bf16[256,1920]{1,0:T(8,128)(2,1)S(1)} custom-call(bf16[2,64,3072]{2,1,0:T(8,128)(2,1)S(1)} %collective-permute-done.5.own_ref, bf16[2,64,3072]{2,1,0:T(8,128)(2,1)S(1)} %collective-permute-done.6.other_ref, bf16[384,3072]{1,0:T(8,128)(2,1)S(1)} %copy-done, bf16[1536,3072]{1,0:T(8,128)(2,1)} %refs_1_.11), custom_call_target="tpu_custom_call" | custom-call | flops 47185920 | bytes 199680 | tf_op jit(solution)/shard_map/cot_product/pallas_call | solution.py:214
  70.7 23.5 %collective-permute-done.3.own_ref = bf16[2,64,3072]{2,1,0:T(8,128)(2,1)S(1)} collective-permute-done((bf16[2,64,3072]{2,1,0:T(8,128)(2,1)}, bf16[2,64,3072]{2,1,0:T(8,128)(2,1)S(1)}, u32[]{:S(2)}, u32[]{:S(2)}) %collective-permute-start.3) | collective-permute-done | bytes 786464 | tf_op jit(solution)/shard_map/ppermute | solution.py:121
  95.0 4.5 pack.6
  101.2 4.3 collective-permute-done.11.refs_2_
  107.5 22.5 %collective-permute-done.4.own_ref = bf16[2,64,3072]{2,1,0:T(8,128)(2,1)} collective-permute-done((bf16[2,64,3072]{2,1,0:T(8,128)(2,1)S(1)}, bf16[2,64,3072]{2,1,0:T(8,128)(2,1)}, u32[]{:S(2)}, u32[]{:S(2)}) %collective-permute-start.4) | collective-permute-done | bytes 786464 | tf_op jit(solution)/shard_map/ppermute | solution.py:121
  130.0 8.5 %cot_product.7 = bf16[256,1920]{1,0:T(8,128)(2,1)S(1)} custom-call(bf16[2,64,3072]{2,1,0:T(8,128)(2,1)S(1)} %collective-permute-done.3.own_ref, bf16[2,64,3072]{2,1,0:T(8,128)(2,1)S(1)} %collective-permute-done.12.other_ref, bf16[384,3072]{1,0:T(8,128)(2,1)S(1)} %copy-done, bf16[1536,3072]{1,0:T(8,128)(2,1)} %refs_1_.11), custom_call_target="tpu_custom_call" | custom-call | flops 47185920 | bytes 199680 | tf_op jit(solution)/shard_map/cot_product/pallas_call | solution.py:214
  139.5 4.6 all-to-all-start.1
  144.2 8.6 %cot_product.5 = bf16[256,1920]{1,0:T(8,128)(2,1)S(1)} custom-call(bf16[2,64,3072]{2,1,0:T(8,128)(2,1)} %collective-permute-done.4.own_ref, bf16[2,64,3072]{2,1,0:T(8,128)(2,1)} %collective-permute-done.8.other_ref, bf16[384,3072]{1,0:T(8,128)(2,1)S(1)} %copy-done, bf16[1536,3072]{1,0:T(8,128)(2,1)} %refs_1_.11), custom_call_target="tpu_custom_call" | custom-call | flops 47185920 | bytes 199680 | tf_op jit(solution)/shard_map/cot_product/pallas_call | solution.py:214
  156.1 17.8 %collective-permute-done.17.refs_6_ = bf16[2,64,3072]{2,1,0:T(8,128)(2,1)S(1)} collective-permute-done((bf16[2,64,3072]{2,1,0:T(8,128)(2,1)}, bf16[2,64,3072]{2,1,0:T(8,128)(2,1)S(1)}, u32[]{:S(2)}, u32[]{:S(2)}) %collective-permute-start.17) | collective-permute-done | bytes 786464 | tf_op jit(solution)/shard_map/ppermute | solution.py:121
  179.9 5.0 %assemble.1.rows_ref = bf16[1024,3072]{1,0:T(8,128)(2,1)} custom-call(bf16[2,64,3072]{2,1,0:T(8,128)(2,1)} %pad_maximum_fusion.refs_0_, bf16[2,64,3072]{2,1,0:T(8,128)(2,1)S(1)} %collective-permute-done.1.refs_1_, bf16[2,64,3072]{2,1,0:T(8,128)(2,1)S(1)} %copy-done.36, bf16[2,64,3072]{2,1,0:T(8,128)(2,1)S(1)} %collective-permute-done.14.refs_3_, ...), custom_call_target="tpu_custom_call" | custom-call | bytes 196608 | tf_op jit(solution)/shard_map/assemble/pallas_call | solution.py:178
  184.9 4.5 all-to-all-start.2
  191.1 6.7 %pack.7 = bf16[4,768,768]{2,1,0:T(8,128)(2,1)S(1)} custom-call(bf16[768,6144]{1,0:T(8,128)(2,1)} %refs_0_.7), custom_call_target="tpu_custom_call" | custom-call | bytes 147456 | tf_op jit(solution)/shard_map/pack/pallas_call | solution.py:148
  199.9 13.7 %collective-permute-done.19 = bf16[256,1920]{1,0:T(8,128)(2,1)S(1)} collective-permute-done((bf16[256,1920]{1,0:T(8,128)(2,1)S(1)}, bf16[256,1920]{1,0:T(8,128)(2,1)S(1)}, u32[]{:S(2)}, u32[]{:S(2)}) %collective-permute-start.19) | collective-permute-done | bytes 983072 | tf_op jit(solution)/shard_map/ppermute | solution.py:121
  214.6 14.0 %in_product.5.q_own.k_own.v_own = bf16[1024,1152]{1,0:T(8,128)(2,1)S(1)} custom-call(bf16[1024,3072]{1,0:T(8,128)(2,1)} %assemble.1.rows_ref, bf16[3072,1152]{1,0:T(8,128)(2,1)} %bitcast.4.weight_ref.refs_5_), custom_call_target="tpu_custom_call" | custom-call | flops 113246208 | bytes 245760 | tf_op jit(solution)/shard_map/in_product/pallas_call | solution.py:268
  230.0 5.1 %all-to-all-start.3 = ((bf16[4,768,768]{2,1,0:T(8,128)(2,1)}), bf16[4,768,768]{2,1,0:T(8,128)(2,1)}, u32[]{:S(2)}, u32[]{:S(2)}) async-start(bf16[4,768,768]{2,1,0:T(8,128)(2,1)} %copy-done.6), calls=%async_computation.3 | async-start | bytes 9437184 | tf_op jit(solution)/shard_map/all_to_all | solution.py:359
  236.7 6.9 %in_product.6 = bf16[1024,512]{1,0:T(8,128)(2,1)S(1)} custom-call(bf16[1024,3072]{1,0:T(8,128)(2,1)} %assemble.1.rows_ref, bf16[3072,512]{1,0:T(8,128)(2,1)} %bitcast.5.weight_ref.refs_6_), custom_call_target="tpu_custom_call" | custom-call | flops 50331648 | bytes 163840 | tf_op jit(solution)/shard_map/in_product/pallas_call | solution.py:268
  244.2 6.1 %in_product.9 = bf16[1024,256]{1,0:T(8,128)(2,1)} custom-call(bf16[1024,3072]{1,0:T(8,128)(2,1)} %assemble.1.rows_ref, bf16[3072,256]{1,0:T(8,128)(2,1)} %bitcast.6.weight_ref.refs_7_), custom_call_target="tpu_custom_call" | custom-call | flops 25165824 | bytes 131072 | tf_op jit(solution)/shard_map/in_product/pallas_call | solution.py:268
  251.7 4.6 add_parts.1
  256.3 33.2 %collective-permute-done.20.q_got.k_got.v_got = bf16[1024,1152]{1,0:T(8,128)(2,1)S(1)} collective-permute-done((bf16[1024,1152]{1,0:T(8,128)(2,1)}, bf16[1024,1152]{1,0:T(8,128)(2,1)S(1)}, u32[]{:S(2)}, u32[]{:S(2)}) %collective-permute-start.20) | collective-permute-done | bytes 2359328 | tf_op jit(solution)/shard_map/ppermute | solution.py:121
  290.9 6.4 %in_product.7 = bf16[512,768]{1,0:T(8,128)(2,1)S(1)} custom-call(bf16[1024,3072]{1,0:T(8,128)(2,1)} %assemble.1.rows_ref, bf16[3072,768]{1,0:T(8,128)(2,1)} %bitcast.16.weight_ref.refs_1_), custom_call_target="tpu_custom_call" | custom-call | flops 37748736 | bytes 184320 | tf_op jit(solution)/shard_map/in_product/pallas_call | solution.py:268
  300.5 14.9 %attend.1 = (bf16[1024,384]{1,0:T(8,128)(2,1)S(1)}, bf16[1024,384]{1,0:T(8,128)(2,1)S(1)}, bf16[1024,384]{1,0:T(8,128)(2,1)S(1)}, bf16[1024,384]{1,0:T(8,128)(2,1)S(1)}) custom-call(bf16[1024,1152]{1,0:T(8,128)(2,1)S(1)} %copy-done.2, bf16[1024,1152]{1,0:T(8,128)(2,1)S(1)} %copy-done.5, bf16[1024,1152]{1,0:T(8,128)(2,1)S(1)} %copy-done.2, ...), custom_call_target="tpu_custom_call" | custom-call | flops 12582912 | bytes 98304 | tf_op jit(solution)/shard_map/attend/pallas_call | solution.py:75
  318.1 5.2 %collective-permute-done.22 = bf16[1024,256]{1,0:T(8,128)(2,1)} collective-permute-done((bf16[1024,256]{1,0:T(8,128)(2,1)}, bf16[1024,256]{1,0:T(8,128)(2,1)}, u32[]{:S(2)}, u32[]{:S(2)}) %collective-permute-start.22) | collective-permute-done | bytes 524320 | tf_op jit(solution)/shard_map/ppermute | solution.py:121
  325.1 6.3 %in_product.8 = bf16[512,768]{1,0:T(8,128)(2,1)S(1)} custom-call(bf16[1024,3072]{1,0:T(8,128)(2,1)} %assemble.1.rows_ref, bf16[3072,768]{1,0:T(8,128)(2,1)} %bitcast.16.weight_ref.refs_1_), custom_call_target="tpu_custom_call" | custom-call | flops 37748736 | bytes 184320 | tf_op jit(solution)/shard_map/in_product/pallas_call | solution.py:268
  333.0 2.5 fusion.5
  335.6 18.5 %back_product.5.refs_2_ = bf16[1024,3072]{1,0:T(8,128)(2,1)} custom-call(bf16[1024,384]{1,0:T(8,128)(2,1)S(1)} %copy-done.30, bf16[1024,384]{1,0:T(8,128)(2,1)S(1)} %copy-done.32, bf16[1024,384]{1,0:T(8,128)(2,1)S(1)} %copy-done.34, bf16[1024,512]{1,0:T(8,128)(2,1)S(1)} %get-tuple-element.68.refs_3_, bf16[1024,256]{1,0:T(8,128)(2,1)S(1)} %get-tuple-element.76.refs_4_, ...), custom_call_target="tpu_custom_call" | custom-call | flops 188743680 | bytes 282624 | tf_op jit(solution)/shard_map/back_product/pallas_call | solution.py:321
  354.1 12.3 %out_product.6.refs_2_ = bf16[1024,3072]{1,0:T(8,128)(2,1)} custom-call(bf16[1024,384]{1,0:T(8,128)(2,1)S(1)} %copy-done.28, bf16[1024,512]{1,0:T(8,128)(2,1)S(1)} %get-tuple-element.69.refs_1_, bf16[1024,256]{1,0:T(8,128)(2,1)S(1)} %get-tuple-element.77.refs_2_, bf16[384,3072]{1,0:T(8,128)(2,1)S(1)} %copy-done, bf16[1536,3072]{1,0:T(8,128)(2,1)} %refs_1_.11), custom_call_target="tpu_custom_call" | custom-call | flops 113246208 | bytes 282624 | tf_op jit(solution)/shard_map/out_product/pallas_call | solution.py:321
  368.4 7.6 %out_product.7 = bf16[512,3072]{1,0:T(8,128)(2,1)} custom-call(bf16[512,768]{1,0:T(8,128)(2,1)S(1)} %get-tuple-element.75.refs_0_, bf16[1536,3072]{1,0:T(8,128)(2,1)} %refs_1_.11, bf16[1024,3072]{1,0:T(8,128)(2,1)} %out_product.6.refs_2_), custom_call_target="tpu_custom_call" | custom-call | flops 37748736 | bytes 196608 | tf_op jit(solution)/shard_map/out_product/pallas_call | solution.py:321
  376.1 6.9 %back_product.6 = bf16[512,3072]{1,0:T(8,128)(2,1)S(1)} custom-call(bf16[512,768]{1,0:T(8,128)(2,1)S(1)} %get-tuple-element.56.refs_0_, bf16[3072,768]{1,0:T(8,128)(2,1)} %bitcast.16.weight_ref.refs_1_, bf16[1024,3072]{1,0:T(8,128)(2,1)} %back_product.5.refs_2_), custom_call_target="tpu_custom_call" | custom-call | flops 37748736 | bytes 122880 | tf_op jit(solution)/shard_map/back_product/pallas_call | solution.py:321
  385.7 3.2 out_product.9
  390.7 3.2 out_product.11
  394.3 3.9 back_product.9
  400.1 3.3 back_product.8
  405.2 3.2 out_product.10
  408.4 3.2 out_product.8
  411.7 3.3 back_product.7
  416.8 9.5 %collective-permute-done.29 = bf16[256,1536]{1,0:T(8,128)(2,1)S(1)} collective-permute-done((bf16[256,1536]{1,0:T(8,128)(2,1)S(1)}, bf16[256,1536]{1,0:T(8,128)(2,1)S(1)}, u32[]{:S(2)}, u32[]{:S(2)}) %collective-permute-start.29) | collective-permute-done | bytes 786464 | tf_op jit(solution)/shard_map/ppermute | solution.py:121
  428.6 13.5 %collective-permute-done.33 = bf16[256,1536]{1,0:T(8,128)(2,1)S(1)} collective-permute-done((bf16[256,1536]{1,0:T(8,128)(2,1)S(1)}, bf16[256,1536]{1,0:T(8,128)(2,1)S(1)}, u32[]{:S(2)}, u32[]{:S(2)}) %collective-permute-start.33) | collective-permute-done | bytes 786464 | tf_op jit(solution)/shard_map/ppermute | solution.py:121
  444.5 3.0 collective-permute-start.31
  449.4 11.7 %collective-permute-done.34 = bf16[2,64,1536]{2,1,0:T(8,128)(2,1)S(1)} collective-permute-done((bf16[2,64,1536]{2,1,0:T(8,128)(2,1)S(1)}, bf16[2,64,1536]{2,1,0:T(8,128)(2,1)S(1)}, u32[]{:S(2)}, u32[]{:S(2)}) %collective-permute-start.34) | collective-permute-done | bytes 393248 | tf_op jit(solution)/shard_map/ppermute | solution.py:121
  461.5 10.8 %collective-permute-done.35 = bf16[64,1536]{1,0:T(8,128)(2,1)S(1)} collective-permute-done((bf16[64,1536]{1,0:T(8,128)(2,1)S(1)}, bf16[64,1536]{1,0:T(8,128)(2,1)S(1)}, u32[]{:S(2)}, u32[]{:S(2)}) %collective-permute-start.35) | collective-permute-done | bytes 196640 | tf_op jit(solution)/shard_map/ppermute | solution.py:121
  473.3 5.6 %all-reduce = (f32[64]{0:T(128)S(1)}, f32[64]{0:T(128)}) all-reduce(f32[64]{0:T(128)S(1)} %fusion.28, f32[64]{0:T(128)} %reduce_sum.48), channel_id=1, replica_groups=mesh['gx'=4,'gy'=4,'gz'=2] {'gz'}, use_global_device_ids=true, to_apply=%region_8.9 | all-reduce | flops 128 | bytes 1024 | tf_op jit(solution)/shard_map/psum | solution.py:489
  (191 shorter events, 73.3 us)
Async XLA Ops:
  0.6 19.0 %collective-permute-start.2 = (bf16[64,3072]{1,0:T(8,128)(2,1)}, bf16[64,3072]{1,0:T(8,128)(2,1)S(1)}, u32[]{:S(2)}, u32[]{:S(2)}) collective-permute-start(bf16[64,3072]{1,0:T(8,128)(2,1)} %param.9), channel_id=1, source_target_pairs={{0,16},{8,24},{16,0},{24,8},{1,17},{9,25},{17,1},{25,9},{2,18},{10... | collective-permute-start | bytes 1179656 | tf_op jit(solution)/shard_map/ppermute | solution.py:121
  10.9 10.4 %collective-permute-start = (bf16[64,3072]{1,0:T(8,128)(2,1)S(1)}, bf16[64,3072]{1,0:T(8,128)(2,1)S(1)}, u32[]{:S(2)}, u32[]{:S(2)}) collective-permute-start(bf16[64,3072]{1,0:T(8,128)(2,1)S(1)} %fusion.27), channel_id=1, source_target_pairs={{0,16},{8,24},{16,0},{24,8},{1,17},{9,25},{17,1},{25,9},{2,18},{10... | collective-permute-start | bytes 1179656 | tf_op jit(solution)/shard_map/ppermute | solution.py:121
  19.7 2.6 collective-permute-start.9
  30.5 28.4 %copy-start.9 = (bf16[256,1920]{1,0:T(8,128)(2,1)}, bf16[256,1920]{1,0:T(8,128)(2,1)S(1)}, u32[]{:S(2)}) copy-start(bf16[256,1920]{1,0:T(8,128)(2,1)S(1)} %cot_product.6) | copy-start | bytes 2949124
  30.5 109.0 %all-to-all-start = ((bf16[4,768,1152]{2,1,0:T(8,128)(2,1)}), bf16[4,768,1152]{2,1,0:T(8,128)(2,1)}, u32[]{:S(2)}, u32[]{:S(2)}) async-start(bf16[4,768,1152]{2,1,0:T(8,128)(2,1)} %pack.4), calls=%async_computation | async-start | bytes 14155776 | tf_op jit(solution)/shard_map/all_to_all | solution.py:359
  35.9 20.2 %collective-permute-start.5 = (bf16[2,64,3072]{2,1,0:T(8,128)(2,1)}, bf16[2,64,3072]{2,1,0:T(8,128)(2,1)S(1)}, u32[]{:S(2)}, u32[]{:S(2)}) collective-permute-start(bf16[2,64,3072]{2,1,0:T(8,128)(2,1)} %copy-done.18), channel_id=1, source_target_pairs={{0,2},{2,0},{4,6},{6,4},{1,3},{3,1},{5,7},{7,5},{8,10},{10,8},{12,... | collective-permute-start | bytes 2359304 | tf_op jit(solution)/shard_map/ppermute | solution.py:121
  56.1 4.3 collective-permute-start.6
  56.1 38.1 %collective-permute-start.3 = (bf16[2,64,3072]{2,1,0:T(8,128)(2,1)}, bf16[2,64,3072]{2,1,0:T(8,128)(2,1)S(1)}, u32[]{:S(2)}, u32[]{:S(2)}) collective-permute-start(bf16[2,64,3072]{2,1,0:T(8,128)(2,1)} %copy-done.18), channel_id=1, source_target_pairs={{0,4},{2,6},{4,0},{6,2},{1,5},{3,7},{5,1},{7,3},{8,12},{10,14},{12... | collective-permute-start | bytes 2359304 | tf_op jit(solution)/shard_map/ppermute | solution.py:121
  58.9 71.1 %collective-permute-start.10 = (bf16[256,1920]{1,0:T(8,128)(2,1)S(1)}, bf16[256,1920]{1,0:T(8,128)(2,1)S(1)}, u32[]{:S(2)}, u32[]{:S(2)}) collective-permute-start(bf16[256,1920]{1,0:T(8,128)(2,1)S(1)} %cot_product.6), channel_id=1, source_target_pairs={{0,1},{1,0},{2,3},{3,2},{4,5},{5,4},{6,7},{7,6},{8,9},{9,8},{10,11... | collective-permute-start | bytes 2949128 | tf_op jit(solution)/shard_map/ppermute | solution.py:121
  68.6 31.0 %copy-start.11 = (bf16[256,1920]{1,0:T(8,128)(2,1)}, bf16[256,1920]{1,0:T(8,128)(2,1)S(1)}, u32[]{:S(2)}) copy-start(bf16[256,1920]{1,0:T(8,128)(2,1)S(1)} %cot_product.4) | copy-start | bytes 2949124
  68.6 70.0 %collective-permute-start.7 = (bf16[256,1920]{1,0:T(8,128)(2,1)S(1)}, bf16[256,1920]{1,0:T(8,128)(2,1)S(1)}, u32[]{:S(2)}, u32[]{:S(2)}) collective-permute-start(bf16[256,1920]{1,0:T(8,128)(2,1)S(1)} %cot_product.4), channel_id=1, source_target_pairs={{0,1},{1,0},{2,3},{3,2},{4,5},{5,4},{6,7},{7,6},{8,9},{9,8},{10,11... | collective-permute-start | bytes 2949128 | tf_op jit(solution)/shard_map/ppermute | solution.py:121
  69.1 36.3 %collective-permute-start.11 = (bf16[2,64,3072]{2,1,0:T(8,128)(2,1)}, bf16[2,64,3072]{2,1,0:T(8,128)(2,1)S(1)}, u32[]{:S(2)}, u32[]{:S(2)}) collective-permute-start(bf16[2,64,3072]{2,1,0:T(8,128)(2,1)} %pad_maximum_fusion.refs_0_), channel_id=1, source_target_pairs={{0,2},{2,0},{4,6},{6,4},{1,3},{3,1},{5,7},{7,5},{8,10},{10,8},{12,... | collective-permute-start | bytes 2359304 | tf_op jit(solution)/shard_map/ppermute | solution.py:121
  94.3 35.7 %collective-permute-start.4 = (bf16[2,64,3072]{2,1,0:T(8,128)(2,1)S(1)}, bf16[2,64,3072]{2,1,0:T(8,128)(2,1)}, u32[]{:S(2)}, u32[]{:S(2)}) collective-permute-start(bf16[2,64,3072]{2,1,0:T(8,128)(2,1)S(1)} %collective-permute-done.3.own_ref), channel_id=1, source_target_pairs={{0,2},{2,0},{4,6},{6,4},{1,3},{3,1},{5,7},{7,5},{8,10},{10,8},{12,... | collective-permute-start | bytes 2359304 | tf_op jit(solution)/shard_map/ppermute | solution.py:121
  95.0 34.9 %collective-permute-start.12 = (bf16[2,64,3072]{2,1,0:T(8,128)(2,1)S(1)}, bf16[2,64,3072]{2,1,0:T(8,128)(2,1)S(1)}, u32[]{:S(2)}, u32[]{:S(2)}) collective-permute-start(bf16[2,64,3072]{2,1,0:T(8,128)(2,1)S(1)} %collective-permute-done.3.own_ref), channel_id=1, source_target_pairs={{0,8},{8,0},{16,24},{24,16},{1,9},{9,1},{17,25},{25,17},{2,10},{10... | collective-permute-start | bytes 2359304 | tf_op jit(solution)/shard_map/ppermute | solution.py:121
  105.5 33.0 %copy-start.35 = (bf16[2,64,3072]{2,1,0:T(8,128)(2,1)}, bf16[2,64,3072]{2,1,0:T(8,128)(2,1)S(1)}, u32[]{:S(2)}) copy-start(bf16[2,64,3072]{2,1,0:T(8,128)(2,1)S(1)} %collective-permute-done.11.refs_2_) | copy-start | bytes 2359300
  105.5 48.3 %collective-permute-start.15 = (bf16[2,64,3072]{2,1,0:T(8,128)(2,1)}, bf16[2,64,3072]{2,1,0:T(8,128)(2,1)}, u32[]{:S(2)}, u32[]{:S(2)}) collective-permute-start(bf16[2,64,3072]{2,1,0:T(8,128)(2,1)} %pad_maximum_fusion.refs_0_), channel_id=1, source_target_pairs={{0,4},{2,6},{4,0},{6,2},{1,5},{3,7},{5,1},{7,3},{8,12},{10,14},{12... | collective-permute-start | bytes 2359304 | tf_op jit(solution)/shard_map/ppermute | solution.py:121
  130.0 14.2 %collective-permute-start.8 = (bf16[2,64,3072]{2,1,0:T(8,128)(2,1)}, bf16[2,64,3072]{2,1,0:T(8,128)(2,1)}, u32[]{:S(2)}, u32[]{:S(2)}) collective-permute-start(bf16[2,64,3072]{2,1,0:T(8,128)(2,1)} %collective-permute-done.4.own_ref), channel_id=1, source_target_pairs={{0,8},{8,0},{16,24},{24,16},{1,9},{9,1},{17,25},{25,17},{2,10},{10... | collective-permute-start | bytes 2359304 | tf_op jit(solution)/shard_map/ppermute | solution.py:121
  138.5 15.3 %copy-start.13 = (bf16[256,1920]{1,0:T(8,128)(2,1)}, bf16[256,1920]{1,0:T(8,128)(2,1)S(1)}, u32[]{:S(2)}) copy-start(bf16[256,1920]{1,0:T(8,128)(2,1)S(1)} %cot_product.7) | copy-start | bytes 2949124
  139.5 45.4 %all-to-all-start.1 = ((bf16[4,768,512]{2,1,0:T(8,128)(2,1)}), bf16[4,768,512]{2,1,0:T(8,128)(2,1)}, u32[]{:S(2)}, u32[]{:S(2)}) async-start(bf16[4,768,512]{2,1,0:T(8,128)(2,1)} %copy-done.7), calls=%async_computation.1 | async-start | bytes 6291456 | tf_op jit(solution)/shard_map/all_to_all | solution.py:359
  153.8 20.2 %collective-permute-start.17 = (bf16[2,64,3072]{2,1,0:T(8,128)(2,1)}, bf16[2,64,3072]{2,1,0:T(8,128)(2,1)S(1)}, u32[]{:S(2)}, u32[]{:S(2)}) collective-permute-start(bf16[2,64,3072]{2,1,0:T(8,128)(2,1)} %collective-permute-done.15.refs_4_), channel_id=1, source_target_pairs={{0,2},{2,0},{4,6},{6,4},{1,3},{3,1},{5,7},{7,5},{8,10},{10,8},{12,... | collective-permute-start | bytes 2359304 | tf_op jit(solution)/shard_map/ppermute | solution.py:121
  153.8 24.3 %collective-permute-start.13 = (bf16[256,1920]{1,0:T(8,128)(2,1)S(1)}, bf16[256,1920]{1,0:T(8,128)(2,1)S(1)}, u32[]{:S(2)}, u32[]{:S(2)}) collective-permute-start(bf16[256,1920]{1,0:T(8,128)(2,1)S(1)} %cot_product.7), channel_id=1, source_target_pairs={{0,1},{1,0},{2,3},{3,2},{4,5},{5,4},{6,7},{7,6},{8,9},{9,8},{10,11... | collective-permute-start | bytes 2949128 | tf_op jit(solution)/shard_map/ppermute | solution.py:121
  155.4 22.0 %collective-permute-start.1 = (bf16[2,64,3072]{2,1,0:T(8,128)(2,1)}, bf16[2,64,3072]{2,1,0:T(8,128)(2,1)S(1)}, u32[]{:S(2)}, u32[]{:S(2)}) collective-permute-start(bf16[2,64,3072]{2,1,0:T(8,128)(2,1)} %pad_maximum_fusion.refs_0_), channel_id=1, source_target_pairs={{0,8},{8,0},{16,24},{24,16},{1,9},{9,1},{17,25},{25,17},{2,10},{10... | collective-permute-start | bytes 2359304 | tf_op jit(solution)/shard_map/ppermute | solution.py:121
  155.6 22.4 %collective-permute-start.16 = (bf16[2,64,3072]{2,1,0:T(8,128)(2,1)}, bf16[2,64,3072]{2,1,0:T(8,128)(2,1)S(1)}, u32[]{:S(2)}, u32[]{:S(2)}) collective-permute-start(bf16[2,64,3072]{2,1,0:T(8,128)(2,1)} %collective-permute-done.15.refs_4_), channel_id=1, source_target_pairs={{0,8},{8,0},{16,24},{24,16},{1,9},{9,1},{17,25},{25,17},{2,10},{10... | collective-permute-start | bytes 2359304 | tf_op jit(solution)/shard_map/ppermute | solution.py:121
  155.9 22.2 %collective-permute-start.14 = (bf16[2,64,3072]{2,1,0:T(8,128)(2,1)S(1)}, bf16[2,64,3072]{2,1,0:T(8,128)(2,1)S(1)}, u32[]{:S(2)}, u32[]{:S(2)}) collective-permute-start(bf16[2,64,3072]{2,1,0:T(8,128)(2,1)S(1)} %copy-done.36), channel_id=1, source_target_pairs={{0,8},{8,0},{16,24},{24,16},{1,9},{9,1},{17,25},{25,17},{2,10},{10... | collective-permute-start | bytes 2359304 | tf_op jit(solution)/shard_map/ppermute | solution.py:121
  174.0 5.1 %collective-permute-start.18 = (bf16[2,64,3072]{2,1,0:T(8,128)(2,1)S(1)}, bf16[2,64,3072]{2,1,0:T(8,128)(2,1)S(1)}, u32[]{:S(2)}, u32[]{:S(2)}) collective-permute-start(bf16[2,64,3072]{2,1,0:T(8,128)(2,1)S(1)} %collective-permute-done.17.refs_6_), channel_id=1, source_target_pairs={{0,8},{8,0},{16,24},{24,16},{1,9},{9,1},{17,25},{25,17},{2,10},{10... | collective-permute-start | bytes 2359304 | tf_op jit(solution)/shard_map/ppermute | solution.py:121
  184.9 45.0 %all-to-all-start.2 = ((bf16[4,768,256]{2,1,0:T(8,128)(2,1)}), bf16[4,768,256]{2,1,0:T(8,128)(2,1)}, u32[]{:S(2)}, u32[]{:S(2)}) async-start(bf16[4,768,256]{2,1,0:T(8,128)(2,1)} %copy-done.8), calls=%async_computation.2 | async-start | bytes 3145728 | tf_op jit(solution)/shard_map/all_to_all | solution.py:359
  189.5 24.1 %collective-permute-start.19 = (bf16[256,1920]{1,0:T(8,128)(2,1)S(1)}, bf16[256,1920]{1,0:T(8,128)(2,1)S(1)}, u32[]{:S(2)}, u32[]{:S(2)}) collective-permute-start(bf16[256,1920]{1,0:T(8,128)(2,1)S(1)} %copy-done.16), channel_id=1, source_target_pairs={{0,1},{1,0},{2,3},{3,2},{4,5},{5,4},{6,7},{7,6},{8,9},{9,8},{10,11... | collective-permute-start | bytes 2949128 | tf_op jit(solution)/shard_map/ppermute | solution.py:121
  230.0 60.9 %all-to-all-start.3 = ((bf16[4,768,768]{2,1,0:T(8,128)(2,1)}), bf16[4,768,768]{2,1,0:T(8,128)(2,1)}, u32[]{:S(2)}, u32[]{:S(2)}) async-start(bf16[4,768,768]{2,1,0:T(8,128)(2,1)} %copy-done.6), calls=%async_computation.3 | async-start | bytes 9437184 | tf_op jit(solution)/shard_map/all_to_all | solution.py:359
  235.1 54.4 %collective-permute-start.20 = (bf16[1024,1152]{1,0:T(8,128)(2,1)}, bf16[1024,1152]{1,0:T(8,128)(2,1)S(1)}, u32[]{:S(2)}, u32[]{:S(2)}) collective-permute-start(bf16[1024,1152]{1,0:T(8,128)(2,1)} %copy-done.1), channel_id=1, source_target_pairs={{0,1},{1,0},{2,3},{3,2},{4,5},{5,4},{6,7},{7,6},{8,9},{9,8},{10,11... | collective-permute-start | bytes 7077896 | tf_op jit(solution)/shard_map/ppermute | solution.py:121
  243.7 89.3 %collective-permute-start.21 = (bf16[1024,512]{1,0:T(8,128)(2,1)S(1)}, bf16[1024,512]{1,0:T(8,128)(2,1)}, u32[]{:S(2)}, u32[]{:S(2)}) collective-permute-start(bf16[1024,512]{1,0:T(8,128)(2,1)S(1)} %in_product.6), channel_id=1, source_target_pairs={{0,1},{1,0},{2,3},{3,2},{4,5},{5,4},{6,7},{7,6},{8,9},{9,8},{10,11... | collective-permute-start | bytes 3145736 | tf_op jit(solution)/shard_map/ppermute | solution.py:121
  250.4 72.9 %collective-permute-start.22 = (bf16[1024,256]{1,0:T(8,128)(2,1)}, bf16[1024,256]{1,0:T(8,128)(2,1)}, u32[]{:S(2)}, u32[]{:S(2)}) collective-permute-start(bf16[1024,256]{1,0:T(8,128)(2,1)} %in_product.9), channel_id=1, source_target_pairs={{0,1},{1,0},{2,3},{3,2},{4,5},{5,4},{6,7},{7,6},{8,9},{9,8},{10,11... | collective-permute-start | bytes 1572872 | tf_op jit(solution)/shard_map/ppermute | solution.py:121
  297.3 69.0 %collective-permute-start.23 = (bf16[512,768]{1,0:T(8,128)(2,1)S(1)}, bf16[512,768]{1,0:T(8,128)(2,1)}, u32[]{:S(2)}, u32[]{:S(2)}) collective-permute-start(bf16[512,768]{1,0:T(8,128)(2,1)S(1)} %in_product.7), channel_id=1, source_target_pairs={{0,1},{1,0},{2,3},{3,2},{4,5},{5,4},{6,7},{7,6},{8,9},{9,8},{10,11... | collective-permute-start | bytes 2359304 | tf_op jit(solution)/shard_map/ppermute | solution.py:121
  331.4 44.6 %collective-permute-start.24 = (bf16[512,768]{1,0:T(8,128)(2,1)S(1)}, bf16[512,768]{1,0:T(8,128)(2,1)}, u32[]{:S(2)}, u32[]{:S(2)}) collective-permute-start(bf16[512,768]{1,0:T(8,128)(2,1)S(1)} %in_product.8), channel_id=1, source_target_pairs={{0,1},{1,0},{2,3},{3,2},{4,5},{5,4},{6,7},{7,6},{8,9},{9,8},{10,11... | collective-permute-start | bytes 2359304 | tf_op jit(solution)/shard_map/ppermute | solution.py:121
  335.5 18.5 %copy-start.28 = (bf16[1024,384]{1,0:T(8,128)(2,1)S(1)}, bf16[1024,384]{1,0:T(8,128)(2,1)}, u32[]{:S(2)}) copy-start(bf16[1024,384]{1,0:T(8,128)(2,1)} %copy-done.27) | copy-start | bytes 2359300
  376.1 9.6 %collective-permute-start.25 = (bf16[512,3072]{1,0:T(8,128)(2,1)}, bf16[512,3072]{1,0:T(8,128)(2,1)S(1)}, u32[]{:S(2)}, u32[]{:S(2)}) collective-permute-start(bf16[512,3072]{1,0:T(8,128)(2,1)} %out_product.7), channel_id=1, source_target_pairs={{0,8},{8,0},{16,24},{24,16},{1,9},{9,1},{17,25},{25,17},{2,10},{10... | collective-permute-start | bytes 9437192 | tf_op jit(solution)/shard_map/ppermute | solution.py:121
  383.0 11.3 %collective-permute-start.32 = (bf16[512,3072]{1,0:T(8,128)(2,1)S(1)}, bf16[512,3072]{1,0:T(8,128)(2,1)S(1)}, u32[]{:S(2)}, u32[]{:S(2)}) collective-permute-start(bf16[512,3072]{1,0:T(8,128)(2,1)S(1)} %back_product.6), channel_id=1, source_target_pairs={{0,8},{8,0},{16,24},{24,16},{1,9},{9,1},{17,25},{25,17},{2,10},{10... | collective-permute-start | bytes 9437192 | tf_op jit(solution)/shard_map/ppermute | solution.py:121
  388.9 26.0 %collective-permute-start.26 = (bf16[256,1536]{1,0:T(8,128)(2,1)S(1)}, bf16[256,1536]{1,0:T(8,128)(2,1)}, u32[]{:S(2)}, u32[]{:S(2)}) collective-permute-start(bf16[256,1536]{1,0:T(8,128)(2,1)S(1)} %out_product.9), channel_id=1, source_target_pairs={{0,16},{8,24},{16,0},{24,8},{1,17},{9,25},{17,1},{25,9},{2,18},{10... | collective-permute-start | bytes 2359304 | tf_op jit(solution)/shard_map/ppermute | solution.py:121
  393.9 32.3 %collective-permute-start.29 = (bf16[256,1536]{1,0:T(8,128)(2,1)S(1)}, bf16[256,1536]{1,0:T(8,128)(2,1)S(1)}, u32[]{:S(2)}, u32[]{:S(2)}) collective-permute-start(bf16[256,1536]{1,0:T(8,128)(2,1)S(1)} %out_product.11), channel_id=1, source_target_pairs={{0,16},{8,24},{16,0},{24,8},{1,17},{9,25},{17,1},{25,9},{2,18},{10... | collective-permute-start | bytes 2359304 | tf_op jit(solution)/shard_map/ppermute | solution.py:121
  398.4 29.9 %collective-permute-start.36 = (bf16[2,2,64,1536]{3,2,0,1:T(8,128)(2,1)S(1)}, bf16[2,2,64,1536]{3,2,0,1:T(8,128)(2,1)S(1)}, u32[]{:S(2)}, u32[]{:S(2)}) collective-permute-start(bf16[2,2,64,1536]{3,2,0,1:T(8,128)(2,1)S(1)} %bitcast.101), channel_id=1, source_target_pairs={{0,2},{2,0},{4,6},{6,4},{1,3},{3,1},{5,7},{7,5},{8,10},{10,8},{12,... | collective-permute-start | bytes 2359304 | tf_op jit(solution)/shard_map/ppermute | solution.py:121
  403.4 38.7 %collective-permute-start.33 = (bf16[256,1536]{1,0:T(8,128)(2,1)S(1)}, bf16[256,1536]{1,0:T(8,128)(2,1)S(1)}, u32[]{:S(2)}, u32[]{:S(2)}) collective-permute-start(bf16[256,1536]{1,0:T(8,128)(2,1)S(1)} %back_product.8), channel_id=1, source_target_pairs={{0,16},{8,24},{16,0},{24,8},{1,17},{9,25},{17,1},{25,9},{2,18},{10... | collective-permute-start | bytes 2359304 | tf_op jit(solution)/shard_map/ppermute | solution.py:121
  416.4 27.8 %collective-permute-start.27 = (bf16[2,64,1536]{2,1,0:T(8,128)(2,1)S(1)}, bf16[2,64,1536]{2,1,0:T(8,128)(2,1)S(1)}, u32[]{:S(2)}, u32[]{:S(2)}) collective-permute-start(bf16[2,64,1536]{2,1,0:T(8,128)(2,1)S(1)} %fusion.40), channel_id=1, source_target_pairs={{0,2},{2,0},{4,6},{6,4},{1,3},{3,1},{5,7},{7,5},{8,10},{10,8},{12,... | collective-permute-start | bytes 1179656 | tf_op jit(solution)/shard_map/ppermute | solution.py:121
  426.5 17.9 %collective-permute-start.30 = (bf16[2,64,1536]{2,1,0:T(8,128)(2,1)S(1)}, bf16[2,64,1536]{2,1,0:T(8,128)(2,1)S(1)}, u32[]{:S(2)}, u32[]{:S(2)}) collective-permute-start(bf16[2,64,1536]{2,1,0:T(8,128)(2,1)S(1)} %fusion.41), channel_id=1, source_target_pairs={{0,2},{2,0},{4,6},{6,4},{1,3},{3,1},{5,7},{7,5},{8,10},{10,8},{12,... | collective-permute-start | bytes 1179656 | tf_op jit(solution)/shard_map/ppermute | solution.py:121
  428.5 18.9 %collective-permute-start.37 = (bf16[2,64,1536]{2,1,0:T(8,128)(2,1)S(1)}, bf16[2,64,1536]{2,1,0:T(8,128)(2,1)S(1)}, u32[]{:S(2)}, u32[]{:S(2)}) collective-permute-start(bf16[2,64,1536]{2,1,0:T(8,128)(2,1)S(1)} %fusion.39), channel_id=1, source_target_pairs={{0,4},{2,6},{4,0},{6,2},{1,5},{3,7},{5,1},{7,3},{8,12},{10,14},{12... | collective-permute-start | bytes 1179656 | tf_op jit(solution)/shard_map/ppermute | solution.py:121
  442.4 18.7 %collective-permute-start.34 = (bf16[2,64,1536]{2,1,0:T(8,128)(2,1)S(1)}, bf16[2,64,1536]{2,1,0:T(8,128)(2,1)S(1)}, u32[]{:S(2)}, u32[]{:S(2)}) collective-permute-start(bf16[2,64,1536]{2,1,0:T(8,128)(2,1)S(1)} %fusion.42), channel_id=1, source_target_pairs={{0,2},{2,0},{4,6},{6,4},{1,3},{3,1},{5,7},{7,5},{8,10},{10,8},{12,... | collective-permute-start | bytes 1179656 | tf_op jit(solution)/shard_map/ppermute | solution.py:121
  444.3 34.5 %collective-permute-start.28 = (bf16[64,1536]{1,0:T(8,128)(2,1)S(1)}, bf16[64,1536]{1,0:T(8,128)(2,1)}, u32[]{:S(2)}, u32[]{:S(2)}) collective-permute-start(bf16[64,1536]{1,0:T(8,128)(2,1)S(1)} %fusion.47), channel_id=1, source_target_pairs={{0,4},{2,6},{4,0},{6,2},{1,5},{3,7},{5,1},{7,3},{8,12},{10,14},{12... | collective-permute-start | bytes 589832 | tf_op jit(solution)/shard_map/ppermute | solution.py:121
  444.5 36.0 %collective-permute-start.31 = (bf16[64,1536]{1,0:T(8,128)(2,1)S(1)}, bf16[64,1536]{1,0:T(8,128)(2,1)}, u32[]{:S(2)}, u32[]{:S(2)}) collective-permute-start(bf16[64,1536]{1,0:T(8,128)(2,1)S(1)} %fusion.48), channel_id=1, source_target_pairs={{0,4},{2,6},{4,0},{6,2},{1,5},{3,7},{5,1},{7,3},{8,12},{10,14},{12... | collective-permute-start | bytes 589832 | tf_op jit(solution)/shard_map/ppermute | solution.py:121
  447.6 13.8 %collective-permute-start.38 = (bf16[64,1536]{1,0:T(8,128)(2,1)S(1)}, bf16[64,1536]{1,0:T(8,128)(2,1)S(1)}, u32[]{:S(2)}, u32[]{:S(2)}) collective-permute-start(bf16[64,1536]{1,0:T(8,128)(2,1)S(1)} %fusion.50), channel_id=1, source_target_pairs={{0,16},{8,24},{16,0},{24,8},{1,17},{9,25},{17,1},{25,9},{2,18},{10... | collective-permute-start | bytes 589832 | tf_op jit(solution)/shard_map/ppermute | solution.py:121
  461.2 11.0 %collective-permute-start.35 = (bf16[64,1536]{1,0:T(8,128)(2,1)S(1)}, bf16[64,1536]{1,0:T(8,128)(2,1)S(1)}, u32[]{:S(2)}, u32[]{:S(2)}) collective-permute-start(bf16[64,1536]{1,0:T(8,128)(2,1)S(1)} %fusion.49), channel_id=1, source_target_pairs={{0,4},{2,6},{4,0},{6,2},{1,5},{3,7},{5,1},{7,3},{8,12},{10,14},{12... | collective-permute-start | bytes 589832 | tf_op jit(solution)/shard_map/ppermute | solution.py:121
  (39 other events, 176.8 us)

commit v17 on v14

--- a/solution.py
+++ b/solution.py
@@ -394,7 +394,7 @@
     in_heads = swap(after(packed_heads, normed_pair, cot_owns[0]))
     early = (cot_owns[2], cot_gots[1], cot_parts[3])
     in_mlp = [swap(after(packed_mlp[0], in_heads, *early))]
-    in_mlp.append(swap(after(packed_mlp[1], in_mlp[0], all_in)))
+    in_mlp.append(swap(after(packed_mlp[1], in_mlp[0], all_in, cot_gots[3])))
     heads_own = in_product(after(all_in, cot_gots[3]), in_heads)
     heads_got = others(heads_own)
     mlp_own = [in_product(after(all_in, heads_own, in_mlp[1]), in_mlp[0])]

time: 477 us -> 467 us (0.979)
  waiting for transfers between devices: 174 us -> 167 us
    ppermute x39, waiting for transfers between devices: 174 us -> 167 us  [trade(): return lax.ppermute(block, axis, pairs)]
    unnamed x93 -> x89, local copies, waits for them, and re-layouts: 21.9 us -> 21.2 us
  transfers between devices with their start and end apart: 43 -> 43, of which waited for: 14 -> 15; matrix products, arithmetic and copies ran while one was open for 4% -> 4% of each run, Pallas kernels for 37% -> 38%
where the time goes in v17:
time: 467 us; the launch traced here: 465 us
  Pallas kernels  184 us (39%)
  waiting for transfers between devices  167 us (36%)
  starting transfers between devices  61.2 us (13%)
  local copies, waits for them, and re-layouts  21.5 us (5%)
  other arithmetic  19.3 us (4%)
  blocking collectives  10.5 us (2%)
    ppermute x39, waiting for transfers between devices, trade(): return lax.ppermute(block, axis, pairs)  167 us
    pallas_call x11, Pallas kernels, product(): pl.pallas_call(kernel, grid=(columns // tile,), in_specs=specs, out_specs...  68.6 us
    ppermute x39, starting transfers between devices, trade(): return lax.ppermute(block, axis, pairs)  41.6 us
    pallas_call x5, Pallas kernels, in_product(): pl.pallas_call(in_kernel, grid=(columns // tile,), in_specs=[pl.BlockSpec...  39.5 us
    pallas_call x4, Pallas kernels, cot_product(): pl.pallas_call(cot_kernel, grid=(columns // tile,), in_specs=[whole, whol...  32.9 us
    unnamed x89, local copies, waits for them, and re-layouts  21.2 us
    all_to_all x4, starting transfers between devices, swap(): lax.all_to_all(packed, 'gx', split_axis=0, concat_axis=0, tiled=True)  19.5 us
    pallas_call x4, Pallas kernels, pack(): pl.pallas_call(pack_kernel, grid=(owners, width // tile), in_specs=[spec]...  18.6 us
  transfers between devices with their start and end apart: 43, of which 15 were waited for; matrix products, arithmetic and copies ran while one was open for 4% of the time, Pallas kernels for 38%

profile of v17, /device:TPU:0, one launch (start us, length us, event | category | flops | bytes accessed | tf_op | source)
XLA Modules:
  0.0 464.7 jit_solution(13066736374286507012)
XLA Ops:
  0.6 3.0 collective-permute-start.2
  4.8 4.9 %all-reduce.1 = (f32[64]{0:T(128)S(1)}, f32[64]{0:T(128)S(1)}) all-reduce(f32[64]{0:T(128)S(1)} %get-tuple-element.59, f32[64]{0:T(128)S(1)} %get-tuple-element.58), channel_id=1, replica_groups=mesh['gx'=4,'gy'=4,'gz'=2] {'gz'}, use_global_device_ids=true, to_apply=%region_3.0 | all-reduce | flops 128 | bytes 1024 | tf_op jit(solution)/shard_map/psum | solution.py:371
  14.4 5.2 %pack.4 = bf16[4,768,1152]{2,1,0:T(8,128)(2,1)} custom-call(bf16[768,1536]{1,0:T(8,128)(2,1)S(1)} %copy-done.20, bf16[768,1536]{1,0:T(8,128)(2,1)S(1)} %copy-done.21, bf16[768,1536]{1,0:T(8,128)(2,1)} %refs_2_.1), custom_call_target="tpu_custom_call" | custom-call | bytes 221184 | tf_op jit(solution)/shard_map/pack/pallas_call | solution.py:148
  22.4 8.2 %cot_product.6 = bf16[256,1920]{1,0:T(8,128)(2,1)S(1)} custom-call(bf16[2,64,3072]{2,1,0:T(8,128)(2,1)S(1)} %pad_maximum_fusion.1.own_ref, bf16[2,64,3072]{2,1,0:T(8,128)(2,1)S(1)} %collective-permute-done.9.other_ref, bf16[384,3072]{1,0:T(8,128)(2,1)S(1)} %copy-done, bf16[1536,3072]{1,0:T(8,128)(2,1)} %refs_1_.11), custom_call_target="tpu_custom_call" | custom-call | flops 47185920 | bytes 199680 | tf_op jit(solution)/shard_map/cot_product/pallas_call | solution.py:214
  30.5 5.4 %all-to-all-start = ((bf16[4,768,1152]{2,1,0:T(8,128)(2,1)}), bf16[4,768,1152]{2,1,0:T(8,128)(2,1)}, u32[]{:S(2)}, u32[]{:S(2)}) async-start(bf16[4,768,1152]{2,1,0:T(8,128)(2,1)} %pack.4), calls=%async_computation | async-start | bytes 14155776 | tf_op jit(solution)/shard_map/all_to_all | solution.py:359
  37.8 18.3 %collective-permute-done.5.own_ref = bf16[2,64,3072]{2,1,0:T(8,128)(2,1)S(1)} collective-permute-done((bf16[2,64,3072]{2,1,0:T(8,128)(2,1)}, bf16[2,64,3072]{2,1,0:T(8,128)(2,1)S(1)}, u32[]{:S(2)}, u32[]{:S(2)}) %collective-permute-start.5) | collective-permute-done | bytes 786464 | tf_op jit(solution)/shard_map/ppermute | solution.py:121
  56.1 2.8 collective-permute-start.3
  60.4 8.1 %cot_product.4 = bf16[256,1920]{1,0:T(8,128)(2,1)S(1)} custom-call(bf16[2,64,3072]{2,1,0:T(8,128)(2,1)S(1)} %collective-permute-done.5.own_ref, bf16[2,64,3072]{2,1,0:T(8,128)(2,1)S(1)} %collective-permute-done.6.other_ref, bf16[384,3072]{1,0:T(8,128)(2,1)S(1)} %copy-done, bf16[1536,3072]{1,0:T(8,128)(2,1)} %refs_1_.11), custom_call_target="tpu_custom_call" | custom-call | flops 47185920 | bytes 199680 | tf_op jit(solution)/shard_map/cot_product/pallas_call | solution.py:214
  70.7 23.5 %collective-permute-done.3.own_ref = bf16[2,64,3072]{2,1,0:T(8,128)(2,1)S(1)} collective-permute-done((bf16[2,64,3072]{2,1,0:T(8,128)(2,1)}, bf16[2,64,3072]{2,1,0:T(8,128)(2,1)S(1)}, u32[]{:S(2)}, u32[]{:S(2)}) %collective-permute-start.3) | collective-permute-done | bytes 786464 | tf_op jit(solution)/shard_map/ppermute | solution.py:121
  95.1 4.5 pack.6
  101.3 4.2 collective-permute-done.11.refs_2_
  107.5 8.5 %cot_product.7 = bf16[256,1920]{1,0:T(8,128)(2,1)S(1)} custom-call(bf16[2,64,3072]{2,1,0:T(8,128)(2,1)S(1)} %collective-permute-done.3.own_ref, bf16[2,64,3072]{2,1,0:T(8,128)(2,1)S(1)} %collective-permute-done.12.other_ref, bf16[384,3072]{1,0:T(8,128)(2,1)S(1)} %copy-done, bf16[1536,3072]{1,0:T(8,128)(2,1)} %refs_1_.11), custom_call_target="tpu_custom_call" | custom-call | flops 47185920 | bytes 199680 | tf_op jit(solution)/shard_map/cot_product/pallas_call | solution.py:214
  116.1 14.3 %collective-permute-done.4.own_ref = bf16[2,64,3072]{2,1,0:T(8,128)(2,1)S(1)} collective-permute-done((bf16[2,64,3072]{2,1,0:T(8,128)(2,1)S(1)}, bf16[2,64,3072]{2,1,0:T(8,128)(2,1)S(1)}, u32[]{:S(2)}, u32[]{:S(2)}) %collective-permute-start.4) | collective-permute-done | bytes 786464 | tf_op jit(solution)/shard_map/ppermute | solution.py:121
  132.2 4.6 all-to-all-start.1
  137.4 3.2 collective-permute-done.15.refs_4_
  143.7 8.1 %cot_product.5 = bf16[256,1920]{1,0:T(8,128)(2,1)S(1)} custom-call(bf16[2,64,3072]{2,1,0:T(8,128)(2,1)S(1)} %copy-done.37, bf16[2,64,3072]{2,1,0:T(8,128)(2,1)S(1)} %collective-permute-done.8.other_ref, bf16[384,3072]{1,0:T(8,128)(2,1)S(1)} %copy-done, bf16[1536,3072]{1,0:T(8,128)(2,1)} %refs_1_.11), custom_call_target="tpu_custom_call" | custom-call | flops 47185920 | bytes 199680 | tf_op jit(solution)/shard_map/cot_product/pallas_call | solution.py:214
  153.9 3.5 collective-permute-done.17.refs_6_
  160.9 5.9 %collective-permute-done.13 = bf16[256,1920]{1,0:T(8,128)(2,1)S(1)} collective-permute-done((bf16[256,1920]{1,0:T(8,128)(2,1)S(1)}, bf16[256,1920]{1,0:T(8,128)(2,1)S(1)}, u32[]{:S(2)}, u32[]{:S(2)}) %collective-permute-start.13) | collective-permute-done | bytes 983072 | tf_op jit(solution)/shard_map/ppermute | solution.py:121
  168.6 5.0 %assemble.1.rows_ref = bf16[1024,3072]{1,0:T(8,128)(2,1)} custom-call(bf16[2,64,3072]{2,1,0:T(8,128)(2,1)} %pad_maximum_fusion.refs_0_, bf16[2,64,3072]{2,1,0:T(8,128)(2,1)S(1)} %collective-permute-done.1.refs_1_, bf16[2,64,3072]{2,1,0:T(8,128)(2,1)S(1)} %copy-done.35, bf16[2,64,3072]{2,1,0:T(8,128)(2,1)S(1)} %collective-permute-done.14.refs_3_, ...), custom_call_target="tpu_custom_call" | custom-call | bytes 196608 | tf_op jit(solution)/shard_map/assemble/pallas_call | solution.py:178
  173.6 10.1 %collective-permute-done.19 = bf16[256,1920]{1,0:T(8,128)(2,1)} collective-permute-done((bf16[256,1920]{1,0:T(8,128)(2,1)S(1)}, bf16[256,1920]{1,0:T(8,128)(2,1)}, u32[]{:S(2)}, u32[]{:S(2)}) %collective-permute-start.19) | collective-permute-done | bytes 983072 | tf_op jit(solution)/shard_map/ppermute | solution.py:121
  183.7 4.4 all-to-all-start.2
  188.1 6.7 %pack.7 = bf16[4,768,768]{2,1,0:T(8,128)(2,1)S(1)} custom-call(bf16[768,6144]{1,0:T(8,128)(2,1)} %refs_0_.7), custom_call_target="tpu_custom_call" | custom-call | bytes 147456 | tf_op jit(solution)/shard_map/pack/pallas_call | solution.py:148
  196.9 14.0 %in_product.5.q_own.k_own.v_own = bf16[1024,1152]{1,0:T(8,128)(2,1)S(1)} custom-call(bf16[1024,3072]{1,0:T(8,128)(2,1)} %assemble.1.rows_ref, bf16[3072,1152]{1,0:T(8,128)(2,1)} %bitcast.4.weight_ref.refs_5_), custom_call_target="tpu_custom_call" | custom-call | flops 113246208 | bytes 245760 | tf_op jit(solution)/shard_map/in_product/pallas_call | solution.py:268
  212.3 5.1 %all-to-all-start.3 = ((bf16[4,768,768]{2,1,0:T(8,128)(2,1)}), bf16[4,768,768]{2,1,0:T(8,128)(2,1)}, u32[]{:S(2)}, u32[]{:S(2)}) async-start(bf16[4,768,768]{2,1,0:T(8,128)(2,1)} %copy-done.6), calls=%async_computation.3 | async-start | bytes 9437184 | tf_op jit(solution)/shard_map/all_to_all | solution.py:359
  218.1 6.9 %in_product.6 = bf16[1024,512]{1,0:T(8,128)(2,1)S(1)} custom-call(bf16[1024,3072]{1,0:T(8,128)(2,1)} %assemble.1.rows_ref, bf16[3072,512]{1,0:T(8,128)(2,1)} %bitcast.5.weight_ref.refs_6_), custom_call_target="tpu_custom_call" | custom-call | flops 50331648 | bytes 163840 | tf_op jit(solution)/shard_map/in_product/pallas_call | solution.py:268
  226.6 6.0 %in_product.9 = bf16[1024,256]{1,0:T(8,128)(2,1)} custom-call(bf16[1024,3072]{1,0:T(8,128)(2,1)} %assemble.1.rows_ref, bf16[3072,256]{1,0:T(8,128)(2,1)} %bitcast.6.weight_ref.refs_7_), custom_call_target="tpu_custom_call" | custom-call | flops 25165824 | bytes 131072 | tf_op jit(solution)/shard_map/in_product/pallas_call | solution.py:268
  233.3 4.6 add_parts.1
  237.9 33.9 %collective-permute-done.20.q_got.k_got.v_got = bf16[1024,1152]{1,0:T(8,128)(2,1)S(1)} collective-permute-done((bf16[1024,1152]{1,0:T(8,128)(2,1)}, bf16[1024,1152]{1,0:T(8,128)(2,1)S(1)}, u32[]{:S(2)}, u32[]{:S(2)}) %collective-permute-start.20) | collective-permute-done | bytes 2359328 | tf_op jit(solution)/shard_map/ppermute | solution.py:121
  273.2 6.4 %in_product.7 = bf16[512,768]{1,0:T(8,128)(2,1)S(1)} custom-call(bf16[1024,3072]{1,0:T(8,128)(2,1)} %assemble.1.rows_ref, bf16[3072,768]{1,0:T(8,128)(2,1)} %bitcast.16.weight_ref.refs_1_), custom_call_target="tpu_custom_call" | custom-call | flops 37748736 | bytes 184320 | tf_op jit(solution)/shard_map/in_product/pallas_call | solution.py:268
  281.9 14.9 %attend.1 = (bf16[1024,384]{1,0:T(8,128)(2,1)S(1)}, bf16[1024,384]{1,0:T(8,128)(2,1)S(1)}, bf16[1024,384]{1,0:T(8,128)(2,1)S(1)}, bf16[1024,384]{1,0:T(8,128)(2,1)S(1)}) custom-call(bf16[1024,1152]{1,0:T(8,128)(2,1)S(1)} %copy-done.2, bf16[1024,1152]{1,0:T(8,128)(2,1)S(1)} %copy-done.5, bf16[1024,1152]{1,0:T(8,128)(2,1)S(1)} %copy-done.2, ...), custom_call_target="tpu_custom_call" | custom-call | flops 12582912 | bytes 98304 | tf_op jit(solution)/shard_map/attend/pallas_call | solution.py:75
  299.4 6.1 %collective-permute-done.22 = bf16[1024,256]{1,0:T(8,128)(2,1)} collective-permute-done((bf16[1024,256]{1,0:T(8,128)(2,1)}, bf16[1024,256]{1,0:T(8,128)(2,1)}, u32[]{:S(2)}, u32[]{:S(2)}) %collective-permute-start.22) | collective-permute-done | bytes 524320 | tf_op jit(solution)/shard_map/ppermute | solution.py:121
  307.4 6.3 %in_product.8 = bf16[512,768]{1,0:T(8,128)(2,1)S(1)} custom-call(bf16[1024,3072]{1,0:T(8,128)(2,1)} %assemble.1.rows_ref, bf16[3072,768]{1,0:T(8,128)(2,1)} %bitcast.16.weight_ref.refs_1_), custom_call_target="tpu_custom_call" | custom-call | flops 37748736 | bytes 184320 | tf_op jit(solution)/shard_map/in_product/pallas_call | solution.py:268
  316.9 18.5 %back_product.5.refs_2_ = bf16[1024,3072]{1,0:T(8,128)(2,1)} custom-call(bf16[1024,384]{1,0:T(8,128)(2,1)S(1)} %copy-done.29, bf16[1024,384]{1,0:T(8,128)(2,1)S(1)} %copy-done.31, bf16[1024,384]{1,0:T(8,128)(2,1)S(1)} %copy-done.33, bf16[1024,512]{1,0:T(8,128)(2,1)S(1)} %get-tuple-element.68.refs_3_, bf16[1024,256]{1,0:T(8,128)(2,1)S(1)} %get-tuple-element.76.refs_4_, ...), custom_call_target="tpu_custom_call" | custom-call | flops 188743680 | bytes 282624 | tf_op jit(solution)/shard_map/back_product/pallas_call | solution.py:321
  335.4 12.3 %out_product.6.refs_2_ = bf16[1024,3072]{1,0:T(8,128)(2,1)} custom-call(bf16[1024,384]{1,0:T(8,128)(2,1)S(1)} %copy-done.27, bf16[1024,512]{1,0:T(8,128)(2,1)S(1)} %get-tuple-element.69.refs_1_, bf16[1024,256]{1,0:T(8,128)(2,1)S(1)} %get-tuple-element.77.refs_2_, bf16[384,3072]{1,0:T(8,128)(2,1)S(1)} %copy-done, bf16[1536,3072]{1,0:T(8,128)(2,1)} %refs_1_.11), custom_call_target="tpu_custom_call" | custom-call | flops 113246208 | bytes 282624 | tf_op jit(solution)/shard_map/out_product/pallas_call | solution.py:321
  349.8 7.6 %out_product.7 = bf16[512,3072]{1,0:T(8,128)(2,1)} custom-call(bf16[512,768]{1,0:T(8,128)(2,1)S(1)} %get-tuple-element.75.refs_0_, bf16[1536,3072]{1,0:T(8,128)(2,1)} %refs_1_.11, bf16[1024,3072]{1,0:T(8,128)(2,1)} %out_product.6.refs_2_), custom_call_target="tpu_custom_call" | custom-call | flops 37748736 | bytes 196608 | tf_op jit(solution)/shard_map/out_product/pallas_call | solution.py:321
  357.5 6.9 %back_product.6 = bf16[512,3072]{1,0:T(8,128)(2,1)S(1)} custom-call(bf16[512,768]{1,0:T(8,128)(2,1)S(1)} %get-tuple-element.56.refs_0_, bf16[3072,768]{1,0:T(8,128)(2,1)} %bitcast.16.weight_ref.refs_1_, bf16[1024,3072]{1,0:T(8,128)(2,1)} %back_product.5.refs_2_), custom_call_target="tpu_custom_call" | custom-call | flops 37748736 | bytes 122880 | tf_op jit(solution)/shard_map/back_product/pallas_call | solution.py:321
  367.1 3.2 out_product.9
  372.4 3.2 out_product.11
  375.7 3.9 back_product.9
  381.5 3.3 back_product.8
  386.8 3.2 out_product.10
  390.0 3.2 out_product.8
  393.3 3.3 back_product.7
  398.4 9.2 %collective-permute-done.29 = bf16[256,1536]{1,0:T(8,128)(2,1)S(1)} collective-permute-done((bf16[256,1536]{1,0:T(8,128)(2,1)S(1)}, bf16[256,1536]{1,0:T(8,128)(2,1)S(1)}, u32[]{:S(2)}, u32[]{:S(2)}) %collective-permute-start.29) | collective-permute-done | bytes 786464 | tf_op jit(solution)/shard_map/ppermute | solution.py:121
  411.9 11.9 %collective-permute-done.33 = bf16[256,1536]{1,0:T(8,128)(2,1)S(1)} collective-permute-done((bf16[256,1536]{1,0:T(8,128)(2,1)S(1)}, bf16[256,1536]{1,0:T(8,128)(2,1)S(1)}, u32[]{:S(2)}, u32[]{:S(2)}) %collective-permute-start.33) | collective-permute-done | bytes 786464 | tf_op jit(solution)/shard_map/ppermute | solution.py:121
  431.0 12.1 %collective-permute-done.34 = bf16[2,64,1536]{2,1,0:T(8,128)(2,1)S(1)} collective-permute-done((bf16[2,64,1536]{2,1,0:T(8,128)(2,1)S(1)}, bf16[2,64,1536]{2,1,0:T(8,128)(2,1)S(1)}, u32[]{:S(2)}, u32[]{:S(2)}) %collective-permute-start.34) | collective-permute-done | bytes 393248 | tf_op jit(solution)/shard_map/ppermute | solution.py:121
  444.6 9.8 %collective-permute-done.35 = bf16[64,1536]{1,0:T(8,128)(2,1)S(1)} collective-permute-done((bf16[64,1536]{1,0:T(8,128)(2,1)S(1)}, bf16[64,1536]{1,0:T(8,128)(2,1)S(1)}, u32[]{:S(2)}, u32[]{:S(2)}) %collective-permute-start.35) | collective-permute-done | bytes 196640 | tf_op jit(solution)/shard_map/ppermute | solution.py:121
  455.3 5.6 %all-reduce = (f32[64]{0:T(128)S(1)}, f32[64]{0:T(128)}) all-reduce(f32[64]{0:T(128)S(1)} %fusion.28, f32[64]{0:T(128)} %reduce_sum.48), channel_id=1, replica_groups=mesh['gx'=4,'gy'=4,'gz'=2] {'gz'}, use_global_device_ids=true, to_apply=%region_8.9 | all-reduce | flops 128 | bytes 1024 | tf_op jit(solution)/shard_map/psum | solution.py:489
  (191 shorter events, 79.7 us)
Async XLA Ops:
  0.6 19.0 %collective-permute-start.2 = (bf16[64,3072]{1,0:T(8,128)(2,1)}, bf16[64,3072]{1,0:T(8,128)(2,1)S(1)}, u32[]{:S(2)}, u32[]{:S(2)}) collective-permute-start(bf16[64,3072]{1,0:T(8,128)(2,1)} %param.9), channel_id=1, source_target_pairs={{0,16},{8,24},{16,0},{24,8},{1,17},{9,25},{17,1},{25,9},{2,18},{10... | collective-permute-start | bytes 1179656 | tf_op jit(solution)/shard_map/ppermute | solution.py:121
  10.9 10.4 %collective-permute-start = (bf16[64,3072]{1,0:T(8,128)(2,1)S(1)}, bf16[64,3072]{1,0:T(8,128)(2,1)S(1)}, u32[]{:S(2)}, u32[]{:S(2)}) collective-permute-start(bf16[64,3072]{1,0:T(8,128)(2,1)S(1)} %fusion.27), channel_id=1, source_target_pairs={{0,16},{8,24},{16,0},{24,8},{1,17},{9,25},{17,1},{25,9},{2,18},{10... | collective-permute-start | bytes 1179656 | tf_op jit(solution)/shard_map/ppermute | solution.py:121
  19.7 2.6 collective-permute-start.9
  30.5 28.4 %copy-start.9 = (bf16[256,1920]{1,0:T(8,128)(2,1)}, bf16[256,1920]{1,0:T(8,128)(2,1)S(1)}, u32[]{:S(2)}) copy-start(bf16[256,1920]{1,0:T(8,128)(2,1)S(1)} %cot_product.6) | copy-start | bytes 2949124
  30.5 101.7 %all-to-all-start = ((bf16[4,768,1152]{2,1,0:T(8,128)(2,1)}), bf16[4,768,1152]{2,1,0:T(8,128)(2,1)}, u32[]{:S(2)}, u32[]{:S(2)}) async-start(bf16[4,768,1152]{2,1,0:T(8,128)(2,1)} %pack.4), calls=%async_computation | async-start | bytes 14155776 | tf_op jit(solution)/shard_map/all_to_all | solution.py:359
  35.9 20.2 %collective-permute-start.5 = (bf16[2,64,3072]{2,1,0:T(8,128)(2,1)}, bf16[2,64,3072]{2,1,0:T(8,128)(2,1)S(1)}, u32[]{:S(2)}, u32[]{:S(2)}) collective-permute-start(bf16[2,64,3072]{2,1,0:T(8,128)(2,1)} %copy-done.17), channel_id=1, source_target_pairs={{0,2},{2,0},{4,6},{6,4},{1,3},{3,1},{5,7},{7,5},{8,10},{10,8},{12,... | collective-permute-start | bytes 2359304 | tf_op jit(solution)/shard_map/ppermute | solution.py:121
  56.1 4.3 collective-permute-start.6
  56.1 38.1 %collective-permute-start.3 = (bf16[2,64,3072]{2,1,0:T(8,128)(2,1)}, bf16[2,64,3072]{2,1,0:T(8,128)(2,1)S(1)}, u32[]{:S(2)}, u32[]{:S(2)}) collective-permute-start(bf16[2,64,3072]{2,1,0:T(8,128)(2,1)} %copy-done.17), channel_id=1, source_target_pairs={{0,4},{2,6},{4,0},{6,2},{1,5},{3,7},{5,1},{7,3},{8,12},{10,14},{12... | collective-permute-start | bytes 2359304 | tf_op jit(solution)/shard_map/ppermute | solution.py:121
  58.9 48.6 %collective-permute-start.10 = (bf16[256,1920]{1,0:T(8,128)(2,1)S(1)}, bf16[256,1920]{1,0:T(8,128)(2,1)S(1)}, u32[]{:S(2)}, u32[]{:S(2)}) collective-permute-start(bf16[256,1920]{1,0:T(8,128)(2,1)S(1)} %cot_product.6), channel_id=1, source_target_pairs={{0,1},{1,0},{2,3},{3,2},{4,5},{5,4},{6,7},{7,6},{8,9},{9,8},{10,11... | collective-permute-start | bytes 2949128 | tf_op jit(solution)/shard_map/ppermute | solution.py:121
  68.6 31.0 %copy-start.11 = (bf16[256,1920]{1,0:T(8,128)(2,1)}, bf16[256,1920]{1,0:T(8,128)(2,1)S(1)}, u32[]{:S(2)}) copy-start(bf16[256,1920]{1,0:T(8,128)(2,1)S(1)} %cot_product.4) | copy-start | bytes 2949124
  68.6 62.7 %collective-permute-start.7 = (bf16[256,1920]{1,0:T(8,128)(2,1)S(1)}, bf16[256,1920]{1,0:T(8,128)(2,1)S(1)}, u32[]{:S(2)}, u32[]{:S(2)}) collective-permute-start(bf16[256,1920]{1,0:T(8,128)(2,1)S(1)} %cot_product.4), channel_id=1, source_target_pairs={{0,1},{1,0},{2,3},{3,2},{4,5},{5,4},{6,7},{7,6},{8,9},{9,8},{10,11... | collective-permute-start | bytes 2949128 | tf_op jit(solution)/shard_map/ppermute | solution.py:121
  69.1 36.3 %collective-permute-start.11 = (bf16[2,64,3072]{2,1,0:T(8,128)(2,1)}, bf16[2,64,3072]{2,1,0:T(8,128)(2,1)S(1)}, u32[]{:S(2)}, u32[]{:S(2)}) collective-permute-start(bf16[2,64,3072]{2,1,0:T(8,128)(2,1)} %pad_maximum_fusion.refs_0_), channel_id=1, source_target_pairs={{0,2},{2,0},{4,6},{6,4},{1,3},{3,1},{5,7},{7,5},{8,10},{10,8},{12,... | collective-permute-start | bytes 2359304 | tf_op jit(solution)/shard_map/ppermute | solution.py:121
  94.3 13.2 %collective-permute-start.12 = (bf16[2,64,3072]{2,1,0:T(8,128)(2,1)S(1)}, bf16[2,64,3072]{2,1,0:T(8,128)(2,1)S(1)}, u32[]{:S(2)}, u32[]{:S(2)}) collective-permute-start(bf16[2,64,3072]{2,1,0:T(8,128)(2,1)S(1)} %collective-permute-done.3.own_ref), channel_id=1, source_target_pairs={{0,8},{8,0},{16,24},{24,16},{1,9},{9,1},{17,25},{25,17},{2,10},{10... | collective-permute-start | bytes 2359304 | tf_op jit(solution)/shard_map/ppermute | solution.py:121
  94.3 36.1 %collective-permute-start.4 = (bf16[2,64,3072]{2,1,0:T(8,128)(2,1)S(1)}, bf16[2,64,3072]{2,1,0:T(8,128)(2,1)S(1)}, u32[]{:S(2)}, u32[]{:S(2)}) collective-permute-start(bf16[2,64,3072]{2,1,0:T(8,128)(2,1)S(1)} %collective-permute-done.3.own_ref), channel_id=1, source_target_pairs={{0,2},{2,0},{4,6},{6,4},{1,3},{3,1},{5,7},{7,5},{8,10},{10,8},{12,... | collective-permute-start | bytes 2359304 | tf_op jit(solution)/shard_map/ppermute | solution.py:121
  105.5 35.1 %collective-permute-start.15 = (bf16[2,64,3072]{2,1,0:T(8,128)(2,1)}, bf16[2,64,3072]{2,1,0:T(8,128)(2,1)}, u32[]{:S(2)}, u32[]{:S(2)}) collective-permute-start(bf16[2,64,3072]{2,1,0:T(8,128)(2,1)} %pad_maximum_fusion.refs_0_), channel_id=1, source_target_pairs={{0,4},{2,6},{4,0},{6,2},{1,5},{3,7},{5,1},{7,3},{8,12},{10,14},{12... | collective-permute-start | bytes 2359304 | tf_op jit(solution)/shard_map/ppermute | solution.py:121
  116.0 26.0 %copy-start.13 = (bf16[256,1920]{1,0:T(8,128)(2,1)}, bf16[256,1920]{1,0:T(8,128)(2,1)S(1)}, u32[]{:S(2)}) copy-start(bf16[256,1920]{1,0:T(8,128)(2,1)S(1)} %cot_product.7) | copy-start | bytes 2949124
  132.2 51.5 %all-to-all-start.1 = ((bf16[4,768,512]{2,1,0:T(8,128)(2,1)}), bf16[4,768,512]{2,1,0:T(8,128)(2,1)}, u32[]{:S(2)}, u32[]{:S(2)}) async-start(bf16[4,768,512]{2,1,0:T(8,128)(2,1)} %copy-done.7), calls=%async_computation.1 | async-start | bytes 6291456 | tf_op jit(solution)/shard_map/all_to_all | solution.py:359
  136.8 16.6 %copy-start.35 = (bf16[2,64,3072]{2,1,0:T(8,128)(2,1)S(1)}, bf16[2,64,3072]{2,1,0:T(8,128)(2,1)}, u32[]{:S(2)}) copy-start(bf16[2,64,3072]{2,1,0:T(8,128)(2,1)} %copy-done.34) | copy-start | bytes 2359300
  136.9 5.7 %collective-permute-start.8 = (bf16[2,64,3072]{2,1,0:T(8,128)(2,1)}, bf16[2,64,3072]{2,1,0:T(8,128)(2,1)S(1)}, u32[]{:S(2)}, u32[]{:S(2)}) collective-permute-start(bf16[2,64,3072]{2,1,0:T(8,128)(2,1)} %copy-done.36), channel_id=1, source_target_pairs={{0,8},{8,0},{16,24},{24,16},{1,9},{9,1},{17,25},{25,17},{2,10},{10... | collective-permute-start | bytes 2359304 | tf_op jit(solution)/shard_map/ppermute | solution.py:121
  137.3 16.1 %collective-permute-start.1 = (bf16[2,64,3072]{2,1,0:T(8,128)(2,1)}, bf16[2,64,3072]{2,1,0:T(8,128)(2,1)S(1)}, u32[]{:S(2)}, u32[]{:S(2)}) collective-permute-start(bf16[2,64,3072]{2,1,0:T(8,128)(2,1)} %pad_maximum_fusion.refs_0_), channel_id=1, source_target_pairs={{0,8},{8,0},{16,24},{24,16},{1,9},{9,1},{17,25},{25,17},{2,10},{10... | collective-permute-start | bytes 2359304 | tf_op jit(solution)/shard_map/ppermute | solution.py:121
  140.6 16.9 %collective-permute-start.17 = (bf16[2,64,3072]{2,1,0:T(8,128)(2,1)}, bf16[2,64,3072]{2,1,0:T(8,128)(2,1)S(1)}, u32[]{:S(2)}, u32[]{:S(2)}) collective-permute-start(bf16[2,64,3072]{2,1,0:T(8,128)(2,1)} %collective-permute-done.15.refs_4_), channel_id=1, source_target_pairs={{0,2},{2,0},{4,6},{6,4},{1,3},{3,1},{5,7},{7,5},{8,10},{10,8},{12,... | collective-permute-start | bytes 2359304 | tf_op jit(solution)/shard_map/ppermute | solution.py:121
  142.0 24.7 %collective-permute-start.13 = (bf16[256,1920]{1,0:T(8,128)(2,1)S(1)}, bf16[256,1920]{1,0:T(8,128)(2,1)S(1)}, u32[]{:S(2)}, u32[]{:S(2)}) collective-permute-start(bf16[256,1920]{1,0:T(8,128)(2,1)S(1)} %cot_product.7), channel_id=1, source_target_pairs={{0,1},{1,0},{2,3},{3,2},{4,5},{5,4},{6,7},{7,6},{8,9},{9,8},{10,11... | collective-permute-start | bytes 2949128 | tf_op jit(solution)/shard_map/ppermute | solution.py:121
  151.8 31.8 %collective-permute-start.19 = (bf16[256,1920]{1,0:T(8,128)(2,1)S(1)}, bf16[256,1920]{1,0:T(8,128)(2,1)}, u32[]{:S(2)}, u32[]{:S(2)}) collective-permute-start(bf16[256,1920]{1,0:T(8,128)(2,1)S(1)} %cot_product.5), channel_id=1, source_target_pairs={{0,1},{1,0},{2,3},{3,2},{4,5},{5,4},{6,7},{7,6},{8,9},{9,8},{10,11... | collective-permute-start | bytes 2949128 | tf_op jit(solution)/shard_map/ppermute | solution.py:121
  153.4 13.3 %collective-permute-start.16 = (bf16[2,64,3072]{2,1,0:T(8,128)(2,1)}, bf16[2,64,3072]{2,1,0:T(8,128)(2,1)S(1)}, u32[]{:S(2)}, u32[]{:S(2)}) collective-permute-start(bf16[2,64,3072]{2,1,0:T(8,128)(2,1)} %collective-permute-done.15.refs_4_), channel_id=1, source_target_pairs={{0,8},{8,0},{16,24},{24,16},{1,9},{9,1},{17,25},{25,17},{2,10},{10... | collective-permute-start | bytes 2359304 | tf_op jit(solution)/shard_map/ppermute | solution.py:121
  153.4 13.3 %collective-permute-start.14 = (bf16[2,64,3072]{2,1,0:T(8,128)(2,1)S(1)}, bf16[2,64,3072]{2,1,0:T(8,128)(2,1)S(1)}, u32[]{:S(2)}, u32[]{:S(2)}) collective-permute-start(bf16[2,64,3072]{2,1,0:T(8,128)(2,1)S(1)} %copy-done.35), channel_id=1, source_target_pairs={{0,8},{8,0},{16,24},{24,16},{1,9},{9,1},{17,25},{25,17},{2,10},{10... | collective-permute-start | bytes 2359304 | tf_op jit(solution)/shard_map/ppermute | solution.py:121
  157.5 10.2 %collective-permute-start.18 = (bf16[2,64,3072]{2,1,0:T(8,128)(2,1)S(1)}, bf16[2,64,3072]{2,1,0:T(8,128)(2,1)S(1)}, u32[]{:S(2)}, u32[]{:S(2)}) collective-permute-start(bf16[2,64,3072]{2,1,0:T(8,128)(2,1)S(1)} %collective-permute-done.17.refs_6_), channel_id=1, source_target_pairs={{0,8},{8,0},{16,24},{24,16},{1,9},{9,1},{17,25},{25,17},{2,10},{10... | collective-permute-start | bytes 2359304 | tf_op jit(solution)/shard_map/ppermute | solution.py:121
  183.7 28.6 %all-to-all-start.2 = ((bf16[4,768,256]{2,1,0:T(8,128)(2,1)}), bf16[4,768,256]{2,1,0:T(8,128)(2,1)}, u32[]{:S(2)}, u32[]{:S(2)}) async-start(bf16[4,768,256]{2,1,0:T(8,128)(2,1)} %copy-done.8), calls=%async_computation.2 | async-start | bytes 3145728 | tf_op jit(solution)/shard_map/all_to_all | solution.py:359
  212.3 60.9 %all-to-all-start.3 = ((bf16[4,768,768]{2,1,0:T(8,128)(2,1)}), bf16[4,768,768]{2,1,0:T(8,128)(2,1)}, u32[]{:S(2)}, u32[]{:S(2)}) async-start(bf16[4,768,768]{2,1,0:T(8,128)(2,1)} %copy-done.6), calls=%async_computation.3 | async-start | bytes 9437184 | tf_op jit(solution)/shard_map/all_to_all | solution.py:359
  217.4 54.3 %collective-permute-start.20 = (bf16[1024,1152]{1,0:T(8,128)(2,1)}, bf16[1024,1152]{1,0:T(8,128)(2,1)S(1)}, u32[]{:S(2)}, u32[]{:S(2)}) collective-permute-start(bf16[1024,1152]{1,0:T(8,128)(2,1)} %copy-done.1), channel_id=1, source_target_pairs={{0,1},{1,0},{2,3},{3,2},{4,5},{5,4},{6,7},{7,6},{8,9},{9,8},{10,11... | collective-permute-start | bytes 7077896 | tf_op jit(solution)/shard_map/ppermute | solution.py:121
  225.0 89.3 %collective-permute-start.21 = (bf16[1024,512]{1,0:T(8,128)(2,1)S(1)}, bf16[1024,512]{1,0:T(8,128)(2,1)}, u32[]{:S(2)}, u32[]{:S(2)}) collective-permute-start(bf16[1024,512]{1,0:T(8,128)(2,1)S(1)} %in_product.6), channel_id=1, source_target_pairs={{0,1},{1,0},{2,3},{3,2},{4,5},{5,4},{6,7},{7,6},{8,9},{9,8},{10,11... | collective-permute-start | bytes 3145736 | tf_op jit(solution)/shard_map/ppermute | solution.py:121
  232.6 73.0 %collective-permute-start.22 = (bf16[1024,256]{1,0:T(8,128)(2,1)}, bf16[1024,256]{1,0:T(8,128)(2,1)}, u32[]{:S(2)}, u32[]{:S(2)}) collective-permute-start(bf16[1024,256]{1,0:T(8,128)(2,1)} %in_product.9), channel_id=1, source_target_pairs={{0,1},{1,0},{2,3},{3,2},{4,5},{5,4},{6,7},{7,6},{8,9},{9,8},{10,11... | collective-permute-start | bytes 1572872 | tf_op jit(solution)/shard_map/ppermute | solution.py:121
  279.6 68.1 %collective-permute-start.23 = (bf16[512,768]{1,0:T(8,128)(2,1)S(1)}, bf16[512,768]{1,0:T(8,128)(2,1)}, u32[]{:S(2)}, u32[]{:S(2)}) collective-permute-start(bf16[512,768]{1,0:T(8,128)(2,1)S(1)} %in_product.7), channel_id=1, source_target_pairs={{0,1},{1,0},{2,3},{3,2},{4,5},{5,4},{6,7},{7,6},{8,9},{9,8},{10,11... | collective-permute-start | bytes 2359304 | tf_op jit(solution)/shard_map/ppermute | solution.py:121
  313.7 43.7 %collective-permute-start.24 = (bf16[512,768]{1,0:T(8,128)(2,1)S(1)}, bf16[512,768]{1,0:T(8,128)(2,1)}, u32[]{:S(2)}, u32[]{:S(2)}) collective-permute-start(bf16[512,768]{1,0:T(8,128)(2,1)S(1)} %in_product.8), channel_id=1, source_target_pairs={{0,1},{1,0},{2,3},{3,2},{4,5},{5,4},{6,7},{7,6},{8,9},{9,8},{10,11... | collective-permute-start | bytes 2359304 | tf_op jit(solution)/shard_map/ppermute | solution.py:121
  316.9 18.5 %copy-start.27 = (bf16[1024,384]{1,0:T(8,128)(2,1)S(1)}, bf16[1024,384]{1,0:T(8,128)(2,1)}, u32[]{:S(2)}) copy-start(bf16[1024,384]{1,0:T(8,128)(2,1)} %copy-done.26) | copy-start | bytes 2359300
  357.5 9.6 %collective-permute-start.25 = (bf16[512,3072]{1,0:T(8,128)(2,1)}, bf16[512,3072]{1,0:T(8,128)(2,1)S(1)}, u32[]{:S(2)}, u32[]{:S(2)}) collective-permute-start(bf16[512,3072]{1,0:T(8,128)(2,1)} %out_product.7), channel_id=1, source_target_pairs={{0,8},{8,0},{16,24},{24,16},{1,9},{9,1},{17,25},{25,17},{2,10},{10... | collective-permute-start | bytes 9437192 | tf_op jit(solution)/shard_map/ppermute | solution.py:121
  364.4 11.3 %collective-permute-start.32 = (bf16[512,3072]{1,0:T(8,128)(2,1)S(1)}, bf16[512,3072]{1,0:T(8,128)(2,1)S(1)}, u32[]{:S(2)}, u32[]{:S(2)}) collective-permute-start(bf16[512,3072]{1,0:T(8,128)(2,1)S(1)} %back_product.6), channel_id=1, source_target_pairs={{0,8},{8,0},{16,24},{24,16},{1,9},{9,1},{17,25},{25,17},{2,10},{10... | collective-permute-start | bytes 9437192 | tf_op jit(solution)/shard_map/ppermute | solution.py:121
  370.3 26.2 %collective-permute-start.26 = (bf16[256,1536]{1,0:T(8,128)(2,1)S(1)}, bf16[256,1536]{1,0:T(8,128)(2,1)}, u32[]{:S(2)}, u32[]{:S(2)}) collective-permute-start(bf16[256,1536]{1,0:T(8,128)(2,1)S(1)} %out_product.9), channel_id=1, source_target_pairs={{0,16},{8,24},{16,0},{24,8},{1,17},{9,25},{17,1},{25,9},{2,18},{10... | collective-permute-start | bytes 2359304 | tf_op jit(solution)/shard_map/ppermute | solution.py:121
  375.6 32.0 %collective-permute-start.29 = (bf16[256,1536]{1,0:T(8,128)(2,1)S(1)}, bf16[256,1536]{1,0:T(8,128)(2,1)S(1)}, u32[]{:S(2)}, u32[]{:S(2)}) collective-permute-start(bf16[256,1536]{1,0:T(8,128)(2,1)S(1)} %out_product.11), channel_id=1, source_target_pairs={{0,16},{8,24},{16,0},{24,8},{1,17},{9,25},{17,1},{25,9},{2,18},{10... | collective-permute-start | bytes 2359304 | tf_op jit(solution)/shard_map/ppermute | solution.py:121
  379.8 29.7 %collective-permute-start.36 = (bf16[2,2,64,1536]{3,2,0,1:T(8,128)(2,1)S(1)}, bf16[2,2,64,1536]{3,2,0,1:T(8,128)(2,1)S(1)}, u32[]{:S(2)}, u32[]{:S(2)}) collective-permute-start(bf16[2,2,64,1536]{3,2,0,1:T(8,128)(2,1)S(1)} %bitcast.100), channel_id=1, source_target_pairs={{0,2},{2,0},{4,6},{6,4},{1,3},{3,1},{5,7},{7,5},{8,10},{10,8},{12,... | collective-permute-start | bytes 2359304 | tf_op jit(solution)/shard_map/ppermute | solution.py:121
  384.7 39.1 %collective-permute-start.33 = (bf16[256,1536]{1,0:T(8,128)(2,1)S(1)}, bf16[256,1536]{1,0:T(8,128)(2,1)S(1)}, u32[]{:S(2)}, u32[]{:S(2)}) collective-permute-start(bf16[256,1536]{1,0:T(8,128)(2,1)S(1)} %back_product.8), channel_id=1, source_target_pairs={{0,16},{8,24},{16,0},{24,8},{1,17},{9,25},{17,1},{25,9},{2,18},{10... | collective-permute-start | bytes 2359304 | tf_op jit(solution)/shard_map/ppermute | solution.py:121
  397.9 27.8 %collective-permute-start.27 = (bf16[2,64,1536]{2,1,0:T(8,128)(2,1)S(1)}, bf16[2,64,1536]{2,1,0:T(8,128)(2,1)S(1)}, u32[]{:S(2)}, u32[]{:S(2)}) collective-permute-start(bf16[2,64,1536]{2,1,0:T(8,128)(2,1)S(1)} %fusion.40), channel_id=1, source_target_pairs={{0,2},{2,0},{4,6},{6,4},{1,3},{3,1},{5,7},{7,5},{8,10},{10,8},{12,... | collective-permute-start | bytes 1179656 | tf_op jit(solution)/shard_map/ppermute | solution.py:121
  407.9 20.1 %collective-permute-start.30 = (bf16[2,64,1536]{2,1,0:T(8,128)(2,1)S(1)}, bf16[2,64,1536]{2,1,0:T(8,128)(2,1)S(1)}, u32[]{:S(2)}, u32[]{:S(2)}) collective-permute-start(bf16[2,64,1536]{2,1,0:T(8,128)(2,1)S(1)} %fusion.41), channel_id=1, source_target_pairs={{0,2},{2,0},{4,6},{6,4},{1,3},{3,1},{5,7},{7,5},{8,10},{10,8},{12,... | collective-permute-start | bytes 1179656 | tf_op jit(solution)/shard_map/ppermute | solution.py:121
  409.8 19.2 %collective-permute-start.37 = (bf16[2,64,1536]{2,1,0:T(8,128)(2,1)S(1)}, bf16[2,64,1536]{2,1,0:T(8,128)(2,1)S(1)}, u32[]{:S(2)}, u32[]{:S(2)}) collective-permute-start(bf16[2,64,1536]{2,1,0:T(8,128)(2,1)S(1)} %fusion.39), channel_id=1, source_target_pairs={{0,4},{2,6},{4,0},{6,2},{1,5},{3,7},{5,1},{7,3},{8,12},{10,14},{12... | collective-permute-start | bytes 1179656 | tf_op jit(solution)/shard_map/ppermute | solution.py:121
  424.1 19.0 %collective-permute-start.34 = (bf16[2,64,1536]{2,1,0:T(8,128)(2,1)S(1)}, bf16[2,64,1536]{2,1,0:T(8,128)(2,1)S(1)}, u32[]{:S(2)}, u32[]{:S(2)}) collective-permute-start(bf16[2,64,1536]{2,1,0:T(8,128)(2,1)S(1)} %fusion.42), channel_id=1, source_target_pairs={{0,2},{2,0},{4,6},{6,4},{1,3},{3,1},{5,7},{7,5},{8,10},{10,8},{12,... | collective-permute-start | bytes 1179656 | tf_op jit(solution)/shard_map/ppermute | solution.py:121
  425.9 35.0 %collective-permute-start.28 = (bf16[64,1536]{1,0:T(8,128)(2,1)S(1)}, bf16[64,1536]{1,0:T(8,128)(2,1)}, u32[]{:S(2)}, u32[]{:S(2)}) collective-permute-start(bf16[64,1536]{1,0:T(8,128)(2,1)S(1)} %fusion.47), channel_id=1, source_target_pairs={{0,4},{2,6},{4,0},{6,2},{1,5},{3,7},{5,1},{7,3},{8,12},{10,14},{12... | collective-permute-start | bytes 589832 | tf_op jit(solution)/shard_map/ppermute | solution.py:121
  428.1 34.4 %collective-permute-start.31 = (bf16[64,1536]{1,0:T(8,128)(2,1)S(1)}, bf16[64,1536]{1,0:T(8,128)(2,1)}, u32[]{:S(2)}, u32[]{:S(2)}) collective-permute-start(bf16[64,1536]{1,0:T(8,128)(2,1)S(1)} %fusion.48), channel_id=1, source_target_pairs={{0,4},{2,6},{4,0},{6,2},{1,5},{3,7},{5,1},{7,3},{8,12},{10,14},{12... | collective-permute-start | bytes 589832 | tf_op jit(solution)/shard_map/ppermute | solution.py:121
  429.2 15.3 %collective-permute-start.38 = (bf16[64,1536]{1,0:T(8,128)(2,1)S(1)}, bf16[64,1536]{1,0:T(8,128)(2,1)S(1)}, u32[]{:S(2)}, u32[]{:S(2)}) collective-permute-start(bf16[64,1536]{1,0:T(8,128)(2,1)S(1)} %fusion.50), channel_id=1, source_target_pairs={{0,16},{8,24},{16,0},{24,8},{1,17},{9,25},{17,1},{25,9},{2,18},{10... | collective-permute-start | bytes 589832 | tf_op jit(solution)/shard_map/ppermute | solution.py:121
  443.2 11.1 %collective-permute-start.35 = (bf16[64,1536]{1,0:T(8,128)(2,1)S(1)}, bf16[64,1536]{1,0:T(8,128)(2,1)S(1)}, u32[]{:S(2)}, u32[]{:S(2)}) collective-permute-start(bf16[64,1536]{1,0:T(8,128)(2,1)S(1)} %fusion.49), channel_id=1, source_target_pairs={{0,4},{2,6},{4,0},{6,2},{1,5},{3,7},{5,1},{7,3},{8,12},{10,14},{12... | collective-permute-start | bytes 589832 | tf_op jit(solution)/shard_map/ppermute | solution.py:121
  (39 other events, 176.7 us)

commit v18 on v17

--- a/solution.py
+++ b/solution.py
@@ -381,7 +381,7 @@
     for place, part in enumerate(cot_parts):
         own, other = with_core(part)
         if place == 2:
-            own = after(own, cot_owns[1], cot_gots[0], normed_parts[1])
+            own = after(own, cot_owns[1], cot_gots[0], normed_parts[1], *packed_mlp[1:])
         if place == 3:
             own = after(own, cot_gots[1])
         cot_owns.append(cot_product((own, other), w_attn_out, w_mlp_out))

time: 467 us -> 477 us (1.021)
  waiting for transfers between devices: 167 us -> 176 us
    ppermute x39, waiting for transfers between devices: 167 us -> 172 us  [trade(): return lax.ppermute(block, axis, pairs)]
  transfers between devices with their start and end apart: 43 -> 43, of which waited for: 15 -> 14; matrix products, arithmetic and copies ran while one was open for 4% -> 4% of each run, Pallas kernels for 38% -> 37%
where the time goes in v18:
time: 477 us; the launch traced here: 474 us
  Pallas kernels  184 us (39%)
  waiting for transfers between devices  176 us (37%)
  starting transfers between devices  61.2 us (13%)
  local copies, waits for them, and re-layouts  20.6 us (4%)
  other arithmetic  19.3 us (4%)
  blocking collectives  10.5 us (2%)
    ppermute x39, waiting for transfers between devices, trade(): return lax.ppermute(block, axis, pairs)  172 us
    pallas_call x11, Pallas kernels, product(): pl.pallas_call(kernel, grid=(columns // tile,), in_specs=specs, out_specs...  68.6 us
    ppermute x39, starting transfers between devices, trade(): return lax.ppermute(block, axis, pairs)  41.7 us
    pallas_call x5, Pallas kernels, in_product(): pl.pallas_call(in_kernel, grid=(columns // tile,), in_specs=[pl.BlockSpec...  39.8 us
    pallas_call x4, Pallas kernels, cot_product(): pl.pallas_call(cot_kernel, grid=(columns // tile,), in_specs=[whole, whol...  32.9 us
    unnamed x89, local copies, waits for them, and re-layouts  20.3 us
    all_to_all x4, starting transfers between devices, swap(): lax.all_to_all(packed, 'gx', split_axis=0, concat_axis=0, tiled=True)  19.5 us
    pallas_call x4, Pallas kernels, pack(): pl.pallas_call(pack_kernel, grid=(owners, width // tile), in_specs=[spec]...  18.6 us
  transfers between devices with their start and end apart: 43, of which 14 were waited for; matrix products, arithmetic and copies ran while one was open for 4% of the time, Pallas kernels for 37%

profile of v18, /device:TPU:0, one launch (start us, length us, event | category | flops | bytes accessed | tf_op | source)
XLA Modules:
  0.0 473.9 jit_solution(3517497967097791579)
XLA Ops:
  0.6 3.0 collective-permute-start.2
  4.8 4.9 %all-reduce.1 = (f32[64]{0:T(128)S(1)}, f32[64]{0:T(128)S(1)}) all-reduce(f32[64]{0:T(128)S(1)} %get-tuple-element.59, f32[64]{0:T(128)S(1)} %get-tuple-element.58), channel_id=1, replica_groups=mesh['gx'=4,'gy'=4,'gz'=2] {'gz'}, use_global_device_ids=true, to_apply=%region_3.0 | all-reduce | flops 128 | bytes 1024 | tf_op jit(solution)/shard_map/psum | solution.py:371
  14.4 5.2 %pack.6 = bf16[4,768,1152]{2,1,0:T(8,128)(2,1)} custom-call(bf16[768,1536]{1,0:T(8,128)(2,1)S(1)} %copy-done.20, bf16[768,1536]{1,0:T(8,128)(2,1)S(1)} %copy-done.21, bf16[768,1536]{1,0:T(8,128)(2,1)} %refs_2_.1), custom_call_target="tpu_custom_call" | custom-call | bytes 221184 | tf_op jit(solution)/shard_map/pack/pallas_call | solution.py:148
  22.3 8.2 %cot_product.6 = bf16[256,1920]{1,0:T(8,128)(2,1)S(1)} custom-call(bf16[2,64,3072]{2,1,0:T(8,128)(2,1)S(1)} %pad_maximum_fusion.1.own_ref, bf16[2,64,3072]{2,1,0:T(8,128)(2,1)S(1)} %collective-permute-done.9.other_ref, bf16[384,3072]{1,0:T(8,128)(2,1)S(1)} %copy-done, bf16[1536,3072]{1,0:T(8,128)(2,1)} %refs_1_.11), custom_call_target="tpu_custom_call" | custom-call | flops 47185920 | bytes 199680 | tf_op jit(solution)/shard_map/cot_product/pallas_call | solution.py:214
  30.5 5.4 %all-to-all-start = ((bf16[4,768,1152]{2,1,0:T(8,128)(2,1)}), bf16[4,768,1152]{2,1,0:T(8,128)(2,1)}, u32[]{:S(2)}, u32[]{:S(2)}) async-start(bf16[4,768,1152]{2,1,0:T(8,128)(2,1)} %pack.6), calls=%async_computation | async-start | bytes 14155776 | tf_op jit(solution)/shard_map/all_to_all | solution.py:359
  37.8 18.3 %collective-permute-done.5.own_ref = bf16[2,64,3072]{2,1,0:T(8,128)(2,1)S(1)} collective-permute-done((bf16[2,64,3072]{2,1,0:T(8,128)(2,1)}, bf16[2,64,3072]{2,1,0:T(8,128)(2,1)S(1)}, u32[]{:S(2)}, u32[]{:S(2)}) %collective-permute-start.5) | collective-permute-done | bytes 786464 | tf_op jit(solution)/shard_map/ppermute | solution.py:121
  56.1 2.8 collective-permute-start.3
  60.4 8.1 %cot_product.4 = bf16[256,1920]{1,0:T(8,128)(2,1)S(1)} custom-call(bf16[2,64,3072]{2,1,0:T(8,128)(2,1)S(1)} %collective-permute-done.5.own_ref, bf16[2,64,3072]{2,1,0:T(8,128)(2,1)S(1)} %collective-permute-done.6.other_ref, bf16[384,3072]{1,0:T(8,128)(2,1)S(1)} %copy-done, bf16[1536,3072]{1,0:T(8,128)(2,1)} %refs_1_.11), custom_call_target="tpu_custom_call" | custom-call | flops 47185920 | bytes 199680 | tf_op jit(solution)/shard_map/cot_product/pallas_call | solution.py:214
  70.7 23.5 %collective-permute-done.3.own_ref = bf16[2,64,3072]{2,1,0:T(8,128)(2,1)S(1)} collective-permute-done((bf16[2,64,3072]{2,1,0:T(8,128)(2,1)}, bf16[2,64,3072]{2,1,0:T(8,128)(2,1)S(1)}, u32[]{:S(2)}, u32[]{:S(2)}) %collective-permute-start.3) | collective-permute-done | bytes 786464 | tf_op jit(solution)/shard_map/ppermute | solution.py:121
  98.5 4.5 pack.7
  104.6 6.7 %pack.5 = bf16[4,768,768]{2,1,0:T(8,128)(2,1)S(1)} custom-call(bf16[768,6144]{1,0:T(8,128)(2,1)} %refs_0_.7), custom_call_target="tpu_custom_call" | custom-call | bytes 147456 | tf_op jit(solution)/shard_map/pack/pallas_call | solution.py:148
  113.4 3.3 collective-permute-start.15
  116.7 8.5 %cot_product.7 = bf16[256,1920]{1,0:T(8,128)(2,1)S(1)} custom-call(bf16[2,64,3072]{2,1,0:T(8,128)(2,1)S(1)} %collective-permute-done.3.own_ref, bf16[2,64,3072]{2,1,0:T(8,128)(2,1)S(1)} %collective-permute-done.12.other_ref, bf16[384,3072]{1,0:T(8,128)(2,1)S(1)} %copy-done, bf16[1536,3072]{1,0:T(8,128)(2,1)} %refs_1_.11), custom_call_target="tpu_custom_call" | custom-call | flops 47185920 | bytes 199680 | tf_op jit(solution)/shard_map/cot_product/pallas_call | solution.py:214
  127.2 4.6 all-to-all-start.1
  132.4 19.4 %collective-permute-done.15.refs_4_ = bf16[2,64,3072]{2,1,0:T(8,128)(2,1)} collective-permute-done((bf16[2,64,3072]{2,1,0:T(8,128)(2,1)}, bf16[2,64,3072]{2,1,0:T(8,128)(2,1)}, u32[]{:S(2)}, u32[]{:S(2)}) %collective-permute-start.15) | collective-permute-done | bytes 786464 | tf_op jit(solution)/shard_map/ppermute | solution.py:121
  154.5 8.1 %cot_product.5 = bf16[256,1920]{1,0:T(8,128)(2,1)S(1)} custom-call(bf16[2,64,3072]{2,1,0:T(8,128)(2,1)S(1)} %copy-done.37, bf16[2,64,3072]{2,1,0:T(8,128)(2,1)S(1)} %collective-permute-done.8.other_ref, bf16[384,3072]{1,0:T(8,128)(2,1)S(1)} %copy-done, bf16[1536,3072]{1,0:T(8,128)(2,1)} %refs_1_.11), custom_call_target="tpu_custom_call" | custom-call | flops 47185920 | bytes 199680 | tf_op jit(solution)/shard_map/cot_product/pallas_call | solution.py:214
  163.7 7.8 %collective-permute-done.17.refs_6_ = bf16[2,64,3072]{2,1,0:T(8,128)(2,1)S(1)} collective-permute-done((bf16[2,64,3072]{2,1,0:T(8,128)(2,1)}, bf16[2,64,3072]{2,1,0:T(8,128)(2,1)S(1)}, u32[]{:S(2)}, u32[]{:S(2)}) %collective-permute-start.17) | collective-permute-done | bytes 786464 | tf_op jit(solution)/shard_map/ppermute | solution.py:121
  171.5 4.9 %collective-permute-done.13 = bf16[256,1920]{1,0:T(8,128)(2,1)S(1)} collective-permute-done((bf16[256,1920]{1,0:T(8,128)(2,1)S(1)}, bf16[256,1920]{1,0:T(8,128)(2,1)S(1)}, u32[]{:S(2)}, u32[]{:S(2)}) %collective-permute-start.13) | collective-permute-done | bytes 983072 | tf_op jit(solution)/shard_map/ppermute | solution.py:121
  177.4 5.0 %assemble.1.rows_ref = bf16[1024,3072]{1,0:T(8,128)(2,1)} custom-call(bf16[2,64,3072]{2,1,0:T(8,128)(2,1)} %pad_maximum_fusion.refs_0_, bf16[2,64,3072]{2,1,0:T(8,128)(2,1)S(1)} %collective-permute-done.1.refs_1_, bf16[2,64,3072]{2,1,0:T(8,128)(2,1)S(1)} %copy-done.35, bf16[2,64,3072]{2,1,0:T(8,128)(2,1)S(1)} %collective-permute-done.14.refs_3_, ...), custom_call_target="tpu_custom_call" | custom-call | bytes 196608 | tf_op jit(solution)/shard_map/assemble/pallas_call | solution.py:178
  182.4 14.3 %collective-permute-done.19 = bf16[256,1920]{1,0:T(8,128)(2,1)} collective-permute-done((bf16[256,1920]{1,0:T(8,128)(2,1)S(1)}, bf16[256,1920]{1,0:T(8,128)(2,1)}, u32[]{:S(2)}, u32[]{:S(2)}) %collective-permute-start.19) | collective-permute-done | bytes 983072 | tf_op jit(solution)/shard_map/ppermute | solution.py:121
  196.7 4.4 all-to-all-start.2
  201.1 14.0 %in_product.5.q_own.k_own.v_own = bf16[1024,1152]{1,0:T(8,128)(2,1)S(1)} custom-call(bf16[1024,3072]{1,0:T(8,128)(2,1)} %assemble.1.rows_ref, bf16[3072,1152]{1,0:T(8,128)(2,1)} %bitcast.4.weight_ref.refs_5_), custom_call_target="tpu_custom_call" | custom-call | flops 113246208 | bytes 245760 | tf_op jit(solution)/shard_map/in_product/pallas_call | solution.py:268
  216.5 4.8 %all-to-all-done.2 = bf16[4,768,256]{2,1,0:T(8,128)(2,1)} async-done(((bf16[4,768,256]{2,1,0:T(8,128)(2,1)}), bf16[4,768,256]{2,1,0:T(8,128)(2,1)}, u32[]{:S(2)}, u32[]{:S(2)}) %all-to-all-start.2) | async-done | bytes 1572896 | tf_op jit(solution)/shard_map/all_to_all | solution.py:359
  221.3 5.1 %all-to-all-start.3 = ((bf16[4,768,768]{2,1,0:T(8,128)(2,1)}), bf16[4,768,768]{2,1,0:T(8,128)(2,1)}, u32[]{:S(2)}, u32[]{:S(2)}) async-start(bf16[4,768,768]{2,1,0:T(8,128)(2,1)} %copy-done.6), calls=%async_computation.3 | async-start | bytes 9437184 | tf_op jit(solution)/shard_map/all_to_all | solution.py:359
  227.9 6.9 %in_product.6 = bf16[1024,512]{1,0:T(8,128)(2,1)S(1)} custom-call(bf16[1024,3072]{1,0:T(8,128)(2,1)} %assemble.1.rows_ref, bf16[3072,512]{1,0:T(8,128)(2,1)} %bitcast.5.weight_ref.refs_6_), custom_call_target="tpu_custom_call" | custom-call | flops 50331648 | bytes 163840 | tf_op jit(solution)/shard_map/in_product/pallas_call | solution.py:268
  235.5 6.2 %in_product.9 = bf16[1024,256]{1,0:T(8,128)(2,1)} custom-call(bf16[1024,3072]{1,0:T(8,128)(2,1)} %assemble.1.rows_ref, bf16[3072,256]{1,0:T(8,128)(2,1)} %bitcast.6.weight_ref.refs_7_), custom_call_target="tpu_custom_call" | custom-call | flops 25165824 | bytes 131072 | tf_op jit(solution)/shard_map/in_product/pallas_call | solution.py:268
  243.0 4.6 add_parts.1
  247.6 33.2 %collective-permute-done.20.q_got.k_got.v_got = bf16[1024,1152]{1,0:T(8,128)(2,1)S(1)} collective-permute-done((bf16[1024,1152]{1,0:T(8,128)(2,1)}, bf16[1024,1152]{1,0:T(8,128)(2,1)S(1)}, u32[]{:S(2)}, u32[]{:S(2)}) %collective-permute-start.20) | collective-permute-done | bytes 2359328 | tf_op jit(solution)/shard_map/ppermute | solution.py:121
  282.1 6.4 %in_product.7 = bf16[512,768]{1,0:T(8,128)(2,1)S(1)} custom-call(bf16[1024,3072]{1,0:T(8,128)(2,1)} %assemble.1.rows_ref, bf16[3072,768]{1,0:T(8,128)(2,1)} %bitcast.16.weight_ref.refs_1_), custom_call_target="tpu_custom_call" | custom-call | flops 37748736 | bytes 184320 | tf_op jit(solution)/shard_map/in_product/pallas_call | solution.py:268
  291.7 14.9 %attend.1 = (bf16[1024,384]{1,0:T(8,128)(2,1)S(1)}, bf16[1024,384]{1,0:T(8,128)(2,1)S(1)}, bf16[1024,384]{1,0:T(8,128)(2,1)S(1)}, bf16[1024,384]{1,0:T(8,128)(2,1)S(1)}) custom-call(bf16[1024,1152]{1,0:T(8,128)(2,1)S(1)} %copy-done.2, bf16[1024,1152]{1,0:T(8,128)(2,1)S(1)} %copy-done.5, bf16[1024,1152]{1,0:T(8,128)(2,1)S(1)} %copy-done.2, ...), custom_call_target="tpu_custom_call" | custom-call | flops 12582912 | bytes 98304 | tf_op jit(solution)/shard_map/attend/pallas_call | solution.py:75
  309.3 5.3 %collective-permute-done.22 = bf16[1024,256]{1,0:T(8,128)(2,1)} collective-permute-done((bf16[1024,256]{1,0:T(8,128)(2,1)}, bf16[1024,256]{1,0:T(8,128)(2,1)}, u32[]{:S(2)}, u32[]{:S(2)}) %collective-permute-start.22) | collective-permute-done | bytes 524320 | tf_op jit(solution)/shard_map/ppermute | solution.py:121
  316.4 6.3 %in_product.8 = bf16[512,768]{1,0:T(8,128)(2,1)S(1)} custom-call(bf16[1024,3072]{1,0:T(8,128)(2,1)} %assemble.1.rows_ref, bf16[3072,768]{1,0:T(8,128)(2,1)} %bitcast.16.weight_ref.refs_1_), custom_call_target="tpu_custom_call" | custom-call | flops 37748736 | bytes 184320 | tf_op jit(solution)/shard_map/in_product/pallas_call | solution.py:268
  326.7 18.5 %back_product.5.refs_2_ = bf16[1024,3072]{1,0:T(8,128)(2,1)} custom-call(bf16[1024,384]{1,0:T(8,128)(2,1)S(1)} %copy-done.29, bf16[1024,384]{1,0:T(8,128)(2,1)S(1)} %copy-done.31, bf16[1024,384]{1,0:T(8,128)(2,1)S(1)} %copy-done.33, bf16[1024,512]{1,0:T(8,128)(2,1)S(1)} %get-tuple-element.68.refs_3_, bf16[1024,256]{1,0:T(8,128)(2,1)S(1)} %get-tuple-element.76.refs_4_, ...), custom_call_target="tpu_custom_call" | custom-call | flops 188743680 | bytes 282624 | tf_op jit(solution)/shard_map/back_product/pallas_call | solution.py:321
  345.2 12.3 %out_product.6.refs_2_ = bf16[1024,3072]{1,0:T(8,128)(2,1)} custom-call(bf16[1024,384]{1,0:T(8,128)(2,1)S(1)} %copy-done.27, bf16[1024,512]{1,0:T(8,128)(2,1)S(1)} %get-tuple-element.69.refs_1_, bf16[1024,256]{1,0:T(8,128)(2,1)S(1)} %get-tuple-element.77.refs_2_, bf16[384,3072]{1,0:T(8,128)(2,1)S(1)} %copy-done, bf16[1536,3072]{1,0:T(8,128)(2,1)} %refs_1_.11), custom_call_target="tpu_custom_call" | custom-call | flops 113246208 | bytes 282624 | tf_op jit(solution)/shard_map/out_product/pallas_call | solution.py:321
  359.6 7.6 %out_product.7 = bf16[512,3072]{1,0:T(8,128)(2,1)} custom-call(bf16[512,768]{1,0:T(8,128)(2,1)S(1)} %get-tuple-element.75.refs_0_, bf16[1536,3072]{1,0:T(8,128)(2,1)} %refs_1_.11, bf16[1024,3072]{1,0:T(8,128)(2,1)} %out_product.6.refs_2_), custom_call_target="tpu_custom_call" | custom-call | flops 37748736 | bytes 196608 | tf_op jit(solution)/shard_map/out_product/pallas_call | solution.py:321
  367.3 6.9 %back_product.6 = bf16[512,3072]{1,0:T(8,128)(2,1)S(1)} custom-call(bf16[512,768]{1,0:T(8,128)(2,1)S(1)} %get-tuple-element.56.refs_0_, bf16[3072,768]{1,0:T(8,128)(2,1)} %bitcast.16.weight_ref.refs_1_, bf16[1024,3072]{1,0:T(8,128)(2,1)} %back_product.5.refs_2_), custom_call_target="tpu_custom_call" | custom-call | flops 37748736 | bytes 122880 | tf_op jit(solution)/shard_map/back_product/pallas_call | solution.py:321
  376.9 3.2 out_product.9
  381.9 3.2 out_product.11
  385.5 3.9 back_product.9
  391.4 3.3 back_product.8
  396.5 3.2 out_product.10
  399.7 3.2 out_product.8
  402.9 3.3 back_product.7
  407.9 9.5 %collective-permute-done.29 = bf16[256,1536]{1,0:T(8,128)(2,1)S(1)} collective-permute-done((bf16[256,1536]{1,0:T(8,128)(2,1)S(1)}, bf16[256,1536]{1,0:T(8,128)(2,1)S(1)}, u32[]{:S(2)}, u32[]{:S(2)}) %collective-permute-start.29) | collective-permute-done | bytes 786464 | tf_op jit(solution)/shard_map/ppermute | solution.py:121
  420.8 12.5 %collective-permute-done.33 = bf16[256,1536]{1,0:T(8,128)(2,1)S(1)} collective-permute-done((bf16[256,1536]{1,0:T(8,128)(2,1)S(1)}, bf16[256,1536]{1,0:T(8,128)(2,1)S(1)}, u32[]{:S(2)}, u32[]{:S(2)}) %collective-permute-start.33) | collective-permute-done | bytes 786464 | tf_op jit(solution)/shard_map/ppermute | solution.py:121
  440.6 11.7 %collective-permute-done.34 = bf16[2,64,1536]{2,1,0:T(8,128)(2,1)S(1)} collective-permute-done((bf16[2,64,1536]{2,1,0:T(8,128)(2,1)S(1)}, bf16[2,64,1536]{2,1,0:T(8,128)(2,1)S(1)}, u32[]{:S(2)}, u32[]{:S(2)}) %collective-permute-start.34) | collective-permute-done | bytes 393248 | tf_op jit(solution)/shard_map/ppermute | solution.py:121
  452.9 10.6 %collective-permute-done.35 = bf16[64,1536]{1,0:T(8,128)(2,1)S(1)} collective-permute-done((bf16[64,1536]{1,0:T(8,128)(2,1)S(1)}, bf16[64,1536]{1,0:T(8,128)(2,1)S(1)}, u32[]{:S(2)}, u32[]{:S(2)}) %collective-permute-start.35) | collective-permute-done | bytes 196640 | tf_op jit(solution)/shard_map/ppermute | solution.py:121
  464.5 5.6 %all-reduce = (f32[64]{0:T(128)S(1)}, f32[64]{0:T(128)}) all-reduce(f32[64]{0:T(128)S(1)} %fusion.28, f32[64]{0:T(128)} %reduce_sum.48), channel_id=1, replica_groups=mesh['gx'=4,'gy'=4,'gz'=2] {'gz'}, use_global_device_ids=true, to_apply=%region_8.9 | all-reduce | flops 128 | bytes 1024 | tf_op jit(solution)/shard_map/psum | solution.py:489
  (191 shorter events, 75.5 us)
Async XLA Ops:
  0.6 19.0 %collective-permute-start.2 = (bf16[64,3072]{1,0:T(8,128)(2,1)}, bf16[64,3072]{1,0:T(8,128)(2,1)S(1)}, u32[]{:S(2)}, u32[]{:S(2)}) collective-permute-start(bf16[64,3072]{1,0:T(8,128)(2,1)} %param.9), channel_id=1, source_target_pairs={{0,16},{8,24},{16,0},{24,8},{1,17},{9,25},{17,1},{25,9},{2,18},{10... | collective-permute-start | bytes 1179656 | tf_op jit(solution)/shard_map/ppermute | solution.py:121
  10.9 10.4 %collective-permute-start = (bf16[64,3072]{1,0:T(8,128)(2,1)S(1)}, bf16[64,3072]{1,0:T(8,128)(2,1)S(1)}, u32[]{:S(2)}, u32[]{:S(2)}) collective-permute-start(bf16[64,3072]{1,0:T(8,128)(2,1)S(1)} %fusion.27), channel_id=1, source_target_pairs={{0,16},{8,24},{16,0},{24,8},{1,17},{9,25},{17,1},{25,9},{2,18},{10... | collective-permute-start | bytes 1179656 | tf_op jit(solution)/shard_map/ppermute | solution.py:121
  19.7 2.6 collective-permute-start.9
  30.5 28.4 %copy-start.9 = (bf16[256,1920]{1,0:T(8,128)(2,1)}, bf16[256,1920]{1,0:T(8,128)(2,1)S(1)}, u32[]{:S(2)}) copy-start(bf16[256,1920]{1,0:T(8,128)(2,1)S(1)} %cot_product.6) | copy-start | bytes 2949124
  30.5 96.7 %all-to-all-start = ((bf16[4,768,1152]{2,1,0:T(8,128)(2,1)}), bf16[4,768,1152]{2,1,0:T(8,128)(2,1)}, u32[]{:S(2)}, u32[]{:S(2)}) async-start(bf16[4,768,1152]{2,1,0:T(8,128)(2,1)} %pack.6), calls=%async_computation | async-start | bytes 14155776 | tf_op jit(solution)/shard_map/all_to_all | solution.py:359
  35.9 20.2 %collective-permute-start.5 = (bf16[2,64,3072]{2,1,0:T(8,128)(2,1)}, bf16[2,64,3072]{2,1,0:T(8,128)(2,1)S(1)}, u32[]{:S(2)}, u32[]{:S(2)}) collective-permute-start(bf16[2,64,3072]{2,1,0:T(8,128)(2,1)} %copy-done.17), channel_id=1, source_target_pairs={{0,2},{2,0},{4,6},{6,4},{1,3},{3,1},{5,7},{7,5},{8,10},{10,8},{12,... | collective-permute-start | bytes 2359304 | tf_op jit(solution)/shard_map/ppermute | solution.py:121
  56.1 4.3 collective-permute-start.6
  56.1 38.1 %collective-permute-start.3 = (bf16[2,64,3072]{2,1,0:T(8,128)(2,1)}, bf16[2,64,3072]{2,1,0:T(8,128)(2,1)S(1)}, u32[]{:S(2)}, u32[]{:S(2)}) collective-permute-start(bf16[2,64,3072]{2,1,0:T(8,128)(2,1)} %copy-done.17), channel_id=1, source_target_pairs={{0,4},{2,6},{4,0},{6,2},{1,5},{3,7},{5,1},{7,3},{8,12},{10,14},{12... | collective-permute-start | bytes 2359304 | tf_op jit(solution)/shard_map/ppermute | solution.py:121
  58.9 57.9 %collective-permute-start.10 = (bf16[256,1920]{1,0:T(8,128)(2,1)S(1)}, bf16[256,1920]{1,0:T(8,128)(2,1)S(1)}, u32[]{:S(2)}, u32[]{:S(2)}) collective-permute-start(bf16[256,1920]{1,0:T(8,128)(2,1)S(1)} %cot_product.6), channel_id=1, source_target_pairs={{0,1},{1,0},{2,3},{3,2},{4,5},{5,4},{6,7},{7,6},{8,9},{9,8},{10,11... | collective-permute-start | bytes 2949128 | tf_op jit(solution)/shard_map/ppermute | solution.py:121
  68.5 28.8 %copy-start.11 = (bf16[256,1920]{1,0:T(8,128)(2,1)}, bf16[256,1920]{1,0:T(8,128)(2,1)S(1)}, u32[]{:S(2)}) copy-start(bf16[256,1920]{1,0:T(8,128)(2,1)S(1)} %cot_product.4) | copy-start | bytes 2949124
  68.5 57.7 %collective-permute-start.7 = (bf16[256,1920]{1,0:T(8,128)(2,1)S(1)}, bf16[256,1920]{1,0:T(8,128)(2,1)S(1)}, u32[]{:S(2)}, u32[]{:S(2)}) collective-permute-start(bf16[256,1920]{1,0:T(8,128)(2,1)S(1)} %cot_product.4), channel_id=1, source_target_pairs={{0,1},{1,0},{2,3},{3,2},{4,5},{5,4},{6,7},{7,6},{8,9},{9,8},{10,11... | collective-permute-start | bytes 2949128 | tf_op jit(solution)/shard_map/ppermute | solution.py:121
  69.1 44.3 %collective-permute-start.11 = (bf16[2,64,3072]{2,1,0:T(8,128)(2,1)}, bf16[2,64,3072]{2,1,0:T(8,128)(2,1)S(1)}, u32[]{:S(2)}, u32[]{:S(2)}) collective-permute-start(bf16[2,64,3072]{2,1,0:T(8,128)(2,1)} %pad_maximum_fusion.refs_0_), channel_id=1, source_target_pairs={{0,2},{2,0},{4,6},{6,4},{1,3},{3,1},{5,7},{7,5},{8,10},{10,8},{12,... | collective-permute-start | bytes 2359304 | tf_op jit(solution)/shard_map/ppermute | solution.py:121
  94.2 22.5 %collective-permute-start.12 = (bf16[2,64,3072]{2,1,0:T(8,128)(2,1)S(1)}, bf16[2,64,3072]{2,1,0:T(8,128)(2,1)S(1)}, u32[]{:S(2)}, u32[]{:S(2)}) collective-permute-start(bf16[2,64,3072]{2,1,0:T(8,128)(2,1)S(1)} %collective-permute-done.3.own_ref), channel_id=1, source_target_pairs={{0,8},{8,0},{16,24},{24,16},{1,9},{9,1},{17,25},{25,17},{2,10},{10... | collective-permute-start | bytes 2359304 | tf_op jit(solution)/shard_map/ppermute | solution.py:121
  94.2 31.0 %collective-permute-start.4 = (bf16[2,64,3072]{2,1,0:T(8,128)(2,1)S(1)}, bf16[2,64,3072]{2,1,0:T(8,128)(2,1)S(1)}, u32[]{:S(2)}, u32[]{:S(2)}) collective-permute-start(bf16[2,64,3072]{2,1,0:T(8,128)(2,1)S(1)} %collective-permute-done.3.own_ref), channel_id=1, source_target_pairs={{0,2},{2,0},{4,6},{6,4},{1,3},{3,1},{5,7},{7,5},{8,10},{10,8},{12,... | collective-permute-start | bytes 2359304 | tf_op jit(solution)/shard_map/ppermute | solution.py:121
  113.4 38.4 %collective-permute-start.15 = (bf16[2,64,3072]{2,1,0:T(8,128)(2,1)}, bf16[2,64,3072]{2,1,0:T(8,128)(2,1)}, u32[]{:S(2)}, u32[]{:S(2)}) collective-permute-start(bf16[2,64,3072]{2,1,0:T(8,128)(2,1)} %pad_maximum_fusion.refs_0_), channel_id=1, source_target_pairs={{0,4},{2,6},{4,0},{6,2},{1,5},{3,7},{5,1},{7,3},{8,12},{10,14},{12... | collective-permute-start | bytes 2359304 | tf_op jit(solution)/shard_map/ppermute | solution.py:121
  125.3 26.5 %copy-start.13 = (bf16[256,1920]{1,0:T(8,128)(2,1)}, bf16[256,1920]{1,0:T(8,128)(2,1)S(1)}, u32[]{:S(2)}) copy-start(bf16[256,1920]{1,0:T(8,128)(2,1)S(1)} %cot_product.7) | copy-start | bytes 2949124
  127.2 69.5 %all-to-all-start.1 = ((bf16[4,768,512]{2,1,0:T(8,128)(2,1)}), bf16[4,768,512]{2,1,0:T(8,128)(2,1)}, u32[]{:S(2)}, u32[]{:S(2)}) async-start(bf16[4,768,512]{2,1,0:T(8,128)(2,1)} %copy-done.7), calls=%async_computation.1 | async-start | bytes 6291456 | tf_op jit(solution)/shard_map/all_to_all | solution.py:359
  131.8 31.4 %copy-start.35 = (bf16[2,64,3072]{2,1,0:T(8,128)(2,1)S(1)}, bf16[2,64,3072]{2,1,0:T(8,128)(2,1)}, u32[]{:S(2)}) copy-start(bf16[2,64,3072]{2,1,0:T(8,128)(2,1)} %copy-done.34) | copy-start | bytes 2359300
  131.8 21.5 %collective-permute-start.8 = (bf16[2,64,3072]{2,1,0:T(8,128)(2,1)}, bf16[2,64,3072]{2,1,0:T(8,128)(2,1)S(1)}, u32[]{:S(2)}, u32[]{:S(2)}) collective-permute-start(bf16[2,64,3072]{2,1,0:T(8,128)(2,1)} %copy-done.36), channel_id=1, source_target_pairs={{0,8},{8,0},{16,24},{24,16},{1,9},{9,1},{17,25},{25,17},{2,10},{10... | collective-permute-start | bytes 2359304 | tf_op jit(solution)/shard_map/ppermute | solution.py:121
  132.3 30.9 %collective-permute-start.1 = (bf16[2,64,3072]{2,1,0:T(8,128)(2,1)}, bf16[2,64,3072]{2,1,0:T(8,128)(2,1)S(1)}, u32[]{:S(2)}, u32[]{:S(2)}) collective-permute-start(bf16[2,64,3072]{2,1,0:T(8,128)(2,1)} %pad_maximum_fusion.refs_0_), channel_id=1, source_target_pairs={{0,8},{8,0},{16,24},{24,16},{1,9},{9,1},{17,25},{25,17},{2,10},{10... | collective-permute-start | bytes 2359304 | tf_op jit(solution)/shard_map/ppermute | solution.py:121
  151.8 19.7 %collective-permute-start.17 = (bf16[2,64,3072]{2,1,0:T(8,128)(2,1)}, bf16[2,64,3072]{2,1,0:T(8,128)(2,1)S(1)}, u32[]{:S(2)}, u32[]{:S(2)}) collective-permute-start(bf16[2,64,3072]{2,1,0:T(8,128)(2,1)} %collective-permute-done.15.refs_4_), channel_id=1, source_target_pairs={{0,2},{2,0},{4,6},{6,4},{1,3},{3,1},{5,7},{7,5},{8,10},{10,8},{12,... | collective-permute-start | bytes 2359304 | tf_op jit(solution)/shard_map/ppermute | solution.py:121
  151.8 24.6 %collective-permute-start.13 = (bf16[256,1920]{1,0:T(8,128)(2,1)S(1)}, bf16[256,1920]{1,0:T(8,128)(2,1)S(1)}, u32[]{:S(2)}, u32[]{:S(2)}) collective-permute-start(bf16[256,1920]{1,0:T(8,128)(2,1)S(1)} %cot_product.7), channel_id=1, source_target_pairs={{0,1},{1,0},{2,3},{3,2},{4,5},{5,4},{6,7},{7,6},{8,9},{9,8},{10,11... | collective-permute-start | bytes 2949128 | tf_op jit(solution)/shard_map/ppermute | solution.py:121
  162.6 19.8 %copy-start.15 = (bf16[256,1920]{1,0:T(8,128)(2,1)}, bf16[256,1920]{1,0:T(8,128)(2,1)S(1)}, u32[]{:S(2)}) copy-start(bf16[256,1920]{1,0:T(8,128)(2,1)S(1)} %cot_product.5) | copy-start | bytes 2949124
  162.6 34.1 %collective-permute-start.19 = (bf16[256,1920]{1,0:T(8,128)(2,1)S(1)}, bf16[256,1920]{1,0:T(8,128)(2,1)}, u32[]{:S(2)}, u32[]{:S(2)}) collective-permute-start(bf16[256,1920]{1,0:T(8,128)(2,1)S(1)} %cot_product.5), channel_id=1, source_target_pairs={{0,1},{1,0},{2,3},{3,2},{4,5},{5,4},{6,7},{7,6},{8,9},{9,8},{10,11... | collective-permute-start | bytes 2949128 | tf_op jit(solution)/shard_map/ppermute | solution.py:121
  163.2 13.2 %collective-permute-start.16 = (bf16[2,64,3072]{2,1,0:T(8,128)(2,1)}, bf16[2,64,3072]{2,1,0:T(8,128)(2,1)S(1)}, u32[]{:S(2)}, u32[]{:S(2)}) collective-permute-start(bf16[2,64,3072]{2,1,0:T(8,128)(2,1)} %collective-permute-done.15.refs_4_), channel_id=1, source_target_pairs={{0,8},{8,0},{16,24},{24,16},{1,9},{9,1},{17,25},{25,17},{2,10},{10... | collective-permute-start | bytes 2359304 | tf_op jit(solution)/shard_map/ppermute | solution.py:121
  163.2 13.2 %collective-permute-start.14 = (bf16[2,64,3072]{2,1,0:T(8,128)(2,1)S(1)}, bf16[2,64,3072]{2,1,0:T(8,128)(2,1)S(1)}, u32[]{:S(2)}, u32[]{:S(2)}) collective-permute-start(bf16[2,64,3072]{2,1,0:T(8,128)(2,1)S(1)} %copy-done.35), channel_id=1, source_target_pairs={{0,8},{8,0},{16,24},{24,16},{1,9},{9,1},{17,25},{25,17},{2,10},{10... | collective-permute-start | bytes 2359304 | tf_op jit(solution)/shard_map/ppermute | solution.py:121
  171.5 4.9 %collective-permute-start.18 = (bf16[2,64,3072]{2,1,0:T(8,128)(2,1)S(1)}, bf16[2,64,3072]{2,1,0:T(8,128)(2,1)S(1)}, u32[]{:S(2)}, u32[]{:S(2)}) collective-permute-start(bf16[2,64,3072]{2,1,0:T(8,128)(2,1)S(1)} %collective-permute-done.17.refs_6_), channel_id=1, source_target_pairs={{0,8},{8,0},{16,24},{24,16},{1,9},{9,1},{17,25},{25,17},{2,10},{10... | collective-permute-start | bytes 2359304 | tf_op jit(solution)/shard_map/ppermute | solution.py:121
  196.7 24.5 %all-to-all-start.2 = ((bf16[4,768,256]{2,1,0:T(8,128)(2,1)}), bf16[4,768,256]{2,1,0:T(8,128)(2,1)}, u32[]{:S(2)}, u32[]{:S(2)}) async-start(bf16[4,768,256]{2,1,0:T(8,128)(2,1)} %copy-done.8), calls=%async_computation.2 | async-start | bytes 3145728 | tf_op jit(solution)/shard_map/all_to_all | solution.py:359
  221.3 60.9 %all-to-all-start.3 = ((bf16[4,768,768]{2,1,0:T(8,128)(2,1)}), bf16[4,768,768]{2,1,0:T(8,128)(2,1)}, u32[]{:S(2)}, u32[]{:S(2)}) async-start(bf16[4,768,768]{2,1,0:T(8,128)(2,1)} %copy-done.6), calls=%async_computation.3 | async-start | bytes 9437184 | tf_op jit(solution)/shard_map/all_to_all | solution.py:359
  226.4 54.4 %collective-permute-start.20 = (bf16[1024,1152]{1,0:T(8,128)(2,1)}, bf16[1024,1152]{1,0:T(8,128)(2,1)S(1)}, u32[]{:S(2)}, u32[]{:S(2)}) collective-permute-start(bf16[1024,1152]{1,0:T(8,128)(2,1)} %copy-done.1), channel_id=1, source_target_pairs={{0,1},{1,0},{2,3},{3,2},{4,5},{5,4},{6,7},{7,6},{8,9},{9,8},{10,11... | collective-permute-start | bytes 7077896 | tf_op jit(solution)/shard_map/ppermute | solution.py:121
  234.9 89.3 %collective-permute-start.21 = (bf16[1024,512]{1,0:T(8,128)(2,1)S(1)}, bf16[1024,512]{1,0:T(8,128)(2,1)}, u32[]{:S(2)}, u32[]{:S(2)}) collective-permute-start(bf16[1024,512]{1,0:T(8,128)(2,1)S(1)} %in_product.6), channel_id=1, source_target_pairs={{0,1},{1,0},{2,3},{3,2},{4,5},{5,4},{6,7},{7,6},{8,9},{9,8},{10,11... | collective-permute-start | bytes 3145736 | tf_op jit(solution)/shard_map/ppermute | solution.py:121
  241.7 72.9 %collective-permute-start.22 = (bf16[1024,256]{1,0:T(8,128)(2,1)}, bf16[1024,256]{1,0:T(8,128)(2,1)}, u32[]{:S(2)}, u32[]{:S(2)}) collective-permute-start(bf16[1024,256]{1,0:T(8,128)(2,1)} %in_product.9), channel_id=1, source_target_pairs={{0,1},{1,0},{2,3},{3,2},{4,5},{5,4},{6,7},{7,6},{8,9},{9,8},{10,11... | collective-permute-start | bytes 1572872 | tf_op jit(solution)/shard_map/ppermute | solution.py:121
  288.6 68.9 %collective-permute-start.23 = (bf16[512,768]{1,0:T(8,128)(2,1)S(1)}, bf16[512,768]{1,0:T(8,128)(2,1)}, u32[]{:S(2)}, u32[]{:S(2)}) collective-permute-start(bf16[512,768]{1,0:T(8,128)(2,1)S(1)} %in_product.7), channel_id=1, source_target_pairs={{0,1},{1,0},{2,3},{3,2},{4,5},{5,4},{6,7},{7,6},{8,9},{9,8},{10,11... | collective-permute-start | bytes 2359304 | tf_op jit(solution)/shard_map/ppermute | solution.py:121
  322.7 44.5 %collective-permute-start.24 = (bf16[512,768]{1,0:T(8,128)(2,1)S(1)}, bf16[512,768]{1,0:T(8,128)(2,1)}, u32[]{:S(2)}, u32[]{:S(2)}) collective-permute-start(bf16[512,768]{1,0:T(8,128)(2,1)S(1)} %in_product.8), channel_id=1, source_target_pairs={{0,1},{1,0},{2,3},{3,2},{4,5},{5,4},{6,7},{7,6},{8,9},{9,8},{10,11... | collective-permute-start | bytes 2359304 | tf_op jit(solution)/shard_map/ppermute | solution.py:121
  367.3 9.6 %collective-permute-start.25 = (bf16[512,3072]{1,0:T(8,128)(2,1)}, bf16[512,3072]{1,0:T(8,128)(2,1)S(1)}, u32[]{:S(2)}, u32[]{:S(2)}) collective-permute-start(bf16[512,3072]{1,0:T(8,128)(2,1)} %out_product.7), channel_id=1, source_target_pairs={{0,8},{8,0},{16,24},{24,16},{1,9},{9,1},{17,25},{25,17},{2,10},{10... | collective-permute-start | bytes 9437192 | tf_op jit(solution)/shard_map/ppermute | solution.py:121
  374.2 11.3 %collective-permute-start.32 = (bf16[512,3072]{1,0:T(8,128)(2,1)S(1)}, bf16[512,3072]{1,0:T(8,128)(2,1)S(1)}, u32[]{:S(2)}, u32[]{:S(2)}) collective-permute-start(bf16[512,3072]{1,0:T(8,128)(2,1)S(1)} %back_product.6), channel_id=1, source_target_pairs={{0,8},{8,0},{16,24},{24,16},{1,9},{9,1},{17,25},{25,17},{2,10},{10... | collective-permute-start | bytes 9437192 | tf_op jit(solution)/shard_map/ppermute | solution.py:121
  380.1 26.1 %collective-permute-start.26 = (bf16[256,1536]{1,0:T(8,128)(2,1)S(1)}, bf16[256,1536]{1,0:T(8,128)(2,1)}, u32[]{:S(2)}, u32[]{:S(2)}) collective-permute-start(bf16[256,1536]{1,0:T(8,128)(2,1)S(1)} %out_product.9), channel_id=1, source_target_pairs={{0,16},{8,24},{16,0},{24,8},{1,17},{9,25},{17,1},{25,9},{2,18},{10... | collective-permute-start | bytes 2359304 | tf_op jit(solution)/shard_map/ppermute | solution.py:121
  385.1 32.3 %collective-permute-start.29 = (bf16[256,1536]{1,0:T(8,128)(2,1)S(1)}, bf16[256,1536]{1,0:T(8,128)(2,1)S(1)}, u32[]{:S(2)}, u32[]{:S(2)}) collective-permute-start(bf16[256,1536]{1,0:T(8,128)(2,1)S(1)} %out_product.11), channel_id=1, source_target_pairs={{0,16},{8,24},{16,0},{24,8},{1,17},{9,25},{17,1},{25,9},{2,18},{10... | collective-permute-start | bytes 2359304 | tf_op jit(solution)/shard_map/ppermute | solution.py:121
  389.6 29.9 %collective-permute-start.36 = (bf16[2,2,64,1536]{3,2,0,1:T(8,128)(2,1)S(1)}, bf16[2,2,64,1536]{3,2,0,1:T(8,128)(2,1)S(1)}, u32[]{:S(2)}, u32[]{:S(2)}) collective-permute-start(bf16[2,2,64,1536]{3,2,0,1:T(8,128)(2,1)S(1)} %bitcast.100), channel_id=1, source_target_pairs={{0,2},{2,0},{4,6},{6,4},{1,3},{3,1},{5,7},{7,5},{8,10},{10,8},{12,... | collective-permute-start | bytes 2359304 | tf_op jit(solution)/shard_map/ppermute | solution.py:121
  394.6 38.7 %collective-permute-start.33 = (bf16[256,1536]{1,0:T(8,128)(2,1)S(1)}, bf16[256,1536]{1,0:T(8,128)(2,1)S(1)}, u32[]{:S(2)}, u32[]{:S(2)}) collective-permute-start(bf16[256,1536]{1,0:T(8,128)(2,1)S(1)} %back_product.8), channel_id=1, source_target_pairs={{0,16},{8,24},{16,0},{24,8},{1,17},{9,25},{17,1},{25,9},{2,18},{10... | collective-permute-start | bytes 2359304 | tf_op jit(solution)/shard_map/ppermute | solution.py:121
  407.6 27.8 %collective-permute-start.27 = (bf16[2,64,1536]{2,1,0:T(8,128)(2,1)S(1)}, bf16[2,64,1536]{2,1,0:T(8,128)(2,1)S(1)}, u32[]{:S(2)}, u32[]{:S(2)}) collective-permute-start(bf16[2,64,1536]{2,1,0:T(8,128)(2,1)S(1)} %fusion.40), channel_id=1, source_target_pairs={{0,2},{2,0},{4,6},{6,4},{1,3},{3,1},{5,7},{7,5},{8,10},{10,8},{12,... | collective-permute-start | bytes 1179656 | tf_op jit(solution)/shard_map/ppermute | solution.py:121
  417.7 18.9 %collective-permute-start.30 = (bf16[2,64,1536]{2,1,0:T(8,128)(2,1)S(1)}, bf16[2,64,1536]{2,1,0:T(8,128)(2,1)S(1)}, u32[]{:S(2)}, u32[]{:S(2)}) collective-permute-start(bf16[2,64,1536]{2,1,0:T(8,128)(2,1)S(1)} %fusion.41), channel_id=1, source_target_pairs={{0,2},{2,0},{4,6},{6,4},{1,3},{3,1},{5,7},{7,5},{8,10},{10,8},{12,... | collective-permute-start | bytes 1179656 | tf_op jit(solution)/shard_map/ppermute | solution.py:121
  419.8 18.9 %collective-permute-start.37 = (bf16[2,64,1536]{2,1,0:T(8,128)(2,1)S(1)}, bf16[2,64,1536]{2,1,0:T(8,128)(2,1)S(1)}, u32[]{:S(2)}, u32[]{:S(2)}) collective-permute-start(bf16[2,64,1536]{2,1,0:T(8,128)(2,1)S(1)} %fusion.39), channel_id=1, source_target_pairs={{0,4},{2,6},{4,0},{6,2},{1,5},{3,7},{5,1},{7,3},{8,12},{10,14},{12... | collective-permute-start | bytes 1179656 | tf_op jit(solution)/shard_map/ppermute | solution.py:121
  433.6 18.7 %collective-permute-start.34 = (bf16[2,64,1536]{2,1,0:T(8,128)(2,1)S(1)}, bf16[2,64,1536]{2,1,0:T(8,128)(2,1)S(1)}, u32[]{:S(2)}, u32[]{:S(2)}) collective-permute-start(bf16[2,64,1536]{2,1,0:T(8,128)(2,1)S(1)} %fusion.42), channel_id=1, source_target_pairs={{0,2},{2,0},{4,6},{6,4},{1,3},{3,1},{5,7},{7,5},{8,10},{10,8},{12,... | collective-permute-start | bytes 1179656 | tf_op jit(solution)/shard_map/ppermute | solution.py:121
  435.5 34.5 %collective-permute-start.28 = (bf16[64,1536]{1,0:T(8,128)(2,1)S(1)}, bf16[64,1536]{1,0:T(8,128)(2,1)}, u32[]{:S(2)}, u32[]{:S(2)}) collective-permute-start(bf16[64,1536]{1,0:T(8,128)(2,1)S(1)} %fusion.47), channel_id=1, source_target_pairs={{0,4},{2,6},{4,0},{6,2},{1,5},{3,7},{5,1},{7,3},{8,12},{10,14},{12... | collective-permute-start | bytes 589832 | tf_op jit(solution)/shard_map/ppermute | solution.py:121
  436.7 35.0 %collective-permute-start.31 = (bf16[64,1536]{1,0:T(8,128)(2,1)S(1)}, bf16[64,1536]{1,0:T(8,128)(2,1)}, u32[]{:S(2)}, u32[]{:S(2)}) collective-permute-start(bf16[64,1536]{1,0:T(8,128)(2,1)S(1)} %fusion.48), channel_id=1, source_target_pairs={{0,4},{2,6},{4,0},{6,2},{1,5},{3,7},{5,1},{7,3},{8,12},{10,14},{12... | collective-permute-start | bytes 589832 | tf_op jit(solution)/shard_map/ppermute | solution.py:121
  438.8 13.9 %collective-permute-start.38 = (bf16[64,1536]{1,0:T(8,128)(2,1)S(1)}, bf16[64,1536]{1,0:T(8,128)(2,1)S(1)}, u32[]{:S(2)}, u32[]{:S(2)}) collective-permute-start(bf16[64,1536]{1,0:T(8,128)(2,1)S(1)} %fusion.50), channel_id=1, source_target_pairs={{0,16},{8,24},{16,0},{24,8},{1,17},{9,25},{17,1},{25,9},{2,18},{10... | collective-permute-start | bytes 589832 | tf_op jit(solution)/shard_map/ppermute | solution.py:121
  452.4 11.1 %collective-permute-start.35 = (bf16[64,1536]{1,0:T(8,128)(2,1)S(1)}, bf16[64,1536]{1,0:T(8,128)(2,1)S(1)}, u32[]{:S(2)}, u32[]{:S(2)}) collective-permute-start(bf16[64,1536]{1,0:T(8,128)(2,1)S(1)} %fusion.49), channel_id=1, source_target_pairs={{0,4},{2,6},{4,0},{6,2},{1,5},{3,7},{5,1},{7,3},{8,12},{10,14},{12... | collective-permute-start | bytes 589832 | tf_op jit(solution)/shard_map/ppermute | solution.py:121
  (39 other events, 196.2 us)

commit v19 on v17

--- a/solution.py
+++ b/solution.py
@@ -363,7 +363,7 @@
     packed_heads = pack((w_query, w_key, w_value), n_gx, 0, heads_width, heads_width)
     starts = [sum(MLP_CUTS[:cut]) for cut in range(len(MLP_CUTS))]
     packed_mlp = [
-        pack((w_mlp_in,), n_gx, start, width, 256) for start, width in zip(starts, MLP_CUTS)
+        pack((w_mlp_in,), n_gx, start, width, 256) for start, width in zip(starts[:2], MLP_CUTS)
     ]
 
     cot_pair = with_x(out_cotangent)
@@ -397,9 +397,11 @@
     in_mlp.append(swap(after(packed_mlp[1], in_mlp[0], all_in, cot_gots[3])))
     heads_own = in_product(after(all_in, cot_gots[3]), in_heads)
     heads_got = others(heads_own)
-    mlp_own = [in_product(after(all_in, heads_own, in_mlp[1]), in_mlp[0])]
+    last_weight = after(w_mlp_in, heads_own)
+    packed_last = pack((last_weight,), n_gx, starts[2], MLP_CUTS[2], 256)
+    mlp_own = [in_product(after(all_in, heads_own, packed_last, in_mlp[1]), in_mlp[0])]
     mlp_got = [others(mlp_own[0])]
-    in_mlp.append(swap(after(packed_mlp[2], in_mlp[1], heads_own)))
+    in_mlp.append(swap(after(packed_last, in_mlp[1])))
     mlp_own.append(in_product(after(all_in, mlp_own[0]), in_mlp[1]))
     mlp_got.append(others(mlp_own[1]))
 

time: 467 us -> 467 us (level)
  no operation moved by 1% of the time
where the time goes in v19:
time: 467 us; the launch traced here: 465 us
  Pallas kernels  184 us (39%)
  waiting for transfers between devices  167 us (36%)
  starting transfers between devices  61.2 us (13%)
  local copies, waits for them, and re-layouts  21.5 us (5%)
  other arithmetic  19.3 us (4%)
  blocking collectives  10.5 us (2%)
    ppermute x39, waiting for transfers between devices, trade(): return lax.ppermute(block, axis, pairs)  167 us
    pallas_call x11, Pallas kernels, product(): pl.pallas_call(kernel, grid=(columns // tile,), in_specs=specs, out_specs...  68.6 us
    ppermute x39, starting transfers between devices, trade(): return lax.ppermute(block, axis, pairs)  41.6 us
    pallas_call x5, Pallas kernels, in_product(): pl.pallas_call(in_kernel, grid=(columns // tile,), in_specs=[pl.BlockSpec...  39.6 us
    pallas_call x4, Pallas kernels, cot_product(): pl.pallas_call(cot_kernel, grid=(columns // tile,), in_specs=[whole, whol...  32.9 us
    unnamed x89, local copies, waits for them, and re-layouts  21.2 us
    all_to_all x4, starting transfers between devices, swap(): lax.all_to_all(packed, 'gx', split_axis=0, concat_axis=0, tiled=True)  19.5 us
    pallas_call x4, Pallas kernels, pack(): pl.pallas_call(pack_kernel, grid=(owners, width // tile), in_specs=[spec]...  18.6 us
  transfers between devices with their start and end apart: 43, of which 15 were waited for; matrix products, arithmetic and copies ran while one was open for 4% of the time, Pallas kernels for 38%

profile of v19, /device:TPU:0, one launch (start us, length us, event | category | flops | bytes accessed | tf_op | source)
XLA Modules:
  0.0 464.7 jit_solution(5006168044882784589)
XLA Ops:
  0.6 3.0 collective-permute-start.2
  4.8 4.9 %all-reduce.1 = (f32[64]{0:T(128)S(1)}, f32[64]{0:T(128)S(1)}) all-reduce(f32[64]{0:T(128)S(1)} %get-tuple-element.61, f32[64]{0:T(128)S(1)} %get-tuple-element.60), channel_id=1, replica_groups=mesh['gx'=4,'gy'=4,'gz'=2] {'gz'}, use_global_device_ids=true, to_apply=%region_3.0 | all-reduce | flops 128 | bytes 1024 | tf_op jit(solution)/shard_map/psum | solution.py:371
  14.4 5.2 %pack.4 = bf16[4,768,1152]{2,1,0:T(8,128)(2,1)} custom-call(bf16[768,1536]{1,0:T(8,128)(2,1)S(1)} %copy-done.20, bf16[768,1536]{1,0:T(8,128)(2,1)S(1)} %copy-done.21, bf16[768,1536]{1,0:T(8,128)(2,1)} %refs_2_.1), custom_call_target="tpu_custom_call" | custom-call | bytes 221184 | tf_op jit(solution)/shard_map/pack/pallas_call | solution.py:148
  22.4 8.2 %cot_product.6 = bf16[256,1920]{1,0:T(8,128)(2,1)S(1)} custom-call(bf16[2,64,3072]{2,1,0:T(8,128)(2,1)S(1)} %pad_maximum_fusion.1.own_ref, bf16[2,64,3072]{2,1,0:T(8,128)(2,1)S(1)} %collective-permute-done.9.other_ref, bf16[384,3072]{1,0:T(8,128)(2,1)S(1)} %copy-done, bf16[1536,3072]{1,0:T(8,128)(2,1)} %refs_1_.11), custom_call_target="tpu_custom_call" | custom-call | flops 47185920 | bytes 199680 | tf_op jit(solution)/shard_map/cot_product/pallas_call | solution.py:214
  30.5 5.4 %all-to-all-start = ((bf16[4,768,1152]{2,1,0:T(8,128)(2,1)}), bf16[4,768,1152]{2,1,0:T(8,128)(2,1)}, u32[]{:S(2)}, u32[]{:S(2)}) async-start(bf16[4,768,1152]{2,1,0:T(8,128)(2,1)} %pack.4), calls=%async_computation | async-start | bytes 14155776 | tf_op jit(solution)/shard_map/all_to_all | solution.py:359
  37.8 18.3 %collective-permute-done.5.own_ref = bf16[2,64,3072]{2,1,0:T(8,128)(2,1)S(1)} collective-permute-done((bf16[2,64,3072]{2,1,0:T(8,128)(2,1)}, bf16[2,64,3072]{2,1,0:T(8,128)(2,1)S(1)}, u32[]{:S(2)}, u32[]{:S(2)}) %collective-permute-start.5) | collective-permute-done | bytes 786464 | tf_op jit(solution)/shard_map/ppermute | solution.py:121
  56.1 2.8 collective-permute-start.3
  60.4 8.1 %cot_product.4 = bf16[256,1920]{1,0:T(8,128)(2,1)S(1)} custom-call(bf16[2,64,3072]{2,1,0:T(8,128)(2,1)S(1)} %collective-permute-done.5.own_ref, bf16[2,64,3072]{2,1,0:T(8,128)(2,1)S(1)} %collective-permute-done.6.other_ref, bf16[384,3072]{1,0:T(8,128)(2,1)S(1)} %copy-done, bf16[1536,3072]{1,0:T(8,128)(2,1)} %refs_1_.11), custom_call_target="tpu_custom_call" | custom-call | flops 47185920 | bytes 199680 | tf_op jit(solution)/shard_map/cot_product/pallas_call | solution.py:214
  70.7 23.5 %collective-permute-done.3.own_ref = bf16[2,64,3072]{2,1,0:T(8,128)(2,1)S(1)} collective-permute-done((bf16[2,64,3072]{2,1,0:T(8,128)(2,1)}, bf16[2,64,3072]{2,1,0:T(8,128)(2,1)S(1)}, u32[]{:S(2)}, u32[]{:S(2)}) %collective-permute-start.3) | collective-permute-done | bytes 786464 | tf_op jit(solution)/shard_map/ppermute | solution.py:121
  95.1 4.5 pack.7
  101.3 4.2 collective-permute-done.11.refs_2_
  107.5 8.5 %cot_product.7 = bf16[256,1920]{1,0:T(8,128)(2,1)S(1)} custom-call(bf16[2,64,3072]{2,1,0:T(8,128)(2,1)S(1)} %collective-permute-done.3.own_ref, bf16[2,64,3072]{2,1,0:T(8,128)(2,1)S(1)} %collective-permute-done.12.other_ref, bf16[384,3072]{1,0:T(8,128)(2,1)S(1)} %copy-done, bf16[1536,3072]{1,0:T(8,128)(2,1)} %refs_1_.11), custom_call_target="tpu_custom_call" | custom-call | flops 47185920 | bytes 199680 | tf_op jit(solution)/shard_map/cot_product/pallas_call | solution.py:214
  116.1 14.3 %collective-permute-done.4.own_ref = bf16[2,64,3072]{2,1,0:T(8,128)(2,1)S(1)} collective-permute-done((bf16[2,64,3072]{2,1,0:T(8,128)(2,1)S(1)}, bf16[2,64,3072]{2,1,0:T(8,128)(2,1)S(1)}, u32[]{:S(2)}, u32[]{:S(2)}) %collective-permute-start.4) | collective-permute-done | bytes 786464 | tf_op jit(solution)/shard_map/ppermute | solution.py:121
  132.2 4.6 all-to-all-start.1
  137.4 3.2 collective-permute-done.15.refs_4_
  143.7 8.1 %cot_product.5 = bf16[256,1920]{1,0:T(8,128)(2,1)S(1)} custom-call(bf16[2,64,3072]{2,1,0:T(8,128)(2,1)S(1)} %copy-done.37, bf16[2,64,3072]{2,1,0:T(8,128)(2,1)S(1)} %collective-permute-done.8.other_ref, bf16[384,3072]{1,0:T(8,128)(2,1)S(1)} %copy-done, bf16[1536,3072]{1,0:T(8,128)(2,1)} %refs_1_.11), custom_call_target="tpu_custom_call" | custom-call | flops 47185920 | bytes 199680 | tf_op jit(solution)/shard_map/cot_product/pallas_call | solution.py:214
  153.9 3.5 collective-permute-done.17.refs_6_
  160.9 5.9 %collective-permute-done.13 = bf16[256,1920]{1,0:T(8,128)(2,1)S(1)} collective-permute-done((bf16[256,1920]{1,0:T(8,128)(2,1)S(1)}, bf16[256,1920]{1,0:T(8,128)(2,1)S(1)}, u32[]{:S(2)}, u32[]{:S(2)}) %collective-permute-start.13) | collective-permute-done | bytes 983072 | tf_op jit(solution)/shard_map/ppermute | solution.py:121
  168.6 5.0 %assemble.1.rows_ref = bf16[1024,3072]{1,0:T(8,128)(2,1)} custom-call(bf16[2,64,3072]{2,1,0:T(8,128)(2,1)} %pad_maximum_fusion.refs_0_, bf16[2,64,3072]{2,1,0:T(8,128)(2,1)S(1)} %collective-permute-done.1.refs_1_, bf16[2,64,3072]{2,1,0:T(8,128)(2,1)S(1)} %copy-done.35, bf16[2,64,3072]{2,1,0:T(8,128)(2,1)S(1)} %collective-permute-done.14.refs_3_, ...), custom_call_target="tpu_custom_call" | custom-call | bytes 196608 | tf_op jit(solution)/shard_map/assemble/pallas_call | solution.py:178
  173.6 10.1 %collective-permute-done.19 = bf16[256,1920]{1,0:T(8,128)(2,1)} collective-permute-done((bf16[256,1920]{1,0:T(8,128)(2,1)S(1)}, bf16[256,1920]{1,0:T(8,128)(2,1)}, u32[]{:S(2)}, u32[]{:S(2)}) %collective-permute-start.19) | collective-permute-done | bytes 983072 | tf_op jit(solution)/shard_map/ppermute | solution.py:121
  183.7 4.4 all-to-all-start.2
  188.1 14.0 %in_product.5.q_own.k_own.v_own = bf16[1024,1152]{1,0:T(8,128)(2,1)S(1)} custom-call(bf16[1024,3072]{1,0:T(8,128)(2,1)} %assemble.1.rows_ref, bf16[3072,1152]{1,0:T(8,128)(2,1)} %bitcast.4.weight_ref.refs_5_), custom_call_target="tpu_custom_call" | custom-call | flops 113246208 | bytes 245760 | tf_op jit(solution)/shard_map/in_product/pallas_call | solution.py:268
  203.5 6.7 %pack.5 = bf16[4,768,768]{2,1,0:T(8,128)(2,1)S(1)} custom-call(bf16[768,6144]{1,0:T(8,128)(2,1)} %refs_0_.6), custom_call_target="tpu_custom_call" | custom-call | bytes 147456 | tf_op jit(solution)/shard_map/pack/pallas_call | solution.py:148
  212.3 5.1 %all-to-all-start.3 = ((bf16[4,768,768]{2,1,0:T(8,128)(2,1)}), bf16[4,768,768]{2,1,0:T(8,128)(2,1)}, u32[]{:S(2)}, u32[]{:S(2)}) async-start(bf16[4,768,768]{2,1,0:T(8,128)(2,1)} %copy-done.6), calls=%async_computation.3 | async-start | bytes 9437184 | tf_op jit(solution)/shard_map/all_to_all | solution.py:359
  218.1 6.9 %in_product.6 = bf16[1024,512]{1,0:T(8,128)(2,1)S(1)} custom-call(bf16[1024,3072]{1,0:T(8,128)(2,1)} %assemble.1.rows_ref, bf16[3072,512]{1,0:T(8,128)(2,1)} %bitcast.5.weight_ref.refs_6_), custom_call_target="tpu_custom_call" | custom-call | flops 50331648 | bytes 163840 | tf_op jit(solution)/shard_map/in_product/pallas_call | solution.py:268
  226.6 6.0 %in_product.9 = bf16[1024,256]{1,0:T(8,128)(2,1)} custom-call(bf16[1024,3072]{1,0:T(8,128)(2,1)} %assemble.1.rows_ref, bf16[3072,256]{1,0:T(8,128)(2,1)} %bitcast.6.weight_ref.refs_7_), custom_call_target="tpu_custom_call" | custom-call | flops 25165824 | bytes 131072 | tf_op jit(solution)/shard_map/in_product/pallas_call | solution.py:268
  233.3 4.6 add_parts.1
  237.9 33.9 %collective-permute-done.20.q_got.k_got.v_got = bf16[1024,1152]{1,0:T(8,128)(2,1)S(1)} collective-permute-done((bf16[1024,1152]{1,0:T(8,128)(2,1)}, bf16[1024,1152]{1,0:T(8,128)(2,1)S(1)}, u32[]{:S(2)}, u32[]{:S(2)}) %collective-permute-start.20) | collective-permute-done | bytes 2359328 | tf_op jit(solution)/shard_map/ppermute | solution.py:121
  273.2 6.4 %in_product.7 = bf16[512,768]{1,0:T(8,128)(2,1)S(1)} custom-call(bf16[1024,3072]{1,0:T(8,128)(2,1)} %assemble.1.rows_ref, bf16[3072,768]{1,0:T(8,128)(2,1)} %bitcast.16.weight_ref.refs_1_), custom_call_target="tpu_custom_call" | custom-call | flops 37748736 | bytes 184320 | tf_op jit(solution)/shard_map/in_product/pallas_call | solution.py:268
  281.9 14.9 %attend.1 = (bf16[1024,384]{1,0:T(8,128)(2,1)S(1)}, bf16[1024,384]{1,0:T(8,128)(2,1)S(1)}, bf16[1024,384]{1,0:T(8,128)(2,1)S(1)}, bf16[1024,384]{1,0:T(8,128)(2,1)S(1)}) custom-call(bf16[1024,1152]{1,0:T(8,128)(2,1)S(1)} %copy-done.2, bf16[1024,1152]{1,0:T(8,128)(2,1)S(1)} %copy-done.5, bf16[1024,1152]{1,0:T(8,128)(2,1)S(1)} %copy-done.2, ...), custom_call_target="tpu_custom_call" | custom-call | flops 12582912 | bytes 98304 | tf_op jit(solution)/shard_map/attend/pallas_call | solution.py:75
  299.4 6.1 %collective-permute-done.22 = bf16[1024,256]{1,0:T(8,128)(2,1)} collective-permute-done((bf16[1024,256]{1,0:T(8,128)(2,1)}, bf16[1024,256]{1,0:T(8,128)(2,1)}, u32[]{:S(2)}, u32[]{:S(2)}) %collective-permute-start.22) | collective-permute-done | bytes 524320 | tf_op jit(solution)/shard_map/ppermute | solution.py:121
  307.4 6.3 %in_product.8 = bf16[512,768]{1,0:T(8,128)(2,1)S(1)} custom-call(bf16[1024,3072]{1,0:T(8,128)(2,1)} %assemble.1.rows_ref, bf16[3072,768]{1,0:T(8,128)(2,1)} %bitcast.16.weight_ref.refs_1_), custom_call_target="tpu_custom_call" | custom-call | flops 37748736 | bytes 184320 | tf_op jit(solution)/shard_map/in_product/pallas_call | solution.py:268
  316.9 18.5 %back_product.5.refs_2_ = bf16[1024,3072]{1,0:T(8,128)(2,1)} custom-call(bf16[1024,384]{1,0:T(8,128)(2,1)S(1)} %copy-done.29, bf16[1024,384]{1,0:T(8,128)(2,1)S(1)} %copy-done.31, bf16[1024,384]{1,0:T(8,128)(2,1)S(1)} %copy-done.33, bf16[1024,512]{1,0:T(8,128)(2,1)S(1)} %get-tuple-element.70.refs_3_, bf16[1024,256]{1,0:T(8,128)(2,1)S(1)} %get-tuple-element.78.refs_4_, ...), custom_call_target="tpu_custom_call" | custom-call | flops 188743680 | bytes 282624 | tf_op jit(solution)/shard_map/back_product/pallas_call | solution.py:321
  335.4 12.3 %out_product.6.refs_2_ = bf16[1024,3072]{1,0:T(8,128)(2,1)} custom-call(bf16[1024,384]{1,0:T(8,128)(2,1)S(1)} %copy-done.27, bf16[1024,512]{1,0:T(8,128)(2,1)S(1)} %get-tuple-element.71.refs_1_, bf16[1024,256]{1,0:T(8,128)(2,1)S(1)} %get-tuple-element.79.refs_2_, bf16[384,3072]{1,0:T(8,128)(2,1)S(1)} %copy-done, bf16[1536,3072]{1,0:T(8,128)(2,1)} %refs_1_.11), custom_call_target="tpu_custom_call" | custom-call | flops 113246208 | bytes 282624 | tf_op jit(solution)/shard_map/out_product/pallas_call | solution.py:321
  349.8 7.6 %out_product.7 = bf16[512,3072]{1,0:T(8,128)(2,1)} custom-call(bf16[512,768]{1,0:T(8,128)(2,1)S(1)} %get-tuple-element.77.refs_0_, bf16[1536,3072]{1,0:T(8,128)(2,1)} %refs_1_.11, bf16[1024,3072]{1,0:T(8,128)(2,1)} %out_product.6.refs_2_), custom_call_target="tpu_custom_call" | custom-call | flops 37748736 | bytes 196608 | tf_op jit(solution)/shard_map/out_product/pallas_call | solution.py:321
  357.5 6.9 %back_product.6 = bf16[512,3072]{1,0:T(8,128)(2,1)S(1)} custom-call(bf16[512,768]{1,0:T(8,128)(2,1)S(1)} %get-tuple-element.58.refs_0_, bf16[3072,768]{1,0:T(8,128)(2,1)} %bitcast.16.weight_ref.refs_1_, bf16[1024,3072]{1,0:T(8,128)(2,1)} %back_product.5.refs_2_), custom_call_target="tpu_custom_call" | custom-call | flops 37748736 | bytes 122880 | tf_op jit(solution)/shard_map/back_product/pallas_call | solution.py:321
  367.1 3.2 out_product.9
  372.4 3.2 out_product.11
  375.7 3.9 back_product.9
  381.5 3.3 back_product.8
  386.8 3.2 out_product.10
  390.0 3.2 out_product.8
  393.3 3.3 back_product.7
  398.4 9.2 %collective-permute-done.29 = bf16[256,1536]{1,0:T(8,128)(2,1)S(1)} collective-permute-done((bf16[256,1536]{1,0:T(8,128)(2,1)S(1)}, bf16[256,1536]{1,0:T(8,128)(2,1)S(1)}, u32[]{:S(2)}, u32[]{:S(2)}) %collective-permute-start.29) | collective-permute-done | bytes 786464 | tf_op jit(solution)/shard_map/ppermute | solution.py:121
  411.9 11.9 %collective-permute-done.33 = bf16[256,1536]{1,0:T(8,128)(2,1)S(1)} collective-permute-done((bf16[256,1536]{1,0:T(8,128)(2,1)S(1)}, bf16[256,1536]{1,0:T(8,128)(2,1)S(1)}, u32[]{:S(2)}, u32[]{:S(2)}) %collective-permute-start.33) | collective-permute-done | bytes 786464 | tf_op jit(solution)/shard_map/ppermute | solution.py:121
  431.0 12.1 %collective-permute-done.34 = bf16[2,64,1536]{2,1,0:T(8,128)(2,1)S(1)} collective-permute-done((bf16[2,64,1536]{2,1,0:T(8,128)(2,1)S(1)}, bf16[2,64,1536]{2,1,0:T(8,128)(2,1)S(1)}, u32[]{:S(2)}, u32[]{:S(2)}) %collective-permute-start.34) | collective-permute-done | bytes 393248 | tf_op jit(solution)/shard_map/ppermute | solution.py:121
  444.6 9.8 %collective-permute-done.35 = bf16[64,1536]{1,0:T(8,128)(2,1)S(1)} collective-permute-done((bf16[64,1536]{1,0:T(8,128)(2,1)S(1)}, bf16[64,1536]{1,0:T(8,128)(2,1)S(1)}, u32[]{:S(2)}, u32[]{:S(2)}) %collective-permute-start.35) | collective-permute-done | bytes 196640 | tf_op jit(solution)/shard_map/ppermute | solution.py:121
  455.3 5.6 %all-reduce = (f32[64]{0:T(128)S(1)}, f32[64]{0:T(128)}) all-reduce(f32[64]{0:T(128)S(1)} %fusion.28, f32[64]{0:T(128)} %reduce_sum.48), channel_id=1, replica_groups=mesh['gx'=4,'gy'=4,'gz'=2] {'gz'}, use_global_device_ids=true, to_apply=%region_8.9 | all-reduce | flops 128 | bytes 1024 | tf_op jit(solution)/shard_map/psum | solution.py:491
  (191 shorter events, 79.7 us)
Async XLA Ops:
  0.6 19.0 %collective-permute-start.2 = (bf16[64,3072]{1,0:T(8,128)(2,1)}, bf16[64,3072]{1,0:T(8,128)(2,1)S(1)}, u32[]{:S(2)}, u32[]{:S(2)}) collective-permute-start(bf16[64,3072]{1,0:T(8,128)(2,1)} %param.9), channel_id=1, source_target_pairs={{0,16},{8,24},{16,0},{24,8},{1,17},{9,25},{17,1},{25,9},{2,18},{10... | collective-permute-start | bytes 1179656 | tf_op jit(solution)/shard_map/ppermute | solution.py:121
  10.9 10.4 %collective-permute-start = (bf16[64,3072]{1,0:T(8,128)(2,1)S(1)}, bf16[64,3072]{1,0:T(8,128)(2,1)S(1)}, u32[]{:S(2)}, u32[]{:S(2)}) collective-permute-start(bf16[64,3072]{1,0:T(8,128)(2,1)S(1)} %fusion.27), channel_id=1, source_target_pairs={{0,16},{8,24},{16,0},{24,8},{1,17},{9,25},{17,1},{25,9},{2,18},{10... | collective-permute-start | bytes 1179656 | tf_op jit(solution)/shard_map/ppermute | solution.py:121
  19.7 2.6 collective-permute-start.9
  30.5 28.4 %copy-start.9 = (bf16[256,1920]{1,0:T(8,128)(2,1)}, bf16[256,1920]{1,0:T(8,128)(2,1)S(1)}, u32[]{:S(2)}) copy-start(bf16[256,1920]{1,0:T(8,128)(2,1)S(1)} %cot_product.6) | copy-start | bytes 2949124
  30.5 101.7 %all-to-all-start = ((bf16[4,768,1152]{2,1,0:T(8,128)(2,1)}), bf16[4,768,1152]{2,1,0:T(8,128)(2,1)}, u32[]{:S(2)}, u32[]{:S(2)}) async-start(bf16[4,768,1152]{2,1,0:T(8,128)(2,1)} %pack.4), calls=%async_computation | async-start | bytes 14155776 | tf_op jit(solution)/shard_map/all_to_all | solution.py:359
  35.9 20.2 %collective-permute-start.5 = (bf16[2,64,3072]{2,1,0:T(8,128)(2,1)}, bf16[2,64,3072]{2,1,0:T(8,128)(2,1)S(1)}, u32[]{:S(2)}, u32[]{:S(2)}) collective-permute-start(bf16[2,64,3072]{2,1,0:T(8,128)(2,1)} %copy-done.17), channel_id=1, source_target_pairs={{0,2},{2,0},{4,6},{6,4},{1,3},{3,1},{5,7},{7,5},{8,10},{10,8},{12,... | collective-permute-start | bytes 2359304 | tf_op jit(solution)/shard_map/ppermute | solution.py:121
  56.1 4.3 collective-permute-start.6
  56.1 38.1 %collective-permute-start.3 = (bf16[2,64,3072]{2,1,0:T(8,128)(2,1)}, bf16[2,64,3072]{2,1,0:T(8,128)(2,1)S(1)}, u32[]{:S(2)}, u32[]{:S(2)}) collective-permute-start(bf16[2,64,3072]{2,1,0:T(8,128)(2,1)} %copy-done.17), channel_id=1, source_target_pairs={{0,4},{2,6},{4,0},{6,2},{1,5},{3,7},{5,1},{7,3},{8,12},{10,14},{12... | collective-permute-start | bytes 2359304 | tf_op jit(solution)/shard_map/ppermute | solution.py:121
  58.9 48.6 %collective-permute-start.10 = (bf16[256,1920]{1,0:T(8,128)(2,1)S(1)}, bf16[256,1920]{1,0:T(8,128)(2,1)S(1)}, u32[]{:S(2)}, u32[]{:S(2)}) collective-permute-start(bf16[256,1920]{1,0:T(8,128)(2,1)S(1)} %cot_product.6), channel_id=1, source_target_pairs={{0,1},{1,0},{2,3},{3,2},{4,5},{5,4},{6,7},{7,6},{8,9},{9,8},{10,11... | collective-permute-start | bytes 2949128 | tf_op jit(solution)/shard_map/ppermute | solution.py:121
  68.6 31.0 %copy-start.11 = (bf16[256,1920]{1,0:T(8,128)(2,1)}, bf16[256,1920]{1,0:T(8,128)(2,1)S(1)}, u32[]{:S(2)}) copy-start(bf16[256,1920]{1,0:T(8,128)(2,1)S(1)} %cot_product.4) | copy-start | bytes 2949124
  68.6 62.7 %collective-permute-start.7 = (bf16[256,1920]{1,0:T(8,128)(2,1)S(1)}, bf16[256,1920]{1,0:T(8,128)(2,1)S(1)}, u32[]{:S(2)}, u32[]{:S(2)}) collective-permute-start(bf16[256,1920]{1,0:T(8,128)(2,1)S(1)} %cot_product.4), channel_id=1, source_target_pairs={{0,1},{1,0},{2,3},{3,2},{4,5},{5,4},{6,7},{7,6},{8,9},{9,8},{10,11... | collective-permute-start | bytes 2949128 | tf_op jit(solution)/shard_map/ppermute | solution.py:121
  69.1 36.3 %collective-permute-start.11 = (bf16[2,64,3072]{2,1,0:T(8,128)(2,1)}, bf16[2,64,3072]{2,1,0:T(8,128)(2,1)S(1)}, u32[]{:S(2)}, u32[]{:S(2)}) collective-permute-start(bf16[2,64,3072]{2,1,0:T(8,128)(2,1)} %pad_maximum_fusion.refs_0_), channel_id=1, source_target_pairs={{0,2},{2,0},{4,6},{6,4},{1,3},{3,1},{5,7},{7,5},{8,10},{10,8},{12,... | collective-permute-start | bytes 2359304 | tf_op jit(solution)/shard_map/ppermute | solution.py:121
  94.3 13.2 %collective-permute-start.12 = (bf16[2,64,3072]{2,1,0:T(8,128)(2,1)S(1)}, bf16[2,64,3072]{2,1,0:T(8,128)(2,1)S(1)}, u32[]{:S(2)}, u32[]{:S(2)}) collective-permute-start(bf16[2,64,3072]{2,1,0:T(8,128)(2,1)S(1)} %collective-permute-done.3.own_ref), channel_id=1, source_target_pairs={{0,8},{8,0},{16,24},{24,16},{1,9},{9,1},{17,25},{25,17},{2,10},{10... | collective-permute-start | bytes 2359304 | tf_op jit(solution)/shard_map/ppermute | solution.py:121
  94.3 36.1 %collective-permute-start.4 = (bf16[2,64,3072]{2,1,0:T(8,128)(2,1)S(1)}, bf16[2,64,3072]{2,1,0:T(8,128)(2,1)S(1)}, u32[]{:S(2)}, u32[]{:S(2)}) collective-permute-start(bf16[2,64,3072]{2,1,0:T(8,128)(2,1)S(1)} %collective-permute-done.3.own_ref), channel_id=1, source_target_pairs={{0,2},{2,0},{4,6},{6,4},{1,3},{3,1},{5,7},{7,5},{8,10},{10,8},{12,... | collective-permute-start | bytes 2359304 | tf_op jit(solution)/shard_map/ppermute | solution.py:121
  105.5 35.1 %collective-permute-start.15 = (bf16[2,64,3072]{2,1,0:T(8,128)(2,1)}, bf16[2,64,3072]{2,1,0:T(8,128)(2,1)}, u32[]{:S(2)}, u32[]{:S(2)}) collective-permute-start(bf16[2,64,3072]{2,1,0:T(8,128)(2,1)} %pad_maximum_fusion.refs_0_), channel_id=1, source_target_pairs={{0,4},{2,6},{4,0},{6,2},{1,5},{3,7},{5,1},{7,3},{8,12},{10,14},{12... | collective-permute-start | bytes 2359304 | tf_op jit(solution)/shard_map/ppermute | solution.py:121
  116.0 26.0 %copy-start.13 = (bf16[256,1920]{1,0:T(8,128)(2,1)}, bf16[256,1920]{1,0:T(8,128)(2,1)S(1)}, u32[]{:S(2)}) copy-start(bf16[256,1920]{1,0:T(8,128)(2,1)S(1)} %cot_product.7) | copy-start | bytes 2949124
  132.2 51.5 %all-to-all-start.1 = ((bf16[4,768,512]{2,1,0:T(8,128)(2,1)}), bf16[4,768,512]{2,1,0:T(8,128)(2,1)}, u32[]{:S(2)}, u32[]{:S(2)}) async-start(bf16[4,768,512]{2,1,0:T(8,128)(2,1)} %copy-done.7), calls=%async_computation.1 | async-start | bytes 6291456 | tf_op jit(solution)/shard_map/all_to_all | solution.py:359
  136.8 16.6 %copy-start.35 = (bf16[2,64,3072]{2,1,0:T(8,128)(2,1)S(1)}, bf16[2,64,3072]{2,1,0:T(8,128)(2,1)}, u32[]{:S(2)}) copy-start(bf16[2,64,3072]{2,1,0:T(8,128)(2,1)} %copy-done.34) | copy-start | bytes 2359300
  136.9 5.7 %collective-permute-start.8 = (bf16[2,64,3072]{2,1,0:T(8,128)(2,1)}, bf16[2,64,3072]{2,1,0:T(8,128)(2,1)S(1)}, u32[]{:S(2)}, u32[]{:S(2)}) collective-permute-start(bf16[2,64,3072]{2,1,0:T(8,128)(2,1)} %copy-done.36), channel_id=1, source_target_pairs={{0,8},{8,0},{16,24},{24,16},{1,9},{9,1},{17,25},{25,17},{2,10},{10... | collective-permute-start | bytes 2359304 | tf_op jit(solution)/shard_map/ppermute | solution.py:121
  137.3 16.1 %collective-permute-start.1 = (bf16[2,64,3072]{2,1,0:T(8,128)(2,1)}, bf16[2,64,3072]{2,1,0:T(8,128)(2,1)S(1)}, u32[]{:S(2)}, u32[]{:S(2)}) collective-permute-start(bf16[2,64,3072]{2,1,0:T(8,128)(2,1)} %pad_maximum_fusion.refs_0_), channel_id=1, source_target_pairs={{0,8},{8,0},{16,24},{24,16},{1,9},{9,1},{17,25},{25,17},{2,10},{10... | collective-permute-start | bytes 2359304 | tf_op jit(solution)/shard_map/ppermute | solution.py:121
  140.6 16.9 %collective-permute-start.17 = (bf16[2,64,3072]{2,1,0:T(8,128)(2,1)}, bf16[2,64,3072]{2,1,0:T(8,128)(2,1)S(1)}, u32[]{:S(2)}, u32[]{:S(2)}) collective-permute-start(bf16[2,64,3072]{2,1,0:T(8,128)(2,1)} %collective-permute-done.15.refs_4_), channel_id=1, source_target_pairs={{0,2},{2,0},{4,6},{6,4},{1,3},{3,1},{5,7},{7,5},{8,10},{10,8},{12,... | collective-permute-start | bytes 2359304 | tf_op jit(solution)/shard_map/ppermute | solution.py:121
  142.0 24.7 %collective-permute-start.13 = (bf16[256,1920]{1,0:T(8,128)(2,1)S(1)}, bf16[256,1920]{1,0:T(8,128)(2,1)S(1)}, u32[]{:S(2)}, u32[]{:S(2)}) collective-permute-start(bf16[256,1920]{1,0:T(8,128)(2,1)S(1)} %cot_product.7), channel_id=1, source_target_pairs={{0,1},{1,0},{2,3},{3,2},{4,5},{5,4},{6,7},{7,6},{8,9},{9,8},{10,11... | collective-permute-start | bytes 2949128 | tf_op jit(solution)/shard_map/ppermute | solution.py:121
  151.8 31.8 %collective-permute-start.19 = (bf16[256,1920]{1,0:T(8,128)(2,1)S(1)}, bf16[256,1920]{1,0:T(8,128)(2,1)}, u32[]{:S(2)}, u32[]{:S(2)}) collective-permute-start(bf16[256,1920]{1,0:T(8,128)(2,1)S(1)} %cot_product.5), channel_id=1, source_target_pairs={{0,1},{1,0},{2,3},{3,2},{4,5},{5,4},{6,7},{7,6},{8,9},{9,8},{10,11... | collective-permute-start | bytes 2949128 | tf_op jit(solution)/shard_map/ppermute | solution.py:121
  153.4 13.3 %collective-permute-start.16 = (bf16[2,64,3072]{2,1,0:T(8,128)(2,1)}, bf16[2,64,3072]{2,1,0:T(8,128)(2,1)S(1)}, u32[]{:S(2)}, u32[]{:S(2)}) collective-permute-start(bf16[2,64,3072]{2,1,0:T(8,128)(2,1)} %collective-permute-done.15.refs_4_), channel_id=1, source_target_pairs={{0,8},{8,0},{16,24},{24,16},{1,9},{9,1},{17,25},{25,17},{2,10},{10... | collective-permute-start | bytes 2359304 | tf_op jit(solution)/shard_map/ppermute | solution.py:121
  153.4 13.3 %collective-permute-start.14 = (bf16[2,64,3072]{2,1,0:T(8,128)(2,1)S(1)}, bf16[2,64,3072]{2,1,0:T(8,128)(2,1)S(1)}, u32[]{:S(2)}, u32[]{:S(2)}) collective-permute-start(bf16[2,64,3072]{2,1,0:T(8,128)(2,1)S(1)} %copy-done.35), channel_id=1, source_target_pairs={{0,8},{8,0},{16,24},{24,16},{1,9},{9,1},{17,25},{25,17},{2,10},{10... | collective-permute-start | bytes 2359304 | tf_op jit(solution)/shard_map/ppermute | solution.py:121
  157.5 10.2 %collective-permute-start.18 = (bf16[2,64,3072]{2,1,0:T(8,128)(2,1)S(1)}, bf16[2,64,3072]{2,1,0:T(8,128)(2,1)S(1)}, u32[]{:S(2)}, u32[]{:S(2)}) collective-permute-start(bf16[2,64,3072]{2,1,0:T(8,128)(2,1)S(1)} %collective-permute-done.17.refs_6_), channel_id=1, source_target_pairs={{0,8},{8,0},{16,24},{24,16},{1,9},{9,1},{17,25},{25,17},{2,10},{10... | collective-permute-start | bytes 2359304 | tf_op jit(solution)/shard_map/ppermute | solution.py:121
  183.7 28.6 %all-to-all-start.2 = ((bf16[4,768,256]{2,1,0:T(8,128)(2,1)}), bf16[4,768,256]{2,1,0:T(8,128)(2,1)}, u32[]{:S(2)}, u32[]{:S(2)}) async-start(bf16[4,768,256]{2,1,0:T(8,128)(2,1)} %copy-done.8), calls=%async_computation.2 | async-start | bytes 3145728 | tf_op jit(solution)/shard_map/all_to_all | solution.py:359
  212.3 60.9 %all-to-all-start.3 = ((bf16[4,768,768]{2,1,0:T(8,128)(2,1)}), bf16[4,768,768]{2,1,0:T(8,128)(2,1)}, u32[]{:S(2)}, u32[]{:S(2)}) async-start(bf16[4,768,768]{2,1,0:T(8,128)(2,1)} %copy-done.6), calls=%async_computation.3 | async-start | bytes 9437184 | tf_op jit(solution)/shard_map/all_to_all | solution.py:359
  217.4 54.3 %collective-permute-start.20 = (bf16[1024,1152]{1,0:T(8,128)(2,1)}, bf16[1024,1152]{1,0:T(8,128)(2,1)S(1)}, u32[]{:S(2)}, u32[]{:S(2)}) collective-permute-start(bf16[1024,1152]{1,0:T(8,128)(2,1)} %copy-done.1), channel_id=1, source_target_pairs={{0,1},{1,0},{2,3},{3,2},{4,5},{5,4},{6,7},{7,6},{8,9},{9,8},{10,11... | collective-permute-start | bytes 7077896 | tf_op jit(solution)/shard_map/ppermute | solution.py:121
  225.0 89.3 %collective-permute-start.21 = (bf16[1024,512]{1,0:T(8,128)(2,1)S(1)}, bf16[1024,512]{1,0:T(8,128)(2,1)}, u32[]{:S(2)}, u32[]{:S(2)}) collective-permute-start(bf16[1024,512]{1,0:T(8,128)(2,1)S(1)} %in_product.6), channel_id=1, source_target_pairs={{0,1},{1,0},{2,3},{3,2},{4,5},{5,4},{6,7},{7,6},{8,9},{9,8},{10,11... | collective-permute-start | bytes 3145736 | tf_op jit(solution)/shard_map/ppermute | solution.py:121
  232.5 73.0 %collective-permute-start.22 = (bf16[1024,256]{1,0:T(8,128)(2,1)}, bf16[1024,256]{1,0:T(8,128)(2,1)}, u32[]{:S(2)}, u32[]{:S(2)}) collective-permute-start(bf16[1024,256]{1,0:T(8,128)(2,1)} %in_product.9), channel_id=1, source_target_pairs={{0,1},{1,0},{2,3},{3,2},{4,5},{5,4},{6,7},{7,6},{8,9},{9,8},{10,11... | collective-permute-start | bytes 1572872 | tf_op jit(solution)/shard_map/ppermute | solution.py:121
  279.6 68.1 %collective-permute-start.23 = (bf16[512,768]{1,0:T(8,128)(2,1)S(1)}, bf16[512,768]{1,0:T(8,128)(2,1)}, u32[]{:S(2)}, u32[]{:S(2)}) collective-permute-start(bf16[512,768]{1,0:T(8,128)(2,1)S(1)} %in_product.7), channel_id=1, source_target_pairs={{0,1},{1,0},{2,3},{3,2},{4,5},{5,4},{6,7},{7,6},{8,9},{9,8},{10,11... | collective-permute-start | bytes 2359304 | tf_op jit(solution)/shard_map/ppermute | solution.py:121
  313.7 43.7 %collective-permute-start.24 = (bf16[512,768]{1,0:T(8,128)(2,1)S(1)}, bf16[512,768]{1,0:T(8,128)(2,1)}, u32[]{:S(2)}, u32[]{:S(2)}) collective-permute-start(bf16[512,768]{1,0:T(8,128)(2,1)S(1)} %in_product.8), channel_id=1, source_target_pairs={{0,1},{1,0},{2,3},{3,2},{4,5},{5,4},{6,7},{7,6},{8,9},{9,8},{10,11... | collective-permute-start | bytes 2359304 | tf_op jit(solution)/shard_map/ppermute | solution.py:121
  316.9 18.5 %copy-start.27 = (bf16[1024,384]{1,0:T(8,128)(2,1)S(1)}, bf16[1024,384]{1,0:T(8,128)(2,1)}, u32[]{:S(2)}) copy-start(bf16[1024,384]{1,0:T(8,128)(2,1)} %copy-done.26) | copy-start | bytes 2359300
  357.5 9.6 %collective-permute-start.25 = (bf16[512,3072]{1,0:T(8,128)(2,1)}, bf16[512,3072]{1,0:T(8,128)(2,1)S(1)}, u32[]{:S(2)}, u32[]{:S(2)}) collective-permute-start(bf16[512,3072]{1,0:T(8,128)(2,1)} %out_product.7), channel_id=1, source_target_pairs={{0,8},{8,0},{16,24},{24,16},{1,9},{9,1},{17,25},{25,17},{2,10},{10... | collective-permute-start | bytes 9437192 | tf_op jit(solution)/shard_map/ppermute | solution.py:121
  364.4 11.3 %collective-permute-start.32 = (bf16[512,3072]{1,0:T(8,128)(2,1)S(1)}, bf16[512,3072]{1,0:T(8,128)(2,1)S(1)}, u32[]{:S(2)}, u32[]{:S(2)}) collective-permute-start(bf16[512,3072]{1,0:T(8,128)(2,1)S(1)} %back_product.6), channel_id=1, source_target_pairs={{0,8},{8,0},{16,24},{24,16},{1,9},{9,1},{17,25},{25,17},{2,10},{10... | collective-permute-start | bytes 9437192 | tf_op jit(solution)/shard_map/ppermute | solution.py:121
  370.3 26.2 %collective-permute-start.26 = (bf16[256,1536]{1,0:T(8,128)(2,1)S(1)}, bf16[256,1536]{1,0:T(8,128)(2,1)}, u32[]{:S(2)}, u32[]{:S(2)}) collective-permute-start(bf16[256,1536]{1,0:T(8,128)(2,1)S(1)} %out_product.9), channel_id=1, source_target_pairs={{0,16},{8,24},{16,0},{24,8},{1,17},{9,25},{17,1},{25,9},{2,18},{10... | collective-permute-start | bytes 2359304 | tf_op jit(solution)/shard_map/ppermute | solution.py:121
  375.6 32.0 %collective-permute-start.29 = (bf16[256,1536]{1,0:T(8,128)(2,1)S(1)}, bf16[256,1536]{1,0:T(8,128)(2,1)S(1)}, u32[]{:S(2)}, u32[]{:S(2)}) collective-permute-start(bf16[256,1536]{1,0:T(8,128)(2,1)S(1)} %out_product.11), channel_id=1, source_target_pairs={{0,16},{8,24},{16,0},{24,8},{1,17},{9,25},{17,1},{25,9},{2,18},{10... | collective-permute-start | bytes 2359304 | tf_op jit(solution)/shard_map/ppermute | solution.py:121
  379.8 29.7 %collective-permute-start.36 = (bf16[2,2,64,1536]{3,2,0,1:T(8,128)(2,1)S(1)}, bf16[2,2,64,1536]{3,2,0,1:T(8,128)(2,1)S(1)}, u32[]{:S(2)}, u32[]{:S(2)}) collective-permute-start(bf16[2,2,64,1536]{3,2,0,1:T(8,128)(2,1)S(1)} %bitcast.100), channel_id=1, source_target_pairs={{0,2},{2,0},{4,6},{6,4},{1,3},{3,1},{5,7},{7,5},{8,10},{10,8},{12,... | collective-permute-start | bytes 2359304 | tf_op jit(solution)/shard_map/ppermute | solution.py:121
  384.7 39.1 %collective-permute-start.33 = (bf16[256,1536]{1,0:T(8,128)(2,1)S(1)}, bf16[256,1536]{1,0:T(8,128)(2,1)S(1)}, u32[]{:S(2)}, u32[]{:S(2)}) collective-permute-start(bf16[256,1536]{1,0:T(8,128)(2,1)S(1)} %back_product.8), channel_id=1, source_target_pairs={{0,16},{8,24},{16,0},{24,8},{1,17},{9,25},{17,1},{25,9},{2,18},{10... | collective-permute-start | bytes 2359304 | tf_op jit(solution)/shard_map/ppermute | solution.py:121
  397.9 27.8 %collective-permute-start.27 = (bf16[2,64,1536]{2,1,0:T(8,128)(2,1)S(1)}, bf16[2,64,1536]{2,1,0:T(8,128)(2,1)S(1)}, u32[]{:S(2)}, u32[]{:S(2)}) collective-permute-start(bf16[2,64,1536]{2,1,0:T(8,128)(2,1)S(1)} %fusion.40), channel_id=1, source_target_pairs={{0,2},{2,0},{4,6},{6,4},{1,3},{3,1},{5,7},{7,5},{8,10},{10,8},{12,... | collective-permute-start | bytes 1179656 | tf_op jit(solution)/shard_map/ppermute | solution.py:121
  407.8 20.1 %collective-permute-start.30 = (bf16[2,64,1536]{2,1,0:T(8,128)(2,1)S(1)}, bf16[2,64,1536]{2,1,0:T(8,128)(2,1)S(1)}, u32[]{:S(2)}, u32[]{:S(2)}) collective-permute-start(bf16[2,64,1536]{2,1,0:T(8,128)(2,1)S(1)} %fusion.41), channel_id=1, source_target_pairs={{0,2},{2,0},{4,6},{6,4},{1,3},{3,1},{5,7},{7,5},{8,10},{10,8},{12,... | collective-permute-start | bytes 1179656 | tf_op jit(solution)/shard_map/ppermute | solution.py:121
  409.8 19.2 %collective-permute-start.37 = (bf16[2,64,1536]{2,1,0:T(8,128)(2,1)S(1)}, bf16[2,64,1536]{2,1,0:T(8,128)(2,1)S(1)}, u32[]{:S(2)}, u32[]{:S(2)}) collective-permute-start(bf16[2,64,1536]{2,1,0:T(8,128)(2,1)S(1)} %fusion.39), channel_id=1, source_target_pairs={{0,4},{2,6},{4,0},{6,2},{1,5},{3,7},{5,1},{7,3},{8,12},{10,14},{12... | collective-permute-start | bytes 1179656 | tf_op jit(solution)/shard_map/ppermute | solution.py:121
  424.1 19.0 %collective-permute-start.34 = (bf16[2,64,1536]{2,1,0:T(8,128)(2,1)S(1)}, bf16[2,64,1536]{2,1,0:T(8,128)(2,1)S(1)}, u32[]{:S(2)}, u32[]{:S(2)}) collective-permute-start(bf16[2,64,1536]{2,1,0:T(8,128)(2,1)S(1)} %fusion.42), channel_id=1, source_target_pairs={{0,2},{2,0},{4,6},{6,4},{1,3},{3,1},{5,7},{7,5},{8,10},{10,8},{12,... | collective-permute-start | bytes 1179656 | tf_op jit(solution)/shard_map/ppermute | solution.py:121
  425.9 35.0 %collective-permute-start.28 = (bf16[64,1536]{1,0:T(8,128)(2,1)S(1)}, bf16[64,1536]{1,0:T(8,128)(2,1)}, u32[]{:S(2)}, u32[]{:S(2)}) collective-permute-start(bf16[64,1536]{1,0:T(8,128)(2,1)S(1)} %fusion.47), channel_id=1, source_target_pairs={{0,4},{2,6},{4,0},{6,2},{1,5},{3,7},{5,1},{7,3},{8,12},{10,14},{12... | collective-permute-start | bytes 589832 | tf_op jit(solution)/shard_map/ppermute | solution.py:121
  428.1 34.4 %collective-permute-start.31 = (bf16[64,1536]{1,0:T(8,128)(2,1)S(1)}, bf16[64,1536]{1,0:T(8,128)(2,1)}, u32[]{:S(2)}, u32[]{:S(2)}) collective-permute-start(bf16[64,1536]{1,0:T(8,128)(2,1)S(1)} %fusion.48), channel_id=1, source_target_pairs={{0,4},{2,6},{4,0},{6,2},{1,5},{3,7},{5,1},{7,3},{8,12},{10,14},{12... | collective-permute-start | bytes 589832 | tf_op jit(solution)/shard_map/ppermute | solution.py:121
  429.2 15.3 %collective-permute-start.38 = (bf16[64,1536]{1,0:T(8,128)(2,1)S(1)}, bf16[64,1536]{1,0:T(8,128)(2,1)S(1)}, u32[]{:S(2)}, u32[]{:S(2)}) collective-permute-start(bf16[64,1536]{1,0:T(8,128)(2,1)S(1)} %fusion.50), channel_id=1, source_target_pairs={{0,16},{8,24},{16,0},{24,8},{1,17},{9,25},{17,1},{25,9},{2,18},{10... | collective-permute-start | bytes 589832 | tf_op jit(solution)/shard_map/ppermute | solution.py:121
  443.2 11.1 %collective-permute-start.35 = (bf16[64,1536]{1,0:T(8,128)(2,1)S(1)}, bf16[64,1536]{1,0:T(8,128)(2,1)S(1)}, u32[]{:S(2)}, u32[]{:S(2)}) collective-permute-start(bf16[64,1536]{1,0:T(8,128)(2,1)S(1)} %fusion.49), channel_id=1, source_target_pairs={{0,4},{2,6},{4,0},{6,2},{1,5},{3,7},{5,1},{7,3},{8,12},{10,14},{12... | collective-permute-start | bytes 589832 | tf_op jit(solution)/shard_map/ppermute | solution.py:121
  (39 other events, 176.7 us)
